TPU v7x, 32 devices: a whole 2x2x4 slice. The times are simulated.
32 devices in a mesh: wide: 8 (over y, x, core), narrow: 4 (over z).
Axes of the slice: x: 2, y: 2, z: 4, core: 2. Of those that a mesh axis runs over, the one named last changes fastest.
Arguments:
- tokens: int32 [8, 1024], P('wide'), may hold values from 0 to 32767
- picks: int32 [8, 128], P('wide'), may hold values from 0 to 1023, as said below
- targets: int32 [8, 128], P('wide'), may hold values from -1 to 32767, as said below
- lengths: int32 [8, 2], P('wide'), may hold values from 256 to 768, as said below
- skip: int32 [8], P('wide'), may hold values 0 or 1
- embed: float32 [32768, 2048], P('narrow', 'wide'), may hold values from -0.26516504 to 0.26516504
- embed_m: float32 [32768, 2048], P('narrow', 'wide'), may hold values from -3.33786e-06 to 3.33786e-06
- embed_v: float32 [32768, 2048], P('narrow', 'wide'), may hold values from 1.8715948e-13 to 7.486379e-13
- attn_qo: float32 [2048, 2, 2048], P('wide', None, 'narrow'), may hold values from -0.125 to 0.125
- attn_qo_mom: float32 [2048, 2, 2048], P('wide', None, 'narrow'), may hold values from -2.670288e-05 to 2.670288e-05
- attn_kv: float32 [2048, 2, 512], P('wide', None, 'narrow'), may hold values from -0.125 to 0.125
- attn_kv_mom: float32 [2048, 2, 512], P('wide', None, 'narrow'), may hold values from -2.670288e-05 to 2.670288e-05
- ffn: float32 [5632, 3, 2048], P('wide', None, 'narrow'), may hold values from -0.125 to 0.125
- ffn_mom: float32 [5632, 3, 2048], P('wide', None, 'narrow'), may hold values from -2.670288e-05 to 2.670288e-05
- gains: float32 [3, 2048], P(None, ('wide', 'narrow')), may hold values from 0.24 to 1.8
- gains_m: float32 [3, 2048], P(None, ('wide', 'narrow')), may hold values from -1.335144e-05 to 1.335144e-05
- gains_v: float32 [3, 2048], P(None, ('wide', 'narrow')), may hold values from 3.030201e-12 to 1.1942557e-11
Outputs:
- loss_sum: float32 [], replicated
- loss_count: float32 [], replicated
- grad_norm: float32 [], replicated
- embed_new: float32 [32768, 2048], P('narrow', 'wide')
- embed_m_new: float32 [32768, 2048], P('narrow', 'wide')
- embed_v_new: float32 [32768, 2048], P('narrow', 'wide')
- attn_qo_new: float32 [2048, 2, 2048], P('wide', None, 'narrow')
- attn_qo_mom_new: float32 [2048, 2, 2048], P('wide', None, 'narrow')
- attn_kv_new: float32 [2048, 2, 512], P('wide', None, 'narrow')
- attn_kv_mom_new: float32 [2048, 2, 512], P('wide', None, 'narrow')
- ffn_new: float32 [5632, 3, 2048], P('wide', None, 'narrow')
- ffn_mom_new: float32 [5632, 3, 2048], P('wide', None, 'narrow')
- gains_new: float32 [3, 2048], P(None, ('wide', 'narrow'))
- gains_m_new: float32 [3, 2048], P(None, ('wide', 'narrow'))
- gains_v_new: float32 [3, 2048], P(None, ('wide', 'narrow'))
Inputs may be any that keep to these rules, and one draw needn't show every extreme that they name: Within a pack the picks are distinct and increasing; the first is 0 and the last 1023. `targets`: -1 marks a picked position that does not count. Each pack's lengths sum to 1024; some pack holds a sequence of 768 tokens.
All inputs are finite; a program needn't handle non-finite values. No bound on the sum of `skip` on one device may be relied on, other than what follows from the above.
Results may differ from a plain program's by a relative error of at most 0.017.
The roundings to bfloat16 on the way count: a program that leaves them out, or rounds other values in their place, can miss the bound.
Values may be sent and summed in bfloat16 or wider, within the bound.
A program may use at most 440 MiB of HBM per device.

v0:
```python
import jax
import jax.numpy as jnp
from jax import lax
from jax.sharding import PartitionSpec as P

HEADS = 16
HD = 128
KVH = 4
NS_STEPS = 5
STEP = 10


HIGHEST = lax.Precision.HIGHEST
NORM_EPS = 1e-05
ROPE_BASE = 10000.0
EXIT_EARLY = 0.25
EXIT_LAST = 1.0
CLIP_NORM = 0.02
BETA_ONE = 0.9
BETA_TWO = 0.95
ADAM_EPS = 1e-08
RATE_ADAM = 0.02
RATE_GAIN = 0.3
RATE_MUON = 0.3
WEIGHT_DECAY = 0.1
MOMENTUM = 0.95
NEWTON_A = 3.4445
NEWTON_B = -4.775
NEWTON_C = 2.0315
MASKED = -1e30
CONTRACT_ROWS = (((0,), (0,)), ((), ()))
CONTRACT_COLS = (((1,), (1,)), ((), ()))


def combined_all(part, axis, combine):
    gathered = jax.tree.map(lambda a: lax.all_gather(a, axis), part)

    def take(source):
        return jax.tree.map(lambda a: lax.dynamic_index_in_dim(a, source, 0, False), gathered)

    return lax.fori_loop(
        1, lax.axis_size(axis), lambda source, state: combine(state, take(source)), take(0)
    )


def norm_rows(values, gain_row):
    return (
        values * lax.rsqrt(jnp.mean(values * values, axis=-1, keepdims=True) + NORM_EPS) * gain_row
    )


def norm_back(values, gain_row, grad):
    output, pull = jax.vjp(norm_rows, values, gain_row)
    return pull(grad)


def positions(lens, seq_len):
    ends = jnp.cumsum(lens)
    where_at = jnp.arange(seq_len, dtype=jnp.int32)
    segment = jnp.sum((where_at[:, None] >= ends[None, :]).astype(jnp.int32), axis=1)
    starts = ends - lens
    member = segment[:, None] == jnp.arange(lens.shape[0], dtype=jnp.int32)[None, :]
    begin = jnp.sum(jnp.where(member, starts[None, :], 0), axis=1)
    offset_pos = (where_at - begin).astype(jnp.float32)
    inverse = ROPE_BASE ** (-2.0 * jnp.arange(HD // 2, dtype=jnp.float32) / HD)
    angle = offset_pos[:, None] * inverse[None, :]
    return (segment, jnp.cos(angle), jnp.sin(angle))


def rotate(values, cosine, sine):
    half = values.shape[-1] // 2
    first, second = (values[..., :half], values[..., half:])
    cosine, sine = (cosine[:, None, :], sine[:, None, :])
    return jnp.concatenate(
        [first * cosine - second * sine, second * cosine + first * sine], axis=-1
    )


def unrotate(values, cosine, sine):
    half = values.shape[-1] // 2
    first, second = (values[..., :half], values[..., half:])
    cosine, sine = (cosine[:, None, :], sine[:, None, :])
    return jnp.concatenate(
        [first * cosine + second * sine, second * cosine - first * sine], axis=-1
    )


def score_block(queries, keys_all, seg_all, seg_mine, start):
    tok_rows = queries.shape[0]
    seq_len = keys_all.shape[0]
    grouped = queries.reshape(tok_rows, KVH, HEADS // KVH, HD)
    keyed = keys_all.reshape(seq_len, KVH, HD)
    scores = jnp.einsum(
        "tkgd,skd->kgts", grouped, keyed, preferred_element_type=jnp.float32
    ) * HD ** (-0.5)
    rows_at = start + jnp.arange(tok_rows, dtype=jnp.int32)
    cols_at = jnp.arange(seq_len, dtype=jnp.int32)
    allowed = (seg_mine[:, None] == seg_all[None, :]) & (rows_at[:, None] >= cols_at[None, :])
    return jnp.where(allowed, scores, MASKED)


def merge_stats(first, second):
    joint_peak = jnp.maximum(first[0], second[0])
    joint_sum = first[1] * jnp.exp(first[0] - joint_peak) + second[1] * jnp.exp(
        second[0] - joint_peak
    )
    return (joint_peak, joint_sum, first[2] + second[2])


def layer_forward(start_h, qo_w, kv_w, ffn_w, gain_w, cosine, sine, seg_all, seg_mine, start):
    tok_rows = start_h.shape[0]
    normed = norm_rows(start_h, gain_w[0]).astype(jnp.bfloat16)
    queries = jnp.dot(normed, qo_w[:, 0], preferred_element_type=jnp.float32).reshape(
        tok_rows, HEADS, HD
    )
    keys_own = jnp.dot(normed, kv_w[:, 0], preferred_element_type=jnp.float32).reshape(
        tok_rows, KVH, HD
    )
    values_own = jnp.dot(normed, kv_w[:, 1], preferred_element_type=jnp.float32).astype(
        jnp.bfloat16
    )
    queries = rotate(queries, cosine, sine).astype(jnp.bfloat16)
    keys_own = rotate(keys_own, cosine, sine).reshape(tok_rows, KVH * HD).astype(jnp.bfloat16)
    keys_all, values_all = (
        lax.all_gather(keys_own, "narrow", axis=0, tiled=True),
        lax.all_gather(values_own, "narrow", axis=0, tiled=True),
    )
    seq_len = keys_all.shape[0]
    scores = score_block(queries, keys_all, seg_all, seg_mine, start)
    row_peak = jnp.max(scores, axis=-1, keepdims=True)
    shifted_exp = jnp.exp(scores - row_peak)
    row_total = jnp.sum(shifted_exp, axis=-1, keepdims=True)
    probs = (shifted_exp / row_total).astype(jnp.bfloat16)
    log_total = row_peak + jnp.log(row_total)
    mixed = jnp.einsum(
        "kgts,skd->tkgd",
        probs,
        values_all.reshape(seq_len, KVH, HD),
        preferred_element_type=jnp.float32,
    )
    mixed = mixed.reshape(tok_rows, HEADS * HD).astype(jnp.bfloat16)
    middle = start_h + lax.dot_general(
        mixed, qo_w[:, 1], CONTRACT_COLS, preferred_element_type=jnp.float32
    )
    inner = norm_rows(middle, gain_w[1]).astype(jnp.bfloat16)
    gate_up = jnp.einsum("td,fjd->jtf", inner, ffn_w[:, 0:2], preferred_element_type=jnp.float32)
    hidden = (jax.nn.silu(gate_up[0]) * gate_up[1]).astype(jnp.bfloat16)
    final_h = middle + jnp.dot(hidden, ffn_w[:, 2], preferred_element_type=jnp.float32)
    kept = (normed, queries, keys_all, values_all, log_total, mixed, middle, inner, gate_up, hidden)
    return (final_h, kept)


def layer_backward(
    grad_h,
    start_h,
    qo_w,
    kv_w,
    ffn_w,
    gain_w,
    cosine,
    sine,
    seg_all,
    seg_mine,
    start,
    kept,
    reduce_ffn,
):
    normed, queries, keys_all, values_all, log_total, mixed, middle, inner, gate_up, hidden = kept
    tok_rows = start_h.shape[0]
    seq_len = keys_all.shape[0]
    grad_out = grad_h.astype(jnp.bfloat16)
    grad_hidden = lax.dot_general(
        grad_out, ffn_w[:, 2], CONTRACT_COLS, preferred_element_type=jnp.float32
    )
    sigma = jax.nn.sigmoid(gate_up[0])
    grad_gate = grad_hidden * gate_up[1] * sigma * (1.0 + gate_up[0] * (1.0 - sigma))
    grad_up = grad_hidden * gate_up[0] * sigma
    grad_act = jnp.stack([grad_gate, grad_up]).astype(jnp.bfloat16)

    def ffn_rows(row_start, row_count):
        pair_part = jnp.einsum("jtf,td->fjd", grad_act, inner, preferred_element_type=jnp.float32)
        down_part = lax.dot_general(
            hidden, grad_out, CONTRACT_ROWS, preferred_element_type=jnp.float32
        )
        return jnp.concatenate([pair_part, down_part[:, None, :]], axis=1)

    grad_ffn = reduce_ffn(ffn_rows, ffn_w.shape[0])
    grad_inner = jnp.einsum(
        "jtf,fjd->td", grad_act, ffn_w[:, 0:2], preferred_element_type=jnp.float32
    )
    extra_mid, gain_mid = norm_back(middle, gain_w[1], grad_inner)
    grad_mid = grad_h + extra_mid
    grad_branch = grad_mid.astype(jnp.bfloat16)
    grad_mixed = jnp.dot(grad_branch, qo_w[:, 1], preferred_element_type=jnp.float32).astype(
        jnp.bfloat16
    )
    grad_proj = lax.dot_general(
        grad_branch, mixed, CONTRACT_ROWS, preferred_element_type=jnp.float32
    )
    scores = score_block(queries, keys_all, seg_all, seg_mine, start)
    probs = jnp.exp(scores - log_total)
    grouped_grad = grad_mixed.reshape(tok_rows, KVH, HEADS // KVH, HD)
    grad_probs = jnp.einsum(
        "tkgd,skd->kgts",
        grouped_grad,
        values_all.reshape(seq_len, KVH, HD),
        preferred_element_type=jnp.float32,
    )
    grad_scores = (
        probs * (grad_probs - jnp.sum(probs * grad_probs, axis=-1, keepdims=True))
    ).astype(jnp.bfloat16)
    scale = HD ** (-0.5)
    grad_queries = (
        jnp.einsum(
            "kgts,skd->tkgd",
            grad_scores,
            keys_all.reshape(seq_len, KVH, HD),
            preferred_element_type=jnp.float32,
        )
        * scale
    )
    grad_keys_part = (
        jnp.einsum(
            "kgts,tkgd->skd",
            grad_scores,
            queries.reshape(tok_rows, KVH, HEADS // KVH, HD),
            preferred_element_type=jnp.float32,
        )
        * scale
    )
    grad_values_part = jnp.einsum(
        "kgts,tkgd->skd",
        probs.astype(jnp.bfloat16),
        grouped_grad,
        preferred_element_type=jnp.float32,
    )
    grad_keys, grad_values = (
        lax.psum_scatter(
            grad_keys_part.reshape(seq_len, KVH * HD), "narrow", scatter_dimension=0, tiled=True
        ),
        lax.psum_scatter(
            grad_values_part.reshape(seq_len, KVH * HD), "narrow", scatter_dimension=0, tiled=True
        ),
    )
    grad_queries = (
        unrotate(grad_queries.reshape(tok_rows, HEADS, HD), cosine, sine)
        .reshape(tok_rows, HEADS * HD)
        .astype(jnp.bfloat16)
    )
    grad_keys = (
        unrotate(grad_keys.reshape(tok_rows, KVH, HD), cosine, sine)
        .reshape(tok_rows, KVH * HD)
        .astype(jnp.bfloat16)
    )
    grad_values = grad_values.astype(jnp.bfloat16)
    grad_query_w = lax.dot_general(
        normed, grad_queries, CONTRACT_ROWS, preferred_element_type=jnp.float32
    )
    grad_key_w = lax.dot_general(
        normed, grad_keys, CONTRACT_ROWS, preferred_element_type=jnp.float32
    )
    grad_value_w = lax.dot_general(
        normed, grad_values, CONTRACT_ROWS, preferred_element_type=jnp.float32
    )
    grad_normed = lax.dot_general(
        grad_queries, qo_w[:, 0], CONTRACT_COLS, preferred_element_type=jnp.float32
    )
    grad_normed = grad_normed + lax.dot_general(
        grad_keys, kv_w[:, 0], CONTRACT_COLS, preferred_element_type=jnp.float32
    )
    grad_normed = grad_normed + lax.dot_general(
        grad_values, kv_w[:, 1], CONTRACT_COLS, preferred_element_type=jnp.float32
    )
    extra_start, gain_attn = norm_back(start_h, gain_w[0], grad_normed)
    grad_start = grad_mid + extra_start
    grad_qo = jnp.stack([grad_query_w, grad_proj], axis=1)
    grad_kv = jnp.stack([grad_key_w, grad_value_w], axis=1)
    return (grad_start, grad_qo, grad_kv, grad_ffn, gain_attn, gain_mid)


def gram_of(blocks):
    return jnp.einsum("jrc,jsc->jrs", blocks, blocks, precision=HIGHEST)


def poly_apply(blocks, gram):
    square = jnp.einsum("jrs,jst->jrt", gram, gram, precision=HIGHEST)
    return NEWTON_A * blocks + jnp.einsum(
        "jrs,jsc->jrc", NEWTON_B * gram + NEWTON_C * square, blocks, precision=HIGHEST
    )


def orthogonalize(first_set, second_set, third_set):
    current = [first_set, second_set, third_set]
    for iteration in range(NS_STEPS):
        summed = lax.psum((gram_of(current[0]), gram_of(current[1]), gram_of(current[2])), "narrow")
        summed = list(summed)
        if iteration == 0:
            scales = [
                1.0 / (jnp.sqrt(jnp.einsum("jrr->j", gram))[:, None, None] + 1e-07)
                for gram in summed
            ]
            current = [blocks * factor for blocks, factor in zip(current, scales)]
            summed = [gram * factor * factor for gram, factor in zip(summed, scales)]
        current = [poly_apply(blocks, gram) for blocks, gram in zip(current, summed)]
    return current


def adamw(weight, first_m, second_m, grad, rate, decay):
    first_new = BETA_ONE * first_m + (1.0 - BETA_ONE) * grad
    second_new = BETA_TWO * second_m + (1.0 - BETA_TWO) * grad * grad
    update = (
        first_new
        / (1.0 - BETA_ONE**STEP)
        / (jnp.sqrt(second_new / (1.0 - BETA_TWO**STEP)) + ADAM_EPS)
    )
    return (weight * (1.0 - rate * decay) - rate * update, first_new, second_new)


def ffn_by_rows(row_fn, ffn_rows_all):
    return lax.psum_scatter(
        row_fn(jnp.int32(0), lax.axis_size("wide") * (ffn_rows_all // lax.axis_size("wide"))),
        "wide",
        scatter_dimension=0,
        tiled=True,
    )


def per_device(
    tokens,
    picks,
    targets,
    lengths,
    skip,
    embed,
    embed_m,
    embed_v,
    attn_qo,
    attn_qo_mom,
    attn_kv,
    attn_kv_mom,
    ffn,
    ffn_mom,
    gains,
    gains_m,
    gains_v,
):
    narrow_count = lax.axis_size("narrow")
    narrow_spot = lax.axis_index("narrow")
    seq_len = tokens.shape[1]
    tok_rows = seq_len // narrow_count
    start = narrow_spot * tok_rows
    vocab_rows = embed.shape[0]
    token_ids = tokens[0]
    pick_ids = picks[0]
    target_ids = targets[0]
    seg_all, cosine_all, sine_all = positions(lengths[0], seq_len)
    seg_mine = lax.dynamic_slice_in_dim(seg_all, start, tok_rows, 0)
    cosine = lax.dynamic_slice_in_dim(cosine_all, start, tok_rows, 0)
    sine = lax.dynamic_slice_in_dim(sine_all, start, tok_rows, 0)
    keep_layer = (1 - skip[0]).astype(jnp.float32)

    def fetch():
        parts = (
            lax.all_gather(attn_qo.astype(jnp.bfloat16), "narrow", axis=2, tiled=True),
            lax.all_gather(attn_kv.astype(jnp.bfloat16), "narrow", axis=2, tiled=True),
            lax.all_gather(ffn.astype(jnp.bfloat16), "narrow", axis=2, tiled=True),
            lax.all_gather(gains.astype(jnp.bfloat16), "narrow", axis=1, tiled=True),
        )
        return (
            lax.all_gather(parts[0], "wide", axis=0, tiled=True),
            lax.all_gather(parts[1], "wide", axis=0, tiled=True),
            lax.all_gather(parts[2], "wide", axis=0, tiled=True),
            lax.all_gather(parts[3], "wide", axis=1, tiled=True),
            lax.all_gather(embed.astype(jnp.bfloat16), "wide", axis=1, tiled=True),
        )

    qo_w, kv_w, ffn_w, gain_low, table = fetch()
    gain_w = gain_low.astype(jnp.float32)
    local_ids = token_ids - narrow_spot * vocab_rows
    inside = (local_ids >= 0) & (local_ids < vocab_rows)
    clipped = jnp.clip(local_ids, 0, vocab_rows - 1)
    picked_rows = jnp.where(
        inside[:, None], jnp.take(table, clipped, axis=0).astype(jnp.float32), 0.0
    )
    start_h = lax.psum_scatter(
        picked_rows.astype(jnp.bfloat16), "narrow", scatter_dimension=0, tiled=True
    ).astype(jnp.float32)
    layer_h, kept = layer_forward(
        start_h, qo_w, kv_w, ffn_w, gain_w, cosine, sine, seg_all, seg_mine, start
    )
    final_h = jnp.where(keep_layer > 0, layer_h, start_h)
    exits = jnp.stack([norm_rows(start_h, gain_w[2]), norm_rows(final_h, gain_w[2])]).astype(
        jnp.bfloat16
    )
    exit_all = lax.all_gather(exits, "narrow", axis=1, tiled=True)
    chosen = jnp.take(exit_all, pick_ids, axis=1)
    sel_rows = pick_ids.shape[0]
    logits = jnp.einsum("esd,vd->esv", chosen, table, preferred_element_type=jnp.float32)
    local_target = target_ids - narrow_spot * vocab_rows
    has_target = (local_target >= 0) & (local_target < vocab_rows)
    target_clip = jnp.clip(local_target, 0, vocab_rows - 1)
    row_peak = jnp.max(logits, axis=-1)
    row_sum = jnp.sum(jnp.exp(logits - row_peak[..., None]), axis=-1)
    index_grid = jnp.broadcast_to(target_clip[None, :, None], (2, sel_rows, 1))
    picked = jnp.where(
        has_target[None, :], jnp.take_along_axis(logits, index_grid, axis=2)[..., 0], 0.0
    )
    peak_all, sum_all, picked_all = combined_all((row_peak, row_sum, picked), "narrow", merge_stats)
    log_norm = peak_all + jnp.log(sum_all)
    counted = (target_ids >= 0).astype(jnp.float32)
    exit_scale = jnp.array([EXIT_EARLY, EXIT_LAST], jnp.float32)[:, None]
    per_pick = jnp.sum(exit_scale * (log_norm - picked_all), axis=0) * counted
    owned = ((pick_ids >= start) & (pick_ids < start + tok_rows)).astype(jnp.float32)
    loss_part = jnp.sum(per_pick * owned)
    count_part = jnp.sum(counted * owned)
    one_hot = (
        (jnp.arange(vocab_rows, dtype=jnp.int32)[None, :] == target_clip[:, None])
        & has_target[:, None]
    ).astype(jnp.float32)
    grad_logits = (
        (jnp.exp(logits - log_norm[..., None]) - one_hot[None])
        * (exit_scale * counted[None, :])[..., None]
    ).astype(jnp.bfloat16)
    grad_chosen = jnp.einsum("esv,vd->esd", grad_logits, table, preferred_element_type=jnp.float32)
    grad_table = jnp.einsum("esv,esd->vd", grad_logits, chosen, preferred_element_type=jnp.float32)
    grad_exit = (
        jnp.zeros((2, seq_len, grad_chosen.shape[2]), jnp.float32).at[:, pick_ids].add(grad_chosen)
    )
    grad_exit_mine = lax.psum_scatter(grad_exit, "narrow", scatter_dimension=1, tiled=True)
    grad_start_exit, gain_early = norm_back(start_h, gain_w[2], grad_exit_mine[0])
    grad_final, gain_late = norm_back(final_h, gain_w[2], grad_exit_mine[1])
    qo_w, kv_w, ffn_w, gain_again, table_again = fetch()
    grad_layer = grad_final * keep_layer
    grad_start_layer, grad_qo, grad_kv, grad_ffn, gain_attn, gain_mid = layer_backward(
        grad_layer,
        start_h,
        qo_w,
        kv_w,
        ffn_w,
        gain_w,
        cosine,
        sine,
        seg_all,
        seg_mine,
        start,
        kept,
        ffn_by_rows,
    )
    grad_start = grad_start_exit + grad_start_layer + grad_final * (1.0 - keep_layer)
    grad_rows_all = lax.all_gather(grad_start, "narrow", axis=0, tiled=True)
    grad_table = grad_table + jax.ops.segment_sum(
        jnp.where(inside[:, None], grad_rows_all, 0.0), clipped, num_segments=vocab_rows
    )
    grad_gain = jnp.stack([gain_attn, gain_mid, gain_early + gain_late])
    wide_qo, wide_kv, wide_gain, summed_table = (
        lax.psum_scatter(grad_qo, "wide", scatter_dimension=0, tiled=True),
        lax.psum_scatter(grad_kv, "wide", scatter_dimension=0, tiled=True),
        lax.psum_scatter(grad_gain, "wide", scatter_dimension=1, tiled=True),
        lax.psum_scatter(grad_table, "wide", scatter_dimension=1, tiled=True),
    )
    summed_qo, summed_kv, summed_ffn, summed_gain = (
        lax.psum_scatter(wide_qo, "narrow", scatter_dimension=2, tiled=True),
        lax.psum_scatter(wide_kv, "narrow", scatter_dimension=2, tiled=True),
        lax.psum_scatter(grad_ffn, "narrow", scatter_dimension=2, tiled=True),
        lax.psum_scatter(wide_gain, "narrow", scatter_dimension=1, tiled=True),
    )
    squares = (
        jnp.sum(summed_qo * summed_qo)
        + jnp.sum(summed_kv * summed_kv)
        + jnp.sum(summed_ffn * summed_ffn)
    )
    squares = squares + jnp.sum(summed_gain * summed_gain) + jnp.sum(summed_table * summed_table)
    square_total, loss_sum, loss_count = lax.psum(
        (squares, loss_part, count_part), ("wide", "narrow")
    )
    grad_norm = jnp.sqrt(square_total) / loss_count
    factor = jnp.minimum(1.0, CLIP_NORM / (grad_norm + 1e-06)) / loss_count
    embed_new, embed_m_new, embed_v_new = adamw(
        embed, embed_m, embed_v, summed_table * factor, RATE_ADAM, WEIGHT_DECAY
    )
    gains_new, gains_m_new, gains_v_new = adamw(
        gains, gains_m, gains_v, summed_gain * factor, RATE_GAIN, 0.0
    )
    mom_qo = MOMENTUM * attn_qo_mom + summed_qo * factor
    mom_kv = MOMENTUM * attn_kv_mom + summed_kv * factor
    mom_ffn = MOMENTUM * ffn_mom + summed_ffn * factor
    dir_qo, dir_kv, dir_ffn = orthogonalize(
        jnp.moveaxis(mom_qo, 1, 0), jnp.moveaxis(mom_kv, 1, 0), jnp.moveaxis(mom_ffn, 1, 0)
    )
    shrink = 1.0 - RATE_MUON * WEIGHT_DECAY
    qo_new = attn_qo * shrink - RATE_MUON * jnp.moveaxis(dir_qo, 0, 1)
    kv_new = attn_kv * shrink - RATE_MUON * jnp.moveaxis(dir_kv, 0, 1)
    ffn_new = ffn * shrink - RATE_MUON * jnp.moveaxis(dir_ffn, 0, 1)
    return (
        loss_sum,
        loss_count,
        grad_norm,
        embed_new,
        embed_m_new,
        embed_v_new,
        qo_new,
        mom_qo,
        kv_new,
        mom_kv,
        ffn_new,
        mom_ffn,
        gains_new,
        gains_m_new,
        gains_v_new,
    )


def solution(mesh):
    return jax.shard_map(
        per_device,
        mesh=mesh,
        in_specs=(
            P("wide", None),
            P("wide", None),
            P("wide", None),
            P("wide", None),
            P("wide"),
            P("narrow", "wide"),
            P("narrow", "wide"),
            P("narrow", "wide"),
            P("wide", None, "narrow"),
            P("wide", None, "narrow"),
            P("wide", None, "narrow"),
            P("wide", None, "narrow"),
            P("wide", None, "narrow"),
            P("wide", None, "narrow"),
            P(None, ("wide", "narrow")),
            P(None, ("wide", "narrow")),
            P(None, ("wide", "narrow")),
        ),
        out_specs=(
            P(),
            P(),
            P(),
            P("narrow", "wide"),
            P("narrow", "wide"),
            P("narrow", "wide"),
            P("wide", None, "narrow"),
            P("wide", None, "narrow"),
            P("wide", None, "narrow"),
            P("wide", None, "narrow"),
            P("wide", None, "narrow"),
            P("wide", None, "narrow"),
            P(None, ("wide", "narrow")),
            P(None, ("wide", "narrow")),
            P(None, ("wide", "narrow")),
        ),
        check_vma=False,
    )
```

profile of v0, /device:TPU:17, one launch (start us, length us, event | category | flops | bytes accessed | tf_op | source)
XLA Modules:
  0.0 5538.4 jit_solution(8379553267589499721)
XLA Ops:
  16.0 166.2 %all-gather.16.cloned.1.call-done = bf16[8192,2048]{1,0:T(8,128)(2,1)} async-done(((bf16[8192,256]{1,0:T(8,128)(2,1)}), bf16[8192,2048]{1,0:T(8,128)(2,1)}) %all-gather.16.cloned.1.call-update) | async-done | bytes 33554448 | tf_op jit(solution)/shard_map/all_gather | solution.py:374
  182.1 40.9 gather_fusion
  227.6 46.0 all_gather.64
  284.8 15.1 all_gather.63
  300.8 36.4 reduce-scatter.20.cloned.1.call-done
  338.8 37.6 all-gather.18.cloned.1.call-done
  388.0 142.2 %all-gather.28.cloned.1.call-done = bf16[704,3,2048]{2,0,1:T(8,128)(2,1)} async-done(((bf16[704,3,512]{2,0,1:T(8,128)(2,1)}), bf16[704,3,2048]{2,0,1:T(8,128)(2,1)}) %all-gather.28.cloned.1.call-update) | async-done | bytes 8650768 | tf_op jit(solution)/shard_map/all_gather | solution.py:366
  531.8 90.6 %all-gather.26.cloned.1.call-done = bf16[2048,2,2048]{2,0,1:T(8,128)(2,1)} async-done(((bf16[256,2,2048]{2,0,1:T(8,128)(2,1)}), bf16[2048,2,2048]{2,0,1:T(8,128)(2,1)}) %all-gather.26.cloned.1.call-update) | async-done | bytes 16777232 | tf_op jit(solution)/shard_map/all_gather | solution.py:370
  630.8 12.3 copy.187
  655.1 26.1 all-gather.22.cloned.1.call-done
  690.1 12.9 fusion.15
  703.0 10.6 fusion.125
  720.2 276.6 %all-gather.30.cloned.1.call-done = bf16[5632,3,2048]{2,0,1:T(8,128)(2,1)} async-done(((bf16[704,3,2048]{2,0,1:T(8,128)(2,1)}), bf16[5632,3,2048]{2,0,1:T(8,128)(2,1)}) %all-gather.30.cloned.1.call-update) | async-done | bytes 69206032 | tf_op jit(solution)/shard_map/all_gather | solution.py:372
  996.7 22.2 fusion.17
  1018.9 14.9 multiply_reduce_fusion.6
  1038.8 144.6 %all-gather.32.cloned.1.call-done = bf16[2,1024,2048]{2,1,0:T(8,128)(2,1)} async-done(((bf16[2,256,2048]{2,1,0:T(8,128)(2,1)}), bf16[2,1024,2048]{2,1,0:T(8,128)(2,1)}) %all-gather.32.cloned.1.call-update) | async-done | bytes 8388624 | tf_op jit(solution)/shard_map/all_gather | solution.py:395
  1183.4 16.6 copy.193
  1210.2 19.2 fusion.247
  1264.0 16.7 fusion.96
  1292.7 21.0 scatter_fusion
  1313.7 17.7 copy.196
  1332.1 287.6 %reduce-scatter.22.cloned.1.call-done = f32[2,256,2048]{2,1,0:T(8,128)} async-done(((f32[2,1024,2048]{2,1,0:T(8,128)}), f32[2,256,2048]{2,1,0:T(8,128)}) %reduce-scatter.22.cloned.1.call-update) | async-done | bytes 4194320 | tf_op jit(solution)/shard_map/reduce_scatter | solution.py:429
  1624.3 18.1 fusion.92
  1642.4 21.9 multiply_reduce_fusion.3
  1675.1 16.5 fusion.12
  1691.6 10.4 fusion.14
  1733.3 19.5 reduce-scatter.28.cloned.1.call-done
  1756.9 41.7 reduce-scatter.30.cloned.1.call-done
  1824.2 18.7 pad_maximum_fusion.1
  1850.2 23.7 convolution_bitcast_fusion.2
  1873.9 36.6 convolution_bitcast_fusion
  1910.5 100.5 %pad_maximum_fusion = f32[5632,3,2048]{0,2,1:T(8,128)} fusion(f32[5632,1,2048]{0,2,1:T(8,128)} %convolution_bitcast_fusion.2, f32[5632,2,2048]{0,2,1:T(8,128)} %convolution_bitcast_fusion), kind=kLoop, calls=%fused_computation.12 | loop fusion | flops 34603008 | bytes 276824064 | tf_op jit(solution)/shard_map/concatenate | solution.py:185
  2011.0 135.5 %copy.244 = f32[5632,6144]{1,0:T(8,128)} copy(f32[5632,6144]{0,1:T(8,128)} %bitcast.127) | data formatting | bytes 276824064
  2148.6 25.7 convolution_bitcast_fusion.1
  2174.3 99.7 %all-gather.34.cloned.1.call-done = f32[1024,2048]{1,0:T(8,128)} async-done(((f32[256,2048]{1,0:T(8,128)}), f32[1024,2048]{1,0:T(8,128)}) %all-gather.34.cloned.1.call-update) | async-done | bytes 8388624 | tf_op jit(solution)/shard_map/all_gather | solution.py:450
  2281.4 198.3 %scatter_fusion.1 = f32[8192,2048]{1,0:T(8,128)} fusion(f32[8192,2048]{1,0:T(8,128)} %convolution_bitcast_fusion.1, s32[1024]{0:T(1024)S(1)} %bitcast.560, f32[1024,2048]{1,0:T(8,128)} %broadcast_select_fusion), kind=kCustom, calls=%fused_computation.4 | custom fusion | flops 2097152 | bytes 25169920 | tf_op jit(solution)/shard_map/scatter-add | solution.py:451
  2479.8 559.8 %reduce-scatter.40.cloned.1.call-done = f32[704,6144]{1,0:T(8,128)} async-done(((f32[5632,6144]{1,0:T(8,128)}), f32[704,6144]{1,0:T(8,128)}) %reduce-scatter.40.cloned.1.call-update) | async-done | bytes 17301520
  3039.5 18.1 copy.245
  3057.7 18.2 copy.206
  3088.9 78.0 %reduce-scatter.26.cloned.1.call-done = f32[256,2,512]{2,0,1:T(8,128)} async-done(((f32[256,2,2048]{2,0,1:T(8,128)}), f32[256,2,512]{2,0,1:T(8,128)}) %reduce-scatter.26.cloned.1.call-update) | async-done | bytes 1048592 | tf_op jit(solution)/shard_map/reduce_scatter | solution.py:462
  3170.3 384.2 %reduce-scatter.38.cloned.1.call-done = f32[8192,256]{1,0:T(8,128)} async-done(((f32[8192,2048]{1,0:T(8,128)}), f32[8192,256]{1,0:T(8,128)}) %reduce-scatter.38.cloned.1.call-update) | async-done | bytes 8388624 | tf_op jit(solution)/shard_map/reduce_scatter | solution.py:459
  3560.7 285.8 %reduce-scatter.36.cloned.1.call-done = f32[704,3,512]{2,0,1:T(8,128)} async-done(((f32[704,3,2048]{2,0,1:T(8,128)}), f32[704,3,512]{2,0,1:T(8,128)}) %reduce-scatter.36.cloned.1.call-update) | async-done | bytes 4325392 | tf_op jit(solution)/shard_map/reduce_scatter | solution.py:464
  3852.4 38.8 all-reduce
  3903.4 13.6 fusion.68
  3917.7 263.7 %all-reduce.20.cloned.1.call-done = (f32[2,256,256]{2,1,0:T(8,128)}, f32[2,256,256]{2,1,0:T(8,128)}, f32[3,704,704]{2,1,0:T(8,128)}) async-done(((f32[2,256,256]{2,1,0:T(8,128)}, f32[2,256,256]{2,1,0:T(8,128)}, f32[3,704,704]{2,1,0:T(8,128)}), (f32[2,256,256]{2,1,0:T(8,128)}, f32[2,256,256]{2,1,0:T(8,128)}, f32[3,704,704]{2,1,0:T(8,128)})) %all-reduce.20.cloned.1.call-update) | async-done | bytes 6995984 | tf_op jit(solution)/shard_map/psum | solution.py:295
  4194.4 19.3 fusion.61
  4213.7 16.3 multiply_add_fusion.4
  4232.0 13.6 fusion.254
  4246.2 262.3 %all-reduce.18.cloned.1.call-done = (f32[2,256,256]{2,1,0:T(8,128)}, f32[2,256,256]{2,1,0:T(8,128)}, f32[3,704,704]{2,1,0:T(8,128)}) async-done(((f32[2,256,256]{2,1,0:T(8,128)}, f32[2,256,256]{2,1,0:T(8,128)}, f32[3,704,704]{2,1,0:T(8,128)}), (f32[2,256,256]{2,1,0:T(8,128)}, f32[2,256,256]{2,1,0:T(8,128)}, f32[3,704,704]{2,1,0:T(8,128)})) %all-reduce.18.cloned.1.call-update) | async-done | bytes 6995984 | tf_op jit(solution)/shard_map/psum | solution.py:295
  4519.8 19.8 fusion.255
  4539.6 16.3 multiply_add_fusion.3
  4558.0 13.6 fusion.256
  4571.9 262.5 %all-reduce.16.cloned.1.call-done = (f32[2,256,256]{2,1,0:T(8,128)}, f32[2,256,256]{2,1,0:T(8,128)}, f32[3,704,704]{2,1,0:T(8,128)}) async-done(((f32[2,256,256]{2,1,0:T(8,128)}, f32[2,256,256]{2,1,0:T(8,128)}, f32[3,704,704]{2,1,0:T(8,128)}), (f32[2,256,256]{2,1,0:T(8,128)}, f32[2,256,256]{2,1,0:T(8,128)}, f32[3,704,704]{2,1,0:T(8,128)})) %all-reduce.16.cloned.1.call-update) | async-done | bytes 6995984 | tf_op jit(solution)/shard_map/psum | solution.py:295
  4842.7 19.8 fusion.257
  4862.5 14.1 fusion.38
  4878.7 13.3 fusion.236
  4892.2 262.5 %all-reduce.14.cloned.1.call-done = (f32[2,256,256]{2,1,0:T(8,128)}, f32[2,256,256]{2,1,0:T(8,128)}, f32[3,704,704]{2,1,0:T(8,128)}) async-done(((f32[2,256,256]{2,1,0:T(8,128)}, f32[2,256,256]{2,1,0:T(8,128)}, f32[3,704,704]{2,1,0:T(8,128)}), (f32[2,256,256]{2,1,0:T(8,128)}, f32[2,256,256]{2,1,0:T(8,128)}, f32[3,704,704]{2,1,0:T(8,128)})) %all-reduce.14.cloned.1.call-update) | async-done | bytes 6995984 | tf_op jit(solution)/shard_map/psum | solution.py:295
  5163.3 19.3 fusion.258
  5182.6 14.1 fusion.34
  5198.8 14.1 fusion.107
  5217.1 23.9 multiply_subtract_fusion
  5241.0 234.6 %all-reduce.12.cloned.1.call-done = (f32[2,256,256]{2,1,0:T(8,128)}, f32[2,256,256]{2,1,0:T(8,128)}, f32[3,704,704]{2,1,0:T(8,128)}) async-done(((f32[2,256,256]{2,1,0:T(8,128)}, f32[2,256,256]{2,1,0:T(8,128)}, f32[3,704,704]{2,1,0:T(8,128)}), (f32[2,256,256]{2,1,0:T(8,128)}, f32[2,256,256]{2,1,0:T(8,128)}, f32[3,704,704]{2,1,0:T(8,128)})) %all-reduce.12.cloned.1.call-update) | async-done | bytes 6995984 | tf_op jit(solution)/shard_map/psum | solution.py:295
  5486.5 19.4 fusion.259
  5505.9 24.3 fusion.63
  (444 shorter events, 331.1 us)
Async XLA Ops:
  7.2 175.0 %all-gather.16.cloned.1.call-start = ((), (), s32[]{:S(2)}) async-start(), calls=%async_computation.13 | async-start | bytes 37748736 | tf_op jit(solution)/shard_map/all_gather | solution.py:374
  13.1 264.7 %all-gather.24.cloned.1.call-start = ((), (), s32[]{:S(2)}) async-start(), calls=%async_computation.18 | async-start | bytes 2621440 | tf_op jit(solution)/shard_map/all_gather | solution.py:364
  15.2 322.0 %reduce-scatter.20.cloned.1.call-start = ((), (), s32[]{:S(2)}) async-start(), calls=%async_computation.14 | async-start | bytes 5242880 | tf_op jit(solution)/shard_map/reduce_scatter | solution.py:385
  15.3 207.7 %copy-start.66 = (pred[1024]{0:T(1024)(128)(4,1)}, pred[1024]{0:T(1024)(128)(4,1)S(1)}, u32[]{:S(2)}) copy-start(pred[1024]{0:T(1024)(128)(4,1)S(1)} %and_reduce_fusion) | copy-start | bytes 3076
  227.5 148.8 %all-gather.18.cloned.1.call-start = ((), (), s32[]{:S(2)}) async-start(), calls=%async_computation.15 | async-start | bytes 4718592 | tf_op jit(solution)/shard_map/all_gather | solution.py:371
  273.7 256.5 %all-gather.28.cloned.1.call-start = ((), (), s32[]{:S(2)}) async-start(), calls=%async_computation.20 | async-start | bytes 10813440 | tf_op jit(solution)/shard_map/all_gather | solution.py:366
  277.7 344.7 %all-gather.26.cloned.1.call-start = ((), (), s32[]{:S(2)}) async-start(), calls=%async_computation.19 | async-start | bytes 18874368 | tf_op jit(solution)/shard_map/all_gather | solution.py:370
  278.2 374.3 %all-gather.20.cloned.1.call-start = ((), (), s32[]{:S(2)}) async-start(), calls=%async_computation.16 | async-start | bytes 1310720 | tf_op jit(solution)/shard_map/all_gather | solution.py:126
  300.8 342.3 %copy-start.51 = (f32[1,2048]{1,0:T(1,128)}, f32[1,2048]{1,0:T(1,128)S(1)}, u32[]{:S(2)}) copy-start(f32[1,2048]{1,0:T(1,128)S(1)} %get-tuple-element.333) | copy-start | bytes 24580
  338.7 41.1 copy-start.68
  379.8 301.4 %all-gather.22.cloned.1.call-start = ((), (), s32[]{:S(2)}) async-start(), calls=%async_computation.17 | async-start | bytes 1310720 | tf_op jit(solution)/shard_map/all_gather | solution.py:125
  380.2 268.8 %copy-start.39 = (f32[256,64]{0,1:T(8,128)}, f32[256,64]{0,1:T(8,128)S(1)}, u32[]{:S(2)}) copy-start(f32[256,64]{0,1:T(8,128)S(1)} %get-tuple-element.329) | copy-start | bytes 196612
  380.2 268.8 %copy-start.41 = (f32[256,64]{0,1:T(8,128)}, f32[256,64]{0,1:T(8,128)S(1)}, u32[]{:S(2)}) copy-start(f32[256,64]{0,1:T(8,128)S(1)} %get-tuple-element.330) | copy-start | bytes 196612
  387.9 608.8 %all-gather.30.cloned.1.call-start = ((), (), s32[]{:S(2)}) async-start(), calls=%async_computation.21 | async-start | bytes 77856768 | tf_op jit(solution)/shard_map/all_gather | solution.py:372
  530.2 653.2 %all-gather.32.cloned.1.call-start = ((), (), s32[]{:S(2)}) async-start(), calls=%async_computation.22 | async-start | bytes 10485760 | tf_op jit(solution)/shard_map/all_gather | solution.py:395
  650.6 39.5 copy-start.18
  652.5 37.6 copy-start.20
  713.6 283.1 %copy-start.55 = (f32[1,2048]{1,0:T(1,128)S(1)}, f32[1,2048]{1,0:T(1,128)}, u32[]{:S(2)}) copy-start(f32[1,2048]{1,0:T(1,128)} %get-tuple-element.332) | copy-start | bytes 24580
  720.1 276.6 %copy-start.15 = (f32[256,2048]{1,0:T(8,128)}, f32[256,2048]{1,0:T(8,128)S(1)}, u32[]{:S(2)}) copy-start(f32[256,2048]{1,0:T(8,128)S(1)} %get-tuple-element.342) | copy-start | bytes 6291460
  720.1 298.8 %copy-start.75 = (f32[256]{0:T(256)}, f32[256]{0:T(256)S(1)}, u32[]{:S(2)}) copy-start(f32[256]{0:T(256)S(1)} %get-tuple-element.341) | copy-start | bytes 3076
  720.1 944.2 %copy-start.59 = (f32[256]{0:T(256)}, f32[256]{0:T(256)S(1)}, u32[]{:S(2)}) copy-start(f32[256]{0:T(256)S(1)} %fusion.204) | copy-start | bytes 3076
  1035.9 583.8 %reduce-scatter.22.cloned.1.call-start = ((), (), s32[]{:S(2)}) async-start(), calls=%async_computation.23 | async-start | bytes 20971520 | tf_op jit(solution)/shard_map/reduce_scatter | solution.py:429
  1233.7 24.1 copy-start.83
  1331.4 421.3 %reduce-scatter.28.cloned.1.call-start = ((), (), s32[]{:S(2)}) async-start(), calls=%async_computation.26 | async-start | bytes 2621440 | tf_op jit(solution)/shard_map/reduce_scatter | solution.py:238
  1624.3 40.0 copy-start.8
  1642.4 21.9 copy-start.76
  1709.6 88.9 %reduce-scatter.30.cloned.1.call-start = ((), (), s32[]{:S(2)}) async-start(), calls=%async_computation.27 | async-start | bytes 2621440 | tf_op jit(solution)/shard_map/reduce_scatter | solution.py:241
  1719.8 426.7 %reduce-scatter.42.cloned.1.call-start = ((), (), s32[]{:S(2)}) async-start(), calls=%async_computation.34 | async-start | bytes 1179648
  1733.3 65.3 %copy-start.52 = (f32[1,2048]{1,0:T(1,128)S(1)}, f32[1,2048]{1,0:T(1,128)}, u32[]{:S(2)}) copy-start(f32[1,2048]{1,0:T(1,128)} %copy-done.51) | copy-start | bytes 24580
  1756.8 46.0 copy-start.70
  1804.3 343.0 %reduce-scatter.32.cloned.1.call-start = ((), (), s32[]{:S(2)}) async-start(), calls=%async_computation.28 | async-start | bytes 9437184 | tf_op jit(solution)/shard_map/reduce_scatter | solution.py:457
  1811.9 335.9 %reduce-scatter.24.cloned.1.call-start = ((), (), s32[]{:S(2)}) async-start(), calls=%async_computation.24 | async-start | bytes 37748736 | tf_op jit(solution)/shard_map/reduce_scatter | solution.py:456
  1842.9 431.1 %all-gather.34.cloned.1.call-start = ((), (), s32[]{:S(2)}) async-start(), calls=%async_computation.31 | async-start | bytes 10485760 | tf_op jit(solution)/shard_map/all_gather | solution.py:450
  1849.9 23.9 copy-start.60
  1850.0 1189.6 %reduce-scatter.40.cloned.1.call-start = ((), (), s32[]{:S(2)}) async-start(), calls=%async_computation.33 | async-start | bytes 155713536
  2146.5 930.7 %reduce-scatter.44.cloned.1.call-start = ((), (), s32[]{:S(2)}) async-start(), calls=%async_computation.35 | async-start | bytes 163840
  2147.2 940.1 %reduce-scatter.34.cloned.1.call-start = ((), (), s32[]{:S(2)}) async-start(), calls=%async_computation.29 | async-start | bytes 1310720 | tf_op jit(solution)/shard_map/reduce_scatter | solution.py:463
  2147.8 1019.1 %reduce-scatter.26.cloned.1.call-start = ((), (), s32[]{:S(2)}) async-start(), calls=%async_computation.25 | async-start | bytes 5242880 | tf_op jit(solution)/shard_map/reduce_scatter | solution.py:462
  2148.5 125.5 %copy-start.67 = (pred[1024]{0:T(1024)(128)(4,1)S(1)}, pred[1024]{0:T(1024)(128)(4,1)}, u32[]{:S(2)}) copy-start(pred[1024]{0:T(1024)(128)(4,1)} %copy-done.66) | copy-start | bytes 3076
  2148.5 1406.0 %reduce-scatter.38.cloned.1.call-start = ((), (), s32[]{:S(2)}) async-start(), calls=%async_computation.32 | async-start | bytes 75497472 | tf_op jit(solution)/shard_map/reduce_scatter | solution.py:459
  2174.3 107.1 %copy-start.62 = (s32[1,1024]{1,0:T(1,128)S(1)}, s32[1,1024]{1,0:T(1,128)}, u32[]{:S(2)}) copy-start(s32[1,1024]{1,0:T(1,128)} %copy-done.61) | copy-start | bytes 12292
  2479.7 1366.8 %reduce-scatter.36.cloned.1.call-start = ((), (), s32[]{:S(2)}) async-start(), calls=%async_computation.30 | async-start | bytes 21626880 | tf_op jit(solution)/shard_map/reduce_scatter | solution.py:464
  3075.9 1105.5 %all-reduce.20.cloned.1.call-start = ((), (), s32[]{:S(2)}) async-start(), calls=%async_computation.40 | async-start | bytes 15073280 | tf_op jit(solution)/shard_map/psum | solution.py:295
  3170.3 723.1 %copy-start.32 = (f32[256,2,512]{2,0,1:T(8,128)S(1)}, f32[256,2,512]{2,0,1:T(8,128)}, u32[]{:S(2)}) copy-start(f32[256,2,512]{2,0,1:T(8,128)} %reduce-scatter.26.cloned.1.call-done) | copy-start | bytes 3145732
  3170.3 723.1 %copy-start.45 = (f32[256,2,512]{2,1,0:T(2,128)S(1)}, f32[256,2,512]{2,1,0:T(2,128)}, u32[]{:S(2)}) copy-start(f32[256,2,512]{2,1,0:T(2,128)} %param.29) | copy-start | bytes 3145732
  3560.7 335.0 %copy-start.46 = (f32[256,2,128]{2,0,1:T(8,128)S(1)}, f32[256,2,128]{2,0,1:T(8,128)}, u32[]{:S(2)}) copy-start(f32[256,2,128]{2,0,1:T(8,128)} %reduce-scatter.34.cloned.1.call-done) | copy-start | bytes 786436
  3896.6 290.8 %copy-start.23 = (f32[256,2,128]{2,0,1:T(8,128)}, f32[256,2,128]{2,0,1:T(8,128)S(1)}, u32[]{:S(2)}) copy-start(f32[256,2,128]{2,0,1:T(8,128)S(1)} %fusion.181) | copy-start | bytes 786436
  3917.0 591.4 %all-reduce.18.cloned.1.call-start = ((), (), s32[]{:S(2)}) async-start(), calls=%async_computation.39 | async-start | bytes 15073280 | tf_op jit(solution)/shard_map/psum | solution.py:295
  4192.4 21.3 slice-start.14
  4194.4 19.3 slice-start.15
  4245.7 588.8 %all-reduce.16.cloned.1.call-start = ((), (), s32[]{:S(2)}) async-start(), calls=%async_computation.38 | async-start | bytes 15073280 | tf_op jit(solution)/shard_map/psum | solution.py:295
  4517.8 21.8 slice-start.12
  4519.8 19.8 slice-start.13
  4571.7 583.1 %all-reduce.14.cloned.1.call-start = ((), (), s32[]{:S(2)}) async-start(), calls=%async_computation.37 | async-start | bytes 15073280 | tf_op jit(solution)/shard_map/psum | solution.py:295
  4841.3 21.2 copy-start.25
  4841.3 21.2 slice-start.4
  4842.7 19.8 slice-start.5
  4892.0 583.6 %all-reduce.12.cloned.1.call-start = ((), (), s32[]{:S(2)}) async-start(), calls=%async_computation.36 | async-start | bytes 15073280 | tf_op jit(solution)/shard_map/psum | solution.py:295
  5161.8 20.8 slice-start.6
  5161.8 20.8 slice-start.10
  5163.3 19.3 slice-start.7
  5163.3 19.3 slice-start.11
  5484.9 21.0 slice-start.8
  5486.5 19.4 slice-start.9
  (71 other events, 427.1 us)
Sparse Core Ops, SparseCore 0:
  13.2 168.9 all-gather.15
  184.3 44.1 all-gather.23
  231.3 105.8 reduce-scatter.19
  339.1 37.1 all-gather.17
  378.4 151.6 all-gather.27
  532.1 90.2 all-gather.25
  624.6 27.0 all-gather.19
  653.9 27.2 all-gather.21
  683.3 313.4 all-gather.29
  1036.0 147.3 all-gather.31
  1331.5 288.1 reduce-scatter.21
  1709.7 42.9 reduce-scatter.27
  1755.1 43.3 reduce-scatter.29
  1804.4 35.8 reduce-scatter.41
  1844.2 71.3 reduce-scatter.31
  1919.4 205.1 reduce-scatter.23
  2126.1 147.8 all-gather.33
  2277.5 762.0 reduce-scatter.39
  3041.8 15.0 reduce-scatter.43
  3059.2 28.0 reduce-scatter.33
  3089.6 77.2 reduce-scatter.25
  3170.9 383.6 reduce-scatter.37
  3556.9 289.5 reduce-scatter.35
  3917.2 264.1 all-reduce.19
  4245.8 262.6 all-reduce.17
  4571.8 262.5 all-reduce.15
  4892.1 262.6 all-reduce.13
  5213.0 262.6 all-reduce.11
where the time goes:
time: 5560 us; the launch traced here: 5540 us
  waiting for transfers between devices  3970 us (71%)
  matrix products  609 us (11%)
  other arithmetic  474 us (9%)
  local copies, waits for them, and re-layouts  329 us (6%)
  blocking collectives  125 us (2%)
    psum x5, waiting for transfers between devices, orthogonalize(): lax.psum((gram_of(current[0]), gram_of(current[1]), gram_of(current[2])),...  1290 us
    unnamed x31, waiting for transfers between devices  563 us
    reduce_scatter x1, waiting for transfers between devices, per_device(): lax.psum_scatter(grad_table, 'wide', scatter_dimension=1, tiled=True)  384 us
    reduce_scatter x1, waiting for transfers between devices, per_device(): lax.psum_scatter(grad_exit, 'narrow', scatter_dimension=1, tiled=True)  288 us
    reduce_scatter x1, waiting for transfers between devices, per_device(): lax.psum_scatter(grad_ffn, 'narrow', scatter_dimension=2, tiled=True)  286 us
    all_gather x1, waiting for transfers between devices, fetch(): lax.all_gather(parts[2], 'wide', axis=0, tiled=True)  277 us
    scatter-add x1, other arithmetic, per_device(): jax.ops.segment_sum(jnp.where(inside[:, None], grad_rows_all, 0.0), clipp...  198 us
    unnamed x227, local copies, waits for them, and re-layouts  180 us
  transfers between devices with their start and end apart: 28, of which 22 were waited for; matrix products, arithmetic and copies ran while one was open for 15% of the time, Pallas kernels for 0%

commit v1 on v0

v1 whole, which is shorter than its diff:
```python
import functools

import jax
import jax.numpy as jnp
from jax import lax
from jax.experimental import pallas as pl
from jax.experimental.pallas import tpu as pltpu
from jax.sharding import PartitionSpec as P

HEADS = 16
HD = 128
KVH = 4
NS_STEPS = 5
STEP = 10


NORM_EPS = 1e-05
ROPE_BASE = 10000.0
EXIT_EARLY = 0.25
EXIT_LAST = 1.0
CLIP_NORM = 0.02
BETA_ONE = 0.9
BETA_TWO = 0.95
ADAM_EPS = 1e-08
RATE_ADAM = 0.02
RATE_GAIN = 0.3
RATE_MUON = 0.3
WEIGHT_DECAY = 0.1
MOMENTUM = 0.95
NEWTON_A = 3.4445
NEWTON_B = -4.775
NEWTON_C = 2.0315
MASKED = -1e30
LOW = jnp.bfloat16
FULL = jnp.float32
BOTH = ("wide", "narrow")
ROWS_IN_BLOCK = 1024
UNROLL = 16
VMEM_BYTES = 56 * 1024 * 1024


def dot(first, second, first_dim, second_dim):
    return lax.dot_general(
        first, second, (((first_dim,), (second_dim,)), ((), ())), preferred_element_type=FULL
    )


def norm_rows(values, gain_row):
    return (
        values * lax.rsqrt(jnp.mean(values * values, axis=-1, keepdims=True) + NORM_EPS) * gain_row
    )


def norm_back(values, gain_row, grad):
    output, pull = jax.vjp(norm_rows, values, gain_row)
    return pull(grad)


def segments_at(lens, where_at):
    ends = jnp.cumsum(lens)
    return jnp.sum((where_at[:, None] >= ends[None, :]).astype(jnp.int32), axis=1)


def angles_at(lens, where_at):
    segment = segments_at(lens, where_at)
    starts = jnp.cumsum(lens) - lens
    member = segment[:, None] == jnp.arange(lens.shape[0], dtype=jnp.int32)[None, :]
    begin = jnp.sum(jnp.where(member, starts[None, :], 0), axis=1)
    offset_pos = (where_at - begin).astype(FULL)
    inverse = ROPE_BASE ** (-2.0 * jnp.arange(HD // 2, dtype=FULL) / HD)
    angle = offset_pos[:, None] * inverse[None, :]
    return (segment, jnp.cos(angle), jnp.sin(angle))


def rotate(values, cosine, sine):
    half = values.shape[-1] // 2
    first, second = (values[..., :half], values[..., half:])
    return jnp.concatenate(
        [first * cosine - second * sine, second * cosine + first * sine], axis=-1
    )


def unrotate(values, cosine, sine):
    return rotate(values, cosine, -sine)


def lookup_body(ids_ref, table_ref, out_ref, held, rows, sem):
    block = pl.program_id(0)
    vocab = table_ref.shape[0]

    @pl.when(block == 0)
    def _():
        load = pltpu.make_async_copy(table_ref, held.at[pl.ds(0, vocab)], sem)
        load.start()
        held[pl.ds(vocab, 8), :] = jnp.zeros((8, held.shape[1]), FULL)
        load.wait()

    def step(group, carry):
        for member in range(UNROLL):
            at = group * UNROLL + member
            spot = ids_ref[block * ROWS_IN_BLOCK + at]
            rows[pl.ds(at, 1), :] = held[pl.ds(spot, 1), :]
        return carry

    lax.fori_loop(0, ROWS_IN_BLOCK // UNROLL, step, 0)
    out_ref[...] = rows[...].astype(LOW)


def lookup(table, ids):
    vocab, columns = table.shape
    count = ids.shape[0]
    return pl.pallas_call(
        lookup_body,
        grid_spec=pltpu.PrefetchScalarGridSpec(
            num_scalar_prefetch=1,
            grid=(count // ROWS_IN_BLOCK,),
            in_specs=[pl.BlockSpec(memory_space=pl.ANY)],
            out_specs=pl.BlockSpec((ROWS_IN_BLOCK, columns), lambda block, ids_ref: (block, 0)),
            scratch_shapes=[
                pltpu.VMEM((vocab + 8, columns), FULL),
                pltpu.VMEM((ROWS_IN_BLOCK, columns), FULL),
                pltpu.SemaphoreType.DMA,
            ],
        ),
        out_shape=jax.ShapeDtypeStruct((count, columns), LOW),
        compiler_params=pltpu.CompilerParams(vmem_limit_bytes=VMEM_BYTES),
        cost_estimate=pl.CostEstimate(
            flops=0, bytes_accessed=vocab * columns * 4 + count * columns * 32, transcendentals=0
        ),
        name="lookup",
    )(ids, table)


def spread_body(ids_ref, rows_ref, head_ref, out_ref, square_ref, even, odd, rows, sem):
    block = pl.program_id(0)
    vocab = out_ref.shape[0]

    @pl.when(block == 0)
    def _():
        even[...] = jnp.zeros_like(even)
        odd[...] = jnp.zeros_like(odd)

    rows[...] = rows_ref[...].astype(FULL)

    def step(group, carry):
        for member in range(UNROLL):
            at = group * UNROLL + member
            spot = pl.ds(ids_ref[block * ROWS_IN_BLOCK + at], 1)
            total = even if member % 2 == 0 else odd
            total[spot, :] = total[spot, :] + rows[pl.ds(at, 1), :]
        return carry

    lax.fori_loop(0, ROWS_IN_BLOCK // UNROLL, step, 0)

    @pl.when(block == pl.num_programs(0) - 1)
    def _():
        chunk = 256

        def finish(part, squares):
            spot = pl.ds(pl.multiple_of(part * chunk, chunk), chunk)
            value = even[spot, :] + odd[spot, :] + head_ref[spot, :].astype(FULL)
            even[spot, :] = value
            return squares + jnp.sum((value * value).reshape(chunk // 8, 8, -1), axis=0)

        squares = lax.fori_loop(
            0, vocab // chunk, finish, jnp.zeros((8, even.shape[1]), FULL)
        )
        square_ref[...] = squares
        store = pltpu.make_async_copy(even.at[pl.ds(0, vocab)], out_ref, sem)
        store.start()
        store.wait()


def spread(ids, rows, head):
    vocab, columns = head.shape
    count = ids.shape[0]
    return pl.pallas_call(
        spread_body,
        grid_spec=pltpu.PrefetchScalarGridSpec(
            num_scalar_prefetch=1,
            grid=(count // ROWS_IN_BLOCK,),
            in_specs=[
                pl.BlockSpec((ROWS_IN_BLOCK, columns), lambda block, ids_ref: (block, 0)),
                pl.BlockSpec((vocab, columns), lambda block, ids_ref: (0, 0)),
            ],
            out_specs=[
                pl.BlockSpec(memory_space=pl.ANY),
                pl.BlockSpec((8, columns), lambda block, ids_ref: (0, 0)),
            ],
            scratch_shapes=[
                pltpu.VMEM((vocab + 8, columns), FULL),
                pltpu.VMEM((vocab + 8, columns), FULL),
                pltpu.VMEM((ROWS_IN_BLOCK, columns), FULL),
                pltpu.SemaphoreType.DMA,
            ],
        ),
        out_shape=[
            jax.ShapeDtypeStruct((vocab, columns), FULL),
            jax.ShapeDtypeStruct((8, columns), FULL),
        ],
        compiler_params=pltpu.CompilerParams(vmem_limit_bytes=VMEM_BYTES),
        cost_estimate=pl.CostEstimate(
            flops=count * columns, bytes_accessed=count * columns * 64, transcendentals=0
        ),
        name="spread",
    )(ids, rows, head)


def orthogonalize(blocks):
    norm = jnp.sqrt(jnp.sum(blocks * blocks, axis=(1, 2), keepdims=True)) + 1e-07
    current = blocks / norm
    rows = blocks.shape[1]
    eye = jnp.eye(rows, dtype=FULL)[None]

    def centre(gram):
        middle = jnp.sum(gram * eye, axis=(1, 2), keepdims=True) / rows
        return (middle, gram - middle * eye)

    for iteration in range(NS_STEPS):
        low = current.astype(LOW)
        gram = jnp.einsum("jrc,jsc->jrs", low, low, preferred_element_type=FULL)
        middle, rest = centre(gram)
        rest_low = rest.astype(LOW)
        square = jnp.einsum("jrs,jst->jrt", rest_low, rest_low, preferred_element_type=FULL)
        square = square + 2.0 * middle * rest + middle * middle * eye
        middle, rest = centre(NEWTON_B * gram + NEWTON_C * square)
        current = (NEWTON_A + middle) * current + jnp.einsum(
            "jrs,jsc->jrc", rest.astype(LOW), low, preferred_element_type=FULL
        )
    return current


def adamw(weight, first_m, second_m, grad, rate, decay):
    first_new = BETA_ONE * first_m + (1.0 - BETA_ONE) * grad
    second_new = BETA_TWO * second_m + (1.0 - BETA_TWO) * grad * grad
    update = (
        first_new
        / (1.0 - BETA_ONE**STEP)
        / (jnp.sqrt(second_new / (1.0 - BETA_TWO**STEP)) + ADAM_EPS)
    )
    return (weight * (1.0 - rate * decay) - rate * update, first_new, second_new)


def exchange(parts, axis):
    return lax.all_to_all(parts, axis, 0, 0, tiled=True)


def side_by_side(parts):
    count, rows, columns = parts.shape
    return jnp.moveaxis(parts, 0, 1).reshape(rows, count * columns)


def cut_columns(values, count):
    rows, columns = values.shape
    return jnp.moveaxis(values.reshape(rows, count, columns // count), 1, 0)


def gather_rows(values, axis):
    return lax.all_gather(values, axis, axis=0, tiled=True)


def gather_columns(values, axis):
    return lax.all_gather(values, axis, axis=1, tiled=True)


def per_device(
    tokens,
    picks,
    targets,
    lengths,
    skip,
    embed,
    embed_m,
    embed_v,
    attn_qo,
    attn_qo_mom,
    attn_kv,
    attn_kv_mom,
    ffn,
    ffn_mom,
    gains,
    gains_m,
    gains_v,
):
    wide_count = lax.axis_size("wide")
    narrow_count = lax.axis_size("narrow")
    narrow_spot = lax.axis_index("narrow")
    wide_spot = lax.axis_index("wide")
    seq_len = tokens.shape[1]
    sel = picks.shape[1]
    vocab_rows, columns = embed.shape
    width = columns * wide_count
    own_rows = sel // narrow_count
    heads_own = HEADS // narrow_count
    repeat = max(1, narrow_count // KVH)
    ffn_rows = ffn.shape[0]
    lens = lengths[0]
    pick_ids = picks[0]
    keep_layer = (1 - skip[0]).astype(FULL)

    all_ints = gather_rows(
        jnp.concatenate([tokens[0], targets[0]])[None], "wide"
    )
    tokens_all = all_ints[:, :seq_len].reshape(-1)
    targets_all = all_ints[:, seq_len:].reshape(-1)
    gain_w = gather_columns(gains.astype(LOW), BOTH).astype(FULL)

    local_ids = tokens_all - narrow_spot * vocab_rows
    inside = (local_ids >= 0) & (local_ids < vocab_rows)
    spots = jnp.where(inside, local_ids, vocab_rows)
    found = lookup(embed, spots)
    hidden_rows = side_by_side(exchange(found.reshape(wide_count, seq_len, columns), "wide"))

    kv_low = jnp.moveaxis(attn_kv, 1, 0).astype(LOW)
    kv_w = lax.all_gather(
        lax.all_gather(kv_low, "narrow", axis=2, tiled=True), "wide", axis=1, tiled=True
    )
    qo_low = jnp.moveaxis(attn_qo, 1, 0).astype(LOW)
    q_w = gather_rows(qo_low[0], "wide")
    o_w = gather_rows(qo_low[1], "wide")
    ffn_low = jnp.moveaxis(ffn, 1, 0).astype(LOW)
    ffn_cut = ffn_low.reshape(3, narrow_count, ffn_rows // narrow_count, ffn_low.shape[2])
    ffn_sub = exchange(jnp.moveaxis(ffn_cut, 1, 0), "narrow")
    ffn_w = [gather_rows(side_by_side(ffn_sub[:, j]), "wide") for j in range(3)]
    table_own = side_by_side(
        exchange(embed.astype(LOW).reshape(wide_count, vocab_rows // wide_count, columns), "wide")
    )
    q_full = gather_rows(gather_columns(qo_low[0], "narrow"), "wide")

    mom_qo = jnp.moveaxis(attn_qo_mom, 1, 0)
    mom_kv = jnp.moveaxis(attn_kv_mom, 1, 0)
    mom_ffn = jnp.moveaxis(ffn_mom, 1, 0)
    slot = mom_ffn.shape[1] * mom_ffn.shape[2]

    def pack_small(qo_part, kv_part):
        flat = jnp.concatenate([qo_part.reshape(-1), kv_part.reshape(-1)])
        return jnp.pad(flat, (0, slot - flat.shape[0]))

    def unpack_small(flat):
        lead = flat.shape[:-1]
        qo_size, kv_size = mom_qo.size, mom_kv.size
        return (
            flat[..., :qo_size].reshape(lead + mom_qo.shape),
            flat[..., qo_size : qo_size + kv_size].reshape(lead + mom_kv.shape),
        )

    def one_per_owner(ffn_part, qo_part, kv_part):
        parts = [ffn_part[j].reshape(-1) for j in range(3)] + [pack_small(qo_part, kv_part)]
        parts = parts + [jnp.zeros_like(parts[0])] * (narrow_count - 4)
        return jnp.stack(parts)

    mom_owned = exchange(one_per_owner(mom_ffn, mom_qo, mom_kv), "narrow")

    seg_all, cosine_all, sine_all = angles_at(lens, jnp.arange(seq_len, dtype=jnp.int32))
    seg_mine, cosine, sine = angles_at(lens, pick_ids)
    inside_mine = lax.dynamic_slice_in_dim(inside, wide_spot * seq_len, seq_len, 0)
    pick_hot = (
        pick_ids[:, None] == jnp.arange(seq_len, dtype=jnp.int32)[None, :]
    ).astype(LOW)

    rows_full = hidden_rows.astype(FULL)
    normed_all = norm_rows(rows_full, gain_w[0]).astype(LOW)
    keys_part = dot(normed_all, kv_w[0], 1, 0).reshape(seq_len, KVH, HD)
    keys_part = rotate(keys_part, cosine_all[:, None], sine_all[:, None]).astype(LOW)
    values_part = dot(normed_all, kv_w[1], 1, 0).reshape(seq_len, KVH, HD).astype(LOW)
    by_head = jnp.moveaxis(jnp.stack([keys_part, values_part]), 2, 0)
    by_head = jnp.repeat(by_head, repeat, axis=0)
    own_head = lax.psum_scatter(by_head, "narrow", scatter_dimension=0, tiled=True)
    groups = own_head.shape[0]
    keys, values = own_head[:, 0], own_head[:, 1]
    start_h = lax.psum(dot(pick_hot, hidden_rows, 1, 0).astype(LOW), "narrow").astype(FULL)

    normed = norm_rows(start_h, gain_w[0]).astype(LOW)
    queries = dot(normed, q_w, 1, 0).reshape(sel, heads_own, HD)
    queries = rotate(queries, cosine[:, None], sine[:, None]).astype(LOW)
    grouped = queries.reshape(sel, groups, heads_own // groups, HD)
    scale = HD ** (-0.5)
    scores = jnp.einsum("tkgd,ksd->kgts", grouped, keys, preferred_element_type=FULL) * scale
    allowed = (seg_mine[:, None] == seg_all[None, :]) & (
        pick_ids[:, None] >= jnp.arange(seq_len, dtype=jnp.int32)[None, :]
    )
    scores = jnp.where(allowed, scores, MASKED)
    shifted_exp = jnp.exp(scores - jnp.max(scores, axis=-1, keepdims=True))
    probs = shifted_exp / jnp.sum(shifted_exp, axis=-1, keepdims=True)
    probs_low = probs.astype(LOW)
    mixed = jnp.einsum("kgts,ksd->tkgd", probs_low, values, preferred_element_type=FULL)
    mixed = mixed.reshape(sel, heads_own * HD).astype(LOW)

    def own(values_all):
        return lax.dynamic_slice_in_dim(values_all, narrow_spot * own_rows, own_rows, 0)

    start_own = own(start_h)
    middle = start_own + lax.psum_scatter(
        dot(mixed, o_w, 1, 1), "narrow", scatter_dimension=0, tiled=True
    )
    inner_own = norm_rows(middle, gain_w[1]).astype(LOW)
    inner = gather_rows(inner_own, "narrow")
    gate = dot(inner, ffn_w[0], 1, 1)
    up = dot(inner, ffn_w[1], 1, 1)
    hidden = (jax.nn.silu(gate) * up).astype(LOW)
    final_own = middle + lax.psum_scatter(
        dot(hidden, ffn_w[2], 1, 0), "narrow", scatter_dimension=0, tiled=True
    )
    final_own = jnp.where(keep_layer > 0, final_own, start_own)

    local_target = targets_all - (
        narrow_spot * vocab_rows + wide_spot * table_own.shape[0]
    )
    has_target = (
        local_target[:, None] == jnp.arange(table_own.shape[0], dtype=jnp.int32)[None, :]
    )
    counted = (targets_all >= 0).astype(FULL)
    loss_count = jnp.sum(counted)

    def exit_part(own_h, weight):
        features = gather_rows(norm_rows(own_h, gain_w[2]).astype(LOW), BOTH)
        logits = dot(features, table_own, 1, 1)
        peak = jnp.max(logits, axis=-1)
        total = jnp.sum(jnp.exp(logits - peak[:, None]), axis=-1)
        picked = jnp.sum(jnp.where(has_target, logits, 0.0), axis=-1)
        stats = lax.all_gather(jnp.stack([peak, total, picked]), BOTH)
        peak_all = jnp.max(stats[:, 0], axis=0)
        total_all = jnp.sum(stats[:, 1] * jnp.exp(stats[:, 0] - peak_all), axis=0)
        log_norm = peak_all + jnp.log(total_all)
        loss = weight * jnp.sum(counted * (log_norm - jnp.sum(stats[:, 2], axis=0)))
        grad_logits = (
            (jnp.exp(logits - log_norm[:, None]) - has_target.astype(FULL))
            * (weight * counted)[:, None]
        ).astype(LOW)
        grad_features = dot(grad_logits, table_own, 1, 0)
        grad_own = lax.psum_scatter(
            lax.psum_scatter(grad_features, "wide", scatter_dimension=0, tiled=True),
            "narrow",
            scatter_dimension=0,
            tiled=True,
        )
        return loss, grad_own, dot(grad_logits, features, 0, 0)

    loss_early, grad_early, head_early = exit_part(start_own, EXIT_EARLY)
    loss_late, grad_late, head_late = exit_part(final_own, EXIT_LAST)
    loss_sum = loss_early + loss_late
    grad_head = (head_early + head_late).astype(LOW)
    head_cols = exchange(cut_columns(grad_head, wide_count), "wide").reshape(vocab_rows, columns)

    grad_start_exit, gain_early = norm_back(start_own, gain_w[2], grad_early)
    grad_final, gain_late = norm_back(final_own, gain_w[2], grad_late)
    grad_layer = grad_final * keep_layer
    grad_out = gather_rows(grad_layer.astype(LOW), "narrow")
    grad_hidden = dot(grad_out, ffn_w[2], 1, 1)
    sigma = jax.nn.sigmoid(gate)
    grad_gate = (grad_hidden * up * sigma * (1.0 + gate * (1.0 - sigma))).astype(LOW)
    grad_up = (grad_hidden * gate * sigma).astype(LOW)
    grad_inner = lax.psum_scatter(
        dot(grad_gate, ffn_w[0], 1, 0) + dot(grad_up, ffn_w[1], 1, 0),
        "narrow",
        scatter_dimension=0,
        tiled=True,
    )
    extra_mid, gain_mid = norm_back(middle, gain_w[1], grad_inner)
    grad_mid = grad_layer + extra_mid
    grad_pass = grad_mid + grad_start_exit + grad_final * (1.0 - keep_layer)
    both_mid = lax.all_gather(
        jnp.stack([grad_mid.astype(LOW), grad_pass.astype(LOW)]), "narrow", axis=1, tiled=True
    )
    grad_branch, grad_extra = both_mid[0], both_mid[1]

    grad_mixed = dot(grad_branch, o_w, 1, 0).astype(LOW)
    grouped_grad = grad_mixed.reshape(sel, groups, heads_own // groups, HD)
    grad_probs = jnp.einsum("tkgd,ksd->kgts", grouped_grad, values, preferred_element_type=FULL)
    grad_scores = (
        probs * (grad_probs - jnp.sum(probs * grad_probs, axis=-1, keepdims=True))
    ).astype(LOW)
    grad_queries = (
        jnp.einsum("kgts,ksd->tkgd", grad_scores, keys, preferred_element_type=FULL) * scale
    ).reshape(sel, heads_own, HD)
    grad_queries = (
        unrotate(grad_queries, cosine[:, None], sine[:, None])
        .reshape(sel, heads_own * HD)
        .astype(LOW)
    )
    grad_keys = jnp.einsum("kgts,tkgd->ksd", grad_scores, grouped, preferred_element_type=FULL)
    grad_keys = unrotate(grad_keys * scale, cosine_all, sine_all).astype(LOW)
    grad_values = jnp.einsum(
        "kgts,tkgd->ksd", probs_low, grouped_grad, preferred_element_type=FULL
    ).astype(LOW)
    grad_kv_all = gather_rows(jnp.stack([grad_keys, grad_values], axis=1), "narrow")
    if repeat > 1:
        grad_kv_all = jnp.sum(
            grad_kv_all.reshape(KVH, repeat, 2, seq_len, HD).astype(FULL), axis=1
        ).astype(LOW)
    grad_kv_all = jnp.transpose(grad_kv_all, (1, 2, 0, 3)).reshape(2, seq_len, KVH * HD)
    grad_q_all = gather_columns(grad_queries, "narrow")

    pick_part = dot(grad_q_all, q_full, 1, 1)
    pick_high = pick_part.astype(LOW)
    pick_low = (pick_part - pick_high.astype(FULL)).astype(LOW)
    grad_normed = (
        dot(grad_kv_all[0], kv_w[0], 1, 1)
        + dot(grad_kv_all[1], kv_w[1], 1, 1)
        + dot(pick_hot, pick_high, 0, 0)
        + dot(pick_hot, pick_low, 0, 0)
    )
    grad_normed = jnp.where(inside_mine[:, None], grad_normed, 0.0)
    extra_start, gain_attn = norm_back(rows_full, gain_w[0], grad_normed)
    grad_start = jnp.where(
        inside_mine[:, None], extra_start + dot(pick_hot, grad_extra, 0, 0), 0.0
    ).astype(LOW)
    grad_rows = exchange(cut_columns(grad_start, wide_count), "wide").reshape(-1, columns)
    summed_table, table_squares = spread(spots, grad_rows, head_cols)

    grad_kv_w = jnp.stack(
        [dot(normed_all, grad_kv_all[0], 0, 0), dot(normed_all, grad_kv_all[1], 0, 0)], axis=1
    )
    grad_kv_w = lax.psum_scatter(grad_kv_w, "wide", scatter_dimension=0, tiled=True)
    summed_kv = lax.psum_scatter(
        jnp.moveaxis(grad_kv_w, 1, 0), "narrow", scatter_dimension=2, tiled=True
    )

    left_cols = exchange(
        jnp.moveaxis(
            jnp.stack([normed, grad_branch]).reshape(2, sel, wide_count, columns), 2, 0
        ),
        "wide",
    )
    left_cols = jnp.moveaxis(left_cols, 1, 0).reshape(2, wide_count * sel, columns)
    summed_qo = jnp.stack(
        [
            dot(left_cols[0], gather_rows(grad_queries, "wide"), 0, 0),
            dot(left_cols[1], gather_rows(mixed, "wide"), 0, 0),
        ]
    )

    inner_all = gather_rows(inner, "wide")
    out_all = gather_rows(grad_out, "wide")
    acts = jnp.stack([grad_gate, grad_up, hidden]).reshape(
        3, sel, wide_count, ffn_rows // narrow_count
    )
    acts = exchange(jnp.moveaxis(acts, 2, 0), "wide")
    acts = jnp.moveaxis(acts, 1, 0).reshape(3, wide_count * sel, ffn_rows // narrow_count)
    acts = lax.all_gather(acts, "narrow", axis=2, tiled=True)

    def cols_own(values_all):
        size = width // narrow_count
        return lax.dynamic_slice_in_dim(values_all, narrow_spot * size, size, 1)

    rights = (inner_all, inner_all, out_all)
    summed_ffn = jnp.stack([dot(acts[j], cols_own(rights[j]), 0, 0) for j in range(3)])
    small_all = lax.all_gather(
        pack_small(summed_qo, summed_kv).astype(LOW), "narrow", axis=0
    )

    gain_grads = jnp.stack([gain_attn, gain_mid, gain_early + gain_late])
    gain_sum = lax.psum(gain_grads, BOTH)
    gain_size = gains.shape[1]
    summed_gain = lax.dynamic_slice_in_dim(
        gain_sum, (wide_spot * narrow_count + narrow_spot) * gain_size, gain_size, 1
    )
    squares = (
        jnp.sum(summed_qo * summed_qo)
        + jnp.sum(summed_kv * summed_kv)
        + jnp.sum(summed_ffn * summed_ffn)
    )
    squares = squares + jnp.sum(summed_gain * summed_gain) + jnp.sum(table_squares)
    square_total = lax.psum(squares, BOTH)
    grad_norm = jnp.sqrt(square_total) / loss_count
    factor = jnp.minimum(1.0, CLIP_NORM / (grad_norm + 1e-06)) / loss_count

    def whole_columns(parts):
        return jnp.moveaxis(parts, 0, 2).reshape(
            parts.shape[1], parts.shape[2], parts.shape[0] * parts.shape[3]
        )

    def ffn_owner():
        left = lax.dynamic_index_in_dim(acts, jnp.minimum(narrow_spot, 2), 0, False)
        right = jnp.where(narrow_spot == 2, out_all, inner_all)
        grad = dot(left, right, 0, 0)
        mom = side_by_side(mom_owned.reshape((narrow_count,) + mom_ffn.shape[1:]))
        result = orthogonalize((MOMENTUM * mom + grad * factor)[None])[0]
        return cut_columns(result.astype(LOW), narrow_count).reshape(narrow_count, slot)

    def small_owner():
        mom_q, mom_k = unpack_small(mom_owned)
        grad_q, grad_k = unpack_small(small_all.astype(FULL))
        results = [
            orthogonalize(whole_columns(MOMENTUM * mom + grad * factor)).astype(LOW)
            for mom, grad in ((mom_q, grad_q), (mom_k, grad_k))
        ]
        parts = [
            jnp.moveaxis(
                result.reshape(2, result.shape[1], narrow_count, -1), 2, 0
            ).reshape(narrow_count, -1)
            for result in results
        ]
        flat = jnp.concatenate(parts, axis=1)
        return jnp.pad(flat, ((0, 0), (0, slot - flat.shape[1])))

    directions = lax.cond(narrow_spot == 3, small_owner, ffn_owner)
    directions = exchange(directions, "narrow")
    dir_ffn = directions[:3].reshape(mom_ffn.shape).astype(FULL)
    dir_qo, dir_kv = unpack_small(directions[3].astype(FULL))

    embed_new, embed_m_new, embed_v_new = adamw(
        embed, embed_m, embed_v, summed_table * factor, RATE_ADAM, WEIGHT_DECAY
    )
    gains_new, gains_m_new, gains_v_new = adamw(
        gains, gains_m, gains_v, summed_gain * factor, RATE_GAIN, 0.0
    )

    def mom_next(mom, grad):
        return MOMENTUM * mom + jnp.moveaxis(grad * factor, 0, 1)

    shrink = 1.0 - RATE_MUON * WEIGHT_DECAY

    def weight_next(weight, direction):
        return weight * shrink - RATE_MUON * jnp.moveaxis(direction, 0, 1)

    return (
        loss_sum,
        loss_count,
        grad_norm,
        embed_new,
        embed_m_new,
        embed_v_new,
        weight_next(attn_qo, dir_qo),
        mom_next(attn_qo_mom, summed_qo),
        weight_next(attn_kv, dir_kv),
        mom_next(attn_kv_mom, summed_kv),
        weight_next(ffn, dir_ffn),
        mom_next(ffn_mom, summed_ffn),
        gains_new,
        gains_m_new,
        gains_v_new,
    )


def solution(mesh):
    by_pack = P("wide", None)
    table = P("narrow", "wide")
    layer = P("wide", None, "narrow")
    gain = P(None, ("wide", "narrow"))
    return jax.shard_map(
        per_device,
        mesh=mesh,
        in_specs=(by_pack,) * 4 + (P("wide"),) + (table,) * 3 + (layer,) * 6 + (gain,) * 3,
        out_specs=(P(),) * 3 + (table,) * 3 + (layer,) * 6 + (gain,) * 3,
        check_vma=False,
    )
```

time: 5560 us -> 2270 us (0.41)
  waiting for transfers between devices: 3970 us -> 1180 us
  matrix products: 609 us -> 250 us
  other arithmetic: 474 us -> 152 us
  blocking collectives: 125 us -> 354 us
  local copies, waits for them, and re-layouts: 329 us -> 131 us
  Pallas kernels: 0 us -> 77.6 us
    psum x5 -> x0, waiting for transfers between devices: 1290 us -> none  [orthogonalize(): lax.psum((gram_of(current[0]), gram_of(current[1]), gram_of(current[2])),...]
    reduce_scatter x10 -> x9, waiting for transfers between devices: 1140 us -> 271 us  [the longest x2 144 us: exit_part(): lax.psum_scatter(grad_features, 'wide', scatter_dimension=0, tiled=True)]
    all_gather x10 -> x18, waiting for transfers between devices: 984 us -> 483 us  [the longest x13 356 us: gather_rows(): return lax.all_gather(values, axis, axis=0, tiled=True)]
    unnamed x31 -> x29, waiting for transfers between devices: 563 us -> 140 us
    dot_general x72 -> x53, matrix products: 609 us -> 250 us  [the longest x32 166 us: dot(): lax.dot_general(first, second, (((first_dim,), (second_dim,)), ((), ())),...]
    all_to_all x0 -> x8, waiting for transfers between devices: none -> 284 us  [exchange(): return lax.all_to_all(parts, axis, 0, 0, tiled=True)]
    scatter-add x2 -> x0, other arithmetic: 219 us -> none  [the longest x1 198 us: per_device(): jax.ops.segment_sum(jnp.where(inside[:, None], grad_rows_all, 0.0), clipp...]
    all_gather x6 -> x8, blocking collectives: 86.3 us -> 250 us  [the longest x2 129 us: exit_part(): stats = lax.all_gather(jnp.stack([peak, total, picked]), BOTH)]
  transfers between devices with their start and end apart: 28 -> 36, of which waited for: 22 -> 27; matrix products, arithmetic and copies ran while one was open for 15% -> 12% of each run, Pallas kernels for 0% -> 3%
where the time goes in v1:
time: 2270 us; the launch traced here: 2260 us
  waiting for transfers between devices  1180 us (52%)
  blocking collectives  354 us (16%)
  matrix products  250 us (11%)
  other arithmetic  152 us (7%)
  local copies, waits for them, and re-layouts  131 us (6%)
  Pallas kernels  77.6 us (3%)
  starting transfers between devices  55.2 us (2%)
  loops' own time  32.4 us (1%)
  between operations  25.9 us (1%)
    all_gather x13, waiting for transfers between devices, gather_rows(): return lax.all_gather(values, axis, axis=0, tiled=True)  356 us
    all_to_all x8, waiting for transfers between devices, exchange(): return lax.all_to_all(parts, axis, 0, 0, tiled=True)  284 us
    dot_general x32, matrix products, dot(): lax.dot_general(first, second, (((first_dim,), (second_dim,)), ((), ())),...  166 us
    reduce_scatter x2, waiting for transfers between devices, exit_part(): lax.psum_scatter(grad_features, 'wide', scatter_dimension=0, tiled=True)  144 us
    unnamed x29, waiting for transfers between devices  140 us
    all_gather x2, blocking collectives, exit_part(): stats = lax.all_gather(jnp.stack([peak, total, picked]), BOTH)  129 us
    all_gather x1, waiting for transfers between devices, per_device(): acts = lax.all_gather(acts, 'narrow', axis=2, tiled=True)  78.8 us
    all_gather x2, blocking collectives, gather_columns(): return lax.all_gather(values, axis, axis=1, tiled=True)  73.9 us
  transfers between devices with their start and end apart: 36, of which 27 were waited for; matrix products, arithmetic and copies ran while one was open for 12% of the time, Pallas kernels for 3%

profile of v1, /device:TPU:17, one launch (start us, length us, event | category | flops | bytes accessed | tf_op | source)
XLA Modules:
  0.0 2256.6 jit_solution(7750892430545601315)
XLA Ops:
  8.2 12.3 all_gather.92
  21.3 11.2 all-gather.8
  33.7 35.3 %lookup.1 = bf16[8192,256]{1,0:T(8,128)(2,1)} custom-call(s32[8192]{0:T(1024)} %bitcast_select_fusion.1.ids_ref, f32[8192,256]{1,0:T(8,128)} %table_ref.1), custom_call_target="tpu_custom_call" | custom-call | bytes 75497472 | tf_op jit(solution)/shard_map/lookup/pallas_call | solution.py:112
  73.7 59.4 %all-gather.9 = bf16[32,64,3]{1,2,0:T(4,128)(2,1)S(1)} all-gather(bf16[1,64,3]{1,2,0:T(4,128)(2,1)S(1)} %convert_bitcast_fusion.2), channel_id=1, replica_groups=mesh['wide'=8,'narrow'=4] {'wide','narrow'}, dimensions={0}, use_global_device_ids=true | all-gather | bytes 12672 | tf_op jit(solution)/shard_map/all_gather | solution.py:263
  145.5 7.5 reshape.1367
  184.9 9.2 all-to-all-start.2
  196.1 136.2 %all-reduce.7.cloned.1.call-done = (bf16[4,2,1024,128]{2,3,0,1:T(8,128)(2,1)}, bf16[128,2048]{1,0:T(8,128)(2,1)}) async-done(((bf16[4,2,1024,128]{2,3,0,1:T(8,128)(2,1)}, bf16[128,2048]{1,0:T(8,128)(2,1)}), (bf16[4,2,1024,128]{2,3,0,1:T(8,128)(2,1)}, bf16[128,2048]{1,0:T(8,128)(2,1)})) %all-reduce.7.cloned.1.call-update) | async-done | bytes 2621456
  334.7 28.3 %all-gather.57.cloned.1.call-done = bf16[1,2048,512]{2,1,0:T(8,128)(2,1)} async-done(((bf16[1,256,512]{2,1,0:T(8,128)(2,1)}), bf16[1,2048,512]{2,1,0:T(8,128)(2,1)}) %all-gather.57.cloned.1.call-update) | async-done | bytes 2097168 | tf_op jit(solution)/shard_map/all_gather | solution.py:259
  372.3 21.0 all-gather.59.cloned.1.call-done
  402.3 20.0 reduce-scatter.13.cloned.1.call-done
  424.8 12.5 all_gather.96
  437.3 31.2 %all-gather.35.cloned.1.call-done = bf16[1408,2048]{1,0:T(8,128)(2,1)} async-done(((bf16[176,2048]{1,0:T(8,128)(2,1)}), bf16[1408,2048]{1,0:T(8,128)(2,1)}) %all-gather.35.cloned.1.call-update) | async-done | bytes 5767184 | tf_op jit(solution)/shard_map/all_gather | solution.py:259
  473.1 41.4 %all-gather.37.cloned.1.call-done = bf16[1408,2048]{1,0:T(8,128)(2,1)} async-done(((bf16[176,2048]{1,0:T(8,128)(2,1)}), bf16[1408,2048]{1,0:T(8,128)(2,1)}) %all-gather.37.cloned.1.call-update) | async-done | bytes 5767184 | tf_op jit(solution)/shard_map/all_gather | solution.py:259
  519.9 40.5 %all-gather.39.cloned.1.call-done = bf16[1408,2048]{1,0:T(8,128)(2,1)} async-done(((bf16[176,2048]{1,0:T(8,128)(2,1)}), bf16[1408,2048]{1,0:T(8,128)(2,1)}) %all-gather.39.cloned.1.call-update) | async-done | bytes 5767184 | tf_op jit(solution)/shard_map/all_gather | solution.py:259
  566.3 24.3 %reduce-scatter.15.cloned.1.call-done = f32[32,2048]{1,0:T(8,128)} async-done(((f32[128,2048]{1,0:T(8,128)}), f32[32,2048]{1,0:T(8,128)}) %reduce-scatter.15.cloned.1.call-update) | async-done | bytes 262160 | tf_op jit(solution)/shard_map/reduce_scatter | solution.py:401
  604.8 48.7 %all-to-all-done.1 = bf16[8,1024,256]{2,1,0:T(8,128)(2,1)} async-done(((bf16[8,1024,256]{2,1,0:T(8,128)(2,1)}), bf16[8,1024,256]{2,1,0:T(8,128)(2,1)}, u32[]{:S(2)}, u32[]{:S(2)}) %all-to-all-start.1) | async-done | bytes 4194336 | tf_op jit(solution)/shard_map/all_to_all | solution.py:245
  659.9 14.9 all-gather.31.cloned.1.call-done
  674.8 10.0 fusion.349
  684.8 54.2 %all-gather.41.cloned.1.call-done = bf16[1024,2048]{1,0:T(8,128)(2,1)} async-done(((bf16[32,2048]{1,0:T(8,128)(2,1)}), bf16[1024,2048]{1,0:T(8,128)(2,1)}) %all-gather.41.cloned.1.call-update) | async-done | bytes 4194320 | tf_op jit(solution)/shard_map/all_gather | solution.py:259
  739.0 7.8 fusion.350
  748.9 61.0 %all-gather.11 = f32[32,3,1024]{2,1,0:T(4,128)S(1)} all-gather(f32[1,3,1024]{2,1,0:T(4,128)S(1)} %maximum_bitcast_fusion.4), channel_id=6, replica_groups=mesh['wide'=8,'narrow'=4] {'wide','narrow'}, dimensions={0}, use_global_device_ids=true | all-gather | bytes 405504 | tf_op jit(solution)/shard_map/all_gather | solution.py:421
  810.2 68.1 %all-gather.10 = f32[32,3,1024]{2,1,0:T(4,128)S(1)} all-gather(f32[1,3,1024]{2,1,0:T(4,128)S(1)} %maximum_bitcast_fusion.3), channel_id=3, replica_groups=mesh['wide'=8,'narrow'=4] {'wide','narrow'}, dimensions={0}, use_global_device_ids=true | all-gather | bytes 405504 | tf_op jit(solution)/shard_map/all_gather | solution.py:421
  879.4 7.0 fusion.334
  886.5 11.5 fusion.331
  898.1 68.4 %reduce-scatter.17.cloned.1.call-done = f32[128,2048]{1,0:T(8,128)} async-done(((f32[1024,2048]{1,0:T(8,128)}), f32[128,2048]{1,0:T(8,128)}) %reduce-scatter.17.cloned.1.call-update) | async-done | bytes 1048592 | tf_op jit(solution)/shard_map/reduce_scatter | solution.py:432
  966.6 75.7 %reduce-scatter.23.cloned.1.call-done = f32[128,2048]{1,0:T(8,128)} async-done(((f32[1024,2048]{1,0:T(8,128)}), f32[128,2048]{1,0:T(8,128)}) %reduce-scatter.23.cloned.1.call-update) | async-done | bytes 1048592 | tf_op jit(solution)/shard_map/reduce_scatter | solution.py:432
  1042.3 27.9 %reduce-scatter.19.cloned.1.call-done = f32[32,2048]{1,0:T(8,128)} async-done(((f32[128,2048]{1,0:T(8,128)}), f32[32,2048]{1,0:T(8,128)}) %reduce-scatter.19.cloned.1.call-update) | async-done | bytes 262160 | tf_op jit(solution)/shard_map/reduce_scatter | solution.py:431
  1072.0 26.3 %reduce-scatter.25.cloned.1.call-done = f32[32,2048]{1,0:T(8,128)} async-done(((f32[128,2048]{1,0:T(8,128)}), f32[32,2048]{1,0:T(8,128)}) %reduce-scatter.25.cloned.1.call-update) | async-done | bytes 262160 | tf_op jit(solution)/shard_map/reduce_scatter | solution.py:431
  1100.9 11.6 all_gather.103
  1125.2 28.5 %reduce-scatter.21.cloned.1.call-done = f32[32,2048]{1,0:T(8,128)} async-done(((f32[128,2048]{1,0:T(8,128)}), f32[32,2048]{1,0:T(8,128)}) %reduce-scatter.21.cloned.1.call-update) | async-done | bytes 262160 | tf_op jit(solution)/shard_map/reduce_scatter | solution.py:453
  1158.7 26.9 %all-gather.43.cloned.1.call-done = bf16[2,128,2048]{2,1,0:T(8,128)(2,1)} async-done(((bf16[2,32,2048]{2,1,0:T(8,128)(2,1)}), bf16[2,128,2048]{2,1,0:T(8,128)(2,1)}) %all-gather.43.cloned.1.call-update) | async-done | bytes 1048592 | tf_op jit(solution)/shard_map/all_gather | solution.py:462
  1193.8 21.4 all-gather.61.cloned.1.call-done
  1221.1 40.9 %all-gather.49.cloned.1.call-done = bf16[4,2,1024,128]{3,2,1,0:T(8,128)(2,1)} async-done(((bf16[1,2,1024,128]{3,2,1,0:T(8,128)(2,1)}), bf16[4,2,1024,128]{3,2,1,0:T(8,128)(2,1)}) %all-gather.49.cloned.1.call-update) | async-done | bytes 2097168 | tf_op jit(solution)/shard_map/all_gather | solution.py:259
  1283.4 27.3 %all_to_all.56 = bf16[8,3,128,176]{2,3,1,0:T(8,128)(2,1)S(1)} all-to-all(bf16[8,3,128,176]{2,3,1,0:T(8,128)(2,1)S(1)} %copy.361), channel_id=1, replica_groups=mesh['wide'=8,'narrow'=4] {'wide'}, dimensions={0} | all-to-all | bytes 2162688 | tf_op jit(solution)/shard_map/all_to_all | solution.py:245
  1312.2 11.6 fusion.329
  1323.9 10.6 add_convert_fusion.2
  1343.6 14.5 all_gather.111
  1378.5 10.3 fusion.206
  1388.9 21.6 all-to-all-done.6
  1410.5 7.3 all-to-all-start.3
  1427.0 12.7 all-to-all-done.3
  1440.6 8.9 all-to-all-start.5
  1465.9 19.0 all-gather.47.cloned.1.call-done
  1486.6 31.0 %all-gather.45.cloned.1.call-done = bf16[1024,512]{0,1:T(8,128)(2,1)} async-done(((bf16[128,512]{0,1:T(8,128)(2,1)}), bf16[1024,512]{0,1:T(8,128)(2,1)}) %all-gather.45.cloned.1.call-update) | async-done | bytes 1048592 | tf_op jit(solution)/shard_map/all_gather | solution.py:259
  1521.1 38.6 %psum.22 = f32[3,2048]{1,0:T(4,128)S(1)} all-reduce(f32[3,2048]{1,0:T(4,128)S(1)} %pad_maximum_fusion.8), channel_id=1, replica_groups=mesh['wide'=8,'narrow'=4] {'wide','narrow'}, use_global_device_ids=true, to_apply=%region_49.50 | all-reduce | flops 6144 | bytes 49152 | tf_op jit(solution)/shard_map/psum | solution.py:553
  1560.4 78.8 %all-gather.51.cloned.1.call-done = bf16[3,1024,704]{1,2,0:T(8,128)(2,1)} async-done(((bf16[3,1024,176]{1,2,0:T(8,128)(2,1)}), bf16[3,1024,704]{1,2,0:T(8,128)(2,1)}) %all-gather.51.cloned.1.call-update) | async-done | bytes 4325392 | tf_op jit(solution)/shard_map/all_gather | solution.py:540
  1645.0 33.3 %all-gather.55.cloned.1.call-done = bf16[1024,2048]{1,0:T(8,128)(2,1)} async-done(((bf16[128,2048]{1,0:T(8,128)(2,1)}), bf16[1024,2048]{1,0:T(8,128)(2,1)}) %all-gather.55.cloned.1.call-update) | async-done | bytes 4194320 | tf_op jit(solution)/shard_map/all_gather | solution.py:259
  1683.6 42.3 %spread.1 = (f32[8192,256]{1,0:T(8,128)}, f32[8,256]{1,0:T(8,128)}) custom-call(s32[8192]{0:T(1024)} %bitcast_select_fusion.1.ids_ref, bf16[8192,256]{1,0:T(8,128)(2,1)} %bitcast.135.rows_ref, bf16[8192,256]{1,0:T(8,128)(2,1)} %bitcast.137.head_ref), custom_call_target="tpu_custom_call" | custom-call | flops 2097152 | bytes 134217728 | tf_op jit(solution)/shard_map/spread/pallas_call | solution.py:177
  1733.4 38.1 %psum.23 = f32[]{:T(128)} all-reduce(f32[]{:T(128)S(6)} %add.618), channel_id=1, replica_groups=mesh['wide'=8,'narrow'=4] {'wide','narrow'}, use_global_device_ids=true, to_apply=%region_53.54 | all-reduce | flops 1 | bytes 8 | tf_op jit(solution)/shard_map/psum | solution.py:564
  1793.9 168.7 %all-to-all-done.7 = f32[4,1,360448]{2,1,0:T(1,128)} async-done(((f32[4,1,360448]{2,1,0:T(1,128)}), f32[4,1,360448]{2,1,0:T(1,128)}, u32[]{:S(2)}, u32[]{:S(2)}) %all-to-all-start.7) | async-done | bytes 5767200 | tf_op jit(solution)/shard_map/all_to_all | solution.py:245
  1962.7 7.5 copy.481
  1970.2 142.6 %conditional.1 = (bf16[4,360448]{1,0:T(4,128)(2,1)S(1)}) conditional(s32[]{:T(128)} %convert_element_type.543, (f32[4,360448]{1,0:T(4,128)}, s32[]{:T(128)}, bf16[3,1024,704]{1,2,0:T(8,128)(2,1)}, bf16[1024,2048]{1,0:T(8,128)(2,1)}, bf16[1024,2048]{1,0:T(8,128)(2,1)}, /*index=5*/f32[]{:T(128)}) %tuple.212, (f32[4,360448]{1,0:T(4,128)}, ...), branch_computations={%region_54.0_spmd, %region_66.89_spmd} | conditional | flops 26843262976 | bytes 274531648 | solution.py:597
  1986.3 11.4 multiply_reduce_fusion
  1998.4 8.7 select_reduce_fusion.9
  2031.4 7.7 multiply_add_fusion.2
  2048.5 7.5 multiply_add_fusion.1
  2065.4 7.5 multiply_add_fusion
  2082.6 8.9 add_convert_fusion
  2114.9 14.7 reduce.45
  2134.1 7.3 all-to-all-start.8
  2148.4 22.1 multiply_subtract_fusion.10
  2170.5 32.6 %all-to-all-done.8 = bf16[4,2,180224]{2,1,0:T(2,128)(2,1)S(1)} async-done(((bf16[4,2,180224]{2,1,0:T(2,128)(2,1)}), bf16[4,2,180224]{2,1,0:T(2,128)(2,1)S(1)}, u32[]{:S(2)}, u32[]{:S(2)}) %all-to-all-start.8) | async-done | bytes 2883616 | tf_op jit(solution)/shard_map/all_to_all | solution.py:245
  2207.2 16.2 fusion.215
  2223.4 12.0 fusion.253
  (492 shorter events, 358.5 us)
Async XLA Ops:
  7.2 152.2 %all-gather.33.cloned.1.call-start = ((), (), s32[]{:S(2)}) async-start(), calls=%async_computation.19 | async-start | bytes 4718592 | tf_op jit(solution)/shard_map/all_gather | solution.py:315
  32.5 36.5 %copy-start.65 = (s32[8,1,1152]{2,0,1:T(8,128)}, s32[8,1,1152]{2,0,1:T(8,128)S(1)}, u32[]{:S(2)}) copy-start(s32[8,1,1152]{2,0,1:T(8,128)S(1)} %copy.488) | copy-start | bytes 110596
  69.1 64.2 %copy-start.111 = (s32[1,2]{1,0:T(1,128)S(1)}, s32[1,2]{1,0:T(1,128)}, u32[]{:S(2)}) copy-start(s32[1,2]{1,0:T(1,128)} %param.22) | copy-start | bytes 28
  69.1 65.6 %all-to-all-start = ((bf16[8,1024,256]{2,1,0:T(8,128)(2,1)}), bf16[8,1024,256]{2,1,0:T(8,128)(2,1)}, u32[]{:S(2)}, u32[]{:S(2)}) async-start(bf16[8,1024,256]{2,1,0:T(8,128)(2,1)} %bitcast.466), calls=%async_computation | async-start | bytes 8388608 | tf_op jit(solution)/shard_map/all_to_all | solution.py:245
  73.7 258.6 %all-reduce.7.cloned.1.call-start = ((), (), s32[]{:S(2)}) async-start(), calls=%async_computation.45 | async-start | bytes 5242880
  133.2 200.3 %copy-start.66 = (f32[1,2048]{1,0:T(1,128)}, f32[1,2048]{1,0:T(1,128)S(1)}, u32[]{:S(2)}) copy-start(f32[1,2048]{1,0:T(1,128)S(1)} %get-tuple-element.377) | copy-start | bytes 24580
  133.5 61.7 %copy-start.95 = (f32[64]{0:T(128)}, f32[64]{0:T(128)S(1)}, u32[]{:S(2)}) copy-start(f32[64]{0:T(128)S(1)} %multiply_power_fusion) | copy-start | bytes 772
  179.2 183.9 %all-gather.57.cloned.1.call-start = ((), (), s32[]{:S(2)}) async-start(), calls=%async_computation.40 | async-start | bytes 2359296 | tf_op jit(solution)/shard_map/all_gather | solution.py:259
  180.3 213.0 %all-gather.59.cloned.1.call-start = ((), (), s32[]{:S(2)}) async-start(), calls=%async_computation.41 | async-start | bytes 2359296 | tf_op jit(solution)/shard_map/all_gather | solution.py:259
  184.9 211.9 %all-to-all-start.2 = ((bf16[4,3,176,512]{3,2,1,0:T(8,128)(2,1)}), bf16[4,3,176,512]{3,2,1,0:T(8,128)(2,1)S(1)}, u32[]{:S(2)}, u32[]{:S(2)}) async-start(bf16[4,3,176,512]{3,2,1,0:T(8,128)(2,1)} %copy.338), calls=%async_computation.3 | async-start | bytes 4325376 | tf_op jit(solution)/shard_map/all_to_all | solution.py:245
  194.1 228.1 %reduce-scatter.13.cloned.1.call-start = ((), (), s32[]{:S(2)}) async-start(), calls=%async_computation.20 | async-start | bytes 1310720 | tf_op jit(solution)/shard_map/reduce_scatter | solution.py:393
  196.1 174.2 %copy-start.57 = (f32[128,64]{1,0:T(8,128)}, f32[128,64]{1,0:T(8,128)S(1)}, u32[]{:S(2)}) copy-start(f32[128,64]{1,0:T(8,128)S(1)} %get-tuple-element.386) | copy-start | bytes 98308
  334.7 35.6 %copy-start.22 = (bf16[128,2048]{1,0:T(8,128)(2,1)}, bf16[128,2048]{1,0:T(8,128)(2,1)S(1)}, u32[]{:S(2)}) copy-start(bf16[128,2048]{1,0:T(8,128)(2,1)S(1)} %multiply_convert_fusion) | copy-start | bytes 1572868
  396.7 71.8 %all-gather.35.cloned.1.call-start = ((), (), s32[]{:S(2)}) async-start(), calls=%async_computation.21 | async-start | bytes 6488064 | tf_op jit(solution)/shard_map/all_gather | solution.py:259
  398.8 115.7 %all-gather.37.cloned.1.call-start = ((), (), s32[]{:S(2)}) async-start(), calls=%async_computation.22 | async-start | bytes 6488064 | tf_op jit(solution)/shard_map/all_gather | solution.py:259
  400.9 159.5 %all-gather.39.cloned.1.call-start = ((), (), s32[]{:S(2)}) async-start(), calls=%async_computation.23 | async-start | bytes 6488064 | tf_op jit(solution)/shard_map/all_gather | solution.py:259
  402.0 188.7 %reduce-scatter.15.cloned.1.call-start = ((), (), s32[]{:S(2)}) async-start(), calls=%async_computation.24 | async-start | bytes 1310720 | tf_op jit(solution)/shard_map/reduce_scatter | solution.py:401
  437.3 82.7 %copy-start.24 = (bf16[128,2048]{1,0:T(8,128)(2,1)}, bf16[128,2048]{1,0:T(8,128)(2,1)S(1)}, u32[]{:S(2)}) copy-start(bf16[128,2048]{1,0:T(8,128)(2,1)S(1)} %all_gather.96) | copy-start | bytes 1572868
  473.1 46.8 %copy-start.56 = (f32[128,1408]{1,0:T(8,128)}, f32[128,1408]{1,0:T(8,128)S(1)}, u32[]{:S(2)}) copy-start(f32[128,1408]{1,0:T(8,128)S(1)} %fusion.352) | copy-start | bytes 2162692
  519.9 71.8 %copy-start.40 = (bf16[128,1408]{1,0:T(8,128)(2,1)}, bf16[128,1408]{1,0:T(8,128)(2,1)S(1)}, u32[]{:S(2)}) copy-start(bf16[128,1408]{1,0:T(8,128)(2,1)S(1)} %get-tuple-element.391) | copy-start | bytes 1081348
  565.1 109.7 %all-gather.31.cloned.1.call-start = ((), (), s32[]{:S(2)}) async-start(), calls=%async_computation.18 | async-start | bytes 4325376 | tf_op jit(solution)/shard_map/all_gather | solution.py:259
  565.6 173.4 %all-gather.41.cloned.1.call-start = ((), (), s32[]{:S(2)}) async-start(), calls=%async_computation.25 | async-start | bytes 4325376 | tf_op jit(solution)/shard_map/all_gather | solution.py:259
  598.3 55.1 %all-to-all-start.1 = ((bf16[8,1024,256]{2,1,0:T(8,128)(2,1)}), bf16[8,1024,256]{2,1,0:T(8,128)(2,1)}, u32[]{:S(2)}, u32[]{:S(2)}) async-start(bf16[8,1024,256]{2,1,0:T(8,128)(2,1)} %bitcast.467), calls=%async_computation.1 | async-start | bytes 8388608 | tf_op jit(solution)/shard_map/all_to_all | solution.py:245
  603.4 363.1 %reduce-scatter.17.cloned.1.call-start = ((), (), s32[]{:S(2)}) async-start(), calls=%async_computation.26 | async-start | bytes 9437184 | tf_op jit(solution)/shard_map/reduce_scatter | solution.py:432
  604.1 282.4 %copy-start.103 = (f32[1024]{0:T(1024)}, f32[1024]{0:T(1024)S(1)}, u32[]{:S(2)}) copy-start(f32[1024]{0:T(1024)S(1)} %get-tuple-element.220) | copy-start | bytes 12292
  604.1 275.3 %copy-start.101 = (f32[1024]{0:T(1024)}, f32[1024]{0:T(1024)S(1)}, u32[]{:S(2)}) copy-start(f32[1024]{0:T(1024)S(1)} %convert_bitcast_fusion.1) | copy-start | bytes 12292
  604.8 281.7 %copy-start.82 = (s32[1024]{0:T(1024)}, s32[1024]{0:T(1024)S(1)}, u32[]{:S(2)}) copy-start(s32[1024]{0:T(1024)S(1)} %subtract_bitcast_fusion) | copy-start | bytes 12292
  746.8 132.5 %copy-start.28 = (f32[1024,1024]{0,1:T(8,128)}, f32[1024,1024]{0,1:T(8,128)S(1)}, u32[]{:S(2)}) copy-start(f32[1024,1024]{0,1:T(8,128)S(1)} %get-tuple-element.394) | copy-start | bytes 12582916
  746.8 132.5 %copy-start.30 = (bf16[1024,8,256]{0,2,1:T(8,128)(2,1)S(1)}, bf16[1024,8,256]{0,2,1:T(8,128)(2,1)}, u32[]{:S(2)}) copy-start(bf16[1024,8,256]{0,2,1:T(8,128)(2,1)} %copy.325) | copy-start | bytes 12582916
  886.4 155.8 %reduce-scatter.23.cloned.1.call-start = ((), (), s32[]{:S(2)}) async-start(), calls=%async_computation.29 | async-start | bytes 9437184 | tf_op jit(solution)/shard_map/reduce_scatter | solution.py:432
  898.0 172.2 %copy-start.94 = (f32[32]{0:T(128)S(1)}, f32[32]{0:T(128)}, u32[]{:S(2)}) copy-start(f32[32]{0:T(128)} %copy-done.93) | copy-start | bytes 388
  898.0 174.0 %copy-start.110 = (f32[32]{0:T(128)S(1)}, f32[32]{0:T(128)}, u32[]{:S(2)}) copy-start(f32[32]{0:T(128)} %copy-done.109) | copy-start | bytes 388
  898.0 200.3 %copy-start.91 = (f32[32]{0:T(128)S(1)}, f32[32]{0:T(128)}, u32[]{:S(2)}) copy-start(f32[32]{0:T(128)} %copy-done.90) | copy-start | bytes 388
  898.1 172.2 %reduce-scatter.19.cloned.1.call-start = ((), (), s32[]{:S(2)}) async-start(), calls=%async_computation.27 | async-start | bytes 1310720 | tf_op jit(solution)/shard_map/reduce_scatter | solution.py:431
  966.5 131.8 %reduce-scatter.25.cloned.1.call-start = ((), (), s32[]{:S(2)}) async-start(), calls=%async_computation.30 | async-start | bytes 1310720 | tf_op jit(solution)/shard_map/reduce_scatter | solution.py:431
  1042.3 111.5 %reduce-scatter.21.cloned.1.call-start = ((), (), s32[]{:S(2)}) async-start(), calls=%async_computation.28 | async-start | bytes 1310720 | tf_op jit(solution)/shard_map/reduce_scatter | solution.py:453
  1070.2 47.5 %slice-start = ((s8[5767168]{0:T(1024)(128)(4,1)}), s8[1572864]{0:T(1024)(128)(4,1)S(1)}, s32[]{:S(2)}) async-start(s8[5767168]{0:T(1024)(128)(4,1)} %bitcast.459), calls=%async_computation.46 | async-start | bytes 3145728
  1123.6 64.3 %copy-start.6 = (f32[1,4,128,1024]{2,3,1,0:T(8,128)S(1)}, f32[1,4,128,1024]{2,3,1,0:T(8,128)}, u32[]{:S(2)}) copy-start(f32[1,4,128,1024]{2,3,1,0:T(8,128)} %copy-done.5) | copy-start | bytes 6291460
  1123.6 62.1 %all-gather.43.cloned.1.call-start = ((), (), s32[]{:S(2)}) async-start(), calls=%async_computation.31 | async-start | bytes 1310720 | tf_op jit(solution)/shard_map/all_gather | solution.py:462
  1158.1 57.1 %all-gather.61.cloned.1.call-start = ((), (), s32[]{:S(2)}) async-start(), calls=%async_computation.42 | async-start | bytes 1310720 | tf_op jit(solution)/shard_map/all_gather | solution.py:263
  1158.7 103.3 %all-gather.49.cloned.1.call-start = ((), (), s32[]{:S(2)}) async-start(), calls=%async_computation.34 | async-start | bytes 2621440 | tf_op jit(solution)/shard_map/all_gather | solution.py:259
  1193.8 164.3 %all-gather.63.cloned.1.call-start = ((), (), s32[]{:S(2)}) async-start(), calls=%async_computation.43 | async-start | bytes 9437184 | tf_op jit(solution)/shard_map/all_gather | solution.py:259
  1215.2 234.4 %reduce-scatter.27.cloned.1.call-start = ((), (), s32[]{:S(2)}) async-start(), calls=%async_computation.35 | async-start | bytes 9437184 | tf_op jit(solution)/shard_map/reduce_scatter | solution.py:514
  1277.4 207.5 %all-gather.47.cloned.1.call-start = ((), (), s32[]{:S(2)}) async-start(), calls=%async_computation.33 | async-start | bytes 1179648 | tf_op jit(solution)/shard_map/all_gather | solution.py:259
  1278.1 239.5 %all-gather.45.cloned.1.call-start = ((), (), s32[]{:S(2)}) async-start(), calls=%async_computation.32 | async-start | bytes 1179648 | tf_op jit(solution)/shard_map/all_gather | solution.py:259
  1281.8 278.6 %all-gather.53.cloned.1.call-start = ((), (), s32[]{:S(2)}) async-start(), calls=%async_computation.38 | async-start | bytes 4718592 | tf_op jit(solution)/shard_map/all_gather | solution.py:259
  1282.4 356.9 %all-gather.51.cloned.1.call-start = ((), (), s32[]{:S(2)}) async-start(), calls=%async_computation.37 | async-start | bytes 5406720 | tf_op jit(solution)/shard_map/all_gather | solution.py:540
  1311.9 366.3 %all-gather.55.cloned.1.call-start = ((), (), s32[]{:S(2)}) async-start(), calls=%async_computation.39 | async-start | bytes 4718592 | tf_op jit(solution)/shard_map/all_gather | solution.py:259
  1336.9 73.6 %all-to-all-start.6 = ((bf16[8,1024,256]{2,1,0:T(8,128)(2,1)}), bf16[8,1024,256]{2,1,0:T(8,128)(2,1)}, u32[]{:S(2)}, u32[]{:S(2)}) async-start(bf16[8,1024,256]{2,1,0:T(8,128)(2,1)} %bitcast.469), calls=%async_computation.15 | async-start | bytes 8388608 | tf_op jit(solution)/shard_map/all_to_all | solution.py:245
  1378.5 39.3 %copy-start.39 = (bf16[2,128,2048]{2,1,0:T(8,128)(2,1)S(1)}, bf16[2,128,2048]{2,1,0:T(8,128)(2,1)}, u32[]{:S(2)}) copy-start(bf16[2,128,2048]{2,1,0:T(8,128)(2,1)} %all-gather.43.cloned.1.call-done) | copy-start | bytes 3145732
  1410.5 29.2 %all-to-all-start.3 = ((bf16[8,2,128,256]{3,2,1,0:T(8,128)(2,1)}), bf16[8,2,128,256]{3,2,1,0:T(8,128)(2,1)S(1)}, u32[]{:S(2)}, u32[]{:S(2)}) async-start(bf16[8,2,128,256]{3,2,1,0:T(8,128)(2,1)} %maximum_bitcast_fusion.2), calls=%async_computation.10 | async-start | bytes 2097152 | tf_op jit(solution)/shard_map/all_to_all | solution.py:245
  1440.6 243.0 %all-to-all-start.5 = ((bf16[8,1024,256]{2,1,0:T(8,128)(2,1)}), bf16[8,1024,256]{2,1,0:T(8,128)(2,1)}, u32[]{:S(2)}, u32[]{:S(2)}) async-start(bf16[8,1024,256]{2,1,0:T(8,128)(2,1)} %bitcast.468), calls=%async_computation.14 | async-start | bytes 8388608 | tf_op jit(solution)/shard_map/all_to_all | solution.py:245
  1449.6 277.8 %reduce-scatter.29.cloned.1.call-start = ((), (), s32[]{:S(2)}) async-start(), calls=%async_computation.36 | async-start | bytes 1310720 | tf_op jit(solution)/shard_map/reduce_scatter | solution.py:515
  1465.8 55.3 %copy-start.79 = (f32[2048]{0:T(1024)S(1)}, f32[2048]{0:T(1024)}, u32[]{:S(2)}) copy-start(f32[2048]{0:T(1024)} %get-tuple-element.199) | copy-start | bytes 24580
  1486.6 155.2 %copy-start.8 = (f32[1,256,512]{2,1,0:T(8,128)}, f32[1,256,512]{2,1,0:T(8,128)S(1)}, u32[]{:S(2)}) copy-start(f32[1,256,512]{2,1,0:T(8,128)S(1)} %convolution_bitcast_fusion.7) | copy-start | bytes 1572868
  1641.8 38.9 %copy-start.11 = (f32[1,704,512]{2,1,0:T(8,128)}, f32[1,704,512]{2,1,0:T(8,128)S(1)}, u32[]{:S(2)}) copy-start(f32[1,704,512]{2,1,0:T(8,128)S(1)} %convolution_bitcast_fusion.4) | copy-start | bytes 4325380
  1644.9 38.7 %copy-start.13 = (f32[1,704,512]{2,1,0:T(8,128)}, f32[1,704,512]{2,1,0:T(8,128)S(1)}, u32[]{:S(2)}) copy-start(f32[1,704,512]{2,1,0:T(8,128)S(1)} %convolution_bitcast_fusion.3) | copy-start | bytes 4325380
  1683.6 48.7 %copy-start.35 = (bf16[2,256,512]{2,1,0:T(8,128)(2,1)S(1)}, bf16[2,256,512]{2,1,0:T(8,128)(2,1)}, u32[]{:S(2)}) copy-start(bf16[2,256,512]{2,1,0:T(8,128)(2,1)} %fusion.260) | copy-start | bytes 1572868
  1725.9 50.9 %copy-start.17 = (f32[1,1,704,512]{3,1,2,0:T(1,128)S(1)}, f32[1,1,704,512]{3,1,2,0:T(1,128)}, u32[]{:S(2)}) copy-start(f32[1,1,704,512]{3,1,2,0:T(1,128)} %copy.415) | copy-start | bytes 4325380
  1725.9 50.9 %copy-start.18 = (f32[1,1,704,512]{3,1,2,0:T(1,128)S(1)}, f32[1,1,704,512]{3,1,2,0:T(1,128)}, u32[]{:S(2)}) copy-start(f32[1,1,704,512]{3,1,2,0:T(1,128)} %copy.416) | copy-start | bytes 4325380
  1787.4 175.3 %all-to-all-start.7 = ((f32[4,1,360448]{2,1,0:T(1,128)}), f32[4,1,360448]{2,1,0:T(1,128)}, u32[]{:S(2)}, u32[]{:S(2)}) async-start(f32[4,1,360448]{2,1,0:T(1,128)} %all_to_all.42), calls=%async_computation.16 | async-start | bytes 11534336 | tf_op jit(solution)/shard_map/all_to_all | solution.py:245
  1793.0 177.2 %all-gather.65.cloned.1.call-start = ((), (), s32[]{:S(2)}) async-start(), calls=%async_computation.44 | async-start | bytes 3604480 | tf_op jit(solution)/shard_map/all_gather | solution.py:548
  2134.1 69.0 %all-to-all-start.8 = ((bf16[4,2,180224]{2,1,0:T(2,128)(2,1)}), bf16[4,2,180224]{2,1,0:T(2,128)(2,1)S(1)}, u32[]{:S(2)}, u32[]{:S(2)}) async-start(bf16[4,2,180224]{2,1,0:T(2,128)(2,1)} %reshape.1392), calls=%async_computation.17 | async-start | bytes 5767168 | tf_op jit(solution)/shard_map/all_to_all | solution.py:245
  2203.1 34.3 %slice-start.2 = ((s8[4325376]{0:T(1024)(128)(4,1)}), s8[131072]{0:T(1024)(128)(4,1)S(1)}, s32[]{:S(2)}) async-start(s8[4325376]{0:T(1024)(128)(4,1)} %bitcast.463), calls=%async_computation.48 | async-start | bytes 262144
  (89 other events, 691.6 us)
Sparse Core Ops, SparseCore 0:
  20.7 40.7 all-gather.32
  179.3 152.8 all-reduce.6
  334.7 28.3 all-gather.56
  365.4 27.8 all-gather.58
  396.9 25.3 reduce-scatter.12
  424.8 43.6 all-gather.34
  471.1 43.3 all-gather.36
  517.1 43.3 all-gather.38
  565.2 25.3 reduce-scatter.14
  594.0 80.7 all-gather.30
  678.3 60.6 all-gather.40
  886.5 79.8 reduce-scatter.16
  970.9 71.2 reduce-scatter.22
  1044.4 25.8 reduce-scatter.18
  1072.5 25.7 reduce-scatter.24
  1123.7 29.9 reduce-scatter.20
  1158.2 27.3 all-gather.42
  1187.7 27.4 all-gather.60
  1217.4 44.5 all-gather.48
  1263.9 62.7 all-gather.62
  1331.1 113.3 reduce-scatter.26
  1446.4 38.4 all-gather.46
  1487.4 30.2 all-gather.44
  1519.4 37.1 all-gather.52
  1558.1 81.1 all-gather.50
  1641.0 37.1 all-gather.54
  1680.3 25.3 reduce-scatter.28
  1796.0 106.8 all-gather.64

commit v2 on v1

--- a/solution.py
+++ b/solution.py
@@ -82,6 +82,640 @@
 
 def unrotate(values, cosine, sine):
     return rotate(values, cosine, -sine)
+
+
+MESH = pl.DeviceIdType.MESH
+ANY = pl.BlockSpec(memory_space=pl.ANY)
+VMEM = pl.BlockSpec(memory_space=pltpu.VMEM)
+
+
+def greet(targets):
+    barrier = pltpu.get_barrier_semaphore()
+    for target in targets:
+        pl.semaphore_signal(barrier, inc=1, device_id=target, device_id_type=MESH)
+    pl.semaphore_wait(barrier, len(targets))
+
+
+def others(axis, count):
+    me = lax.axis_index(axis)
+    return [{axis: lax.rem(me + step, count)} for step in range(1, count)]
+
+
+def push(source, target, send, receive, device):
+    return pltpu.make_async_remote_copy(
+        src_ref=source,
+        dst_ref=target,
+        send_sem=send,
+        recv_sem=receive,
+        device_id=device,
+        device_id_type=MESH,
+    )
+
+
+def call_kernel(body, ident, inputs, outputs, scratch, name, in_place=None, out_place=None):
+    in_specs = [VMEM if in_place is None else in_place[i] for i in range(len(inputs))]
+    out_specs = [VMEM if out_place is None else out_place[i] for i in range(len(outputs))]
+    size = sum(a.size * a.dtype.itemsize for a in list(inputs) + list(outputs))
+    return pl.pallas_call(
+        body,
+        out_shape=outputs,
+        in_specs=in_specs,
+        out_specs=out_specs,
+        scratch_shapes=scratch,
+        compiler_params=pltpu.CompilerParams(
+            collective_id=ident, has_side_effects=True, vmem_limit_bytes=VMEM_BYTES
+        ),
+        cost_estimate=pl.CostEstimate(flops=0, bytes_accessed=8 * size, transcendentals=0),
+        name=name,
+    )(*inputs)
+
+
+def gather_wide_body(count, x_ref, out_ref, send, receive, local):
+    me = lax.axis_index("wide")
+    mate = me + 1 - 2 * lax.rem(me, 2)
+    chips = count // 2
+    peers = [lax.rem(me + 2 * step, count) for step in range(1, chips)]
+    greet([{"wide": mate}] + [{"wide": peer} for peer in peers])
+    keep = pltpu.make_async_copy(x_ref, out_ref.at[me], local)
+    keep.start()
+    first = []
+    for step, peer in enumerate(peers + [mate]):
+        copy = push(x_ref, out_ref.at[me], send.at[step], receive.at[me], {"wide": peer})
+        copy.start()
+        first.append(copy)
+    second = []
+    for step in range(1, chips):
+        source = lax.rem(me - 2 * step + count, count)
+        block = out_ref.at[source]
+        push(block, block, send.at[0], receive.at[source], {"wide": mate}).wait_recv()
+        copy = push(block, block, send.at[chips + step - 1], receive.at[source], {"wide": mate})
+        copy.start()
+        second.append(copy)
+    for step in range(chips):
+        source = lax.rem(mate - 2 * step + count, count)
+        block = out_ref.at[source]
+        push(block, block, send.at[0], receive.at[source], {"wide": mate}).wait_recv()
+    for copy in first + second:
+        copy.wait_send()
+    keep.wait()
+
+
+def gather_wide(values, ident, name):
+    count = lax.axis_size("wide")
+    return call_kernel(
+        functools.partial(gather_wide_body, count),
+        ident,
+        [values],
+        [jax.ShapeDtypeStruct((count,) + values.shape, values.dtype)],
+        [
+            pltpu.SemaphoreType.DMA((count - 1,)),
+            pltpu.SemaphoreType.DMA((count,)),
+            pltpu.SemaphoreType.DMA,
+        ],
+        name,
+        [ANY],
+        [ANY],
+    )[0]
+
+
+def trade_body(count, splits, *refs):
+    inputs = refs[: len(splits)]
+    outputs = refs[len(splits) : 2 * len(splits)]
+    send, receive, local = refs[2 * len(splits) :]
+    me = lax.axis_index("narrow")
+    greet(others("narrow", count))
+    copies = []
+    for at, split in enumerate(splits):
+        for step in range(1, count):
+            peer = lax.rem(me + step, count)
+            source = inputs[at].at[peer] if split else inputs[at]
+            copy = push(
+                source,
+                outputs[at].at[me],
+                send.at[at, step - 1],
+                receive.at[at, me],
+                {"narrow": peer},
+            )
+            copy.start()
+            copies.append(copy)
+    keeps = []
+    for at, split in enumerate(splits):
+        keep = pltpu.make_async_copy(
+            inputs[at].at[me] if split else inputs[at], outputs[at].at[me], local.at[at]
+        )
+        keep.start()
+        keeps.append(keep)
+    for at in range(len(splits)):
+        for step in range(1, count):
+            source = lax.rem(me - step + count, count)
+            block = outputs[at].at[source]
+            push(
+                block, block, send.at[at, 0], receive.at[at, source], {"narrow": source}
+            ).wait_recv()
+    for copy in copies:
+        copy.wait_send()
+    for keep in keeps:
+        keep.wait()
+
+
+def trade(values, splits, ident, name):
+    count = lax.axis_size("narrow")
+    shapes = [a.shape if split else (count,) + a.shape for a, split in zip(values, splits)]
+    return call_kernel(
+        functools.partial(trade_body, count, splits),
+        ident,
+        values,
+        [jax.ShapeDtypeStruct(shape, a.dtype) for shape, a in zip(shapes, values)],
+        [
+            pltpu.SemaphoreType.DMA((len(values), count - 1)),
+            pltpu.SemaphoreType.DMA((len(values), count)),
+            pltpu.SemaphoreType.DMA((len(values),)),
+        ],
+        name,
+        [ANY] * len(values),
+        [ANY] * len(values),
+    )
+
+
+def collect(count, parts_ref, slots, send, receive):
+    me = lax.axis_index("narrow")
+    copies = []
+    for step in range(1, count):
+        peer = lax.rem(me + step, count)
+        copy = push(
+            parts_ref.at[peer],
+            slots.at[me],
+            send.at[step - 1],
+            receive.at[me],
+            {"narrow": peer},
+        )
+        copy.start()
+        copies.append(copy)
+    total = parts_ref[me]
+    for step in range(1, count):
+        source = lax.rem(me - step + count, count)
+        block = slots.at[source]
+        push(block, block, send.at[0], receive.at[source], {"narrow": source}).wait_recv()
+        total = total + slots[source]
+    return total, copies
+
+
+def share(count, low, all_ref, send, receive):
+    me = lax.axis_index("narrow")
+    all_ref[me] = low
+    copies = []
+    for step in range(1, count):
+        peer = lax.rem(me + step, count)
+        copy = push(
+            all_ref.at[me], all_ref.at[me], send.at[step - 1], receive.at[me], {"narrow": peer}
+        )
+        copy.start()
+        copies.append(copy)
+    for step in range(1, count):
+        source = lax.rem(me - step + count, count)
+        block = all_ref.at[source]
+        push(block, block, send.at[0], receive.at[source], {"narrow": source}).wait_recv()
+    return copies
+
+
+def settle_body(
+    count, parts_ref, base_ref, other_ref, keep_ref, gain_ref, own_ref, all_ref, slots, *sems
+):
+    send, receive, send_all, receive_all = sems
+    greet(others("narrow", count))
+    total, copies = collect(count, parts_ref, slots, send, receive)
+    total = jnp.where(keep_ref[...] > 0, total + base_ref[...], other_ref[...])
+    own_ref[...] = total
+    low = norm_rows(total, gain_ref[...]).astype(LOW)
+    copies = copies + share(count, low, all_ref, send_all, receive_all)
+    for copy in copies:
+        copy.wait_send()
+
+
+def narrow_sems(count):
+    return [
+        pltpu.SemaphoreType.DMA((count - 1,)),
+        pltpu.SemaphoreType.DMA((count,)),
+    ]
+
+
+def settle(partial, base, other, keep_row, gain_row, ident, name):
+    count = lax.axis_size("narrow")
+    rows, width = base.shape
+    own, shared = call_kernel(
+        functools.partial(settle_body, count),
+        ident,
+        [partial.reshape(count, rows, width), base, other, keep_row, gain_row],
+        [
+            jax.ShapeDtypeStruct((rows, width), FULL),
+            jax.ShapeDtypeStruct((count, rows, width), LOW),
+        ],
+        [pltpu.VMEM((count, rows, width), FULL)] + narrow_sems(count) + narrow_sems(count),
+        name,
+    )
+    return own, shared.reshape(count * rows, width)
+
+
+def settle_back_body(
+    count,
+    parts_ref,
+    values_ref,
+    add_ref,
+    keep_ref,
+    gain_ref,
+    own_ref,
+    gain_grad_ref,
+    all_ref,
+    slots,
+    *sems
+):
+    send, receive, send_all, receive_all = sems
+    greet(others("narrow", count))
+    grad, copies = collect(count, parts_ref, slots, send, receive)
+    values = values_ref[...]
+    root = lax.rsqrt(jnp.mean(values * values, axis=-1, keepdims=True) + NORM_EPS)
+    scaled = gain_ref[...] * grad
+    inner = jnp.mean(values * scaled, axis=-1, keepdims=True)
+    own = add_ref[...] + root * scaled - values * (root * root * root * inner)
+    gain_grad_ref[...] = jnp.sum(values * root * grad, axis=0, keepdims=True)
+    own_ref[...] = own
+    low = (own * keep_ref[...]).astype(LOW)
+    copies = copies + share(count, low, all_ref, send_all, receive_all)
+    for copy in copies:
+        copy.wait_send()
+
+
+def settle_back(partial, values, add, keep_row, gain_row, ident, name):
+    count = lax.axis_size("narrow")
+    rows, width = values.shape
+    own, gain_grad, shared = call_kernel(
+        functools.partial(settle_back_body, count),
+        ident,
+        [partial.reshape(count, rows, width), values, add, keep_row, gain_row],
+        [
+            jax.ShapeDtypeStruct((rows, width), FULL),
+            jax.ShapeDtypeStruct((1, width), FULL),
+            jax.ShapeDtypeStruct((count, rows, width), LOW),
+        ],
+        [pltpu.VMEM((count, rows, width), FULL)] + narrow_sems(count) + narrow_sems(count),
+        name,
+    )
+    return own, gain_grad[0], shared.reshape(count * rows, width)
+
+
+def fetch_rows_body(deep, wide, found_ref, out_ref, rightward, leftward, final, *sems):
+    send_right, receive_right, send_left, receive_left, send_wide, receive_wide, local = sems
+    spot = lax.axis_index("narrow")
+    me = lax.axis_index("wide")
+    columns = found_ref.shape[2]
+    rows = out_ref.shape[0]
+    greet(others("narrow", deep) + others("wide", wide))
+
+    def right_copy(part, source):
+        return push(
+            source,
+            rightward.at[part],
+            send_right.at[part],
+            receive_right.at[part],
+            {"narrow": lax.rem(spot + 1, deep)},
+        )
+
+    def left_copy(part, source):
+        return push(
+            source,
+            leftward.at[part],
+            send_left.at[part],
+            receive_left.at[part],
+            {"narrow": lax.rem(spot + deep - 1, deep)},
+        )
+
+    for step in range(deep - 1):
+        right, left = deep - 1 - step, step
+
+        @pl.when((spot == 0) & (right > 0))
+        def _():
+            right_copy(right, found_ref.at[right]).start()
+
+        @pl.when((spot == deep - 1) & (left < deep - 1))
+        def _():
+            left_copy(left, found_ref.at[left]).start()
+
+        @pl.when((spot > 0) & (right > spot))
+        def _():
+            right_copy(right, rightward.at[right]).wait_recv()
+            rightward[right] = rightward[right] + found_ref[right]
+            right_copy(right, rightward.at[right]).start()
+
+        @pl.when((spot < deep - 1) & (left < spot))
+        def _():
+            left_copy(left, leftward.at[left]).wait_recv()
+            leftward[left] = leftward[left] + found_ref[left]
+            left_copy(left, leftward.at[left]).start()
+
+    final[...] = found_ref[spot]
+
+    @pl.when(spot > 0)
+    def _():
+        right_copy(spot, rightward.at[spot]).wait_recv()
+        final[...] = final[...] + rightward[spot]
+
+    @pl.when(spot < deep - 1)
+    def _():
+        left_copy(spot, leftward.at[spot]).wait_recv()
+        final[...] = final[...] + leftward[spot]
+
+    mine = pl.ds(pl.multiple_of(me * columns, columns), columns)
+    copies = []
+    for step in range(1, wide):
+        peer = lax.rem(me + step, wide)
+        copy = push(
+            final.at[pl.ds(pl.multiple_of(peer * rows, rows), rows)],
+            out_ref.at[:, mine],
+            send_wide.at[step - 1],
+            receive_wide.at[me],
+            {"wide": peer},
+        )
+        copy.start()
+        copies.append(copy)
+    keep = pltpu.make_async_copy(
+        final.at[pl.ds(pl.multiple_of(me * rows, rows), rows)], out_ref.at[:, mine], local
+    )
+    keep.start()
+    for step in range(1, wide):
+        source = lax.rem(me - step + wide, wide)
+        block = out_ref.at[:, pl.ds(pl.multiple_of(source * columns, columns), columns)]
+        push(block, block, send_wide.at[0], receive_wide.at[source], {"wide": source}).wait_recv()
+    for copy in copies:
+        copy.wait_send()
+    keep.wait()
+    for step in range(deep - 1):
+        right, left = deep - 1 - step, step
+
+        @pl.when(right > spot)
+        def _():
+            right_copy(right, found_ref.at[right]).wait_send()
+
+        @pl.when(left < spot)
+        def _():
+            left_copy(left, found_ref.at[left]).wait_send()
+
+
+def fetch_rows(found, rows, ident, name):
+    deep, wide = lax.axis_size("narrow"), lax.axis_size("wide")
+    columns = found.shape[2]
+    return call_kernel(
+        functools.partial(fetch_rows_body, deep, wide),
+        ident,
+        [found],
+        [jax.ShapeDtypeStruct((rows, wide * columns), found.dtype)],
+        [pltpu.VMEM(found.shape, found.dtype)] * 2
+        + [pltpu.VMEM(found.shape[1:], found.dtype)]
+        + [pltpu.SemaphoreType.DMA((deep,))] * 4
+        + [
+            pltpu.SemaphoreType.DMA((wide - 1,)),
+            pltpu.SemaphoreType.DMA((wide,)),
+            pltpu.SemaphoreType.DMA,
+        ],
+        name,
+        None,
+        [ANY],
+    )[0]
+
+
+def return_rows_body(deep, wide, rows_ref, out_ref, *sems):
+    send_right, send_left, receive_deep, send_wide, receive_wide, local = sems
+    spot = lax.axis_index("narrow")
+    me = lax.axis_index("wide")
+    columns = out_ref.shape[2]
+    rows = rows_ref.shape[0]
+    greet(others("narrow", deep) + others("wide", wide))
+    mine = out_ref.at[spot, pl.ds(pl.multiple_of(me * rows, rows), rows)]
+
+    def part_of(device):
+        return rows_ref.at[:, pl.ds(pl.multiple_of(device * columns, columns), columns)]
+
+    copies = []
+    for step in range(1, wide):
+        peer = lax.rem(me + step, wide)
+        copy = push(
+            part_of(peer), mine, send_wide.at[step - 1], receive_wide.at[me], {"wide": peer}
+        )
+        copy.start()
+        copies.append(copy)
+    keep = pltpu.make_async_copy(part_of(me), mine, local)
+    keep.start()
+    for step in range(1, wide):
+        source = lax.rem(me - step + wide, wide)
+        block = out_ref.at[spot, pl.ds(pl.multiple_of(source * rows, rows), rows)]
+        push(block, block, send_wide.at[0], receive_wide.at[source], {"wide": source}).wait_recv()
+    keep.wait()
+
+    def right_copy(part):
+        return push(
+            out_ref.at[part],
+            out_ref.at[part],
+            send_right.at[part],
+            receive_deep.at[part],
+            {"narrow": lax.rem(spot + 1, deep)},
+        )
+
+    def left_copy(part):
+        return push(
+            out_ref.at[part],
+            out_ref.at[part],
+            send_left.at[part],
+            receive_deep.at[part],
+            {"narrow": lax.rem(spot + deep - 1, deep)},
+        )
+
+    @pl.when(spot < deep - 1)
+    def _():
+        right_copy(spot).start()
+
+    @pl.when(spot > 0)
+    def _():
+        left_copy(spot).start()
+
+    for step in range(1, deep):
+
+        @pl.when(spot >= step)
+        def _():
+            right_copy(spot - step).wait_recv()
+
+            @pl.when(spot < deep - 1)
+            def _():
+                right_copy(spot - step).start()
+
+        @pl.when(spot + step < deep)
+        def _():
+            left_copy(spot + step).wait_recv()
+
+            @pl.when(spot > 0)
+            def _():
+                left_copy(spot + step).start()
+
+    for part in range(deep):
+
+        @pl.when((part <= spot) & (spot < deep - 1))
+        def _():
+            right_copy(part).wait_send()
+
+        @pl.when((part >= spot) & (spot > 0))
+        def _():
+            left_copy(part).wait_send()
+
+    for copy in copies:
+        copy.wait_send()
+
+
+def return_rows(rows, ident, name):
+    deep, wide = lax.axis_size("narrow"), lax.axis_size("wide")
+    count, width = rows.shape
+    return call_kernel(
+        functools.partial(return_rows_body, deep, wide),
+        ident,
+        [rows],
+        [jax.ShapeDtypeStruct((deep, wide * count, width // wide), rows.dtype)],
+        [pltpu.SemaphoreType.DMA((deep,))] * 3
+        + [
+            pltpu.SemaphoreType.DMA((wide - 1,)),
+            pltpu.SemaphoreType.DMA((wide,)),
+            pltpu.SemaphoreType.DMA,
+        ],
+        name,
+        [ANY],
+        [ANY],
+    )[0]
+
+
+def sum_wide_body(count, parts_ref, out_ref, from_mate, paired, slots, *sems):
+    send_mate, receive_mate, send, receive = sems
+    me = lax.axis_index("wide")
+    side = lax.rem(me, 2)
+    mate = me + 1 - 2 * side
+    chips = count // 2
+    my_chip = me // 2
+    greet([{"wide": mate}] + [{"wide": lax.rem(me + 2 * s, count)} for s in range(1, chips)])
+    mate_copies = []
+    for step in range(chips):
+        chip = lax.rem(my_chip + 1 + step, chips)
+        copy = push(
+            parts_ref.at[2 * chip + 1 - side],
+            from_mate.at[chip],
+            send_mate.at[step],
+            receive_mate.at[chip],
+            {"wide": mate},
+        )
+        copy.start()
+        mate_copies.append(copy)
+    copies = []
+    for step in range(chips):
+        chip = lax.rem(my_chip + 1 + step, chips)
+        block = from_mate.at[chip]
+        push(block, block, send_mate.at[0], receive_mate.at[chip], {"wide": mate}).wait_recv()
+        both = parts_ref[2 * chip + side].astype(FULL) + from_mate[chip].astype(FULL)
+        if step < chips - 1:
+            paired[chip] = both.astype(LOW)
+            copy = push(
+                paired.at[chip],
+                slots.at[my_chip],
+                send.at[step],
+                receive.at[my_chip],
+                {"wide": 2 * chip + side},
+            )
+            copy.start()
+            copies.append(copy)
+        else:
+            out_ref[...] = both
+    for step in range(1, chips):
+        chip = lax.rem(my_chip - step + chips, chips)
+        block = slots.at[chip]
+        push(block, block, send.at[0], receive.at[chip], {"wide": 2 * chip + side}).wait_recv()
+        out_ref[...] = out_ref[...] + slots[chip].astype(FULL)
+    for copy in mate_copies + copies:
+        copy.wait_send()
+
+
+def sum_wide(partial, ident, name):
+    count = lax.axis_size("wide")
+    chips = count // 2
+    rows, width = partial.shape[0] // count, partial.shape[1]
+    return call_kernel(
+        functools.partial(sum_wide_body, count),
+        ident,
+        [partial.reshape(count, rows, width)],
+        [jax.ShapeDtypeStruct((rows, width), FULL)],
+        [pltpu.VMEM((chips, rows, width), LOW)] * 3
+        + [
+            pltpu.SemaphoreType.DMA((chips,)),
+            pltpu.SemaphoreType.DMA((chips,)),
+            pltpu.SemaphoreType.DMA((max(chips - 1, 1),)),
+            pltpu.SemaphoreType.DMA((chips,)),
+        ],
+        name,
+    )[0]
+
+
+def merge_two(first, second):
+    peak = jnp.maximum(first[0:1], second[0:1])
+    total = first[1:2] * jnp.exp(first[0:1] - peak) + second[1:2] * jnp.exp(second[0:1] - peak)
+    return jnp.concatenate([peak, total, first[2:] + second[2:]], axis=0)
+
+
+def add_two(first, second):
+    return first + second
+
+
+def combine_body(deep, wide, join, x_ref, out_ref, wide_slots, deep_slots, *sems):
+    send_wide, receive_wide, send_deep, receive_deep = sems
+    me = lax.axis_index("wide")
+    spot = lax.axis_index("narrow")
+    greet(others("narrow", deep) + others("wide", wide))
+
+    def round_of(axis, at, count, slots, send, receive):
+        copies = []
+        for step in range(1, count):
+            peer = lax.rem(at + step, count)
+            copy = push(
+                slots.at[at], slots.at[at], send.at[step - 1], receive.at[at], {axis: peer}
+            )
+            copy.start()
+            copies.append(copy)
+        for step in range(1, count):
+            source = lax.rem(at - step + count, count)
+            block = slots.at[source]
+            push(block, block, send.at[0], receive.at[source], {axis: source}).wait_recv()
+        total = slots[0]
+        for source in range(1, count):
+            total = join(total, slots[source])
+        return total, copies
+
+    wide_slots[me] = x_ref[...]
+    total, first = round_of("wide", me, wide, wide_slots, send_wide, receive_wide)
+    deep_slots[spot] = total
+    total, second = round_of("narrow", spot, deep, deep_slots, send_deep, receive_deep)
+    out_ref[...] = total
+    for copy in first + second:
+        copy.wait_send()
+
+
+def combine(values, join, ident, name):
+    deep, wide = lax.axis_size("narrow"), lax.axis_size("wide")
+    return call_kernel(
+        functools.partial(combine_body, deep, wide, join),
+        ident,
+        [values],
+        [jax.ShapeDtypeStruct(values.shape, values.dtype)],
+        [
+            pltpu.VMEM((wide,) + values.shape, values.dtype),
+            pltpu.VMEM((deep,) + values.shape, values.dtype),
+            pltpu.SemaphoreType.DMA((wide - 1,)),
+            pltpu.SemaphoreType.DMA((wide,)),
+            pltpu.SemaphoreType.DMA((deep - 1,)),
+            pltpu.SemaphoreType.DMA((deep,)),
+        ],
+        name,
+    )[0]
 
 
 def lookup_body(ids_ref, table_ref, out_ref, held, rows, sem):
@@ -291,33 +925,48 @@
     vocab_rows, columns = embed.shape
     width = columns * wide_count
     own_rows = sel // narrow_count
+    tok_rows = seq_len // narrow_count
+    all_rows = own_rows + tok_rows
     heads_own = HEADS // narrow_count
     repeat = max(1, narrow_count // KVH)
+    groups = KVH * repeat // narrow_count
     ffn_rows = ffn.shape[0]
     lens = lengths[0]
     pick_ids = picks[0]
     keep_layer = (1 - skip[0]).astype(FULL)
-
-    all_ints = gather_rows(
-        jnp.concatenate([tokens[0], targets[0]])[None], "wide"
-    )
-    tokens_all = all_ints[:, :seq_len].reshape(-1)
-    targets_all = all_ints[:, seq_len:].reshape(-1)
-    gain_w = gather_columns(gains.astype(LOW), BOTH).astype(FULL)
-
-    local_ids = tokens_all - narrow_spot * vocab_rows
+    keep_row = jnp.full((1, width), keep_layer)
+    always_row = jnp.ones((1, width), FULL)
+
+    where_at = jnp.arange(seq_len, dtype=jnp.int32)
+    pick_tokens = jnp.sum(
+        jnp.where(pick_ids[:, None] == where_at[None, :], tokens[0][None, :], 0), axis=1
+    )
+    ints = jnp.concatenate([tokens[0], pick_tokens, targets[0]])
+    lanes = 128
+    height = -(-ints.shape[0] // (8 * lanes)) * 8
+    ints_box = jnp.pad(ints, (0, height * lanes - ints.shape[0])).reshape(height, lanes)
+    all_ints = gather_wide(ints_box, 0, "gather_ids").reshape(wide_count, -1)
+    tokens_all = all_ints[:, :seq_len].reshape(wide_count, narrow_count, tok_rows)
+    picked_all = all_ints[:, seq_len : seq_len + sel].reshape(wide_count, narrow_count, own_rows)
+    targets_all = all_ints[:, seq_len + sel : seq_len + 2 * sel].reshape(-1)
+    wanted = jnp.moveaxis(jnp.concatenate([tokens_all, picked_all], axis=2), 1, 0).reshape(-1)
+
+    local_ids = wanted - narrow_spot * vocab_rows
     inside = (local_ids >= 0) & (local_ids < vocab_rows)
     spots = jnp.where(inside, local_ids, vocab_rows)
     found = lookup(embed, spots)
-    hidden_rows = side_by_side(exchange(found.reshape(wide_count, seq_len, columns), "wide"))
-
+    rows_low = fetch_rows(
+        found.reshape(narrow_count, wide_count * all_rows, columns), all_rows, 1, "fetch_rows"
+    )
+
+    gain_w = gather_columns(gains.astype(LOW), BOTH).astype(FULL)
     kv_low = jnp.moveaxis(attn_kv, 1, 0).astype(LOW)
     kv_w = lax.all_gather(
         lax.all_gather(kv_low, "narrow", axis=2, tiled=True), "wide", axis=1, tiled=True
     )
     qo_low = jnp.moveaxis(attn_qo, 1, 0).astype(LOW)
-    q_w = gather_rows(qo_low[0], "wide")
-    o_w = gather_rows(qo_low[1], "wide")
+    qo_w = lax.all_gather(qo_low, "wide", axis=1, tiled=True)
+    q_w, o_w = qo_w[0], qo_w[1]
     ffn_low = jnp.moveaxis(ffn, 1, 0).astype(LOW)
     ffn_cut = ffn_low.reshape(3, narrow_count, ffn_rows // narrow_count, ffn_low.shape[2])
     ffn_sub = exchange(jnp.moveaxis(ffn_cut, 1, 0), "narrow")
@@ -325,7 +974,6 @@
     table_own = side_by_side(
         exchange(embed.astype(LOW).reshape(wide_count, vocab_rows // wide_count, columns), "wide")
     )
-    q_full = gather_rows(gather_columns(qo_low[0], "narrow"), "wide")
 
     mom_qo = jnp.moveaxis(attn_qo_mom, 1, 0)
     mom_kv = jnp.moveaxis(attn_kv_mom, 1, 0)
@@ -351,34 +999,32 @@
 
     mom_owned = exchange(one_per_owner(mom_ffn, mom_qo, mom_kv), "narrow")
 
-    seg_all, cosine_all, sine_all = angles_at(lens, jnp.arange(seq_len, dtype=jnp.int32))
+    tok_at = narrow_spot * tok_rows + jnp.arange(tok_rows, dtype=jnp.int32)
+    seg_all = segments_at(lens, where_at)
+    _, cosine_tok, sine_tok = angles_at(lens, tok_at)
     seg_mine, cosine, sine = angles_at(lens, pick_ids)
-    inside_mine = lax.dynamic_slice_in_dim(inside, wide_spot * seq_len, seq_len, 0)
-    pick_hot = (
-        pick_ids[:, None] == jnp.arange(seq_len, dtype=jnp.int32)[None, :]
-    ).astype(LOW)
-
-    rows_full = hidden_rows.astype(FULL)
+
+    rows_full = rows_low.astype(FULL)
     normed_all = norm_rows(rows_full, gain_w[0]).astype(LOW)
-    keys_part = dot(normed_all, kv_w[0], 1, 0).reshape(seq_len, KVH, HD)
-    keys_part = rotate(keys_part, cosine_all[:, None], sine_all[:, None]).astype(LOW)
-    values_part = dot(normed_all, kv_w[1], 1, 0).reshape(seq_len, KVH, HD).astype(LOW)
+    normed_tok, normed_own = normed_all[:tok_rows], normed_all[tok_rows:]
+    start_own = rows_full[tok_rows:]
+    keys_part = dot(normed_tok, kv_w[0], 1, 0).reshape(tok_rows, KVH, HD)
+    keys_part = rotate(keys_part, cosine_tok[:, None], sine_tok[:, None]).astype(LOW)
+    values_part = dot(normed_tok, kv_w[1], 1, 0).reshape(tok_rows, KVH, HD).astype(LOW)
     by_head = jnp.moveaxis(jnp.stack([keys_part, values_part]), 2, 0)
     by_head = jnp.repeat(by_head, repeat, axis=0)
-    own_head = lax.psum_scatter(by_head, "narrow", scatter_dimension=0, tiled=True)
-    groups = own_head.shape[0]
-    keys, values = own_head[:, 0], own_head[:, 1]
-    start_h = lax.psum(dot(pick_hot, hidden_rows, 1, 0).astype(LOW), "narrow").astype(FULL)
-
-    normed = norm_rows(start_h, gain_w[0]).astype(LOW)
+    by_head = by_head.reshape(narrow_count, groups, 2, tok_rows, HD)
+    own_head, normed_parts = trade([by_head, normed_own], (True, False), 2, "trade_heads")
+    own_head = jnp.transpose(own_head, (2, 1, 0, 3, 4)).reshape(2, groups, seq_len, HD)
+    keys, values = own_head[0], own_head[1]
+    normed = normed_parts.reshape(sel, width)
+
     queries = dot(normed, q_w, 1, 0).reshape(sel, heads_own, HD)
     queries = rotate(queries, cosine[:, None], sine[:, None]).astype(LOW)
     grouped = queries.reshape(sel, groups, heads_own // groups, HD)
     scale = HD ** (-0.5)
     scores = jnp.einsum("tkgd,ksd->kgts", grouped, keys, preferred_element_type=FULL) * scale
-    allowed = (seg_mine[:, None] == seg_all[None, :]) & (
-        pick_ids[:, None] >= jnp.arange(seq_len, dtype=jnp.int32)[None, :]
-    )
+    allowed = (seg_mine[:, None] == seg_all[None, :]) & (pick_ids[:, None] >= where_at[None, :])
     scores = jnp.where(allowed, scores, MASKED)
     shifted_exp = jnp.exp(scores - jnp.max(scores, axis=-1, keepdims=True))
     probs = shifted_exp / jnp.sum(shifted_exp, axis=-1, keepdims=True)
@@ -386,83 +1032,80 @@
     mixed = jnp.einsum("kgts,ksd->tkgd", probs_low, values, preferred_element_type=FULL)
     mixed = mixed.reshape(sel, heads_own * HD).astype(LOW)
 
-    def own(values_all):
-        return lax.dynamic_slice_in_dim(values_all, narrow_spot * own_rows, own_rows, 0)
-
-    start_own = own(start_h)
-    middle = start_own + lax.psum_scatter(
-        dot(mixed, o_w, 1, 1), "narrow", scatter_dimension=0, tiled=True
-    )
-    inner_own = norm_rows(middle, gain_w[1]).astype(LOW)
-    inner = gather_rows(inner_own, "narrow")
+    middle, inner = settle(
+        dot(mixed, o_w, 1, 1), start_own, start_own, always_row, gain_w[1:2], 3, "settle"
+    )
     gate = dot(inner, ffn_w[0], 1, 1)
     up = dot(inner, ffn_w[1], 1, 1)
     hidden = (jax.nn.silu(gate) * up).astype(LOW)
-    final_own = middle + lax.psum_scatter(
-        dot(hidden, ffn_w[2], 1, 0), "narrow", scatter_dimension=0, tiled=True
-    )
-    final_own = jnp.where(keep_layer > 0, final_own, start_own)
-
-    local_target = targets_all - (
-        narrow_spot * vocab_rows + wide_spot * table_own.shape[0]
-    )
-    has_target = (
-        local_target[:, None] == jnp.arange(table_own.shape[0], dtype=jnp.int32)[None, :]
-    )
+    final_own, late_part = settle(
+        dot(hidden, ffn_w[2], 1, 0), middle, start_own, keep_row, gain_w[2:3], 3, "settle"
+    )
+
+    table_count = table_own.shape[0]
+    local_target = targets_all - (narrow_spot * vocab_rows + wide_spot * table_count)
+    has_target = local_target[:, None] == jnp.arange(table_count, dtype=jnp.int32)[None, :]
     counted = (targets_all >= 0).astype(FULL)
     loss_count = jnp.sum(counted)
-
-    def exit_part(own_h, weight):
-        features = gather_rows(norm_rows(own_h, gain_w[2]).astype(LOW), BOTH)
+    total_rows = wide_count * sel
+
+    early = gather_rows(norm_rows(start_own, gain_w[2]).astype(LOW), BOTH)
+    late = gather_wide(late_part, 4, "gather_late").reshape(total_rows, width)
+
+    def exit_logits(features):
         logits = dot(features, table_own, 1, 1)
         peak = jnp.max(logits, axis=-1)
         total = jnp.sum(jnp.exp(logits - peak[:, None]), axis=-1)
         picked = jnp.sum(jnp.where(has_target, logits, 0.0), axis=-1)
-        stats = lax.all_gather(jnp.stack([peak, total, picked]), BOTH)
-        peak_all = jnp.max(stats[:, 0], axis=0)
-        total_all = jnp.sum(stats[:, 1] * jnp.exp(stats[:, 0] - peak_all), axis=0)
-        log_norm = peak_all + jnp.log(total_all)
-        loss = weight * jnp.sum(counted * (log_norm - jnp.sum(stats[:, 2], axis=0)))
+        return logits, jnp.stack([peak, total, picked])
+
+    early_logits, early_stats = exit_logits(early)
+    late_logits, late_stats = exit_logits(late)
+    stats = jnp.pad(jnp.concatenate([early_stats, late_stats], axis=1), ((0, 5), (0, 0)))
+    stats = combine(stats, merge_two, 5, "combine_stats")
+    log_norms = stats[0] + jnp.log(stats[1])
+    losses = log_norms - stats[2]
+    loss_sum = jnp.sum(
+        counted * (EXIT_EARLY * losses[:total_rows] + EXIT_LAST * losses[total_rows:])
+    )
+
+    def exit_back(logits, log_norm, weight, features):
         grad_logits = (
             (jnp.exp(logits - log_norm[:, None]) - has_target.astype(FULL))
             * (weight * counted)[:, None]
         ).astype(LOW)
-        grad_features = dot(grad_logits, table_own, 1, 0)
-        grad_own = lax.psum_scatter(
-            lax.psum_scatter(grad_features, "wide", scatter_dimension=0, tiled=True),
-            "narrow",
-            scatter_dimension=0,
-            tiled=True,
-        )
-        return loss, grad_own, dot(grad_logits, features, 0, 0)
-
-    loss_early, grad_early, head_early = exit_part(start_own, EXIT_EARLY)
-    loss_late, grad_late, head_late = exit_part(final_own, EXIT_LAST)
-    loss_sum = loss_early + loss_late
-    grad_head = (head_early + head_late).astype(LOW)
+        return dot(grad_logits, table_own, 1, 0), dot(grad_logits, features, 0, 0)
+
+    late_back, late_head = exit_back(late_logits, log_norms[total_rows:], EXIT_LAST, late)
+    early_back, early_head = exit_back(early_logits, log_norms[:total_rows], EXIT_EARLY, early)
+    grad_late = sum_wide(late_back.astype(LOW), 6, "sum_late")
+    grad_early = lax.psum_scatter(
+        lax.psum_scatter(early_back, "wide", scatter_dimension=0, tiled=True),
+        "narrow",
+        scatter_dimension=0,
+        tiled=True,
+    )
+    grad_head = (early_head + late_head).astype(LOW)
     head_cols = exchange(cut_columns(grad_head, wide_count), "wide").reshape(vocab_rows, columns)
-
     grad_start_exit, gain_early = norm_back(start_own, gain_w[2], grad_early)
-    grad_final, gain_late = norm_back(final_own, gain_w[2], grad_late)
+
+    grad_final, gain_late, grad_out = settle_back(
+        grad_late, final_own, jnp.zeros_like(final_own), keep_row, gain_w[2:3], 7, "settle_back"
+    )
     grad_layer = grad_final * keep_layer
-    grad_out = gather_rows(grad_layer.astype(LOW), "narrow")
     grad_hidden = dot(grad_out, ffn_w[2], 1, 1)
     sigma = jax.nn.sigmoid(gate)
     grad_gate = (grad_hidden * up * sigma * (1.0 + gate * (1.0 - sigma))).astype(LOW)
     grad_up = (grad_hidden * gate * sigma).astype(LOW)
-    grad_inner = lax.psum_scatter(
+    grad_mid, gain_mid, grad_branch = settle_back(
         dot(grad_gate, ffn_w[0], 1, 0) + dot(grad_up, ffn_w[1], 1, 0),
-        "narrow",
-        scatter_dimension=0,
-        tiled=True,
-    )
-    extra_mid, gain_mid = norm_back(middle, gain_w[1], grad_inner)
-    grad_mid = grad_layer + extra_mid
-    grad_pass = grad_mid + grad_start_exit + grad_final * (1.0 - keep_layer)
-    both_mid = lax.all_gather(
-        jnp.stack([grad_mid.astype(LOW), grad_pass.astype(LOW)]), "narrow", axis=1, tiled=True
-    )
-    grad_branch, grad_extra = both_mid[0], both_mid[1]
+        middle,
+        grad_layer,
+        keep_row,
+        gain_w[1:2],
+        7,
+        "settle_back",
+    )
 
     grad_mixed = dot(grad_branch, o_w, 1, 0).astype(LOW)
     grouped_grad = grad_mixed.reshape(sel, groups, heads_own // groups, HD)
@@ -479,54 +1122,46 @@
         .astype(LOW)
     )
     grad_keys = jnp.einsum("kgts,tkgd->ksd", grad_scores, grouped, preferred_element_type=FULL)
+    _, cosine_all, sine_all = angles_at(lens, where_at)
     grad_keys = unrotate(grad_keys * scale, cosine_all, sine_all).astype(LOW)
     grad_values = jnp.einsum(
         "kgts,tkgd->ksd", probs_low, grouped_grad, preferred_element_type=FULL
     ).astype(LOW)
-    grad_kv_all = gather_rows(jnp.stack([grad_keys, grad_values], axis=1), "narrow")
+    kv_parts = jnp.stack([grad_keys, grad_values]).reshape(
+        2, groups, narrow_count, tok_rows, HD
+    )
+    kv_parts = jnp.transpose(kv_parts, (2, 1, 0, 3, 4))
+    pick_parts = dot(grad_queries, q_w, 1, 1).reshape(narrow_count, own_rows, width)
+    grad_kv, pick_parts = trade([kv_parts, pick_parts], (True, True), 8, "trade_grads")
+    grad_kv = grad_kv.reshape(KVH, repeat, 2, tok_rows, HD)
     if repeat > 1:
-        grad_kv_all = jnp.sum(
-            grad_kv_all.reshape(KVH, repeat, 2, seq_len, HD).astype(FULL), axis=1
-        ).astype(LOW)
-    grad_kv_all = jnp.transpose(grad_kv_all, (1, 2, 0, 3)).reshape(2, seq_len, KVH * HD)
-    grad_q_all = gather_columns(grad_queries, "narrow")
-
-    pick_part = dot(grad_q_all, q_full, 1, 1)
-    pick_high = pick_part.astype(LOW)
-    pick_low = (pick_part - pick_high.astype(FULL)).astype(LOW)
-    grad_normed = (
-        dot(grad_kv_all[0], kv_w[0], 1, 1)
-        + dot(grad_kv_all[1], kv_w[1], 1, 1)
-        + dot(pick_hot, pick_high, 0, 0)
-        + dot(pick_hot, pick_low, 0, 0)
-    )
-    grad_normed = jnp.where(inside_mine[:, None], grad_normed, 0.0)
-    extra_start, gain_attn = norm_back(rows_full, gain_w[0], grad_normed)
-    grad_start = jnp.where(
-        inside_mine[:, None], extra_start + dot(pick_hot, grad_extra, 0, 0), 0.0
-    ).astype(LOW)
-    grad_rows = exchange(cut_columns(grad_start, wide_count), "wide").reshape(-1, columns)
+        grad_kv = jnp.sum(grad_kv.astype(FULL), axis=1, keepdims=True).astype(LOW)
+    grad_kv = jnp.transpose(grad_kv[:, 0], (1, 2, 0, 3)).reshape(2, tok_rows, KVH * HD)
+
+    grad_normed = jnp.concatenate(
+        [
+            dot(grad_kv[0], kv_w[0], 1, 1) + dot(grad_kv[1], kv_w[1], 1, 1),
+            jnp.sum(pick_parts, axis=0),
+        ]
+    )
+    grad_rows, gain_attn = norm_back(rows_full, gain_w[0], grad_normed)
+    grad_pass = grad_mid + grad_start_exit + grad_final * (1.0 - keep_layer)
+    grad_rows = jnp.concatenate([grad_rows[:tok_rows], grad_rows[tok_rows:] + grad_pass])
+    grad_rows = return_rows(grad_rows.astype(LOW), 9, "return_rows").reshape(-1, columns)
     summed_table, table_squares = spread(spots, grad_rows, head_cols)
 
-    grad_kv_w = jnp.stack(
-        [dot(normed_all, grad_kv_all[0], 0, 0), dot(normed_all, grad_kv_all[1], 0, 0)], axis=1
-    )
-    grad_kv_w = lax.psum_scatter(grad_kv_w, "wide", scatter_dimension=0, tiled=True)
-    summed_kv = lax.psum_scatter(
-        jnp.moveaxis(grad_kv_w, 1, 0), "narrow", scatter_dimension=2, tiled=True
-    )
-
-    left_cols = exchange(
-        jnp.moveaxis(
-            jnp.stack([normed, grad_branch]).reshape(2, sel, wide_count, columns), 2, 0
-        ),
-        "wide",
-    )
-    left_cols = jnp.moveaxis(left_cols, 1, 0).reshape(2, wide_count * sel, columns)
+    tok_cols = exchange(cut_columns(normed_tok, wide_count), "wide").reshape(-1, columns)
+    grad_kv_wide = lax.all_gather(grad_kv, "wide", axis=1, tiled=True)
+    grad_kv_w = jnp.stack([dot(tok_cols, grad_kv_wide[j], 0, 0) for j in range(2)])
+    summed_kv = lax.psum_scatter(grad_kv_w, "narrow", scatter_dimension=2, tiled=True)
+
+    def left_cols(values_all):
+        return exchange(cut_columns(values_all, wide_count), "wide").reshape(-1, columns)
+
     summed_qo = jnp.stack(
         [
-            dot(left_cols[0], gather_rows(grad_queries, "wide"), 0, 0),
-            dot(left_cols[1], gather_rows(mixed, "wide"), 0, 0),
+            dot(left_cols(normed), gather_rows(grad_queries, "wide"), 0, 0),
+            dot(left_cols(grad_branch), gather_rows(mixed, "wide"), 0, 0),
         ]
     )
 
@@ -549,19 +1184,19 @@
         pack_small(summed_qo, summed_kv).astype(LOW), "narrow", axis=0
     )
 
-    gain_grads = jnp.stack([gain_attn, gain_mid, gain_early + gain_late])
-    gain_sum = lax.psum(gain_grads, BOTH)
-    gain_size = gains.shape[1]
-    summed_gain = lax.dynamic_slice_in_dim(
-        gain_sum, (wide_spot * narrow_count + narrow_spot) * gain_size, gain_size, 1
-    )
     squares = (
         jnp.sum(summed_qo * summed_qo)
         + jnp.sum(summed_kv * summed_kv)
         + jnp.sum(summed_ffn * summed_ffn)
-    )
-    squares = squares + jnp.sum(summed_gain * summed_gain) + jnp.sum(table_squares)
-    square_total = lax.psum(squares, BOTH)
+        + jnp.sum(table_squares)
+    )
+    sums = jnp.stack([gain_attn, gain_mid, gain_early + gain_late, jnp.full((width,), squares)])
+    sums = combine(jnp.pad(sums, ((0, 4), (0, 0))), add_two, 10, "combine_sums")
+    gain_size = gains.shape[1]
+    summed_gain = lax.dynamic_slice_in_dim(
+        sums[:3], (wide_spot * narrow_count + narrow_spot) * gain_size, gain_size, 1
+    )
+    square_total = sums[3, 0] + jnp.sum(sums[:3] * sums[:3])
     grad_norm = jnp.sqrt(square_total) / loss_count
     factor = jnp.minimum(1.0, CLIP_NORM / (grad_norm + 1e-06)) / loss_count
 

time: 2270 us -> 1920 us (0.85)
  waiting for transfers between devices: 1180 us -> 535 us
  Pallas kernels: 77.6 us -> 626 us
  blocking collectives: 354 us -> 167 us
  matrix products: 250 us -> 224 us
    pallas_call x0 -> x13, Pallas kernels: none -> 541 us  [call_kernel(): pl.pallas_call(body, out_shape=outputs, in_specs=in_specs, out_specs=out_...]
    all_gather x13 -> x8, waiting for transfers between devices: 356 us -> 132 us  [gather_rows(): return lax.all_gather(values, axis, axis=0, tiled=True)]
    reduce_scatter x9 -> x3, waiting for transfers between devices: 271 us -> 63.6 us  [the longest x1 24.3 us: per_device(): lax.psum_scatter(lax.psum_scatter(early_back, 'wide', scatter_dimension=0...]
    all_gather x5 -> x0, blocking collectives: 164 us -> none  [the longest x2 129 us: exit_part(): stats = lax.all_gather(jnp.stack([peak, total, picked]), BOTH)]
    unnamed x29 -> x16, waiting for transfers between devices: 140 us -> 2.79 us
    psum x2 -> x0, blocking collectives: 76.7 us -> none  [the longest x1 38.6 us: per_device(): gain_sum = lax.psum(gain_grads, BOTH)]
    all_to_all x1 -> x2, blocking collectives: 27.3 us -> 97.9 us  [exchange(): return lax.all_to_all(parts, axis, 0, 0, tiled=True)]
    all_gather x2, waiting for transfers between devices: 48.3 us -> 0.02 us  [the longest x1 0.02 us: per_device(): grad_kv_wide = lax.all_gather(grad_kv, 'wide', axis=1, tiled=True)]
  transfers between devices with their start and end apart: 36 -> 23, of which waited for: 27 -> 12; matrix products, arithmetic and copies ran while one was open for 12% -> 12% of each run, Pallas kernels for 3% -> 17%
where the time goes in v2:
time: 1920 us; the launch traced here: 1910 us
  Pallas kernels  626 us (33%)
  waiting for transfers between devices  535 us (28%)
  matrix products  224 us (12%)
  blocking collectives  167 us (9%)
  other arithmetic  141 us (7%)
  local copies, waits for them, and re-layouts  119 us (6%)
  starting transfers between devices  41.7 us (2%)
  loops' own time  32.3 us (2%)
  between operations  23 us (1%)
    pallas_call x13, Pallas kernels, call_kernel(): pl.pallas_call(body, out_shape=outputs, in_specs=in_specs, out_specs=out_...  541 us
    all_to_all x7, waiting for transfers between devices, exchange(): return lax.all_to_all(parts, axis, 0, 0, tiled=True)  254 us
    dot_general x28, matrix products, dot(): lax.dot_general(first, second, (((first_dim,), (second_dim,)), ((), ())),...  144 us
    all_gather x8, waiting for transfers between devices, gather_rows(): return lax.all_gather(values, axis, axis=0, tiled=True)  132 us
    all_to_all x2, blocking collectives, exchange(): return lax.all_to_all(parts, axis, 0, 0, tiled=True)  97.9 us
    all_gather x1, waiting for transfers between devices, per_device(): acts = lax.all_gather(acts, 'narrow', axis=2, tiled=True)  82.5 us
    all_gather x1, blocking collectives, gather_columns(): return lax.all_gather(values, axis, axis=1, tiled=True)  57 us
    unnamed x183, local copies, waits for them, and re-layouts  46.3 us
  transfers between devices with their start and end apart: 23, of which 12 were waited for; matrix products, arithmetic and copies ran while one was open for 12% of the time, Pallas kernels for 17%

profile of v2, /device:TPU:17, one launch (start us, length us, event | category | flops | bytes accessed | tf_op | source)
XLA Modules:
  0.0 1909.0 jit_solution(16467647841445958651)
XLA Ops:
  8.2 12.3 all_gather.50
  23.8 8.5 gather_ids.1
  34.6 39.1 %lookup.1 = bf16[9216,256]{1,0:T(8,128)(2,1)} custom-call(s32[9216]{0:T(1024)} %and_select_fusion.ids_ref, f32[8192,256]{1,0:T(8,128)} %table_ref.1), custom_call_target="tpu_custom_call" | custom-call | bytes 83886080 | tf_op jit(solution)/shard_map/lookup/pallas_call | solution.py:746
  73.7 120.3 %fetch_rows.1 = bf16[288,2048]{1,0:T(8,128)(2,1)} custom-call(bf16[4,2304,256]{2,1,0:T(8,128)(2,1)} %bitcast.414), custom_call_target="tpu_custom_call" | custom-call | bytes 47185920 | tf_op jit(solution)/shard_map/fetch_rows/pallas_call | solution.py:119
  194.0 57.0 %all-gather.1 = bf16[32,64,3]{1,2,0:T(4,128)(2,1)S(1)} all-gather(bf16[1,64,3]{1,2,0:T(4,128)(2,1)S(1)} %convert_bitcast_fusion.1), channel_id=1, replica_groups=mesh['wide'=8,'narrow'=4] {'wide','narrow'}, dimensions={0}, use_global_device_ids=true | all-gather | bytes 12672 | tf_op jit(solution)/shard_map/all_gather | solution.py:897
  257.7 73.0 %all_to_all.56 = bf16[4,3,176,512]{3,2,1,0:T(8,128)(2,1)S(1)} all-to-all(bf16[4,3,176,512]{3,2,1,0:T(8,128)(2,1)S(1)} %copy.335), channel_id=1, replica_groups=mesh['wide'=8,'narrow'=4] {'narrow'}, dimensions={0} | all-to-all | bytes 4325376 | tf_op jit(solution)/shard_map/all_to_all | solution.py:879
  333.8 5.8 convert_element_type.483
  339.6 7.7 all-to-all-start
  355.3 57.2 %all-to-all-done = bf16[8,1024,256]{2,1,0:T(8,128)(2,1)} async-done(((bf16[8,1024,256]{2,1,0:T(8,128)(2,1)}), bf16[8,1024,256]{2,1,0:T(8,128)(2,1)}, u32[]{:S(2)}, u32[]{:S(2)}) %all-to-all-start) | async-done | bytes 4194336 | tf_op jit(solution)/shard_map/all_to_all | solution.py:879
  412.5 6.4 copy.322
  440.3 23.3 %trade_heads.1 = (bf16[4,1,2,256,128]{4,3,2,1,0:T(8,128)(2,1)}, bf16[4,32,2048]{2,1,0:T(8,128)(2,1)}) custom-call(bf16[4,1,2,256,128]{4,3,2,1,0:T(8,128)(2,1)} %maximum_bitcast_fusion.1.refs_0_, bf16[32,2048]{1,0:T(8,128)(2,1)} %slice.274.refs_1_), custom_call_target="tpu_custom_call" | custom-call | bytes 13631488 | tf_op jit(solution)/shard_map/trade_heads/pallas_call | solution.py:119
  475.7 35.8 %settle.2 = (f32[32,2048]{1,0:T(8,128)}, bf16[4,32,2048]{2,1,0:T(8,128)(2,1)}) custom-call(f32[4,32,2048]{2,1,0:T(8,128)} %fusion.216.parts_ref, f32[32,2048]{1,0:T(8,128)} %slice.266.base_ref.other_ref, f32[32,2048]{1,0:T(8,128)} %slice.266.base_ref.other_ref, f32[1,2048]{1,0:T(1,128)} %broadcast_in_dim.84.keep_ref, f32[1,2048]{1,0:T(1,128)} %get-tuple-element.375.gain_ref), custom_call_target="tpu_custom_call" | custom-call | bytes 19005440 | tf_op jit(solution)/shard_map/settle/pallas_call | solution.py:119
  511.6 10.6 fusion.320
  522.2 5.6 fusion.324
  527.9 6.0 multiply_convert_fusion.3
  539.3 39.4 %settle.3 = (f32[32,2048]{1,0:T(8,128)}, bf16[4,32,2048]{2,1,0:T(8,128)(2,1)}) custom-call(f32[4,32,2048]{2,1,0:T(8,128)} %bitcast.436, f32[32,2048]{1,0:T(8,128)} %get-tuple-element.64.base_ref.values_ref, f32[32,2048]{1,0:T(8,128)} %slice.266.base_ref.other_ref, f32[1,2048]{1,0:T(1,128)} %broadcast_in_dim.89.keep_ref, f32[1,2048]{1,0:T(1,128)} %copy-done.50), custom_call_target="tpu_custom_call" | custom-call | bytes 19005440 | tf_op jit(solution)/shard_map/settle/pallas_call | solution.py:119
  578.7 33.2 %gather_late.1 = bf16[8,128,2048]{2,1,0:T(8,128)(2,1)} custom-call(bf16[128,2048]{1,0:T(8,128)(2,1)} %bitcast.481), custom_call_target="tpu_custom_call" | custom-call | bytes 37748736 | tf_op jit(solution)/shard_map/gather_late/pallas_call | solution.py:119
  612.0 7.8 fusion.322
  622.5 17.2 combine_stats.1
  641.3 8.7 convolution_convert_fusion
  650.0 31.8 %sum_late.1 = f32[128,2048]{1,0:T(8,128)} custom-call(bf16[8,128,2048]{2,1,0:T(8,128)(2,1)} %bitcast.434), custom_call_target="tpu_custom_call" | custom-call | bytes 41943040 | tf_op jit(solution)/shard_map/sum_late/pallas_call | solution.py:119
  682.5 37.8 %settle_back.2 = (f32[32,2048]{1,0:T(8,128)}, f32[1,2048]{1,0:T(1,128)}, bf16[4,32,2048]{2,1,0:T(8,128)(2,1)}) custom-call(f32[4,32,2048]{2,1,0:T(8,128)} %bitcast.435, f32[32,2048]{1,0:T(8,128)} %get-tuple-element.66.values_ref, f32[32,2048]{1,0:T(8,128)} %broadcast_in_dim.90.add_ref, f32[1,2048]{1,0:T(1,128)} %broadcast_in_dim.89.keep_ref, ...), custom_call_target="tpu_custom_call" | custom-call | bytes 19070976 | tf_op jit(solution)/shard_map/settle_back/pallas_call | solution.py:119
  722.0 5.2 multiply_convert_fusion.1
  736.1 39.5 %settle_back.3 = (f32[32,2048]{1,0:T(8,128)}, f32[1,2048]{1,0:T(1,128)}, bf16[4,32,2048]{2,1,0:T(8,128)(2,1)}) custom-call(f32[4,32,2048]{2,1,0:T(8,128)} %bitcast.448, f32[32,2048]{1,0:T(8,128)} %get-tuple-element.64.base_ref.values_ref, f32[32,2048]{1,0:T(8,128)} %broadcast_multiply_fusion.31.add_ref, f32[1,2048]{1,0:T(1,128)} %broadcast_in_dim.89.keep_ref, ...), custom_call_target="tpu_custom_call" | custom-call | bytes 19070976 | tf_op jit(solution)/shard_map/settle_back/pallas_call | solution.py:119
  787.9 38.4 %trade_grads.1 = (bf16[4,1,2,256,128]{4,3,2,1,0:T(8,128)(2,1)}, f32[4,32,2048]{2,1,0:T(8,128)}) custom-call(bf16[4,1,2,256,128]{4,3,2,1,0:T(8,128)(2,1)} %maximum_bitcast_fusion.2.refs_0_, f32[4,32,2048]{2,1,0:T(8,128)} %fusion.211.refs_1_), custom_call_target="tpu_custom_call" | custom-call | bytes 25165824 | tf_op jit(solution)/shard_map/trade_grads/pallas_call | solution.py:119
  829.3 11.5 fusion.304
  843.9 25.0 %all_to_all.57 = bf16[8,3,128,176]{2,3,1,0:T(8,128)(2,1)S(1)} all-to-all(bf16[8,3,128,176]{2,3,1,0:T(8,128)(2,1)S(1)} %copy.356), channel_id=1, replica_groups=mesh['wide'=8,'narrow'=4] {'wide'}, dimensions={0} | all-to-all | bytes 2162688 | tf_op jit(solution)/shard_map/all_to_all | solution.py:879
  872.3 5.5 all-to-all-start.4
  890.8 13.0 fusion.302
  914.5 12.9 add_convert_fusion.2
  942.8 5.5 all-to-all-start.6
  950.4 16.5 reduce-scatter.4.cloned.1.call-done
  970.7 39.8 %all-gather.30.cloned.1.call-done = bf16[1024,512]{0,1:T(8,128)(2,1)} async-done(((bf16[128,512]{0,1:T(8,128)(2,1)}), bf16[1024,512]{0,1:T(8,128)(2,1)}) %all-gather.30.cloned.1.call-update) | async-done | bytes 1048592 | tf_op jit(solution)/shard_map/all_gather | solution.py:893
  1012.4 23.3 %all-gather.28.cloned.1.call-done = bf16[1024,512]{0,1:T(8,128)(2,1)} async-done(((bf16[128,512]{0,1:T(8,128)(2,1)}), bf16[1024,512]{0,1:T(8,128)(2,1)}) %all-gather.28.cloned.1.call-update) | async-done | bytes 1048592 | tf_op jit(solution)/shard_map/all_gather | solution.py:893
  1039.1 35.4 %all-gather.36.cloned.1.call-done = bf16[1024,2048]{1,0:T(8,128)(2,1)} async-done(((bf16[128,2048]{1,0:T(8,128)(2,1)}), bf16[1024,2048]{1,0:T(8,128)(2,1)}) %all-gather.36.cloned.1.call-update) | async-done | bytes 4194320 | tf_op jit(solution)/shard_map/all_gather | solution.py:893
  1074.5 82.5 %all-gather.34.cloned.1.call-done = bf16[3,1024,704]{1,2,0:T(8,128)(2,1)} async-done(((bf16[3,1024,176]{1,2,0:T(8,128)(2,1)}), bf16[3,1024,704]{1,2,0:T(8,128)(2,1)}) %all-gather.34.cloned.1.call-update) | async-done | bytes 4325392 | tf_op jit(solution)/shard_map/all_gather | solution.py:1175
  1162.7 33.6 %all-gather.38.cloned.1.call-done = bf16[1024,2048]{1,0:T(8,128)(2,1)} async-done(((bf16[128,2048]{1,0:T(8,128)(2,1)}), bf16[1024,2048]{1,0:T(8,128)(2,1)}) %all-gather.38.cloned.1.call-update) | async-done | bytes 4194320 | tf_op jit(solution)/shard_map/all_gather | solution.py:893
  1201.7 22.8 %reduce-scatter.8.cloned.1.call-done = f32[2,256,128]{2,1,0:T(8,128)} async-done(((f32[2,256,512]{2,1,0:T(8,128)}), f32[2,256,128]{2,1,0:T(8,128)}) %reduce-scatter.8.cloned.1.call-update) | async-done | bytes 262160 | tf_op jit(solution)/shard_map/reduce_scatter | solution.py:1156
  1228.2 24.3 %reduce-scatter.6.cloned.1.call-done = f32[32,2048]{1,0:T(8,128)} async-done(((f32[128,2048]{1,0:T(8,128)}), f32[32,2048]{1,0:T(8,128)}) %reduce-scatter.6.cloned.1.call-update) | async-done | bytes 262160 | tf_op jit(solution)/shard_map/reduce_scatter | solution.py:1082
  1256.9 94.6 %return_rows.1 = bf16[4,2304,256]{2,1,0:T(8,128)(2,1)} custom-call(bf16[288,2048]{1,0:T(8,128)(2,1)} %pad_maximum_fusion.3.rows_ref), custom_call_target="tpu_custom_call" | custom-call | bytes 47185920 | tf_op jit(solution)/shard_map/return_rows/pallas_call | solution.py:119
  1351.5 46.1 %spread.1 = (f32[8192,256]{1,0:T(8,128)}, f32[8,256]{1,0:T(8,128)}) custom-call(s32[9216]{0:T(1024)} %and_select_fusion.ids_ref, bf16[9216,256]{1,0:T(8,128)(2,1)} %bitcast.415, bf16[8192,256]{1,0:T(8,128)(2,1)} %bitcast.152.head_ref), custom_call_target="tpu_custom_call" | custom-call | flops 2359296 | bytes 150994944 | tf_op jit(solution)/shard_map/spread/pallas_call | solution.py:811
  1402.0 20.6 %combine_sums.1 = f32[8,2048]{1,0:T(8,128)} custom-call(f32[8,2048]{1,0:T(8,128)} %pad.26.x_ref), custom_call_target="tpu_custom_call" | custom-call | bytes 1048576 | tf_op jit(solution)/shard_map/combine_sums/pallas_call | solution.py:119
  1431.7 6.5 pad_maximum_fusion
  1443.3 6.2 all-to-all-start.7
  1450.7 168.5 %all-to-all-done.7 = f32[4,1,360448]{2,1,0:T(1,128)} async-done(((f32[4,1,360448]{2,1,0:T(1,128)}), f32[4,1,360448]{2,1,0:T(1,128)}, u32[]{:S(2)}, u32[]{:S(2)}) %all-to-all-start.7) | async-done | bytes 5767200 | tf_op jit(solution)/shard_map/all_to_all | solution.py:879
  1619.2 7.5 copy.430
  1626.8 142.6 %conditional.1 = (bf16[4,360448]{1,0:T(4,128)(2,1)S(1)}) conditional(s32[]{:T(128)} %convert_element_type.523, (f32[4,360448]{1,0:T(4,128)}, s32[]{:T(128)}, bf16[3,1024,704]{1,2,0:T(8,128)(2,1)}, bf16[1024,2048]{1,0:T(8,128)(2,1)}, bf16[1024,2048]{1,0:T(8,128)(2,1)}, /*index=5*/f32[]{:T(128)}) %tuple.168, (f32[4,360448]{1,0:T(4,128)}, ...), branch_computations={%region_34.46_spmd, %region_46.69_spmd} | conditional | flops 26843262976 | bytes 274531648 | solution.py:1232
  1630.9 5.3 copy.381
  1636.2 7.0 copy.362
  1643.1 11.4 multiply_reduce_fusion
  1655.3 8.7 select_reduce_fusion.9
  1672.1 6.8 multiply_add_fusion.3
  1688.3 7.5 multiply_add_fusion.2
  1705.3 7.4 multiply_add_fusion.1
  1722.1 7.4 multiply_add_fusion
  1739.2 8.9 add_convert_fusion
  1748.1 6.0 convert_element_type.349
  1771.5 14.7 reduce.35
  1790.7 7.1 all-to-all-start.8
  1803.7 5.4 bitcast_add_fusion
  1809.1 22.1 %multiply_subtract_fusion.10 = (f32[8192,256]{1,0:T(8,128)}, f32[8192,256]{1,0:T(8,128)}, f32[8192,256]{1,0:T(8,128)}) fusion(f32[8192,256]{1,0:T(8,128)} %table_ref.1, f32[8192,256]{1,0:T(8,128)} %get-tuple-element.76, f32[]{:T(128)} %div.217, f32[8192,256]{1,0:T(8,128)} %param.25, f32[8192,256]{1,0:T(8,128)} %param.26), kind=kLoop, calls=%fused_computation.329 | loop fusion | flops 31457280 | bytes 58720260 | tf_op jit(solution)/shard_map/sub | solution.py:875
  1831.2 28.1 %all-to-all-done.8 = bf16[4,2,180224]{2,1,0:T(2,128)(2,1)S(1)} async-done(((bf16[4,2,180224]{2,1,0:T(2,128)(2,1)}), bf16[4,2,180224]{2,1,0:T(2,128)(2,1)S(1)}, u32[]{:S(2)}, u32[]{:S(2)}) %all-to-all-start.8) | async-done | bytes 2883616 | tf_op jit(solution)/shard_map/all_to_all | solution.py:879
  1863.4 16.2 fusion.204
  1879.6 12.0 fusion.247
  (396 shorter events, 242.1 us)
Async XLA Ops:
  7.2 15.7 copy-start.78
  7.2 15.7 copy-start.65
  7.2 15.9 copy-start.82
  7.2 411.7 %all-gather.18.cloned.1.call-start = ((), (), s32[]{:S(2)}) async-start(), calls=%async_computation.13 | async-start | bytes 4718592 | tf_op jit(solution)/shard_map/all_gather | solution.py:964
  20.6 408.5 %all-gather.20.cloned.1.call-start = ((), (), s32[]{:S(2)}) async-start(), calls=%async_computation.14 | async-start | bytes 4718592 | tf_op jit(solution)/shard_map/all_gather | solution.py:968
  22.8 488.8 %all-gather.16.cloned.1.call-start = ((), (), s32[]{:S(2)}) async-start(), calls=%async_computation.12 | async-start | bytes 4325376 | tf_op jit(solution)/shard_map/all_gather | solution.py:893
  73.7 120.3 %copy-start.66 = (f32[3,64]{1,0:T(4,128)S(1)}, f32[3,64]{1,0:T(4,128)}, u32[]{:S(2)}) copy-start(f32[3,64]{1,0:T(4,128)} %param.33) | copy-start | bytes 2308
  254.9 267.3 %all-gather.22.cloned.1.call-start = ((), (), s32[]{:S(2)}) async-start(), calls=%async_computation.15 | async-start | bytes 6488064 | tf_op jit(solution)/shard_map/all_gather | solution.py:893
  331.8 196.1 %all-gather.24.cloned.1.call-start = ((), (), s32[]{:S(2)}) async-start(), calls=%async_computation.16 | async-start | bytes 6488064 | tf_op jit(solution)/shard_map/all_gather | solution.py:893
  332.8 201.2 %all-gather.26.cloned.1.call-start = ((), (), s32[]{:S(2)}) async-start(), calls=%async_computation.17 | async-start | bytes 6488064 | tf_op jit(solution)/shard_map/all_gather | solution.py:893
  339.6 7.7 copy-start
  339.6 72.9 %all-to-all-start = ((bf16[8,1024,256]{2,1,0:T(8,128)(2,1)}), bf16[8,1024,256]{2,1,0:T(8,128)(2,1)}, u32[]{:S(2)}, u32[]{:S(2)}) async-start(bf16[8,1024,256]{2,1,0:T(8,128)(2,1)} %bitcast.419), calls=%async_computation | async-start | bytes 8388608 | tf_op jit(solution)/shard_map/all_to_all | solution.py:879
  347.4 560.8 %all-gather.32.cloned.1.call-start = ((), (), s32[]{:S(2)}) async-start(), calls=%async_computation.22 | async-start | bytes 4718592 | tf_op jit(solution)/shard_map/all_gather | solution.py:1154
  351.3 67.6 %copy-start.71 = (f32[64]{0:T(128)}, f32[64]{0:T(128)S(1)}, u32[]{:S(2)}) copy-start(f32[64]{0:T(128)S(1)} %multiply_power_fusion) | copy-start | bytes 772
  439.4 26.2 %copy-start.52 = (f32[128,64]{0,1:T(8,128)S(1)}, f32[128,64]{0,1:T(8,128)}, u32[]{:S(2)}) copy-start(f32[128,64]{0,1:T(8,128)} %get-tuple-element.385) | copy-start | bytes 98308
  439.4 26.2 %copy-start.57 = (f32[128,64]{0,1:T(8,128)S(1)}, f32[128,64]{0,1:T(8,128)}, u32[]{:S(2)}) copy-start(f32[128,64]{0,1:T(8,128)} %get-tuple-element.384) | copy-start | bytes 98308
  611.9 7.8 copy-start.23
  611.9 7.8 copy-start.61
  612.0 7.8 copy-start.62
  619.8 21.6 %copy-start.22 = (f32[1024,1024]{0,1:T(8,128)}, f32[1024,1024]{0,1:T(8,128)S(1)}, u32[]{:S(2)}) copy-start(f32[1024,1024]{0,1:T(8,128)S(1)} %get-tuple-element.394) | copy-start | bytes 12582916
  619.8 21.5 %copy-start.76 = (f32[1024]{0:T(1024)S(1)}, f32[1024]{0:T(1024)}, u32[]{:S(2)}) copy-start(f32[1024]{0:T(1024)} %get-tuple-element.235) | copy-start | bytes 12292
  641.3 8.7 copy-start.72
  731.2 44.4 %copy-start.5 = (bf16[2,2048,512]{2,1,0:T(8,128)(2,1)S(1)}, bf16[2,2048,512]{2,1,0:T(8,128)(2,1)}, u32[]{:S(2)}) copy-start(bf16[2,2048,512]{2,1,0:T(8,128)(2,1)} %all-gather.20.cloned.1.call-done) | copy-start | bytes 12582916
  736.1 41.1 %copy-start.55 = (bf16[1,1,4,256,128]{4,3,0,1,2:T(8,128)(2,1)S(1)}, bf16[1,1,4,256,128]{4,3,0,1,2:T(8,128)(2,1)}, u32[]{:S(2)}) copy-start(bf16[1,1,4,256,128]{4,3,0,1,2:T(8,128)(2,1)} %copy-done.54) | copy-start | bytes 786436
  736.1 41.1 %copy-start.60 = (f32[4,128]{1,0:T(4,128)S(1)}, f32[4,128]{1,0:T(4,128)}, u32[]{:S(2)}) copy-start(f32[4,128]{1,0:T(4,128)} %copy-done.59) | copy-start | bytes 6148
  736.1 41.1 %copy-start.69 = (f32[4,128]{1,0:T(4,128)S(1)}, f32[4,128]{1,0:T(4,128)}, u32[]{:S(2)}) copy-start(f32[4,128]{1,0:T(4,128)} %copy-done.68) | copy-start | bytes 6148
  780.8 7.1 copy-start.38
  787.9 40.8 %copy-start.64 = (f32[1,1024]{1,0:T(1,128)S(1)}, f32[1,1024]{1,0:T(1,128)}, u32[]{:S(2)}) copy-start(f32[1,1024]{1,0:T(1,128)} %get-tuple-element.397) | copy-start | bytes 12292
  787.9 40.8 %copy-start.75 = (pred[8,128]{1,0:T(8,128)(4,1)S(1)}, pred[8,128]{1,0:T(8,128)(4,1)}, u32[]{:S(2)}) copy-start(pred[8,128]{1,0:T(8,128)(4,1)} %get-tuple-element.236) | copy-start | bytes 3076
  787.9 41.4 %copy-start.63 = (s32[1024]{0:T(1024)S(1)}, s32[1024]{0:T(1024)}, u32[]{:S(2)}) copy-start(s32[1024]{0:T(1024)} %get-tuple-element.372) | copy-start | bytes 12292
  787.9 41.4 %copy-start.74 = (f32[1,1024]{1,0:T(1,128)S(1)}, f32[1,1024]{1,0:T(1,128)}, u32[]{:S(2)}) copy-start(f32[1,1024]{1,0:T(1,128)} %get-tuple-element.378) | copy-start | bytes 12292
  828.4 138.5 %reduce-scatter.4.cloned.1.call-start = ((), (), s32[]{:S(2)}) async-start(), calls=%async_computation.18 | async-start | bytes 9437184 | tf_op jit(solution)/shard_map/reduce_scatter | solution.py:1083
  840.9 169.6 %all-gather.30.cloned.1.call-start = ((), (), s32[]{:S(2)}) async-start(), calls=%async_computation.21 | async-start | bytes 1179648 | tf_op jit(solution)/shard_map/all_gather | solution.py:893
  841.6 194.1 %all-gather.28.cloned.1.call-start = ((), (), s32[]{:S(2)}) async-start(), calls=%async_computation.20 | async-start | bytes 1179648 | tf_op jit(solution)/shard_map/all_gather | solution.py:893
  842.2 232.3 %all-gather.36.cloned.1.call-start = ((), (), s32[]{:S(2)}) async-start(), calls=%async_computation.25 | async-start | bytes 4718592 | tf_op jit(solution)/shard_map/all_gather | solution.py:893
  843.0 314.1 %all-gather.34.cloned.1.call-start = ((), (), s32[]{:S(2)}) async-start(), calls=%async_computation.24 | async-start | bytes 5406720 | tf_op jit(solution)/shard_map/all_gather | solution.py:1175
  870.1 326.2 %all-gather.38.cloned.1.call-start = ((), (), s32[]{:S(2)}) async-start(), calls=%async_computation.26 | async-start | bytes 4718592 | tf_op jit(solution)/shard_map/all_gather | solution.py:893
  870.8 7.0 copy-start.26
  872.3 31.5 %all-to-all-start.4 = ((bf16[8,256,256]{2,1,0:T(8,128)(2,1)}), bf16[8,256,256]{2,1,0:T(8,128)(2,1)}, u32[]{:S(2)}, u32[]{:S(2)}) async-start(bf16[8,256,256]{2,1,0:T(8,128)(2,1)} %bitcast.446), calls=%async_computation.6 | async-start | bytes 2097152 | tf_op jit(solution)/shard_map/all_to_all | solution.py:879
  903.8 24.8 %all-to-all-start.2 = ((bf16[8,128,256]{2,1,0:T(8,128)(2,1)}), bf16[8,128,256]{2,1,0:T(8,128)(2,1)S(1)}, u32[]{:S(2)}, u32[]{:S(2)}) async-start(bf16[8,128,256]{2,1,0:T(8,128)(2,1)} %bitcast.405), calls=%async_computation.4 | async-start | bytes 1048576 | tf_op jit(solution)/shard_map/all_to_all | solution.py:879
  908.0 316.5 %reduce-scatter.8.cloned.1.call-start = ((), (), s32[]{:S(2)}) async-start(), calls=%async_computation.23 | async-start | bytes 1310720 | tf_op jit(solution)/shard_map/reduce_scatter | solution.py:1156
  914.4 12.9 copy-start.29
  914.4 13.1 copy-start.47
  928.6 7.9 copy-start.31
  928.6 14.2 all-to-all-start.3
  942.8 408.7 %all-to-all-start.6 = ((bf16[8,1024,256]{2,1,0:T(8,128)(2,1)}), bf16[8,1024,256]{2,1,0:T(8,128)(2,1)}, u32[]{:S(2)}, u32[]{:S(2)}) async-start(bf16[8,1024,256]{2,1,0:T(8,128)(2,1)} %bitcast.420), calls=%async_computation.9 | async-start | bytes 8388608 | tf_op jit(solution)/shard_map/all_to_all | solution.py:879
  948.3 304.2 %reduce-scatter.6.cloned.1.call-start = ((), (), s32[]{:S(2)}) async-start(), calls=%async_computation.19 | async-start | bytes 1310720 | tf_op jit(solution)/shard_map/reduce_scatter | solution.py:1082
  969.6 66.1 %copy-start.32 = (bf16[8,128,256]{2,1,0:T(8,128)(2,1)S(1)}, bf16[8,128,256]{2,1,0:T(8,128)(2,1)}, u32[]{:S(2)}) copy-start(bf16[8,128,256]{2,1,0:T(8,128)(2,1)} %copy-done.31) | copy-start | bytes 1572868
  1012.4 25.3 %copy-start.6 = (f32[1,256,512]{2,1,0:T(8,128)}, f32[1,256,512]{2,1,0:T(8,128)S(1)}, u32[]{:S(2)}) copy-start(f32[1,256,512]{2,1,0:T(8,128)S(1)} %convolution_bitcast_fusion.3) | copy-start | bytes 1572868
  1159.6 39.2 %copy-start.9 = (f32[1,704,512]{2,1,0:T(8,128)}, f32[1,704,512]{2,1,0:T(8,128)S(1)}, u32[]{:S(2)}) copy-start(f32[1,704,512]{2,1,0:T(8,128)S(1)} %convolution_bitcast_fusion.2) | copy-start | bytes 4325380
  1162.7 36.2 %copy-start.11 = (f32[1,704,512]{2,1,0:T(8,128)}, f32[1,704,512]{2,1,0:T(8,128)S(1)}, u32[]{:S(2)}) copy-start(f32[1,704,512]{2,1,0:T(8,128)S(1)} %convolution_bitcast_fusion.1) | copy-start | bytes 4325380
  1200.0 52.5 %copy-start.51 = (f32[1,2048]{1,0:T(1,128)S(1)}, f32[1,2048]{1,0:T(1,128)}, u32[]{:S(2)}) copy-start(f32[1,2048]{1,0:T(1,128)} %copy-done.50) | copy-start | bytes 24580
  1201.7 54.1 %copy-start.27 = (bf16[256,2048]{1,0:T(8,128)(2,1)S(1)}, bf16[256,2048]{1,0:T(8,128)(2,1)}, u32[]{:S(2)}) copy-start(bf16[256,2048]{1,0:T(8,128)(2,1)} %slice.433) | copy-start | bytes 3145732
  1351.5 49.0 %copy-start.58 = (f32[2048]{0:T(1024)S(1)}, f32[2048]{0:T(1024)}, u32[]{:S(2)}) copy-start(f32[2048]{0:T(1024)} %get-tuple-element.224) | copy-start | bytes 24580
  1397.6 34.0 %copy-start.15 = (f32[1,1,704,512]{3,1,2,0:T(1,128)S(1)}, f32[1,1,704,512]{3,1,2,0:T(1,128)}, u32[]{:S(2)}) copy-start(f32[1,1,704,512]{3,1,2,0:T(1,128)} %copy.392) | copy-start | bytes 4325380
  1397.6 34.0 %copy-start.16 = (f32[1,1,704,512]{3,1,2,0:T(1,128)S(1)}, f32[1,1,704,512]{3,1,2,0:T(1,128)}, u32[]{:S(2)}) copy-start(f32[1,1,704,512]{3,1,2,0:T(1,128)} %copy.393) | copy-start | bytes 4325380
  1443.3 176.0 %all-to-all-start.7 = ((f32[4,1,360448]{2,1,0:T(1,128)}), f32[4,1,360448]{2,1,0:T(1,128)}, u32[]{:S(2)}, u32[]{:S(2)}) async-start(f32[4,1,360448]{2,1,0:T(1,128)} %all_to_all.42), calls=%async_computation.10 | async-start | bytes 11534336 | tf_op jit(solution)/shard_map/all_to_all | solution.py:879
  1449.5 177.2 %all-gather.40.cloned.1.call-start = ((), (), s32[]{:S(2)}) async-start(), calls=%async_computation.27 | async-start | bytes 3604480 | tf_op jit(solution)/shard_map/all_gather | solution.py:1183
  1790.6 7.1 copy-start.7
  1790.7 68.6 %all-to-all-start.8 = ((bf16[4,2,180224]{2,1,0:T(2,128)(2,1)}), bf16[4,2,180224]{2,1,0:T(2,128)(2,1)S(1)}, u32[]{:S(2)}, u32[]{:S(2)}) async-start(bf16[4,2,180224]{2,1,0:T(2,128)(2,1)} %reshape.1366), calls=%async_computation.11 | async-start | bytes 5767168 | tf_op jit(solution)/shard_map/all_to_all | solution.py:879
  1797.8 5.9 copy-start.10
  1797.8 5.9 copy-start.12
  1859.3 33.7 %slice-start = ((s8[4325376]{0:T(1024)(128)(4,1)}), s8[131072]{0:T(1024)(128)(4,1)S(1)}, s32[]{:S(2)}) async-start(s8[4325376]{0:T(1024)(128)(4,1)} %bitcast.416), calls=%async_computation.28 | async-start | bytes 262144
  1863.4 29.6 %slice-start.1 = ((s8[4325376]{0:T(1024)(128)(4,1)}), s8[4194304]{0:T(1024)(128)(4,1)S(1)}, s32[]{:S(2)}) async-start(s8[4325376]{0:T(1024)(128)(4,1)} %bitcast.416), calls=%async_computation.29 | async-start | bytes 8388608
  (46 other events, 117.0 us)
Sparse Core Ops, SparseCore 0:
  20.7 40.7 all-gather.17
  63.9 36.7 all-gather.19
  255.0 76.8 all-gather.15
  334.2 75.9 all-gather.21
  412.5 49.8 all-gather.23
  464.1 43.3 all-gather.25
  828.5 46.5 all-gather.31
  879.2 87.7 reduce-scatter.3
  969.0 41.5 all-gather.29
  1013.0 22.6 all-gather.27
  1037.7 36.7 all-gather.35
  1076.0 80.9 all-gather.33
  1159.1 37.1 all-gather.37
  1199.1 25.3 reduce-scatter.7
  1226.7 25.7 reduce-scatter.5
  1452.2 104.2 all-gather.39

commit v3 on v1

v3 whole, which is shorter than its diff:
```python
import functools

import jax
import jax.numpy as jnp
from jax import lax
from jax.experimental import pallas as pl
from jax.experimental.pallas import tpu as pltpu
from jax.sharding import PartitionSpec as P

HEADS = 16
HD = 128
KVH = 4
NS_STEPS = 5
STEP = 10


NORM_EPS = 1e-05
ROPE_BASE = 10000.0
EXIT_EARLY = 0.25
EXIT_LAST = 1.0
CLIP_NORM = 0.02
BETA_ONE = 0.9
BETA_TWO = 0.95
ADAM_EPS = 1e-08
RATE_ADAM = 0.02
RATE_GAIN = 0.3
RATE_MUON = 0.3
WEIGHT_DECAY = 0.1
MOMENTUM = 0.95
NEWTON_A = 3.4445
NEWTON_B = -4.775
NEWTON_C = 2.0315
MASKED = -1e30
LOW = jnp.bfloat16
FULL = jnp.float32
BOTH = ("wide", "narrow")
ROWS_IN_BLOCK = 1024
UNROLL = 16
VMEM_BYTES = 56 * 1024 * 1024


def dot(first, second, first_dim, second_dim):
    return lax.dot_general(
        first, second, (((first_dim,), (second_dim,)), ((), ())), preferred_element_type=FULL
    )


def norm_rows(values, gain_row):
    return (
        values * lax.rsqrt(jnp.mean(values * values, axis=-1, keepdims=True) + NORM_EPS) * gain_row
    )


def norm_back(values, gain_row, grad):
    output, pull = jax.vjp(norm_rows, values, gain_row)
    return pull(grad)


def segments_at(lens, where_at):
    ends = jnp.cumsum(lens)
    return jnp.sum((where_at[:, None] >= ends[None, :]).astype(jnp.int32), axis=1)


def angles_at(lens, where_at):
    segment = segments_at(lens, where_at)
    starts = jnp.cumsum(lens) - lens
    member = segment[:, None] == jnp.arange(lens.shape[0], dtype=jnp.int32)[None, :]
    begin = jnp.sum(jnp.where(member, starts[None, :], 0), axis=1)
    offset_pos = (where_at - begin).astype(FULL)
    inverse = ROPE_BASE ** (-2.0 * jnp.arange(HD // 2, dtype=FULL) / HD)
    angle = offset_pos[:, None] * inverse[None, :]
    return (segment, jnp.cos(angle), jnp.sin(angle))


def rotate(values, cosine, sine):
    half = values.shape[-1] // 2
    first, second = (values[..., :half], values[..., half:])
    return jnp.concatenate(
        [first * cosine - second * sine, second * cosine + first * sine], axis=-1
    )


def unrotate(values, cosine, sine):
    return rotate(values, cosine, -sine)


MESH = pl.DeviceIdType.MESH
ANY = pl.BlockSpec(memory_space=pl.ANY)
VMEM = pl.BlockSpec(memory_space=pltpu.VMEM)


def others(axis, count):
    me = lax.axis_index(axis)
    return [{axis: lax.rem(me + step, count)} for step in range(1, count)]


def push(source, target, send, receive, device):
    return pltpu.make_async_remote_copy(
        src_ref=source,
        dst_ref=target,
        send_sem=send,
        recv_sem=receive,
        device_id=device,
        device_id_type=MESH,
    )


def arrived(block, send, receive, device):
    push(block, block, send, receive, device).wait_recv()


def like(values):
    return jax.ShapeDtypeStruct(values.shape, values.dtype)


def struct(shape, dtype):
    return jax.ShapeDtypeStruct(shape, dtype)


def sems(*shape):
    return pltpu.SemaphoreType.DMA(shape)


class Task:
    def __init__(self, inputs, outputs, scratch, steps, place_in, place_out, axes):
        self.inputs, self.outputs, self.scratch, self.steps = inputs, outputs, scratch, steps
        self.place_in = [place_in] * len(inputs)
        self.place_out = [place_out] * len(outputs)
        self.axes = axes


def launch(tasks, ident, name):
    axes = sorted(set(axis for task in tasks for axis in task.axes))
    inputs = [a for task in tasks for a in task.inputs]
    outputs = [a for task in tasks for a in task.outputs]
    scratch = [a for task in tasks for a in task.scratch]

    def body(*refs):
        refs = list(refs)
        ins = refs[: len(inputs)]
        outs = refs[len(inputs) : len(inputs) + len(outputs)]
        extra = refs[len(inputs) + len(outputs) :]
        barrier = pltpu.get_barrier_semaphore()
        targets = [device for axis in axes for device in others(axis, lax.axis_size(axis))]
        for device in targets:
            pl.semaphore_signal(barrier, inc=1, device_id=device, device_id_type=MESH)
        pl.semaphore_wait(barrier, len(targets))
        live = []
        for task in tasks:
            counts = (len(task.inputs), len(task.outputs), len(task.scratch))
            live.append(task.steps(ins[: counts[0]], outs[: counts[1]], extra[: counts[2]]))
            ins, outs, extra = ins[counts[0] :], outs[counts[1] :], extra[counts[2] :]
        while live:
            live = [steps for steps in live if next(steps, 0) is None]

    size = sum(a.size * a.dtype.itemsize for a in list(inputs) + list(outputs))
    return pl.pallas_call(
        body,
        out_shape=outputs,
        in_specs=[place for task in tasks for place in task.place_in],
        out_specs=[place for task in tasks for place in task.place_out],
        scratch_shapes=scratch,
        compiler_params=pltpu.CompilerParams(
            collective_id=ident, has_side_effects=True, vmem_limit_bytes=VMEM_BYTES
        ),
        cost_estimate=pl.CostEstimate(flops=0, bytes_accessed=8 * size, transcendentals=0),
        name=name,
    )(*inputs)


def gather_wide(values):
    count = lax.axis_size("wide")
    chips = count // 2

    def steps(ins, outs, scratch):
        (x_ref,), (out_ref,), (send, receive, local) = ins, outs, scratch
        me = lax.axis_index("wide")
        mate = me + 1 - 2 * lax.rem(me, 2)
        peers = [lax.rem(me + 2 * step, count) for step in range(1, chips)] + [mate]
        first = []
        for step, peer in enumerate(peers):
            copy = push(x_ref, out_ref.at[me], send.at[step], receive.at[me], {"wide": peer})
            copy.start()
            first.append(copy)
        keep = pltpu.make_async_copy(x_ref, out_ref.at[me], local)
        keep.start()
        yield
        second = []
        for step in range(1, chips):
            source = lax.rem(me - 2 * step + count, count)
            block = out_ref.at[source]
            arrived(block, send.at[0], receive.at[source], {"wide": mate})
            copy = push(
                block, block, send.at[chips + step - 1], receive.at[source], {"wide": mate}
            )
            copy.start()
            second.append(copy)
        yield
        for step in range(chips):
            source = lax.rem(mate - 2 * step + count, count)
            arrived(out_ref.at[source], send.at[0], receive.at[source], {"wide": mate})
        for copy in first + second:
            copy.wait_send()
        keep.wait()

    shape = struct((count,) + values.shape, values.dtype)
    return Task(
        [values], [shape], [sems(count - 1), sems(count), sems()], steps, ANY, ANY, ["wide"]
    )


def trade(axis, values, source_of, target_of, shape):
    count = lax.axis_size(axis)

    def steps(ins, outs, scratch):
        (x_ref,), (out_ref,), (send, receive, local) = ins, outs, scratch
        me = lax.axis_index(axis)
        copies = []
        for step in range(1, count):
            peer = lax.rem(me + step, count)
            copy = push(
                source_of(x_ref, peer),
                target_of(out_ref, me),
                send.at[step - 1],
                receive.at[me],
                {axis: peer},
            )
            copy.start()
            copies.append(copy)
        keep = pltpu.make_async_copy(source_of(x_ref, me), target_of(out_ref, me), local)
        keep.start()
        yield
        yield
        for step in range(1, count):
            source = lax.rem(me - step + count, count)
            arrived(
                target_of(out_ref, source), send.at[0], receive.at[source], {axis: source}
            )
        for copy in copies:
            copy.wait_send()
        keep.wait()

    return Task(
        [values],
        [struct(shape, values.dtype)],
        [sems(count - 1), sems(count), sems()],
        steps,
        ANY,
        ANY,
        [axis],
    )


def block_at(ref, spot):
    return ref.at[spot]


def whole_at(ref, spot):
    return ref


def columns_of(size):
    def at(ref, spot):
        return ref.at[:, pl.ds(pl.multiple_of(spot * size, size), size)]

    return at


def swap_blocks(axis, values):
    return trade(axis, values, block_at, block_at, values.shape)


def gather_blocks(axis, values):
    shape = (lax.axis_size(axis),) + values.shape
    return trade(axis, values, whole_at, block_at, shape)


def split_columns(axis, values):
    count = lax.axis_size(axis)
    rows, size = values.shape[0], values.shape[1] // count
    return trade(axis, values, columns_of(size), block_at, (count, rows, size))


def join_columns(axis, values):
    count, rows, size = values.shape
    return trade(axis, values, block_at, columns_of(size), (rows, count * size))


def collect(count, parts_ref, slots, send, receive):
    me = lax.axis_index("narrow")
    copies = []
    for step in range(1, count):
        peer = lax.rem(me + step, count)
        copy = push(
            parts_ref.at[peer],
            slots.at[me],
            send.at[step - 1],
            receive.at[me],
            {"narrow": peer},
        )
        copy.start()
        copies.append(copy)
    return copies


def collected(count, parts_ref, slots, send, receive):
    me = lax.axis_index("narrow")
    total = parts_ref[me].astype(FULL)
    for step in range(1, count):
        source = lax.rem(me - step + count, count)
        arrived(slots.at[source], send.at[0], receive.at[source], {"narrow": source})
        total = total + slots[source].astype(FULL)
    return total


def share(count, low, all_ref, send, receive):
    me = lax.axis_index("narrow")
    all_ref[me] = low
    copies = []
    for step in range(1, count):
        peer = lax.rem(me + step, count)
        copy = push(
            all_ref.at[me], all_ref.at[me], send.at[step - 1], receive.at[me], {"narrow": peer}
        )
        copy.start()
        copies.append(copy)
    return copies


def shared(count, all_ref, send, receive):
    me = lax.axis_index("narrow")
    for step in range(1, count):
        source = lax.rem(me - step + count, count)
        arrived(all_ref.at[source], send.at[0], receive.at[source], {"narrow": source})


def narrow_sems(count):
    return [sems(count - 1), sems(count)]


def settle(partial, base, other, keep_row, gain_row):
    count = lax.axis_size("narrow")
    rows, width = base.shape

    def steps(ins, outs, scratch):
        parts_ref, base_ref, other_ref, keep_ref, gain_ref = ins
        own_ref, all_ref = outs
        slots, send, receive, send_all, receive_all = scratch
        copies = collect(count, parts_ref, slots, send, receive)
        yield
        total = collected(count, parts_ref, slots, send, receive)
        total = jnp.where(keep_ref[...] > 0, total + base_ref[...], other_ref[...])
        own_ref[...] = total
        low = norm_rows(total, gain_ref[...]).astype(LOW)
        copies = copies + share(count, low, all_ref, send_all, receive_all)
        yield
        shared(count, all_ref, send_all, receive_all)
        for copy in copies:
            copy.wait_send()

    return Task(
        [partial.reshape(count, rows, width), base, other, keep_row, gain_row],
        [struct((rows, width), FULL), struct((count, rows, width), LOW)],
        [pltpu.VMEM((count, rows, width), partial.dtype)]
        + narrow_sems(count)
        + narrow_sems(count),
        steps,
        VMEM,
        VMEM,
        ["narrow"],
    )


def settle_back(partial, values, add, keep_row, gain_row):
    count = lax.axis_size("narrow")
    rows, width = values.shape

    def steps(ins, outs, scratch):
        parts_ref, values_ref, add_ref, keep_ref, gain_ref = ins
        own_ref, gain_grad_ref, all_ref = outs
        slots, send, receive, send_all, receive_all = scratch
        copies = collect(count, parts_ref, slots, send, receive)
        yield
        grad = collected(count, parts_ref, slots, send, receive)
        held = values_ref[...]
        root = lax.rsqrt(jnp.mean(held * held, axis=-1, keepdims=True) + NORM_EPS)
        scaled = gain_ref[...] * grad
        inner = jnp.mean(held * scaled, axis=-1, keepdims=True)
        own = add_ref[...] + root * scaled - held * (root * root * root * inner)
        gain_grad_ref[...] = jnp.sum(held * root * grad, axis=0, keepdims=True)
        own_ref[...] = own
        low = (own * keep_ref[...]).astype(LOW)
        copies = copies + share(count, low, all_ref, send_all, receive_all)
        yield
        shared(count, all_ref, send_all, receive_all)
        for copy in copies:
            copy.wait_send()

    return Task(
        [partial.reshape(count, rows, width), values, add, keep_row, gain_row],
        [
            struct((rows, width), FULL),
            struct((1, width), FULL),
            struct((count, rows, width), LOW),
        ],
        [pltpu.VMEM((count, rows, width), partial.dtype)]
        + narrow_sems(count)
        + narrow_sems(count),
        steps,
        VMEM,
        VMEM,
        ["narrow"],
    )


def sum_narrow(partial):
    count = lax.axis_size("narrow")
    rows, width = partial.shape[0] // count, partial.shape[1]

    def steps(ins, outs, scratch):
        (parts_ref,), (own_ref,), (slots, send, receive) = ins, outs, scratch
        copies = collect(count, parts_ref, slots, send, receive)
        yield
        yield
        own_ref[...] = collected(count, parts_ref, slots, send, receive)
        for copy in copies:
            copy.wait_send()

    return Task(
        [partial.reshape(count, rows, width)],
        [struct((rows, width), FULL)],
        [pltpu.VMEM((count, rows, width), partial.dtype)] + narrow_sems(count),
        steps,
        VMEM,
        VMEM,
        ["narrow"],
    )


def fetch_rows(found, rows):
    deep, wide = lax.axis_size("narrow"), lax.axis_size("wide")
    columns = found.shape[2]

    def steps(ins, outs, scratch):
        (found_ref,), (out_ref,) = ins, outs
        rightward, leftward, final = scratch[:3]
        send_right, receive_right, send_left, receive_left = scratch[3:7]
        send_wide, receive_wide, local = scratch[7:]
        spot = lax.axis_index("narrow")
        me = lax.axis_index("wide")

        def right_copy(part, source):
            return push(
                source,
                rightward.at[part],
                send_right.at[part],
                receive_right.at[part],
                {"narrow": lax.rem(spot + 1, deep)},
            )

        def left_copy(part, source):
            return push(
                source,
                leftward.at[part],
                send_left.at[part],
                receive_left.at[part],
                {"narrow": lax.rem(spot + deep - 1, deep)},
            )

        for step in range(deep - 1):
            right, left = deep - 1 - step, step

            @pl.when((spot == 0) & (right > 0))
            def _():
                right_copy(right, found_ref.at[right]).start()

            @pl.when((spot == deep - 1) & (left < deep - 1))
            def _():
                left_copy(left, found_ref.at[left]).start()

        yield
        for step in range(deep - 1):
            right, left = deep - 1 - step, step

            @pl.when((spot > 0) & (right > spot))
            def _():
                right_copy(right, rightward.at[right]).wait_recv()
                rightward[right] = rightward[right] + found_ref[right]
                right_copy(right, rightward.at[right]).start()

            @pl.when((spot < deep - 1) & (left < spot))
            def _():
                left_copy(left, leftward.at[left]).wait_recv()
                leftward[left] = leftward[left] + found_ref[left]
                left_copy(left, leftward.at[left]).start()

        final[...] = found_ref[spot]

        @pl.when(spot > 0)
        def _():
            right_copy(spot, rightward.at[spot]).wait_recv()
            final[...] = final[...] + rightward[spot]

        @pl.when(spot < deep - 1)
        def _():
            left_copy(spot, leftward.at[spot]).wait_recv()
            final[...] = final[...] + leftward[spot]

        def rows_for(device):
            return final.at[pl.ds(pl.multiple_of(device * rows, rows), rows)]

        def columns_from(device):
            return columns_of(columns)(out_ref, device)

        copies = []
        for step in range(1, wide):
            peer = lax.rem(me + step, wide)
            copy = push(
                rows_for(peer),
                columns_from(me),
                send_wide.at[step - 1],
                receive_wide.at[me],
                {"wide": peer},
            )
            copy.start()
            copies.append(copy)
        keep = pltpu.make_async_copy(rows_for(me), columns_from(me), local)
        keep.start()
        for step in range(1, wide):
            source = lax.rem(me - step + wide, wide)
            arrived(
                columns_from(source), send_wide.at[0], receive_wide.at[source], {"wide": source}
            )
        yield
        for copy in copies:
            copy.wait_send()
        keep.wait()
        for step in range(deep - 1):
            right, left = deep - 1 - step, step

            @pl.when(right > spot)
            def _():
                right_copy(right, found_ref.at[right]).wait_send()

            @pl.when(left < spot)
            def _():
                left_copy(left, found_ref.at[left]).wait_send()

    task = Task(
        [found],
        [struct((rows, wide * columns), found.dtype)],
        [pltpu.VMEM(found.shape, found.dtype)] * 2
        + [pltpu.VMEM(found.shape[1:], found.dtype)]
        + [sems(deep)] * 4
        + [sems(wide - 1), sems(wide), sems()],
        steps,
        VMEM,
        ANY,
        ["narrow", "wide"],
    )
    return task


def return_rows(rows):
    deep, wide = lax.axis_size("narrow"), lax.axis_size("wide")
    count, width = rows.shape
    columns = width // wide

    def steps(ins, outs, scratch):
        (rows_ref,), (out_ref,) = ins, outs
        send_right, send_left, receive_deep, send_wide, receive_wide, local = scratch
        spot = lax.axis_index("narrow")
        me = lax.axis_index("wide")
        part_of = functools.partial(columns_of(columns), rows_ref)

        def landing(device):
            return out_ref.at[spot, pl.ds(pl.multiple_of(device * count, count), count)]

        copies = []
        for step in range(1, wide):
            peer = lax.rem(me + step, wide)
            copy = push(
                part_of(peer),
                landing(me),
                send_wide.at[step - 1],
                receive_wide.at[me],
                {"wide": peer},
            )
            copy.start()
            copies.append(copy)
        keep = pltpu.make_async_copy(part_of(me), landing(me), local)
        keep.start()
        yield
        for step in range(1, wide):
            source = lax.rem(me - step + wide, wide)
            arrived(landing(source), send_wide.at[0], receive_wide.at[source], {"wide": source})
        keep.wait()

        def right_copy(part):
            return push(
                out_ref.at[part],
                out_ref.at[part],
                send_right.at[part],
                receive_deep.at[part],
                {"narrow": lax.rem(spot + 1, deep)},
            )

        def left_copy(part):
            return push(
                out_ref.at[part],
                out_ref.at[part],
                send_left.at[part],
                receive_deep.at[part],
                {"narrow": lax.rem(spot + deep - 1, deep)},
            )

        @pl.when(spot < deep - 1)
        def _():
            right_copy(spot).start()

        @pl.when(spot > 0)
        def _():
            left_copy(spot).start()

        for step in range(1, deep):
            yield

            @pl.when(spot >= step)
            def _():
                right_copy(spot - step).wait_recv()

                @pl.when(spot < deep - 1)
                def _():
                    right_copy(spot - step).start()

            @pl.when(spot + step < deep)
            def _():
                left_copy(spot + step).wait_recv()

                @pl.when(spot > 0)
                def _():
                    left_copy(spot + step).start()

        for part in range(deep):

            @pl.when((part <= spot) & (spot < deep - 1))
            def _():
                right_copy(part).wait_send()

            @pl.when((part >= spot) & (spot > 0))
            def _():
                left_copy(part).wait_send()

        for copy in copies:
            copy.wait_send()

    return Task(
        [rows],
        [struct((deep, wide * count, columns), rows.dtype)],
        [sems(deep)] * 3 + [sems(wide - 1), sems(wide), sems()],
        steps,
        ANY,
        ANY,
        ["narrow", "wide"],
    )


def sum_wide(partial):
    count = lax.axis_size("wide")
    chips = count // 2
    rows, width = partial.shape[0] // count, partial.shape[1]

    def steps(ins, outs, scratch):
        (parts_ref,), (out_ref,) = ins, outs
        from_mate, paired, slots, send_mate, receive_mate, send, receive = scratch
        me = lax.axis_index("wide")
        side = lax.rem(me, 2)
        mate = me + 1 - 2 * side
        my_chip = me // 2
        mate_copies = []
        for step in range(chips):
            chip = lax.rem(my_chip + 1 + step, chips)
            copy = push(
                parts_ref.at[2 * chip + 1 - side],
                from_mate.at[chip],
                send_mate.at[step],
                receive_mate.at[chip],
                {"wide": mate},
            )
            copy.start()
            mate_copies.append(copy)
        yield
        copies = []
        for step in range(chips):
            chip = lax.rem(my_chip + 1 + step, chips)
            arrived(from_mate.at[chip], send_mate.at[0], receive_mate.at[chip], {"wide": mate})
            both = parts_ref[2 * chip + side].astype(FULL) + from_mate[chip].astype(FULL)
            if step < chips - 1:
                paired[chip] = both.astype(LOW)
                copy = push(
                    paired.at[chip],
                    slots.at[my_chip],
                    send.at[step],
                    receive.at[my_chip],
                    {"wide": 2 * chip + side},
                )
                copy.start()
                copies.append(copy)
            else:
                out_ref[...] = both
        yield
        for step in range(1, chips):
            chip = lax.rem(my_chip - step + chips, chips)
            arrived(slots.at[chip], send.at[0], receive.at[chip], {"wide": 2 * chip + side})
            out_ref[...] = out_ref[...] + slots[chip].astype(FULL)
        for copy in mate_copies + copies:
            copy.wait_send()

    return Task(
        [partial.reshape(count, rows, width)],
        [struct((rows, width), FULL)],
        [pltpu.VMEM((chips, rows, width), LOW)] * 3
        + [sems(chips), sems(chips), sems(max(chips - 1, 1)), sems(chips)],
        steps,
        VMEM,
        VMEM,
        ["wide"],
    )


def merge_stats(first, second):
    peak = jnp.maximum(first[0:1], second[0:1])
    total = first[1:2] * jnp.exp(first[0:1] - peak) + second[1:2] * jnp.exp(second[0:1] - peak)
    return jnp.concatenate([peak, total, first[2:3] + second[2:3]], axis=0)


def add_two(first, second):
    return first + second


def combine(values, join):
    deep, wide = lax.axis_size("narrow"), lax.axis_size("wide")

    def steps(ins, outs, scratch):
        (x_ref,), (out_ref,) = ins, outs
        wide_slots, deep_slots, send_wide, receive_wide, send_deep, receive_deep = scratch

        def start(axis, count, slots, value, send, receive):
            me = lax.axis_index(axis)
            slots[me] = value
            copies = []
            for step in range(1, count):
                peer = lax.rem(me + step, count)
                copy = push(
                    slots.at[me], slots.at[me], send.at[step - 1], receive.at[me], {axis: peer}
                )
                copy.start()
                copies.append(copy)
            return copies

        def finish(axis, count, slots, send, receive):
            me = lax.axis_index(axis)
            for step in range(1, count):
                source = lax.rem(me - step + count, count)
                arrived(slots.at[source], send.at[0], receive.at[source], {axis: source})
            total = slots[0]
            for source in range(1, count):
                total = join(total, slots[source])
            return total

        first = start("wide", wide, wide_slots, x_ref[...], send_wide, receive_wide)
        yield
        total = finish("wide", wide, wide_slots, send_wide, receive_wide)
        second = start("narrow", deep, deep_slots, total, send_deep, receive_deep)
        yield
        out_ref[...] = finish("narrow", deep, deep_slots, send_deep, receive_deep)
        for copy in first + second:
            copy.wait_send()

    return Task(
        [values],
        [like(values)],
        [
            pltpu.VMEM((wide,) + values.shape, values.dtype),
            pltpu.VMEM((deep,) + values.shape, values.dtype),
            sems(wide - 1),
            sems(wide),
            sems(deep - 1),
            sems(deep),
        ],
        steps,
        VMEM,
        VMEM,
        ["narrow", "wide"],
    )


def gather_both(values):
    deep, wide = lax.axis_size("narrow"), lax.axis_size("wide")

    def steps(ins, outs, scratch):
        (x_ref,), (out_ref,) = ins, outs
        send_wide, receive_wide, send_deep, receive_deep = scratch
        me = lax.axis_index("wide")
        spot = lax.axis_index("narrow")
        out_ref[spot, me] = x_ref[...]
        copies = []
        for step in range(1, wide):
            peer = lax.rem(me + step, wide)
            block = out_ref.at[spot, me]
            copy = push(block, block, send_wide.at[step - 1], receive_wide.at[me], {"wide": peer})
            copy.start()
            copies.append(copy)
        yield
        for step in range(1, wide):
            source = lax.rem(me - step + wide, wide)
            block = out_ref.at[spot, source]
            arrived(block, send_wide.at[0], receive_wide.at[source], {"wide": source})
        for step in range(1, deep):
            peer = lax.rem(spot + step, deep)
            block = out_ref.at[spot]
            copy = push(
                block, block, send_deep.at[step - 1], receive_deep.at[spot], {"narrow": peer}
            )
            copy.start()
            copies.append(copy)
        yield
        for step in range(1, deep):
            source = lax.rem(spot - step + deep, deep)
            block = out_ref.at[source]
            arrived(block, send_deep.at[0], receive_deep.at[source], {"narrow": source})
        for copy in copies:
            copy.wait_send()

    return Task(
        [values],
        [struct((deep, wide) + values.shape, values.dtype)],
        [sems(wide - 1), sems(wide), sems(deep - 1), sems(deep)],
        steps,
        VMEM,
        VMEM,
        ["narrow", "wide"],
    )


def feed_body(inner_ref, weight_ref, gate_ref, up_ref, hidden_ref, out_ref, total):
    part = pl.program_id(0)
    inner = inner_ref[...]
    gate = dot(inner, weight_ref[0, 0], 1, 1)
    up = dot(inner, weight_ref[0, 1], 1, 1)
    hidden = (jax.nn.silu(gate) * up).astype(LOW)
    gate_ref[0] = gate
    up_ref[0] = up
    hidden_ref[0] = hidden
    product = dot(hidden, weight_ref[0, 2], 1, 0)

    @pl.when(part == 0)
    def _():
        total[...] = product

    @pl.when(part > 0)
    def _():
        total[...] = total[...] + product

    @pl.when(part == pl.num_programs(0) - 1)
    def _():
        out_ref[...] = total[...].astype(LOW)


def feed(inner, weight):
    parts, _, size, width = weight.shape
    sel = inner.shape[0]
    same = pl.BlockSpec((sel, width), lambda part: (0, 0))
    slab = pl.BlockSpec((1, sel, size), lambda part: (part, 0, 0))
    return pl.pallas_call(
        feed_body,
        grid=(parts,),
        in_specs=[same, pl.BlockSpec((1, 3, size, width), lambda part: (part, 0, 0, 0))],
        out_specs=[slab, slab, slab, same],
        out_shape=[
            struct((parts, sel, size), FULL),
            struct((parts, sel, size), FULL),
            struct((parts, sel, size), LOW),
            struct((sel, width), LOW),
        ],
        scratch_shapes=[pltpu.VMEM((sel, width), FULL)],
        compiler_params=pltpu.CompilerParams(vmem_limit_bytes=VMEM_BYTES),
        cost_estimate=pl.CostEstimate(
            flops=6 * sel * parts * size * width,
            bytes_accessed=weight.size * 2,
            transcendentals=0,
        ),
        name="feed",
    )(inner, weight)


def feed_back_body(grad_ref, weight_ref, gate_ref, up_ref, hidden_ref, acts_ref, out_ref, total):
    part = pl.program_id(0)
    grad_hidden = dot(grad_ref[...], weight_ref[0, 2], 1, 1)
    gate = gate_ref[0]
    sigma = jax.nn.sigmoid(gate)
    grad_gate = (grad_hidden * up_ref[0] * sigma * (1.0 + gate * (1.0 - sigma))).astype(LOW)
    grad_up = (grad_hidden * gate * sigma).astype(LOW)
    acts_ref[0, 0] = grad_gate
    acts_ref[0, 1] = grad_up
    acts_ref[0, 2] = hidden_ref[0]
    product = dot(grad_gate, weight_ref[0, 0], 1, 0) + dot(grad_up, weight_ref[0, 1], 1, 0)

    @pl.when(part == 0)
    def _():
        total[...] = product

    @pl.when(part > 0)
    def _():
        total[...] = total[...] + product

    @pl.when(part == pl.num_programs(0) - 1)
    def _():
        out_ref[...] = total[...].astype(LOW)


def feed_back(grad, weight, gate, up, hidden):
    parts, _, size, width = weight.shape
    sel = grad.shape[0]
    same = pl.BlockSpec((sel, width), lambda part: (0, 0))
    slab = pl.BlockSpec((1, sel, size), lambda part: (part, 0, 0))
    return pl.pallas_call(
        feed_back_body,
        grid=(parts,),
        in_specs=[same, pl.BlockSpec((1, 3, size, width), lambda part: (part, 0, 0, 0))]
        + [slab] * 3,
        out_specs=[pl.BlockSpec((1, 3, sel, size), lambda part: (part, 0, 0, 0)), same],
        out_shape=[struct((parts, 3, sel, size), LOW), struct((sel, width), LOW)],
        scratch_shapes=[pltpu.VMEM((sel, width), FULL)],
        compiler_params=pltpu.CompilerParams(vmem_limit_bytes=VMEM_BYTES),
        cost_estimate=pl.CostEstimate(
            flops=6 * sel * parts * size * width,
            bytes_accessed=weight.size * 2,
            transcendentals=0,
        ),
        name="feed_back",
    )(grad, weight, gate, up, hidden)


def newton_body(chunk, x_ref, out_ref, current, low, gram, rest_low):
    rows, width = current.shape
    parts = rows // chunk
    eye_rows = lax.broadcasted_iota(jnp.int32, (chunk, rows), 0)
    eye_columns = lax.broadcasted_iota(jnp.int32, (chunk, rows), 1)

    def strip(part):
        return pl.ds(pl.multiple_of(part * chunk, chunk), chunk)

    def eye(part):
        return eye_rows + part * chunk == eye_columns

    def over(function, start):
        return lax.fori_loop(0, parts, function, start)

    def square_sum(part, total):
        values = x_ref[0, strip(part), :]
        return total + jnp.sum(values * values)

    scale = 1.0 / (jnp.sqrt(over(square_sum, jnp.float32(0.0))) + 1e-07)

    def begin(part, carry):
        values = x_ref[0, strip(part), :] * scale
        current[strip(part), :] = values
        low[strip(part), :] = values.astype(LOW)
        return carry

    over(begin, 0)

    def iteration(turn, carry):
        def gram_rows(part, trace):
            rows_here = dot(low[strip(part), :], low[...], 1, 1)
            gram[strip(part), :] = rows_here
            return trace + jnp.sum(jnp.where(eye(part), rows_here, 0.0))

        middle = over(gram_rows, jnp.float32(0.0)) / rows

        def centre(part, carry):
            rest = gram[strip(part), :] - jnp.where(eye(part), middle, 0.0)
            rest_low[strip(part), :] = rest.astype(LOW)
            return carry

        over(centre, 0)

        def poly_rows(part, trace):
            square = dot(rest_low[strip(part), :], rest_low[...], 1, 0)
            rows_here = gram[strip(part), :]
            rest = rows_here - jnp.where(eye(part), middle, 0.0)
            square = square + 2.0 * middle * rest + jnp.where(eye(part), middle * middle, 0.0)
            rows_here = NEWTON_B * rows_here + NEWTON_C * square
            gram[strip(part), :] = rows_here
            return trace + jnp.sum(jnp.where(eye(part), rows_here, 0.0))

        second = over(poly_rows, jnp.float32(0.0)) / rows

        def centre_again(part, carry):
            rest = gram[strip(part), :] - jnp.where(eye(part), second, 0.0)
            rest_low[strip(part), :] = rest.astype(LOW)
            return carry

        over(centre_again, 0)

        def apply(part, carry):
            current[strip(part), :] = (NEWTON_A + second) * current[strip(part), :] + dot(
                rest_low[strip(part), :], low[...], 1, 0
            )
            return carry

        over(apply, 0)

        def lower(part, carry):
            low[strip(part), :] = current[strip(part), :].astype(LOW)
            return carry

        over(lower, 0)
        return carry

    lax.fori_loop(0, NS_STEPS, iteration, 0)
    out_ref[0] = low[...]


def newton(blocks):
    count, rows, width = blocks.shape
    chunk = next(size for size in (176, 128, 88, 64, rows) if rows % size == 0)
    spec = pl.BlockSpec((1, rows, width), lambda block: (block, 0, 0))
    return pl.pallas_call(
        functools.partial(newton_body, chunk),
        grid=(count,),
        in_specs=[spec],
        out_specs=spec,
        out_shape=struct(blocks.shape, LOW),
        scratch_shapes=[
            pltpu.VMEM((rows, width), FULL),
            pltpu.VMEM((rows, width), LOW),
            pltpu.VMEM((rows, rows), FULL),
            pltpu.VMEM((rows, rows), LOW),
        ],
        compiler_params=pltpu.CompilerParams(vmem_limit_bytes=VMEM_BYTES),
        cost_estimate=pl.CostEstimate(
            flops=NS_STEPS * count * (4 * rows * rows * width + 2 * rows * rows * rows),
            bytes_accessed=6 * blocks.size,
            transcendentals=0,
        ),
        name="newton",
    )(blocks)


def lookup_body(ids_ref, table_ref, out_ref, held, rows, sem):
    block = pl.program_id(0)
    vocab = table_ref.shape[0]

    @pl.when(block == 0)
    def _():
        load = pltpu.make_async_copy(table_ref, held.at[pl.ds(0, vocab)], sem)
        load.start()
        held[pl.ds(vocab, 8), :] = jnp.zeros((8, held.shape[1]), FULL)
        load.wait()

    def step(group, carry):
        for member in range(UNROLL):
            at = group * UNROLL + member
            spot = ids_ref[block * ROWS_IN_BLOCK + at]
            rows[pl.ds(at, 1), :] = held[pl.ds(spot, 1), :]
        return carry

    lax.fori_loop(0, ROWS_IN_BLOCK // UNROLL, step, 0)
    out_ref[...] = rows[...].astype(LOW)


def lookup(table, ids):
    vocab, columns = table.shape
    count = ids.shape[0]
    return pl.pallas_call(
        lookup_body,
        grid_spec=pltpu.PrefetchScalarGridSpec(
            num_scalar_prefetch=1,
            grid=(count // ROWS_IN_BLOCK,),
            in_specs=[pl.BlockSpec(memory_space=pl.ANY)],
            out_specs=pl.BlockSpec((ROWS_IN_BLOCK, columns), lambda block, ids_ref: (block, 0)),
            scratch_shapes=[
                pltpu.VMEM((vocab + 8, columns), FULL),
                pltpu.VMEM((ROWS_IN_BLOCK, columns), FULL),
                pltpu.SemaphoreType.DMA,
            ],
        ),
        out_shape=jax.ShapeDtypeStruct((count, columns), LOW),
        compiler_params=pltpu.CompilerParams(vmem_limit_bytes=VMEM_BYTES),
        cost_estimate=pl.CostEstimate(
            flops=0, bytes_accessed=vocab * columns * 4 + count * columns * 32, transcendentals=0
        ),
        name="lookup",
    )(ids, table)


def spread_body(ids_ref, rows_ref, head_ref, out_ref, square_ref, even, odd, rows, sem):
    block = pl.program_id(0)
    vocab = out_ref.shape[0]

    @pl.when(block == 0)
    def _():
        even[...] = jnp.zeros_like(even)
        odd[...] = jnp.zeros_like(odd)

    rows[...] = rows_ref[...].astype(FULL)

    def step(group, carry):
        for member in range(UNROLL):
            at = group * UNROLL + member
            spot = pl.ds(ids_ref[block * ROWS_IN_BLOCK + at], 1)
            total = even if member % 2 == 0 else odd
            total[spot, :] = total[spot, :] + rows[pl.ds(at, 1), :]
        return carry

    lax.fori_loop(0, ROWS_IN_BLOCK // UNROLL, step, 0)

    @pl.when(block == pl.num_programs(0) - 1)
    def _():
        chunk = 256

        def finish(part, squares):
            spot = pl.ds(pl.multiple_of(part * chunk, chunk), chunk)
            value = even[spot, :] + odd[spot, :] + head_ref[spot, :].astype(FULL)
            even[spot, :] = value
            return squares + jnp.sum((value * value).reshape(chunk // 8, 8, -1), axis=0)

        squares = lax.fori_loop(
            0, vocab // chunk, finish, jnp.zeros((8, even.shape[1]), FULL)
        )
        square_ref[...] = squares
        store = pltpu.make_async_copy(even.at[pl.ds(0, vocab)], out_ref, sem)
        store.start()
        store.wait()


def spread(ids, rows, head):
    vocab, columns = head.shape
    count = ids.shape[0]
    return pl.pallas_call(
        spread_body,
        grid_spec=pltpu.PrefetchScalarGridSpec(
            num_scalar_prefetch=1,
            grid=(count // ROWS_IN_BLOCK,),
            in_specs=[
                pl.BlockSpec((ROWS_IN_BLOCK, columns), lambda block, ids_ref: (block, 0)),
                pl.BlockSpec((vocab, columns), lambda block, ids_ref: (0, 0)),
            ],
            out_specs=[
                pl.BlockSpec(memory_space=pl.ANY),
                pl.BlockSpec((8, columns), lambda block, ids_ref: (0, 0)),
            ],
            scratch_shapes=[
                pltpu.VMEM((vocab + 8, columns), FULL),
                pltpu.VMEM((vocab + 8, columns), FULL),
                pltpu.VMEM((ROWS_IN_BLOCK, columns), FULL),
                pltpu.SemaphoreType.DMA,
            ],
        ),
        out_shape=[
            jax.ShapeDtypeStruct((vocab, columns), FULL),
            jax.ShapeDtypeStruct((8, columns), FULL),
        ],
        compiler_params=pltpu.CompilerParams(vmem_limit_bytes=VMEM_BYTES),
        cost_estimate=pl.CostEstimate(
            flops=count * columns, bytes_accessed=count * columns * 64, transcendentals=0
        ),
        name="spread",
    )(ids, rows, head)


def adamw(weight, first_m, second_m, grad, rate, decay):
    first_new = BETA_ONE * first_m + (1.0 - BETA_ONE) * grad
    second_new = BETA_TWO * second_m + (1.0 - BETA_TWO) * grad * grad
    update = (
        first_new
        / (1.0 - BETA_ONE**STEP)
        / (jnp.sqrt(second_new / (1.0 - BETA_TWO**STEP)) + ADAM_EPS)
    )
    return (weight * (1.0 - rate * decay) - rate * update, first_new, second_new)


def cut_columns(values, count):
    rows, columns = values.shape
    return jnp.moveaxis(values.reshape(rows, count, columns // count), 1, 0)


def side_by_side(parts):
    count, rows, columns = parts.shape
    return jnp.moveaxis(parts, 0, 1).reshape(rows, count * columns)


def swap_by_shifts(parts, axis):
    count = lax.axis_size(axis)
    me = lax.axis_index(axis)
    result = parts
    for step in range(1, count):
        pairs = [(source, (source + step) % count) for source in range(count)]
        part = lax.dynamic_index_in_dim(parts, lax.rem(me + step, count), 0, False)
        part = lax.ppermute(part, axis, pairs)
        result = lax.dynamic_update_index_in_dim(
            result, part, lax.rem(me - step + count, count), 0
        )
    return result


def per_device(
    tokens,
    picks,
    targets,
    lengths,
    skip,
    embed,
    embed_m,
    embed_v,
    attn_qo,
    attn_qo_mom,
    attn_kv,
    attn_kv_mom,
    ffn,
    ffn_mom,
    gains,
    gains_m,
    gains_v,
):
    wide_count = lax.axis_size("wide")
    narrow_count = lax.axis_size("narrow")
    narrow_spot = lax.axis_index("narrow")
    wide_spot = lax.axis_index("wide")
    seq_len = tokens.shape[1]
    sel = picks.shape[1]
    vocab_rows, columns = embed.shape
    width = columns * wide_count
    own_rows = sel // narrow_count
    tok_rows = seq_len // narrow_count
    all_rows = own_rows + tok_rows
    heads_own = HEADS // narrow_count
    head_cols = heads_own * HD
    repeat = max(1, narrow_count // KVH)
    groups = KVH * repeat // narrow_count
    ffn_rows = ffn.shape[0]
    ffn_size = ffn_rows // narrow_count
    total_rows = wide_count * sel
    lens = lengths[0]
    pick_ids = picks[0]
    keep_layer = (1 - skip[0]).astype(FULL)
    keep_row = jnp.full((1, width), keep_layer)
    lanes = 128

    def box(flat):
        height = -(-flat.shape[0] // (8 * lanes)) * 8
        return jnp.pad(flat, (0, height * lanes - flat.shape[0])).reshape(height, lanes)

    ffn_low = jnp.moveaxis(ffn, 1, 0).astype(LOW)
    ffn_cut = ffn_low.reshape(3, narrow_count, ffn_size, ffn_low.shape[2])
    ffn_sub = swap_by_shifts(jnp.moveaxis(ffn_cut, 1, 0), "narrow")
    proj_own = jnp.concatenate(
        [attn_qo.reshape(columns, -1), attn_kv.reshape(columns, -1)], axis=1
    ).astype(LOW)
    proj = lax.all_gather(
        lax.all_gather(proj_own, "narrow", axis=0), "wide", axis=1, tiled=True
    )
    ffn_sub = jnp.moveaxis(ffn_sub, 0, 2).reshape(3, ffn_size, width)
    ffn_w = lax.all_gather(ffn_sub, "wide", axis=0)

    where_at = jnp.arange(seq_len, dtype=jnp.int32)
    pick_tokens = jnp.sum(
        jnp.where(pick_ids[:, None] == where_at[None, :], tokens[0][None, :], 0), axis=1
    )
    ints = box(jnp.concatenate([tokens[0], pick_tokens, targets[0]]))
    all_ints, all_gains = launch(
        [gather_wide(ints), gather_both(box(gains.astype(LOW).astype(FULL).reshape(-1)))],
        0,
        "gather_ids",
    )
    gain_size = gains.shape[1]
    gain_w = all_gains.reshape(narrow_count, wide_count, -1)[:, :, : 3 * gain_size]
    gain_w = gain_w.reshape(narrow_count, wide_count, 3, gain_size)
    gain_w = jnp.transpose(gain_w, (2, 1, 0, 3)).reshape(3, width)
    all_ints = all_ints.reshape(wide_count, -1)
    tokens_all = all_ints[:, :seq_len].reshape(wide_count, narrow_count, tok_rows)
    picked_all = all_ints[:, seq_len : seq_len + sel].reshape(wide_count, narrow_count, own_rows)
    targets_all = all_ints[:, seq_len + sel : seq_len + 2 * sel].reshape(-1)
    wanted = jnp.moveaxis(jnp.concatenate([tokens_all, picked_all], axis=2), 1, 0).reshape(-1)
    local_ids = wanted - narrow_spot * vocab_rows
    inside = (local_ids >= 0) & (local_ids < vocab_rows)
    spots = jnp.where(inside, local_ids, vocab_rows)
    found = lookup(embed, spots).reshape(narrow_count, wide_count * all_rows, columns)
    embed_cut = embed.astype(LOW).reshape(wide_count, vocab_rows // wide_count, columns)
    rows_low, table_own = launch(
        [fetch_rows(found, all_rows), join_columns("wide", embed_cut)], 1, "fetch_rows"
    )

    mom_qo = jnp.moveaxis(attn_qo_mom, 1, 0)
    mom_kv = jnp.moveaxis(attn_kv_mom, 1, 0)
    mom_ffn = jnp.moveaxis(ffn_mom, 1, 0)
    slot_rows, slot_cols = mom_ffn.shape[1:]

    def pack_small(qo_part, kv_part):
        flat = jnp.concatenate([qo_part.reshape(-1), kv_part.reshape(-1)])
        return jnp.pad(flat, (0, slot_rows * slot_cols - flat.shape[0])).reshape(
            slot_rows, slot_cols
        )

    def unpack_small(box_values):
        lead = box_values.shape[:-2]
        flat = box_values.reshape(lead + (-1,))
        qo_size, kv_size = mom_qo.size, mom_kv.size
        return (
            flat[..., :qo_size].reshape(lead + mom_qo.shape),
            flat[..., qo_size : qo_size + kv_size].reshape(lead + mom_kv.shape),
        )

    mom_parts = [mom_ffn[0], mom_ffn[1], mom_ffn[2], pack_small(mom_qo, mom_kv)]
    mom_parts = mom_parts + [jnp.zeros_like(mom_parts[0])] * (narrow_count - 4)
    mom_parts = jnp.stack(mom_parts).astype(LOW)

    seg_all = segments_at(lens, where_at)
    tok_at = narrow_spot * tok_rows + jnp.arange(tok_rows, dtype=jnp.int32)
    own_at = lax.dynamic_slice_in_dim(pick_ids, narrow_spot * own_rows, own_rows, 0)
    _, cosine_all, sine_all = angles_at(lens, where_at)
    _, cosine_tok, sine_tok = angles_at(lens, tok_at)
    _, cosine_own, sine_own = angles_at(lens, own_at)
    seg_mine, cosine, sine = angles_at(lens, pick_ids)

    q_w, o_w = proj[:, :, :head_cols], proj[:, :, head_cols : 2 * head_cols]
    kv_size = attn_kv.shape[2]
    k_w = proj[:, :, 2 * head_cols : 2 * head_cols + kv_size]
    v_w = proj[:, :, 2 * head_cols + kv_size :]

    def each_owner(rows, weight):
        return jnp.einsum("td,ndf->ntf", rows, weight, preferred_element_type=FULL)

    def by_heads(parts):
        return jnp.moveaxis(parts, 0, 1).reshape(tok_rows, KVH, HD)

    rows_full = rows_low.astype(FULL)
    normed_all = norm_rows(rows_full, gain_w[0]).astype(LOW)
    normed_tok, normed_own = normed_all[:tok_rows], normed_all[tok_rows:]
    keys_part = by_heads(each_owner(normed_tok, k_w))
    keys_part = rotate(keys_part, cosine_tok[:, None], sine_tok[:, None]).astype(LOW)
    values_part = by_heads(each_owner(normed_tok, v_w)).astype(LOW)
    by_head = jnp.moveaxis(jnp.stack([keys_part, values_part]), 2, 0)
    by_head = jnp.repeat(by_head, repeat, axis=0)
    by_head = by_head.reshape(narrow_count, groups, 2, tok_rows, HD)
    queries_part = each_owner(normed_own, q_w).reshape(narrow_count, own_rows, heads_own, HD)
    queries_part = rotate(queries_part, cosine_own[:, None], sine_own[:, None])
    queries_part = queries_part.astype(LOW).reshape(narrow_count, own_rows, head_cols)
    own_head, queries, start_low, tok_cols, pick_cols = launch(
        [
            swap_blocks("narrow", by_head),
            swap_blocks("narrow", queries_part),
            gather_blocks("narrow", rows_low[tok_rows:]),
            split_columns("wide", normed_tok),
            split_columns("wide", normed_own),
        ],
        2,
        "trade_heads",
    )
    own_head = jnp.transpose(own_head, (2, 1, 0, 3, 4)).reshape(2, groups, seq_len, HD)
    keys, values = own_head[0], own_head[1]
    start_h = start_low.reshape(sel, width).astype(FULL)

    grouped = queries.reshape(sel, groups, heads_own // groups, HD)
    scale = HD ** (-0.5)
    scores = jnp.einsum("tkgd,ksd->kgts", grouped, keys, preferred_element_type=FULL) * scale
    allowed = (seg_mine[:, None] == seg_all[None, :]) & (pick_ids[:, None] >= where_at[None, :])
    scores = jnp.where(allowed, scores, MASKED)
    shifted_exp = jnp.exp(scores - jnp.max(scores, axis=-1, keepdims=True))
    probs = shifted_exp / jnp.sum(shifted_exp, axis=-1, keepdims=True)
    probs_low = probs.astype(LOW)
    mixed = jnp.einsum("kgts,ksd->tkgd", probs_low, values, preferred_element_type=FULL)
    mixed = mixed.reshape(sel, head_cols).astype(LOW)

    early_part = norm_rows(start_h, gain_w[2]).astype(LOW)
    mixed_all, early, mixed_wide = launch(
        [
            gather_blocks("narrow", mixed),
            gather_wide(early_part),
            gather_wide(mixed),
        ],
        3,
        "gather_mixed",
    )
    early = early.reshape(total_rows, width)

    def own(values_all):
        return lax.dynamic_slice_in_dim(values_all, narrow_spot * own_rows, own_rows, 0)

    start_own = own(start_h)
    middle_all = start_h + jnp.einsum(
        "ntf,ndf->td", mixed_all, o_w, preferred_element_type=FULL
    )
    middle = own(middle_all)
    inner = norm_rows(middle_all, gain_w[1]).astype(LOW)
    gate, up, hidden, fed = feed(inner, ffn_w)
    final_own, late_part, inner_all = launch(
        [settle(fed, middle, start_own, keep_row, gain_w[2:3]), gather_wide(inner)], 4, "settle"
    )
    inner_all = inner_all.reshape(total_rows, width)

    table_count = table_own.shape[0]
    local_target = targets_all - (narrow_spot * vocab_rows + wide_spot * table_count)
    has_target = local_target[:, None] == jnp.arange(table_count, dtype=jnp.int32)[None, :]
    counted = (targets_all >= 0).astype(FULL)
    loss_count = jnp.sum(counted)

    def exit_logits(features):
        logits = dot(features, table_own, 1, 1)
        peak = jnp.max(logits, axis=-1)
        total = jnp.sum(jnp.exp(logits - peak[:, None]), axis=-1)
        picked = jnp.sum(jnp.where(has_target, logits, 0.0), axis=-1)
        return logits, jnp.stack([peak, total, picked])

    half = slot_rows // 2
    late, mom_top = launch(
        [
            gather_wide(late_part.reshape(sel, width)),
            swap_blocks("narrow", mom_parts[:, :half]),
        ],
        5,
        "gather_late",
    )
    late = late.reshape(total_rows, width)
    early_logits, early_stats = exit_logits(early)
    late_logits, late_stats = exit_logits(late)
    stats = jnp.concatenate([early_stats, late_stats], axis=1).reshape(3, 8, -1)
    stats = launch([combine(stats, merge_stats)], 6, "combine_stats")[0].reshape(3, -1)
    log_norms = stats[0] + jnp.log(stats[1])
    losses = log_norms - stats[2]
    loss_sum = jnp.sum(
        counted * (EXIT_EARLY * losses[:total_rows] + EXIT_LAST * losses[total_rows:])
    )

    def exit_back(logits, log_norm, weight, features):
        grad_logits = (
            (jnp.exp(logits - log_norm[:, None]) - has_target.astype(FULL))
            * (weight * counted)[:, None]
        ).astype(LOW)
        return dot(grad_logits, table_own, 1, 0).astype(LOW), dot(grad_logits, features, 0, 0)

    late_back, late_head = exit_back(late_logits, log_norms[total_rows:], EXIT_LAST, late)
    early_back, early_head = exit_back(early_logits, log_norms[:total_rows], EXIT_EARLY, early)
    grad_late, mom_low = launch(
        [sum_wide(late_back), swap_blocks("narrow", mom_parts[:, half:])], 7, "sum_late"
    )
    mom_owned = jnp.concatenate([mom_top, mom_low], axis=1)
    grad_head = (early_head + late_head).astype(LOW)

    grad_final, gain_late, grad_out, grad_early = launch(
        [
            settle_back(
                grad_late.astype(LOW),
                final_own,
                jnp.zeros_like(final_own),
                keep_row,
                gain_w[2:3],
            ),
            sum_wide(early_back),
        ],
        8,
        "settle_late",
    )
    grad_layer = grad_final * keep_layer
    grad_out = grad_out.reshape(sel, width)
    acts, fed_back = feed_back(grad_out, ffn_w, gate, up, hidden)
    grad_mid, gain_mid, grad_branch, grad_early, out_all = launch(
        [
            settle_back(fed_back, middle, grad_layer, keep_row, gain_w[1:2]),
            sum_narrow(grad_early.astype(LOW)),
            gather_wide(grad_out),
        ],
        9,
        "settle_middle",
    )
    grad_branch = grad_branch.reshape(sel, width)
    out_all = out_all.reshape(total_rows, width)
    grad_start_exit, gain_early = norm_back(start_own, gain_w[2], grad_early)

    o_own = lax.dynamic_index_in_dim(o_w, narrow_spot, 0, False)
    grad_mixed = dot(grad_branch, o_own, 1, 0).astype(LOW)
    grouped_grad = grad_mixed.reshape(sel, groups, heads_own // groups, HD)
    grad_probs = jnp.einsum("tkgd,ksd->kgts", grouped_grad, values, preferred_element_type=FULL)
    grad_scores = (
        probs * (grad_probs - jnp.sum(probs * grad_probs, axis=-1, keepdims=True))
    ).astype(LOW)
    grad_queries = (
        jnp.einsum("kgts,ksd->tkgd", grad_scores, keys, preferred_element_type=FULL) * scale
    ).reshape(sel, heads_own, HD)
    grad_queries = (
        unrotate(grad_queries, cosine[:, None], sine[:, None])
        .reshape(sel, head_cols)
        .astype(LOW)
    )
    grad_keys = jnp.einsum("kgts,tkgd->ksd", grad_scores, grouped, preferred_element_type=FULL)
    grad_keys = unrotate(grad_keys * scale, cosine_all, sine_all).astype(LOW)
    grad_values = jnp.einsum(
        "kgts,tkgd->ksd", probs_low, grouped_grad, preferred_element_type=FULL
    ).astype(LOW)
    kv_parts = jnp.stack([grad_keys, grad_values]).reshape(
        2, groups, narrow_count, tok_rows, HD
    )
    kv_parts = jnp.transpose(kv_parts, (2, 1, 0, 3, 4))
    grad_kv, grad_q, acts, queries_wide, branch_cols = launch(
        [
            swap_blocks("narrow", kv_parts),
            swap_blocks("narrow", grad_queries.reshape(narrow_count, own_rows, head_cols)),
            swap_blocks("wide", acts),
            gather_wide(grad_queries),
            split_columns("wide", grad_branch),
        ],
        10,
        "trade_grads",
    )
    grad_kv = grad_kv.reshape(KVH, repeat, 2, tok_rows, HD)
    if repeat > 1:
        grad_kv = jnp.sum(grad_kv.astype(FULL), axis=1, keepdims=True).astype(LOW)
    grad_kv = grad_kv[:, 0]
    kv_rows = jnp.transpose(grad_kv, (1, 2, 0, 3)).reshape(2, tok_rows, narrow_count, kv_size)

    def from_owners(parts, weight):
        return jnp.einsum("tnf,ndf->td", parts, weight, preferred_element_type=FULL)

    grad_normed = jnp.concatenate(
        [
            from_owners(kv_rows[0], k_w) + from_owners(kv_rows[1], v_w),
            jnp.einsum("ntf,ndf->td", grad_q, q_w, preferred_element_type=FULL),
        ]
    )
    grad_rows, gain_attn = norm_back(rows_full, gain_w[0], grad_normed)
    grad_pass = grad_mid + grad_start_exit + grad_final * (1.0 - keep_layer)
    grad_rows = jnp.concatenate([grad_rows[:tok_rows], grad_rows[tok_rows:] + grad_pass])
    grad_kv_flat = kv_rows.reshape(2 * tok_rows, narrow_count * kv_size)
    grad_rows, head_cols_all, kv_wide = launch(
        [
            return_rows(grad_rows.astype(LOW)),
            split_columns("wide", grad_head),
            gather_wide(grad_kv_flat),
        ],
        11,
        "return_rows",
    )
    acts = jnp.moveaxis(acts, 1, 0).reshape(3, total_rows, ffn_size)
    acts = lax.all_gather(acts, "narrow", axis=2, tiled=True)
    summed_table, table_squares = spread(
        spots, grad_rows.reshape(-1, columns), head_cols_all.reshape(vocab_rows, columns)
    )

    kv_wide = kv_wide.reshape(wide_count, 2, tok_rows, narrow_count * kv_size)
    grad_kv_w = jnp.einsum(
        "wtc,wjtf->jcf", tok_cols, kv_wide, preferred_element_type=FULL
    )
    summed_kv = lax.psum_scatter(grad_kv_w, "narrow", scatter_dimension=2, tiled=True)
    pick_cols = lax.all_gather(pick_cols, "narrow", axis=1, tiled=True)
    summed_qo = jnp.stack(
        [
            jnp.einsum("wtc,wtf->cf", pick_cols, queries_wide, preferred_element_type=FULL),
            jnp.einsum("wtc,wtf->cf", branch_cols, mixed_wide, preferred_element_type=FULL),
        ]
    )

    def cols_own(values_all):
        size = width // narrow_count
        return lax.dynamic_slice_in_dim(values_all, narrow_spot * size, size, 1)

    rights = (inner_all, inner_all, out_all)
    summed_ffn = jnp.stack([dot(acts[j], cols_own(rights[j]), 0, 0) for j in range(3)])
    small_all = lax.all_gather(
        pack_small(summed_qo, summed_kv).astype(LOW), "narrow", axis=0
    )

    squares = (
        jnp.sum(summed_qo * summed_qo)
        + jnp.sum(summed_kv * summed_kv)
        + jnp.sum(summed_ffn * summed_ffn)
        + jnp.sum(table_squares)
    )
    sums = jnp.stack(
        [gain_attn, gain_mid[0], gain_early + gain_late[0], jnp.full((width,), squares)]
    )
    sums = launch([combine(sums.reshape(4, 8, -1), add_two)], 12, "combine_sums")[0]
    sums = sums.reshape(4, width)
    summed_gain = lax.dynamic_slice_in_dim(
        sums[:3], (wide_spot * narrow_count + narrow_spot) * gain_size, gain_size, 1
    )
    square_total = sums[3, 0] + jnp.sum(sums[:3] * sums[:3])
    grad_norm = jnp.sqrt(square_total) / loss_count
    factor = jnp.minimum(1.0, CLIP_NORM / (grad_norm + 1e-06)) / loss_count

    def whole_columns(parts):
        return jnp.moveaxis(parts, 0, 2).reshape(
            parts.shape[1], parts.shape[2], parts.shape[0] * parts.shape[3]
        )

    def ffn_owner():
        left = lax.dynamic_index_in_dim(acts, jnp.minimum(narrow_spot, 2), 0, False)
        right = jnp.where(narrow_spot == 2, out_all, inner_all)
        grad = dot(left, right, 0, 0)
        mom = side_by_side(mom_owned).astype(FULL)
        result = newton((MOMENTUM * mom + grad * factor)[None])[0]
        return cut_columns(result, narrow_count)

    def small_owner():
        mom_q, mom_k = unpack_small(mom_owned.astype(FULL))
        grad_q, grad_k = unpack_small(small_all.astype(FULL))
        results = [
            newton(whole_columns(MOMENTUM * mom + grad * factor))
            for mom, grad in ((mom_q, grad_q), (mom_k, grad_k))
        ]
        parts = [
            jnp.moveaxis(
                result.reshape(2, result.shape[1], narrow_count, -1), 2, 0
            ).reshape(narrow_count, -1)
            for result in results
        ]
        flat = jnp.concatenate(parts, axis=1)
        flat = jnp.pad(flat, ((0, 0), (0, slot_rows * slot_cols - flat.shape[1])))
        return flat.reshape(narrow_count, slot_rows, slot_cols)

    directions = lax.cond(narrow_spot == 3, small_owner, ffn_owner)
    directions = swap_by_shifts(directions, "narrow")
    dir_ffn = directions[:3].astype(FULL)
    dir_qo, dir_kv = unpack_small(directions[3].astype(FULL))

    embed_new, embed_m_new, embed_v_new = adamw(
        embed, embed_m, embed_v, summed_table * factor, RATE_ADAM, WEIGHT_DECAY
    )
    gains_new, gains_m_new, gains_v_new = adamw(
        gains, gains_m, gains_v, summed_gain * factor, RATE_GAIN, 0.0
    )

    def mom_next(mom, grad):
        return MOMENTUM * mom + jnp.moveaxis(grad * factor, 0, 1)

    shrink = 1.0 - RATE_MUON * WEIGHT_DECAY

    def weight_next(weight, direction):
        return weight * shrink - RATE_MUON * jnp.moveaxis(direction, 0, 1)

    return (
        loss_sum,
        loss_count,
        grad_norm,
        embed_new,
        embed_m_new,
        embed_v_new,
        weight_next(attn_qo, dir_qo),
        mom_next(attn_qo_mom, summed_qo),
        weight_next(attn_kv, dir_kv),
        mom_next(attn_kv_mom, summed_kv),
        weight_next(ffn, dir_ffn),
        mom_next(ffn_mom, summed_ffn),
        gains_new,
        gains_m_new,
        gains_v_new,
    )


def solution(mesh):
    by_pack = P("wide", None)
    table = P("narrow", "wide")
    layer = P("wide", None, "narrow")
    gain = P(None, ("wide", "narrow"))
    return jax.shard_map(
        per_device,
        mesh=mesh,
        in_specs=(by_pack,) * 4 + (P("wide"),) + (table,) * 3 + (layer,) * 6 + (gain,) * 3,
        out_specs=(P(),) * 3 + (table,) * 3 + (layer,) * 6 + (gain,) * 3,
        check_vma=False,
    )
```

time: 2270 us -> 1370 us (0.60)
  waiting for transfers between devices: 1180 us -> 189 us
  Pallas kernels: 77.6 us -> 763 us
  blocking collectives: 354 us -> 20.6 us
  matrix products: 250 us -> 99.2 us
  other arithmetic: 152 us -> 96.5 us
  starting transfers between devices: 55.2 us -> 8.64 us
    pallas_call x0 -> x16, Pallas kernels: none -> 677 us  [the longest x13 584 us: launch(): pl.pallas_call(body, out_shape=outputs, in_specs=[place for task in tasks...]
    all_gather x16 -> x3, waiting for transfers between devices: 404 us -> 54.8 us  [the longest x1 54.8 us: per_device(): lax.all_gather(proj_own, 'narrow', axis=0)]
    all_to_all x8 -> x0, waiting for transfers between devices: 284 us -> none  [exchange(): return lax.all_to_all(parts, axis, 0, 0, tiled=True)]
    reduce_scatter x9 -> x1, waiting for transfers between devices: 271 us -> 9.33 us  [per_device(): lax.psum_scatter(grad_kv_w, 'narrow', scatter_dimension=2, tiled=True)]
    all_gather x8 -> x1, blocking collectives: 250 us -> 20.6 us  [per_device(): pick_cols = lax.all_gather(pick_cols, 'narrow', axis=1, tiled=True)]
    unnamed x29 -> x6, waiting for transfers between devices: 140 us -> 0.1 us
    dot_general x32 -> x11, matrix products: 166 us -> 65 us  [dot(): lax.dot_general(first, second, (((first_dim,), (second_dim,)), ((), ())),...]
    psum x2 -> x0, blocking collectives: 76.7 us -> none  [the longest x1 38.6 us: per_device(): gain_sum = lax.psum(gain_grads, BOTH)]
  transfers between devices with their start and end apart: 36 -> 12, of which waited for: 27 -> 9; matrix products, arithmetic and copies ran while one was open for 12% -> 13% of each run, Pallas kernels for 3% -> 22%
where the time goes in v3:
time: 1370 us; the launch traced here: 1350 us
  Pallas kernels  763 us (56%)
  waiting for transfers between devices  189 us (14%)
  local copies, waits for them, and re-layouts  138 us (10%)
  matrix products  99.2 us (7%)
  other arithmetic  96.5 us (7%)
  between operations  23.3 us (2%)
  blocking collectives  20.6 us (2%)
  loops' own time  13.8 us (1%)
    pallas_call x13, Pallas kernels, launch(): pl.pallas_call(body, out_shape=outputs, in_specs=[place for task in tasks...  584 us
    ppermute x6, waiting for transfers between devices, swap_by_shifts(): part = lax.ppermute(part, axis, pairs)  70.4 us
    pallas_call x1, Pallas kernels, newton(): pl.pallas_call(functools.partial(newton_body, chunk), grid=(count,), in_s...  65.5 us
    dot_general x11, matrix products, dot(): lax.dot_general(first, second, (((first_dim,), (second_dim,)), ((), ())),...  65 us
    all_gather x1, waiting for transfers between devices, per_device(): lax.all_gather(proj_own, 'narrow', axis=0)  54.8 us
    dynamic_update_slice x5, local copies, waits for them, and re-layouts, swap_by_shifts(): lax.dynamic_update_index_in_dim(result, part, lax.rem(me - step + count,...  46.8 us
    pallas_call x1, Pallas kernels, spread(): pl.pallas_call(spread_body, grid_spec=pltpu.PrefetchScalarGridSpec(num_sc...  46.1 us
    pallas_call x1, Pallas kernels, lookup(): pl.pallas_call(lookup_body, grid_spec=pltpu.PrefetchScalarGridSpec(num_sc...  39.7 us
  transfers between devices with their start and end apart: 12, of which 9 were waited for; matrix products, arithmetic and copies ran while one was open for 13% of the time, Pallas kernels for 22%

profile of v3, /device:TPU:17, one launch (start us, length us, event | category | flops | bytes accessed | tf_op | source)
XLA Modules:
  0.0 1352.6 jit_solution(15041541788758828800)
XLA Ops:
  11.3 54.8 %all-gather.6.cloned.1.call-done = bf16[4,256,1280]{2,1,0:T(8,128)(2,1)} async-done(((bf16[1,256,1280]{2,1,0:T(8,128)(2,1)}), bf16[4,256,1280]{2,1,0:T(8,128)(2,1)}) %all-gather.6.cloned.1.call-update) | async-done | bytes 2621456 | tf_op jit(solution)/shard_map/all_gather | solution.py:1263
  66.1 4.4 copy.232
  70.5 2.5 convert_element_type.242
  77.0 3.0 copy.247
  80.0 6.5 collective-permute-done
  87.3 21.8 %collective-permute-done.1 = bf16[3,176,512]{2,1,0:T(8,128)(2,1)S(1)} collective-permute-done((bf16[3,176,512]{2,1,0:T(8,128)(2,1)S(1)}, bf16[3,176,512]{2,1,0:T(8,128)(2,1)S(1)}, u32[]{:S(2)}, u32[]{:S(2)}) %collective-permute-start.1) | collective-permute-done | bytes 540704 | tf_op jit(solution)/shard_map/ppermute | solution.py:1202
  110.9 9.8 collective-permute-done.2
  122.5 9.4 dynamic_update_slice.20
  131.9 17.6 %dynamic_update_slice.21 = bf16[4,3,176,512]{3,0,2,1:T(4,128)(2,1)S(1)} dynamic-update-slice(bf16[4,3,176,512]{3,0,2,1:T(4,128)(2,1)S(1)} %dynamic_update_slice.20, bf16[1,3,176,512]{3,0,2,1:T(2,128)(2,1)} %copy.250, s32[]{:T(128)S(6)} %select_n.95, s32[]{:T(128)} %constant.100.clone.1, s32[]{:T(128)} %constant.100.clone.1, s32[]{:T(128)} %constant.100.clone.1) | dynamic-update-slice | bytes 1081348 | tf_op jit(solution)/shard_map/jit(dynamic_update_index_in_dim)/dynamic_update_slice | solution.py:1203
  149.5 17.6 %dynamic_update_slice.22 = bf16[4,3,176,512]{3,0,2,1:T(4,128)(2,1)S(1)} dynamic-update-slice(bf16[4,3,176,512]{3,0,2,1:T(4,128)(2,1)S(1)} %dynamic_update_slice.21, bf16[1,3,176,512]{3,0,2,1:T(2,128)(2,1)} %copy.252, s32[]{:T(128)S(6)} %select_n.93, s32[]{:T(128)} %constant.100.clone.1, s32[]{:T(128)} %constant.100.clone.1, s32[]{:T(128)} %constant.100.clone.1) | dynamic-update-slice | bytes 1081348 | tf_op jit(solution)/shard_map/jit(dynamic_update_index_in_dim)/dynamic_update_slice | solution.py:1203
  167.0 2.8 all_gather_reshape.3
  171.4 14.9 %gather_ids.1 = (s32[8,16,128]{2,1,0:T(8,128)}, f32[4,8,8,128]{3,2,1,0:T(8,128)}) custom-call(s32[16,128]{1,0:T(8,128)} %pad_bitcast_fusion.refs_0_, f32[8,128]{1,0:T(8,128)} %bitcast_convert_fusion.refs_1_), custom_call_target="tpu_custom_call" | custom-call | bytes 1671168 | tf_op jit(solution)/shard_map/gather_ids/pallas_call | solution.py:157
  188.0 6.0 convert_element_type.221
  194.6 39.7 %lookup.1 = bf16[9216,256]{1,0:T(8,128)(2,1)} custom-call(s32[9216]{0:T(1024)} %and_select_fusion.ids_ref, f32[8192,256]{1,0:T(8,128)} %table_ref.1), custom_call_target="tpu_custom_call" | custom-call | bytes 83886080 | tf_op jit(solution)/shard_map/lookup/pallas_call | solution.py:1077
  234.7 116.1 %fetch_rows.1 = (bf16[288,2048]{1,0:T(8,128)(2,1)}, bf16[1024,2048]{1,0:T(8,128)(2,1)}) custom-call(bf16[4,2304,256]{2,1,0:T(8,128)(2,1)} %bitcast.373, bf16[8,1024,256]{2,1,0:T(8,128)(2,1)} %bitcast.374), custom_call_target="tpu_custom_call" | custom-call | bytes 114294784 | tf_op jit(solution)/shard_map/fetch_rows/pallas_call | solution.py:157
  362.4 2.5 convert_bitcast_fusion.2
  374.5 6.0 fusion.58
  385.3 30.6 %trade_heads.1 = (bf16[4,1,2,256,128]{4,3,2,1,0:T(8,128)(2,1)}, bf16[4,32,512]{2,1,0:T(8,128)(2,1)}, bf16[4,32,2048]{2,1,0:T(8,128)(2,1)}, bf16[8,256,256]{2,1,0:T(8,128)(2,1)}, bf16[8,32,256]{2,1,0:T(8,128)(2,1)}) custom-call(bf16[4,1,2,256,128]{4,3,2,1,0:T(8,128)(2,1)} %maximum_bitcast_fusion.refs_0_, bf16[4,32,512]{2,1,0:T(8,128)(2,1)} %convert_element_type.229.refs_1_, ...), custom_call_target="tpu_custom_call" | custom-call | bytes 34603008 | tf_op jit(solution)/shard_map/trade_heads/pallas_call | solution.py:157
  421.4 36.8 %gather_mixed.1 = (bf16[4,128,512]{2,1,0:T(8,128)(2,1)}, bf16[8,128,2048]{2,1,0:T(8,128)(2,1)}, bf16[8,128,512]{2,1,0:T(8,128)(2,1)}) custom-call(bf16[128,512]{1,0:T(8,128)(2,1)} %copy.298.refs_0_.refs_2_, bf16[128,2048]{1,0:T(8,128)(2,1)} %get-tuple-element.260.refs_1_, bf16[128,512]{1,0:T(8,128)(2,1)} %copy.298.refs_0_.refs_2_), custom_call_target="tpu_custom_call" | custom-call | bytes 52428800 | tf_op jit(solution)/shard_map/gather_mixed/pallas_call | solution.py:157
  459.0 5.5 multiply_reduce_fusion.2
  466.2 6.1 fusion.143
  472.3 13.1 feed.1
  486.1 31.9 %settle.1 = (f32[32,2048]{1,0:T(8,128)}, bf16[4,32,2048]{2,1,0:T(8,128)(2,1)}, bf16[8,128,2048]{2,1,0:T(8,128)(2,1)}) custom-call(bf16[4,32,2048]{2,1,0:T(8,128)(2,1)} %bitcast.416, f32[32,2048]{1,0:T(8,128)} %constant_dynamic-slice_fusion.2.refs_1_, f32[32,2048]{1,0:T(8,128)} %get-tuple-element.255.refs_2_, f32[1,2048]{1,0:T(1,128)} %broadcast_in_dim.186.refs_3_, ...), custom_call_target="tpu_custom_call" | custom-call | bytes 52559872 | tf_op jit(solution)/shard_map/settle/pallas_call | solution.py:157
  518.0 33.3 %gather_late.1 = (bf16[8,128,2048]{2,1,0:T(8,128)(2,1)}, bf16[4,352,512]{2,1,0:T(8,128)(2,1)}) custom-call(bf16[128,2048]{1,0:T(8,128)(2,1)} %bitcast.420, bf16[4,352,512]{2,1,0:T(8,128)(2,1)} %get-tuple-element.268.refs_1_), custom_call_target="tpu_custom_call" | custom-call | bytes 60817408 | tf_op jit(solution)/shard_map/gather_late/pallas_call | solution.py:157
  551.3 7.8 fusion.144
  561.8 12.5 combine_stats.1
  575.1 8.6 convolution_convert_fusion.1
  583.6 37.6 %sum_late.1 = (f32[128,2048]{1,0:T(8,128)}, bf16[4,352,512]{2,1,0:T(8,128)(2,1)}) custom-call(bf16[8,128,2048]{2,1,0:T(8,128)(2,1)} %bitcast.387, bf16[4,352,512]{2,1,0:T(8,128)(2,1)} %get-tuple-element.267.refs_1_), custom_call_target="tpu_custom_call" | custom-call | bytes 65011712 | tf_op jit(solution)/shard_map/sum_late/pallas_call | solution.py:157
  623.3 8.7 convolution_convert_fusion
  632.8 42.0 %settle_late.1 = (f32[32,2048]{1,0:T(8,128)}, f32[1,2048]{1,0:T(1,128)}, bf16[4,32,2048]{2,1,0:T(8,128)(2,1)}, f32[128,2048]{1,0:T(8,128)}) custom-call(bf16[4,32,2048]{2,1,0:T(8,128)(2,1)} %bitcast.391, f32[32,2048]{1,0:T(8,128)} %get-tuple-element.102.refs_1_, f32[32,2048]{1,0:T(8,128)} %broadcast_in_dim.187.refs_2_, f32[1,2048]{1,0:T(1,128)} %broadcast_in_dim.186.refs_3_, ...), custom_call_target="tpu_custom_call" | custom-call | bytes 56819712 | tf_op jit(solution)/shard_map/settle_late/pallas_call | solution.py:157
  678.6 14.4 %feed_back.1 = (bf16[8,3,128,176]{3,2,1,0:T(8,128)(2,1)}, bf16[128,2048]{1,0:T(8,128)(2,1)}) custom-call(bf16[128,2048]{1,0:T(8,128)(2,1)} %bitcast.398, bf16[8,3,176,2048]{3,2,1,0:T(8,128)(2,1)} %all-gather.10.cloned.1.call-done.weight_ref, f32[8,128,176]{2,1,0:T(8,128)} %get-tuple-element.104.gate_ref, f32[8,128,176]{2,1,0:T(8,128)} %get-tuple-element.105.up_ref, ...), custom_call_target="tpu_custom_call" | custom-call | flops 2214592512 | bytes 17301504 | tf_op jit(solution)/shard_map/feed_back/pallas_call | solution.py:927
  693.0 37.2 %settle_middle.1 = (f32[32,2048]{1,0:T(8,128)}, f32[1,2048]{1,0:T(1,128)}, bf16[4,32,2048]{2,1,0:T(8,128)(2,1)}, f32[32,2048]{1,0:T(8,128)}, bf16[8,128,2048]{2,1,0:T(8,128)(2,1)}) custom-call(bf16[4,32,2048]{2,1,0:T(8,128)(2,1)} %bitcast.419, f32[32,2048]{1,0:T(8,128)} %constant_dynamic-slice_fusion.2.refs_1_, f32[32,2048]{1,0:T(8,128)} %broadcast_multiply_fusion.refs_2_, ...), custom_call_target="tpu_custom_call" | custom-call | bytes 58916864 | tf_op jit(solution)/shard_map/settle_middle/pallas_call | solution.py:157
  730.2 8.5 slice.270
  738.7 2.4 fusion.65
  745.7 6.9 fusion.124
  757.0 38.2 %trade_grads.1 = (bf16[4,1,2,256,128]{4,3,2,1,0:T(8,128)(2,1)}, bf16[4,32,512]{2,1,0:T(8,128)(2,1)}, bf16[8,3,128,176]{3,2,1,0:T(8,128)(2,1)}, bf16[8,128,512]{2,1,0:T(8,128)(2,1)}, bf16[8,128,256]{2,1,0:T(8,128)(2,1)}) custom-call(bf16[4,1,2,256,128]{4,3,2,1,0:T(8,128)(2,1)} %maximum_bitcast_fusion.1.refs_0_, ...), custom_call_target="tpu_custom_call" | custom-call | bytes 45613056 | tf_op jit(solution)/shard_map/trade_grads/pallas_call | solution.py:157
  799.2 5.1 fusion.30
  804.3 2.5 fusion.24
  811.1 6.3 add_convert_fusion.refs_1_
  819.6 137.9 %return_rows.1 = (bf16[4,2304,256]{2,1,0:T(8,128)(2,1)}, bf16[8,1024,256]{2,1,0:T(8,128)(2,1)}, bf16[8,512,512]{2,1,0:T(8,128)(2,1)}) custom-call(bf16[288,2048]{1,0:T(8,128)(2,1)} %pad_maximum_fusion.3.refs_0_, bf16[1024,2048]{1,0:T(8,128)(2,1)} %add_convert_fusion.refs_1_, bf16[512,512]{1,0:T(8,128)(2,1)} %bitcast.392), custom_call_target="tpu_custom_call" | custom-call | bytes 152043520 | tf_op jit(solution)/shard_map/return_rows/pallas_call | solution.py:157
  957.5 4.6 convolution_bitcast_fusion.6
  965.0 20.6 %all_gather.23 = bf16[8,128,256]{2,1,0:T(8,128)(2,1)S(1)} all-gather(bf16[8,32,256]{2,1,0:T(8,128)(2,1)S(1)} %copy-done.33), channel_id=1, replica_groups=mesh['wide'=8,'narrow'=4] {'narrow'}, dimensions={1}, use_global_device_ids=true | all-gather | bytes 655360 | tf_op jit(solution)/shard_map/all_gather | solution.py:1556
  988.2 9.3 reduce-scatter.2.cloned.1.call-done
  1001.7 46.1 %spread.1 = (f32[8192,256]{1,0:T(8,128)}, f32[8,256]{1,0:T(8,128)}) custom-call(s32[9216]{0:T(1024)} %and_select_fusion.ids_ref, bf16[9216,256]{1,0:T(8,128)(2,1)} %bitcast.383, bf16[8192,256]{1,0:T(8,128)(2,1)} %bitcast.386), custom_call_target="tpu_custom_call" | custom-call | flops 2359296 | bytes 150994944 | tf_op jit(solution)/shard_map/spread/pallas_call | solution.py:1142
  1054.8 26.4 %all-gather.12.cloned.1.call-done = bf16[3,1024,704]{1,2,0:T(8,128)(2,1)} async-done(((bf16[3,1024,176]{1,2,0:T(8,128)(2,1)}), bf16[3,1024,704]{1,2,0:T(8,128)(2,1)}) %all-gather.12.cloned.1.call-update) | async-done | bytes 4325392 | tf_op jit(solution)/shard_map/all_gather | solution.py:1546
  1081.1 2.7 convolution_bitcast_fusion.4
  1084.1 2.7 convolution_bitcast_fusion.5
  1086.8 2.7 convolution_bitcast_fusion.3
  1094.4 15.5 %combine_sums.1 = f32[4,8,256]{2,1,0:T(8,128)} custom-call(f32[4,8,256]{2,1,0:T(8,128)} %maximum_maximum_fusion.1.refs_0_), custom_call_target="tpu_custom_call" | custom-call | bytes 524288 | tf_op jit(solution)/shard_map/combine_sums/pallas_call | solution.py:157
  1115.3 27.9 %all-gather.14.cloned.1.call-done = bf16[4,704,512]{2,1,0:T(8,128)(2,1)} async-done(((bf16[1,704,512]{2,1,0:T(8,128)(2,1)}), bf16[4,704,512]{2,1,0:T(8,128)(2,1)}) %all-gather.14.cloned.1.call-update) | async-done | bytes 2883600 | tf_op jit(solution)/shard_map/all_gather | solution.py:1570
  1143.2 115.4 %conditional.1 = (bf16[4,704,512]{2,1,0:T(8,128)(2,1)S(1)}) conditional(s32[]{:T(128)} %convert_element_type.265, (bf16[4,704,512]{2,1,0:T(8,128)(2,1)S(1)}, s32[]{:T(128)}, bf16[3,1024,704]{1,2,0:T(8,128)(2,1)}, bf16[1024,2048]{1,0:T(8,128)(2,1)}, bf16[1024,2048]{1,0:T(8,128)(2,1)}, /*index=5*/f32[]{:T(128)}) %tuple.83, ...), branch_computations={%region_35.36_spmd, %region_36.37_spmd} | conditional | flops 26750222336 | bytes 137101376 | solution.py:1622
  1144.5 3.7 copy.321
  1148.2 5.3 copy.307
  1153.5 6.6 copy.276
  1160.2 10.1 add_bitcast_fusion.x_ref
  1170.3 65.5 %newton.3 = bf16[1,704,2048]{2,1,0:T(8,128)(2,1)} custom-call(f32[1,704,2048]{2,1,0:T(8,128)} %add_bitcast_fusion.x_ref), custom_call_target="tpu_custom_call" | custom-call | flops 23789568000 | bytes 8650752 | tf_op jit(solution)/shard_map/cond/branch_0_fun/newton/pallas_call | solution.py:1030
  1235.7 7.1 squeeze.51
  1259.5 22.1 %multiply_subtract_fusion = (f32[8192,256]{1,0:T(8,128)}, f32[8192,256]{1,0:T(8,128)}, f32[8192,256]{1,0:T(8,128)}) fusion(f32[8192,256]{1,0:T(8,128)} %table_ref.1, f32[8192,256]{1,0:T(8,128)} %get-tuple-element.130, f32[]{:T(128)} %div.106, f32[8192,256]{1,0:T(8,128)} %param.25, f32[8192,256]{1,0:T(8,128)} %param.26), kind=kLoop, calls=%fused_computation.24 | loop fusion | flops 31457280 | bytes 58720260 | tf_op jit(solution)/shard_map/sub | solution.py:1182
  1283.4 2.4 dynamic-slice_bitcast_fusion
  1288.0 2.4 collective-permute-start.5
  1293.7 6.9 bitcast_add_fusion
  1300.6 18.1 %collective-permute-done.4 = bf16[704,512]{1,0:T(8,128)(2,1)} collective-permute-done((bf16[704,512]{1,0:T(8,128)(2,1)}, bf16[704,512]{1,0:T(8,128)(2,1)}, u32[]{:S(2)}, u32[]{:S(2)}) %collective-permute-start.4) | collective-permute-done | bytes 720928 | tf_op jit(solution)/shard_map/ppermute | solution.py:1202
  1319.8 14.3 %collective-permute-done.5 = bf16[704,512]{1,0:T(8,128)(2,1)} collective-permute-done((bf16[704,512]{1,0:T(8,128)(2,1)}, bf16[704,512]{1,0:T(8,128)(2,1)}, u32[]{:S(2)}, u32[]{:S(2)}) %collective-permute-start.5) | collective-permute-done | bytes 720928 | tf_op jit(solution)/shard_map/ppermute | solution.py:1202
  1335.6 5.2 bitcast_subtract_fusion
  (335 shorter events, 118.4 us)
Async XLA Ops:
  7.2 58.9 %all-gather.6.cloned.1.call-start = ((), (), s32[]{:S(2)}) async-start(), calls=%async_computation.1 | async-start | bytes 3276800 | tf_op jit(solution)/shard_map/all_gather | solution.py:1263
  11.2 360.4 %all-gather.8.cloned.1.call-start = ((), (), s32[]{:S(2)}) async-start(), calls=%async_computation.2 | async-start | bytes 23592960 | tf_op jit(solution)/shard_map/all_gather | solution.py:1262
  70.4 401.9 %all-gather.10.cloned.1.call-start = ((), (), s32[]{:S(2)}) async-start(), calls=%async_computation.3 | async-start | bytes 19464192 | tf_op jit(solution)/shard_map/all_gather | solution.py:1266
  73.2 13.3 collective-permute-start
  73.4 35.7 %collective-permute-start.1 = (bf16[3,176,512]{2,1,0:T(8,128)(2,1)S(1)}, bf16[3,176,512]{2,1,0:T(8,128)(2,1)S(1)}, u32[]{:S(2)}, u32[]{:S(2)}) collective-permute-start(bf16[3,176,512]{2,1,0:T(8,128)(2,1)S(1)} %get-tuple-element.270), channel_id=1, source_target_pairs={{0,2},{1,3},{2,0},{3,1},{4,6},{5,7},{6,4},{7,5},{8,10},{9,11},{10,... | collective-permute-start | bytes 1622024 | tf_op jit(solution)/shard_map/ppermute | solution.py:1202
  74.7 46.0 %collective-permute-start.2 = (bf16[3,176,512]{2,1,0:T(8,128)(2,1)S(1)}, bf16[3,176,512]{2,1,0:T(8,128)(2,1)S(1)}, u32[]{:S(2)}, u32[]{:S(2)}) collective-permute-start(bf16[3,176,512]{2,1,0:T(8,128)(2,1)S(1)} %get-tuple-element.269), channel_id=1, source_target_pairs={{0,3},{1,0},{2,1},{3,2},{4,7},{5,4},{6,5},{7,6},{8,11},{9,8},{10,9... | collective-permute-start | bytes 1622024 | tf_op jit(solution)/shard_map/ppermute | solution.py:1202
  80.0 42.5 %copy-start.3 = (bf16[4,3,176,512]{3,0,2,1:T(4,128)(2,1)S(1)}, bf16[4,3,176,512]{3,0,2,1:T(4,128)(2,1)}, u32[]{:S(2)}) copy-start(bf16[4,3,176,512]{3,0,2,1:T(4,128)(2,1)} %copy.247) | copy-start | bytes 6488068
  149.4 20.5 %copy-start.48 = (f32[3,64]{1,0:T(4,128)S(1)}, f32[3,64]{1,0:T(4,128)}, u32[]{:S(2)}) copy-start(f32[3,64]{1,0:T(4,128)} %param.33) | copy-start | bytes 2308
  149.4 21.1 %copy-start.44 = (s32[1,1024]{1,0:T(1,128)S(1)}, s32[1,1024]{1,0:T(1,128)}, u32[]{:S(2)}) copy-start(s32[1,1024]{1,0:T(1,128)} %param.19) | copy-start | bytes 12292
  149.5 21.1 %copy-start.53 = (s32[1,128]{1,0:T(1,128)S(1)}, s32[1,128]{1,0:T(1,128)}, u32[]{:S(2)}) copy-start(s32[1,128]{1,0:T(1,128)} %param.20) | copy-start | bytes 1540
  149.5 21.3 %copy-start.58 = (s32[1,128]{1,0:T(1,128)S(1)}, s32[1,128]{1,0:T(1,128)}, u32[]{:S(2)}) copy-start(s32[1,128]{1,0:T(1,128)} %param.21) | copy-start | bytes 1540
  169.8 827.7 %reduce-scatter.2.cloned.1.call-start = ((), (), s32[]{:S(2)}) async-start(), calls=%async_computation.4 | async-start | bytes 1310720 | tf_op jit(solution)/shard_map/reduce_scatter | solution.py:1555
  194.6 39.7 %copy-start.34 = (f32[4,8,8,128]{3,2,1,0:T(8,128)S(1)}, f32[4,8,8,128]{3,2,1,0:T(8,128)}, u32[]{:S(2)}) copy-start(f32[4,8,8,128]{3,2,1,0:T(8,128)} %get-tuple-element.91) | copy-start | bytes 393220
  350.8 8.8 copy-start.65
  350.8 9.6 copy-start.23
  350.8 9.6 copy-start.15
  354.1 7.0 copy-start.40
  354.1 7.0 copy-start.37
  361.6 9.5 copy-start.51
  374.4 6.2 copy-start.35
  374.5 6.2 copy-start.36
  382.0 36.1 %copy-start.29 = (pred[128,1024]{0,1:T(8,128)(4,1)S(1)}, pred[128,1024]{0,1:T(8,128)(4,1)}, u32[]{:S(2)}) copy-start(pred[128,1024]{0,1:T(8,128)(4,1)} %fusion.81) | copy-start | bytes 393220
  459.0 6.3 copy-start.39
  459.0 7.2 copy-start.59
  459.0 7.2 copy-start.61
  551.3 7.8 copy-start.12
  551.3 7.8 copy-start.43
  559.1 16.0 %copy-start.10 = (f32[1024,1024]{0,1:T(8,128)}, f32[1024,1024]{0,1:T(8,128)S(1)}, u32[]{:S(2)}) copy-start(f32[1024,1024]{0,1:T(8,128)S(1)} %get-tuple-element.310) | copy-start | bytes 12582916
  559.1 15.9 %copy-start.54 = (f32[1024]{0:T(1024)S(1)}, f32[1024]{0:T(1024)}, u32[]{:S(2)}) copy-start(f32[1024]{0:T(1024)} %convert_bitcast_fusion.4) | copy-start | bytes 12292
  583.6 39.7 %copy-start.13 = (f32[1024,1024]{0,1:T(8,128)S(1)}, f32[1024,1024]{0,1:T(8,128)}, u32[]{:S(2)}) copy-start(f32[1024,1024]{0,1:T(8,128)} %get-tuple-element.306) | copy-start | bytes 12582916
  583.6 39.7 %copy-start.55 = (f32[1024]{0:T(1024)S(1)}, f32[1024]{0:T(1024)}, u32[]{:S(2)}) copy-start(f32[1024]{0:T(1024)} %get-tuple-element.256) | copy-start | bytes 12292
  730.2 8.5 copy-start.19
  742.2 3.5 copy-start.62
  745.7 7.0 copy-start.42
  745.7 7.0 copy-start.52
  745.7 8.7 copy-start.31
  745.7 8.7 copy-start.32
  795.2 3.9 copy-start.64
  799.1 5.1 copy-start.18
  799.2 9.4 slice-start.1
  804.3 4.3 slice-start.2
  811.1 7.2 copy-start.25
  811.1 7.2 copy-start.30
  818.4 139.1 %copy-start.63 = (bf16[8,256,256]{2,1,0:T(8,128)(2,1)S(1)}, bf16[8,256,256]{2,1,0:T(8,128)(2,1)}, u32[]{:S(2)}) copy-start(bf16[8,256,256]{2,1,0:T(8,128)(2,1)} %get-tuple-element.123) | copy-start | bytes 3145732
  957.5 4.7 copy-start.20
  962.1 119.0 %all-gather.12.cloned.1.call-start = ((), (), s32[]{:S(2)}) async-start(), calls=%async_computation.5 | async-start | bytes 5406720 | tf_op jit(solution)/shard_map/all_gather | solution.py:1546
  963.6 23.8 %copy-start.22 = (bf16[8,128,512]{2,1,0:T(8,128)(2,1)S(1)}, bf16[8,128,512]{2,1,0:T(8,128)(2,1)}, u32[]{:S(2)}) copy-start(bf16[8,128,512]{2,1,0:T(8,128)(2,1)} %get-tuple-element.118) | copy-start | bytes 3145732
  964.9 178.3 %all-gather.14.cloned.1.call-start = ((), (), s32[]{:S(2)}) async-start(), calls=%async_computation.6 | async-start | bytes 3604480 | tf_op jit(solution)/shard_map/all_gather | solution.py:1570
  987.4 13.3 copy-start.24
  987.9 61.2 %copy-start.4 = (f32[1,256,512]{2,1,0:T(8,128)}, f32[1,256,512]{2,1,0:T(8,128)S(1)}, u32[]{:S(2)}) copy-start(f32[1,256,512]{2,1,0:T(8,128)S(1)} %convolution_bitcast_fusion.8) | copy-start | bytes 1572868
  987.9 13.7 %copy-start.47 = (f32[1,2048]{1,0:T(1,128)S(1)}, f32[1,2048]{1,0:T(1,128)}, u32[]{:S(2)}) copy-start(f32[1,2048]{1,0:T(1,128)} %get-tuple-element.116) | copy-start | bytes 24580
  987.9 13.7 %copy-start.50 = (f32[1,2048]{1,0:T(1,128)S(1)}, f32[1,2048]{1,0:T(1,128)}, u32[]{:S(2)}) copy-start(f32[1,2048]{1,0:T(1,128)} %get-tuple-element.114) | copy-start | bytes 24580
  1001.7 48.3 %copy-start.46 = (pred[8,128]{1,0:T(8,128)(4,1)S(1)}, pred[8,128]{1,0:T(8,128)(4,1)}, u32[]{:S(2)}) copy-start(pred[8,128]{1,0:T(8,128)(4,1)} %copy-done.45) | copy-start | bytes 3076
  1084.1 5.3 copy-start.5
  1259.5 23.9 %collective-permute-start.3 = (bf16[704,512]{1,0:T(8,128)(2,1)}, bf16[704,512]{1,0:T(8,128)(2,1)}, u32[]{:S(2)}, u32[]{:S(2)}) collective-permute-start(bf16[704,512]{1,0:T(8,128)(2,1)} %dynamic-slice_bitcast_fusion.2), channel_id=1, source_target_pairs={{0,1},{1,2},{2,3},{3,0},{4,5},{5,6},{6,7},{7,4},{8,9},{9,10},{10,1... | collective-permute-start | bytes 2162696 | tf_op jit(solution)/shard_map/ppermute | solution.py:1202
  1281.6 6.3 copy-start.26
  1281.6 6.3 copy-start.27
  1281.6 8.8 copy-start.49
  1281.6 8.8 copy-start.56
  1281.6 8.8 copy-start.57
  1285.8 32.9 %collective-permute-start.4 = (bf16[704,512]{1,0:T(8,128)(2,1)}, bf16[704,512]{1,0:T(8,128)(2,1)}, u32[]{:S(2)}, u32[]{:S(2)}) collective-permute-start(bf16[704,512]{1,0:T(8,128)(2,1)} %get-tuple-element.265), channel_id=1, source_target_pairs={{0,2},{1,3},{2,0},{3,1},{4,6},{5,7},{6,4},{7,5},{8,10},{9,11},{10,... | collective-permute-start | bytes 2162696 | tf_op jit(solution)/shard_map/ppermute | solution.py:1202
  1288.0 46.1 %collective-permute-start.5 = (bf16[704,512]{1,0:T(8,128)(2,1)}, bf16[704,512]{1,0:T(8,128)(2,1)}, u32[]{:S(2)}, u32[]{:S(2)}) collective-permute-start(bf16[704,512]{1,0:T(8,128)(2,1)} %get-tuple-element.264), channel_id=1, source_target_pairs={{0,3},{1,0},{2,1},{3,2},{4,7},{5,4},{6,5},{7,6},{8,11},{9,8},{10,9... | collective-permute-start | bytes 2162696 | tf_op jit(solution)/shard_map/ppermute | solution.py:1202
  1335.6 5.2 copy-start.9
  1335.6 7.5 copy-start.21
  (15 other events, 34.4 us)
Sparse Core Ops, SparseCore 0:
  11.4 54.6 all-gather.5
  70.6 112.1 all-gather.7
  185.2 137.0 all-gather.9
  962.2 35.2 reduce-scatter.1
  999.6 81.4 all-gather.11
  1083.2 59.9 all-gather.13

commit v4 on v3

--- a/solution.py
+++ b/solution.py
@@ -34,7 +34,6 @@
 LOW = jnp.bfloat16
 FULL = jnp.float32
 BOTH = ("wide", "narrow")
-ROWS_IN_BLOCK = 1024
 UNROLL = 16
 VMEM_BYTES = 56 * 1024 * 1024
 
@@ -168,6 +167,18 @@
     )(*inputs)
 
 
+def later(task, turns):
+    begin = task.steps
+
+    def steps(ins, outs, scratch):
+        for turn in range(turns):
+            yield
+        yield from begin(ins, outs, scratch)
+
+    task.steps = steps
+    return task
+
+
 def gather_wide(values):
     count = lax.axis_size("wide")
     chips = count // 2
@@ -264,6 +275,58 @@
         return ref.at[:, pl.ds(pl.multiple_of(spot * size, size), size)]
 
     return at
+
+
+def turned(ref, spot):
+    count = lax.axis_size("narrow")
+    return ref.at[lax.rem(spot + count - lax.rem(lax.axis_index("wide"), 2), count)]
+
+
+def swap_turned(values):
+    return trade("narrow", values, turned, block_at, values.shape)
+
+
+def send_owner(values):
+    count = lax.axis_size("narrow")
+
+    def steps(ins, outs, scratch):
+        (x_ref,), (out_ref,), (send, receive, local) = ins, outs, scratch
+        me = lax.axis_index("narrow")
+        owner = lax.rem(3 + lax.rem(lax.axis_index("wide"), 2), count)
+        keep = pltpu.make_async_copy(x_ref, out_ref.at[me], local)
+        keep.start()
+
+        def to_owner():
+            return push(x_ref, out_ref.at[me], send.at[0], receive.at[me], {"narrow": owner})
+
+        @pl.when(me != owner)
+        def _():
+            to_owner().start()
+
+        yield
+        yield
+
+        @pl.when(me != owner)
+        def _():
+            to_owner().wait_send()
+
+        @pl.when(me == owner)
+        def _():
+            for step in range(1, count):
+                source = lax.rem(owner + step, count)
+                arrived(out_ref.at[source], send.at[0], receive.at[source], {"narrow": source})
+
+        keep.wait()
+
+    return Task(
+        [values],
+        [struct((count,) + values.shape, values.dtype)],
+        [sems(1), sems(count), sems()],
+        steps,
+        ANY,
+        ANY,
+        ["narrow"],
+    )
 
 
 def swap_blocks(axis, values):
@@ -942,133 +1005,179 @@
     )(grad, weight, gate, up, hidden)
 
 
-def newton_body(chunk, x_ref, out_ref, current, low, gram, rest_low):
+def newton_steps(current, low, gram, rest_low):
     rows, width = current.shape
-    parts = rows // chunk
-    eye_rows = lax.broadcasted_iota(jnp.int32, (chunk, rows), 0)
-    eye_columns = lax.broadcasted_iota(jnp.int32, (chunk, rows), 1)
+    block = min(512, width)
+    eye = lax.broadcasted_iota(jnp.int32, (rows, rows), 0) == lax.broadcasted_iota(
+        jnp.int32, (rows, rows), 1
+    )
 
     def strip(part):
-        return pl.ds(pl.multiple_of(part * chunk, chunk), chunk)
-
-    def eye(part):
-        return eye_rows + part * chunk == eye_columns
+        return pl.ds(pl.multiple_of(part * block, block), block)
 
     def over(function, start):
-        return lax.fori_loop(0, parts, function, start)
-
-    def square_sum(part, total):
-        values = x_ref[0, strip(part), :]
+        return lax.fori_loop(0, width // block, function, start)
+
+    def add_squares(part, total):
+        values = current[:, strip(part)]
         return total + jnp.sum(values * values)
 
-    scale = 1.0 / (jnp.sqrt(over(square_sum, jnp.float32(0.0))) + 1e-07)
+    scale = 1.0 / (jnp.sqrt(over(add_squares, jnp.float32(0.0))) + 1e-07)
 
     def begin(part, carry):
-        values = x_ref[0, strip(part), :] * scale
-        current[strip(part), :] = values
-        low[strip(part), :] = values.astype(LOW)
+        values = current[:, strip(part)] * scale
+        current[:, strip(part)] = values
+        low[:, strip(part)] = values.astype(LOW)
         return carry
 
     over(begin, 0)
 
     def iteration(turn, carry):
-        def gram_rows(part, trace):
-            rows_here = dot(low[strip(part), :], low[...], 1, 1)
-            gram[strip(part), :] = rows_here
-            return trace + jnp.sum(jnp.where(eye(part), rows_here, 0.0))
-
-        middle = over(gram_rows, jnp.float32(0.0)) / rows
-
-        def centre(part, carry):
-            rest = gram[strip(part), :] - jnp.where(eye(part), middle, 0.0)
-            rest_low[strip(part), :] = rest.astype(LOW)
+        gram[...] = jnp.zeros_like(gram)
+
+        def add_gram(part, carry):
+            values = low[:, strip(part)]
+            gram[...] = gram[...] + dot(values, values, 1, 1)
             return carry
 
-        over(centre, 0)
-
-        def poly_rows(part, trace):
-            square = dot(rest_low[strip(part), :], rest_low[...], 1, 0)
-            rows_here = gram[strip(part), :]
-            rest = rows_here - jnp.where(eye(part), middle, 0.0)
-            square = square + 2.0 * middle * rest + jnp.where(eye(part), middle * middle, 0.0)
-            rows_here = NEWTON_B * rows_here + NEWTON_C * square
-            gram[strip(part), :] = rows_here
-            return trace + jnp.sum(jnp.where(eye(part), rows_here, 0.0))
-
-        second = over(poly_rows, jnp.float32(0.0)) / rows
-
-        def centre_again(part, carry):
-            rest = gram[strip(part), :] - jnp.where(eye(part), second, 0.0)
-            rest_low[strip(part), :] = rest.astype(LOW)
+        over(add_gram, 0)
+        whole = gram[...]
+        middle = jnp.sum(jnp.where(eye, whole, 0.0)) / rows
+        rest_low[...] = (whole - jnp.where(eye, middle, 0.0)).astype(LOW)
+        square = dot(rest_low[...], rest_low[...], 1, 0)
+        whole = gram[...]
+        rest = whole - jnp.where(eye, middle, 0.0)
+        square = square + 2.0 * middle * rest + jnp.where(eye, middle * middle, 0.0)
+        whole = NEWTON_B * whole + NEWTON_C * square
+        second = jnp.sum(jnp.where(eye, whole, 0.0)) / rows
+        rest_low[...] = (whole - jnp.where(eye, second, 0.0)).astype(LOW)
+
+        def apply(part, carry):
+            values = (NEWTON_A + second) * current[:, strip(part)] + dot(
+                rest_low[...], low[:, strip(part)], 1, 0
+            )
+            current[:, strip(part)] = values
+            low[:, strip(part)] = values.astype(LOW)
             return carry
 
-        over(centre_again, 0)
-
-        def apply(part, carry):
-            current[strip(part), :] = (NEWTON_A + second) * current[strip(part), :] + dot(
-                rest_low[strip(part), :], low[...], 1, 0
-            )
-            return carry
-
         over(apply, 0)
-
-        def lower(part, carry):
-            low[strip(part), :] = current[strip(part), :].astype(LOW)
-            return carry
-
-        over(lower, 0)
         return carry
 
     lax.fori_loop(0, NS_STEPS, iteration, 0)
+
+
+def newton_scratch(rows, width):
+    return [
+        pltpu.VMEM((rows, width), FULL),
+        pltpu.VMEM((rows, width), LOW),
+        pltpu.VMEM((rows, rows), FULL),
+        pltpu.VMEM((rows, rows), LOW),
+    ]
+
+
+def newton_cost(count, rows, width):
+    return pl.CostEstimate(
+        flops=NS_STEPS * count * (4 * rows * rows * width + 2 * rows * rows * rows),
+        bytes_accessed=6 * count * rows * width,
+        transcendentals=0,
+    )
+
+
+def newton_small_body(x_ref, out_ref, current, low, gram, rest_low):
+    current[...] = x_ref[0]
+    newton_steps(current, low, gram, rest_low)
     out_ref[0] = low[...]
 
 
-def newton(blocks):
+def newton_small(blocks):
     count, rows, width = blocks.shape
-    chunk = next(size for size in (176, 128, 88, 64, rows) if rows % size == 0)
     spec = pl.BlockSpec((1, rows, width), lambda block: (block, 0, 0))
     return pl.pallas_call(
-        functools.partial(newton_body, chunk),
+        newton_small_body,
         grid=(count,),
         in_specs=[spec],
         out_specs=spec,
         out_shape=struct(blocks.shape, LOW),
-        scratch_shapes=[
-            pltpu.VMEM((rows, width), FULL),
-            pltpu.VMEM((rows, width), LOW),
-            pltpu.VMEM((rows, rows), FULL),
-            pltpu.VMEM((rows, rows), LOW),
-        ],
+        scratch_shapes=newton_scratch(rows, width),
         compiler_params=pltpu.CompilerParams(vmem_limit_bytes=VMEM_BYTES),
-        cost_estimate=pl.CostEstimate(
-            flops=NS_STEPS * count * (4 * rows * rows * width + 2 * rows * rows * rows),
-            bytes_accessed=6 * blocks.size,
-            transcendentals=0,
-        ),
+        cost_estimate=newton_cost(count, rows, width),
+        name="newton_small",
+    )(blocks)
+
+
+def newton_body(factor_ref, mom_ref, *refs):
+    parts = mom_ref.shape[0]
+    pieces, (out_ref, current, low, gram, rest_low) = refs[:parts], refs[parts:]
+    me = lax.axis_index("narrow")
+    columns = mom_ref.shape[2]
+    rows = pieces[0].shape[0]
+    for part in range(parts):
+        current[:, part * columns : (part + 1) * columns] = MOMENTUM * mom_ref[part].astype(FULL)
+    factor = factor_ref[0]
+    for step, piece in enumerate(pieces):
+        source = lax.rem(me - step + parts, parts)
+        added = factor * piece[...].astype(FULL)
+        if rows % 8 == 0:
+            spot = pl.ds(pl.multiple_of(source * rows, 8), rows)
+            current[spot, :] = current[spot, :] + added
+            continue
+        for at in range(parts):
+
+            @pl.when(source == at)
+            def _():
+                spot = slice(at * rows, (at + 1) * rows)
+                current[spot, :] = current[spot, :] + added
+
+    newton_steps(current, low, gram, rest_low)
+    for part in range(parts):
+        out_ref[part] = low[:, part * columns : (part + 1) * columns]
+
+
+def newton(factor, mom, pieces):
+    parts, rows, columns = mom.shape
+    width = parts * columns
+    return pl.pallas_call(
+        newton_body,
+        in_specs=[pl.BlockSpec(memory_space=pltpu.SMEM), VMEM] + [VMEM] * parts,
+        out_specs=VMEM,
+        out_shape=struct(mom.shape, LOW),
+        scratch_shapes=newton_scratch(rows, width),
+        compiler_params=pltpu.CompilerParams(vmem_limit_bytes=VMEM_BYTES),
+        cost_estimate=newton_cost(1, rows, width),
         name="newton",
-    )(blocks)
-
-
-def lookup_body(ids_ref, table_ref, out_ref, held, rows, sem):
-    block = pl.program_id(0)
+    )(factor.reshape(1), mom, *pieces)
+
+
+def lookup_body(ids_ref, table_ref, out_ref, low_ref, list_ref, held, rows, sem):
     vocab = table_ref.shape[0]
-
-    @pl.when(block == 0)
-    def _():
-        load = pltpu.make_async_copy(table_ref, held.at[pl.ds(0, vocab)], sem)
-        load.start()
-        held[pl.ds(vocab, 8), :] = jnp.zeros((8, held.shape[1]), FULL)
-        load.wait()
+    count = out_ref.shape[0]
+    load = pltpu.make_async_copy(table_ref, held, sem)
+    load.start()
+    rows[...] = jnp.zeros_like(rows)
+
+    def note(group, found):
+        for member in range(UNROLL):
+            at = group * UNROLL + member
+            list_ref[found] = at
+            found = found + (ids_ref[at] < vocab).astype(jnp.int32)
+        return found
+
+    found = lax.fori_loop(0, count // UNROLL, note, jnp.int32(0))
+    for member in range(UNROLL):
+        list_ref[found + member] = count
+    list_ref[count + UNROLL] = found
+    load.wait()
 
     def step(group, carry):
         for member in range(UNROLL):
-            at = group * UNROLL + member
-            spot = ids_ref[block * ROWS_IN_BLOCK + at]
+            at = list_ref[group * UNROLL + member]
+            spot = jnp.minimum(ids_ref[jnp.minimum(at, count - 1)], vocab - 1)
             rows[pl.ds(at, 1), :] = held[pl.ds(spot, 1), :]
         return carry
 
-    lax.fori_loop(0, ROWS_IN_BLOCK // UNROLL, step, 0)
-    out_ref[...] = rows[...].astype(LOW)
+    lax.fori_loop(0, (found + UNROLL - 1) // UNROLL, step, 0)
+    out_ref[...] = rows[pl.ds(0, count), :].astype(LOW)
+    low_ref[...] = held[...].astype(LOW)
 
 
 def lookup(table, ids):
@@ -1076,99 +1185,95 @@
     count = ids.shape[0]
     return pl.pallas_call(
         lookup_body,
-        grid_spec=pltpu.PrefetchScalarGridSpec(
-            num_scalar_prefetch=1,
-            grid=(count // ROWS_IN_BLOCK,),
-            in_specs=[pl.BlockSpec(memory_space=pl.ANY)],
-            out_specs=pl.BlockSpec((ROWS_IN_BLOCK, columns), lambda block, ids_ref: (block, 0)),
-            scratch_shapes=[
-                pltpu.VMEM((vocab + 8, columns), FULL),
-                pltpu.VMEM((ROWS_IN_BLOCK, columns), FULL),
-                pltpu.SemaphoreType.DMA,
-            ],
-        ),
-        out_shape=jax.ShapeDtypeStruct((count, columns), LOW),
+        in_specs=[pl.BlockSpec(memory_space=pltpu.SMEM), ANY],
+        out_specs=[VMEM, VMEM, pl.BlockSpec(memory_space=pltpu.SMEM)],
+        scratch_shapes=[
+            pltpu.VMEM((vocab, columns), FULL),
+            pltpu.VMEM((count + 8, columns), FULL),
+            pltpu.SemaphoreType.DMA,
+        ],
+        out_shape=[
+            struct((count, columns), LOW),
+            struct((vocab, columns), LOW),
+            struct((count + 2 * UNROLL,), jnp.int32),
+        ],
         compiler_params=pltpu.CompilerParams(vmem_limit_bytes=VMEM_BYTES),
         cost_estimate=pl.CostEstimate(
-            flops=0, bytes_accessed=vocab * columns * 4 + count * columns * 32, transcendentals=0
+            flops=0, bytes_accessed=vocab * columns * 4 + count * columns * 24, transcendentals=0
         ),
         name="lookup",
     )(ids, table)
 
 
-def spread_body(ids_ref, rows_ref, head_ref, out_ref, square_ref, even, odd, rows, sem):
-    block = pl.program_id(0)
+def spread_body(
+    ids_ref, list_ref, rows_ref, head_ref, out_ref, square_ref, even, odd, rows, sem
+):
     vocab = out_ref.shape[0]
-
-    @pl.when(block == 0)
-    def _():
-        even[...] = jnp.zeros_like(even)
-        odd[...] = jnp.zeros_like(odd)
-
-    rows[...] = rows_ref[...].astype(FULL)
+    count = rows_ref.shape[0]
+    chunk = 256
+
+    def strip(part):
+        return pl.ds(pl.multiple_of(part * chunk, chunk), chunk)
+
+    def begin(part, carry):
+        even[strip(part), :] = head_ref[strip(part), :].astype(FULL)
+        odd[strip(part), :] = jnp.zeros((chunk, odd.shape[1]), FULL)
+        return carry
+
+    lax.fori_loop(0, vocab // chunk, begin, 0)
+
+    def widen(part, carry):
+        rows[strip(part), :] = rows_ref[strip(part), :].astype(FULL)
+        return carry
+
+    lax.fori_loop(0, count // chunk, widen, 0)
+    rows[pl.ds(count, 8), :] = jnp.zeros((8, rows.shape[1]), FULL)
 
     def step(group, carry):
         for member in range(UNROLL):
-            at = group * UNROLL + member
-            spot = pl.ds(ids_ref[block * ROWS_IN_BLOCK + at], 1)
+            at = list_ref[group * UNROLL + member]
+            spot = jnp.minimum(ids_ref[jnp.minimum(at, count - 1)], vocab - 1)
             total = even if member % 2 == 0 else odd
-            total[spot, :] = total[spot, :] + rows[pl.ds(at, 1), :]
+            total[pl.ds(spot, 1), :] = total[pl.ds(spot, 1), :] + rows[pl.ds(at, 1), :]
         return carry
 
-    lax.fori_loop(0, ROWS_IN_BLOCK // UNROLL, step, 0)
-
-    @pl.when(block == pl.num_programs(0) - 1)
-    def _():
-        chunk = 256
-
-        def finish(part, squares):
-            spot = pl.ds(pl.multiple_of(part * chunk, chunk), chunk)
-            value = even[spot, :] + odd[spot, :] + head_ref[spot, :].astype(FULL)
-            even[spot, :] = value
-            return squares + jnp.sum((value * value).reshape(chunk // 8, 8, -1), axis=0)
-
-        squares = lax.fori_loop(
-            0, vocab // chunk, finish, jnp.zeros((8, even.shape[1]), FULL)
-        )
-        square_ref[...] = squares
-        store = pltpu.make_async_copy(even.at[pl.ds(0, vocab)], out_ref, sem)
-        store.start()
-        store.wait()
-
-
-def spread(ids, rows, head):
+    found = list_ref[count + UNROLL]
+    lax.fori_loop(0, (found + UNROLL - 1) // UNROLL, step, 0)
+
+    def finish(part, squares):
+        value = even[strip(part), :] + odd[strip(part), :]
+        even[strip(part), :] = value
+        return squares + jnp.sum((value * value).reshape(chunk // 8, 8, -1), axis=0)
+
+    square_ref[...] = lax.fori_loop(
+        0, vocab // chunk, finish, jnp.zeros((8, even.shape[1]), FULL)
+    )
+    store = pltpu.make_async_copy(even, out_ref, sem)
+    store.start()
+    store.wait()
+
+
+def spread(ids, listed, rows, head):
     vocab, columns = head.shape
     count = ids.shape[0]
+    smem = pl.BlockSpec(memory_space=pltpu.SMEM)
     return pl.pallas_call(
         spread_body,
-        grid_spec=pltpu.PrefetchScalarGridSpec(
-            num_scalar_prefetch=1,
-            grid=(count // ROWS_IN_BLOCK,),
-            in_specs=[
-                pl.BlockSpec((ROWS_IN_BLOCK, columns), lambda block, ids_ref: (block, 0)),
-                pl.BlockSpec((vocab, columns), lambda block, ids_ref: (0, 0)),
-            ],
-            out_specs=[
-                pl.BlockSpec(memory_space=pl.ANY),
-                pl.BlockSpec((8, columns), lambda block, ids_ref: (0, 0)),
-            ],
-            scratch_shapes=[
-                pltpu.VMEM((vocab + 8, columns), FULL),
-                pltpu.VMEM((vocab + 8, columns), FULL),
-                pltpu.VMEM((ROWS_IN_BLOCK, columns), FULL),
-                pltpu.SemaphoreType.DMA,
-            ],
-        ),
-        out_shape=[
-            jax.ShapeDtypeStruct((vocab, columns), FULL),
-            jax.ShapeDtypeStruct((8, columns), FULL),
+        in_specs=[smem, smem, VMEM, VMEM],
+        out_specs=[ANY, VMEM],
+        scratch_shapes=[
+            pltpu.VMEM((vocab, columns), FULL),
+            pltpu.VMEM((vocab, columns), FULL),
+            pltpu.VMEM((count + 8, columns), FULL),
+            pltpu.SemaphoreType.DMA,
         ],
+        out_shape=[struct((vocab, columns), FULL), struct((8, columns), FULL)],
         compiler_params=pltpu.CompilerParams(vmem_limit_bytes=VMEM_BYTES),
         cost_estimate=pl.CostEstimate(
-            flops=count * columns, bytes_accessed=count * columns * 64, transcendentals=0
+            flops=count * columns, bytes_accessed=count * columns * 48, transcendentals=0
         ),
         name="spread",
-    )(ids, rows, head)
+    )(ids, listed, rows, head)
 
 
 def adamw(weight, first_m, second_m, grad, rate, decay):
@@ -1187,23 +1292,10 @@
     return jnp.moveaxis(values.reshape(rows, count, columns // count), 1, 0)
 
 
-def side_by_side(parts):
-    count, rows, columns = parts.shape
-    return jnp.moveaxis(parts, 0, 1).reshape(rows, count * columns)
-
-
-def swap_by_shifts(parts, axis):
+def shifted(parts, axis, step):
     count = lax.axis_size(axis)
-    me = lax.axis_index(axis)
-    result = parts
-    for step in range(1, count):
-        pairs = [(source, (source + step) % count) for source in range(count)]
-        part = lax.dynamic_index_in_dim(parts, lax.rem(me + step, count), 0, False)
-        part = lax.ppermute(part, axis, pairs)
-        result = lax.dynamic_update_index_in_dim(
-            result, part, lax.rem(me - step + count, count), 0
-        )
-    return result
+    pairs = [(source, (source + step) % count) for source in range(count)]
+    return lax.ppermute(parts, axis, pairs)
 
 
 def per_device(
@@ -1255,15 +1347,11 @@
 
     ffn_low = jnp.moveaxis(ffn, 1, 0).astype(LOW)
     ffn_cut = ffn_low.reshape(3, narrow_count, ffn_size, ffn_low.shape[2])
-    ffn_sub = swap_by_shifts(jnp.moveaxis(ffn_cut, 1, 0), "narrow")
+    ffn_cut = jnp.moveaxis(ffn_cut, 1, 0).reshape(narrow_count, 3 * ffn_size, -1)
     proj_own = jnp.concatenate(
         [attn_qo.reshape(columns, -1), attn_kv.reshape(columns, -1)], axis=1
     ).astype(LOW)
-    proj = lax.all_gather(
-        lax.all_gather(proj_own, "narrow", axis=0), "wide", axis=1, tiled=True
-    )
-    ffn_sub = jnp.moveaxis(ffn_sub, 0, 2).reshape(3, ffn_size, width)
-    ffn_w = lax.all_gather(ffn_sub, "wide", axis=0)
+    proj_part = lax.all_gather(proj_own, "narrow", axis=0)
 
     where_at = jnp.arange(seq_len, dtype=jnp.int32)
     pick_tokens = jnp.sum(
@@ -1287,11 +1375,21 @@
     local_ids = wanted - narrow_spot * vocab_rows
     inside = (local_ids >= 0) & (local_ids < vocab_rows)
     spots = jnp.where(inside, local_ids, vocab_rows)
-    found = lookup(embed, spots).reshape(narrow_count, wide_count * all_rows, columns)
-    embed_cut = embed.astype(LOW).reshape(wide_count, vocab_rows // wide_count, columns)
-    rows_low, table_own = launch(
-        [fetch_rows(found, all_rows), join_columns("wide", embed_cut)], 1, "fetch_rows"
-    )
+    found, embed_low, listed = lookup(embed, spots)
+    proj_part, found = lax.optimization_barrier((proj_part, found))
+    proj = lax.all_gather(proj_part, "wide", axis=1, tiled=True)
+    found = found.reshape(narrow_count, wide_count * all_rows, columns)
+    embed_cut = embed_low.reshape(wide_count, vocab_rows // wide_count, columns)
+    rows_low, ffn_sub, table_own = launch(
+        [
+            fetch_rows(found, all_rows),
+            join_columns("narrow", ffn_cut),
+            join_columns("wide", embed_cut),
+        ],
+        1,
+        "fetch_rows",
+    )
+    ffn_w = lax.all_gather(ffn_sub.reshape(3, ffn_size, width), "wide", axis=0)
 
     mom_qo = jnp.moveaxis(attn_qo_mom, 1, 0)
     mom_kv = jnp.moveaxis(attn_kv_mom, 1, 0)
@@ -1348,13 +1446,11 @@
     queries_part = each_owner(normed_own, q_w).reshape(narrow_count, own_rows, heads_own, HD)
     queries_part = rotate(queries_part, cosine_own[:, None], sine_own[:, None])
     queries_part = queries_part.astype(LOW).reshape(narrow_count, own_rows, head_cols)
-    own_head, queries, start_low, tok_cols, pick_cols = launch(
+    own_head, queries, start_low = launch(
         [
             swap_blocks("narrow", by_head),
             swap_blocks("narrow", queries_part),
             gather_blocks("narrow", rows_low[tok_rows:]),
-            split_columns("wide", normed_tok),
-            split_columns("wide", normed_own),
         ],
         2,
         "trade_heads",
@@ -1418,7 +1514,7 @@
     late, mom_top = launch(
         [
             gather_wide(late_part.reshape(sel, width)),
-            swap_blocks("narrow", mom_parts[:, :half]),
+            swap_turned(mom_parts[:, :half]),
         ],
         5,
         "gather_late",
@@ -1427,7 +1523,17 @@
     early_logits, early_stats = exit_logits(early)
     late_logits, late_stats = exit_logits(late)
     stats = jnp.concatenate([early_stats, late_stats], axis=1).reshape(3, 8, -1)
-    stats = launch([combine(stats, merge_stats)], 6, "combine_stats")[0].reshape(3, -1)
+    normed_picks = norm_rows(start_h, gain_w[0]).astype(LOW)
+    stats, tok_cols, pick_cols = launch(
+        [
+            combine(stats, merge_stats),
+            split_columns("wide", normed_tok),
+            split_columns("wide", normed_picks),
+        ],
+        6,
+        "combine_stats",
+    )
+    stats = stats.reshape(3, -1)
     log_norms = stats[0] + jnp.log(stats[1])
     losses = log_norms - stats[2]
     loss_sum = jnp.sum(
@@ -1444,13 +1550,14 @@
     late_back, late_head = exit_back(late_logits, log_norms[total_rows:], EXIT_LAST, late)
     early_back, early_head = exit_back(early_logits, log_norms[:total_rows], EXIT_EARLY, early)
     grad_late, mom_low = launch(
-        [sum_wide(late_back), swap_blocks("narrow", mom_parts[:, half:])], 7, "sum_late"
+        [sum_wide(late_back), swap_turned(mom_parts[:, half:])], 7, "sum_late"
     )
     mom_owned = jnp.concatenate([mom_top, mom_low], axis=1)
     grad_head = (early_head + late_head).astype(LOW)
 
-    grad_final, gain_late, grad_out, grad_early = launch(
+    grad_early, grad_final, gain_late, grad_out = launch(
         [
+            sum_wide(early_back),
             settle_back(
                 grad_late.astype(LOW),
                 final_own,
@@ -1458,7 +1565,6 @@
                 keep_row,
                 gain_w[2:3],
             ),
-            sum_wide(early_back),
         ],
         8,
         "settle_late",
@@ -1466,10 +1572,9 @@
     grad_layer = grad_final * keep_layer
     grad_out = grad_out.reshape(sel, width)
     acts, fed_back = feed_back(grad_out, ffn_w, gate, up, hidden)
-    grad_mid, gain_mid, grad_branch, grad_early, out_all = launch(
+    grad_mid, gain_mid, grad_branch, out_all = launch(
         [
             settle_back(fed_back, middle, grad_layer, keep_row, gain_w[1:2]),
-            sum_narrow(grad_early.astype(LOW)),
             gather_wide(grad_out),
         ],
         9,
@@ -1477,9 +1582,8 @@
     )
     grad_branch = grad_branch.reshape(sel, width)
     out_all = out_all.reshape(total_rows, width)
-    grad_start_exit, gain_early = norm_back(start_own, gain_w[2], grad_early)
-
-    o_own = lax.dynamic_index_in_dim(o_w, narrow_spot, 0, False)
+
+    o_own = lax.dynamic_slice(proj, (narrow_spot, 0, head_cols), (1, width, head_cols))[0]
     grad_mixed = dot(grad_branch, o_own, 1, 0).astype(LOW)
     grouped_grad = grad_mixed.reshape(sel, groups, heads_own // groups, HD)
     grad_probs = jnp.einsum("tkgd,ksd->kgts", grouped_grad, values, preferred_element_type=FULL)
@@ -1503,10 +1607,11 @@
         2, groups, narrow_count, tok_rows, HD
     )
     kv_parts = jnp.transpose(kv_parts, (2, 1, 0, 3, 4))
-    grad_kv, grad_q, acts, queries_wide, branch_cols = launch(
+    grad_kv, grad_q, grad_early, acts, queries_wide, branch_cols = launch(
         [
             swap_blocks("narrow", kv_parts),
             swap_blocks("narrow", grad_queries.reshape(narrow_count, own_rows, head_cols)),
+            sum_narrow(grad_early.astype(LOW)),
             swap_blocks("wide", acts),
             gather_wide(grad_queries),
             split_columns("wide", grad_branch),
@@ -1514,6 +1619,7 @@
         10,
         "trade_grads",
     )
+    grad_start_exit, gain_early = norm_back(start_own, gain_w[2], grad_early)
     grad_kv = grad_kv.reshape(KVH, repeat, 2, tok_rows, HD)
     if repeat > 1:
         grad_kv = jnp.sum(grad_kv.astype(FULL), axis=1, keepdims=True).astype(LOW)
@@ -1536,51 +1642,64 @@
     grad_rows, head_cols_all, kv_wide = launch(
         [
             return_rows(grad_rows.astype(LOW)),
-            split_columns("wide", grad_head),
-            gather_wide(grad_kv_flat),
+            later(split_columns("wide", grad_head), 2),
+            later(gather_wide(grad_kv_flat), 2),
         ],
         11,
         "return_rows",
     )
     acts = jnp.moveaxis(acts, 1, 0).reshape(3, total_rows, ffn_size)
-    acts = lax.all_gather(acts, "narrow", axis=2, tiled=True)
-    summed_table, table_squares = spread(
-        spots, grad_rows.reshape(-1, columns), head_cols_all.reshape(vocab_rows, columns)
-    )
-
-    kv_wide = kv_wide.reshape(wide_count, 2, tok_rows, narrow_count * kv_size)
-    grad_kv_w = jnp.einsum(
-        "wtc,wjtf->jcf", tok_cols, kv_wide, preferred_element_type=FULL
-    )
-    summed_kv = lax.psum_scatter(grad_kv_w, "narrow", scatter_dimension=2, tiled=True)
-    pick_cols = lax.all_gather(pick_cols, "narrow", axis=1, tiled=True)
+    rights = (inner_all, inner_all, out_all)
+    grad_ffn = [dot(acts[j], rights[j], 0, 0) for j in range(3)]
+    ffn_squares = sum(jnp.sum(part * part) for part in grad_ffn)
     summed_qo = jnp.stack(
         [
             jnp.einsum("wtc,wtf->cf", pick_cols, queries_wide, preferred_element_type=FULL),
             jnp.einsum("wtc,wtf->cf", branch_cols, mixed_wide, preferred_element_type=FULL),
         ]
     )
-
-    def cols_own(values_all):
-        size = width // narrow_count
-        return lax.dynamic_slice_in_dim(values_all, narrow_spot * size, size, 1)
-
-    rights = (inner_all, inner_all, out_all)
-    summed_ffn = jnp.stack([dot(acts[j], cols_own(rights[j]), 0, 0) for j in range(3)])
-    small_all = lax.all_gather(
-        pack_small(summed_qo, summed_kv).astype(LOW), "narrow", axis=0
+    qo_flat = summed_qo.astype(LOW).reshape(-1)
+    qo_flat = jnp.pad(qo_flat, (0, ffn_size * width - qo_flat.shape[0]))
+    for_owners = jnp.stack(
+        [part.astype(LOW) for part in grad_ffn] + [qo_flat.reshape(ffn_size, width)]
+    )
+    for_owners, grad_rows = lax.optimization_barrier((for_owners, grad_rows))
+    turn = lax.rem(wide_spot, 2)
+
+    def for_device(spot):
+        matrix = lax.rem(spot + narrow_count - turn, narrow_count)
+        return lax.dynamic_index_in_dim(for_owners, jnp.minimum(matrix, 3), 0, False)
+
+    owned = [for_device(narrow_spot)] + [
+        shifted(for_device(lax.rem(narrow_spot + step, narrow_count)), "narrow", step)
+        for step in range(1, narrow_count)
+    ]
+    kv_wide = kv_wide.reshape(wide_count, 2, tok_rows, narrow_count * kv_size)
+    grad_kv_w = jnp.einsum(
+        "wtc,wjtf->jcf", tok_cols, kv_wide, preferred_element_type=FULL
+    )
+    summed_kv = lax.psum_scatter(grad_kv_w, "narrow", scatter_dimension=2, tiled=True)
+    summed_table, table_squares = spread(
+        spots, listed, grad_rows.reshape(-1, columns), head_cols_all.reshape(vocab_rows, columns)
     )
 
     squares = (
         jnp.sum(summed_qo * summed_qo)
         + jnp.sum(summed_kv * summed_kv)
-        + jnp.sum(summed_ffn * summed_ffn)
+        + ffn_squares
         + jnp.sum(table_squares)
     )
     sums = jnp.stack(
         [gain_attn, gain_mid[0], gain_early + gain_late[0], jnp.full((width,), squares)]
     )
-    sums = launch([combine(sums.reshape(4, 8, -1), add_two)], 12, "combine_sums")[0]
+    sums, kv_owned = launch(
+        [
+            combine(sums.reshape(4, 8, -1), add_two),
+            send_owner(summed_kv.astype(LOW).reshape(-1, lanes)),
+        ],
+        12,
+        "combine_sums",
+    )
     sums = sums.reshape(4, width)
     summed_gain = lax.dynamic_slice_in_dim(
         sums[:3], (wide_spot * narrow_count + narrow_spot) * gain_size, gain_size, 1
@@ -1594,19 +1713,34 @@
             parts.shape[1], parts.shape[2], parts.shape[0] * parts.shape[3]
         )
 
+    final_parts, factor = lax.optimization_barrier((for_owners[:3], factor))
+    size = width // narrow_count
+
+    def final_piece(spot):
+        return lax.dynamic_slice_in_dim(final_parts, spot * size, size, 2)
+
+    summed_ffn = jnp.zeros((3, narrow_count, ffn_size, size), LOW)
+    for step in range(narrow_count):
+        piece = final_piece(lax.rem(narrow_spot + step, narrow_count))
+        if step:
+            piece = shifted(piece, "narrow", step)
+        source = lax.rem(narrow_spot - step + narrow_count, narrow_count)
+        summed_ffn = lax.dynamic_update_index_in_dim(summed_ffn, piece, source, 1)
+    summed_ffn = summed_ffn.reshape(3, ffn_rows, size).astype(FULL)
+
     def ffn_owner():
-        left = lax.dynamic_index_in_dim(acts, jnp.minimum(narrow_spot, 2), 0, False)
-        right = jnp.where(narrow_spot == 2, out_all, inner_all)
-        grad = dot(left, right, 0, 0)
-        mom = side_by_side(mom_owned).astype(FULL)
-        result = newton((MOMENTUM * mom + grad * factor)[None])[0]
-        return cut_columns(result, narrow_count)
+        return newton(factor, mom_owned, owned)
 
     def small_owner():
         mom_q, mom_k = unpack_small(mom_owned.astype(FULL))
-        grad_q, grad_k = unpack_small(small_all.astype(FULL))
+        order = lax.rem(
+            narrow_spot - jnp.arange(narrow_count, dtype=jnp.int32) + narrow_count, narrow_count
+        )
+        grad_q = jnp.stack(owned).reshape(narrow_count, -1)[:, : mom_qo.size]
+        grad_q = jnp.take(grad_q, order, axis=0).reshape((narrow_count,) + mom_qo.shape)
+        grad_k = kv_owned.reshape((narrow_count,) + mom_kv.shape)
         results = [
-            newton(whole_columns(MOMENTUM * mom + grad * factor))
+            newton_small(whole_columns(MOMENTUM * mom + grad.astype(FULL) * factor))
             for mom, grad in ((mom_q, grad_q), (mom_k, grad_k))
         ]
         parts = [
@@ -1619,10 +1753,28 @@
         flat = jnp.pad(flat, ((0, 0), (0, slot_rows * slot_cols - flat.shape[1])))
         return flat.reshape(narrow_count, slot_rows, slot_cols)
 
-    directions = lax.cond(narrow_spot == 3, small_owner, ffn_owner)
-    directions = swap_by_shifts(directions, "narrow")
-    dir_ffn = directions[:3].astype(FULL)
-    dir_qo, dir_kv = unpack_small(directions[3].astype(FULL))
+    small_spot = lax.rem(3 + turn, narrow_count)
+    directions = lax.cond(narrow_spot == small_spot, small_owner, ffn_owner)
+    received = [lax.dynamic_index_in_dim(directions, narrow_spot, 0, False)] + [
+        shifted(
+            lax.dynamic_index_in_dim(
+                directions, lax.rem(narrow_spot + step, narrow_count), 0, False
+            ),
+            "narrow",
+            step,
+        )
+        for step in range(1, narrow_count)
+    ]
+
+    def direction_of(matrix):
+        step = lax.rem(narrow_spot - matrix - turn + 2 * narrow_count, narrow_count)
+        result = received[0]
+        for at in range(1, narrow_count):
+            result = jnp.where(step == at, received[at], result)
+        return result
+
+    dir_ffn = jnp.stack([direction_of(matrix) for matrix in range(3)]).astype(FULL)
+    dir_qo, dir_kv = unpack_small(direction_of(3).astype(FULL))
 
     embed_new, embed_m_new, embed_v_new = adamw(
         embed, embed_m, embed_v, summed_table * factor, RATE_ADAM, WEIGHT_DECAY

time: 1370 us -> 1180 us (0.86)
  waiting for transfers between devices: 189 us -> 25.1 us
  starting transfers between devices: 8.64 us -> 87.9 us
  local copies, waits for them, and re-layouts: 138 us -> 62 us
  blocking collectives: 20.6 us -> 0 us
  Pallas kernels: 763 us -> 782 us
    all_gather x5 -> x3, waiting for transfers between devices: 109 us -> 0.02 us  [the longest x1 0.02 us: per_device(): proj_part = lax.all_gather(proj_own, 'narrow', axis=0)]
    ppermute x6 -> x9, starting transfers between devices: 8.39 us -> 87.5 us  [shifted(): return lax.ppermute(parts, axis, pairs)]
    pallas_call x13, Pallas kernels: 584 us -> 650 us  [launch(): pl.pallas_call(body, out_shape=outputs, in_specs=[place for task in tasks...]
    pallas_call x3, Pallas kernels: 151 us -> 105 us  [the longest x1 45 us: newton(): pl.pallas_call(newton_body, in_specs=[pl.BlockSpec(memory_space=pltpu.SME...]
    ppermute x6 -> x9, waiting for transfers between devices: 70.4 us -> 25 us  [shifted(): return lax.ppermute(parts, axis, pairs)]
    dynamic_update_slice x5, local copies, waits for them, and re-layouts: 46.8 us -> 4.69 us  [per_device(): summed_ffn = lax.dynamic_update_index_in_dim(summed_ffn, piece, source, 1)]
    all_gather x1 -> x0, blocking collectives: 20.6 us -> none  [per_device(): pick_cols = lax.all_gather(pick_cols, 'narrow', axis=1, tiled=True)]
    dot_general x11 -> x10, matrix products: 65 us -> 60.3 us  [dot(): lax.dot_general(first, second, (((first_dim,), (second_dim,)), ((), ())),...]
  transfers between devices with their start and end apart: 12 -> 13, of which waited for: 9 -> 1; matrix products, arithmetic and copies ran while one was open for 13% -> 11% of each run, Pallas kernels for 22% -> 35%
where the time goes in v4:
time: 1180 us; the launch traced here: 1170 us
  Pallas kernels  782 us (66%)
  matrix products  94.6 us (8%)
  other arithmetic  91.8 us (8%)
  starting transfers between devices  87.9 us (7%)
  local copies, waits for them, and re-layouts  62 us (5%)
  waiting for transfers between devices  25.1 us (2%)
  between operations  24.3 us (2%)
    pallas_call x13, Pallas kernels, launch(): pl.pallas_call(body, out_shape=outputs, in_specs=[place for task in tasks...  650 us
    ppermute x9, starting transfers between devices, shifted(): return lax.ppermute(parts, axis, pairs)  87.5 us
    dot_general x10, matrix products, dot(): lax.dot_general(first, second, (((first_dim,), (second_dim,)), ((), ())),...  60.3 us
    pallas_call x1, Pallas kernels, newton(): pl.pallas_call(newton_body, in_specs=[pl.BlockSpec(memory_space=pltpu.SME...  45 us
    pallas_call x1, Pallas kernels, lookup(): pl.pallas_call(lookup_body, in_specs=[pl.BlockSpec(memory_space=pltpu.SME...  38.1 us
    ppermute x9, waiting for transfers between devices, shifted(): return lax.ppermute(parts, axis, pairs)  25 us
  transfers between devices with their start and end apart: 13, of which 1 were waited for; matrix products, arithmetic and copies ran while one was open for 11% of the time, Pallas kernels for 35%

profile of v4, /device:TPU:17, one launch (start us, length us, event | category | flops | bytes accessed | tf_op | source)
XLA Modules:
  0.0 1174.6 jit_solution(13173428518257215952)
XLA Ops:
  12.9 14.0 %gather_ids.1 = (s32[8,16,128]{2,1,0:T(8,128)}, f32[4,8,8,128]{3,2,1,0:T(8,128)}) custom-call(s32[16,128]{1,0:T(8,128)} %pad_bitcast_fusion.refs_0_, f32[8,128]{1,0:T(8,128)} %bitcast_convert_fusion.refs_1_), custom_call_target="tpu_custom_call" | custom-call | bytes 1671168 | tf_op jit(solution)/shard_map/gather_ids/pallas_call | solution.py:156
  29.1 38.1 %lookup.1 = (bf16[9216,256]{1,0:T(8,128)(2,1)}, bf16[8192,256]{1,0:T(8,128)(2,1)}, s32[9248]{0:T(1024)}) custom-call(s32[9216]{0:T(1024)} %and_select_fusion.ids_ref, f32[8192,256]{1,0:T(8,128)} %table_ref.1), custom_call_target="tpu_custom_call" | custom-call | bytes 65011712 | tf_op jit(solution)/shard_map/lookup/pallas_call | solution.py:1186
  67.3 4.4 copy.221
  71.7 2.5 convert_element_type.234
  75.8 163.0 %fetch_rows.1 = (bf16[288,2048]{1,0:T(8,128)(2,1)}, bf16[528,2048]{1,0:T(8,128)(2,1)}, bf16[1024,2048]{1,0:T(8,128)(2,1)}) custom-call(bf16[4,2304,256]{2,1,0:T(8,128)(2,1)} %bitcast.423, bf16[4,528,512]{2,1,0:T(8,128)(2,1)} %bitcast.419, bf16[8,1024,256]{2,1,0:T(8,128)(2,1)} %bitcast.429), custom_call_target="tpu_custom_call" | custom-call | bytes 148897792 | tf_op jit(solution)/shard_map/fetch_rows/pallas_call | solution.py:156
  245.2 2.5 convert_bitcast_fusion.1
  247.8 1.9 pad_maximum_fusion.8
  256.3 6.1 fusion.56
  269.2 2.3 fusion.53
  272.5 25.7 %trade_heads.1 = (bf16[4,1,2,256,128]{4,3,2,1,0:T(8,128)(2,1)}, bf16[4,32,512]{2,1,0:T(8,128)(2,1)}, bf16[4,32,2048]{2,1,0:T(8,128)(2,1)}) custom-call(bf16[4,1,2,256,128]{4,3,2,1,0:T(8,128)(2,1)} %maximum_bitcast_fusion.refs_0_, bf16[4,32,512]{2,1,0:T(8,128)(2,1)} %convert_element_type.243.refs_1_, bf16[32,2048]{1,0:T(8,128)(2,1)} %slice.207.refs_2_), custom_call_target="tpu_custom_call" | custom-call | bytes 15728640 | tf_op jit(solution)/shard_map/trade_heads/pallas_call | solution.py:156
  305.9 1.7 copy.281.refs_0_.refs_2_
  307.6 2.3 multiply_convert_fusion
  309.8 52.8 %gather_mixed.1 = (bf16[4,128,512]{2,1,0:T(8,128)(2,1)}, bf16[8,128,2048]{2,1,0:T(8,128)(2,1)}, bf16[8,128,512]{2,1,0:T(8,128)(2,1)}) custom-call(bf16[128,512]{1,0:T(8,128)(2,1)} %copy.281.refs_0_.refs_2_, bf16[128,2048]{1,0:T(8,128)(2,1)} %get-tuple-element.343.refs_1_, bf16[128,512]{1,0:T(8,128)(2,1)} %copy.281.refs_0_.refs_2_), custom_call_target="tpu_custom_call" | custom-call | bytes 52428800 | tf_op jit(solution)/shard_map/gather_mixed/pallas_call | solution.py:156
  365.2 5.5 multiply_reduce_fusion.4
  372.4 13.1 %feed.1 = (f32[8,128,176]{2,1,0:T(8,128)}, f32[8,128,176]{2,1,0:T(8,128)}, bf16[8,128,176]{2,1,0:T(8,128)(2,1)}, bf16[128,2048]{1,0:T(8,128)(2,1)}) custom-call(bf16[128,2048]{1,0:T(8,128)(2,1)} %multiply_convert_fusion.1.inner_ref.refs_5_, bf16[8,3,176,2048]{3,2,1,0:T(8,128)(2,1)} %all-gather.8.cloned.1.call-done.weight_ref), custom_call_target="tpu_custom_call" | custom-call | flops 2214592512 | bytes 17301504 | tf_op jit(solution)/shard_map/feed/pallas_call | solution.py:938
  386.1 31.9 %settle.1 = (f32[32,2048]{1,0:T(8,128)}, bf16[4,32,2048]{2,1,0:T(8,128)(2,1)}, bf16[8,128,2048]{2,1,0:T(8,128)(2,1)}) custom-call(bf16[4,32,2048]{2,1,0:T(8,128)(2,1)} %bitcast.462, f32[32,2048]{1,0:T(8,128)} %constant_dynamic-slice_fusion.5.refs_1_, f32[32,2048]{1,0:T(8,128)} %get-tuple-element.306.refs_2_, f32[1,2048]{1,0:T(1,128)} %broadcast_in_dim.187.refs_3_.refs_4_, ...), custom_call_target="tpu_custom_call" | custom-call | bytes 52559872 | tf_op jit(solution)/shard_map/settle/pallas_call | solution.py:156
  418.0 33.3 %gather_late.1 = (bf16[8,128,2048]{2,1,0:T(8,128)(2,1)}, bf16[4,352,512]{2,1,0:T(8,128)(2,1)}) custom-call(bf16[128,2048]{1,0:T(8,128)(2,1)} %bitcast.467, bf16[4,352,512]{2,1,0:T(8,128)(2,1)} %get-tuple-element.325.refs_1_), custom_call_target="tpu_custom_call" | custom-call | bytes 60817408 | tf_op jit(solution)/shard_map/gather_late/pallas_call | solution.py:156
  451.4 7.8 fusion.146
  459.2 4.5 fusion.145
  463.8 2.0 exponential_reduce_fusion.1
  466.4 24.8 %combine_stats.1 = (f32[3,8,256]{2,1,0:T(8,128)}, bf16[8,256,256]{2,1,0:T(8,128)(2,1)}, bf16[8,128,256]{2,1,0:T(8,128)(2,1)}) custom-call(f32[3,8,256]{2,1,0:T(8,128)} %bitcast.480, bf16[256,2048]{1,0:T(8,128)(2,1)} %slice.260.refs_1_, bf16[128,2048]{1,0:T(8,128)(2,1)} %get-tuple-element.342.refs_2_), custom_call_target="tpu_custom_call" | custom-call | bytes 25559040 | tf_op jit(solution)/shard_map/combine_stats/pallas_call | solution.py:156
  492.6 8.7 convolution_convert_fusion
  501.3 36.9 %sum_late.1 = (f32[128,2048]{1,0:T(8,128)}, bf16[4,352,512]{2,1,0:T(8,128)(2,1)}) custom-call(bf16[8,128,2048]{2,1,0:T(8,128)(2,1)} %bitcast.430, bf16[4,352,512]{2,1,0:T(8,128)(2,1)} %get-tuple-element.324.refs_1_), custom_call_target="tpu_custom_call" | custom-call | bytes 65011712 | tf_op jit(solution)/shard_map/sum_late/pallas_call | solution.py:156
  538.2 2.1 convert_element_type.267
  544.2 10.2 convolution_convert_fusion.1
  555.2 34.8 %settle_late.1 = (f32[128,2048]{1,0:T(8,128)}, f32[32,2048]{1,0:T(8,128)}, f32[1,2048]{1,0:T(1,128)}, bf16[4,32,2048]{2,1,0:T(8,128)(2,1)}) custom-call(bf16[8,128,2048]{2,1,0:T(8,128)(2,1)} %bitcast.425, bf16[4,32,2048]{2,1,0:T(8,128)(2,1)} %bitcast.441, f32[32,2048]{1,0:T(8,128)} %get-tuple-element.136.refs_2_, f32[32,2048]{1,0:T(8,128)} %broadcast_in_dim.188.refs_3_, ...), custom_call_target="tpu_custom_call" | custom-call | bytes 56819712 | tf_op jit(solution)/shard_map/settle_late/pallas_call | solution.py:156
  590.0 1.7 broadcast_multiply_fusion.refs_2_
  591.7 14.4 %feed_back.1 = (bf16[8,3,128,176]{3,2,1,0:T(8,128)(2,1)}, bf16[128,2048]{1,0:T(8,128)(2,1)}) custom-call(bf16[128,2048]{1,0:T(8,128)(2,1)} %bitcast.439, bf16[8,3,176,2048]{3,2,1,0:T(8,128)(2,1)} %all-gather.8.cloned.1.call-done.weight_ref, f32[8,128,176]{2,1,0:T(8,128)} %get-tuple-element.138.gate_ref, f32[8,128,176]{2,1,0:T(8,128)} %get-tuple-element.139.up_ref, ...), custom_call_target="tpu_custom_call" | custom-call | flops 2214592512 | bytes 17301504 | tf_op jit(solution)/shard_map/feed_back/pallas_call | solution.py:990
  606.1 31.9 %settle_middle.1 = (f32[32,2048]{1,0:T(8,128)}, f32[1,2048]{1,0:T(1,128)}, bf16[4,32,2048]{2,1,0:T(8,128)(2,1)}, bf16[8,128,2048]{2,1,0:T(8,128)(2,1)}) custom-call(bf16[4,32,2048]{2,1,0:T(8,128)(2,1)} %bitcast.461, f32[32,2048]{1,0:T(8,128)} %constant_dynamic-slice_fusion.5.refs_1_, f32[32,2048]{1,0:T(8,128)} %broadcast_multiply_fusion.refs_2_, ...), custom_call_target="tpu_custom_call" | custom-call | bytes 52625408 | tf_op jit(solution)/shard_map/settle_middle/pallas_call | solution.py:156
  638.0 2.6 fusion.63
  644.0 1.7 copy-done.12
  647.0 6.9 fusion.128
  659.4 34.5 %trade_grads.1 = (bf16[4,1,2,256,128]{4,3,2,1,0:T(8,128)(2,1)}, bf16[4,32,512]{2,1,0:T(8,128)(2,1)}, f32[32,2048]{1,0:T(8,128)}, bf16[8,3,128,176]{3,2,1,0:T(8,1...) custom-call(bf16[4,1,2,256,128]{4,3,2,1,0:T(8,128)(2,1)} %maximum_bitcast_fusion.1.refs_0_, ...), custom_call_target="tpu_custom_call" | custom-call | bytes 51904512 | tf_op jit(solution)/shard_map/trade_grads/pallas_call | solution.py:156
  693.9 1.7 convolution_bitcast_fusion.4
  698.6 2.5 fusion.139
  701.2 12.7 %add_convert_fusion.refs_1_ = bf16[1024,2048]{1,0:T(8,128)(2,1)} fusion(f32[1024,2048]{1,0:T(8,128)} %fusion.128, bf16[1024,2048]{1,0:T(8,128)(2,1)} %bitcast.508, f32[1024,1024]{0,1:T(8,128)} %copy-done.10, f32[1024]{0:T(1024)S(1)} %copy-done.63, f32[1024]{0:T(1024)S(1)} %bitcast.499, s32[1024]{0:T(1024)S(1)} %copy-done.51), kind=kOutput, calls=%fused_computation.37 | convolution fusion | flops 4305453056 | bytes 20983808 | tf_op jit(solution)/shard_map/dot_general | solution.py:42
  714.3 2.5 convolution_bitcast_fusion
  716.8 2.4 fusion.19
  725.0 113.8 %return_rows.1 = (bf16[4,2304,256]{2,1,0:T(8,128)(2,1)}, bf16[8,1024,256]{2,1,0:T(8,128)(2,1)}, bf16[8,512,512]{2,1,0:T(8,128)(2,1)}) custom-call(bf16[288,2048]{1,0:T(8,128)(2,1)} %pad_maximum_fusion.9.refs_0_, bf16[1024,2048]{1,0:T(8,128)(2,1)} %add_convert_fusion.refs_1_, bf16[512,512]{1,0:T(8,128)(2,1)} %bitcast.445), custom_call_target="tpu_custom_call" | custom-call | bytes 152043520 | tf_op jit(solution)/shard_map/return_rows/pallas_call | solution.py:156
  838.8 4.7 convolution_bitcast_fusion.2
  843.6 4.1 convert_bitcast_fusion.2
  848.6 1.8 convert_bitcast_fusion.3
  850.8 21.7 %spread.1 = (f32[8192,256]{1,0:T(8,128)}, f32[8,256]{1,0:T(8,128)}) custom-call(s32[9216]{0:T(1024)} %and_select_fusion.ids_ref, s32[9248]{0:T(1024)} %get-tuple-element.161.list_ref, bf16[9216,256]{1,0:T(8,128)(2,1)} %bitcast.422, bf16[8192,256]{1,0:T(8,128)(2,1)} %bitcast.424), custom_call_target="tpu_custom_call" | custom-call | flops 2359296 | bytes 113246208 | tf_op jit(solution)/shard_map/spread/pallas_call | solution.py:1260
  875.5 1.6 dynamic-slice_bitcast_fusion.3
  877.1 5.2 collective-permute-start.1
  882.4 2.4 collective-permute-start.2
  886.7 1.9 multiply_reduce_fusion.3
  888.6 2.7 constant_dynamic-update-slice_fusion.1
  891.3 2.6 constant_dynamic-update-slice_fusion
  893.9 1.8 fusion.142
  899.1 52.4 %combine_sums.1 = (f32[4,8,256]{2,1,0:T(8,128)}, bf16[4,512,128]{2,1,0:T(8,128)(2,1)}) custom-call(f32[4,8,256]{2,1,0:T(8,128)} %maximum_maximum_fusion.1.refs_0_, bf16[512,128]{1,0:T(8,128)(2,1)} %bitcast.463), custom_call_target="tpu_custom_call" | custom-call | bytes 5767168 | tf_op jit(solution)/shard_map/combine_sums/pallas_call | solution.py:156
  958.7 3.1 collective-permute-start.7
  963.1 1.7 collective-permute-start.8
  964.9 51.7 %conditional.1 = (bf16[4,704,512]{2,1,0:T(8,128)(2,1)S(1)}) conditional(s32[]{:T(128)} %convert_element_type.284, (f32[]{:T(128)}, bf16[4,704,512]{2,1,0:T(8,128)(2,1)}, bf16[176,2048]{1,0:T(8,128)(2,1)S(1)}, bf16[176,2048]{1,0:T(8,128)(2,1)}, bf16[176,2048]{1,0:T(8,128)(2,1)}, /*index=5*/bf16[176,2048]{1,0:T(8,128)(2,1)}) %tuple.98, ...), branch_computations={%region_37.38_spmd, %region_38.39_spmd} | conditional | flops 23789568000 | bytes 138678528 | solution.py:1757
  964.9 45.0 %newton.1 = bf16[4,704,512]{2,1,0:T(8,128)(2,1)S(1)} custom-call(f32[1]{0:T(128)} %bitcast.factor_ref, bf16[4,704,512]{2,1,0:T(8,128)(2,1)} %get-tuple-element.32.mom_ref, bf16[176,2048]{1,0:T(8,128)(2,1)S(1)} %get-tuple-element.33.refs_0_, bf16[176,2048]{1,0:T(8,128)(2,1)} %get-tuple-element.34.refs_1_, bf16[176,2048]{1,0:T(8,128)(2,1)} %get-tuple-element.35.refs_2_, ...), custom_call_target="tpu_custom_call" | custom-call | flops 23789568000 | bytes 8650752 | tf_op jit(solution)/shard_map/cond/branch_0_fun/newton/pallas_call | solution.py:1139
  1018.2 73.6 %collective-permute-start.4 = (bf16[704,512]{1,0:T(8,128)(2,1)}, bf16[704,512]{1,0:T(8,128)(2,1)}, u32[]{:S(2)}, u32[]{:S(2)}) collective-permute-start(bf16[704,512]{1,0:T(8,128)(2,1)} %get-tuple-element.318), channel_id=1, source_target_pairs={{0,2},{1,3},{2,0},{3,1},{4,6},{5,7},{6,4},{7,5},{8,10},{9,11},{10,... | collective-permute-start | bytes 2162696 | tf_op jit(solution)/shard_map/ppermute | solution.py:1298
  1091.8 22.2 %multiply_subtract_fusion = (f32[8192,256]{1,0:T(8,128)}, f32[8192,256]{1,0:T(8,128)}, f32[8192,256]{1,0:T(8,128)}) fusion(f32[8192,256]{1,0:T(8,128)} %table_ref.1, f32[8192,256]{1,0:T(8,128)} %get-tuple-element.167, f32[]{:T(128)} %div.107, f32[8192,256]{1,0:T(8,128)} %param.25, f32[8192,256]{1,0:T(8,128)} %param.26), kind=kLoop, calls=%fused_computation.35 | loop fusion | flops 31457280 | bytes 58720260 | tf_op jit(solution)/shard_map/sub | solution.py:1287
  1114.0 1.8 bitcast_add_fusion.2
  1119.3 1.8 copy.263
  1126.9 3.1 bitcast_add_fusion
  1130.0 24.9 %collective-permute-done.5 = bf16[704,512]{1,0:T(8,128)(2,1)S(1)} collective-permute-done((bf16[704,512]{1,0:T(8,128)(2,1)}, bf16[704,512]{1,0:T(8,128)(2,1)S(1)}, u32[]{:S(2)}, u32[]{:S(2)}) %collective-permute-start.5) | collective-permute-done | bytes 720928 | tf_op jit(solution)/shard_map/ppermute | solution.py:1298
  1155.0 1.9 fusion.77
  1158.1 2.2 bitcast_subtract_fusion.2
  1161.4 5.1 bitcast_subtract_fusion
  (347 shorter events, 92.1 us)
Async XLA Ops:
  7.2 4.2 copy-start.54
  7.2 4.8 copy-start.61
  7.2 4.8 copy-start.52
  7.2 5.0 copy-start.68
  7.2 60.1 %all-gather.4.cloned.1.call-start = ((), (), s32[]{:S(2)}) async-start(), calls=%async_computation.1 | async-start | bytes 3276800 | tf_op jit(solution)/shard_map/all_gather | solution.py:1354
  11.3 245.1 %all-gather.6.cloned.1.call-start = ((), (), s32[]{:S(2)}) async-start(), calls=%async_computation.2 | async-start | bytes 23592960 | tf_op jit(solution)/shard_map/all_gather | solution.py:1380
  71.7 300.7 %all-gather.8.cloned.1.call-start = ((), (), s32[]{:S(2)}) async-start(), calls=%async_computation.3 | async-start | bytes 19464192 | tf_op jit(solution)/shard_map/all_gather | solution.py:1392
  75.8 163.3 %copy-start.40 = (f32[4,8,8,128]{3,2,1,0:T(8,128)S(1)}, f32[4,8,8,128]{3,2,1,0:T(8,128)}, u32[]{:S(2)}) copy-start(f32[4,8,8,128]{3,2,1,0:T(8,128)} %get-tuple-element.122) | copy-start | bytes 393220
  238.8 4.4 copy-start.13
  238.8 655.0 %reduce-scatter.2.cloned.1.call-start = ((), (), s32[]{:S(2)}) async-start(), calls=%async_computation.4 | async-start | bytes 1310720 | tf_op jit(solution)/shard_map/reduce_scatter | solution.py:1681
  244.5 8.3 copy-start.57
  247.7 6.2 copy-start.1
  254.9 7.5 copy-start.44
  254.9 7.5 copy-start.41
  365.2 6.3 copy-start.43
  451.3 7.8 copy-start.70
  451.4 7.8 copy-start.71
  459.1 33.5 %copy-start.10 = (f32[1024,1024]{0,1:T(8,128)}, f32[1024,1024]{0,1:T(8,128)S(1)}, u32[]{:S(2)}) copy-start(f32[1024,1024]{0,1:T(8,128)S(1)} %get-tuple-element.379) | copy-start | bytes 12582916
  459.2 4.6 copy-start.49
  463.8 28.9 %copy-start.62 = (f32[1024]{0:T(1024)S(1)}, f32[1024]{0:T(1024)}, u32[]{:S(2)}) copy-start(f32[1024]{0:T(1024)} %get-tuple-element.307) | copy-start | bytes 12292
  492.6 8.7 copy-start.64
  606.1 34.6 %copy-start.36 = (bf16[1,1,4,256,128]{4,3,0,1,2:T(8,128)(2,1)S(1)}, bf16[1,1,4,256,128]{4,3,0,1,2:T(8,128)(2,1)}, u32[]{:S(2)}) copy-start(bf16[1,1,4,256,128]{4,3,0,1,2:T(8,128)(2,1)} %copy-done.35) | copy-start | bytes 786436
  606.1 34.6 %copy-start.47 = (f32[4,128]{1,0:T(4,128)S(1)}, f32[4,128]{1,0:T(4,128)}, u32[]{:S(2)}) copy-start(f32[4,128]{1,0:T(4,128)} %copy-done.46) | copy-start | bytes 6148
  606.1 34.6 %copy-start.60 = (f32[4,128]{1,0:T(4,128)S(1)}, f32[4,128]{1,0:T(4,128)}, u32[]{:S(2)}) copy-start(f32[4,128]{1,0:T(4,128)} %copy-done.59) | copy-start | bytes 6148
  646.9 6.9 copy-start.38
  647.0 6.9 copy-start.39
  647.0 8.6 copy-start.22
  647.0 8.6 copy-start.48
  647.0 8.6 copy-start.58
  657.5 36.3 %copy-start.33 = (bf16[8,128,256]{2,1,0:T(8,128)(2,1)S(1)}, bf16[8,128,256]{2,1,0:T(8,128)(2,1)}, u32[]{:S(2)}) copy-start(bf16[8,128,256]{2,1,0:T(8,128)(2,1)} %get-tuple-element.151) | copy-start | bytes 1572868
  659.4 36.2 %copy-start.26 = (bf16[8,128,512]{2,1,0:T(8,128)(2,1)S(1)}, bf16[8,128,512]{2,1,0:T(8,128)(2,1)}, u32[]{:S(2)}) copy-start(bf16[8,128,512]{2,1,0:T(8,128)(2,1)} %get-tuple-element.154) | copy-start | bytes 3145732
  697.1 4.1 copy-start.7
  697.4 3.8 copy-start.51
  701.2 12.7 %copy-start.20 = (bf16[4,1,2,256,128]{4,3,2,1,0:T(8,128)(2,1)S(1)}, bf16[4,1,2,256,128]{4,3,2,1,0:T(8,128)(2,1)}, u32[]{:S(2)}) copy-start(bf16[4,1,2,256,128]{4,3,2,1,0:T(8,128)(2,1)} %get-tuple-element.146) | copy-start | bytes 1572868
  701.2 18.1 %slice-start.2 = ((s8[20971520]{0:T(1024)(128)(4,1)}), s8[4194304]{0:T(1024)(128)(4,1)S(1)}, s32[]{:S(2)}) async-start(s8[20971520]{0:T(1024)(128)(4,1)} %bitcast.431), calls=%async_computation.7 | async-start | bytes 8388608
  701.2 18.0 %slice-start.3 = ((s8[20971520]{0:T(1024)(128)(4,1)}), s8[4194304]{0:T(1024)(128)(4,1)S(1)}, s32[]{:S(2)}) async-start(s8[20971520]{0:T(1024)(128)(4,1)} %bitcast.431), calls=%async_computation.8 | async-start | bytes 8388608
  701.2 18.0 %slice-start.4 = ((s8[20971520]{0:T(1024)(128)(4,1)}), s8[4194304]{0:T(1024)(128)(4,1)S(1)}, s32[]{:S(2)}) async-start(s8[20971520]{0:T(1024)(128)(4,1)} %bitcast.431), calls=%async_computation.9 | async-start | bytes 8388608
  701.2 18.0 %slice-start.5 = ((s8[20971520]{0:T(1024)(128)(4,1)}), s8[4194304]{0:T(1024)(128)(4,1)S(1)}, s32[]{:S(2)}) async-start(s8[20971520]{0:T(1024)(128)(4,1)} %bitcast.431), calls=%async_computation.10 | async-start | bytes 8388608
  713.9 5.4 slice-start.6
  725.0 113.8 %copy-start.73 = (bf16[8,256,256]{2,1,0:T(8,128)(2,1)S(1)}, bf16[8,256,256]{2,1,0:T(8,128)(2,1)}, u32[]{:S(2)}) copy-start(bf16[8,256,256]{2,1,0:T(8,128)(2,1)} %get-tuple-element.157) | copy-start | bytes 3145732
  838.8 4.8 copy-start.34
  843.5 4.1 copy-start.2
  843.5 4.1 copy-start.21
  850.8 23.1 %copy-start.53 = (f32[1,2048]{1,0:T(1,128)S(1)}, f32[1,2048]{1,0:T(1,128)}, u32[]{:S(2)}) copy-start(f32[1,2048]{1,0:T(1,128)} %get-tuple-element.150) | copy-start | bytes 24580
  850.8 23.1 %copy-start.56 = (f32[1,2048]{1,0:T(1,128)S(1)}, f32[1,2048]{1,0:T(1,128)}, u32[]{:S(2)}) copy-start(f32[1,2048]{1,0:T(1,128)} %get-tuple-element.148) | copy-start | bytes 24580
  877.1 86.0 %collective-permute-start = (bf16[176,2048]{1,0:T(8,128)(2,1)}, bf16[176,2048]{1,0:T(8,128)(2,1)}, u32[]{:S(2)}, u32[]{:S(2)}) collective-permute-start(bf16[176,2048]{1,0:T(8,128)(2,1)} %get-tuple-element.322), channel_id=1, source_target_pairs={{0,1},{1,2},{2,3},{3,0},{4,5},{5,6},{6,7},{7,4},{8,9},{9,10},{10,1... | collective-permute-start | bytes 2162696 | tf_op jit(solution)/shard_map/ppermute | solution.py:1298
  877.1 87.7 %collective-permute-start.1 = (bf16[176,2048]{1,0:T(8,128)(2,1)}, bf16[176,2048]{1,0:T(8,128)(2,1)}, u32[]{:S(2)}, u32[]{:S(2)}) collective-permute-start(bf16[176,2048]{1,0:T(8,128)(2,1)} %get-tuple-element.321), channel_id=1, source_target_pairs={{0,2},{1,3},{2,0},{3,1},{4,6},{5,7},{6,4},{7,5},{8,10},{9,11},{10,... | collective-permute-start | bytes 2162696 | tf_op jit(solution)/shard_map/ppermute | solution.py:1298
  882.4 82.5 %collective-permute-start.2 = (bf16[176,2048]{1,0:T(8,128)(2,1)}, bf16[176,2048]{1,0:T(8,128)(2,1)}, u32[]{:S(2)}, u32[]{:S(2)}) collective-permute-start(bf16[176,2048]{1,0:T(8,128)(2,1)} %get-tuple-element.320), channel_id=1, source_target_pairs={{0,3},{1,0},{2,1},{3,2},{4,7},{5,4},{6,5},{7,6},{8,11},{9,8},{10,9... | collective-permute-start | bytes 2162696 | tf_op jit(solution)/shard_map/ppermute | solution.py:1298
  888.6 68.9 %copy-start.6 = (bf16[3,176,2048]{2,1,0:T(8,128)(2,1)S(1)}, bf16[3,176,2048]{2,1,0:T(8,128)(2,1)}, u32[]{:S(2)}) copy-start(bf16[3,176,2048]{2,1,0:T(8,128)(2,1)} %slice.240) | copy-start | bytes 6488068
  893.9 68.0 %copy-start.8 = (f32[1,256,512]{2,1,0:T(8,128)S(1)}, f32[1,256,512]{2,1,0:T(8,128)}, u32[]{:S(2)}) copy-start(f32[1,256,512]{2,1,0:T(8,128)} %copy-done.7) | copy-start | bytes 1572868
  956.9 5.0 copy-start.14
  957.5 7.4 copy-start.18
  958.7 162.4 %collective-permute-start.6 = (bf16[3,176,512]{2,1,0:T(8,128)(2,1)}, bf16[3,176,512]{2,1,0:T(8,128)(2,1)}, u32[]{:S(2)}, u32[]{:S(2)}) collective-permute-start(bf16[3,176,512]{2,1,0:T(8,128)(2,1)} %get-tuple-element.328), channel_id=1, source_target_pairs={{0,1},{1,2},{2,3},{3,0},{4,5},{5,6},{6,7},{7,4},{8,9},{9,10},{10,1... | collective-permute-start | bytes 1622024 | tf_op jit(solution)/shard_map/ppermute | solution.py:1298
  958.7 164.9 %collective-permute-start.7 = (bf16[3,176,512]{2,1,0:T(8,128)(2,1)}, bf16[3,176,512]{2,1,0:T(8,128)(2,1)}, u32[]{:S(2)}, u32[]{:S(2)}) collective-permute-start(bf16[3,176,512]{2,1,0:T(8,128)(2,1)} %get-tuple-element.327), channel_id=1, source_target_pairs={{0,2},{1,3},{2,0},{3,1},{4,6},{5,7},{6,4},{7,5},{8,10},{9,11},{10,... | collective-permute-start | bytes 1622024 | tf_op jit(solution)/shard_map/ppermute | solution.py:1298
  963.1 162.0 %collective-permute-start.8 = (bf16[3,176,512]{2,1,0:T(8,128)(2,1)}, bf16[3,176,512]{2,1,0:T(8,128)(2,1)}, u32[]{:S(2)}, u32[]{:S(2)}) collective-permute-start(bf16[3,176,512]{2,1,0:T(8,128)(2,1)} %get-tuple-element.326), channel_id=1, source_target_pairs={{0,3},{1,0},{2,1},{3,2},{4,7},{5,4},{6,5},{7,6},{8,11},{9,8},{10,9... | collective-permute-start | bytes 1622024 | tf_op jit(solution)/shard_map/ppermute | solution.py:1298
  1016.6 75.2 %copy-start.17 = (bf16[4,704,512]{2,1,0:T(8,128)(2,1)}, bf16[4,704,512]{2,1,0:T(8,128)(2,1)S(1)}, u32[]{:S(2)}) copy-start(bf16[4,704,512]{2,1,0:T(8,128)(2,1)S(1)} %get-tuple-element.384) | copy-start | bytes 8650756
  1018.1 111.9 %collective-permute-start.3 = (bf16[704,512]{1,0:T(8,128)(2,1)}, bf16[704,512]{1,0:T(8,128)(2,1)}, u32[]{:S(2)}, u32[]{:S(2)}) collective-permute-start(bf16[704,512]{1,0:T(8,128)(2,1)} %get-tuple-element.319), channel_id=1, source_target_pairs={{0,3},{1,0},{2,1},{3,2},{4,7},{5,4},{6,5},{7,6},{8,11},{9,8},{10,9... | collective-permute-start | bytes 2162696 | tf_op jit(solution)/shard_map/ppermute | solution.py:1298
  1018.2 111.9 %collective-permute-start.4 = (bf16[704,512]{1,0:T(8,128)(2,1)}, bf16[704,512]{1,0:T(8,128)(2,1)}, u32[]{:S(2)}, u32[]{:S(2)}) collective-permute-start(bf16[704,512]{1,0:T(8,128)(2,1)} %get-tuple-element.318), channel_id=1, source_target_pairs={{0,2},{1,3},{2,0},{3,1},{4,6},{5,7},{6,4},{7,5},{8,10},{9,11},{10,... | collective-permute-start | bytes 2162696 | tf_op jit(solution)/shard_map/ppermute | solution.py:1298
  1091.8 22.2 %copy-start.29 = (f32[256,2,128]{0,2,1:T(8,128)S(1)}, f32[256,2,128]{0,2,1:T(8,128)}, u32[]{:S(2)}) copy-start(f32[256,2,128]{0,2,1:T(8,128)} %copy.260) | copy-start | bytes 786436
  1091.8 24.0 %copy-start.55 = (f32[3,64]{1,0:T(4,128)S(1)}, f32[3,64]{1,0:T(4,128)}, u32[]{:S(2)}) copy-start(f32[3,64]{1,0:T(4,128)} %param.33) | copy-start | bytes 2308
  1091.8 24.0 %copy-start.66 = (f32[3,64]{1,0:T(4,128)S(1)}, f32[3,64]{1,0:T(4,128)}, u32[]{:S(2)}) copy-start(f32[3,64]{1,0:T(4,128)} %param.34) | copy-start | bytes 2308
  1091.8 24.0 %copy-start.67 = (f32[3,64]{1,0:T(4,128)S(1)}, f32[3,64]{1,0:T(4,128)}, u32[]{:S(2)}) copy-start(f32[3,64]{1,0:T(4,128)} %param.35) | copy-start | bytes 2308
  1114.0 5.3 copy-start.15
  1121.1 33.9 %collective-permute-start.5 = (bf16[704,512]{1,0:T(8,128)(2,1)}, bf16[704,512]{1,0:T(8,128)(2,1)S(1)}, u32[]{:S(2)}, u32[]{:S(2)}) collective-permute-start(bf16[704,512]{1,0:T(8,128)(2,1)} %get-tuple-element.317), channel_id=1, source_target_pairs={{0,1},{1,2},{2,3},{3,0},{4,5},{5,6},{6,7},{7,4},{8,9},{9,10},{10,1... | collective-permute-start | bytes 2162696 | tf_op jit(solution)/shard_map/ppermute | solution.py:1298
  (28 other events, 60.4 us)
Sparse Core Ops, SparseCore 0:
  11.4 55.0 all-gather.3
  71.8 157.9 all-gather.5
  239.0 124.2 all-gather.7
  843.6 24.8 reduce-scatter.1

commit v5 on v4

--- a/solution.py
+++ b/solution.py
@@ -179,7 +179,7 @@
     return task
 
 
-def gather_wide(values):
+def gather_wide(values, patience=1):
     count = lax.axis_size("wide")
     chips = count // 2
 
@@ -195,7 +195,8 @@
             first.append(copy)
         keep = pltpu.make_async_copy(x_ref, out_ref.at[me], local)
         keep.start()
-        yield
+        for turn in range(patience):
+            yield
         second = []
         for step in range(1, chips):
             source = lax.rem(me - 2 * step + count, count)
@@ -220,7 +221,7 @@
     )
 
 
-def trade(axis, values, source_of, target_of, shape):
+def trade(axis, values, source_of, target_of, shape, patience=2):
     count = lax.axis_size(axis)
 
     def steps(ins, outs, scratch):
@@ -240,8 +241,8 @@
             copies.append(copy)
         keep = pltpu.make_async_copy(source_of(x_ref, me), target_of(out_ref, me), local)
         keep.start()
-        yield
-        yield
+        for turn in range(patience):
+            yield
         for step in range(1, count):
             source = lax.rem(me - step + count, count)
             arrived(
@@ -279,11 +280,13 @@
 
 def turned(ref, spot):
     count = lax.axis_size("narrow")
-    return ref.at[lax.rem(spot + count - lax.rem(lax.axis_index("wide"), 2), count)]
-
-
-def swap_turned(values):
-    return trade("narrow", values, turned, block_at, values.shape)
+    matrix = lax.rem(spot + count - lax.rem(lax.axis_index("wide"), 2), count)
+    return ref.at[jnp.minimum(matrix, 3)]
+
+
+def swap_turned(values, patience=2):
+    shape = (lax.axis_size("narrow"),) + values.shape[1:]
+    return trade("narrow", values, turned, block_at, shape, patience)
 
 
 def send_owner(values):
@@ -338,10 +341,10 @@
     return trade(axis, values, whole_at, block_at, shape)
 
 
-def split_columns(axis, values):
+def split_columns(axis, values, patience=2):
     count = lax.axis_size(axis)
     rows, size = values.shape[0], values.shape[1] // count
-    return trade(axis, values, columns_of(size), block_at, (count, rows, size))
+    return trade(axis, values, columns_of(size), block_at, (count, rows, size), patience)
 
 
 def join_columns(axis, values):
@@ -1005,8 +1008,8 @@
     )(grad, weight, gate, up, hidden)
 
 
-def newton_steps(current, low, gram, rest_low):
-    rows, width = current.shape
+def newton_steps(problems):
+    rows, width = problems[0][0].shape
     block = min(512, width)
     eye = lax.broadcasted_iota(jnp.int32, (rows, rows), 0) == lax.broadcasted_iota(
         jnp.int32, (rows, rows), 1
@@ -1018,46 +1021,54 @@
     def over(function, start):
         return lax.fori_loop(0, width // block, function, start)
 
-    def add_squares(part, total):
-        values = current[:, strip(part)]
-        return total + jnp.sum(values * values)
-
-    scale = 1.0 / (jnp.sqrt(over(add_squares, jnp.float32(0.0))) + 1e-07)
+    def add_squares(part, totals):
+        values = [current[:, strip(part)] for current, low, gram, rest in problems]
+        return [total + jnp.sum(value * value) for total, value in zip(totals, values)]
+
+    totals = over(add_squares, [jnp.float32(0.0)] * len(problems))
+    scales = [1.0 / (jnp.sqrt(total) + 1e-07) for total in totals]
 
     def begin(part, carry):
-        values = current[:, strip(part)] * scale
-        current[:, strip(part)] = values
-        low[:, strip(part)] = values.astype(LOW)
-        return carry
-
-    over(begin, 0)
-
-    def iteration(turn, carry):
-        gram[...] = jnp.zeros_like(gram)
-
-        def add_gram(part, carry):
-            values = low[:, strip(part)]
-            gram[...] = gram[...] + dot(values, values, 1, 1)
-            return carry
-
-        over(add_gram, 0)
-        whole = gram[...]
-        middle = jnp.sum(jnp.where(eye, whole, 0.0)) / rows
-        rest_low[...] = (whole - jnp.where(eye, middle, 0.0)).astype(LOW)
-        square = dot(rest_low[...], rest_low[...], 1, 0)
-        whole = gram[...]
-        rest = whole - jnp.where(eye, middle, 0.0)
-        square = square + 2.0 * middle * rest + jnp.where(eye, middle * middle, 0.0)
-        whole = NEWTON_B * whole + NEWTON_C * square
-        second = jnp.sum(jnp.where(eye, whole, 0.0)) / rows
-        rest_low[...] = (whole - jnp.where(eye, second, 0.0)).astype(LOW)
-
-        def apply(part, carry):
-            values = (NEWTON_A + second) * current[:, strip(part)] + dot(
-                rest_low[...], low[:, strip(part)], 1, 0
-            )
+        for scale, (current, low, gram, rest) in zip(scales, problems):
+            values = current[:, strip(part)] * scale
             current[:, strip(part)] = values
             low[:, strip(part)] = values.astype(LOW)
+        return carry
+
+    over(begin, 0)
+
+    def iteration(turn, carry):
+        for current, low, gram, rest in problems:
+            gram[...] = jnp.zeros_like(gram)
+
+        def add_gram(part, carry):
+            for current, low, gram, rest in problems:
+                values = low[:, strip(part)]
+                gram[...] = gram[...] + dot(values, values, 1, 1)
+            return carry
+
+        over(add_gram, 0)
+        seconds = []
+        for current, low, gram, rest in problems:
+            whole = gram[...]
+            middle = jnp.sum(jnp.where(eye, whole, 0.0)) / rows
+            rest[...] = (whole - jnp.where(eye, middle, 0.0)).astype(LOW)
+            square = dot(rest[...], rest[...], 1, 0)
+            whole = gram[...]
+            centred = whole - jnp.where(eye, middle, 0.0)
+            square = square + 2.0 * middle * centred + jnp.where(eye, middle * middle, 0.0)
+            whole = NEWTON_B * whole + NEWTON_C * square
+            second = jnp.sum(jnp.where(eye, whole, 0.0)) / rows
+            rest[...] = (whole - jnp.where(eye, second, 0.0)).astype(LOW)
+            seconds.append(second)
+
+        def apply(part, carry):
+            for second, (current, low, gram, rest) in zip(seconds, problems):
+                values = (NEWTON_A + second) * current[:, strip(part)] + dot(
+                    rest[...], low[:, strip(part)], 1, 0
+                )
+                current[:, strip(part)] = values
+                low[:, strip(part)] = values.astype(LOW)
             return carry
 
         over(apply, 0)
@@ -1083,86 +1094,115 @@
     )
 
 
-def newton_small_body(x_ref, out_ref, current, low, gram, rest_low):
-    current[...] = x_ref[0]
-    newton_steps(current, low, gram, rest_low)
-    out_ref[0] = low[...]
-
-
-def newton_small(blocks):
-    count, rows, width = blocks.shape
-    spec = pl.BlockSpec((1, rows, width), lambda block: (block, 0, 0))
-    return pl.pallas_call(
-        newton_small_body,
-        grid=(count,),
-        in_specs=[spec],
-        out_specs=spec,
-        out_shape=struct(blocks.shape, LOW),
-        scratch_shapes=newton_scratch(rows, width),
-        compiler_params=pltpu.CompilerParams(vmem_limit_bytes=VMEM_BYTES),
-        cost_estimate=newton_cost(count, rows, width),
-        name="newton_small",
-    )(blocks)
-
-
-def newton_body(factor_ref, mom_ref, *refs):
-    parts = mom_ref.shape[0]
-    pieces, (out_ref, current, low, gram, rest_low) = refs[:parts], refs[parts:]
-    me = lax.axis_index("narrow")
-    columns = mom_ref.shape[2]
-    rows = pieces[0].shape[0]
+def newton_body(factor_ref, mom_ref, grad_ref, out_ref, *problem):
+    current, low = problem[:2]
+    parts, rows, columns = mom_ref.shape
+    factor = factor_ref[0]
     for part in range(parts):
-        current[:, part * columns : (part + 1) * columns] = MOMENTUM * mom_ref[part].astype(FULL)
-    factor = factor_ref[0]
-    for step, piece in enumerate(pieces):
-        source = lax.rem(me - step + parts, parts)
-        added = factor * piece[...].astype(FULL)
-        if rows % 8 == 0:
-            spot = pl.ds(pl.multiple_of(source * rows, 8), rows)
-            current[spot, :] = current[spot, :] + added
-            continue
-        for at in range(parts):
-
-            @pl.when(source == at)
-            def _():
-                spot = slice(at * rows, (at + 1) * rows)
-                current[spot, :] = current[spot, :] + added
-
-    newton_steps(current, low, gram, rest_low)
+        spot = slice(part * columns, (part + 1) * columns)
+        current[:, spot] = MOMENTUM * mom_ref[part].astype(FULL) + factor * grad_ref[
+            :, spot
+        ].astype(FULL)
+    newton_steps([problem])
     for part in range(parts):
         out_ref[part] = low[:, part * columns : (part + 1) * columns]
 
 
-def newton(factor, mom, pieces):
+def newton(factor, mom, grad):
     parts, rows, columns = mom.shape
     width = parts * columns
     return pl.pallas_call(
         newton_body,
-        in_specs=[pl.BlockSpec(memory_space=pltpu.SMEM), VMEM] + [VMEM] * parts,
+        in_specs=[pl.BlockSpec(memory_space=pltpu.SMEM), VMEM, VMEM],
         out_specs=VMEM,
         out_shape=struct(mom.shape, LOW),
         scratch_shapes=newton_scratch(rows, width),
         compiler_params=pltpu.CompilerParams(vmem_limit_bytes=VMEM_BYTES),
         cost_estimate=newton_cost(1, rows, width),
         name="newton",
-    )(factor.reshape(1), mom, *pieces)
-
-
-def lookup_body(ids_ref, table_ref, out_ref, low_ref, list_ref, held, rows, sem):
+    )(factor.reshape(1), mom, grad)
+
+
+def newton_small_body(rows, factor_ref, mom_ref, grad_ref, kv_ref, out_ref, *scratch):
+    problems = [scratch[4 * at : 4 * at + 4] for at in range(4)]
+    parts, _, columns = mom_ref.shape
+    piece_rows = 2 * rows // parts
+    kv_columns = kv_ref.shape[2]
+    half = rows // 2
+    factor = factor_ref[0]
+    for part in range(parts):
+        spot = slice(part * columns, (part + 1) * columns)
+        for member in range(2):
+            current = problems[member][0]
+            current[:, spot] = MOMENTUM * mom_ref[
+                part, member * rows : (member + 1) * rows, :
+            ].astype(FULL)
+        for block in range(parts):
+            current = problems[block // (parts // 2)][0]
+            at = block % (parts // 2) * piece_rows
+            piece = grad_ref[part, 0:piece_rows, block * columns : (block + 1) * columns]
+            current[at : at + piece_rows, spot] = (
+                current[at : at + piece_rows, spot] + factor * piece.astype(FULL)
+            )
+        spot = slice(part * kv_columns, (part + 1) * kv_columns)
+        for member in range(2):
+            current = problems[2 + member][0]
+            piece = kv_ref[part, member * rows : (member + 1) * rows, :].astype(FULL)
+            for side in range(2):
+                lane = (2 * member + side) * kv_columns
+                mom = mom_ref[part, 2 * rows : 2 * rows + half, lane : lane + kv_columns]
+                here = slice(side * half, (side + 1) * half)
+                current[here, spot] = MOMENTUM * mom.astype(FULL) + factor * piece[here]
+    newton_steps(problems[:2])
+    newton_steps(problems[2:])
+    out_ref[...] = jnp.zeros_like(out_ref)
+    for part in range(parts):
+        for member in range(2):
+            out_ref[part, member * rows : (member + 1) * rows, :] = problems[member][1][
+                :, part * columns : (part + 1) * columns
+            ]
+            low = problems[2 + member][1]
+            for side in range(2):
+                lane = (2 * member + side) * kv_columns
+                out_ref[part, 2 * rows : 2 * rows + half, lane : lane + kv_columns] = low[
+                    side * half : (side + 1) * half,
+                    part * kv_columns : (part + 1) * kv_columns,
+                ]
+
+
+def newton_small(factor, mom, grad, kv_grad):
+    parts, _, columns = mom.shape
+    rows = kv_grad.shape[1] // 2
+    kv_width = parts * kv_grad.shape[2]
+    return pl.pallas_call(
+        functools.partial(newton_small_body, rows),
+        in_specs=[pl.BlockSpec(memory_space=pltpu.SMEM), VMEM, VMEM, VMEM],
+        out_specs=VMEM,
+        out_shape=struct(mom.shape, LOW),
+        scratch_shapes=newton_scratch(rows, parts * columns) * 2
+        + newton_scratch(rows, kv_width) * 2,
+        compiler_params=pltpu.CompilerParams(vmem_limit_bytes=VMEM_BYTES),
+        cost_estimate=newton_cost(2, rows, parts * columns),
+        name="newton_small",
+    )(factor.reshape(1), mom, grad, kv_grad)
+
+
+def lookup_body(ids_ref, turn_ref, table_ref, out_ref, low_ref, list_ref, held, rows, sem):
     vocab = table_ref.shape[0]
     count = out_ref.shape[0]
     load = pltpu.make_async_copy(table_ref, held, sem)
     load.start()
     rows[...] = jnp.zeros_like(rows)
 
-    def note(group, found):
+    found = turn_ref[count]
+
+    def note(group, carry):
         for member in range(UNROLL):
             at = group * UNROLL + member
-            list_ref[found] = at
-            found = found + (ids_ref[at] < vocab).astype(jnp.int32)
-        return found
-
-    found = lax.fori_loop(0, count // UNROLL, note, jnp.int32(0))
+            list_ref[turn_ref[at]] = at
+        return carry
+
+    lax.fori_loop(0, count // UNROLL, note, 0)
     for member in range(UNROLL):
         list_ref[found + member] = count
     list_ref[count + UNROLL] = found
@@ -1183,9 +1223,19 @@
 def lookup(table, ids):
     vocab, columns = table.shape
     count = ids.shape[0]
+    mine = (ids < vocab).reshape(-1, 128)
+    before = jnp.arange(128)[:, None] < jnp.arange(128)[None, :]
+    in_row = dot(mine.astype(LOW), before.astype(LOW), 1, 0)
+    per_row = jnp.sum(mine.astype(FULL), axis=1)
+    lines = jnp.arange(mine.shape[0])
+    ahead = jnp.sum(jnp.where(lines[:, None] > lines[None, :], per_row[None, :], 0.0), axis=1)
+    found = jnp.sum(per_row).astype(jnp.int32)
+    turns = (in_row + ahead[:, None]).astype(jnp.int32)
+    turns = jnp.where(mine, turns, count + UNROLL + 1).reshape(-1)
+    turns = jnp.concatenate([turns, jnp.full((128,), found)])
     return pl.pallas_call(
         lookup_body,
-        in_specs=[pl.BlockSpec(memory_space=pltpu.SMEM), ANY],
+        in_specs=[pl.BlockSpec(memory_space=pltpu.SMEM)] * 2 + [ANY],
         out_specs=[VMEM, VMEM, pl.BlockSpec(memory_space=pltpu.SMEM)],
         scratch_shapes=[
             pltpu.VMEM((vocab, columns), FULL),
@@ -1202,7 +1252,7 @@
             flops=0, bytes_accessed=vocab * columns * 4 + count * columns * 24, transcendentals=0
         ),
         name="lookup",
-    )(ids, table)
+    )(ids, turns, table)
 
 
 def spread_body(
@@ -1348,21 +1398,26 @@
     ffn_low = jnp.moveaxis(ffn, 1, 0).astype(LOW)
     ffn_cut = ffn_low.reshape(3, narrow_count, ffn_size, ffn_low.shape[2])
     ffn_cut = jnp.moveaxis(ffn_cut, 1, 0).reshape(narrow_count, 3 * ffn_size, -1)
-    proj_own = jnp.concatenate(
-        [attn_qo.reshape(columns, -1), attn_kv.reshape(columns, -1)], axis=1
-    ).astype(LOW)
-    proj_part = lax.all_gather(proj_own, "narrow", axis=0)
+    kv_part = lax.all_gather(attn_kv.reshape(columns, -1).astype(LOW), "narrow", axis=0)
+    kv_part = jnp.moveaxis(kv_part, 0, 1).reshape(columns, -1)
+    proj_own = jnp.concatenate([attn_qo.reshape(columns, -1).astype(LOW), kv_part], axis=1)
+    proj = lax.all_gather(proj_own, "wide", axis=0, tiled=True)
 
     where_at = jnp.arange(seq_len, dtype=jnp.int32)
     pick_tokens = jnp.sum(
         jnp.where(pick_ids[:, None] == where_at[None, :], tokens[0][None, :], 0), axis=1
     )
     ints = box(jnp.concatenate([tokens[0], pick_tokens, targets[0]]))
-    all_ints, all_gains = launch(
-        [gather_wide(ints), gather_both(box(gains.astype(LOW).astype(FULL).reshape(-1)))],
+    all_ints, all_gains, ffn_sub = launch(
+        [
+            gather_wide(ints),
+            gather_both(box(gains.astype(LOW).astype(FULL).reshape(-1))),
+            join_columns("narrow", ffn_cut),
+        ],
         0,
         "gather_ids",
     )
+    ffn_w = lax.all_gather(ffn_sub.reshape(3, ffn_size, width), "wide", axis=0)
     gain_size = gains.shape[1]
     gain_w = all_gains.reshape(narrow_count, wide_count, -1)[:, :, : 3 * gain_size]
     gain_w = gain_w.reshape(narrow_count, wide_count, 3, gain_size)
@@ -1376,81 +1431,52 @@
     inside = (local_ids >= 0) & (local_ids < vocab_rows)
     spots = jnp.where(inside, local_ids, vocab_rows)
     found, embed_low, listed = lookup(embed, spots)
-    proj_part, found = lax.optimization_barrier((proj_part, found))
-    proj = lax.all_gather(proj_part, "wide", axis=1, tiled=True)
     found = found.reshape(narrow_count, wide_count * all_rows, columns)
     embed_cut = embed_low.reshape(wide_count, vocab_rows // wide_count, columns)
-    rows_low, ffn_sub, table_own = launch(
-        [
-            fetch_rows(found, all_rows),
-            join_columns("narrow", ffn_cut),
-            join_columns("wide", embed_cut),
-        ],
-        1,
-        "fetch_rows",
-    )
-    ffn_w = lax.all_gather(ffn_sub.reshape(3, ffn_size, width), "wide", axis=0)
+    rows_low, table_own = launch(
+        [fetch_rows(found, all_rows), join_columns("wide", embed_cut)], 1, "fetch_rows"
+    )
 
     mom_qo = jnp.moveaxis(attn_qo_mom, 1, 0)
     mom_kv = jnp.moveaxis(attn_kv_mom, 1, 0)
     mom_ffn = jnp.moveaxis(ffn_mom, 1, 0)
     slot_rows, slot_cols = mom_ffn.shape[1:]
 
-    def pack_small(qo_part, kv_part):
-        flat = jnp.concatenate([qo_part.reshape(-1), kv_part.reshape(-1)])
-        return jnp.pad(flat, (0, slot_rows * slot_cols - flat.shape[0])).reshape(
-            slot_rows, slot_cols
-        )
-
-    def unpack_small(box_values):
-        lead = box_values.shape[:-2]
-        flat = box_values.reshape(lead + (-1,))
-        qo_size, kv_size = mom_qo.size, mom_kv.size
-        return (
-            flat[..., :qo_size].reshape(lead + mom_qo.shape),
-            flat[..., qo_size : qo_size + kv_size].reshape(lead + mom_kv.shape),
-        )
-
-    mom_parts = [mom_ffn[0], mom_ffn[1], mom_ffn[2], pack_small(mom_qo, mom_kv)]
-    mom_parts = mom_parts + [jnp.zeros_like(mom_parts[0])] * (narrow_count - 4)
-    mom_parts = jnp.stack(mom_parts).astype(LOW)
+    block_rows, q_size = mom_qo.shape[1:]
+    kv_size = mom_kv.shape[2]
+    half_rows = block_rows // 2
+    kv_box = jnp.moveaxis(mom_kv.reshape(4, half_rows, kv_size), 0, 1).reshape(half_rows, -1)
+    small_box = jnp.concatenate([mom_qo.reshape(2 * block_rows, q_size), kv_box])
+    small_box = jnp.pad(small_box, ((0, slot_rows - small_box.shape[0]), (0, 0)))
+    mom_parts = jnp.concatenate([mom_ffn, small_box[None]]).astype(LOW)
 
     seg_all = segments_at(lens, where_at)
     tok_at = narrow_spot * tok_rows + jnp.arange(tok_rows, dtype=jnp.int32)
-    own_at = lax.dynamic_slice_in_dim(pick_ids, narrow_spot * own_rows, own_rows, 0)
     _, cosine_all, sine_all = angles_at(lens, where_at)
     _, cosine_tok, sine_tok = angles_at(lens, tok_at)
-    _, cosine_own, sine_own = angles_at(lens, own_at)
     seg_mine, cosine, sine = angles_at(lens, pick_ids)
 
-    q_w, o_w = proj[:, :, :head_cols], proj[:, :, head_cols : 2 * head_cols]
-    kv_size = attn_kv.shape[2]
-    k_w = proj[:, :, 2 * head_cols : 2 * head_cols + kv_size]
-    v_w = proj[:, :, 2 * head_cols + kv_size :]
-
-    def each_owner(rows, weight):
-        return jnp.einsum("td,ndf->ntf", rows, weight, preferred_element_type=FULL)
-
-    def by_heads(parts):
-        return jnp.moveaxis(parts, 0, 1).reshape(tok_rows, KVH, HD)
+    q_w, o_w, kv_w = (
+        proj[:, :head_cols],
+        proj[:, head_cols : 2 * head_cols],
+        proj[:, 2 * head_cols :],
+    )
 
     rows_full = rows_low.astype(FULL)
     normed_all = norm_rows(rows_full, gain_w[0]).astype(LOW)
     normed_tok, normed_own = normed_all[:tok_rows], normed_all[tok_rows:]
-    keys_part = by_heads(each_owner(normed_tok, k_w))
-    keys_part = rotate(keys_part, cosine_tok[:, None], sine_tok[:, None]).astype(LOW)
-    values_part = by_heads(each_owner(normed_tok, v_w)).astype(LOW)
+    kv_part = dot(normed_tok, kv_w, 1, 0).reshape(tok_rows, narrow_count, 2, kv_size)
+    kv_part = jnp.moveaxis(kv_part, 2, 0).reshape(2, tok_rows, KVH, HD)
+    keys_part = rotate(kv_part[0], cosine_tok[:, None], sine_tok[:, None]).astype(LOW)
+    values_part = kv_part[1].astype(LOW)
     by_head = jnp.moveaxis(jnp.stack([keys_part, values_part]), 2, 0)
     by_head = jnp.repeat(by_head, repeat, axis=0)
     by_head = by_head.reshape(narrow_count, groups, 2, tok_rows, HD)
-    queries_part = each_owner(normed_own, q_w).reshape(narrow_count, own_rows, heads_own, HD)
-    queries_part = rotate(queries_part, cosine_own[:, None], sine_own[:, None])
-    queries_part = queries_part.astype(LOW).reshape(narrow_count, own_rows, head_cols)
-    own_head, queries, start_low = launch(
+    own_head, start_low, tok_cols = launch(
         [
             swap_blocks("narrow", by_head),
-            swap_blocks("narrow", queries_part),
             gather_blocks("narrow", rows_low[tok_rows:]),
+            split_columns("wide", normed_tok),
         ],
         2,
         "trade_heads",
@@ -1459,6 +1485,9 @@
     keys, values = own_head[0], own_head[1]
     start_h = start_low.reshape(sel, width).astype(FULL)
 
+    normed = norm_rows(start_h, gain_w[0]).astype(LOW)
+    queries = dot(normed, q_w, 1, 0).reshape(sel, heads_own, HD)
+    queries = rotate(queries, cosine[:, None], sine[:, None]).astype(LOW)
     grouped = queries.reshape(sel, groups, heads_own // groups, HD)
     scale = HD ** (-0.5)
     scores = jnp.einsum("tkgd,ksd->kgts", grouped, keys, preferred_element_type=FULL) * scale
@@ -1471,31 +1500,29 @@
     mixed = mixed.reshape(sel, head_cols).astype(LOW)
 
     early_part = norm_rows(start_h, gain_w[2]).astype(LOW)
-    mixed_all, early, mixed_wide = launch(
+    early = lax.all_gather(early_part, "wide", axis=0, tiled=True)
+    start_own = lax.dynamic_slice_in_dim(start_h, narrow_spot * own_rows, own_rows, 0)
+    middle, inner, mixed_wide, pick_cols = launch(
         [
-            gather_blocks("narrow", mixed),
-            gather_wide(early_part),
+            settle(
+                dot(mixed, o_w, 1, 1).astype(LOW),
+                start_own,
+                start_own,
+                jnp.ones((1, width), FULL),
+                gain_w[1:2],
+            ),
             gather_wide(mixed),
+            split_columns("wide", normed),
         ],
         3,
-        "gather_mixed",
-    )
-    early = early.reshape(total_rows, width)
-
-    def own(values_all):
-        return lax.dynamic_slice_in_dim(values_all, narrow_spot * own_rows, own_rows, 0)
-
-    start_own = own(start_h)
-    middle_all = start_h + jnp.einsum(
-        "ntf,ndf->td", mixed_all, o_w, preferred_element_type=FULL
-    )
-    middle = own(middle_all)
-    inner = norm_rows(middle_all, gain_w[1]).astype(LOW)
+        "settle_middle",
+    )
+    inner = inner.reshape(sel, width)
+    inner_all = lax.all_gather(inner, "wide", axis=0, tiled=True)
     gate, up, hidden, fed = feed(inner, ffn_w)
-    final_own, late_part, inner_all = launch(
-        [settle(fed, middle, start_own, keep_row, gain_w[2:3]), gather_wide(inner)], 4, "settle"
-    )
-    inner_all = inner_all.reshape(total_rows, width)
+    final_own, late_part = launch(
+        [settle(fed, middle, start_own, keep_row, gain_w[2:3])], 4, "settle_late"
+    )
 
     table_count = table_own.shape[0]
     local_target = targets_all - (narrow_spot * vocab_rows + wide_spot * table_count)
@@ -1523,16 +1550,8 @@
     early_logits, early_stats = exit_logits(early)
     late_logits, late_stats = exit_logits(late)
     stats = jnp.concatenate([early_stats, late_stats], axis=1).reshape(3, 8, -1)
-    normed_picks = norm_rows(start_h, gain_w[0]).astype(LOW)
-    stats, tok_cols, pick_cols = launch(
-        [
-            combine(stats, merge_stats),
-            split_columns("wide", normed_tok),
-            split_columns("wide", normed_picks),
-        ],
-        6,
-        "combine_stats",
-    )
+    stats = launch([combine(stats, merge_stats)], 6, "combine_stats")[0]
+    stats, inner_all = lax.optimization_barrier((stats, inner_all))
     stats = stats.reshape(3, -1)
     log_norms = stats[0] + jnp.log(stats[1])
     losses = log_norms - stats[2]
@@ -1555,9 +1574,9 @@
     mom_owned = jnp.concatenate([mom_top, mom_low], axis=1)
     grad_head = (early_head + late_head).astype(LOW)
 
-    grad_early, grad_final, gain_late, grad_out = launch(
+    grad_early = lax.psum_scatter(early_back, "wide", scatter_dimension=0, tiled=True)
+    grad_final, gain_late, grad_out = launch(
         [
-            sum_wide(early_back),
             settle_back(
                 grad_late.astype(LOW),
                 final_own,
@@ -1567,24 +1586,19 @@
             ),
         ],
         8,
-        "settle_late",
+        "back_late",
     )
     grad_layer = grad_final * keep_layer
     grad_out = grad_out.reshape(sel, width)
+    out_all = lax.all_gather(grad_out, "wide", axis=0, tiled=True)
     acts, fed_back = feed_back(grad_out, ffn_w, gate, up, hidden)
-    grad_mid, gain_mid, grad_branch, out_all = launch(
-        [
-            settle_back(fed_back, middle, grad_layer, keep_row, gain_w[1:2]),
-            gather_wide(grad_out),
-        ],
-        9,
-        "settle_middle",
-    )
+    grad_mid, gain_mid, grad_branch = launch(
+        [settle_back(fed_back, middle, grad_layer, keep_row, gain_w[1:2])], 9, "back_middle"
+    )
+    grad_branch, grad_early = lax.optimization_barrier((grad_branch, grad_early))
     grad_branch = grad_branch.reshape(sel, width)
-    out_all = out_all.reshape(total_rows, width)
-
-    o_own = lax.dynamic_slice(proj, (narrow_spot, 0, head_cols), (1, width, head_cols))[0]
-    grad_mixed = dot(grad_branch, o_own, 1, 0).astype(LOW)
+
+    grad_mixed = dot(grad_branch, o_w, 1, 0).astype(LOW)
     grouped_grad = grad_mixed.reshape(sel, groups, heads_own // groups, HD)
     grad_probs = jnp.einsum("tkgd,ksd->kgts", grouped_grad, values, preferred_element_type=FULL)
     grad_scores = (
@@ -1607,11 +1621,12 @@
         2, groups, narrow_count, tok_rows, HD
     )
     kv_parts = jnp.transpose(kv_parts, (2, 1, 0, 3, 4))
-    grad_kv, grad_q, grad_early, acts, queries_wide, branch_cols = launch(
+    pick_part = dot(grad_queries, q_w, 1, 1).astype(LOW)
+    grad_kv, grad_pick, grad_early, acts, queries_wide, branch_cols = launch(
         [
             swap_blocks("narrow", kv_parts),
-            swap_blocks("narrow", grad_queries.reshape(narrow_count, own_rows, head_cols)),
-            sum_narrow(grad_early.astype(LOW)),
+            sum_narrow(pick_part),
+            sum_narrow(grad_early),
             swap_blocks("wide", acts),
             gather_wide(grad_queries),
             split_columns("wide", grad_branch),
@@ -1625,29 +1640,12 @@
         grad_kv = jnp.sum(grad_kv.astype(FULL), axis=1, keepdims=True).astype(LOW)
     grad_kv = grad_kv[:, 0]
     kv_rows = jnp.transpose(grad_kv, (1, 2, 0, 3)).reshape(2, tok_rows, narrow_count, kv_size)
-
-    def from_owners(parts, weight):
-        return jnp.einsum("tnf,ndf->td", parts, weight, preferred_element_type=FULL)
-
-    grad_normed = jnp.concatenate(
-        [
-            from_owners(kv_rows[0], k_w) + from_owners(kv_rows[1], v_w),
-            jnp.einsum("ntf,ndf->td", grad_q, q_w, preferred_element_type=FULL),
-        ]
-    )
+    kv_rows = jnp.moveaxis(kv_rows, 0, 2).reshape(tok_rows, -1)
+    grad_kv, out_all = lax.optimization_barrier((kv_rows, out_all))
+    grad_normed = jnp.concatenate([dot(grad_kv, kv_w, 1, 1), grad_pick])
     grad_rows, gain_attn = norm_back(rows_full, gain_w[0], grad_normed)
     grad_pass = grad_mid + grad_start_exit + grad_final * (1.0 - keep_layer)
     grad_rows = jnp.concatenate([grad_rows[:tok_rows], grad_rows[tok_rows:] + grad_pass])
-    grad_kv_flat = kv_rows.reshape(2 * tok_rows, narrow_count * kv_size)
-    grad_rows, head_cols_all, kv_wide = launch(
-        [
-            return_rows(grad_rows.astype(LOW)),
-            later(split_columns("wide", grad_head), 2),
-            later(gather_wide(grad_kv_flat), 2),
-        ],
-        11,
-        "return_rows",
-    )
     acts = jnp.moveaxis(acts, 1, 0).reshape(3, total_rows, ffn_size)
     rights = (inner_all, inner_all, out_all)
     grad_ffn = [dot(acts[j], rights[j], 0, 0) for j in range(3)]
@@ -1658,27 +1656,26 @@
             jnp.einsum("wtc,wtf->cf", branch_cols, mixed_wide, preferred_element_type=FULL),
         ]
     )
-    qo_flat = summed_qo.astype(LOW).reshape(-1)
-    qo_flat = jnp.pad(qo_flat, (0, ffn_size * width - qo_flat.shape[0]))
-    for_owners = jnp.stack(
-        [part.astype(LOW) for part in grad_ffn] + [qo_flat.reshape(ffn_size, width)]
-    )
-    for_owners, grad_rows = lax.optimization_barrier((for_owners, grad_rows))
+    qo_box = summed_qo.astype(LOW).reshape(narrow_count, -1, q_size)
+    qo_box = jnp.moveaxis(qo_box, 0, 1).reshape(-1, width)
+    qo_box = jnp.pad(qo_box, ((0, ffn_size - qo_box.shape[0]), (0, 0)))
+    for_owners = jnp.stack([part.astype(LOW) for part in grad_ffn] + [qo_box])
+    grad_rows, owned, kv_wide, head_cols_all = launch(
+        [
+            return_rows(grad_rows.astype(LOW)),
+            swap_turned(for_owners, 5),
+            later(gather_wide(grad_kv, 3), 2),
+            later(split_columns("wide", grad_head, 3), 2),
+        ],
+        11,
+        "return_rows",
+    )
     turn = lax.rem(wide_spot, 2)
-
-    def for_device(spot):
-        matrix = lax.rem(spot + narrow_count - turn, narrow_count)
-        return lax.dynamic_index_in_dim(for_owners, jnp.minimum(matrix, 3), 0, False)
-
-    owned = [for_device(narrow_spot)] + [
-        shifted(for_device(lax.rem(narrow_spot + step, narrow_count)), "narrow", step)
-        for step in range(1, narrow_count)
-    ]
-    kv_wide = kv_wide.reshape(wide_count, 2, tok_rows, narrow_count * kv_size)
     grad_kv_w = jnp.einsum(
-        "wtc,wjtf->jcf", tok_cols, kv_wide, preferred_element_type=FULL
-    )
-    summed_kv = lax.psum_scatter(grad_kv_w, "narrow", scatter_dimension=2, tiled=True)
+        "wtc,wtf->cf", tok_cols, kv_wide, preferred_element_type=FULL
+    ).reshape(columns, narrow_count, 2, kv_size)
+    grad_kv_w = jnp.moveaxis(grad_kv_w, 0, 2)
+    summed_kv = lax.psum_scatter(grad_kv_w, "narrow", scatter_dimension=0, tiled=True)[0]
     summed_table, table_squares = spread(
         spots, listed, grad_rows.reshape(-1, columns), head_cols_all.reshape(vocab_rows, columns)
     )
@@ -1695,7 +1692,7 @@
     sums, kv_owned = launch(
         [
             combine(sums.reshape(4, 8, -1), add_two),
-            send_owner(summed_kv.astype(LOW).reshape(-1, lanes)),
+            send_owner(summed_kv.astype(LOW).reshape(2 * block_rows, kv_size)),
         ],
         12,
         "combine_sums",
@@ -1707,11 +1704,6 @@
     square_total = sums[3, 0] + jnp.sum(sums[:3] * sums[:3])
     grad_norm = jnp.sqrt(square_total) / loss_count
     factor = jnp.minimum(1.0, CLIP_NORM / (grad_norm + 1e-06)) / loss_count
-
-    def whole_columns(parts):
-        return jnp.moveaxis(parts, 0, 2).reshape(
-            parts.shape[1], parts.shape[2], parts.shape[0] * parts.shape[3]
-        )
 
     final_parts, factor = lax.optimization_barrier((for_owners[:3], factor))
     size = width // narrow_count
@@ -1729,29 +1721,10 @@
     summed_ffn = summed_ffn.reshape(3, ffn_rows, size).astype(FULL)
 
     def ffn_owner():
-        return newton(factor, mom_owned, owned)
+        return newton(factor, mom_owned, owned.reshape(ffn_rows, width))
 
     def small_owner():
-        mom_q, mom_k = unpack_small(mom_owned.astype(FULL))
-        order = lax.rem(
-            narrow_spot - jnp.arange(narrow_count, dtype=jnp.int32) + narrow_count, narrow_count
-        )
-        grad_q = jnp.stack(owned).reshape(narrow_count, -1)[:, : mom_qo.size]
-        grad_q = jnp.take(grad_q, order, axis=0).reshape((narrow_count,) + mom_qo.shape)
-        grad_k = kv_owned.reshape((narrow_count,) + mom_kv.shape)
-        results = [
-            newton_small(whole_columns(MOMENTUM * mom + grad.astype(FULL) * factor))
-            for mom, grad in ((mom_q, grad_q), (mom_k, grad_k))
-        ]
-        parts = [
-            jnp.moveaxis(
-                result.reshape(2, result.shape[1], narrow_count, -1), 2, 0
-            ).reshape(narrow_count, -1)
-            for result in results
-        ]
-        flat = jnp.concatenate(parts, axis=1)
-        flat = jnp.pad(flat, ((0, 0), (0, slot_rows * slot_cols - flat.shape[1])))
-        return flat.reshape(narrow_count, slot_rows, slot_cols)
+        return newton_small(factor, mom_owned, owned, kv_owned)
 
     small_spot = lax.rem(3 + turn, narrow_count)
     directions = lax.cond(narrow_spot == small_spot, small_owner, ffn_owner)
@@ -1774,7 +1747,10 @@
         return result
 
     dir_ffn = jnp.stack([direction_of(matrix) for matrix in range(3)]).astype(FULL)
-    dir_qo, dir_kv = unpack_small(direction_of(3).astype(FULL))
+    small = direction_of(3).astype(FULL)
+    dir_qo = small[: 2 * block_rows].reshape(mom_qo.shape)
+    dir_kv = small[2 * block_rows : 2 * block_rows + half_rows].reshape(half_rows, 4, kv_size)
+    dir_kv = jnp.moveaxis(dir_kv, 1, 0).reshape(mom_kv.shape)
 
     embed_new, embed_m_new, embed_v_new = adamw(
         embed, embed_m, embed_v, summed_table * factor, RATE_ADAM, WEIGHT_DECAY

time: 1180 us -> 1200 us (1.017)
  waiting for transfers between devices: 25.1 us -> 146 us
  starting transfers between devices: 87.9 us -> 7.52 us
  Pallas kernels: 782 us -> 748 us
  blocking collectives: 0 us -> 12.8 us
    ppermute x9 -> x6, starting transfers between devices: 87.5 us -> 6.34 us  [shifted(): return lax.ppermute(parts, axis, pairs)]
    all_gather x1, waiting for transfers between devices: 0.01 us -> 78 us  [per_device(): ffn_w = lax.all_gather(ffn_sub.reshape(3, ffn_size, width), 'wide', axis=0)]
    ppermute x9 -> x6, waiting for transfers between devices: 25 us -> 66.8 us  [shifted(): return lax.ppermute(parts, axis, pairs)]
    pallas_call x13, Pallas kernels: 650 us -> 625 us  [launch(): pl.pallas_call(body, out_shape=outputs, in_specs=[place for task in tasks...]
    dot_general x7 -> x1, matrix products: 25.1 us -> 3.46 us  [per_device(): jnp.einsum('wtc,wtf->cf', tok_cols, kv_wide, preferred_element_type=FULL)]
    dot_general x10 -> x16, matrix products: 60.3 us -> 78.1 us  [dot(): lax.dot_general(first, second, (((first_dim,), (second_dim,)), ((), ())),...]
    all_gather x0 -> x1, blocking collectives: none -> 12.8 us  [per_device(): lax.all_gather(attn_kv.reshape(columns, -1).astype(LOW), 'narrow', axis=0)]
    unnamed x174 -> x190, local copies, waits for them, and re-layouts: 17.6 us -> 27.4 us
  transfers between devices with their start and end apart: 13 -> 13, of which waited for: 1 -> 4; matrix products, arithmetic and copies ran while one was open for 11% -> 14% of each run, Pallas kernels for 35% -> 42%
where the time goes in v5:
time: 1200 us; the launch traced here: 1190 us
  Pallas kernels  748 us (62%)
  waiting for transfers between devices  146 us (12%)
  other arithmetic  92.8 us (8%)
  matrix products  88.6 us (7%)
  local copies, waits for them, and re-layouts  67.8 us (6%)
  between operations  25.5 us (2%)
  blocking collectives  12.8 us (1%)
    pallas_call x13, Pallas kernels, launch(): pl.pallas_call(body, out_shape=outputs, in_specs=[place for task in tasks...  625 us
    dot_general x16, matrix products, dot(): lax.dot_general(first, second, (((first_dim,), (second_dim,)), ((), ())),...  78.1 us
    all_gather x1, waiting for transfers between devices, per_device(): ffn_w = lax.all_gather(ffn_sub.reshape(3, ffn_size, width), 'wide', axis=0)  78 us
    ppermute x6, waiting for transfers between devices, shifted(): return lax.ppermute(parts, axis, pairs)  66.8 us
    pallas_call x1, Pallas kernels, newton(): pl.pallas_call(newton_body, in_specs=[pl.BlockSpec(memory_space=pltpu.SME...  45.1 us
    pallas_call x1, Pallas kernels, lookup(): pl.pallas_call(lookup_body, in_specs=[pl.BlockSpec(memory_space=pltpu.SME...  28.5 us
    unnamed x190, local copies, waits for them, and re-layouts  27.4 us
  transfers between devices with their start and end apart: 13, of which 4 were waited for; matrix products, arithmetic and copies ran while one was open for 14% of the time, Pallas kernels for 42%

profile of v5, /device:TPU:17, one launch (start us, length us, event | category | flops | bytes accessed | tf_op | source)
XLA Modules:
  0.0 1188.6 jit_solution(13401066966566552970)
XLA Ops:
  8.5 12.8 %all_gather.19 = bf16[4,256,256]{2,1,0:T(8,128)(2,1)S(1)} all-gather(bf16[1,256,256]{2,1,0:T(8,128)(2,1)S(1)} %convert_element_type.253), channel_id=1, replica_groups=mesh['wide'=8,'narrow'=4] {'narrow'}, dimensions={0}, use_global_device_ids=true | all-gather | bytes 655360 | tf_op jit(solution)/shard_map/all_gather | solution.py:1401
  23.6 2.5 convert_element_type.242
  29.1 57.4 %gather_ids.1 = (s32[8,16,128]{2,1,0:T(8,128)}, f32[4,8,8,128]{3,2,1,0:T(8,128)}, bf16[528,2048]{1,0:T(8,128)(2,1)}) custom-call(s32[16,128]{1,0:T(8,128)} %pad_bitcast_fusion.1.refs_0_, f32[8,128]{1,0:T(8,128)} %bitcast_convert_fusion.refs_1_, bf16[4,528,512]{2,1,0:T(8,128)(2,1)} %bitcast.348), custom_call_target="tpu_custom_call" | custom-call | bytes 36274176 | tf_op jit(solution)/shard_map/gather_ids/pallas_call | solution.py:156
  92.5 28.5 %lookup.1 = (bf16[9216,256]{1,0:T(8,128)(2,1)}, bf16[8192,256]{1,0:T(8,128)(2,1)}, s32[9248]{0:T(1024)}) custom-call(s32[9216]{0:T(1024)} %and_select_fusion.ids_ref, s32[9344]{0:T(1024)} %concatenate.82.turn_ref, f32[8192,256]{1,0:T(8,128)} %table_ref.1), custom_call_target="tpu_custom_call" | custom-call | bytes 65011712 | tf_op jit(solution)/shard_map/lookup/pallas_call | solution.py:1236
  121.1 113.1 %fetch_rows.1 = (bf16[288,2048]{1,0:T(8,128)(2,1)}, bf16[1024,2048]{1,0:T(8,128)(2,1)}) custom-call(bf16[4,2304,256]{2,1,0:T(8,128)(2,1)} %bitcast.351, bf16[8,1024,256]{2,1,0:T(8,128)(2,1)} %bitcast.353), custom_call_target="tpu_custom_call" | custom-call | bytes 114294784 | tf_op jit(solution)/shard_map/fetch_rows/pallas_call | solution.py:156
  240.1 3.8 fusion.7
  245.6 30.8 %trade_heads.1 = (bf16[4,1,2,256,128]{4,3,2,1,0:T(8,128)(2,1)}, bf16[4,32,2048]{2,1,0:T(8,128)(2,1)}, bf16[8,256,256]{2,1,0:T(8,128)(2,1)}) custom-call(bf16[4,1,2,256,128]{4,3,2,1,0:T(8,128)(2,1)} %maximum_bitcast_fusion.refs_0_, bf16[32,2048]{1,0:T(8,128)(2,1)} %slice.183.refs_1_, bf16[256,2048]{1,0:T(8,128)(2,1)} %copy-done.11), custom_call_target="tpu_custom_call" | custom-call | bytes 30408704 | tf_op jit(solution)/shard_map/trade_heads/pallas_call | solution.py:156
  277.8 2.3 multiply_convert_fusion.2
  287.7 3.0 convolution_convert_fusion.3
  291.4 30.1 %settle_middle.1 = (f32[32,2048]{1,0:T(8,128)}, bf16[4,32,2048]{2,1,0:T(8,128)(2,1)}, bf16[8,128,512]{2,1,0:T(8,128)(2,1)}, bf16[8,128,256]{2,1,0:T(8,128)(2,1)}) custom-call(bf16[4,32,2048]{2,1,0:T(8,128)(2,1)} %bitcast.372, f32[32,2048]{1,0:T(8,128)} %get-tuple-element.256.refs_1_.refs_2_, f32[32,2048]{1,0:T(8,128)} %get-tuple-element.256.refs_1_.refs_2_, ...), custom_call_target="tpu_custom_call" | custom-call | bytes 32636928 | tf_op jit(solution)/shard_map/settle_middle/pallas_call | solution.py:156
  325.1 2.5 convert_bitcast_fusion
  327.6 1.9 pad_maximum_fusion.3
  330.2 10.3 fusion.108
  340.5 78.0 %all-gather.10.cloned.1.call-done.weight_ref = bf16[8,3,176,2048]{3,2,1,0:T(8,128)(2,1)} async-done(((bf16[1,3,176,2048]{3,2,1,0:T(8,128)(2,1)}), bf16[8,3,176,2048]{3,2,1,0:T(8,128)(2,1)}) %all-gather.10.cloned.1.call-update) | async-done | bytes 17301520 | tf_op jit(solution)/shard_map/all_gather | solution.py:1420
  418.4 13.7 %feed.1 = (f32[8,128,176]{2,1,0:T(8,128)}, f32[8,128,176]{2,1,0:T(8,128)}, bf16[8,128,176]{2,1,0:T(8,128)(2,1)}, bf16[128,2048]{1,0:T(8,128)(2,1)}) custom-call(bf16[128,2048]{1,0:T(8,128)(2,1)} %bitcast.364, bf16[8,3,176,2048]{3,2,1,0:T(8,128)(2,1)} %all-gather.10.cloned.1.call-done.weight_ref), custom_call_target="tpu_custom_call" | custom-call | flops 2214592512 | bytes 17301504 | tf_op jit(solution)/shard_map/feed/pallas_call | solution.py:941
  432.7 26.9 %settle_late.1 = (f32[32,2048]{1,0:T(8,128)}, bf16[4,32,2048]{2,1,0:T(8,128)(2,1)}) custom-call(bf16[4,32,2048]{2,1,0:T(8,128)(2,1)} %bitcast.390, f32[32,2048]{1,0:T(8,128)} %get-tuple-element.105.refs_1_, f32[32,2048]{1,0:T(8,128)} %get-tuple-element.256.refs_1_.refs_2_, f32[1,2048]{1,0:T(1,128)} %broadcast_in_dim.193.refs_3_, f32[1,2048]{1,0:T(1,128)} %slice.193.refs_4_), custom_call_target="tpu_custom_call" | custom-call | bytes 14811136 | tf_op jit(solution)/shard_map/settle_late/pallas_call | solution.py:156
  459.6 34.9 %gather_late.1 = (bf16[8,128,2048]{2,1,0:T(8,128)(2,1)}, bf16[4,352,512]{2,1,0:T(8,128)(2,1)}) custom-call(bf16[128,2048]{1,0:T(8,128)(2,1)} %bitcast.391, bf16[4,352,512]{2,1,0:T(8,128)(2,1)} %get-tuple-element.274.refs_1_), custom_call_target="tpu_custom_call" | custom-call | bytes 60817408 | tf_op jit(solution)/shard_map/gather_late/pallas_call | solution.py:156
  494.6 6.5 fusion.110
  501.1 2.0 exponential_reduce_fusion.1
  503.8 13.7 %combine_stats.1 = f32[3,8,256]{2,1,0:T(8,128)} custom-call(f32[3,8,256]{2,1,0:T(8,128)} %bitcast.409), custom_call_target="tpu_custom_call" | custom-call | bytes 393216 | tf_op jit(solution)/shard_map/combine_stats/pallas_call | solution.py:156
  518.9 10.2 convolution_convert_fusion
  531.0 10.2 convolution_convert_fusion.1
  541.3 44.5 %sum_late.1 = (f32[128,2048]{1,0:T(8,128)}, bf16[4,352,512]{2,1,0:T(8,128)(2,1)}) custom-call(bf16[8,128,2048]{2,1,0:T(8,128)(2,1)} %bitcast.354, bf16[4,352,512]{2,1,0:T(8,128)(2,1)} %get-tuple-element.273.refs_1_), custom_call_target="tpu_custom_call" | custom-call | bytes 65011712 | tf_op jit(solution)/shard_map/sum_late/pallas_call | solution.py:156
  585.8 2.1 convert_element_type.280
  588.6 26.1 %back_late.1 = (f32[32,2048]{1,0:T(8,128)}, f32[1,2048]{1,0:T(1,128)}, bf16[4,32,2048]{2,1,0:T(8,128)(2,1)}) custom-call(bf16[4,32,2048]{2,1,0:T(8,128)(2,1)} %bitcast.365, f32[32,2048]{1,0:T(8,128)} %get-tuple-element.110.refs_1_, f32[32,2048]{1,0:T(8,128)} %broadcast_in_dim.195.refs_2_, f32[1,2048]{1,0:T(1,128)} %broadcast_in_dim.193.refs_3_, ...), custom_call_target="tpu_custom_call" | custom-call | bytes 14876672 | tf_op jit(solution)/shard_map/back_late/pallas_call | solution.py:156
  616.9 14.8 %feed_back.1 = (bf16[8,3,128,176]{3,2,1,0:T(8,128)(2,1)}, bf16[128,2048]{1,0:T(8,128)(2,1)}) custom-call(bf16[128,2048]{1,0:T(8,128)(2,1)} %bitcast.362, bf16[8,3,176,2048]{3,2,1,0:T(8,128)(2,1)} %all-gather.10.cloned.1.call-done.weight_ref, f32[8,128,176]{2,1,0:T(8,128)} %get-tuple-element.112.gate_ref, f32[8,128,176]{2,1,0:T(8,128)} %get-tuple-element.113.up_ref, ...), custom_call_target="tpu_custom_call" | custom-call | flops 2214592512 | bytes 17301504 | tf_op jit(solution)/shard_map/feed_back/pallas_call | solution.py:993
  631.7 29.9 %back_middle.1 = (f32[32,2048]{1,0:T(8,128)}, f32[1,2048]{1,0:T(1,128)}, bf16[4,32,2048]{2,1,0:T(8,128)(2,1)}) custom-call(bf16[4,32,2048]{2,1,0:T(8,128)(2,1)} %bitcast.388, f32[32,2048]{1,0:T(8,128)} %get-tuple-element.105.refs_1_, f32[32,2048]{1,0:T(8,128)} %broadcast_multiply_fusion.refs_2_, f32[1,2048]{1,0:T(1,128)} %broadcast_in_dim.193.refs_3_, ...), custom_call_target="tpu_custom_call" | custom-call | bytes 14876672 | tf_op jit(solution)/shard_map/back_middle/pallas_call | solution.py:156
  661.7 9.2 fusion.93
  670.9 8.6 add_convert_fusion.refs_3_
  679.5 2.5 fusion.30
  683.9 1.9 fusion.60
  685.8 1.7 copy.281
  692.8 2.9 convolution_convert_fusion.2
  695.7 40.4 %trade_grads.1 = (bf16[4,1,2,256,128]{4,3,2,1,0:T(8,128)(2,1)}, f32[32,2048]{1,0:T(8,128)}, f32[32,2048]{1,0:T(8,128)}, bf16[8,3,128,176]{3,2,1,0:T(8,128)(2,1)}...) custom-call(bf16[4,1,2,256,128]{4,3,2,1,0:T(8,128)(2,1)} %maximum_bitcast_fusion.1.refs_0_, ...), custom_call_target="tpu_custom_call" | custom-call | bytes 56098816 | tf_op jit(solution)/shard_map/trade_grads/pallas_call | solution.py:156
  740.4 1.7 convolution_bitcast_fusion.2
  745.2 2.4 multiply_reduce_fusion.3
  747.6 2.0 fusion.112
  749.6 3.7 fusion.5
  757.9 1.8 multiply_reduce_fusion.1
  760.8 1.9 pad_maximum_fusion.refs_1_
  762.8 163.3 %return_rows.1 = (bf16[4,2304,256]{2,1,0:T(8,128)(2,1)}, bf16[4,176,2048]{2,1,0:T(8,128)(2,1)}, bf16[8,256,1024]{2,1,0:T(8,128)(2,1)}, bf16[8,1024,256]{2,1,0:T(8,128)(2,1)}) custom-call(bf16[288,2048]{1,0:T(8,128)(2,1)} %pad_maximum_fusion.4.refs_0_, bf16[4,176,2048]{2,1,0:T(8,128)(2,1)} %pad_maximum_fusion.refs_1_, bf16[256,1024]{1,0:T(8,128)(2,1)} %reshape.810.refs_2_, ...), custom_call_target="tpu_custom_call" | custom-call | bytes 198180864 | tf_op jit(solution)/shard_map/return_rows/pallas_call | solution.py:156
  926.0 3.5 convolution_bitcast_fusion
  931.7 6.0 copy.301
  941.7 20.6 %spread.1 = (f32[8192,256]{1,0:T(8,128)}, f32[8,256]{1,0:T(8,128)}) custom-call(s32[9216]{0:T(1024)} %and_select_fusion.ids_ref, s32[9248]{0:T(1024)} %get-tuple-element.137.list_ref, bf16[9216,256]{1,0:T(8,128)(2,1)} %bitcast.350, bf16[8192,256]{1,0:T(8,128)(2,1)} %bitcast.352), custom_call_target="tpu_custom_call" | custom-call | flops 2359296 | bytes 113246208 | tf_op jit(solution)/shard_map/spread/pallas_call | solution.py:1310
  965.6 1.8 pad_maximum_fusion.2
  967.4 2.3 fusion.106
  972.4 13.9 %combine_sums.1 = (f32[4,8,256]{2,1,0:T(8,128)}, bf16[4,512,128]{2,1,0:T(8,128)(2,1)}) custom-call(f32[4,8,256]{2,1,0:T(8,128)} %maximum_maximum_fusion.1.refs_0_, bf16[512,128]{1,0:T(8,128)(2,1)} %bitcast.386), custom_call_target="tpu_custom_call" | custom-call | bytes 5767168 | tf_op jit(solution)/shard_map/combine_sums/pallas_call | solution.py:156
  991.8 2.6 bitcast_add_fusion.1
  994.4 45.3 %conditional.1 = (bf16[4,704,512]{2,1,0:T(8,128)(2,1)}) conditional(s32[]{:T(128)} %convert_element_type.297, (f32[]{:T(128)}, bf16[4,176,2048]{2,1,0:T(8,128)(2,1)}, bf16[4,704,512]{2,1,0:T(8,128)(2,1)S(1)}) %tuple.98, (f32[]{:T(128)}, bf16[4,704,512]{2,1,0:T(8,128)(2,1)S(1)}, bf16[4,176,2048]{2,1,0:T(8,128)(2,1)}, ...), branch_computations={%region_38.39_spmd, %region_39.40_spmd} | conditional | flops 23789568000 | bytes 8650760 | solution.py:1730
  994.4 45.1 %newton.1 = bf16[4,704,512]{2,1,0:T(8,128)(2,1)} custom-call(f32[1]{0:T(128)} %bitcast.factor_ref, bf16[4,704,512]{2,1,0:T(8,128)(2,1)S(1)} %get-tuple-element.18.mom_ref, bf16[704,2048]{1,0:T(8,128)(2,1)} %bitcast.437), custom_call_target="tpu_custom_call" | custom-call | flops 23789568000 | bytes 8650752 | tf_op jit(solution)/shard_map/cond/branch_0_fun/newton/pallas_call | solution.py:1114
  1039.8 3.4 constant_dynamic-slice_fusion.3
  1043.6 3.5 collective-permute-start.1
  1048.7 2.1 collective-permute-start.5
  1050.8 22.2 %multiply_subtract_fusion = (f32[8192,256]{1,0:T(8,128)}, f32[8192,256]{1,0:T(8,128)}, f32[8192,256]{1,0:T(8,128)}) fusion(f32[8192,256]{1,0:T(8,128)} %table_ref.1, f32[8192,256]{1,0:T(8,128)} %get-tuple-element.142, f32[]{:T(128)} %div.100, f32[8192,256]{1,0:T(8,128)} %param.25, f32[8192,256]{1,0:T(8,128)} %param.26), kind=kLoop, calls=%fused_computation.2 | loop fusion | flops 31457280 | bytes 58720260 | tf_op jit(solution)/shard_map/sub | solution.py:1337
  1073.0 1.8 bitcast_add_fusion.2
  1077.0 2.4 copy.292
  1079.5 1.8 copy.313
  1082.1 45.3 %collective-permute-done.3 = bf16[3,176,512]{2,1,0:T(8,128)(2,1)} collective-permute-done((bf16[3,176,512]{2,1,0:T(8,128)(2,1)}, bf16[3,176,512]{2,1,0:T(8,128)(2,1)}, u32[]{:S(2)}, u32[]{:S(2)}) %collective-permute-start.3) | collective-permute-done | bytes 540704 | tf_op jit(solution)/shard_map/ppermute | solution.py:1348
  1128.6 11.3 collective-permute-done.4
  1141.3 10.2 collective-permute-done.5
  1153.2 3.1 bitcast_add_fusion
  1164.9 1.7 bitcast_subtract_fusion.2
  1168.6 5.7 bitcast_subtract_fusion
  1174.3 5.9 copy.316
  (365 shorter events, 90.0 us)
Async XLA Ops:
  7.2 14.3 %copy-start.8 = (f32[256,2,512]{2,1,0:T(2,128)S(1)}, f32[256,2,512]{2,1,0:T(2,128)}, u32[]{:S(2)}) copy-start(f32[256,2,512]{2,1,0:T(2,128)} %param.27) | copy-start | bytes 3145732
  7.2 232.9 %all-gather.6.cloned.1.call-start = ((), (), s32[]{:S(2)}) async-start(), calls=%async_computation.2 | async-start | bytes 9437184 | tf_op jit(solution)/shard_map/all_gather | solution.py:1404
  23.5 306.7 %all-gather.8.cloned.1.call-start = ((), (), s32[]{:S(2)}) async-start(), calls=%async_computation.3 | async-start | bytes 4718592 | tf_op jit(solution)/shard_map/all_gather | solution.py:1503
  90.0 31.0 %copy-start.47 = (f32[1,8,4,64]{3,2,1,0:T(4,128)}, f32[1,8,4,64]{3,2,1,0:T(4,128)S(1)}, u32[]{:S(2)}) copy-start(f32[1,8,4,64]{3,2,1,0:T(4,128)S(1)} %copy.268) | copy-start | bytes 24580
  121.1 114.7 %copy-start.83 = (s32[1,2]{1,0:T(1,128)S(1)}, s32[1,2]{1,0:T(1,128)}, u32[]{:S(2)}) copy-start(s32[1,2]{1,0:T(1,128)} %param.22) | copy-start | bytes 28
  236.0 46.1 %copy-start.70 = (f32[64]{0:T(128)}, f32[64]{0:T(128)S(1)}, u32[]{:S(2)}) copy-start(f32[64]{0:T(128)S(1)} %multiply_power_fusion) | copy-start | bytes 772
  236.1 45.9 %copy-start.75 = (s32[2]{0:T(128)}, s32[2]{0:T(128)S(1)}, u32[]{:S(2)}) copy-start(s32[2]{0:T(128)S(1)} %fusion.89) | copy-start | bytes 28
  240.0 3.9 copy-start.11
  280.1 138.4 %all-gather.10.cloned.1.call-start = ((), (), s32[]{:S(2)}) async-start(), calls=%async_computation.4 | async-start | bytes 19464192 | tf_op jit(solution)/shard_map/all_gather | solution.py:1420
  280.1 2.9 copy-start.4
  280.8 2.4 slice-start.2
  280.8 236.7 %all-gather.12.cloned.1.call-start = ((), (), s32[]{:S(2)}) async-start(), calls=%async_computation.5 | async-start | bytes 4718592 | tf_op jit(solution)/shard_map/all_gather | solution.py:1521
  287.7 36.8 %copy-start.17 = (f32[256,2,512]{2,1,0:T(2,128)S(1)}, f32[256,2,512]{2,1,0:T(2,128)}, u32[]{:S(2)}) copy-start(f32[256,2,512]{2,1,0:T(2,128)} %param.28) | copy-start | bytes 3145732
  321.5 358.0 %reduce-scatter.3.cloned.1.call-start = ((), (), s32[]{:S(2)}) async-start(), calls=%async_computation.6 | async-start | bytes 4718592 | tf_op jit(solution)/shard_map/reduce_scatter | solution.py:1577
  330.2 199.7 %copy-start.61 = (pred[8,128]{1,0:T(8,128)(4,1)}, pred[8,128]{1,0:T(8,128)(4,1)S(1)}, u32[]{:S(2)}) copy-start(pred[8,128]{1,0:T(8,128)(4,1)S(1)} %get-tuple-element.258) | copy-start | bytes 3076
  418.4 76.1 %copy-start.81 = (bf16[1024,2048]{1,0:T(8,128)(2,1)S(1)}, bf16[1024,2048]{1,0:T(8,128)(2,1)}, u32[]{:S(2)}) copy-start(bf16[1024,2048]{1,0:T(8,128)(2,1)} %get-tuple-element.100) | copy-start | bytes 12582916
  494.5 6.6 copy-start.13
  494.6 6.6 copy-start.59
  529.1 220.5 %all-gather.14.cloned.1.call-start = ((), (), s32[]{:S(2)}) async-start(), calls=%async_computation.7 | async-start | bytes 4718592 | tf_op jit(solution)/shard_map/all_gather | solution.py:1593
  616.4 351.0 %reduce-scatter.5.cloned.1.call-start = ((), (), s32[]{:S(2)}) async-start(), calls=%async_computation.8 | async-start | bytes 1310720 | tf_op jit(solution)/shard_map/reduce_scatter | solution.py:1678
  616.9 44.7 %copy-start.14 = (f32[1024,1024]{0,1:T(8,128)S(1)}, f32[1024,1024]{0,1:T(8,128)}, u32[]{:S(2)}) copy-start(f32[1024,1024]{0,1:T(8,128)} %get-tuple-element.318) | copy-start | bytes 12582916
  661.6 9.2 copy-start.16
  661.6 9.2 copy-start.82
  670.9 8.6 copy-start.40
  679.4 2.5 copy-start.44
  679.4 2.5 copy-start.56
  679.4 2.5 copy-start.68
  695.7 43.2 %copy-start.30 = (bf16[8,128,512]{2,1,0:T(8,128)(2,1)S(1)}, bf16[8,128,512]{2,1,0:T(8,128)(2,1)}, u32[]{:S(2)}) copy-start(bf16[8,128,512]{2,1,0:T(8,128)(2,1)} %get-tuple-element.130) | copy-start | bytes 3145732
  736.1 4.3 copy-start.39
  740.4 2.4 copy-start.1
  740.4 2.4 copy-start.33
  740.4 2.5 copy-start.80
  742.7 2.5 copy-start.10
  749.6 3.7 copy-start
  749.6 3.7 copy-start.51
  749.6 3.7 copy-start.35
  754.8 3.1 copy-start.12
  757.9 2.9 copy-start.22
  762.7 163.3 %copy-start.19 = (bf16[8,256,256]{2,1,0:T(8,128)(2,1)S(1)}, bf16[8,256,256]{2,1,0:T(8,128)(2,1)}, u32[]{:S(2)}) copy-start(bf16[8,256,256]{2,1,0:T(8,128)(2,1)} %get-tuple-element.131) | copy-start | bytes 3145732
  931.6 6.0 copy-start.52
  931.7 6.0 copy-start.66
  931.7 6.1 copy-start.62
  931.7 6.7 copy-start.25
  938.3 2.4 copy-start.63
  991.8 2.7 copy-start.37
  1043.2 113.2 %collective-permute-start = (bf16[704,512]{1,0:T(8,128)(2,1)}, bf16[704,512]{1,0:T(8,128)(2,1)}, u32[]{:S(2)}, u32[]{:S(2)}) collective-permute-start(bf16[704,512]{1,0:T(8,128)(2,1)} %get-tuple-element.272), channel_id=1, source_target_pairs={{0,3},{1,0},{2,1},{3,2},{4,7},{5,4},{6,5},{7,6},{8,11},{9,8},{10,9... | collective-permute-start | bytes 2162696 | tf_op jit(solution)/shard_map/ppermute | solution.py:1348
  1043.6 114.2 %collective-permute-start.1 = (bf16[704,512]{1,0:T(8,128)(2,1)}, bf16[704,512]{1,0:T(8,128)(2,1)}, u32[]{:S(2)}, u32[]{:S(2)}) collective-permute-start(bf16[704,512]{1,0:T(8,128)(2,1)} %get-tuple-element.271), channel_id=1, source_target_pairs={{0,2},{1,3},{2,0},{3,1},{4,6},{5,7},{6,4},{7,5},{8,10},{9,11},{10,... | collective-permute-start | bytes 2162696 | tf_op jit(solution)/shard_map/ppermute | solution.py:1348
  1048.4 79.1 %collective-permute-start.3 = (bf16[3,176,512]{2,1,0:T(8,128)(2,1)}, bf16[3,176,512]{2,1,0:T(8,128)(2,1)}, u32[]{:S(2)}, u32[]{:S(2)}) collective-permute-start(bf16[3,176,512]{2,1,0:T(8,128)(2,1)} %get-tuple-element.277), channel_id=1, source_target_pairs={{0,1},{1,2},{2,3},{3,0},{4,5},{5,6},{6,7},{7,4},{8,9},{9,10},{10,1... | collective-permute-start | bytes 1622024 | tf_op jit(solution)/shard_map/ppermute | solution.py:1348
  1048.4 91.5 %collective-permute-start.4 = (bf16[3,176,512]{2,1,0:T(8,128)(2,1)}, bf16[3,176,512]{2,1,0:T(8,128)(2,1)}, u32[]{:S(2)}, u32[]{:S(2)}) collective-permute-start(bf16[3,176,512]{2,1,0:T(8,128)(2,1)} %get-tuple-element.276), channel_id=1, source_target_pairs={{0,2},{1,3},{2,0},{3,1},{4,6},{5,7},{6,4},{7,5},{8,10},{9,11},{10,... | collective-permute-start | bytes 1622024 | tf_op jit(solution)/shard_map/ppermute | solution.py:1348
  1048.7 102.8 %collective-permute-start.5 = (bf16[3,176,512]{2,1,0:T(8,128)(2,1)}, bf16[3,176,512]{2,1,0:T(8,128)(2,1)}, u32[]{:S(2)}, u32[]{:S(2)}) collective-permute-start(bf16[3,176,512]{2,1,0:T(8,128)(2,1)} %get-tuple-element.275), channel_id=1, source_target_pairs={{0,3},{1,0},{2,1},{3,2},{4,7},{5,4},{6,5},{7,6},{8,11},{9,8},{10,9... | collective-permute-start | bytes 1622024 | tf_op jit(solution)/shard_map/ppermute | solution.py:1348
  1050.8 22.2 %copy-start.32 = (f32[256,2,128]{2,1,0:T(2,128)S(1)}, f32[256,2,128]{2,1,0:T(2,128)}, u32[]{:S(2)}) copy-start(f32[256,2,128]{2,1,0:T(2,128)} %param.30) | copy-start | bytes 786436
  1050.8 24.0 %copy-start.65 = (f32[3,64]{1,0:T(4,128)S(1)}, f32[3,64]{1,0:T(4,128)}, u32[]{:S(2)}) copy-start(f32[3,64]{1,0:T(4,128)} %param.33) | copy-start | bytes 2308
  1050.8 24.0 %copy-start.73 = (f32[3,64]{1,0:T(4,128)S(1)}, f32[3,64]{1,0:T(4,128)}, u32[]{:S(2)}) copy-start(f32[3,64]{1,0:T(4,128)} %param.34) | copy-start | bytes 2308
  1050.8 24.0 %copy-start.74 = (f32[3,64]{1,0:T(4,128)S(1)}, f32[3,64]{1,0:T(4,128)}, u32[]{:S(2)}) copy-start(f32[3,64]{1,0:T(4,128)} %param.35) | copy-start | bytes 2308
  1073.0 6.5 copy-start.18
  1075.6 5.6 copy-start.34
  1077.0 50.4 %copy-start.3 = (bf16[3,4,176,512]{3,2,0,1:T(8,128)(2,1)S(1)}, bf16[3,4,176,512]{3,2,0,1:T(8,128)(2,1)}, u32[]{:S(2)}) copy-start(bf16[3,4,176,512]{3,2,0,1:T(8,128)(2,1)} %copy-done.2) | copy-start | bytes 6488068
  1127.5 31.7 %collective-permute-start.2 = (bf16[704,512]{1,0:T(8,128)(2,1)}, bf16[704,512]{1,0:T(8,128)(2,1)}, u32[]{:S(2)}, u32[]{:S(2)}) collective-permute-start(bf16[704,512]{1,0:T(8,128)(2,1)} %get-tuple-element.270), channel_id=1, source_target_pairs={{0,1},{1,2},{2,3},{3,0},{4,5},{5,6},{6,7},{7,4},{8,9},{9,10},{10,1... | collective-permute-start | bytes 2162696 | tf_op jit(solution)/shard_map/ppermute | solution.py:1348
  1139.9 13.3 %slice-start = ((s8[4325376]{0:T(1024)(128)(4,1)}), s8[4194304]{0:T(1024)(128)(4,1)S(1)}, s32[]{:S(2)}) async-start(s8[4325376]{0:T(1024)(128)(4,1)} %bitcast.345), calls=%async_computation.9 | async-start | bytes 8388608
  1141.3 11.9 %slice-start.1 = ((s8[4325376]{0:T(1024)(128)(4,1)}), s8[131072]{0:T(1024)(128)(4,1)S(1)}, s32[]{:S(2)}) async-start(s8[4325376]{0:T(1024)(128)(4,1)} %bitcast.345), calls=%async_computation.10 | async-start | bytes 262144
  1156.3 4.3 copy-start.21
  1162.2 2.7 copy-start.9
  1163.7 3.9 copy-start.27
  1164.9 3.8 copy-start.20
  (37 other events, 50.8 us)
Sparse Core Ops, SparseCore 0:
  23.6 61.2 all-gather.5
  280.2 43.8 all-gather.7
  325.9 92.4 all-gather.9
  420.2 36.7 all-gather.11
  529.3 71.0 reduce-scatter.2
  616.5 39.7 all-gather.13
  931.7 24.3 reduce-scatter.4

commit v6 on v5

--- a/solution.py
+++ b/solution.py
@@ -162,7 +162,7 @@
         compiler_params=pltpu.CompilerParams(
             collective_id=ident, has_side_effects=True, vmem_limit_bytes=VMEM_BYTES
         ),
-        cost_estimate=pl.CostEstimate(flops=0, bytes_accessed=8 * size, transcendentals=0),
+        cost_estimate=pl.CostEstimate(flops=0, bytes_accessed=size // 8, transcendentals=0),
         name=name,
     )(*inputs)
 
@@ -1249,7 +1249,7 @@
         ],
         compiler_params=pltpu.CompilerParams(vmem_limit_bytes=VMEM_BYTES),
         cost_estimate=pl.CostEstimate(
-            flops=0, bytes_accessed=vocab * columns * 4 + count * columns * 24, transcendentals=0
+            flops=0, bytes_accessed=vocab * columns * 4, transcendentals=0
         ),
         name="lookup",
     )(ids, turns, table)
@@ -1320,7 +1320,7 @@
         out_shape=[struct((vocab, columns), FULL), struct((8, columns), FULL)],
         compiler_params=pltpu.CompilerParams(vmem_limit_bytes=VMEM_BYTES),
         cost_estimate=pl.CostEstimate(
-            flops=count * columns, bytes_accessed=count * columns * 48, transcendentals=0
+            flops=count * columns, bytes_accessed=vocab * columns * 8, transcendentals=0
         ),
         name="spread",
     )(ids, listed, rows, head)
@@ -1398,25 +1398,26 @@
     ffn_low = jnp.moveaxis(ffn, 1, 0).astype(LOW)
     ffn_cut = ffn_low.reshape(3, narrow_count, ffn_size, ffn_low.shape[2])
     ffn_cut = jnp.moveaxis(ffn_cut, 1, 0).reshape(narrow_count, 3 * ffn_size, -1)
-    kv_part = lax.all_gather(attn_kv.reshape(columns, -1).astype(LOW), "narrow", axis=0)
-    kv_part = jnp.moveaxis(kv_part, 0, 1).reshape(columns, -1)
-    proj_own = jnp.concatenate([attn_qo.reshape(columns, -1).astype(LOW), kv_part], axis=1)
-    proj = lax.all_gather(proj_own, "wide", axis=0, tiled=True)
+    kv_own = attn_kv.reshape(columns, -1).astype(LOW)
 
     where_at = jnp.arange(seq_len, dtype=jnp.int32)
     pick_tokens = jnp.sum(
         jnp.where(pick_ids[:, None] == where_at[None, :], tokens[0][None, :], 0), axis=1
     )
     ints = box(jnp.concatenate([tokens[0], pick_tokens, targets[0]]))
-    all_ints, all_gains, ffn_sub = launch(
+    all_ints, all_gains, kv_part, ffn_sub = launch(
         [
             gather_wide(ints),
             gather_both(box(gains.astype(LOW).astype(FULL).reshape(-1))),
+            gather_blocks("narrow", kv_own),
             join_columns("narrow", ffn_cut),
         ],
         0,
         "gather_ids",
     )
+    kv_part = jnp.moveaxis(kv_part, 0, 1).reshape(columns, -1)
+    proj_own = jnp.concatenate([attn_qo.reshape(columns, -1).astype(LOW), kv_part], axis=1)
+    proj = lax.all_gather(proj_own, "wide", axis=0, tiled=True)
     ffn_w = lax.all_gather(ffn_sub.reshape(3, ffn_size, width), "wide", axis=0)
     gain_size = gains.shape[1]
     gain_w = all_gains.reshape(narrow_count, wide_count, -1)[:, :, : 3 * gain_size]
@@ -1481,6 +1482,7 @@
         2,
         "trade_heads",
     )
+    start_low, ffn_w = lax.optimization_barrier((start_low, ffn_w))
     own_head = jnp.transpose(own_head, (2, 1, 0, 3, 4)).reshape(2, groups, seq_len, HD)
     keys, values = own_head[0], own_head[1]
     start_h = start_low.reshape(sel, width).astype(FULL)
@@ -1670,6 +1672,19 @@
         11,
         "return_rows",
     )
+    final_parts, grad_rows = lax.optimization_barrier((for_owners[:3], grad_rows))
+    size = width // narrow_count
+
+    def final_piece(spot):
+        return lax.dynamic_slice_in_dim(final_parts, spot * size, size, 2)
+
+    summed_ffn = jnp.zeros((3, narrow_count, ffn_size, size), LOW)
+    for step in range(narrow_count):
+        piece = final_piece(lax.rem(narrow_spot + step, narrow_count))
+        if step:
+            piece = shifted(piece, "narrow", step)
+        source = lax.rem(narrow_spot - step + narrow_count, narrow_count)
+        summed_ffn = lax.dynamic_update_index_in_dim(summed_ffn, piece, source, 1)
     turn = lax.rem(wide_spot, 2)
     grad_kv_w = jnp.einsum(
         "wtc,wtf->cf", tok_cols, kv_wide, preferred_element_type=FULL
@@ -1689,6 +1704,8 @@
     sums = jnp.stack(
         [gain_attn, gain_mid[0], gain_early + gain_late[0], jnp.full((width,), squares)]
     )
+    sums, summed_ffn = lax.optimization_barrier((sums, summed_ffn))
+    summed_ffn = summed_ffn.reshape(3, ffn_rows, size).astype(FULL)
     sums, kv_owned = launch(
         [
             combine(sums.reshape(4, 8, -1), add_two),
@@ -1704,21 +1721,6 @@
     square_total = sums[3, 0] + jnp.sum(sums[:3] * sums[:3])
     grad_norm = jnp.sqrt(square_total) / loss_count
     factor = jnp.minimum(1.0, CLIP_NORM / (grad_norm + 1e-06)) / loss_count
-
-    final_parts, factor = lax.optimization_barrier((for_owners[:3], factor))
-    size = width // narrow_count
-
-    def final_piece(spot):
-        return lax.dynamic_slice_in_dim(final_parts, spot * size, size, 2)
-
-    summed_ffn = jnp.zeros((3, narrow_count, ffn_size, size), LOW)
-    for step in range(narrow_count):
-        piece = final_piece(lax.rem(narrow_spot + step, narrow_count))
-        if step:
-            piece = shifted(piece, "narrow", step)
-        source = lax.rem(narrow_spot - step + narrow_count, narrow_count)
-        summed_ffn = lax.dynamic_update_index_in_dim(summed_ffn, piece, source, 1)
-    summed_ffn = summed_ffn.reshape(3, ffn_rows, size).astype(FULL)
 
     def ffn_owner():
         return newton(factor, mom_owned, owned.reshape(ffn_rows, width))

time: 1200 us -> 1130 us (0.942)
  waiting for transfers between devices: 146 us -> 49.5 us
  Pallas kernels: 748 us -> 784 us
  blocking collectives: 12.8 us -> 0 us
    all_gather x1, waiting for transfers between devices: 78 us -> 4.72 us  [per_device(): ffn_w = lax.all_gather(ffn_sub.reshape(3, ffn_size, width), 'wide', axis=0)]
    pallas_call x13, Pallas kernels: 625 us -> 665 us  [launch(): pl.pallas_call(body, out_shape=outputs, in_specs=[place for task in tasks...]
    ppermute x6, waiting for transfers between devices: 66.8 us -> 43.9 us  [shifted(): return lax.ppermute(parts, axis, pairs)]
    all_gather x1 -> x0, blocking collectives: 12.8 us -> none  [per_device(): lax.all_gather(attn_kv.reshape(columns, -1).astype(LOW), 'narrow', axis=0)]
    unnamed x190 -> x181, local copies, waits for them, and re-layouts: 27.4 us -> 26.7 us
  transfers between devices with their start and end apart: 13 -> 13, of which waited for: 4 -> 5; matrix products, arithmetic and copies ran while one was open for 14% -> 15% of each run, Pallas kernels for 42% -> 44%
where the time goes in v6:
time: 1130 us; the launch traced here: 1120 us
  Pallas kernels  784 us (69%)
  other arithmetic  93.3 us (8%)
  matrix products  88.1 us (8%)
  local copies, waits for them, and re-layouts  71.7 us (6%)
  waiting for transfers between devices  49.5 us (4%)
  between operations  25.1 us (2%)
    pallas_call x13, Pallas kernels, launch(): pl.pallas_call(body, out_shape=outputs, in_specs=[place for task in tasks...  665 us
    dot_general x16, matrix products, dot(): lax.dot_general(first, second, (((first_dim,), (second_dim,)), ((), ())),...  77.5 us
    ppermute x6, waiting for transfers between devices, shifted(): return lax.ppermute(parts, axis, pairs)  43.9 us
    pallas_call x1, Pallas kernels, newton(): pl.pallas_call(newton_body, in_specs=[pl.BlockSpec(memory_space=pltpu.SME...  43.5 us
    pallas_call x1, Pallas kernels, lookup(): pl.pallas_call(lookup_body, in_specs=[pl.BlockSpec(memory_space=pltpu.SME...  27.7 us
    unnamed x181, local copies, waits for them, and re-layouts  26.7 us
    sub x2, other arithmetic, adamw(): weight * (1.0 - rate * decay) - rate * update  22.8 us
  transfers between devices with their start and end apart: 13, of which 5 were waited for; matrix products, arithmetic and copies ran while one was open for 15% of the time, Pallas kernels for 44%

profile of v6, /device:TPU:17, one launch (start us, length us, event | category | flops | bytes accessed | tf_op | source)
XLA Modules:
  0.0 1116.4 jit_solution(10350546549190357401)
XLA Ops:
  9.4 2.5 convert_element_type.236
  15.0 65.3 %gather_ids.1 = (s32[8,16,128]{2,1,0:T(8,128)}, f32[4,8,8,128]{3,2,1,0:T(8,128)}, bf16[4,256,256]{2,1,0:T(8,128)(2,1)}, bf16[528,2048]{1,0:T(8,128)(2,1)}) custom-call(s32[16,128]{1,0:T(8,128)} %pad_bitcast_fusion.1.refs_0_, f32[8,128]{1,0:T(8,128)} %bitcast_convert_fusion.refs_1_, bf16[256,256]{1,0:T(8,128)(2,1)} %bitcast.389, bf16[4,528,512]{2,1,0:T(8,128)(2,1)} %bitcast.352), custom_call_target="tpu_custom_call" | custom-call | bytes 648704 | tf_op jit(solution)/shard_map/gather_ids/pallas_call | solution.py:156
  88.5 27.7 %lookup.1 = (bf16[9216,256]{1,0:T(8,128)(2,1)}, bf16[8192,256]{1,0:T(8,128)(2,1)}, s32[9248]{0:T(1024)}) custom-call(s32[9216]{0:T(1024)} %and_select_fusion.ids_ref, s32[9344]{0:T(1024)} %concatenate.81.turn_ref, f32[8192,256]{1,0:T(8,128)} %table_ref.1), custom_call_target="tpu_custom_call" | custom-call | bytes 8388608 | tf_op jit(solution)/shard_map/lookup/pallas_call | solution.py:1236
  116.2 142.2 %fetch_rows.1 = (bf16[288,2048]{1,0:T(8,128)(2,1)}, bf16[1024,2048]{1,0:T(8,128)(2,1)}) custom-call(bf16[4,2304,256]{2,1,0:T(8,128)(2,1)} %bitcast.355, bf16[8,1024,256]{2,1,0:T(8,128)(2,1)} %bitcast.357), custom_call_target="tpu_custom_call" | custom-call | bytes 1785856 | tf_op jit(solution)/shard_map/fetch_rows/pallas_call | solution.py:156
  264.4 4.1 fusion.7
  270.2 27.0 %trade_heads.1 = (bf16[4,1,2,256,128]{4,3,2,1,0:T(8,128)(2,1)}, bf16[4,32,2048]{2,1,0:T(8,128)(2,1)}, bf16[8,256,256]{2,1,0:T(8,128)(2,1)}) custom-call(bf16[4,1,2,256,128]{4,3,2,1,0:T(8,128)(2,1)} %maximum_bitcast_fusion.refs_0_, bf16[32,2048]{1,0:T(8,128)(2,1)} %slice.183.refs_1_, bf16[256,2048]{1,0:T(8,128)(2,1)} %copy-done.9), custom_call_target="tpu_custom_call" | custom-call | bytes 475136 | tf_op jit(solution)/shard_map/trade_heads/pallas_call | solution.py:156
  297.1 4.7 all-gather.8.cloned.1.call-done.weight_ref
  303.2 2.3 multiply_convert_fusion.2
  313.8 2.9 convolution_convert_fusion.3
  317.3 27.3 %settle_middle.1 = (f32[32,2048]{1,0:T(8,128)}, bf16[4,32,2048]{2,1,0:T(8,128)(2,1)}, bf16[8,128,512]{2,1,0:T(8,128)(2,1)}, bf16[8,128,256]{2,1,0:T(8,128)(2,1)}) custom-call(bf16[4,32,2048]{2,1,0:T(8,128)(2,1)} %bitcast.376, f32[32,2048]{1,0:T(8,128)} %get-tuple-element.251.refs_1_.refs_2_, f32[32,2048]{1,0:T(8,128)} %get-tuple-element.251.refs_1_.refs_2_, ...), custom_call_target="tpu_custom_call" | custom-call | bytes 509952 | tf_op jit(solution)/shard_map/settle_middle/pallas_call | solution.py:156
  348.3 2.5 convert_bitcast_fusion
  350.8 1.9 pad_maximum_fusion.3
  353.4 13.7 %feed.1 = (f32[8,128,176]{2,1,0:T(8,128)}, f32[8,128,176]{2,1,0:T(8,128)}, bf16[8,128,176]{2,1,0:T(8,128)(2,1)}, bf16[128,2048]{1,0:T(8,128)(2,1)}) custom-call(bf16[128,2048]{1,0:T(8,128)(2,1)} %bitcast.368, bf16[8,3,176,2048]{3,2,1,0:T(8,128)(2,1)} %all-gather.8.cloned.1.call-done.weight_ref), custom_call_target="tpu_custom_call" | custom-call | flops 2214592512 | bytes 17301504 | tf_op jit(solution)/shard_map/feed/pallas_call | solution.py:941
  367.7 28.9 %settle_late.1 = (f32[32,2048]{1,0:T(8,128)}, bf16[4,32,2048]{2,1,0:T(8,128)(2,1)}) custom-call(bf16[4,32,2048]{2,1,0:T(8,128)(2,1)} %bitcast.397, f32[32,2048]{1,0:T(8,128)} %get-tuple-element.113.refs_1_, f32[32,2048]{1,0:T(8,128)} %get-tuple-element.251.refs_1_.refs_2_, f32[1,2048]{1,0:T(1,128)} %broadcast_in_dim.193.refs_3_, f32[1,2048]{1,0:T(1,128)} %slice.193.refs_4_), custom_call_target="tpu_custom_call" | custom-call | bytes 231424 | tf_op jit(solution)/shard_map/settle_late/pallas_call | solution.py:156
  396.5 34.7 %gather_late.1 = (bf16[8,128,2048]{2,1,0:T(8,128)(2,1)}, bf16[4,352,512]{2,1,0:T(8,128)(2,1)}) custom-call(bf16[128,2048]{1,0:T(8,128)(2,1)} %bitcast.398, bf16[4,352,512]{2,1,0:T(8,128)(2,1)} %get-tuple-element.269.refs_1_), custom_call_target="tpu_custom_call" | custom-call | bytes 950272 | tf_op jit(solution)/shard_map/gather_late/pallas_call | solution.py:156
  431.3 8.3 fusion.110
  439.6 7.8 fusion.108
  447.4 2.0 exponential_reduce_fusion.1
  450.0 13.6 %combine_stats.1 = f32[3,8,256]{2,1,0:T(8,128)} custom-call(f32[3,8,256]{2,1,0:T(8,128)} %bitcast.418), custom_call_target="tpu_custom_call" | custom-call | bytes 6144 | tf_op jit(solution)/shard_map/combine_stats/pallas_call | solution.py:156
  465.0 10.2 convolution_convert_fusion
  477.2 10.2 convolution_convert_fusion.1
  487.4 44.8 %sum_late.1 = (f32[128,2048]{1,0:T(8,128)}, bf16[4,352,512]{2,1,0:T(8,128)(2,1)}) custom-call(bf16[8,128,2048]{2,1,0:T(8,128)(2,1)} %bitcast.358, bf16[4,352,512]{2,1,0:T(8,128)(2,1)} %get-tuple-element.268.refs_1_), custom_call_target="tpu_custom_call" | custom-call | bytes 1015808 | tf_op jit(solution)/shard_map/sum_late/pallas_call | solution.py:156
  532.2 2.1 convert_element_type.272
  535.0 26.1 %back_late.1 = (f32[32,2048]{1,0:T(8,128)}, f32[1,2048]{1,0:T(1,128)}, bf16[4,32,2048]{2,1,0:T(8,128)(2,1)}) custom-call(bf16[4,32,2048]{2,1,0:T(8,128)(2,1)} %bitcast.369, f32[32,2048]{1,0:T(8,128)} %get-tuple-element.118.refs_1_, f32[32,2048]{1,0:T(8,128)} %broadcast_in_dim.195.refs_2_, f32[1,2048]{1,0:T(1,128)} %broadcast_in_dim.193.refs_3_, ...), custom_call_target="tpu_custom_call" | custom-call | bytes 232448 | tf_op jit(solution)/shard_map/back_late/pallas_call | solution.py:156
  563.1 14.8 %feed_back.1 = (bf16[8,3,128,176]{3,2,1,0:T(8,128)(2,1)}, bf16[128,2048]{1,0:T(8,128)(2,1)}) custom-call(bf16[128,2048]{1,0:T(8,128)(2,1)} %bitcast.366, bf16[8,3,176,2048]{3,2,1,0:T(8,128)(2,1)} %all-gather.8.cloned.1.call-done.weight_ref, f32[8,128,176]{2,1,0:T(8,128)} %get-tuple-element.120.gate_ref, f32[8,128,176]{2,1,0:T(8,128)} %get-tuple-element.121.up_ref, ...), custom_call_target="tpu_custom_call" | custom-call | flops 2214592512 | bytes 17301504 | tf_op jit(solution)/shard_map/feed_back/pallas_call | solution.py:993
  577.9 28.9 %back_middle.1 = (f32[32,2048]{1,0:T(8,128)}, f32[1,2048]{1,0:T(1,128)}, bf16[4,32,2048]{2,1,0:T(8,128)(2,1)}) custom-call(bf16[4,32,2048]{2,1,0:T(8,128)(2,1)} %bitcast.394, f32[32,2048]{1,0:T(8,128)} %get-tuple-element.113.refs_1_, f32[32,2048]{1,0:T(8,128)} %broadcast_multiply_fusion.refs_2_, f32[1,2048]{1,0:T(1,128)} %broadcast_in_dim.193.refs_3_, ...), custom_call_target="tpu_custom_call" | custom-call | bytes 232448 | tf_op jit(solution)/shard_map/back_middle/pallas_call | solution.py:156
  606.8 9.2 fusion.93
  616.0 8.6 add_convert_fusion.refs_3_
  624.6 2.5 fusion.30
  630.1 2.1 fusion.60
  635.0 2.9 convolution_convert_fusion.2
  637.9 40.0 %trade_grads.1 = (bf16[4,1,2,256,128]{4,3,2,1,0:T(8,128)(2,1)}, f32[32,2048]{1,0:T(8,128)}, f32[32,2048]{1,0:T(8,128)}, bf16[8,3,128,176]{3,2,1,0:T(8,128)(2,1)}...) custom-call(bf16[4,1,2,256,128]{4,3,2,1,0:T(8,128)(2,1)} %maximum_bitcast_fusion.1.refs_0_, ...), custom_call_target="tpu_custom_call" | custom-call | bytes 876544 | tf_op jit(solution)/shard_map/trade_grads/pallas_call | solution.py:156
  682.4 1.7 convolution_bitcast_fusion.1
  687.1 2.4 multiply_reduce_fusion.3
  689.5 2.0 fusion.112
  691.6 3.7 fusion.5
  699.8 1.8 multiply_reduce_fusion.1
  702.8 2.1 pad_maximum_fusion.refs_1_
  704.9 163.8 %return_rows.1 = (bf16[4,2304,256]{2,1,0:T(8,128)(2,1)}, bf16[4,176,2048]{2,1,0:T(8,128)(2,1)}, bf16[8,256,1024]{2,1,0:T(8,128)(2,1)}, bf16[8,1024,256]{2,1,0:T(8,128)(2,1)}) custom-call(bf16[288,2048]{1,0:T(8,128)(2,1)} %pad_maximum_fusion.4.refs_0_, bf16[4,176,2048]{2,1,0:T(8,128)(2,1)} %pad_maximum_fusion.refs_1_, bf16[256,1024]{1,0:T(8,128)(2,1)} %reshape.799.refs_2_, ...), custom_call_target="tpu_custom_call" | custom-call | bytes 3096576 | tf_op jit(solution)/shard_map/return_rows/pallas_call | solution.py:156
  868.8 3.5 convolution_bitcast_fusion
  874.4 6.0 copy.246
  881.6 1.8 pad_maximum_fusion.2
  885.3 2.6 constant_dynamic-update-slice_fusion
  892.5 19.4 %spread.1 = (f32[8192,256]{1,0:T(8,128)}, f32[8,256]{1,0:T(8,128)}) custom-call(s32[9216]{0:T(1024)} %and_select_fusion.ids_ref, s32[9248]{0:T(1024)} %get-tuple-element.145.list_ref, bf16[9216,256]{1,0:T(8,128)(2,1)} %bitcast.354, bf16[8192,256]{1,0:T(8,128)(2,1)} %bitcast.356), custom_call_target="tpu_custom_call" | custom-call | flops 2359296 | bytes 16777216 | tf_op jit(solution)/shard_map/spread/pallas_call | solution.py:1310
  915.2 1.9 bitcast_dynamic-update-slice_fusion.2
  917.1 10.2 collective-permute-done.1
  927.3 1.9 bitcast_dynamic-update-slice_fusion.1
  929.2 1.8 copy.235
  931.0 7.9 collective-permute-done.2
  940.0 2.3 fusion.106
  945.0 22.5 %combine_sums.1 = (f32[4,8,256]{2,1,0:T(8,128)}, bf16[4,512,128]{2,1,0:T(8,128)(2,1)}) custom-call(f32[4,8,256]{2,1,0:T(8,128)} %bitcast.415, bf16[512,128]{1,0:T(8,128)(2,1)} %bitcast.392), custom_call_target="tpu_custom_call" | custom-call | bytes 90112 | tf_op jit(solution)/shard_map/combine_sums/pallas_call | solution.py:156
  973.0 2.5 bitcast_add_fusion.1
  975.5 2.7 convert_multiply_fusion
  978.2 43.7 %conditional.1 = (bf16[4,704,512]{2,1,0:T(8,128)(2,1)S(1)}) conditional(s32[]{:T(128)} %convert_element_type.289, (f32[]{:T(128)}, bf16[4,176,2048]{2,1,0:T(8,128)(2,1)}, bf16[4,704,512]{2,1,0:T(8,128)(2,1)S(1)}) %tuple.101, (f32[]{:T(128)}, bf16[4,704,512]{2,1,0:T(8,128)(2,1)S(1)}, bf16[4,176,2048]{2,1,0:T(8,128)(2,1)}, ...), branch_computations={%region_38.39_spmd, %region_39.40_spmd} | conditional | flops 23789568000 | bytes 8650760 | solution.py:1732
  978.2 43.5 %newton.1 = bf16[4,704,512]{2,1,0:T(8,128)(2,1)S(1)} custom-call(f32[1]{0:T(128)} %bitcast.factor_ref, bf16[4,704,512]{2,1,0:T(8,128)(2,1)S(1)} %get-tuple-element.18.mom_ref, bf16[704,2048]{1,0:T(8,128)(2,1)} %bitcast.445), custom_call_target="tpu_custom_call" | custom-call | flops 23789568000 | bytes 8650752 | tf_op jit(solution)/shard_map/cond/branch_0_fun/newton/pallas_call | solution.py:1114
  1023.5 3.3 constant_dynamic-slice_fusion
  1029.9 1.8 copy.256
  1031.7 22.1 %multiply_subtract_fusion = (f32[8192,256]{1,0:T(8,128)}, f32[8192,256]{1,0:T(8,128)}, f32[8192,256]{1,0:T(8,128)}) fusion(f32[8192,256]{1,0:T(8,128)} %table_ref.1, f32[8192,256]{1,0:T(8,128)} %get-tuple-element.153, f32[]{:T(128)} %div.100, f32[8192,256]{1,0:T(8,128)} %param.25, f32[8192,256]{1,0:T(8,128)} %param.26), kind=kLoop, calls=%fused_computation.2 | loop fusion | flops 31457280 | bytes 58720260 | tf_op jit(solution)/shard_map/sub | solution.py:1337
  1054.5 6.7 bitcast_add_fusion
  1062.6 11.7 %collective-permute-done.4 = bf16[704,512]{1,0:T(8,128)(2,1)} collective-permute-done((bf16[704,512]{1,0:T(8,128)(2,1)}, bf16[704,512]{1,0:T(8,128)(2,1)}, u32[]{:S(2)}, u32[]{:S(2)}) %collective-permute-start.4) | collective-permute-done | bytes 720928 | tf_op jit(solution)/shard_map/ppermute | solution.py:1348
  1075.7 14.1 %collective-permute-done.3 = bf16[704,512]{1,0:T(8,128)(2,1)} collective-permute-done((bf16[704,512]{1,0:T(8,128)(2,1)}, bf16[704,512]{1,0:T(8,128)(2,1)}, u32[]{:S(2)}, u32[]{:S(2)}) %collective-permute-start.3) | collective-permute-done | bytes 720928 | tf_op jit(solution)/shard_map/ppermute | solution.py:1348
  1089.8 2.3 copy.240
  1094.7 3.1 bitcast_subtract_fusion
  1097.7 5.9 copy.259
  (352 shorter events, 90.7 us)
Async XLA Ops:
  7.2 257.2 %all-gather.6.cloned.1.call-start = ((), (), s32[]{:S(2)}) async-start(), calls=%async_computation.2 | async-start | bytes 9437184 | tf_op jit(solution)/shard_map/all_gather | solution.py:1420
  13.5 68.0 %copy-start.6 = (f32[256,2,512]{2,1,0:T(2,128)S(1)}, f32[256,2,512]{2,1,0:T(2,128)}, u32[]{:S(2)}) copy-start(f32[256,2,512]{2,1,0:T(2,128)} %param.27) | copy-start | bytes 3145732
  82.5 4.1 copy-start.45
  83.5 218.3 %all-gather.8.cloned.1.call-start = ((), (), s32[]{:S(2)}) async-start(), calls=%async_computation.3 | async-start | bytes 19464192 | tf_op jit(solution)/shard_map/all_gather | solution.py:1421
  84.3 355.3 %all-gather.10.cloned.1.call-start = ((), (), s32[]{:S(2)}) async-start(), calls=%async_computation.4 | async-start | bytes 4718592 | tf_op jit(solution)/shard_map/all_gather | solution.py:1505
  116.2 143.9 %copy-start.78 = (s32[1,2]{1,0:T(1,128)S(1)}, s32[1,2]{1,0:T(1,128)}, u32[]{:S(2)}) copy-start(s32[1,2]{1,0:T(1,128)} %param.22) | copy-start | bytes 28
  260.0 2.6 copy-start.43
  260.3 46.5 %copy-start.67 = (f32[64]{0:T(128)}, f32[64]{0:T(128)S(1)}, u32[]{:S(2)}) copy-start(f32[64]{0:T(128)S(1)} %multiply_power_fusion) | copy-start | bytes 772
  260.4 46.3 %copy-start.71 = (s32[2]{0:T(128)}, s32[2]{0:T(128)S(1)}, u32[]{:S(2)}) copy-start(s32[2]{0:T(128)S(1)} %fusion.89) | copy-start | bytes 28
  264.3 4.1 copy-start.9
  269.3 37.2 %copy-start.68 = (s32[1,128]{1,0:T(1,128)S(1)}, s32[1,128]{1,0:T(1,128)}, u32[]{:S(2)}) copy-start(s32[1,128]{1,0:T(1,128)} %param.20) | copy-start | bytes 1540
  305.5 2.3 copy-start.2
  305.5 158.1 %all-gather.12.cloned.1.call-start = ((), (), s32[]{:S(2)}) async-start(), calls=%async_computation.5 | async-start | bytes 4718592 | tf_op jit(solution)/shard_map/all_gather | solution.py:1523
  307.5 2.6 copy-start.37
  307.8 3.1 copy-start.39
  312.4 34.3 %copy-start.15 = (f32[256,2,512]{2,1,0:T(2,128)S(1)}, f32[256,2,512]{2,1,0:T(2,128)}, u32[]{:S(2)}) copy-start(f32[256,2,512]{2,1,0:T(2,128)} %param.28) | copy-start | bytes 3145732
  344.6 279.9 %reduce-scatter.3.cloned.1.call-start = ((), (), s32[]{:S(2)}) async-start(), calls=%async_computation.6 | async-start | bytes 4718592 | tf_op jit(solution)/shard_map/reduce_scatter | solution.py:1579
  353.4 122.6 %copy-start.58 = (pred[8,128]{1,0:T(8,128)(4,1)}, pred[8,128]{1,0:T(8,128)(4,1)S(1)}, u32[]{:S(2)}) copy-start(pred[8,128]{1,0:T(8,128)(4,1)S(1)} %get-tuple-element.253) | copy-start | bytes 3076
  353.4 77.9 %copy-start.76 = (bf16[1024,2048]{1,0:T(8,128)(2,1)S(1)}, bf16[1024,2048]{1,0:T(8,128)(2,1)}, u32[]{:S(2)}) copy-start(bf16[1024,2048]{1,0:T(8,128)(2,1)} %get-tuple-element.108) | copy-start | bytes 12582916
  439.6 7.8 copy-start.57
  439.6 7.8 copy-start.11
  475.2 216.4 %all-gather.14.cloned.1.call-start = ((), (), s32[]{:S(2)}) async-start(), calls=%async_computation.7 | async-start | bytes 4718592 | tf_op jit(solution)/shard_map/all_gather | solution.py:1595
  562.9 377.1 %reduce-scatter.5.cloned.1.call-start = ((), (), s32[]{:S(2)}) async-start(), calls=%async_computation.8 | async-start | bytes 1310720 | tf_op jit(solution)/shard_map/reduce_scatter | solution.py:1693
  563.1 43.6 %copy-start.14 = (f32[1024,1024]{0,1:T(8,128)S(1)}, f32[1024,1024]{0,1:T(8,128)}, u32[]{:S(2)}) copy-start(f32[1024,1024]{0,1:T(8,128)} %copy-done.13) | copy-start | bytes 12582916
  606.7 9.2 copy-start.12
  606.7 9.2 copy-start.77
  615.9 8.6 copy-start.35
  624.5 2.5 copy-start.40
  624.5 2.5 copy-start.55
  624.5 2.5 copy-start.65
  637.9 42.8 %copy-start.33 = (bf16[8,128,256]{2,1,0:T(8,128)(2,1)S(1)}, bf16[8,128,256]{2,1,0:T(8,128)(2,1)}, u32[]{:S(2)}) copy-start(bf16[8,128,256]{2,1,0:T(8,128)(2,1)} %get-tuple-element.135) | copy-start | bytes 1572868
  677.9 4.5 copy-start.34
  682.4 2.4 copy-start.1
  682.4 2.4 copy-start.29
  682.4 2.4 copy-start.73
  682.4 2.5 copy-start.75
  684.6 2.5 copy-start.8
  691.6 3.7 copy-start
  691.6 3.7 copy-start.50
  691.6 3.7 copy-start.30
  696.7 3.1 copy-start.10
  699.8 2.9 copy-start.19
  704.9 163.9 %copy-start.17 = (bf16[8,256,256]{2,1,0:T(8,128)(2,1)S(1)}, bf16[8,256,256]{2,1,0:T(8,128)(2,1)}, u32[]{:S(2)}) copy-start(bf16[8,256,256]{2,1,0:T(8,128)(2,1)} %get-tuple-element.139) | copy-start | bytes 3145732
  874.4 6.0 copy-start.22
  881.6 3.0 copy-start.51
  881.6 3.0 copy-start.59
  883.4 4.4 copy-start.61
  884.6 30.6 %collective-permute-start = (bf16[3,176,512]{2,1,0:T(8,128)(2,1)}, bf16[3,176,512]{2,1,0:T(8,128)(2,1)}, u32[]{:S(2)}, u32[]{:S(2)}) collective-permute-start(bf16[3,176,512]{2,1,0:T(8,128)(2,1)} %get-tuple-element.272), channel_id=1, source_target_pairs={{0,1},{1,2},{2,3},{3,0},{4,5},{5,6},{6,7},{7,4},{8,9},{9,10},{10,1... | collective-permute-start | bytes 1622024 | tf_op jit(solution)/shard_map/ppermute | solution.py:1348
  885.3 42.0 %collective-permute-start.1 = (bf16[3,176,512]{2,1,0:T(8,128)(2,1)}, bf16[3,176,512]{2,1,0:T(8,128)(2,1)}, u32[]{:S(2)}, u32[]{:S(2)}) collective-permute-start(bf16[3,176,512]{2,1,0:T(8,128)(2,1)} %get-tuple-element.271), channel_id=1, source_target_pairs={{0,2},{1,3},{2,0},{3,1},{4,6},{5,7},{6,4},{7,5},{8,10},{9,11},{10,... | collective-permute-start | bytes 1622024 | tf_op jit(solution)/shard_map/ppermute | solution.py:1348
  888.7 50.2 %collective-permute-start.2 = (bf16[3,176,512]{2,1,0:T(8,128)(2,1)}, bf16[3,176,512]{2,1,0:T(8,128)(2,1)}, u32[]{:S(2)}, u32[]{:S(2)}) collective-permute-start(bf16[3,176,512]{2,1,0:T(8,128)(2,1)} %get-tuple-element.270), channel_id=1, source_target_pairs={{0,3},{1,0},{2,1},{3,2},{4,7},{5,4},{6,5},{7,6},{8,11},{9,8},{10,9... | collective-permute-start | bytes 1622024 | tf_op jit(solution)/shard_map/ppermute | solution.py:1348
  929.2 15.2 %copy-start.60 = (f32[1,2048]{1,0:T(1,128)S(1)}, f32[1,2048]{1,0:T(1,128)}, u32[]{:S(2)}) copy-start(f32[1,2048]{1,0:T(1,128)} %get-tuple-element.132) | copy-start | bytes 24580
  975.5 2.7 copy-start.31
  1023.5 5.5 copy-start.27
  1023.5 5.5 copy-start.28
  1023.5 6.5 copy-start.16
  1026.7 34.5 %collective-permute-start.5 = (bf16[704,512]{1,0:T(8,128)(2,1)}, bf16[704,512]{1,0:T(8,128)(2,1)}, u32[]{:S(2)}, u32[]{:S(2)}) collective-permute-start(bf16[704,512]{1,0:T(8,128)(2,1)} %get-tuple-element.265), channel_id=1, source_target_pairs={{0,1},{1,2},{2,3},{3,0},{4,5},{5,6},{6,7},{7,4},{8,9},{9,10},{10,1... | collective-permute-start | bytes 2162696 | tf_op jit(solution)/shard_map/ppermute | solution.py:1348
  1027.5 46.8 %collective-permute-start.4 = (bf16[704,512]{1,0:T(8,128)(2,1)}, bf16[704,512]{1,0:T(8,128)(2,1)}, u32[]{:S(2)}, u32[]{:S(2)}) collective-permute-start(bf16[704,512]{1,0:T(8,128)(2,1)} %get-tuple-element.266), channel_id=1, source_target_pairs={{0,2},{1,3},{2,0},{3,1},{4,6},{5,7},{6,4},{7,5},{8,10},{9,11},{10,... | collective-permute-start | bytes 2162696 | tf_op jit(solution)/shard_map/ppermute | solution.py:1348
  1028.4 61.4 %collective-permute-start.3 = (bf16[704,512]{1,0:T(8,128)(2,1)}, bf16[704,512]{1,0:T(8,128)(2,1)}, u32[]{:S(2)}, u32[]{:S(2)}) collective-permute-start(bf16[704,512]{1,0:T(8,128)(2,1)} %get-tuple-element.267), channel_id=1, source_target_pairs={{0,3},{1,0},{2,1},{3,2},{4,7},{5,4},{6,5},{7,6},{8,11},{9,8},{10,9... | collective-permute-start | bytes 2162696 | tf_op jit(solution)/shard_map/ppermute | solution.py:1348
  1031.7 22.1 %copy-start.63 = (f32[3,64]{1,0:T(4,128)S(1)}, f32[3,64]{1,0:T(4,128)}, u32[]{:S(2)}) copy-start(f32[3,64]{1,0:T(4,128)} %param.33) | copy-start | bytes 2308
  1031.7 22.1 %copy-start.69 = (f32[3,64]{1,0:T(4,128)S(1)}, f32[3,64]{1,0:T(4,128)}, u32[]{:S(2)}) copy-start(f32[3,64]{1,0:T(4,128)} %param.34) | copy-start | bytes 2308
  1031.7 22.1 %copy-start.70 = (f32[3,64]{1,0:T(4,128)S(1)}, f32[3,64]{1,0:T(4,128)}, u32[]{:S(2)}) copy-start(f32[3,64]{1,0:T(4,128)} %param.35) | copy-start | bytes 2308
  1089.8 4.9 slice-start
  1092.1 2.6 slice-start.1
  1104.3 3.0 copy-start.24
  (32 other events, 42.4 us)
Sparse Core Ops, SparseCore 0:
  83.7 91.0 all-gather.5
  176.6 125.1 all-gather.7
  305.6 41.2 all-gather.9
  348.7 36.2 all-gather.11
  475.4 71.1 reduce-scatter.2
  563.0 39.8 all-gather.13
  874.4 63.3 reduce-scatter.4

commit v7 on v6

--- a/solution.py
+++ b/solution.py
@@ -50,11 +50,6 @@
     )
 
 
-def norm_back(values, gain_row, grad):
-    output, pull = jax.vjp(norm_rows, values, gain_row)
-    return pull(grad)
-
-
 def segments_at(lens, where_at):
     ends = jnp.cumsum(lens)
     return jnp.sum((where_at[:, None] >= ends[None, :]).astype(jnp.int32), axis=1)
@@ -69,18 +64,6 @@
     inverse = ROPE_BASE ** (-2.0 * jnp.arange(HD // 2, dtype=FULL) / HD)
     angle = offset_pos[:, None] * inverse[None, :]
     return (segment, jnp.cos(angle), jnp.sin(angle))
-
-
-def rotate(values, cosine, sine):
-    half = values.shape[-1] // 2
-    first, second = (values[..., :half], values[..., half:])
-    return jnp.concatenate(
-        [first * cosine - second * sine, second * cosine + first * sine], axis=-1
-    )
-
-
-def unrotate(values, cosine, sine):
-    return rotate(values, cosine, -sine)
 
 
 MESH = pl.DeviceIdType.MESH
@@ -592,6 +575,7 @@
             copies.append(copy)
         keep = pltpu.make_async_copy(rows_for(me), columns_from(me), local)
         keep.start()
+        yield
         for step in range(1, wide):
             source = lax.rem(me - step + wide, wide)
             arrived(
@@ -909,6 +893,308 @@
     )
 
 
+def turn_heads(values, cosine, sine):
+    half = values.shape[1] // 2
+    swapped = jnp.concatenate([values[:, half:], values[:, :half]], axis=1)
+    return values * cosine + swapped * sine
+
+
+def wide_angles(cosine, sine):
+    return jnp.concatenate([cosine, cosine], axis=1), jnp.concatenate([-sine, sine], axis=1)
+
+
+def local_call(body, inputs, specs, outputs, flops, name):
+    return pl.pallas_call(
+        body,
+        grid=(1,),
+        in_specs=specs,
+        out_specs=[
+            pl.BlockSpec(a.shape, lambda step, rank=len(a.shape): (0,) * rank) for a in outputs
+        ],
+        out_shape=outputs,
+        compiler_params=pltpu.CompilerParams(vmem_limit_bytes=VMEM_BYTES),
+        cost_estimate=pl.CostEstimate(flops=flops, bytes_accessed=8 << 20, transcendentals=0),
+        name=name,
+    )(*inputs)
+
+
+def entire(values):
+    return pl.BlockSpec(values.shape, lambda step: (0,) * values.ndim)
+
+
+def column_block(values, size, index):
+    return pl.BlockSpec((values.shape[0], size), lambda step: (0, index))
+
+
+def heads_body(groups, rep, rows_ref, gain_ref, kv_ref, cos_ref, sin_ref, out_ref, normed_ref):
+    count, _, _, tok_rows, head = out_ref.shape
+    size = kv_ref.shape[1] // (2 * count)
+    per_head = head // size
+    rows = rows_ref[0:tok_rows, :].astype(FULL)
+    normed = norm_rows(rows, gain_ref[...]).astype(LOW)
+    normed_ref[...] = normed
+    both = dot(normed, kv_ref[...], 1, 0)
+
+    def head_of(kind, index):
+        pieces = [
+            both[:, (2 * part + kind) * size : (2 * part + kind + 1) * size]
+            for part in range(index * per_head, (index + 1) * per_head)
+        ]
+        return pieces[0] if per_head == 1 else jnp.concatenate(pieces, axis=1)
+
+    for owner in range(count):
+        for group in range(groups):
+            index = (owner * groups + group) // rep
+            keys = turn_heads(head_of(0, index), cos_ref[...], sin_ref[...])
+            out_ref[owner, group, 0] = keys.astype(LOW)
+            out_ref[owner, group, 1] = head_of(1, index).astype(LOW)
+
+
+def make_heads(rows_low, gain_row, proj, cosine, sine, groups, rep):
+    count = lax.axis_size("narrow")
+    tok_rows, head = cosine.shape
+    width = rows_low.shape[1]
+    size = 2 * KVH * HD
+    return local_call(
+        functools.partial(heads_body, groups, rep),
+        [rows_low, gain_row, proj, cosine, sine],
+        [entire(rows_low), entire(gain_row), column_block(proj, size, 0)]
+        + [entire(cosine), entire(sine)],
+        [struct((count, groups, 2, tok_rows, head), LOW), struct((tok_rows, width), LOW)],
+        2 * tok_rows * width * size,
+        "make_heads",
+    )
+
+
+def attend_body(
+    start_ref,
+    gains_ref,
+    q_ref,
+    o_ref,
+    kv_ref,
+    cos_ref,
+    sin_ref,
+    seg_ref,
+    seg_all_ref,
+    pick_ref,
+    queries_ref,
+    probs_ref,
+    mixed_ref,
+    part_ref,
+    normed_ref,
+    early_ref,
+):
+    count, groups, _, tok_rows, head = kv_ref.shape
+    heads_own = probs_ref.shape[0]
+    start = start_ref[...].astype(FULL)
+    root = lax.rsqrt(jnp.mean(start * start, axis=-1, keepdims=True) + NORM_EPS)
+    normed = (start * root * gains_ref[0:1, :]).astype(LOW)
+    normed_ref[...] = normed
+    early_ref[...] = (start * root * gains_ref[2:3, :]).astype(LOW)
+    queries = dot(normed, q_ref[...], 1, 0)
+    spots = lax.broadcasted_iota(jnp.int32, (1, count * tok_rows), 1)
+    allowed = (seg_ref[...] == seg_all_ref[...]) & (pick_ref[...] >= spots)
+    for group in range(groups):
+        keys = jnp.concatenate([kv_ref[part, group, 0] for part in range(count)], axis=0)
+        values = jnp.concatenate([kv_ref[part, group, 1] for part in range(count)], axis=0)
+        for member in range(heads_own // groups):
+            at = group * (heads_own // groups) + member
+            spot = slice(at * head, (at + 1) * head)
+            query = turn_heads(queries[:, spot], cos_ref[...], sin_ref[...]).astype(LOW)
+            queries_ref[:, spot] = query
+            scores = jnp.where(allowed, dot(query, keys, 1, 1) * head ** (-0.5), MASKED)
+            shifted = jnp.exp(scores - jnp.max(scores, axis=-1, keepdims=True))
+            probs = shifted / jnp.sum(shifted, axis=-1, keepdims=True)
+            probs_ref[at] = probs
+            mixed_ref[:, spot] = dot(probs.astype(LOW), values, 1, 0).astype(LOW)
+    part_ref[...] = dot(mixed_ref[...], o_ref[...], 1, 1).astype(LOW)
+
+
+def attend(start_low, gains, proj, own_head, cosine, sine, seg, seg_all, picks):
+    count, groups, _, tok_rows, head = own_head.shape
+    sel, width = start_low.shape
+    heads_own = HEADS // count
+    size = heads_own * head
+    first = 2 * KVH * HD // size
+    seq_len = count * tok_rows
+    return local_call(
+        attend_body,
+        [start_low, gains, proj, proj, own_head, cosine, sine, seg, seg_all, picks],
+        [
+            entire(start_low),
+            entire(gains),
+            column_block(proj, size, first),
+            column_block(proj, size, first + 1),
+        ]
+        + [entire(a) for a in (own_head, cosine, sine, seg, seg_all, picks)],
+        [
+            struct((sel, size), LOW),
+            struct((heads_own, sel, seq_len), FULL),
+            struct((sel, size), LOW),
+            struct((sel, width), LOW),
+            struct((sel, width), LOW),
+            struct((sel, width), LOW),
+        ],
+        4 * sel * size * (width + seq_len),
+        "attend",
+    )
+
+
+def attend_back_body(
+    grad_ref,
+    q_ref,
+    o_ref,
+    kv_ref,
+    queries_ref,
+    probs_ref,
+    cos_ref,
+    sin_ref,
+    cos_all_ref,
+    sin_all_ref,
+    out_ref,
+    grad_q_ref,
+    part_ref,
+):
+    count, groups, _, tok_rows, head = kv_ref.shape
+    heads_own = probs_ref.shape[0]
+    scale = head ** (-0.5)
+    grad_mixed = dot(grad_ref[...], o_ref[...], 1, 0).astype(LOW)
+    for group in range(groups):
+        keys = jnp.concatenate([kv_ref[part, group, 0] for part in range(count)], axis=0)
+        values = jnp.concatenate([kv_ref[part, group, 1] for part in range(count)], axis=0)
+        grad_keys = jnp.zeros(keys.shape, FULL)
+        grad_values = jnp.zeros(keys.shape, FULL)
+        for member in range(heads_own // groups):
+            at = group * (heads_own // groups) + member
+            spot = slice(at * head, (at + 1) * head)
+            probs = probs_ref[at]
+            grad_probs = dot(grad_mixed[:, spot], values, 1, 1)
+            inner = jnp.sum(probs * grad_probs, axis=-1, keepdims=True)
+            grad_scores = (probs * (grad_probs - inner)).astype(LOW)
+            grad_query = dot(grad_scores, keys, 1, 0) * scale
+            grad_q_ref[:, spot] = turn_heads(grad_query, cos_ref[...], -sin_ref[...]).astype(LOW)
+            grad_keys = grad_keys + dot(grad_scores, queries_ref[:, spot], 0, 0)
+            grad_values = grad_values + dot(probs.astype(LOW), grad_mixed[:, spot], 0, 0)
+        grad_keys = turn_heads(grad_keys * scale, cos_all_ref[...], -sin_all_ref[...])
+        for part in range(count):
+            rows = slice(part * tok_rows, (part + 1) * tok_rows)
+            out_ref[part, group, 0] = grad_keys[rows].astype(LOW)
+            out_ref[part, group, 1] = grad_values[rows].astype(LOW)
+    part_ref[...] = dot(grad_q_ref[...], q_ref[...], 1, 1).astype(LOW)
+
+
+def attend_back(grad, proj, own_head, queries, probs, cosine, sine, cosine_all, sine_all):
+    count, groups, _, tok_rows, head = own_head.shape
+    sel, width = grad.shape
+    size = queries.shape[1]
+    first = 2 * KVH * HD // size
+    return local_call(
+        attend_back_body,
+        [grad, proj, proj, own_head, queries, probs, cosine, sine, cosine_all, sine_all],
+        [entire(grad), column_block(proj, size, first), column_block(proj, size, first + 1)]
+        + [
+            entire(a)
+            for a in (own_head, queries, probs, cosine, sine, cosine_all, sine_all)
+        ],
+        [struct(own_head.shape, LOW), struct((sel, size), LOW), struct((sel, width), LOW)],
+        8 * sel * size * width,
+        "attend_back",
+    )
+
+
+def norm_back_rows(values, gain_row, grad):
+    root = lax.rsqrt(jnp.mean(values * values, axis=-1, keepdims=True) + NORM_EPS)
+    scaled = gain_row * grad
+    inner = jnp.mean(values * scaled, axis=-1, keepdims=True)
+    result = root * scaled - values * (root * root * root * inner)
+    return result, jnp.sum(values * root * grad, axis=0, keepdims=True)
+
+
+def rows_back_body(
+    rep,
+    rows_ref,
+    gains_ref,
+    kv_ref,
+    heads_ref,
+    pick_ref,
+    early_ref,
+    base_ref,
+    out_ref,
+    attn_gain_ref,
+    early_gain_ref,
+    grad_kv_ref,
+):
+    count, groups, _, tok_rows, head = heads_ref.shape
+    size = kv_ref.shape[1] // (2 * count)
+    per_head = head // size
+    for index in range(KVH):
+        for kind in range(2):
+            copies = [
+                heads_ref[at // groups, at % groups, kind]
+                for at in range(index * rep, (index + 1) * rep)
+            ]
+            total = copies[0]
+            if rep > 1:
+                total = sum(copy.astype(FULL) for copy in copies).astype(LOW)
+            for piece in range(per_head):
+                lane = (2 * (index * per_head + piece) + kind) * size
+                grad_kv_ref[:, lane : lane + size] = total[:, piece * size : (piece + 1) * size]
+    values = rows_ref[...].astype(FULL)
+    own = values[tok_rows:]
+    tok_part, tok_gain = norm_back_rows(
+        values[:tok_rows], gains_ref[0:1, :], dot(grad_kv_ref[...], kv_ref[...], 1, 1)
+    )
+    pick_part, pick_gain = norm_back_rows(own, gains_ref[0:1, :], pick_ref[...])
+    early_part, early_gain = norm_back_rows(own, gains_ref[2:3, :], early_ref[...])
+    attn_gain_ref[...] = tok_gain + pick_gain
+    early_gain_ref[...] = early_gain
+    out_ref[0:tok_rows, :] = tok_part.astype(LOW)
+    out_ref[tok_rows:, :] = (pick_part + early_part + base_ref[...]).astype(LOW)
+
+
+def rows_back(rows_low, gains, proj, heads, grad_pick, grad_early, base, rep):
+    tok_rows = heads.shape[3]
+    width = rows_low.shape[1]
+    size = 2 * KVH * HD
+    return local_call(
+        functools.partial(rows_back_body, rep),
+        [rows_low, gains, proj, heads, grad_pick, grad_early, base],
+        [entire(rows_low), entire(gains), column_block(proj, size, 0)]
+        + [entire(a) for a in (heads, grad_pick, grad_early, base)],
+        [
+            struct(rows_low.shape, LOW),
+            struct((1, width), FULL),
+            struct((1, width), FULL),
+            struct((tok_rows, size), LOW),
+        ],
+        2 * tok_rows * width * size,
+        "rows_back",
+    )
+
+
+def assemble_body(out_columns, *refs):
+    pieces, out_ref = refs[:-1], refs[-1]
+    count = len(pieces)
+    me = lax.axis_index("narrow")
+    for step, piece in enumerate(pieces):
+        source = lax.rem(me - step + count, count)
+        spot = pl.ds(pl.multiple_of(source * out_columns, out_columns), out_columns)
+        out_ref[:, spot] = piece[...]
+
+
+def assemble(pieces):
+    rows, columns = pieces[0].shape
+    outputs = [struct((rows, columns * len(pieces)), pieces[0].dtype)]
+    return local_call(
+        functools.partial(assemble_body, columns),
+        list(pieces),
+        [entire(piece) for piece in pieces],
+        outputs,
+        0,
+        "assemble",
+    )[0]
+
+
 def feed_body(inner_ref, weight_ref, gate_ref, up_ref, hidden_ref, out_ref, total):
     part = pl.program_id(0)
     inner = inner_ref[...]
@@ -1405,20 +1691,29 @@
         jnp.where(pick_ids[:, None] == where_at[None, :], tokens[0][None, :], 0), axis=1
     )
     ints = box(jnp.concatenate([tokens[0], pick_tokens, targets[0]]))
-    all_ints, all_gains, kv_part, ffn_sub = launch(
+    all_ints, all_gains, kv_part = launch(
         [
             gather_wide(ints),
             gather_both(box(gains.astype(LOW).astype(FULL).reshape(-1))),
             gather_blocks("narrow", kv_own),
-            join_columns("narrow", ffn_cut),
         ],
         0,
         "gather_ids",
     )
     kv_part = jnp.moveaxis(kv_part, 0, 1).reshape(columns, -1)
-    proj_own = jnp.concatenate([attn_qo.reshape(columns, -1).astype(LOW), kv_part], axis=1)
+    proj_own = jnp.concatenate([kv_part, attn_qo.reshape(columns, -1).astype(LOW)], axis=1)
     proj = lax.all_gather(proj_own, "wide", axis=0, tiled=True)
-    ffn_w = lax.all_gather(ffn_sub.reshape(3, ffn_size, width), "wide", axis=0)
+    ffn_cut, all_ints = lax.optimization_barrier((ffn_cut, all_ints))
+    ffn_pieces = [lax.dynamic_index_in_dim(ffn_cut, narrow_spot, 0, False)] + [
+        shifted(
+            lax.dynamic_index_in_dim(
+                ffn_cut, lax.rem(narrow_spot + step, narrow_count), 0, False
+            ),
+            "narrow",
+            step,
+        )
+        for step in range(1, narrow_count)
+    ]
     gain_size = gains.shape[1]
     gain_w = all_gains.reshape(narrow_count, wide_count, -1)[:, :, : 3 * gain_size]
     gain_w = gain_w.reshape(narrow_count, wide_count, 3, gain_size)
@@ -1432,6 +1727,10 @@
     inside = (local_ids >= 0) & (local_ids < vocab_rows)
     spots = jnp.where(inside, local_ids, vocab_rows)
     found, embed_low, listed = lookup(embed, spots)
+    ffn_pieces, found = lax.optimization_barrier((ffn_pieces, found))
+    ffn_sub = assemble(ffn_pieces).reshape(3, ffn_size, width)
+    ffn_sub, found = lax.optimization_barrier((ffn_sub, found))
+    ffn_w = lax.all_gather(ffn_sub, "wide", axis=0)
     found = found.reshape(narrow_count, wide_count * all_rows, columns)
     embed_cut = embed_low.reshape(wide_count, vocab_rows // wide_count, columns)
     rows_low, table_own = launch(
@@ -1451,28 +1750,17 @@
     small_box = jnp.pad(small_box, ((0, slot_rows - small_box.shape[0]), (0, 0)))
     mom_parts = jnp.concatenate([mom_ffn, small_box[None]]).astype(LOW)
 
-    seg_all = segments_at(lens, where_at)
-    tok_at = narrow_spot * tok_rows + jnp.arange(tok_rows, dtype=jnp.int32)
-    _, cosine_all, sine_all = angles_at(lens, where_at)
-    _, cosine_tok, sine_tok = angles_at(lens, tok_at)
+    seg_all, cosine_all, sine_all = angles_at(lens, where_at)
+    cosine_all, sine_all = wide_angles(cosine_all, sine_all)
     seg_mine, cosine, sine = angles_at(lens, pick_ids)
-
-    q_w, o_w, kv_w = (
-        proj[:, :head_cols],
-        proj[:, head_cols : 2 * head_cols],
-        proj[:, 2 * head_cols :],
-    )
-
-    rows_full = rows_low.astype(FULL)
-    normed_all = norm_rows(rows_full, gain_w[0]).astype(LOW)
-    normed_tok, normed_own = normed_all[:tok_rows], normed_all[tok_rows:]
-    kv_part = dot(normed_tok, kv_w, 1, 0).reshape(tok_rows, narrow_count, 2, kv_size)
-    kv_part = jnp.moveaxis(kv_part, 2, 0).reshape(2, tok_rows, KVH, HD)
-    keys_part = rotate(kv_part[0], cosine_tok[:, None], sine_tok[:, None]).astype(LOW)
-    values_part = kv_part[1].astype(LOW)
-    by_head = jnp.moveaxis(jnp.stack([keys_part, values_part]), 2, 0)
-    by_head = jnp.repeat(by_head, repeat, axis=0)
-    by_head = by_head.reshape(narrow_count, groups, 2, tok_rows, HD)
+    cosine, sine = wide_angles(cosine, sine)
+
+    def tok_part(angles):
+        return lax.dynamic_slice_in_dim(angles, narrow_spot * tok_rows, tok_rows, 0)
+
+    by_head, normed_tok = make_heads(
+        rows_low, gain_w[0:1], proj, tok_part(cosine_all), tok_part(sine_all), groups, repeat
+    )
     own_head, start_low, tok_cols = launch(
         [
             swap_blocks("narrow", by_head),
@@ -1483,31 +1771,24 @@
         "trade_heads",
     )
     start_low, ffn_w = lax.optimization_barrier((start_low, ffn_w))
-    own_head = jnp.transpose(own_head, (2, 1, 0, 3, 4)).reshape(2, groups, seq_len, HD)
-    keys, values = own_head[0], own_head[1]
-    start_h = start_low.reshape(sel, width).astype(FULL)
-
-    normed = norm_rows(start_h, gain_w[0]).astype(LOW)
-    queries = dot(normed, q_w, 1, 0).reshape(sel, heads_own, HD)
-    queries = rotate(queries, cosine[:, None], sine[:, None]).astype(LOW)
-    grouped = queries.reshape(sel, groups, heads_own // groups, HD)
-    scale = HD ** (-0.5)
-    scores = jnp.einsum("tkgd,ksd->kgts", grouped, keys, preferred_element_type=FULL) * scale
-    allowed = (seg_mine[:, None] == seg_all[None, :]) & (pick_ids[:, None] >= where_at[None, :])
-    scores = jnp.where(allowed, scores, MASKED)
-    shifted_exp = jnp.exp(scores - jnp.max(scores, axis=-1, keepdims=True))
-    probs = shifted_exp / jnp.sum(shifted_exp, axis=-1, keepdims=True)
-    probs_low = probs.astype(LOW)
-    mixed = jnp.einsum("kgts,ksd->tkgd", probs_low, values, preferred_element_type=FULL)
-    mixed = mixed.reshape(sel, head_cols).astype(LOW)
-
-    early_part = norm_rows(start_h, gain_w[2]).astype(LOW)
+    start_low = start_low.reshape(sel, width)
+    queries, probs, mixed, attn_part, normed, early_part = attend(
+        start_low,
+        gain_w,
+        proj,
+        own_head,
+        cosine,
+        sine,
+        seg_mine[:, None],
+        seg_all[None, :],
+        pick_ids[:, None],
+    )
     early = lax.all_gather(early_part, "wide", axis=0, tiled=True)
-    start_own = lax.dynamic_slice_in_dim(start_h, narrow_spot * own_rows, own_rows, 0)
+    start_own = rows_low[tok_rows:].astype(FULL)
     middle, inner, mixed_wide, pick_cols = launch(
         [
             settle(
-                dot(mixed, o_w, 1, 1).astype(LOW),
+                attn_part,
                 start_own,
                 start_own,
                 jnp.ones((1, width), FULL),
@@ -1569,10 +1850,11 @@
         return dot(grad_logits, table_own, 1, 0).astype(LOW), dot(grad_logits, features, 0, 0)
 
     late_back, late_head = exit_back(late_logits, log_norms[total_rows:], EXIT_LAST, late)
-    early_back, early_head = exit_back(early_logits, log_norms[:total_rows], EXIT_EARLY, early)
     grad_late, mom_low = launch(
         [sum_wide(late_back), swap_turned(mom_parts[:, half:])], 7, "sum_late"
     )
+    early_norms, grad_late = lax.optimization_barrier((log_norms[:total_rows], grad_late))
+    early_back, early_head = exit_back(early_logits, early_norms, EXIT_EARLY, early)
     mom_owned = jnp.concatenate([mom_top, mom_low], axis=1)
     grad_head = (early_head + late_head).astype(LOW)
 
@@ -1600,30 +1882,9 @@
     grad_branch, grad_early = lax.optimization_barrier((grad_branch, grad_early))
     grad_branch = grad_branch.reshape(sel, width)
 
-    grad_mixed = dot(grad_branch, o_w, 1, 0).astype(LOW)
-    grouped_grad = grad_mixed.reshape(sel, groups, heads_own // groups, HD)
-    grad_probs = jnp.einsum("tkgd,ksd->kgts", grouped_grad, values, preferred_element_type=FULL)
-    grad_scores = (
-        probs * (grad_probs - jnp.sum(probs * grad_probs, axis=-1, keepdims=True))
-    ).astype(LOW)
-    grad_queries = (
-        jnp.einsum("kgts,ksd->tkgd", grad_scores, keys, preferred_element_type=FULL) * scale
-    ).reshape(sel, heads_own, HD)
-    grad_queries = (
-        unrotate(grad_queries, cosine[:, None], sine[:, None])
-        .reshape(sel, head_cols)
-        .astype(LOW)
-    )
-    grad_keys = jnp.einsum("kgts,tkgd->ksd", grad_scores, grouped, preferred_element_type=FULL)
-    grad_keys = unrotate(grad_keys * scale, cosine_all, sine_all).astype(LOW)
-    grad_values = jnp.einsum(
-        "kgts,tkgd->ksd", probs_low, grouped_grad, preferred_element_type=FULL
-    ).astype(LOW)
-    kv_parts = jnp.stack([grad_keys, grad_values]).reshape(
-        2, groups, narrow_count, tok_rows, HD
-    )
-    kv_parts = jnp.transpose(kv_parts, (2, 1, 0, 3, 4))
-    pick_part = dot(grad_queries, q_w, 1, 1).astype(LOW)
+    kv_parts, grad_queries, pick_part = attend_back(
+        grad_branch, proj, own_head, queries, probs, cosine, sine, cosine_all, sine_all
+    )
     grad_kv, grad_pick, grad_early, acts, queries_wide, branch_cols = launch(
         [
             swap_blocks("narrow", kv_parts),
@@ -1636,18 +1897,11 @@
         10,
         "trade_grads",
     )
-    grad_start_exit, gain_early = norm_back(start_own, gain_w[2], grad_early)
-    grad_kv = grad_kv.reshape(KVH, repeat, 2, tok_rows, HD)
-    if repeat > 1:
-        grad_kv = jnp.sum(grad_kv.astype(FULL), axis=1, keepdims=True).astype(LOW)
-    grad_kv = grad_kv[:, 0]
-    kv_rows = jnp.transpose(grad_kv, (1, 2, 0, 3)).reshape(2, tok_rows, narrow_count, kv_size)
-    kv_rows = jnp.moveaxis(kv_rows, 0, 2).reshape(tok_rows, -1)
-    grad_kv, out_all = lax.optimization_barrier((kv_rows, out_all))
-    grad_normed = jnp.concatenate([dot(grad_kv, kv_w, 1, 1), grad_pick])
-    grad_rows, gain_attn = norm_back(rows_full, gain_w[0], grad_normed)
-    grad_pass = grad_mid + grad_start_exit + grad_final * (1.0 - keep_layer)
-    grad_rows = jnp.concatenate([grad_rows[:tok_rows], grad_rows[tok_rows:] + grad_pass])
+    grad_kv, out_all = lax.optimization_barrier((grad_kv, out_all))
+    grad_base = grad_mid + grad_final * (1.0 - keep_layer)
+    grad_rows, gain_attn, gain_early, grad_kv = rows_back(
+        rows_low, gain_w, proj, grad_kv, grad_pick, grad_early, grad_base, repeat
+    )
     acts = jnp.moveaxis(acts, 1, 0).reshape(3, total_rows, ffn_size)
     rights = (inner_all, inner_all, out_all)
     grad_ffn = [dot(acts[j], rights[j], 0, 0) for j in range(3)]
@@ -1664,7 +1918,7 @@
     for_owners = jnp.stack([part.astype(LOW) for part in grad_ffn] + [qo_box])
     grad_rows, owned, kv_wide, head_cols_all = launch(
         [
-            return_rows(grad_rows.astype(LOW)),
+            return_rows(grad_rows),
             swap_turned(for_owners, 5),
             later(gather_wide(grad_kv, 3), 2),
             later(split_columns("wide", grad_head, 3), 2),
@@ -1702,7 +1956,7 @@
         + jnp.sum(table_squares)
     )
     sums = jnp.stack(
-        [gain_attn, gain_mid[0], gain_early + gain_late[0], jnp.full((width,), squares)]
+        [gain_attn[0], gain_mid[0], gain_early[0] + gain_late[0], jnp.full((width,), squares)]
     )
     sums, summed_ffn = lax.optimization_barrier((sums, summed_ffn))
     summed_ffn = summed_ffn.reshape(3, ffn_rows, size).astype(FULL)

time: 1130 us -> 1070 us (0.947)
  matrix products: 88.1 us -> 67.7 us
  Pallas kernels: 784 us -> 765 us
    pallas_call x13, Pallas kernels: 665 us -> 606 us  [launch(): pl.pallas_call(body, out_shape=outputs, in_specs=[place for task in tasks...]
    pallas_call x0 -> x5, Pallas kernels: none -> 28.5 us  [local_call(): pl.pallas_call(body, grid=(1,), in_specs=specs, out_specs=[pl.BlockSpec(a...]
    dot_general x16 -> x10, matrix products: 77.5 us -> 61 us  [dot(): lax.dot_general(first, second, (((first_dim,), (second_dim,)), ((), ())),...]
    ppermute x6 -> x9, waiting for transfers between devices: 43.9 us -> 38.7 us  [shifted(): return lax.ppermute(parts, axis, pairs)]
    unnamed x181 -> x100, local copies, waits for them, and re-layouts: 26.7 us -> 22.5 us
  transfers between devices with their start and end apart: 13 -> 16, of which waited for: 5 -> 6; matrix products, arithmetic and copies ran while one was open for 15% -> 13% of each run, Pallas kernels for 44% -> 44%
where the time goes in v7:
time: 1070 us; the launch traced here: 1060 us
  Pallas kernels  765 us (71%)
  other arithmetic  84.7 us (8%)
  matrix products  67.7 us (6%)
  local copies, waits for them, and re-layouts  62.5 us (6%)
  waiting for transfers between devices  39.4 us (4%)
  between operations  24.6 us (2%)
  starting transfers between devices  11 us (1%)
    pallas_call x13, Pallas kernels, launch(): pl.pallas_call(body, out_shape=outputs, in_specs=[place for task in tasks...  606 us
    dot_general x10, matrix products, dot(): lax.dot_general(first, second, (((first_dim,), (second_dim,)), ((), ())),...  61 us
    pallas_call x1, Pallas kernels, newton(): pl.pallas_call(newton_body, in_specs=[pl.BlockSpec(memory_space=pltpu.SME...  46 us
    ppermute x9, waiting for transfers between devices, shifted(): return lax.ppermute(parts, axis, pairs)  38.7 us
    pallas_call x1, Pallas kernels, lookup(): pl.pallas_call(lookup_body, in_specs=[pl.BlockSpec(memory_space=pltpu.SME...  32.3 us
    pallas_call x5, Pallas kernels, local_call(): pl.pallas_call(body, grid=(1,), in_specs=specs, out_specs=[pl.BlockSpec(a...  28.5 us
    pallas_call x1, Pallas kernels, spread(): pl.pallas_call(spread_body, in_specs=[smem, smem, VMEM, VMEM], out_specs=...  24.3 us
    sub x2, other arithmetic, adamw(): weight * (1.0 - rate * decay) - rate * update  22.8 us
  transfers between devices with their start and end apart: 16, of which 6 were waited for; matrix products, arithmetic and copies ran while one was open for 13% of the time, Pallas kernels for 44%

profile of v7, /device:TPU:17, one launch (start us, length us, event | category | flops | bytes accessed | tf_op | source)
XLA Modules:
  0.0 1055.4 jit_solution(16858097831618911524)
XLA Ops:
  14.2 18.9 %gather_ids.1 = (s32[8,16,128]{2,1,0:T(8,128)}, f32[4,8,8,128]{3,2,1,0:T(8,128)}, bf16[4,256,256]{2,1,0:T(8,128)(2,1)}) custom-call(s32[16,128]{1,0:T(8,128)} %pad_bitcast_fusion.1.refs_0_, f32[8,128]{1,0:T(8,128)} %bitcast_convert_fusion.refs_1_, bf16[256,256]{1,0:T(8,128)(2,1)} %bitcast.286), custom_call_target="tpu_custom_call" | custom-call | bytes 108032 | tf_op jit(solution)/shard_map/gather_ids/pallas_call | solution.py:139
  35.4 2.5 convert_element_type.142
  39.2 1.9 collective-permute-start
  46.9 32.3 %lookup.1 = (bf16[9216,256]{1,0:T(8,128)(2,1)}, bf16[8192,256]{1,0:T(8,128)(2,1)}, s32[9248]{0:T(1024)}) custom-call(s32[9216]{0:T(1024)} %and_select_fusion.ids_ref, s32[9344]{0:T(1024)} %concatenate.41.turn_ref, f32[8192,256]{1,0:T(8,128)} %table_ref.1), custom_call_target="tpu_custom_call" | custom-call | bytes 8388608 | tf_op jit(solution)/shard_map/lookup/pallas_call | solution.py:1522
  79.3 9.8 collective-permute-done.2.refs_3_
  89.8 3.1 assemble.1
  97.8 1.9 multiply_sine_fusion
  100.6 135.2 %fetch_rows.1 = (bf16[288,2048]{1,0:T(8,128)(2,1)}, bf16[1024,2048]{1,0:T(8,128)(2,1)}) custom-call(bf16[4,2304,256]{2,1,0:T(8,128)(2,1)} %bitcast.256, bf16[8,1024,256]{2,1,0:T(8,128)(2,1)} %bitcast.258), custom_call_target="tpu_custom_call" | custom-call | bytes 1785856 | tf_op jit(solution)/shard_map/fetch_rows/pallas_call | solution.py:139
  235.8 1.7 slice_convert_fusion
  237.5 5.0 make_heads.1
  242.5 25.3 %trade_heads.1 = (bf16[4,1,2,256,128]{4,3,2,1,0:T(8,128)(2,1)}, bf16[4,32,2048]{2,1,0:T(8,128)(2,1)}, bf16[8,256,256]{2,1,0:T(8,128)(2,1)}) custom-call(bf16[4,1,2,256,128]{4,3,2,1,0:T(8,128)(2,1)} %get-tuple-element.138.refs_0_, bf16[32,2048]{1,0:T(8,128)(2,1)} %get-tuple-element.331.refs_1_, bf16[256,2048]{1,0:T(8,128)(2,1)} %get-tuple-element.139.refs_2_), custom_call_target="tpu_custom_call" | custom-call | bytes 475136 | tf_op jit(solution)/shard_map/trade_heads/pallas_call | solution.py:139
  267.8 6.9 attend.1
  276.1 28.1 %settle_middle.1 = (f32[32,2048]{1,0:T(8,128)}, bf16[4,32,2048]{2,1,0:T(8,128)(2,1)}, bf16[8,128,512]{2,1,0:T(8,128)(2,1)}, bf16[8,128,256]{2,1,0:T(8,128)(2,1)}) custom-call(bf16[4,32,2048]{2,1,0:T(8,128)(2,1)} %bitcast.282, f32[32,2048]{1,0:T(8,128)} %get-tuple-element.330.refs_1_.refs_2_, f32[32,2048]{1,0:T(8,128)} %get-tuple-element.330.refs_1_.refs_2_, ...), custom_call_target="tpu_custom_call" | custom-call | bytes 509952 | tf_op jit(solution)/shard_map/settle_middle/pallas_call | solution.py:139
  306.4 2.5 convert_bitcast_fusion
  308.9 1.9 pad_maximum_fusion.2
  310.8 13.4 %feed.1 = (f32[8,128,176]{2,1,0:T(8,128)}, f32[8,128,176]{2,1,0:T(8,128)}, bf16[8,128,176]{2,1,0:T(8,128)(2,1)}, bf16[128,2048]{1,0:T(8,128)(2,1)}) custom-call(bf16[128,2048]{1,0:T(8,128)(2,1)} %bitcast.264, bf16[8,3,176,2048]{3,2,1,0:T(8,128)(2,1)} %bitcast.250), custom_call_target="tpu_custom_call" | custom-call | flops 2214592512 | bytes 17301504 | tf_op jit(solution)/shard_map/feed/pallas_call | solution.py:1227
  324.8 29.1 %settle_late.1 = (f32[32,2048]{1,0:T(8,128)}, bf16[4,32,2048]{2,1,0:T(8,128)(2,1)}) custom-call(bf16[4,32,2048]{2,1,0:T(8,128)(2,1)} %bitcast.284, f32[32,2048]{1,0:T(8,128)} %get-tuple-element.152.refs_1_, f32[32,2048]{1,0:T(8,128)} %get-tuple-element.330.refs_1_.refs_2_, f32[1,2048]{1,0:T(1,128)} %broadcast_in_dim.139.refs_3_, f32[1,2048]{1,0:T(1,128)} %slice.123.refs_4_), custom_call_target="tpu_custom_call" | custom-call | bytes 231424 | tf_op jit(solution)/shard_map/settle_late/pallas_call | solution.py:139
  353.9 34.6 %gather_late.1 = (bf16[8,128,2048]{2,1,0:T(8,128)(2,1)}, bf16[4,352,512]{2,1,0:T(8,128)(2,1)}) custom-call(bf16[128,2048]{1,0:T(8,128)(2,1)} %bitcast.289, bf16[4,352,512]{2,1,0:T(8,128)(2,1)} %get-tuple-element.313.refs_1_), custom_call_target="tpu_custom_call" | custom-call | bytes 950272 | tf_op jit(solution)/shard_map/gather_late/pallas_call | solution.py:139
  388.6 8.3 fusion.51
  396.9 7.8 fusion.50
  404.7 2.2 exponential_reduce_fusion.1
  407.5 13.6 %combine_stats.1 = f32[3,8,256]{2,1,0:T(8,128)} custom-call(f32[3,8,256]{2,1,0:T(8,128)} %bitcast.304), custom_call_target="tpu_custom_call" | custom-call | bytes 6144 | tf_op jit(solution)/shard_map/combine_stats/pallas_call | solution.py:139
  421.9 10.2 convolution_convert_fusion.1
  432.2 37.3 %sum_late.1 = (f32[128,2048]{1,0:T(8,128)}, bf16[4,352,512]{2,1,0:T(8,128)(2,1)}) custom-call(bf16[8,128,2048]{2,1,0:T(8,128)(2,1)} %bitcast.259, bf16[4,352,512]{2,1,0:T(8,128)(2,1)} %get-tuple-element.312.refs_1_), custom_call_target="tpu_custom_call" | custom-call | bytes 1015808 | tf_op jit(solution)/shard_map/sum_late/pallas_call | solution.py:139
  469.5 8.5 convolution_convert_fusion
  480.8 26.4 %back_late.1 = (f32[32,2048]{1,0:T(8,128)}, f32[1,2048]{1,0:T(1,128)}, bf16[4,32,2048]{2,1,0:T(8,128)(2,1)}) custom-call(bf16[4,32,2048]{2,1,0:T(8,128)(2,1)} %bitcast.265, f32[32,2048]{1,0:T(8,128)} %get-tuple-element.158.refs_1_, f32[32,2048]{1,0:T(8,128)} %broadcast_in_dim.141.refs_2_, f32[1,2048]{1,0:T(1,128)} %broadcast_in_dim.139.refs_3_, ...), custom_call_target="tpu_custom_call" | custom-call | bytes 232448 | tf_op jit(solution)/shard_map/back_late/pallas_call | solution.py:139
  508.6 14.9 %feed_back.1 = (bf16[8,3,128,176]{3,2,1,0:T(8,128)(2,1)}, bf16[128,2048]{1,0:T(8,128)(2,1)}) custom-call(bf16[128,2048]{1,0:T(8,128)(2,1)} %bitcast.262, bf16[8,3,176,2048]{3,2,1,0:T(8,128)(2,1)} %bitcast.251, f32[8,128,176]{2,1,0:T(8,128)} %get-tuple-element.160.gate_ref, f32[8,128,176]{2,1,0:T(8,128)} %get-tuple-element.161.up_ref, ...), custom_call_target="tpu_custom_call" | custom-call | flops 2214592512 | bytes 17301504 | tf_op jit(solution)/shard_map/feed_back/pallas_call | solution.py:1279
  524.3 29.4 %back_middle.1 = (f32[32,2048]{1,0:T(8,128)}, f32[1,2048]{1,0:T(1,128)}, bf16[4,32,2048]{2,1,0:T(8,128)(2,1)}) custom-call(bf16[4,32,2048]{2,1,0:T(8,128)(2,1)} %bitcast.283, f32[32,2048]{1,0:T(8,128)} %get-tuple-element.152.refs_1_, f32[32,2048]{1,0:T(8,128)} %broadcast_multiply_fusion.refs_2_, f32[1,2048]{1,0:T(1,128)} %broadcast_in_dim.139.refs_3_, ...), custom_call_target="tpu_custom_call" | custom-call | bytes 232448 | tf_op jit(solution)/shard_map/back_middle/pallas_call | solution.py:139
  555.3 9.2 fusion.39
  564.5 9.0 add_convert_fusion.refs_3_
  573.6 7.4 attend_back.1
  581.0 39.8 %trade_grads.1 = (bf16[4,1,2,256,128]{4,3,2,1,0:T(8,128)(2,1)}, f32[32,2048]{1,0:T(8,128)}, f32[32,2048]{1,0:T(8,128)}, bf16[8,3,128,176]{3,2,1,0:T(8,128)(2,1)}...) custom-call(bf16[4,1,2,256,128]{4,3,2,1,0:T(8,128)(2,1)} %get-tuple-element.170.refs_0_, ...), custom_call_target="tpu_custom_call" | custom-call | bytes 876544 | tf_op jit(solution)/shard_map/trade_grads/pallas_call | solution.py:139
  626.6 1.7 multiply_reduce_fusion.1
  628.3 1.7 multiply_reduce_fusion.2
  630.0 4.3 multiply_reduce_fusion
  634.4 2.0 pad_maximum_fusion.refs_1_
  636.4 6.0 rows_back.1
  642.3 163.6 %return_rows.1 = (bf16[4,2304,256]{2,1,0:T(8,128)(2,1)}, bf16[4,176,2048]{2,1,0:T(8,128)(2,1)}, bf16[8,256,1024]{2,1,0:T(8,128)(2,1)}, bf16[8,1024,256]{2,1,0:T(8,128)(2,1)}) custom-call(bf16[288,2048]{1,0:T(8,128)(2,1)} %get-tuple-element.189.refs_0_, bf16[4,176,2048]{2,1,0:T(8,128)(2,1)} %pad_maximum_fusion.refs_1_, ...), custom_call_target="tpu_custom_call" | custom-call | bytes 3096576 | tf_op jit(solution)/shard_map/return_rows/pallas_call | solution.py:139
  806.0 3.5 convolution_bitcast_fusion
  811.6 6.0 copy.176
  818.8 1.8 pad_maximum_fusion.1
  822.6 2.6 constant_dynamic-update-slice_fusion
  831.0 24.3 %spread.1 = (f32[8192,256]{1,0:T(8,128)}, f32[8,256]{1,0:T(8,128)}) custom-call(s32[9216]{0:T(1024)} %and_select_fusion.ids_ref, s32[9248]{0:T(1024)} %get-tuple-element.195.list_ref, bf16[9216,256]{1,0:T(8,128)(2,1)} %bitcast.255, bf16[8192,256]{1,0:T(8,128)(2,1)} %bitcast.257), custom_call_target="tpu_custom_call" | custom-call | flops 2359296 | bytes 16777216 | tf_op jit(solution)/shard_map/spread/pallas_call | solution.py:1596
  857.3 1.9 bitcast_dynamic-update-slice_fusion.2
  859.2 2.3 collective-permute-done.4
  861.5 1.9 bitcast_dynamic-update-slice_fusion.1
  863.4 1.8 copy.165
  865.2 7.8 collective-permute-done.5
  874.7 2.3 fusion.48
  879.7 24.5 %combine_sums.1 = (f32[4,8,256]{2,1,0:T(8,128)}, bf16[4,512,128]{2,1,0:T(8,128)(2,1)}) custom-call(f32[4,8,256]{2,1,0:T(8,128)} %bitcast.301, bf16[512,128]{1,0:T(8,128)(2,1)} %bitcast.281), custom_call_target="tpu_custom_call" | custom-call | bytes 90112 | tf_op jit(solution)/shard_map/combine_sums/pallas_call | solution.py:139
  909.7 2.5 bitcast_add_fusion.1
  912.2 46.2 %conditional.1 = (bf16[4,704,512]{2,1,0:T(8,128)(2,1)}) conditional(s32[]{:T(128)} %convert_element_type.177, (f32[]{:T(128)}, bf16[4,176,2048]{2,1,0:T(8,128)(2,1)}, bf16[4,704,512]{2,1,0:T(8,128)(2,1)}) %tuple.34, (f32[]{:T(128)}, bf16[4,704,512]{2,1,0:T(8,128)(2,1)}, bf16[4,176,2048]{2,1,0:T(8,128)(2,1)}, bf16[4,512,128]{2,1,0:T(8,128)(2,1)}) %tuple.35), branch_computations={%region_26.27_spmd, %region_27.28_spmd} | conditional | flops 23789568000 | bytes 8650760 | solution.py:1986
  912.2 46.0 %newton.1 = bf16[4,704,512]{2,1,0:T(8,128)(2,1)} custom-call(f32[1]{0:T(128)} %bitcast.factor_ref, bf16[4,704,512]{2,1,0:T(8,128)(2,1)} %get-tuple-element.18.mom_ref, bf16[704,2048]{1,0:T(8,128)(2,1)} %bitcast.330), custom_call_target="tpu_custom_call" | custom-call | flops 23789568000 | bytes 8650752 | tf_op jit(solution)/shard_map/cond/branch_0_fun/newton/pallas_call | solution.py:1400
  958.4 3.5 constant_dynamic-slice_fusion.1
  962.3 2.5 collective-permute-start.7
  964.8 1.7 collective-permute-start.8
  966.5 2.3 copy.167
  968.8 1.8 copy.186
  972.5 2.7 convert_multiply_fusion
  975.2 22.1 %multiply_subtract_fusion = (f32[8192,256]{1,0:T(8,128)}, f32[8192,256]{1,0:T(8,128)}, f32[8192,256]{1,0:T(8,128)}) fusion(f32[8192,256]{1,0:T(8,128)} %table_ref.1, f32[8192,256]{1,0:T(8,128)} %get-tuple-element.203, f32[]{:T(128)} %div.51, f32[8192,256]{1,0:T(8,128)} %param.25, f32[8192,256]{1,0:T(8,128)} %param.26), kind=kLoop, calls=%fused_computation.2 | loop fusion | flops 31457280 | bytes 58720260 | tf_op jit(solution)/shard_map/sub | solution.py:1623
  998.0 6.7 bitcast_add_fusion
  1006.1 18.1 %collective-permute-done.7 = bf16[704,512]{1,0:T(8,128)(2,1)} collective-permute-done((bf16[704,512]{1,0:T(8,128)(2,1)}, bf16[704,512]{1,0:T(8,128)(2,1)}, u32[]{:S(2)}, u32[]{:S(2)}) %collective-permute-start.7) | collective-permute-done | bytes 720928 | tf_op jit(solution)/shard_map/ppermute | solution.py:1634
  1035.7 5.7 bitcast_subtract_fusion
  1041.3 5.9 copy.189
  (229 shorter events, 71.2 us)
Async XLA Ops:
  7.2 230.3 %all-gather.7.cloned.1.call-start = ((), (), s32[]{:S(2)}) async-start(), calls=%async_computation.2 | async-start | bytes 9437184 | tf_op jit(solution)/shard_map/all_gather | solution.py:1705
  35.3 232.5 %all-gather.15.cloned.1.call-start = ((), (), s32[]{:S(2)}) async-start(), calls=%async_computation.8 | async-start | bytes 19464192 | tf_op jit(solution)/shard_map/all_gather | solution.py:1733
  37.9 5.8 copy-start.27
  39.2 40.0 %collective-permute-start = (bf16[528,512]{1,0:T(8,128)(2,1)}, bf16[528,512]{1,0:T(8,128)(2,1)S(1)}, u32[]{:S(2)}, u32[]{:S(2)}) collective-permute-start(bf16[528,512]{1,0:T(8,128)(2,1)} %get-tuple-element.319), channel_id=1, source_target_pairs={{0,1},{1,2},{2,3},{3,0},{4,5},{5,6},{6,7},{7,4},{8,9},{9,10},{10,1... | collective-permute-start | bytes 1622024 | tf_op jit(solution)/shard_map/ppermute | solution.py:1634
  41.1 38.2 %collective-permute-start.1 = (bf16[528,512]{1,0:T(8,128)(2,1)S(1)}, bf16[528,512]{1,0:T(8,128)(2,1)S(1)}, u32[]{:S(2)}, u32[]{:S(2)}) collective-permute-start(bf16[528,512]{1,0:T(8,128)(2,1)S(1)} %get-tuple-element.318), channel_id=1, source_target_pairs={{0,2},{1,3},{2,0},{3,1},{4,6},{5,7},{6,4},{7,5},{8,10},{9,11},{10,... | collective-permute-start | bytes 1622024 | tf_op jit(solution)/shard_map/ppermute | solution.py:1634
  42.3 46.7 %collective-permute-start.2 = (bf16[528,512]{1,0:T(8,128)(2,1)S(1)}, bf16[528,512]{1,0:T(8,128)(2,1)S(1)}, u32[]{:S(2)}, u32[]{:S(2)}) collective-permute-start(bf16[528,512]{1,0:T(8,128)(2,1)S(1)} %get-tuple-element.317), channel_id=1, source_target_pairs={{0,3},{1,0},{2,1},{3,2},{4,7},{5,4},{6,5},{7,6},{8,11},{9,8},{10,9... | collective-permute-start | bytes 1622024 | tf_op jit(solution)/shard_map/ppermute | solution.py:1634
  79.2 13.8 %copy-start.26 = (f32[4,8,8,128]{3,2,1,0:T(8,128)S(1)}, f32[4,8,8,128]{3,2,1,0:T(8,128)}, u32[]{:S(2)}) copy-start(f32[4,8,8,128]{3,2,1,0:T(8,128)} %get-tuple-element.136) | copy-start | bytes 393220
  79.2 14.8 %copy-start.40 = (s32[1,2]{1,0:T(1,128)S(1)}, s32[1,2]{1,0:T(1,128)}, u32[]{:S(2)}) copy-start(s32[1,2]{1,0:T(1,128)} %param.22) | copy-start | bytes 28
  79.2 15.6 %copy-start.34 = (s32[1,128]{1,0:T(1,128)S(1)}, s32[1,128]{1,0:T(1,128)}, u32[]{:S(2)}) copy-start(s32[1,128]{1,0:T(1,128)} %param.20) | copy-start | bytes 1540
  79.3 9.8 copy-start.22
  79.3 9.8 copy-start.23
  89.0 0.8 copy-start.24
  93.0 303.9 %all-gather.9.cloned.1.call-start = ((), (), s32[]{:S(2)}) async-start(), calls=%async_computation.3 | async-start | bytes 4718592 | tf_op jit(solution)/shard_map/all_gather | solution.py:1786
  96.5 139.2 %copy-start.28 = (s32[1024]{0:T(1024)}, s32[1024]{0:T(1024)S(1)}, u32[]{:S(2)}) copy-start(s32[1024]{0:T(1024)S(1)} %fusion.32) | copy-start | bytes 12292
  267.8 38.0 %copy-start.20 = (f32[256,2,128]{2,1,0:T(2,128)S(1)}, f32[256,2,128]{2,1,0:T(2,128)}, u32[]{:S(2)}) copy-start(f32[256,2,128]{2,1,0:T(2,128)} %param.30) | copy-start | bytes 786436
  274.7 31.2 %copy-start.6 = (f32[256,2,512]{2,1,0:T(2,128)S(1)}, f32[256,2,512]{2,1,0:T(2,128)}, u32[]{:S(2)}) copy-start(f32[256,2,512]{2,1,0:T(2,128)} %param.28) | copy-start | bytes 3145732
  274.8 146.4 %all-gather.11.cloned.1.call-start = ((), (), s32[]{:S(2)}) async-start(), calls=%async_computation.4 | async-start | bytes 4718592 | tf_op jit(solution)/shard_map/all_gather | solution.py:1804
  304.3 269.3 %reduce-scatter.3.cloned.1.call-start = ((), (), s32[]{:S(2)}) async-start(), calls=%async_computation.5 | async-start | bytes 4718592 | tf_op jit(solution)/shard_map/reduce_scatter | solution.py:1861
  310.8 77.8 %copy-start.38 = (bf16[1024,2048]{1,0:T(8,128)(2,1)S(1)}, bf16[1024,2048]{1,0:T(8,128)(2,1)}, u32[]{:S(2)}) copy-start(bf16[1024,2048]{1,0:T(8,128)(2,1)} %get-tuple-element.145) | copy-start | bytes 12582916
  396.9 7.8 copy-start.1
  404.6 2.2 copy-start.3
  432.2 37.3 %copy-start.4 = (f32[1024,1024]{0,1:T(8,128)S(1)}, f32[1024,1024]{0,1:T(8,128)}, u32[]{:S(2)}) copy-start(f32[1024,1024]{0,1:T(8,128)} %copy-done.3) | copy-start | bytes 12582916
  478.0 1.2 copy-start.17
  478.0 152.0 %all-gather.13.cloned.1.call-start = ((), (), s32[]{:S(2)}) async-start(), calls=%async_computation.6 | async-start | bytes 4718592 | tf_op jit(solution)/shard_map/all_gather | solution.py:1877
  507.2 367.5 %reduce-scatter.5.cloned.1.call-start = ((), (), s32[]{:S(2)}) async-start(), calls=%async_computation.7 | async-start | bytes 1310720 | tf_op jit(solution)/shard_map/reduce_scatter | solution.py:1947
  508.6 14.9 %copy-start.19 = (f32[32,2048]{1,0:T(8,128)S(1)}, f32[32,2048]{1,0:T(8,128)}, u32[]{:S(2)}) copy-start(f32[32,2048]{1,0:T(8,128)} %get-tuple-element.164) | copy-start | bytes 786436
  508.6 46.7 %copy-start.5 = (f32[1024,1024]{0,1:T(8,128)S(1)}, f32[1024,1024]{0,1:T(8,128)}, u32[]{:S(2)}) copy-start(f32[1024,1024]{0,1:T(8,128)} %copy-done.3) | copy-start | bytes 12582916
  555.3 9.2 copy-start.2
  555.3 9.2 copy-start.39
  573.6 47.3 %copy-start.18 = (bf16[8,128,512]{2,1,0:T(8,128)(2,1)S(1)}, bf16[8,128,512]{2,1,0:T(8,128)(2,1)}, u32[]{:S(2)}) copy-start(bf16[8,128,512]{2,1,0:T(8,128)(2,1)} %get-tuple-element.187) | copy-start | bytes 3145732
  581.0 41.5 %copy-start.25 = (bf16[8,128,256]{2,1,0:T(8,128)(2,1)S(1)}, bf16[8,128,256]{2,1,0:T(8,128)(2,1)}, u32[]{:S(2)}) copy-start(bf16[8,128,256]{2,1,0:T(8,128)(2,1)} %get-tuple-element.184) | copy-start | bytes 1572868
  620.9 4.0 copy-start.14
  624.2 2.4 copy-start.37
  628.3 6.1 copy-start.11
  630.0 6.3 copy-start.12
  634.4 2.0 copy-start.13
  642.3 163.6 %copy-start.8 = (bf16[8,256,256]{2,1,0:T(8,128)(2,1)S(1)}, bf16[8,256,256]{2,1,0:T(8,128)(2,1)}, u32[]{:S(2)}) copy-start(bf16[8,256,256]{2,1,0:T(8,128)(2,1)} %get-tuple-element.188) | copy-start | bytes 3145732
  811.6 6.0 copy-start.15
  821.8 35.5 %collective-permute-start.3 = (bf16[3,176,512]{2,1,0:T(8,128)(2,1)}, bf16[3,176,512]{2,1,0:T(8,128)(2,1)}, u32[]{:S(2)}, u32[]{:S(2)}) collective-permute-start(bf16[3,176,512]{2,1,0:T(8,128)(2,1)} %get-tuple-element.316), channel_id=1, source_target_pairs={{0,1},{1,2},{2,3},{3,0},{4,5},{5,6},{6,7},{7,4},{8,9},{9,10},{10,1... | collective-permute-start | bytes 1622024 | tf_op jit(solution)/shard_map/ppermute | solution.py:1634
  822.4 39.1 %collective-permute-start.4 = (bf16[3,176,512]{2,1,0:T(8,128)(2,1)}, bf16[3,176,512]{2,1,0:T(8,128)(2,1)}, u32[]{:S(2)}, u32[]{:S(2)}) collective-permute-start(bf16[3,176,512]{2,1,0:T(8,128)(2,1)} %get-tuple-element.315), channel_id=1, source_target_pairs={{0,2},{1,3},{2,0},{3,1},{4,6},{5,7},{6,4},{7,5},{8,10},{9,11},{10,... | collective-permute-start | bytes 1622024 | tf_op jit(solution)/shard_map/ppermute | solution.py:1634
  827.3 45.7 %collective-permute-start.5 = (bf16[3,176,512]{2,1,0:T(8,128)(2,1)}, bf16[3,176,512]{2,1,0:T(8,128)(2,1)}, u32[]{:S(2)}, u32[]{:S(2)}) collective-permute-start(bf16[3,176,512]{2,1,0:T(8,128)(2,1)} %get-tuple-element.314), channel_id=1, source_target_pairs={{0,3},{1,0},{2,1},{3,2},{4,7},{5,4},{6,5},{7,6},{8,11},{9,8},{10,9... | collective-permute-start | bytes 1622024 | tf_op jit(solution)/shard_map/ppermute | solution.py:1634
  831.0 25.7 %copy-start.30 = (f32[1,2048]{1,0:T(1,128)S(1)}, f32[1,2048]{1,0:T(1,128)}, u32[]{:S(2)}) copy-start(f32[1,2048]{1,0:T(1,128)} %get-tuple-element.183) | copy-start | bytes 24580
  831.0 25.7 %copy-start.32 = (f32[1,2048]{1,0:T(1,128)S(1)}, f32[1,2048]{1,0:T(1,128)}, u32[]{:S(2)}) copy-start(f32[1,2048]{1,0:T(1,128)} %get-tuple-element.182) | copy-start | bytes 24580
  855.3 23.7 %copy-start.29 = (f32[1,2048]{1,0:T(1,128)S(1)}, f32[1,2048]{1,0:T(1,128)}, u32[]{:S(2)}) copy-start(f32[1,2048]{1,0:T(1,128)} %get-tuple-element.181) | copy-start | bytes 24580
  855.3 23.7 %copy-start.31 = (f32[1,2048]{1,0:T(1,128)S(1)}, f32[1,2048]{1,0:T(1,128)}, u32[]{:S(2)}) copy-start(f32[1,2048]{1,0:T(1,128)} %get-tuple-element.180) | copy-start | bytes 24580
  958.4 10.4 copy-start.7
  958.4 12.2 %copy-start.21 = (f32[256,2,128]{2,1,0:T(2,128)S(1)}, f32[256,2,128]{2,1,0:T(2,128)}, u32[]{:S(2)}) copy-start(f32[256,2,128]{2,1,0:T(2,128)} %param.30) | copy-start | bytes 786436
  961.9 42.8 %collective-permute-start.6 = (bf16[704,512]{1,0:T(8,128)(2,1)}, bf16[704,512]{1,0:T(8,128)(2,1)}, u32[]{:S(2)}, u32[]{:S(2)}) collective-permute-start(bf16[704,512]{1,0:T(8,128)(2,1)} %get-tuple-element.311), channel_id=1, source_target_pairs={{0,3},{1,0},{2,1},{3,2},{4,7},{5,4},{6,5},{7,6},{8,11},{9,8},{10,9... | collective-permute-start | bytes 2162696 | tf_op jit(solution)/shard_map/ppermute | solution.py:1634
  962.3 61.9 %collective-permute-start.7 = (bf16[704,512]{1,0:T(8,128)(2,1)}, bf16[704,512]{1,0:T(8,128)(2,1)}, u32[]{:S(2)}, u32[]{:S(2)}) collective-permute-start(bf16[704,512]{1,0:T(8,128)(2,1)} %get-tuple-element.310), channel_id=1, source_target_pairs={{0,2},{1,3},{2,0},{3,1},{4,6},{5,7},{6,4},{7,5},{8,10},{9,11},{10,... | collective-permute-start | bytes 2162696 | tf_op jit(solution)/shard_map/ppermute | solution.py:1634
  964.8 61.5 %collective-permute-start.8 = (bf16[704,512]{1,0:T(8,128)(2,1)}, bf16[704,512]{1,0:T(8,128)(2,1)}, u32[]{:S(2)}, u32[]{:S(2)}) collective-permute-start(bf16[704,512]{1,0:T(8,128)(2,1)} %get-tuple-element.309), channel_id=1, source_target_pairs={{0,1},{1,2},{2,3},{3,0},{4,5},{5,6},{6,7},{7,4},{8,9},{9,10},{10,1... | collective-permute-start | bytes 2162696 | tf_op jit(solution)/shard_map/ppermute | solution.py:1634
  975.1 22.1 %copy-start.33 = (f32[3,64]{1,0:T(4,128)S(1)}, f32[3,64]{1,0:T(4,128)}, u32[]{:S(2)}) copy-start(f32[3,64]{1,0:T(4,128)} %param.33) | copy-start | bytes 2308
  975.2 22.1 %copy-start.35 = (f32[3,64]{1,0:T(4,128)S(1)}, f32[3,64]{1,0:T(4,128)}, u32[]{:S(2)}) copy-start(f32[3,64]{1,0:T(4,128)} %param.34) | copy-start | bytes 2308
  975.2 22.1 %copy-start.36 = (f32[3,64]{1,0:T(4,128)S(1)}, f32[3,64]{1,0:T(4,128)}, u32[]{:S(2)}) copy-start(f32[3,64]{1,0:T(4,128)} %param.35) | copy-start | bytes 2308
  1004.7 23.0 %copy-start.10 = (bf16[1,704,512]{1,2,0:T(8,128)(2,1)S(1)}, bf16[1,704,512]{1,2,0:T(8,128)(2,1)}, u32[]{:S(2)}) copy-start(bf16[1,704,512]{1,2,0:T(8,128)(2,1)} %copy.167) | copy-start | bytes 2162692
  1029.2 2.7 copy-start
  1029.4 5.3 copy-start.16
  1031.9 3.8 copy-start.9
Sparse Core Ops, SparseCore 0:
  35.4 56.3 all-gather.6
  94.3 149.6 all-gather.14
  274.9 46.1 all-gather.8
  322.8 36.7 all-gather.10
  478.2 52.9 reduce-scatter.2
  533.0 37.1 all-gather.12
  811.6 63.0 reduce-scatter.4

commit v8 on v7

--- a/solution.py
+++ b/solution.py
@@ -1412,7 +1412,6 @@
 def newton_small_body(rows, factor_ref, mom_ref, grad_ref, kv_ref, out_ref, *scratch):
     problems = [scratch[4 * at : 4 * at + 4] for at in range(4)]
     parts, _, columns = mom_ref.shape
-    piece_rows = 2 * rows // parts
     kv_columns = kv_ref.shape[2]
     half = rows // 2
     factor = factor_ref[0]
@@ -1420,16 +1419,9 @@
         spot = slice(part * columns, (part + 1) * columns)
         for member in range(2):
             current = problems[member][0]
-            current[:, spot] = MOMENTUM * mom_ref[
-                part, member * rows : (member + 1) * rows, :
-            ].astype(FULL)
-        for block in range(parts):
-            current = problems[block // (parts // 2)][0]
-            at = block % (parts // 2) * piece_rows
-            piece = grad_ref[part, 0:piece_rows, block * columns : (block + 1) * columns]
-            current[at : at + piece_rows, spot] = (
-                current[at : at + piece_rows, spot] + factor * piece.astype(FULL)
-            )
+            here = slice(member * rows, (member + 1) * rows)
+            mom, grad = mom_ref[part, here, :], grad_ref[part, here, :]
+            current[:, spot] = MOMENTUM * mom.astype(FULL) + factor * grad.astype(FULL)
         spot = slice(part * kv_columns, (part + 1) * kv_columns)
         for member in range(2):
             current = problems[2 + member][0]
@@ -1733,9 +1725,8 @@
     ffn_w = lax.all_gather(ffn_sub, "wide", axis=0)
     found = found.reshape(narrow_count, wide_count * all_rows, columns)
     embed_cut = embed_low.reshape(wide_count, vocab_rows // wide_count, columns)
-    rows_low, table_own = launch(
-        [fetch_rows(found, all_rows), join_columns("wide", embed_cut)], 1, "fetch_rows"
-    )
+    table_half = embed_cut.shape[1] // 2
+    rows_low = launch([fetch_rows(found, all_rows)], 1, "fetch_rows")[0]
 
     mom_qo = jnp.moveaxis(attn_qo_mom, 1, 0)
     mom_kv = jnp.moveaxis(attn_kv_mom, 1, 0)
@@ -1785,7 +1776,7 @@
     )
     early = lax.all_gather(early_part, "wide", axis=0, tiled=True)
     start_own = rows_low[tok_rows:].astype(FULL)
-    middle, inner, mixed_wide, pick_cols = launch(
+    middle, inner, mixed_wide, pick_cols, table_top = launch(
         [
             settle(
                 attn_part,
@@ -1796,6 +1787,7 @@
             ),
             gather_wide(mixed),
             split_columns("wide", normed),
+            join_columns("wide", embed_cut[:, :table_half]),
         ],
         3,
         "settle_middle",
@@ -1803,9 +1795,15 @@
     inner = inner.reshape(sel, width)
     inner_all = lax.all_gather(inner, "wide", axis=0, tiled=True)
     gate, up, hidden, fed = feed(inner, ffn_w)
-    final_own, late_part = launch(
-        [settle(fed, middle, start_own, keep_row, gain_w[2:3])], 4, "settle_late"
-    )
+    final_own, late_part, table_low = launch(
+        [
+            settle(fed, middle, start_own, keep_row, gain_w[2:3]),
+            join_columns("wide", embed_cut[:, table_half:]),
+        ],
+        4,
+        "settle_late",
+    )
+    table_own = jnp.concatenate([table_top, table_low])
 
     table_count = table_own.shape[0]
     local_target = targets_all - (narrow_spot * vocab_rows + wide_spot * table_count)
@@ -1876,21 +1874,27 @@
     grad_out = grad_out.reshape(sel, width)
     out_all = lax.all_gather(grad_out, "wide", axis=0, tiled=True)
     acts, fed_back = feed_back(grad_out, ffn_w, gate, up, hidden)
-    grad_mid, gain_mid, grad_branch = launch(
-        [settle_back(fed_back, middle, grad_layer, keep_row, gain_w[1:2])], 9, "back_middle"
-    )
+    grad_mid, gain_mid, grad_branch, acts = launch(
+        [
+            settle_back(fed_back, middle, grad_layer, keep_row, gain_w[1:2]),
+            swap_blocks("wide", acts),
+        ],
+        9,
+        "back_middle",
+    )
+    acts = jnp.moveaxis(acts, 1, 0).reshape(3, total_rows, ffn_size)
+    acts = lax.all_gather(acts, "narrow", axis=0)
     grad_branch, grad_early = lax.optimization_barrier((grad_branch, grad_early))
     grad_branch = grad_branch.reshape(sel, width)
 
     kv_parts, grad_queries, pick_part = attend_back(
         grad_branch, proj, own_head, queries, probs, cosine, sine, cosine_all, sine_all
     )
-    grad_kv, grad_pick, grad_early, acts, queries_wide, branch_cols = launch(
+    grad_kv, grad_pick, grad_early, queries_wide, branch_cols = launch(
         [
             swap_blocks("narrow", kv_parts),
             sum_narrow(pick_part),
             sum_narrow(grad_early),
-            swap_blocks("wide", acts),
             gather_wide(grad_queries),
             split_columns("wide", grad_branch),
         ],
@@ -1902,43 +1906,39 @@
     grad_rows, gain_attn, gain_early, grad_kv = rows_back(
         rows_low, gain_w, proj, grad_kv, grad_pick, grad_early, grad_base, repeat
     )
-    acts = jnp.moveaxis(acts, 1, 0).reshape(3, total_rows, ffn_size)
-    rights = (inner_all, inner_all, out_all)
-    grad_ffn = [dot(acts[j], rights[j], 0, 0) for j in range(3)]
-    ffn_squares = sum(jnp.sum(part * part) for part in grad_ffn)
+    grad_rows, acts = lax.optimization_barrier((grad_rows, acts))
     summed_qo = jnp.stack(
         [
             jnp.einsum("wtc,wtf->cf", pick_cols, queries_wide, preferred_element_type=FULL),
             jnp.einsum("wtc,wtf->cf", branch_cols, mixed_wide, preferred_element_type=FULL),
         ]
     )
-    qo_box = summed_qo.astype(LOW).reshape(narrow_count, -1, q_size)
-    qo_box = jnp.moveaxis(qo_box, 0, 1).reshape(-1, width)
-    qo_box = jnp.pad(qo_box, ((0, ffn_size - qo_box.shape[0]), (0, 0)))
-    for_owners = jnp.stack([part.astype(LOW) for part in grad_ffn] + [qo_box])
-    grad_rows, owned, kv_wide, head_cols_all = launch(
+    qo_owned = lax.all_gather(
+        summed_qo.astype(LOW).reshape(2 * columns, q_size), "narrow", axis=0
+    )
+    grad_rows, kv_wide, head_cols_all = launch(
         [
             return_rows(grad_rows),
-            swap_turned(for_owners, 5),
             later(gather_wide(grad_kv, 3), 2),
             later(split_columns("wide", grad_head, 3), 2),
         ],
         11,
         "return_rows",
     )
-    final_parts, grad_rows = lax.optimization_barrier((for_owners[:3], grad_rows))
     size = width // narrow_count
 
-    def final_piece(spot):
-        return lax.dynamic_slice_in_dim(final_parts, spot * size, size, 2)
-
-    summed_ffn = jnp.zeros((3, narrow_count, ffn_size, size), LOW)
-    for step in range(narrow_count):
-        piece = final_piece(lax.rem(narrow_spot + step, narrow_count))
-        if step:
-            piece = shifted(piece, "narrow", step)
-        source = lax.rem(narrow_spot - step + narrow_count, narrow_count)
-        summed_ffn = lax.dynamic_update_index_in_dim(summed_ffn, piece, source, 1)
+    def cols_own(values_all):
+        return lax.dynamic_slice_in_dim(values_all, narrow_spot * size, size, 1)
+
+    rights = (inner_all, inner_all, out_all)
+    summed_ffn = jnp.stack(
+        [
+            jnp.einsum(
+                "stf,td->sfd", acts[:, j], cols_own(rights[j]), preferred_element_type=FULL
+            ).reshape(ffn_rows, size)
+            for j in range(3)
+        ]
+    )
     turn = lax.rem(wide_spot, 2)
     grad_kv_w = jnp.einsum(
         "wtc,wtf->cf", tok_cols, kv_wide, preferred_element_type=FULL
@@ -1952,14 +1952,12 @@
     squares = (
         jnp.sum(summed_qo * summed_qo)
         + jnp.sum(summed_kv * summed_kv)
-        + ffn_squares
+        + jnp.sum(summed_ffn * summed_ffn)
         + jnp.sum(table_squares)
     )
     sums = jnp.stack(
         [gain_attn[0], gain_mid[0], gain_early[0] + gain_late[0], jnp.full((width,), squares)]
     )
-    sums, summed_ffn = lax.optimization_barrier((sums, summed_ffn))
-    summed_ffn = summed_ffn.reshape(3, ffn_rows, size).astype(FULL)
     sums, kv_owned = launch(
         [
             combine(sums.reshape(4, 8, -1), add_two),
@@ -1977,10 +1975,14 @@
     factor = jnp.minimum(1.0, CLIP_NORM / (grad_norm + 1e-06)) / loss_count
 
     def ffn_owner():
-        return newton(factor, mom_owned, owned.reshape(ffn_rows, width))
+        matrix = jnp.minimum(lax.rem(narrow_spot + narrow_count - turn, narrow_count), 2)
+        left = lax.dynamic_index_in_dim(acts, matrix, 1, False)
+        right = jnp.where(matrix == 2, out_all, inner_all)
+        grad = jnp.einsum("stf,td->sfd", left, right, preferred_element_type=FULL)
+        return newton(factor, mom_owned, grad.reshape(ffn_rows, width))
 
     def small_owner():
-        return newton_small(factor, mom_owned, owned, kv_owned)
+        return newton_small(factor, mom_owned, qo_owned, kv_owned)
 
     small_spot = lax.rem(3 + turn, narrow_count)
     directions = lax.cond(narrow_spot == small_spot, small_owner, ffn_owner)

time: 1070 us -> 1090 us (1.019)
  waiting for transfers between devices: 39.4 us -> 57.7 us
    all_gather x0 -> x2, waiting for transfers between devices: none -> 19.8 us  [the longest x1 19.8 us: per_device(): acts = lax.all_gather(acts, 'narrow', axis=0)]
    pallas_call x13, Pallas kernels: 606 us -> 620 us  [launch(): pl.pallas_call(body, out_shape=outputs, in_specs=[place for task in tasks...]
    dot_general x10 -> x7, matrix products: 61 us -> 47.9 us  [dot(): lax.dot_general(first, second, (((first_dim,), (second_dim,)), ((), ())),...]
    dot_general x0 -> x4, matrix products: none -> 13 us  [the longest x1 8.46 us: ffn_owner(): grad = jnp.einsum('stf,td->sfd', left, right, preferred_element_type=FULL)]
    unnamed x100 -> x105, local copies, waits for them, and re-layouts: 22.5 us -> 27.7 us
    ppermute x9 -> x6, waiting for transfers between devices: 38.7 us -> 37.7 us  [shifted(): return lax.ppermute(parts, axis, pairs)]
  transfers between devices with their start and end apart: 16 -> 15, of which waited for: 6 -> 5; matrix products, arithmetic and copies ran while one was open for 13% -> 13% of each run, Pallas kernels for 44% -> 51%
where the time goes in v8:
time: 1090 us; the launch traced here: 1080 us
  Pallas kernels  772 us (71%)
  other arithmetic  79.7 us (7%)
  local copies, waits for them, and re-layouts  69 us (6%)
  matrix products  66.6 us (6%)
  waiting for transfers between devices  57.7 us (5%)
  between operations  23 us (2%)
    pallas_call x13, Pallas kernels, launch(): pl.pallas_call(body, out_shape=outputs, in_specs=[place for task in tasks...  620 us
    dot_general x7, matrix products, dot(): lax.dot_general(first, second, (((first_dim,), (second_dim,)), ((), ())),...  47.9 us
    pallas_call x1, Pallas kernels, newton(): pl.pallas_call(newton_body, in_specs=[pl.BlockSpec(memory_space=pltpu.SME...  45.8 us
    ppermute x6, waiting for transfers between devices, shifted(): return lax.ppermute(parts, axis, pairs)  37.7 us
    pallas_call x1, Pallas kernels, lookup(): pl.pallas_call(lookup_body, in_specs=[pl.BlockSpec(memory_space=pltpu.SME...  28.8 us
    pallas_call x5, Pallas kernels, local_call(): pl.pallas_call(body, grid=(1,), in_specs=specs, out_specs=[pl.BlockSpec(a...  28.3 us
    unnamed x105, local copies, waits for them, and re-layouts  27.7 us
    sub x2, other arithmetic, adamw(): weight * (1.0 - rate * decay) - rate * update  23.2 us
  transfers between devices with their start and end apart: 15, of which 5 were waited for; matrix products, arithmetic and copies ran while one was open for 13% of the time, Pallas kernels for 51%

profile of v8, /device:TPU:17, one launch (start us, length us, event | category | flops | bytes accessed | tf_op | source)
XLA Modules:
  0.0 1075.8 jit_solution(3896536151772265329)
XLA Ops:
  14.2 18.9 %gather_ids.1 = (s32[8,16,128]{2,1,0:T(8,128)}, f32[4,8,8,128]{3,2,1,0:T(8,128)}, bf16[4,256,256]{2,1,0:T(8,128)(2,1)}) custom-call(s32[16,128]{1,0:T(8,128)} %pad_bitcast_fusion.refs_0_, f32[8,128]{1,0:T(8,128)} %bitcast_convert_fusion.refs_1_, bf16[256,256]{1,0:T(8,128)(2,1)} %bitcast.293), custom_call_target="tpu_custom_call" | custom-call | bytes 108032 | tf_op jit(solution)/shard_map/gather_ids/pallas_call | solution.py:139
  35.4 2.5 convert_element_type.133
  39.2 1.9 collective-permute-start
  46.9 28.8 %lookup.1 = (bf16[9216,256]{1,0:T(8,128)(2,1)}, bf16[8192,256]{1,0:T(8,128)(2,1)}, s32[9248]{0:T(1024)}) custom-call(s32[9216]{0:T(1024)} %and_select_fusion.ids_ref, s32[9344]{0:T(1024)} %concatenate.44.turn_ref, f32[8192,256]{1,0:T(8,128)} %table_ref.1), custom_call_target="tpu_custom_call" | custom-call | bytes 8388608 | tf_op jit(solution)/shard_map/lookup/pallas_call | solution.py:1514
  75.7 1.7 collective-permute-done.1.refs_2_
  77.4 11.6 %collective-permute-done.2.refs_3_ = bf16[528,512]{1,0:T(8,128)(2,1)S(1)} collective-permute-done((bf16[528,512]{1,0:T(8,128)(2,1)S(1)}, bf16[528,512]{1,0:T(8,128)(2,1)S(1)}, u32[]{:S(2)}, u32[]{:S(2)}) %collective-permute-start.2) | collective-permute-done | bytes 540704 | tf_op jit(solution)/shard_map/ppermute | solution.py:1626
  89.8 3.1 assemble.1
  97.8 1.9 multiply_sine_fusion
  100.5 117.8 %fetch_rows.1.rows_ref = bf16[288,2048]{1,0:T(8,128)(2,1)} custom-call(bf16[4,2304,256]{2,1,0:T(8,128)(2,1)} %bitcast.261), custom_call_target="tpu_custom_call" | custom-call | bytes 737280 | tf_op jit(solution)/shard_map/fetch_rows/pallas_call | solution.py:139
  218.4 1.7 slice_convert_fusion
  220.1 5.0 make_heads.1
  225.1 27.1 %trade_heads.1 = (bf16[4,1,2,256,128]{4,3,2,1,0:T(8,128)(2,1)}, bf16[4,32,2048]{2,1,0:T(8,128)(2,1)}, bf16[8,256,256]{2,1,0:T(8,128)(2,1)}) custom-call(bf16[4,1,2,256,128]{4,3,2,1,0:T(8,128)(2,1)} %get-tuple-element.145.refs_0_, bf16[32,2048]{1,0:T(8,128)(2,1)} %get-tuple-element.358.refs_1_, bf16[256,2048]{1,0:T(8,128)(2,1)} %get-tuple-element.146.refs_2_), custom_call_target="tpu_custom_call" | custom-call | bytes 475136 | tf_op jit(solution)/shard_map/trade_heads/pallas_call | solution.py:139
  252.2 6.9 attend.1
  259.8 4.6 fusion.57
  265.1 59.0 %settle_middle.1 = (f32[32,2048]{1,0:T(8,128)}, bf16[4,32,2048]{2,1,0:T(8,128)(2,1)}, bf16[8,128,512]{2,1,0:T(8,128)(2,1)}, bf16[8,128,256]{2,1,0:T(8,128)(2,1)}, bf16[512,2048]{1,0:T(8,128)(2,1)}) custom-call(bf16[4,32,2048]{2,1,0:T(8,128)(2,1)} %bitcast.297, f32[32,2048]{1,0:T(8,128)} %get-tuple-element.357.refs_1_.refs_2_, ...), custom_call_target="tpu_custom_call" | custom-call | bytes 1034240 | tf_op jit(solution)/shard_map/settle_middle/pallas_call | solution.py:139
  326.2 2.5 convert_bitcast_fusion
  328.7 1.9 pad_maximum_fusion.1
  330.6 13.3 %feed.1 = (f32[8,128,176]{2,1,0:T(8,128)}, f32[8,128,176]{2,1,0:T(8,128)}, bf16[8,128,176]{2,1,0:T(8,128)(2,1)}, bf16[128,2048]{1,0:T(8,128)(2,1)}) custom-call(bf16[128,2048]{1,0:T(8,128)(2,1)} %bitcast.268, bf16[8,3,176,2048]{3,2,1,0:T(8,128)(2,1)} %bitcast.255), custom_call_target="tpu_custom_call" | custom-call | flops 2214592512 | bytes 17301504 | tf_op jit(solution)/shard_map/feed/pallas_call | solution.py:1227
  344.5 40.0 %settle_late.1 = (f32[32,2048]{1,0:T(8,128)}, bf16[4,32,2048]{2,1,0:T(8,128)(2,1)}, bf16[512,2048]{1,0:T(8,128)(2,1)}) custom-call(bf16[4,32,2048]{2,1,0:T(8,128)(2,1)} %bitcast.294, f32[32,2048]{1,0:T(8,128)} %get-tuple-element.160.refs_1_, f32[32,2048]{1,0:T(8,128)} %get-tuple-element.357.refs_1_.refs_2_, f32[1,2048]{1,0:T(1,128)} %broadcast_in_dim.122.refs_3_, ...), custom_call_target="tpu_custom_call" | custom-call | bytes 755712 | tf_op jit(solution)/shard_map/settle_late/pallas_call | solution.py:139
  384.5 32.8 %gather_late.1 = (bf16[8,128,2048]{2,1,0:T(8,128)(2,1)}, bf16[4,352,512]{2,1,0:T(8,128)(2,1)}) custom-call(bf16[128,2048]{1,0:T(8,128)(2,1)} %bitcast.295, bf16[4,352,512]{2,1,0:T(8,128)(2,1)} %get-tuple-element.352.refs_1_), custom_call_target="tpu_custom_call" | custom-call | bytes 950272 | tf_op jit(solution)/shard_map/gather_late/pallas_call | solution.py:139
  417.9 2.1 copy-done.17
  421.0 6.1 fusion.61
  427.1 7.8 fusion.60
  434.9 2.4 exponential_reduce_fusion.1
  438.0 12.2 %combine_stats.1 = f32[3,8,256]{2,1,0:T(8,128)} custom-call(f32[3,8,256]{2,1,0:T(8,128)} %bitcast.306), custom_call_target="tpu_custom_call" | custom-call | bytes 6144 | tf_op jit(solution)/shard_map/combine_stats/pallas_call | solution.py:139
  451.0 10.2 convolution_convert_fusion.1
  461.3 37.9 %sum_late.1 = (f32[128,2048]{1,0:T(8,128)}, bf16[4,352,512]{2,1,0:T(8,128)(2,1)}) custom-call(bf16[8,128,2048]{2,1,0:T(8,128)(2,1)} %bitcast.264, bf16[4,352,512]{2,1,0:T(8,128)(2,1)} %get-tuple-element.351.refs_1_), custom_call_target="tpu_custom_call" | custom-call | bytes 1015808 | tf_op jit(solution)/shard_map/sum_late/pallas_call | solution.py:139
  499.2 8.5 convolution_convert_fusion
  510.6 25.8 %back_late.1 = (f32[32,2048]{1,0:T(8,128)}, f32[1,2048]{1,0:T(1,128)}, bf16[4,32,2048]{2,1,0:T(8,128)(2,1)}) custom-call(bf16[4,32,2048]{2,1,0:T(8,128)(2,1)} %bitcast.271, f32[32,2048]{1,0:T(8,128)} %get-tuple-element.167.refs_1_, f32[32,2048]{1,0:T(8,128)} %broadcast_in_dim.125.refs_2_, f32[1,2048]{1,0:T(1,128)} %broadcast_in_dim.122.refs_3_, ...), custom_call_target="tpu_custom_call" | custom-call | bytes 232448 | tf_op jit(solution)/shard_map/back_late/pallas_call | solution.py:139
  536.5 14.6 %feed_back.1 = (bf16[8,3,128,176]{3,2,1,0:T(8,128)(2,1)}, bf16[128,2048]{1,0:T(8,128)(2,1)}) custom-call(bf16[128,2048]{1,0:T(8,128)(2,1)} %bitcast.270, bf16[8,3,176,2048]{3,2,1,0:T(8,128)(2,1)} %bitcast.256, f32[8,128,176]{2,1,0:T(8,128)} %get-tuple-element.169.gate_ref, f32[8,128,176]{2,1,0:T(8,128)} %get-tuple-element.170.up_ref, ...), custom_call_target="tpu_custom_call" | custom-call | flops 2214592512 | bytes 17301504 | tf_op jit(solution)/shard_map/feed_back/pallas_call | solution.py:1279
  551.9 30.3 %back_middle.1 = (f32[32,2048]{1,0:T(8,128)}, f32[1,2048]{1,0:T(1,128)}, bf16[4,32,2048]{2,1,0:T(8,128)(2,1)}, bf16[8,3,128,176]{3,2,1,0:T(8,128)(2,1)}) custom-call(bf16[4,32,2048]{2,1,0:T(8,128)(2,1)} %bitcast.288, f32[32,2048]{1,0:T(8,128)} %get-tuple-element.160.refs_1_, f32[32,2048]{1,0:T(8,128)} %broadcast_multiply_fusion.refs_2_, ...), custom_call_target="tpu_custom_call" | custom-call | bytes 502784 | tf_op jit(solution)/shard_map/back_middle/pallas_call | solution.py:139
  582.1 2.3 copy.159
  587.8 8.7 fusion.48
  596.6 6.3 add_convert_fusion.refs_2_
  602.9 7.4 attend_back.1
  610.3 82.0 %trade_grads.1 = (bf16[4,1,2,256,128]{4,3,2,1,0:T(8,128)(2,1)}, f32[32,2048]{1,0:T(8,128)}, f32[32,2048]{1,0:T(8,128)}, bf16[8,128,512]{2,1,0:T(8,128)(2,1)}, bf16[8,128,256]{2,1,0:T(8,128)(2,1)}) custom-call(bf16[4,1,2,256,128]{4,3,2,1,0:T(8,128)(2,1)} %get-tuple-element.180.refs_0_, bf16[4,32,2048]{2,1,0:T(8,128)(2,1)} %bitcast.287, ...), custom_call_target="tpu_custom_call" | custom-call | bytes 606208 | tf_op jit(solution)/shard_map/trade_grads/pallas_call | solution.py:139
  692.3 6.0 rows_back.1
  698.3 19.8 %all-gather.17.cloned.1.call-done = bf16[4,3,1024,176]{2,3,1,0:T(8,128)(2,1)} async-done(((bf16[1,3,1024,176]{2,3,1,0:T(8,128)(2,1)}), bf16[4,3,1024,176]{2,3,1,0:T(8,128)(2,1)}) %all-gather.17.cloned.1.call-update) | async-done | bytes 4325392 | tf_op jit(solution)/shard_map/all_gather | solution.py:1886
  718.0 114.6 %return_rows.1 = (bf16[4,2304,256]{2,1,0:T(8,128)(2,1)}, bf16[8,256,1024]{2,1,0:T(8,128)(2,1)}, bf16[8,1024,256]{2,1,0:T(8,128)(2,1)}) custom-call(bf16[288,2048]{1,0:T(8,128)(2,1)} %get-tuple-element.200.refs_0_, bf16[256,1024]{1,0:T(8,128)(2,1)} %get-tuple-element.201.refs_1_, bf16[1024,2048]{1,0:T(8,128)(2,1)} %add_convert_fusion.refs_2_), custom_call_target="tpu_custom_call" | custom-call | bytes 2375680 | tf_op jit(solution)/shard_map/return_rows/pallas_call | solution.py:139
  832.6 3.5 convolution_bitcast_fusion.3
  838.3 6.3 copy.175
  845.1 1.8 convolution_bitcast_fusion.5
  849.7 2.6 constant_dynamic-update-slice_fusion.2
  853.8 20.9 %spread.1 = (f32[8192,256]{1,0:T(8,128)}, f32[8,256]{1,0:T(8,128)}) custom-call(s32[9216]{0:T(1024)} %and_select_fusion.ids_ref, s32[9248]{0:T(1024)} %get-tuple-element.206.list_ref, bf16[9216,256]{1,0:T(8,128)(2,1)} %bitcast.260, bf16[8192,256]{1,0:T(8,128)(2,1)} %bitcast.262), custom_call_target="tpu_custom_call" | custom-call | flops 2359296 | bytes 16777216 | tf_op jit(solution)/shard_map/spread/pallas_call | solution.py:1588
  876.0 2.9 fusion.56
  881.3 2.7 convolution_bitcast_fusion
  885.2 1.7 multiply_reduce_fusion
  886.9 2.3 fusion.58
  893.2 21.6 %combine_sums.1 = (f32[4,8,256]{2,1,0:T(8,128)}, bf16[4,512,128]{2,1,0:T(8,128)(2,1)}) custom-call(f32[4,8,256]{2,1,0:T(8,128)} %maximum_maximum_fusion.1.refs_0_, bf16[512,128]{1,0:T(8,128)(2,1)} %bitcast.291), custom_call_target="tpu_custom_call" | custom-call | bytes 90112 | tf_op jit(solution)/shard_map/combine_sums/pallas_call | solution.py:139
  916.1 1.9 slice_bitcast_fusion
  922.1 56.8 %conditional.1 = (bf16[4,704,512]{2,1,0:T(8,128)(2,1)}) conditional(s32[]{:T(128)} %convert_element_type.163, (f32[]{:T(128)}, s32[]{:T(128)}, s32[]{:T(128)}, bf16[4,3,1024,176]{2,3,1,0:T(8,128)(2,1)}, bf16[1024,2048]{1,0:T(8,128)(2,1)}, /*index=5*/bf16[1024,2048]{1,0:T(8,128)(2,1)}, bf16[4,704,512]{2,1,0:T(8,128)(2,1)}) %tuple.32, (f32[]{:T(128)}, ...), branch_computations={%region_24.25_spmd, %region_25.26_spmd} | conditional | flops 26744455168 | bytes 38666424 | solution.py:1988
  922.1 2.6 constant_dynamic-slice_fusion
  924.7 8.5 fusion.grad_ref
  933.1 45.8 %newton.1 = bf16[4,704,512]{2,1,0:T(8,128)(2,1)} custom-call(f32[1]{0:T(128)} %bitcast.factor_ref, bf16[4,704,512]{2,1,0:T(8,128)(2,1)S(1)} %copy-done.23, f32[704,2048]{1,0:T(8,128)} %fusion.grad_ref), custom_call_target="tpu_custom_call" | custom-call | flops 23789568000 | bytes 8650752 | tf_op jit(solution)/shard_map/cond/branch_0_fun/newton/pallas_call | solution.py:1400
  978.9 3.4 constant_dynamic-slice_fusion.2
  982.3 1.9 collective-permute-start.3
  985.5 22.5 %multiply_subtract_fusion = (f32[8192,256]{1,0:T(8,128)}, f32[8192,256]{1,0:T(8,128)}, f32[8192,256]{1,0:T(8,128)}) fusion(f32[8192,256]{1,0:T(8,128)} %table_ref.1, f32[8192,256]{1,0:T(8,128)} %get-tuple-element.211, f32[]{:T(128)} %div.51, f32[8192,256]{1,0:T(8,128)} %param.25, f32[8192,256]{1,0:T(8,128)} %param.26), kind=kLoop, calls=%fused_computation.6 | loop fusion | flops 31457280 | bytes 58720260 | tf_op jit(solution)/shard_map/sub | solution.py:1615
  1009.5 1.8 copy.185
  1013.7 6.2 bitcast_add_fusion
  1019.9 11.3 %collective-permute-done.3 = bf16[704,512]{1,0:T(8,128)(2,1)} collective-permute-done((bf16[704,512]{1,0:T(8,128)(2,1)}, bf16[704,512]{1,0:T(8,128)(2,1)}, u32[]{:S(2)}, u32[]{:S(2)}) %collective-permute-start.3) | collective-permute-done | bytes 720928 | tf_op jit(solution)/shard_map/ppermute | solution.py:1626
  1032.6 13.1 %collective-permute-done.4 = bf16[704,512]{1,0:T(8,128)(2,1)} collective-permute-done((bf16[704,512]{1,0:T(8,128)(2,1)}, bf16[704,512]{1,0:T(8,128)(2,1)}, u32[]{:S(2)}, u32[]{:S(2)}) %collective-permute-start.4) | collective-permute-done | bytes 720928 | tf_op jit(solution)/shard_map/ppermute | solution.py:1626
  1052.7 1.7 bitcast_subtract_fusion.1
  1056.5 5.6 bitcast_subtract_fusion
  1062.1 5.9 copy.188
  (232 shorter events, 66.6 us)
Async XLA Ops:
  7.2 212.9 %all-gather.9.cloned.1.call-start = ((), (), s32[]{:S(2)}) async-start(), calls=%async_computation.2 | async-start | bytes 9437184 | tf_op jit(solution)/shard_map/all_gather | solution.py:1697
  35.3 216.9 %all-gather.21.cloned.1.call-start = ((), (), s32[]{:S(2)}) async-start(), calls=%async_computation.10 | async-start | bytes 19464192 | tf_op jit(solution)/shard_map/all_gather | solution.py:1725
  37.9 5.8 copy-start.30
  39.2 36.5 %collective-permute-start = (bf16[528,512]{1,0:T(8,128)(2,1)}, bf16[528,512]{1,0:T(8,128)(2,1)S(1)}, u32[]{:S(2)}, u32[]{:S(2)}) collective-permute-start(bf16[528,512]{1,0:T(8,128)(2,1)} %get-tuple-element.355), channel_id=1, source_target_pairs={{0,1},{1,2},{2,3},{3,0},{4,5},{5,6},{6,7},{7,4},{8,9},{9,10},{10,1... | collective-permute-start | bytes 1622024 | tf_op jit(solution)/shard_map/ppermute | solution.py:1626
  41.0 36.4 %collective-permute-start.1 = (bf16[528,512]{1,0:T(8,128)(2,1)S(1)}, bf16[528,512]{1,0:T(8,128)(2,1)S(1)}, u32[]{:S(2)}, u32[]{:S(2)}) collective-permute-start(bf16[528,512]{1,0:T(8,128)(2,1)S(1)} %get-tuple-element.354), channel_id=1, source_target_pairs={{0,2},{1,3},{2,0},{3,1},{4,6},{5,7},{6,4},{7,5},{8,10},{9,11},{10,... | collective-permute-start | bytes 1622024 | tf_op jit(solution)/shard_map/ppermute | solution.py:1626
  42.3 46.7 %collective-permute-start.2 = (bf16[528,512]{1,0:T(8,128)(2,1)S(1)}, bf16[528,512]{1,0:T(8,128)(2,1)S(1)}, u32[]{:S(2)}, u32[]{:S(2)}) collective-permute-start(bf16[528,512]{1,0:T(8,128)(2,1)S(1)} %get-tuple-element.353), channel_id=1, source_target_pairs={{0,3},{1,0},{2,1},{3,2},{4,7},{5,4},{6,5},{7,6},{8,11},{9,8},{10,9... | collective-permute-start | bytes 1622024 | tf_op jit(solution)/shard_map/ppermute | solution.py:1626
  75.7 17.3 %copy-start.29 = (f32[4,8,8,128]{3,2,1,0:T(8,128)S(1)}, f32[4,8,8,128]{3,2,1,0:T(8,128)}, u32[]{:S(2)}) copy-start(f32[4,8,8,128]{3,2,1,0:T(8,128)} %get-tuple-element.143) | copy-start | bytes 393220
  75.7 18.3 %copy-start.43 = (s32[1,2]{1,0:T(1,128)S(1)}, s32[1,2]{1,0:T(1,128)}, u32[]{:S(2)}) copy-start(s32[1,2]{1,0:T(1,128)} %param.22) | copy-start | bytes 28
  75.7 19.1 %copy-start.37 = (s32[1,128]{1,0:T(1,128)S(1)}, s32[1,128]{1,0:T(1,128)}, u32[]{:S(2)}) copy-start(s32[1,128]{1,0:T(1,128)} %param.20) | copy-start | bytes 1540
  75.7 13.3 %copy-start.24 = (bf16[528,512]{1,0:T(8,128)(2,1)}, bf16[528,512]{1,0:T(8,128)(2,1)S(1)}, u32[]{:S(2)}) copy-start(bf16[528,512]{1,0:T(8,128)(2,1)S(1)} %collective-permute-done.refs_1_) | copy-start | bytes 1622020
  77.4 11.6 %copy-start.25 = (bf16[528,512]{1,0:T(8,128)(2,1)}, bf16[528,512]{1,0:T(8,128)(2,1)S(1)}, u32[]{:S(2)}) copy-start(bf16[528,512]{1,0:T(8,128)(2,1)S(1)} %collective-permute-done.1.refs_2_) | copy-start | bytes 1622020
  89.0 0.8 copy-start.26
  93.0 334.2 %all-gather.11.cloned.1.call-start = ((), (), s32[]{:S(2)}) async-start(), calls=%async_computation.3 | async-start | bytes 4718592 | tf_op jit(solution)/shard_map/all_gather | solution.py:1777
  96.5 121.9 %copy-start.31 = (s32[1024]{0:T(1024)}, s32[1024]{0:T(1024)S(1)}, u32[]{:S(2)}) copy-start(s32[1024]{0:T(1024)S(1)} %fusion.38) | copy-start | bytes 12292
  259.1 191.2 %all-gather.13.cloned.1.call-start = ((), (), s32[]{:S(2)}) async-start(), calls=%async_computation.4 | async-start | bytes 4718592 | tf_op jit(solution)/shard_map/all_gather | solution.py:1796
  264.5 61.2 %copy-start.20 = (f32[256,2,128]{2,1,0:T(2,128)S(1)}, f32[256,2,128]{2,1,0:T(2,128)}, u32[]{:S(2)}) copy-start(f32[256,2,128]{2,1,0:T(2,128)} %param.30) | copy-start | bytes 786436
  264.5 61.3 %copy-start.7 = (f32[256,2,512]{2,1,0:T(2,128)S(1)}, f32[256,2,512]{2,1,0:T(2,128)}, u32[]{:S(2)}) copy-start(f32[256,2,512]{2,1,0:T(2,128)} %param.28) | copy-start | bytes 3145732
  324.0 278.9 %reduce-scatter.3.cloned.1.call-start = ((), (), s32[]{:S(2)}) async-start(), calls=%async_computation.5 | async-start | bytes 4718592 | tf_op jit(solution)/shard_map/reduce_scatter | solution.py:1859
  343.9 73.4 %copy-start.12 = (bf16[512,2048]{1,0:T(8,128)(2,1)S(1)}, bf16[512,2048]{1,0:T(8,128)(2,1)}, u32[]{:S(2)}) copy-start(bf16[512,2048]{1,0:T(8,128)(2,1)} %get-tuple-element.156) | copy-start | bytes 6291460
  384.5 33.1 %copy-start.13 = (bf16[512,2048]{1,0:T(8,128)(2,1)S(1)}, bf16[512,2048]{1,0:T(8,128)(2,1)}, u32[]{:S(2)}) copy-start(bf16[512,2048]{1,0:T(8,128)(2,1)} %get-tuple-element.161) | copy-start | bytes 6291460
  417.3 3.7 copy-start.41
  417.9 2.1 copy-start.17
  427.1 7.8 copy-start.3
  434.9 2.4 copy-start.5
  461.3 37.9 %copy-start.6 = (f32[1024,1024]{0,1:T(8,128)S(1)}, f32[1024,1024]{0,1:T(8,128)}, u32[]{:S(2)}) copy-start(f32[1024,1024]{0,1:T(8,128)} %copy-done.5) | copy-start | bytes 12582916
  507.8 1.2 copy-start.16
  507.8 184.5 %all-gather.15.cloned.1.call-start = ((), (), s32[]{:S(2)}) async-start(), calls=%async_computation.6 | async-start | bytes 4718592 | tf_op jit(solution)/shard_map/all_gather | solution.py:1875
  536.4 181.6 %all-gather.17.cloned.1.call-start = ((), (), s32[]{:S(2)}) async-start(), calls=%async_computation.7 | async-start | bytes 5406720 | tf_op jit(solution)/shard_map/all_gather | solution.py:1886
  536.5 14.6 %copy-start.19 = (f32[32,2048]{1,0:T(8,128)S(1)}, f32[32,2048]{1,0:T(8,128)}, u32[]{:S(2)}) copy-start(f32[32,2048]{1,0:T(8,128)} %get-tuple-element.173) | copy-start | bytes 786436
  582.1 5.0 copy-start.28
  585.7 301.1 %reduce-scatter.5.cloned.1.call-start = ((), (), s32[]{:S(2)}) async-start(), calls=%async_computation.8 | async-start | bytes 1310720 | tf_op jit(solution)/shard_map/reduce_scatter | solution.py:1947
  587.8 8.8 copy-start.4
  587.8 8.8 copy-start.42
  698.3 134.3 %copy-start.10 = (bf16[8,256,256]{2,1,0:T(8,128)(2,1)S(1)}, bf16[8,256,256]{2,1,0:T(8,128)(2,1)}, u32[]{:S(2)}) copy-start(bf16[8,256,256]{2,1,0:T(8,128)(2,1)} %get-tuple-element.197) | copy-start | bytes 3145732
  838.2 83.9 %all-gather.19.cloned.1.call-start = ((), (), s32[]{:S(2)}) async-start(), calls=%async_computation.9 | async-start | bytes 2621440 | tf_op jit(solution)/shard_map/all_gather | solution.py:1916
  838.2 6.4 copy-start.18
  838.3 6.3 copy-start.27
  844.6 3.2 copy-start.14
  845.1 4.0 copy-start.35
  846.9 6.2 copy-start.32
  846.9 6.2 copy-start.33
  846.9 6.2 copy-start.36
  876.0 3.5 copy-start.40
  881.3 2.7 copy-start
  881.3 39.5 %copy-start.8 = (f32[256,2,512]{2,1,0:T(2,128)S(1)}, f32[256,2,512]{2,1,0:T(2,128)}, u32[]{:S(2)}) copy-start(f32[256,2,512]{2,1,0:T(2,128)} %param.28) | copy-start | bytes 3145732
  884.0 1.1 copy-start.1
  924.7 8.5 copy-start.23
  982.3 48.9 %collective-permute-start.3 = (bf16[704,512]{1,0:T(8,128)(2,1)}, bf16[704,512]{1,0:T(8,128)(2,1)}, u32[]{:S(2)}, u32[]{:S(2)}) collective-permute-start(bf16[704,512]{1,0:T(8,128)(2,1)} %get-tuple-element.350), channel_id=1, source_target_pairs={{0,3},{1,0},{2,1},{3,2},{4,7},{5,4},{6,5},{7,6},{8,11},{9,8},{10,9... | collective-permute-start | bytes 2162696 | tf_op jit(solution)/shard_map/ppermute | solution.py:1626
  984.2 61.5 %collective-permute-start.4 = (bf16[704,512]{1,0:T(8,128)(2,1)}, bf16[704,512]{1,0:T(8,128)(2,1)}, u32[]{:S(2)}, u32[]{:S(2)}) collective-permute-start(bf16[704,512]{1,0:T(8,128)(2,1)} %get-tuple-element.349), channel_id=1, source_target_pairs={{0,2},{1,3},{2,0},{3,1},{4,6},{5,7},{6,4},{7,5},{8,10},{9,11},{10,... | collective-permute-start | bytes 2162696 | tf_op jit(solution)/shard_map/ppermute | solution.py:1626
  984.2 62.9 %collective-permute-start.5 = (bf16[704,512]{1,0:T(8,128)(2,1)}, bf16[704,512]{1,0:T(8,128)(2,1)}, u32[]{:S(2)}, u32[]{:S(2)}) collective-permute-start(bf16[704,512]{1,0:T(8,128)(2,1)} %get-tuple-element.348), channel_id=1, source_target_pairs={{0,1},{1,2},{2,3},{3,0},{4,5},{5,6},{6,7},{7,4},{8,9},{9,10},{10,1... | collective-permute-start | bytes 2162696 | tf_op jit(solution)/shard_map/ppermute | solution.py:1626
  985.5 22.5 %copy-start.21 = (f32[256,2,128]{2,1,0:T(2,128)S(1)}, f32[256,2,128]{2,1,0:T(2,128)}, u32[]{:S(2)}) copy-start(f32[256,2,128]{2,1,0:T(2,128)} %param.30) | copy-start | bytes 786436
  985.5 22.5 %copy-start.22 = (f32[1,2,256,128]{3,2,1,0:T(8,128)S(1)}, f32[1,2,256,128]{3,2,1,0:T(8,128)}, u32[]{:S(2)}) copy-start(f32[1,2,256,128]{3,2,1,0:T(8,128)} %reduce-scatter.5.cloned.1.call-done) | copy-start | bytes 786436
  985.5 24.0 %copy-start.9 = (f32[256,2,512]{2,0,1:T(8,128)S(1)}, f32[256,2,512]{2,0,1:T(8,128)}, u32[]{:S(2)}) copy-start(f32[256,2,512]{2,0,1:T(8,128)} %bitcast_add_fusion.1) | copy-start | bytes 3145732
  1008.1 4.9 copy-start.34
  1008.1 4.9 copy-start.38
  1008.1 4.9 copy-start.39
  1050.1 2.7 copy-start.2
  1050.2 5.3 copy-start.15
  1052.7 3.8 copy-start.11
Sparse Core Ops, SparseCore 0:
  35.4 56.3 all-gather.8
  94.3 92.0 all-gather.20
  259.2 65.3 all-gather.10
  326.3 58.6 all-gather.12
  507.9 52.5 reduce-scatter.2
  562.4 41.4 all-gather.14
  605.6 112.4 all-gather.16
  838.3 24.9 reduce-scatter.4
  865.4 48.0 all-gather.18

commit v9 on v8

--- a/solution.py
+++ b/solution.py
@@ -272,6 +272,67 @@
     return trade("narrow", values, turned, block_at, shape, patience)
 
 
+def swap_owned(values, patience):
+    count = lax.axis_size("narrow")
+
+    def steps(ins, outs, scratch):
+        (x_ref,), (out_ref,), (send, receive, local) = ins, outs, scratch
+        me = lax.axis_index("narrow")
+        turn = lax.rem(lax.axis_index("wide"), 2)
+
+        def matrix_of(device):
+            return lax.rem(device + count - turn, count)
+
+        def copy_to(step):
+            peer = lax.rem(me + step, count)
+            return push(
+                x_ref.at[jnp.minimum(matrix_of(peer), 2)],
+                out_ref.at[me],
+                send.at[step - 1],
+                receive.at[me],
+                {"narrow": peer},
+            )
+
+        def keep():
+            return pltpu.make_async_copy(
+                x_ref.at[jnp.minimum(matrix_of(me), 2)], out_ref.at[me], local
+            )
+
+        keep().start()
+        for step in range(1, count):
+
+            @pl.when(matrix_of(lax.rem(me + step, count)) < 3)
+            def _():
+                copy_to(step).start()
+
+        for turn_at in range(patience):
+            yield
+
+        @pl.when(matrix_of(me) < 3)
+        def _():
+            for step in range(1, count):
+                source = lax.rem(me - step + count, count)
+                arrived(out_ref.at[source], send.at[0], receive.at[source], {"narrow": source})
+
+        for step in range(1, count):
+
+            @pl.when(matrix_of(lax.rem(me + step, count)) < 3)
+            def _():
+                copy_to(step).wait_send()
+
+        keep().wait()
+
+    return Task(
+        [values],
+        [struct((count,) + values.shape[1:], values.dtype)],
+        [sems(count - 1), sems(count), sems()],
+        steps,
+        ANY,
+        ANY,
+        ["narrow"],
+    )
+
+
 def send_owner(values):
     count = lax.axis_size("narrow")
 
@@ -531,17 +592,20 @@
         for step in range(deep - 1):
             right, left = deep - 1 - step, step
 
-            @pl.when((spot > 0) & (right > spot))
-            def _():
+            def pass_right():
                 right_copy(right, rightward.at[right]).wait_recv()
                 rightward[right] = rightward[right] + found_ref[right]
                 right_copy(right, rightward.at[right]).start()
+
+            pl.when((spot > 0) & (right > spot) & (2 * spot < deep))(pass_right)
 
             @pl.when((spot < deep - 1) & (left < spot))
             def _():
                 left_copy(left, leftward.at[left]).wait_recv()
                 leftward[left] = leftward[left] + found_ref[left]
                 left_copy(left, leftward.at[left]).start()
+
+            pl.when((right > spot) & (2 * spot >= deep))(pass_right)
 
         final[...] = found_ref[spot]
 
@@ -1394,21 +1458,6 @@
         out_ref[part] = low[:, part * columns : (part + 1) * columns]
 
 
-def newton(factor, mom, grad):
-    parts, rows, columns = mom.shape
-    width = parts * columns
-    return pl.pallas_call(
-        newton_body,
-        in_specs=[pl.BlockSpec(memory_space=pltpu.SMEM), VMEM, VMEM],
-        out_specs=VMEM,
-        out_shape=struct(mom.shape, LOW),
-        scratch_shapes=newton_scratch(rows, width),
-        compiler_params=pltpu.CompilerParams(vmem_limit_bytes=VMEM_BYTES),
-        cost_estimate=newton_cost(1, rows, width),
-        name="newton",
-    )(factor.reshape(1), mom, grad)
-
-
 def newton_small_body(rows, factor_ref, mom_ref, grad_ref, kv_ref, out_ref, *scratch):
     problems = [scratch[4 * at : 4 * at + 4] for at in range(4)]
     parts, _, columns = mom_ref.shape
@@ -1448,21 +1497,37 @@
                 ]
 
 
-def newton_small(factor, mom, grad, kv_grad):
-    parts, _, columns = mom.shape
+def newton_any_body(rows, factor_ref, mom_ref, grad_ref, qo_ref, kv_ref, out_ref, *scratch):
+    parts = mom_ref.shape[0]
+    owner = lax.rem(3 + lax.rem(lax.axis_index("wide"), 2), parts)
+    small = lax.axis_index("narrow") == owner
+
+    @pl.when(small)
+    def _():
+        newton_small_body(rows, factor_ref, mom_ref, qo_ref, kv_ref, out_ref, *scratch[4:])
+
+    @pl.when(jnp.logical_not(small))
+    def _():
+        newton_body(factor_ref, mom_ref, grad_ref, out_ref, *scratch[:4])
+
+
+def newton(factor, mom, grad, qo_grad, kv_grad):
+    parts, slot_rows, columns = mom.shape
+    width = parts * columns
     rows = kv_grad.shape[1] // 2
     kv_width = parts * kv_grad.shape[2]
     return pl.pallas_call(
-        functools.partial(newton_small_body, rows),
-        in_specs=[pl.BlockSpec(memory_space=pltpu.SMEM), VMEM, VMEM, VMEM],
+        functools.partial(newton_any_body, rows),
+        in_specs=[pl.BlockSpec(memory_space=pltpu.SMEM)] + [VMEM] * 4,
         out_specs=VMEM,
         out_shape=struct(mom.shape, LOW),
-        scratch_shapes=newton_scratch(rows, parts * columns) * 2
+        scratch_shapes=newton_scratch(slot_rows, width)
+        + newton_scratch(rows, width) * 2
         + newton_scratch(rows, kv_width) * 2,
         compiler_params=pltpu.CompilerParams(vmem_limit_bytes=VMEM_BYTES),
-        cost_estimate=newton_cost(2, rows, parts * columns),
-        name="newton_small",
-    )(factor.reshape(1), mom, grad, kv_grad)
+        cost_estimate=newton_cost(1, slot_rows, width),
+        name="newton",
+    )(factor.reshape(1), mom, grad, qo_grad, kv_grad)
 
 
 def lookup_body(ids_ref, turn_ref, table_ref, out_ref, low_ref, list_ref, held, rows, sem):
@@ -1726,7 +1791,11 @@
     found = found.reshape(narrow_count, wide_count * all_rows, columns)
     embed_cut = embed_low.reshape(wide_count, vocab_rows // wide_count, columns)
     table_half = embed_cut.shape[1] // 2
-    rows_low = launch([fetch_rows(found, all_rows)], 1, "fetch_rows")[0]
+    rows_low, table_top = launch(
+        [fetch_rows(found, all_rows), join_columns("wide", embed_cut[:, :table_half])],
+        1,
+        "fetch_rows",
+    )
 
     mom_qo = jnp.moveaxis(attn_qo_mom, 1, 0)
     mom_kv = jnp.moveaxis(attn_kv_mom, 1, 0)
@@ -1752,11 +1821,12 @@
     by_head, normed_tok = make_heads(
         rows_low, gain_w[0:1], proj, tok_part(cosine_all), tok_part(sine_all), groups, repeat
     )
-    own_head, start_low, tok_cols = launch(
+    own_head, start_low, tok_cols, table_low = launch(
         [
             swap_blocks("narrow", by_head),
             gather_blocks("narrow", rows_low[tok_rows:]),
             split_columns("wide", normed_tok),
+            join_columns("wide", embed_cut[:, table_half:]),
         ],
         2,
         "trade_heads",
@@ -1776,7 +1846,7 @@
     )
     early = lax.all_gather(early_part, "wide", axis=0, tiled=True)
     start_own = rows_low[tok_rows:].astype(FULL)
-    middle, inner, mixed_wide, pick_cols, table_top = launch(
+    middle, inner, mixed_wide, pick_cols = launch(
         [
             settle(
                 attn_part,
@@ -1787,7 +1857,6 @@
             ),
             gather_wide(mixed),
             split_columns("wide", normed),
-            join_columns("wide", embed_cut[:, :table_half]),
         ],
         3,
         "settle_middle",
@@ -1795,13 +1864,8 @@
     inner = inner.reshape(sel, width)
     inner_all = lax.all_gather(inner, "wide", axis=0, tiled=True)
     gate, up, hidden, fed = feed(inner, ffn_w)
-    final_own, late_part, table_low = launch(
-        [
-            settle(fed, middle, start_own, keep_row, gain_w[2:3]),
-            join_columns("wide", embed_cut[:, table_half:]),
-        ],
-        4,
-        "settle_late",
+    final_own, late_part = launch(
+        [settle(fed, middle, start_own, keep_row, gain_w[2:3])], 4, "settle_late"
     )
     table_own = jnp.concatenate([table_top, table_low])
 
@@ -1883,7 +1947,6 @@
         "back_middle",
     )
     acts = jnp.moveaxis(acts, 1, 0).reshape(3, total_rows, ffn_size)
-    acts = lax.all_gather(acts, "narrow", axis=0)
     grad_branch, grad_early = lax.optimization_barrier((grad_branch, grad_early))
     grad_branch = grad_branch.reshape(sel, width)
 
@@ -1906,7 +1969,10 @@
     grad_rows, gain_attn, gain_early, grad_kv = rows_back(
         rows_low, gain_w, proj, grad_kv, grad_pick, grad_early, grad_base, repeat
     )
-    grad_rows, acts = lax.optimization_barrier((grad_rows, acts))
+    rights = (inner_all, inner_all, out_all)
+    grad_ffn = [dot(acts[j], rights[j], 0, 0) for j in range(3)]
+    ffn_squares = sum(jnp.sum(part * part) for part in grad_ffn)
+    final_parts = jnp.stack([part.astype(LOW) for part in grad_ffn])
     summed_qo = jnp.stack(
         [
             jnp.einsum("wtc,wtf->cf", pick_cols, queries_wide, preferred_element_type=FULL),
@@ -1916,28 +1982,15 @@
     qo_owned = lax.all_gather(
         summed_qo.astype(LOW).reshape(2 * columns, q_size), "narrow", axis=0
     )
-    grad_rows, kv_wide, head_cols_all = launch(
+    grad_rows, acts_owned, kv_wide, head_cols_all = launch(
         [
             return_rows(grad_rows),
+            swap_owned(acts, 5),
             later(gather_wide(grad_kv, 3), 2),
             later(split_columns("wide", grad_head, 3), 2),
         ],
         11,
         "return_rows",
-    )
-    size = width // narrow_count
-
-    def cols_own(values_all):
-        return lax.dynamic_slice_in_dim(values_all, narrow_spot * size, size, 1)
-
-    rights = (inner_all, inner_all, out_all)
-    summed_ffn = jnp.stack(
-        [
-            jnp.einsum(
-                "stf,td->sfd", acts[:, j], cols_own(rights[j]), preferred_element_type=FULL
-            ).reshape(ffn_rows, size)
-            for j in range(3)
-        ]
     )
     turn = lax.rem(wide_spot, 2)
     grad_kv_w = jnp.einsum(
@@ -1952,7 +2005,7 @@
     squares = (
         jnp.sum(summed_qo * summed_qo)
         + jnp.sum(summed_kv * summed_kv)
-        + jnp.sum(summed_ffn * summed_ffn)
+        + ffn_squares
         + jnp.sum(table_squares)
     )
     sums = jnp.stack(
@@ -1974,18 +2027,28 @@
     grad_norm = jnp.sqrt(square_total) / loss_count
     factor = jnp.minimum(1.0, CLIP_NORM / (grad_norm + 1e-06)) / loss_count
 
-    def ffn_owner():
-        matrix = jnp.minimum(lax.rem(narrow_spot + narrow_count - turn, narrow_count), 2)
-        left = lax.dynamic_index_in_dim(acts, matrix, 1, False)
-        right = jnp.where(matrix == 2, out_all, inner_all)
-        grad = jnp.einsum("stf,td->sfd", left, right, preferred_element_type=FULL)
-        return newton(factor, mom_owned, grad.reshape(ffn_rows, width))
-
-    def small_owner():
-        return newton_small(factor, mom_owned, qo_owned, kv_owned)
-
-    small_spot = lax.rem(3 + turn, narrow_count)
-    directions = lax.cond(narrow_spot == small_spot, small_owner, ffn_owner)
+    matrix = jnp.minimum(lax.rem(narrow_spot + narrow_count - turn, narrow_count), 2)
+    right = jnp.where(matrix == 2, out_all, inner_all)
+    owned = jnp.einsum("stf,td->sfd", acts_owned, right, preferred_element_type=FULL)
+    final_parts, factor = lax.optimization_barrier((final_parts, factor))
+    size = width // narrow_count
+
+    def final_piece(spot):
+        return lax.dynamic_slice_in_dim(final_parts, spot * size, size, 2)
+
+    pieces = [final_piece(narrow_spot)] + [
+        shifted(final_piece(lax.rem(narrow_spot + step, narrow_count)), "narrow", step)
+        for step in range(1, narrow_count)
+    ]
+    directions = newton(
+        factor, mom_owned, owned.reshape(ffn_rows, width), qo_owned, kv_owned
+    )
+    directions, pieces, ffn = lax.optimization_barrier((directions, pieces, ffn))
+    summed_ffn = jnp.zeros((3, narrow_count, ffn_size, size), LOW)
+    for step, piece in enumerate(pieces):
+        source = lax.rem(narrow_spot - step + narrow_count, narrow_count)
+        summed_ffn = lax.dynamic_update_index_in_dim(summed_ffn, piece, source, 1)
+    summed_ffn = summed_ffn.reshape(3, ffn_rows, size).astype(FULL)
     received = [lax.dynamic_index_in_dim(directions, narrow_spot, 0, False)] + [
         shifted(
             lax.dynamic_index_in_dim(

time: 1090 us -> 1020 us (0.936); the launches traced: 1080 us -> 1020 us
  Pallas kernels: 772 us -> 712 us
  local copies, waits for them, and re-layouts: 69 us -> 37.2 us
  waiting for transfers between devices: 57.7 us -> 71.1 us
  matrix products: 66.6 us -> 77.8 us
    pallas_call x13, Pallas kernels: 620 us -> 559 us  [launch(): pl.pallas_call(body, out_shape=outputs, in_specs=[place for task in tasks...]
    ppermute x6 -> x9, waiting for transfers between devices: 37.7 us -> 70.8 us  [shifted(): return lax.ppermute(parts, axis, pairs)]
    all_gather x1 -> x0, waiting for transfers between devices: 19.8 us -> none  [per_device(): acts = lax.all_gather(acts, 'narrow', axis=0)]
    dot_general x7 -> x10, matrix products: 47.9 us -> 66 us  [dot(): lax.dot_general(first, second, (((first_dim,), (second_dim,)), ((), ())),...]
    unnamed x105 -> x116, local copies, waits for them, and re-layouts: 27.7 us -> 10.3 us
  transfers between devices with their start and end apart: 15 -> 17, of which waited for: 5 -> 5; matrix products, arithmetic and copies ran while one was open for 13% -> 15% of each run, Pallas kernels for 51% -> 50%
where the time goes in v9:
time: 1020 us
  Pallas kernels  712 us (70%)
  other arithmetic  84.3 us (8%)
  matrix products  77.8 us (8%)
  waiting for transfers between devices  71.1 us (7%)
  local copies, waits for them, and re-layouts  37.2 us (4%)
  between operations  24.8 us (2%)
  starting transfers between devices  11.5 us (1%)
    pallas_call x13, Pallas kernels, launch(): pl.pallas_call(body, out_shape=outputs, in_specs=[place for task in tasks...  559 us
    ppermute x9, waiting for transfers between devices, shifted(): return lax.ppermute(parts, axis, pairs)  70.8 us
    dot_general x10, matrix products, dot(): lax.dot_general(first, second, (((first_dim,), (second_dim,)), ((), ())),...  66 us
    pallas_call x1, Pallas kernels, newton(): pl.pallas_call(functools.partial(newton_any_body, rows), in_specs=[pl.Blo...  47.6 us
    pallas_call x5, Pallas kernels, local_call(): pl.pallas_call(body, grid=(1,), in_specs=specs, out_specs=[pl.BlockSpec(a...  28.7 us
    pallas_call x1, Pallas kernels, lookup(): pl.pallas_call(lookup_body, in_specs=[pl.BlockSpec(memory_space=pltpu.SME...  27.6 us
    sub x2, other arithmetic, adamw(): weight * (1.0 - rate * decay) - rate * update  22.8 us
  transfers between devices with their start and end apart: 17, of which 5 were waited for; matrix products, arithmetic and copies ran while one was open for 15% of the time, Pallas kernels for 50%

profile of v9, /device:TPU:17, one launch (start us, length us, event | category | flops | bytes accessed | tf_op | source)
XLA Modules:
  0.0 1018.4 jit_solution(2742009289563974359)
XLA Ops:
  12.5 1.6 convert_element_type.152
  14.2 18.9 %gather_ids.1 = (s32[8,16,128]{2,1,0:T(8,128)}, f32[4,8,8,128]{3,2,1,0:T(8,128)}, bf16[4,256,256]{2,1,0:T(8,128)(2,1)}) custom-call(s32[16,128]{1,0:T(8,128)} %pad_bitcast_fusion.refs_0_, f32[8,128]{1,0:T(8,128)} %bitcast_convert_fusion.refs_1_, bf16[256,256]{1,0:T(8,128)(2,1)} %bitcast.294), custom_call_target="tpu_custom_call" | custom-call | bytes 108032 | tf_op jit(solution)/shard_map/gather_ids/pallas_call | solution.py:139
  35.4 2.5 convert_element_type.143
  39.2 1.9 collective-permute-start
  46.9 27.6 %lookup.1 = (bf16[9216,256]{1,0:T(8,128)(2,1)}, bf16[8192,256]{1,0:T(8,128)(2,1)}, s32[9248]{0:T(1024)}) custom-call(s32[9216]{0:T(1024)} %and_select_fusion.ids_ref, s32[9344]{0:T(1024)} %concatenate.44.turn_ref, f32[8192,256]{1,0:T(8,128)} %table_ref.1), custom_call_target="tpu_custom_call" | custom-call | bytes 8388608 | tf_op jit(solution)/shard_map/lookup/pallas_call | solution.py:1579
  74.6 2.9 collective-permute-done.1.refs_2_
  77.4 11.6 %collective-permute-done.2.refs_3_ = bf16[528,512]{1,0:T(8,128)(2,1)S(1)} collective-permute-done((bf16[528,512]{1,0:T(8,128)(2,1)S(1)}, bf16[528,512]{1,0:T(8,128)(2,1)S(1)}, u32[]{:S(2)}, u32[]{:S(2)}) %collective-permute-start.2) | collective-permute-done | bytes 540704 | tf_op jit(solution)/shard_map/ppermute | solution.py:1691
  89.8 3.1 assemble.1
  97.8 1.9 multiply_sine_fusion
  100.5 5.4 fusion.51
  106.0 111.2 %fetch_rows.1 = (bf16[288,2048]{1,0:T(8,128)(2,1)}, bf16[512,2048]{1,0:T(8,128)(2,1)}) custom-call(bf16[4,2304,256]{2,1,0:T(8,128)(2,1)} %bitcast.264, bf16[8,512,256]{2,1,0:T(8,128)(2,1)} %get-tuple-element.310.refs_1_), custom_call_target="tpu_custom_call" | custom-call | bytes 1261568 | tf_op jit(solution)/shard_map/fetch_rows/pallas_call | solution.py:139
  217.2 1.7 slice_convert_fusion
  218.9 5.2 make_heads.1
  224.2 37.7 %trade_heads.1 = (bf16[4,1,2,256,128]{4,3,2,1,0:T(8,128)(2,1)}, bf16[4,32,2048]{2,1,0:T(8,128)(2,1)}, bf16[8,256,256]{2,1,0:T(8,128)(2,1)}, bf16[512,2048]{1,0:T(8,128)(2,1)}) custom-call(bf16[4,1,2,256,128]{4,3,2,1,0:T(8,128)(2,1)} %get-tuple-element.119.refs_0_, bf16[32,2048]{1,0:T(8,128)(2,1)} %get-tuple-element.334.refs_1_, ...), custom_call_target="tpu_custom_call" | custom-call | bytes 999424 | tf_op jit(solution)/shard_map/trade_heads/pallas_call | solution.py:139
  261.9 6.9 attend.1
  270.2 27.1 %settle_middle.1 = (f32[32,2048]{1,0:T(8,128)}, bf16[4,32,2048]{2,1,0:T(8,128)(2,1)}, bf16[8,128,512]{2,1,0:T(8,128)(2,1)}, bf16[8,128,256]{2,1,0:T(8,128)(2,1)}) custom-call(bf16[4,32,2048]{2,1,0:T(8,128)(2,1)} %bitcast.291, f32[32,2048]{1,0:T(8,128)} %get-tuple-element.333.refs_1_.refs_2_, f32[32,2048]{1,0:T(8,128)} %get-tuple-element.333.refs_1_.refs_2_, ...), custom_call_target="tpu_custom_call" | custom-call | bytes 509952 | tf_op jit(solution)/shard_map/settle_middle/pallas_call | solution.py:139
  299.3 2.5 convert_bitcast_fusion
  301.8 1.9 pad_maximum_fusion.2
  305.2 14.7 %feed.1 = (f32[8,128,176]{2,1,0:T(8,128)}, f32[8,128,176]{2,1,0:T(8,128)}, bf16[8,128,176]{2,1,0:T(8,128)(2,1)}, bf16[128,2048]{1,0:T(8,128)(2,1)}) custom-call(bf16[128,2048]{1,0:T(8,128)(2,1)} %bitcast.274, bf16[8,3,176,2048]{3,2,1,0:T(8,128)(2,1)} %bitcast.252), custom_call_target="tpu_custom_call" | custom-call | flops 2214592512 | bytes 17301504 | tf_op jit(solution)/shard_map/feed/pallas_call | solution.py:1291
  320.5 29.5 %settle_late.1 = (f32[32,2048]{1,0:T(8,128)}, bf16[4,32,2048]{2,1,0:T(8,128)(2,1)}) custom-call(bf16[4,32,2048]{2,1,0:T(8,128)(2,1)} %bitcast.292, f32[32,2048]{1,0:T(8,128)} %get-tuple-element.134.refs_1_, f32[32,2048]{1,0:T(8,128)} %get-tuple-element.333.refs_1_.refs_2_, f32[1,2048]{1,0:T(1,128)} %broadcast_in_dim.139.refs_3_, f32[1,2048]{1,0:T(1,128)} %slice.129.refs_4_), custom_call_target="tpu_custom_call" | custom-call | bytes 231424 | tf_op jit(solution)/shard_map/settle_late/pallas_call | solution.py:139
  350.0 34.9 %gather_late.1 = (bf16[8,128,2048]{2,1,0:T(8,128)(2,1)}, bf16[4,352,512]{2,1,0:T(8,128)(2,1)}) custom-call(bf16[128,2048]{1,0:T(8,128)(2,1)} %bitcast.297, bf16[4,352,512]{2,1,0:T(8,128)(2,1)} %get-tuple-element.315.refs_1_), custom_call_target="tpu_custom_call" | custom-call | bytes 950272 | tf_op jit(solution)/shard_map/gather_late/pallas_call | solution.py:139
  384.9 8.3 fusion.56
  393.2 7.8 fusion.55
  400.9 12.5 %exponential_reduce_fusion.1 = (f32[1024]{0:T(1024)S(1)}, f32[1024]{0:T(1024)S(1)}, f32[1024]{0:T(1024)S(1)}, f32[1024]{0:T(1024)S(1)}) fusion(f32[1024,1024]{0,1:T(8,128)S(1)} %get-tuple-element.355, f32[1024]{0:T(1024)S(1)} %get-tuple-element.354, s32[1024]{0:T(1024)S(1)} %get-tuple-element.337, f32[1024,1024]{0,1:T(8,128)S(1)} %copy-done.3, ...), kind=kLoop, calls=%fused_computation.21 | loop fusion | flops 9433088 | bytes 8417280 | tf_op jit(solution)/shard_map/reduce_sum | solution.py:1881
  414.1 13.8 %combine_stats.1 = f32[3,8,256]{2,1,0:T(8,128)} custom-call(f32[3,8,256]{2,1,0:T(8,128)} %bitcast.308), custom_call_target="tpu_custom_call" | custom-call | bytes 6144 | tf_op jit(solution)/shard_map/combine_stats/pallas_call | solution.py:139
  428.7 10.2 %convolution_convert_fusion.1 = bf16[1024,2048]{1,0:T(8,128)(2,1)} fusion(bf16[1024,2048]{1,0:T(8,128)(2,1)} %copy-done.20, f32[1024,1024]{0,1:T(8,128)} %get-tuple-element.357, f32[1024]{0:T(1024)S(1)} %convert_bitcast_fusion.5, f32[1024]{0:T(1024)S(1)} %bitcast.325, s32[1024]{0:T(1024)S(1)} %get-tuple-element.337), kind=kOutput, calls=%fused_computation.24 | convolution fusion | flops 4303355904 | bytes 12595200 | tf_op jit(solution)/shard_map/dot_general | solution.py:42
  439.0 37.0 %sum_late.1 = (f32[128,2048]{1,0:T(8,128)}, bf16[4,352,512]{2,1,0:T(8,128)(2,1)}) custom-call(bf16[8,128,2048]{2,1,0:T(8,128)(2,1)} %bitcast.268, bf16[4,352,512]{2,1,0:T(8,128)(2,1)} %get-tuple-element.314.refs_1_), custom_call_target="tpu_custom_call" | custom-call | bytes 1015808 | tf_op jit(solution)/shard_map/sum_late/pallas_call | solution.py:139
  476.0 8.5 convolution_convert_fusion
  487.4 26.8 %back_late.1 = (f32[32,2048]{1,0:T(8,128)}, f32[1,2048]{1,0:T(1,128)}, bf16[4,32,2048]{2,1,0:T(8,128)(2,1)}) custom-call(bf16[4,32,2048]{2,1,0:T(8,128)(2,1)} %bitcast.275, f32[32,2048]{1,0:T(8,128)} %get-tuple-element.140.refs_1_, f32[32,2048]{1,0:T(8,128)} %broadcast_in_dim.141.refs_2_, f32[1,2048]{1,0:T(1,128)} %broadcast_in_dim.139.refs_3_, ...), custom_call_target="tpu_custom_call" | custom-call | bytes 232448 | tf_op jit(solution)/shard_map/back_late/pallas_call | solution.py:139
  515.7 14.5 %feed_back.1 = (bf16[8,3,128,176]{3,2,1,0:T(8,128)(2,1)}, bf16[128,2048]{1,0:T(8,128)(2,1)}) custom-call(bf16[128,2048]{1,0:T(8,128)(2,1)} %bitcast.271, bf16[8,3,176,2048]{3,2,1,0:T(8,128)(2,1)} %bitcast.253, f32[8,128,176]{2,1,0:T(8,128)} %get-tuple-element.142.gate_ref, f32[8,128,176]{2,1,0:T(8,128)} %get-tuple-element.143.up_ref, ...), custom_call_target="tpu_custom_call" | custom-call | flops 2214592512 | bytes 17301504 | tf_op jit(solution)/shard_map/feed_back/pallas_call | solution.py:1343
  531.0 31.7 %back_middle.1 = (f32[32,2048]{1,0:T(8,128)}, f32[1,2048]{1,0:T(1,128)}, bf16[4,32,2048]{2,1,0:T(8,128)(2,1)}, bf16[8,3,128,176]{3,2,1,0:T(8,128)(2,1)}) custom-call(bf16[4,32,2048]{2,1,0:T(8,128)(2,1)} %bitcast.287, f32[32,2048]{1,0:T(8,128)} %get-tuple-element.134.refs_1_, f32[32,2048]{1,0:T(8,128)} %broadcast_multiply_fusion.refs_2_, ...), custom_call_target="tpu_custom_call" | custom-call | bytes 502784 | tf_op jit(solution)/shard_map/back_middle/pallas_call | solution.py:139
  562.7 2.7 copy.176
  565.4 1.7 multiply_add_fusion.1.base_ref
  567.1 9.9 fusion.43
  577.0 8.9 add_convert_fusion.refs_3_
  585.9 7.4 attend_back.1
  593.3 39.6 %trade_grads.1 = (bf16[4,1,2,256,128]{4,3,2,1,0:T(8,128)(2,1)}, f32[32,2048]{1,0:T(8,128)}, f32[32,2048]{1,0:T(8,128)}, bf16[8,128,512]{2,1,0:T(8,128)(2,1)}, bf16[8,128,256]{2,1,0:T(8,128)(2,1)}) custom-call(bf16[4,1,2,256,128]{4,3,2,1,0:T(8,128)(2,1)} %get-tuple-element.153.refs_0_, bf16[4,32,2048]{2,1,0:T(8,128)(2,1)} %bitcast.286, ...), custom_call_target="tpu_custom_call" | custom-call | bytes 606208 | tf_op jit(solution)/shard_map/trade_grads/pallas_call | solution.py:139
  632.9 6.0 rows_back.1
  639.0 130.3 %return_rows.1 = (bf16[4,2304,256]{2,1,0:T(8,128)(2,1)}, bf16[4,1024,176]{2,1,0:T(8,128)(2,1)}, bf16[8,256,1024]{2,1,0:T(8,128)(2,1)}, bf16[8,1024,256]{2,1,0:T(8,128)(2,1)}) custom-call(bf16[288,2048]{1,0:T(8,128)(2,1)} %get-tuple-element.171.refs_0_, bf16[3,1024,176]{2,1,0:T(8,128)(2,1)} %bitcast.261, bf16[256,1024]{1,0:T(8,128)(2,1)} %get-tuple-element.173.refs_2_, ...), custom_call_target="tpu_custom_call" | custom-call | bytes 2691072 | tf_op jit(solution)/shard_map/return_rows/pallas_call | solution.py:139
  769.4 3.5 convolution_bitcast_fusion
  772.9 1.9 reshape.346
  774.7 2.4 copy.224
  778.2 5.1 convert_bitcast_fusion.3
  783.3 2.4 convert_bitcast_fusion.2
  787.7 1.8 pad_maximum_fusion.mom_ref
  792.3 19.9 %spread.1 = (f32[8192,256]{1,0:T(8,128)}, f32[8,256]{1,0:T(8,128)}) custom-call(s32[9216]{0:T(1024)} %and_select_fusion.ids_ref, s32[9248]{0:T(1024)} %get-tuple-element.177.list_ref, bf16[9216,256]{1,0:T(8,128)(2,1)} %bitcast.263, bf16[8192,256]{1,0:T(8,128)(2,1)} %bitcast.265), custom_call_target="tpu_custom_call" | custom-call | flops 2359296 | bytes 16777216 | tf_op jit(solution)/shard_map/spread/pallas_call | solution.py:1653
  812.2 1.5 reduce_sum.208
  813.7 4.8 convert_bitcast_fusion.1
  819.1 7.4 fusion.5
  826.8 2.3 fusion.53
  831.8 20.3 %combine_sums.1 = (f32[4,8,256]{2,1,0:T(8,128)}, bf16[4,512,128]{2,1,0:T(8,128)(2,1)}) custom-call(f32[4,8,256]{2,1,0:T(8,128)} %maximum_maximum_fusion.1.refs_0_, bf16[512,128]{1,0:T(8,128)(2,1)} %bitcast.290), custom_call_target="tpu_custom_call" | custom-call | bytes 90112 | tf_op jit(solution)/shard_map/combine_sums/pallas_call | solution.py:139
  857.5 1.4 constant_dynamic-slice_fusion.1
  858.9 3.1 collective-permute-start.4
  862.0 1.4 collective-permute-start.5
  863.4 22.1 %multiply_subtract_fusion = (f32[8192,256]{1,0:T(8,128)}, f32[8192,256]{1,0:T(8,128)}, f32[8192,256]{1,0:T(8,128)}) fusion(f32[8192,256]{1,0:T(8,128)} %table_ref.1, f32[8192,256]{1,0:T(8,128)} %get-tuple-element.182, f32[]{:T(128)} %div.51, f32[8192,256]{1,0:T(8,128)} %param.23, f32[8192,256]{1,0:T(8,128)} %param.24), kind=kLoop, calls=%fused_computation.2 | loop fusion | flops 31457280 | bytes 58720260 | tf_op jit(solution)/shard_map/sub | solution.py:1680
  885.5 47.6 %newton.1 = bf16[4,704,512]{2,1,0:T(8,128)(2,1)} custom-call(f32[1]{0:T(128)} %bitcast.77.factor_ref, bf16[4,704,512]{2,1,0:T(8,128)(2,1)} %pad_maximum_fusion.mom_ref, f32[704,2048]{1,0:T(8,128)} %bitcast.262, bf16[4,512,512]{2,1,0:T(8,128)(2,1)} %all-gather.16.cloned.1.call-done.qo_ref, bf16[4,512,128]{2,1,0:T(8,128)(2,1)} %get-tuple-element.187.kv_ref), custom_call_target="tpu_custom_call" | custom-call | flops 23789568000 | bytes 8650752 | tf_op jit(solution)/shard_map/newton/pallas_call | solution.py:1519
  933.5 1.8 copy.188
  937.2 2.1 collective-permute-start.7
  941.6 3.2 bitcast_add_fusion
  944.7 10.5 %collective-permute-done.6 = bf16[704,512]{1,0:T(8,128)(2,1)S(1)} collective-permute-done((bf16[704,512]{1,0:T(8,128)(2,1)S(1)}, bf16[704,512]{1,0:T(8,128)(2,1)S(1)}, u32[]{:S(2)}, u32[]{:S(2)}) %collective-permute-start.6) | collective-permute-done | bytes 720928 | tf_op jit(solution)/shard_map/ppermute | solution.py:1691
  955.3 42.9 %collective-permute-done.7 = bf16[704,512]{1,0:T(8,128)(2,1)S(1)} collective-permute-done((bf16[704,512]{1,0:T(8,128)(2,1)S(1)}, bf16[704,512]{1,0:T(8,128)(2,1)S(1)}, u32[]{:S(2)}, u32[]{:S(2)}) %collective-permute-start.7) | collective-permute-done | bytes 720928 | tf_op jit(solution)/shard_map/ppermute | solution.py:1691
  998.2 2.9 collective-permute-done.8
  1001.6 2.2 bitcast_subtract_fusion.1
  1005.1 5.1 bitcast_subtract_fusion
  (245 shorter events, 45.7 us)
Async XLA Ops:
  7.2 211.7 %all-gather.8.cloned.1.call-start = ((), (), s32[]{:S(2)}) async-start(), calls=%async_computation.2 | async-start | bytes 9437184 | tf_op jit(solution)/shard_map/all_gather | solution.py:1762
  35.3 226.6 %all-gather.18.cloned.1.call-start = ((), (), s32[]{:S(2)}) async-start(), calls=%async_computation.9 | async-start | bytes 19464192 | tf_op jit(solution)/shard_map/all_gather | solution.py:1790
  37.9 5.8 copy-start.36
  39.2 35.3 %collective-permute-start = (bf16[528,512]{1,0:T(8,128)(2,1)}, bf16[528,512]{1,0:T(8,128)(2,1)S(1)}, u32[]{:S(2)}, u32[]{:S(2)}) collective-permute-start(bf16[528,512]{1,0:T(8,128)(2,1)} %get-tuple-element.322), channel_id=1, source_target_pairs={{0,1},{1,2},{2,3},{3,0},{4,5},{5,6},{6,7},{7,4},{8,9},{9,10},{10,1... | collective-permute-start | bytes 1622024 | tf_op jit(solution)/shard_map/ppermute | solution.py:1691
  41.1 36.4 %collective-permute-start.1 = (bf16[528,512]{1,0:T(8,128)(2,1)S(1)}, bf16[528,512]{1,0:T(8,128)(2,1)S(1)}, u32[]{:S(2)}, u32[]{:S(2)}) collective-permute-start(bf16[528,512]{1,0:T(8,128)(2,1)S(1)} %get-tuple-element.321), channel_id=1, source_target_pairs={{0,2},{1,3},{2,0},{3,1},{4,6},{5,7},{6,4},{7,5},{8,10},{9,11},{10,... | collective-permute-start | bytes 1622024 | tf_op jit(solution)/shard_map/ppermute | solution.py:1691
  42.3 46.7 %collective-permute-start.2 = (bf16[528,512]{1,0:T(8,128)(2,1)S(1)}, bf16[528,512]{1,0:T(8,128)(2,1)S(1)}, u32[]{:S(2)}, u32[]{:S(2)}) collective-permute-start(bf16[528,512]{1,0:T(8,128)(2,1)S(1)} %get-tuple-element.320), channel_id=1, source_target_pairs={{0,3},{1,0},{2,1},{3,2},{4,7},{5,4},{6,5},{7,6},{8,11},{9,8},{10,9... | collective-permute-start | bytes 1622024 | tf_op jit(solution)/shard_map/ppermute | solution.py:1691
  74.5 18.5 %copy-start.35 = (f32[4,8,8,128]{3,2,1,0:T(8,128)S(1)}, f32[4,8,8,128]{3,2,1,0:T(8,128)}, u32[]{:S(2)}) copy-start(f32[4,8,8,128]{3,2,1,0:T(8,128)} %get-tuple-element.117) | copy-start | bytes 393220
  74.5 19.5 %copy-start.47 = (s32[1,2]{1,0:T(1,128)S(1)}, s32[1,2]{1,0:T(1,128)}, u32[]{:S(2)}) copy-start(s32[1,2]{1,0:T(1,128)} %param.20) | copy-start | bytes 28
  74.5 20.3 %copy-start.43 = (s32[1,128]{1,0:T(1,128)S(1)}, s32[1,128]{1,0:T(1,128)}, u32[]{:S(2)}) copy-start(s32[1,128]{1,0:T(1,128)} %param.18) | copy-start | bytes 1540
  74.5 14.5 %copy-start.30 = (bf16[528,512]{1,0:T(8,128)(2,1)}, bf16[528,512]{1,0:T(8,128)(2,1)S(1)}, u32[]{:S(2)}) copy-start(bf16[528,512]{1,0:T(8,128)(2,1)S(1)} %collective-permute-done.refs_1_) | copy-start | bytes 1622020
  77.4 11.6 %copy-start.31 = (bf16[528,512]{1,0:T(8,128)(2,1)}, bf16[528,512]{1,0:T(8,128)(2,1)S(1)}, u32[]{:S(2)}) copy-start(bf16[528,512]{1,0:T(8,128)(2,1)S(1)} %collective-permute-done.1.refs_2_) | copy-start | bytes 1622020
  93.0 300.2 %all-gather.10.cloned.1.call-start = ((), (), s32[]{:S(2)}) async-start(), calls=%async_computation.3 | async-start | bytes 4718592 | tf_op jit(solution)/shard_map/all_gather | solution.py:1847
  96.5 9.5 copy-start.37
  261.9 36.8 %copy-start.24 = (f32[256,2,128]{2,1,0:T(2,128)S(1)}, f32[256,2,128]{2,1,0:T(2,128)}, u32[]{:S(2)}) copy-start(f32[256,2,128]{2,1,0:T(2,128)} %param.28) | copy-start | bytes 786436
  268.8 29.9 %copy-start.8 = (f32[256,2,512]{2,1,0:T(2,128)S(1)}, f32[256,2,512]{2,1,0:T(2,128)}, u32[]{:S(2)}) copy-start(f32[256,2,512]{2,1,0:T(2,128)} %param.26) | copy-start | bytes 3145732
  268.8 159.1 %all-gather.12.cloned.1.call-start = ((), (), s32[]{:S(2)}) async-start(), calls=%async_computation.4 | async-start | bytes 4718592 | tf_op jit(solution)/shard_map/all_gather | solution.py:1865
  297.3 288.6 %reduce-scatter.3.cloned.1.call-start = ((), (), s32[]{:S(2)}) async-start(), calls=%async_computation.5 | async-start | bytes 4718592 | tf_op jit(solution)/shard_map/reduce_scatter | solution.py:1923
  301.8 2.3 copy-start.14
  301.8 3.3 copy-start.15
  305.2 79.7 %copy-start.20 = (bf16[1024,2048]{1,0:T(8,128)(2,1)}, bf16[1024,2048]{1,0:T(8,128)(2,1)S(1)}, u32[]{:S(2)}) copy-start(bf16[1024,2048]{1,0:T(8,128)(2,1)S(1)} %constant_dynamic-update-slice_fusion) | copy-start | bytes 12582916
  393.2 7.8 copy-start.3
  400.9 12.6 %copy-start.5 = (f32[1024,1024]{0,1:T(8,128)}, f32[1024,1024]{0,1:T(8,128)S(1)}, u32[]{:S(2)}) copy-start(f32[1024,1024]{0,1:T(8,128)S(1)} %get-tuple-element.355) | copy-start | bytes 12582916
  439.0 37.0 %copy-start.6 = (f32[1024,1024]{0,1:T(8,128)S(1)}, f32[1024,1024]{0,1:T(8,128)}, u32[]{:S(2)}) copy-start(f32[1024,1024]{0,1:T(8,128)} %copy-done.5) | copy-start | bytes 12582916
  484.6 148.4 %all-gather.14.cloned.1.call-start = ((), (), s32[]{:S(2)}) async-start(), calls=%async_computation.6 | async-start | bytes 4718592 | tf_op jit(solution)/shard_map/all_gather | solution.py:1939
  514.2 312.6 %reduce-scatter.5.cloned.1.call-start = ((), (), s32[]{:S(2)}) async-start(), calls=%async_computation.7 | async-start | bytes 1310720 | tf_op jit(solution)/shard_map/reduce_scatter | solution.py:2000
  515.7 14.5 %copy-start.23 = (f32[32,2048]{1,0:T(8,128)S(1)}, f32[32,2048]{1,0:T(8,128)}, u32[]{:S(2)}) copy-start(f32[32,2048]{1,0:T(8,128)} %get-tuple-element.146) | copy-start | bytes 786436
  530.2 36.9 %copy-start.7 = (f32[1024,1024]{0,1:T(8,128)S(1)}, f32[1024,1024]{0,1:T(8,128)}, u32[]{:S(2)}) copy-start(f32[1024,1024]{0,1:T(8,128)} %copy-done.5) | copy-start | bytes 12582916
  567.1 9.9 copy-start.4
  567.1 9.9 copy-start.46
  639.0 130.4 %copy-start.10 = (bf16[8,256,256]{2,1,0:T(8,128)(2,1)S(1)}, bf16[8,256,256]{2,1,0:T(8,128)(2,1)}, u32[]{:S(2)}) copy-start(bf16[8,256,256]{2,1,0:T(8,128)(2,1)} %get-tuple-element.170) | copy-start | bytes 3145732
  772.8 4.4 copy-start.41
  772.8 4.4 copy-start
  777.1 108.4 %all-gather.16.cloned.1.call-start = ((), (), s32[]{:S(2)}) async-start(), calls=%async_computation.8 | async-start | bytes 2621440 | tf_op jit(solution)/shard_map/all_gather | solution.py:1982
  777.2 6.1 copy-start.1
  783.3 4.4 copy-start.16
  783.3 4.4 copy-start.17
  785.7 4.3 copy-start.33
  787.1 2.4 copy-start.21
  787.1 2.4 copy-start.34
  787.1 2.9 copy-start.22
  789.5 2.7 copy-start.38
  789.5 2.8 copy-start.39
  789.5 2.8 copy-start.42
  812.2 6.9 copy-start.13
  819.1 7.4 copy-start.27
  819.1 7.4 copy-start.28
  819.1 7.4 copy-start.29
  858.9 78.0 %collective-permute-start.3 = (bf16[3,176,512]{2,1,0:T(8,128)(2,1)}, bf16[3,176,512]{2,1,0:T(8,128)(2,1)S(1)}, u32[]{:S(2)}, u32[]{:S(2)}) collective-permute-start(bf16[3,176,512]{2,1,0:T(8,128)(2,1)} %get-tuple-element.318), channel_id=1, source_target_pairs={{0,1},{1,2},{2,3},{3,0},{4,5},{5,6},{6,7},{7,4},{8,9},{9,10},{10,1... | collective-permute-start | bytes 1622024 | tf_op jit(solution)/shard_map/ppermute | solution.py:1691
  858.9 78.0 %collective-permute-start.4 = (bf16[3,176,512]{2,1,0:T(8,128)(2,1)}, bf16[3,176,512]{2,1,0:T(8,128)(2,1)S(1)}, u32[]{:S(2)}, u32[]{:S(2)}) collective-permute-start(bf16[3,176,512]{2,1,0:T(8,128)(2,1)} %get-tuple-element.317), channel_id=1, source_target_pairs={{0,2},{1,3},{2,0},{3,1},{4,6},{5,7},{6,4},{7,5},{8,10},{9,11},{10,... | collective-permute-start | bytes 1622024 | tf_op jit(solution)/shard_map/ppermute | solution.py:1691
  862.0 74.9 %collective-permute-start.5 = (bf16[3,176,512]{2,1,0:T(8,128)(2,1)}, bf16[3,176,512]{2,1,0:T(8,128)(2,1)S(1)}, u32[]{:S(2)}, u32[]{:S(2)}) collective-permute-start(bf16[3,176,512]{2,1,0:T(8,128)(2,1)} %get-tuple-element.316), channel_id=1, source_target_pairs={{0,3},{1,0},{2,1},{3,2},{4,7},{5,4},{6,5},{7,6},{8,11},{9,8},{10,9... | collective-permute-start | bytes 1622024 | tf_op jit(solution)/shard_map/ppermute | solution.py:1691
  885.5 47.6 %copy-start.9 = (f32[256,2,512]{2,1,0:T(2,128)S(1)}, f32[256,2,512]{2,1,0:T(2,128)}, u32[]{:S(2)}) copy-start(f32[256,2,512]{2,1,0:T(2,128)} %param.26) | copy-start | bytes 3145732
  933.1 2.1 copy-start.25
  933.1 2.1 copy-start.26
  933.1 3.1 copy-start.40
  933.1 3.1 copy-start.44
  933.1 3.1 copy-start.45
  933.1 3.8 copy-start.11
  935.3 4.3 copy-start.12
  937.1 18.1 %collective-permute-start.6 = (bf16[704,512]{1,0:T(8,128)(2,1)S(1)}, bf16[704,512]{1,0:T(8,128)(2,1)S(1)}, u32[]{:S(2)}, u32[]{:S(2)}) collective-permute-start(bf16[704,512]{1,0:T(8,128)(2,1)S(1)} %get-tuple-element.313), channel_id=1, source_target_pairs={{0,3},{1,0},{2,1},{3,2},{4,7},{5,4},{6,5},{7,6},{8,11},{9,8},{10,9... | collective-permute-start | bytes 2162696 | tf_op jit(solution)/shard_map/ppermute | solution.py:1691
  937.2 61.0 %collective-permute-start.7 = (bf16[704,512]{1,0:T(8,128)(2,1)S(1)}, bf16[704,512]{1,0:T(8,128)(2,1)S(1)}, u32[]{:S(2)}, u32[]{:S(2)}) collective-permute-start(bf16[704,512]{1,0:T(8,128)(2,1)S(1)} %get-tuple-element.312), channel_id=1, source_target_pairs={{0,2},{1,3},{2,0},{3,1},{4,6},{5,7},{6,4},{7,5},{8,10},{9,11},{10,... | collective-permute-start | bytes 2162696 | tf_op jit(solution)/shard_map/ppermute | solution.py:1691
  939.3 61.8 %collective-permute-start.8 = (bf16[704,512]{1,0:T(8,128)(2,1)S(1)}, bf16[704,512]{1,0:T(8,128)(2,1)S(1)}, u32[]{:S(2)}, u32[]{:S(2)}) collective-permute-start(bf16[704,512]{1,0:T(8,128)(2,1)S(1)} %get-tuple-element.311), channel_id=1, source_target_pairs={{0,1},{1,2},{2,3},{3,0},{4,5},{5,6},{6,7},{7,4},{8,9},{9,10},{10,1... | collective-permute-start | bytes 2162696 | tf_op jit(solution)/shard_map/ppermute | solution.py:1691
  939.3 2.2 slice-start
  944.7 56.9 %copy-start.2 = (f32[256,2,512]{2,1,0:T(2,128)S(1)}, f32[256,2,512]{2,1,0:T(2,128)}, u32[]{:S(2)}) copy-start(f32[256,2,512]{2,1,0:T(2,128)} %param.25) | copy-start | bytes 3145732
  1001.5 2.7 copy-start.18
  (3 other events, 3.9 us)
Sparse Core Ops, SparseCore 0:
  35.4 56.3 all-gather.7
  94.3 127.1 all-gather.17
  269.0 42.5 all-gather.9
  313.3 36.7 all-gather.11
  484.7 53.2 reduce-scatter.2
  539.9 43.0 all-gather.13
  777.3 24.7 reduce-scatter.4
  803.6 48.5 all-gather.15

commit v10 on v9

--- a/solution.py
+++ b/solution.py
@@ -270,6 +270,47 @@
 def swap_turned(values, patience=2):
     shape = (lax.axis_size("narrow"),) + values.shape[1:]
     return trade("narrow", values, turned, block_at, shape, patience)
+
+
+def product(lefts, rights, sums):
+    count = len(lefts)
+    columns = rights[0].shape[1]
+    block = min(512, columns)
+    outputs = 1 if sums else count
+    rows = lefts[0].shape[1]
+
+    def steps(ins, outs, scratch):
+        left_refs, right_refs = ins[:count], ins[count:]
+        result_refs, square_ref = outs[:outputs], outs[outputs]
+        yield
+        square_ref[...] = jnp.zeros_like(square_ref)
+        for at in range(outputs):
+            members = range(count) if sums else [at]
+
+            def strip(part, carry):
+                spot = pl.ds(pl.multiple_of(part * block, block), block)
+                value = jnp.zeros((rows, block), FULL)
+                for member in members:
+                    value = value + dot(left_refs[member][...], right_refs[member][:, spot], 0, 0)
+                result_refs[at][:, spot] = value.astype(LOW)
+                if not sums:
+                    square_ref[:, spot] = square_ref[:, spot] + jnp.sum(
+                        value * value, axis=0, keepdims=True
+                    )
+                return carry
+
+            lax.fori_loop(0, columns // block, strip, 0)
+            yield
+
+    return Task(
+        list(lefts) + list(rights),
+        [struct((rows, columns), LOW)] * outputs + [struct((1, columns), FULL)],
+        [],
+        steps,
+        VMEM,
+        VMEM,
+        [],
+    )
 
 
 def swap_owned(values, patience):
@@ -1791,11 +1832,7 @@
     found = found.reshape(narrow_count, wide_count * all_rows, columns)
     embed_cut = embed_low.reshape(wide_count, vocab_rows // wide_count, columns)
     table_half = embed_cut.shape[1] // 2
-    rows_low, table_top = launch(
-        [fetch_rows(found, all_rows), join_columns("wide", embed_cut[:, :table_half])],
-        1,
-        "fetch_rows",
-    )
+    rows_low = launch([fetch_rows(found, all_rows)], 1, "fetch_rows")[0]
 
     mom_qo = jnp.moveaxis(attn_qo_mom, 1, 0)
     mom_kv = jnp.moveaxis(attn_kv_mom, 1, 0)
@@ -1862,10 +1899,14 @@
         "settle_middle",
     )
     inner = inner.reshape(sel, width)
-    inner_all = lax.all_gather(inner, "wide", axis=0, tiled=True)
     gate, up, hidden, fed = feed(inner, ffn_w)
-    final_own, late_part = launch(
-        [settle(fed, middle, start_own, keep_row, gain_w[2:3])], 4, "settle_late"
+    final_own, late_part, table_top = launch(
+        [
+            settle(fed, middle, start_own, keep_row, gain_w[2:3]),
+            join_columns("wide", embed_cut[:, :table_half]),
+        ],
+        4,
+        "settle_late",
     )
     table_own = jnp.concatenate([table_top, table_low])
 
@@ -1896,7 +1937,6 @@
     late_logits, late_stats = exit_logits(late)
     stats = jnp.concatenate([early_stats, late_stats], axis=1).reshape(3, 8, -1)
     stats = launch([combine(stats, merge_stats)], 6, "combine_stats")[0]
-    stats, inner_all = lax.optimization_barrier((stats, inner_all))
     stats = stats.reshape(3, -1)
     log_norms = stats[0] + jnp.log(stats[1])
     losses = log_norms - stats[2]
@@ -1904,21 +1944,20 @@
         counted * (EXIT_EARLY * losses[:total_rows] + EXIT_LAST * losses[total_rows:])
     )
 
-    def exit_back(logits, log_norm, weight, features):
+    def exit_back(logits, log_norm, weight):
         grad_logits = (
             (jnp.exp(logits - log_norm[:, None]) - has_target.astype(FULL))
             * (weight * counted)[:, None]
         ).astype(LOW)
-        return dot(grad_logits, table_own, 1, 0).astype(LOW), dot(grad_logits, features, 0, 0)
-
-    late_back, late_head = exit_back(late_logits, log_norms[total_rows:], EXIT_LAST, late)
+        return dot(grad_logits, table_own, 1, 0).astype(LOW), grad_logits
+
+    late_back, late_grad = exit_back(late_logits, log_norms[total_rows:], EXIT_LAST)
     grad_late, mom_low = launch(
         [sum_wide(late_back), swap_turned(mom_parts[:, half:])], 7, "sum_late"
     )
     early_norms, grad_late = lax.optimization_barrier((log_norms[:total_rows], grad_late))
-    early_back, early_head = exit_back(early_logits, early_norms, EXIT_EARLY, early)
+    early_back, early_grad = exit_back(early_logits, early_norms, EXIT_EARLY)
     mom_owned = jnp.concatenate([mom_top, mom_low], axis=1)
-    grad_head = (early_head + late_head).astype(LOW)
 
     grad_early = lax.psum_scatter(early_back, "wide", scatter_dimension=0, tiled=True)
     grad_final, gain_late, grad_out = launch(
@@ -1947,47 +1986,47 @@
         "back_middle",
     )
     acts = jnp.moveaxis(acts, 1, 0).reshape(3, total_rows, ffn_size)
-    grad_branch, grad_early = lax.optimization_barrier((grad_branch, grad_early))
+    grad_branch, grad_early, out_all = lax.optimization_barrier(
+        (grad_branch, grad_early, out_all)
+    )
+    inner, out_all = lax.optimization_barrier((inner, out_all))
+    inner_all = lax.all_gather(inner, "wide", axis=0, tiled=True)
     grad_branch = grad_branch.reshape(sel, width)
 
     kv_parts, grad_queries, pick_part = attend_back(
         grad_branch, proj, own_head, queries, probs, cosine, sine, cosine_all, sine_all
     )
-    grad_kv, grad_pick, grad_early, queries_wide, branch_cols = launch(
+    grad_kv, grad_pick, grad_early, queries_wide, branch_cols, grad_head, _ = launch(
         [
             swap_blocks("narrow", kv_parts),
             sum_narrow(pick_part),
             sum_narrow(grad_early),
             gather_wide(grad_queries),
             split_columns("wide", grad_branch),
+            product([early_grad, late_grad], [early, late], True),
         ],
         10,
         "trade_grads",
     )
-    grad_kv, out_all = lax.optimization_barrier((grad_kv, out_all))
+    grad_kv, inner_all = lax.optimization_barrier((grad_kv, inner_all))
     grad_base = grad_mid + grad_final * (1.0 - keep_layer)
     grad_rows, gain_attn, gain_early, grad_kv = rows_back(
         rows_low, gain_w, proj, grad_kv, grad_pick, grad_early, grad_base, repeat
     )
     rights = (inner_all, inner_all, out_all)
-    grad_ffn = [dot(acts[j], rights[j], 0, 0) for j in range(3)]
-    ffn_squares = sum(jnp.sum(part * part) for part in grad_ffn)
-    final_parts = jnp.stack([part.astype(LOW) for part in grad_ffn])
     summed_qo = jnp.stack(
         [
             jnp.einsum("wtc,wtf->cf", pick_cols, queries_wide, preferred_element_type=FULL),
             jnp.einsum("wtc,wtf->cf", branch_cols, mixed_wide, preferred_element_type=FULL),
         ]
     )
-    qo_owned = lax.all_gather(
-        summed_qo.astype(LOW).reshape(2 * columns, q_size), "narrow", axis=0
-    )
-    grad_rows, acts_owned, kv_wide, head_cols_all = launch(
+    grad_rows, acts_owned, kv_wide, head_cols_all, *grad_ffn, ffn_squares = launch(
         [
             return_rows(grad_rows),
             swap_owned(acts, 5),
             later(gather_wide(grad_kv, 3), 2),
             later(split_columns("wide", grad_head, 3), 2),
+            product([acts[j] for j in range(3)], rights, False),
         ],
         11,
         "return_rows",
@@ -2005,16 +2044,17 @@
     squares = (
         jnp.sum(summed_qo * summed_qo)
         + jnp.sum(summed_kv * summed_kv)
-        + ffn_squares
+        + jnp.sum(ffn_squares)
         + jnp.sum(table_squares)
     )
     sums = jnp.stack(
         [gain_attn[0], gain_mid[0], gain_early[0] + gain_late[0], jnp.full((width,), squares)]
     )
-    sums, kv_owned = launch(
+    sums, kv_owned, qo_owned = launch(
         [
             combine(sums.reshape(4, 8, -1), add_two),
             send_owner(summed_kv.astype(LOW).reshape(2 * block_rows, kv_size)),
+            later(send_owner(summed_qo.astype(LOW).reshape(2 * columns, q_size)), 1),
         ],
         12,
         "combine_sums",
@@ -2030,7 +2070,7 @@
     matrix = jnp.minimum(lax.rem(narrow_spot + narrow_count - turn, narrow_count), 2)
     right = jnp.where(matrix == 2, out_all, inner_all)
     owned = jnp.einsum("stf,td->sfd", acts_owned, right, preferred_element_type=FULL)
-    final_parts, factor = lax.optimization_barrier((final_parts, factor))
+    final_parts, factor = lax.optimization_barrier((jnp.stack(grad_ffn), factor))
     size = width // narrow_count
 
     def final_piece(spot):
@@ -2043,7 +2083,9 @@
     directions = newton(
         factor, mom_owned, owned.reshape(ffn_rows, width), qo_owned, kv_owned
     )
-    directions, pieces, ffn = lax.optimization_barrier((directions, pieces, ffn))
+    directions, pieces, ffn, factor = lax.optimization_barrier(
+        (directions, pieces, ffn, factor)
+    )
     summed_ffn = jnp.zeros((3, narrow_count, ffn_size, size), LOW)
     for step, piece in enumerate(pieces):
         source = lax.rem(narrow_spot - step + narrow_count, narrow_count)

time: 1020 us -> 1020 us (level); the launches traced: 1020 us -> 1000 us
  matrix products: 77.8 us -> 42.9 us
  other arithmetic: 84.3 us -> 97.1 us
  local copies, waits for them, and re-layouts: 37.2 us -> 48.4 us
    dot_general x10 -> x5, matrix products: 66 us -> 28.8 us  [dot(): lax.dot_general(first, second, (((first_dim,), (second_dim,)), ((), ())),...]
    ppermute x9, waiting for transfers between devices: 70.8 us -> 44.3 us  [shifted(): return lax.ppermute(parts, axis, pairs)]
    all_gather x1, waiting for transfers between devices: 0.02 us -> 22.4 us  [per_device(): out_all = lax.all_gather(grad_out, 'wide', axis=0, tiled=True)]
    dot_general x0 -> x2, local copies, waits for them, and re-layouts: none -> 10.7 us  [dot(): lax.dot_general(first, second, (((first_dim,), (second_dim,)), ((), ())),...]
  transfers between devices with their start and end apart: 17 -> 16, of which waited for: 5 -> 5; matrix products, arithmetic and copies ran while one was open for 15% -> 10% of each run, Pallas kernels for 50% -> 46%
where the time goes in v10:
time: 1020 us; the launch traced here: 1000 us
  Pallas kernels  711 us (70%)
  other arithmetic  97.1 us (10%)
  waiting for transfers between devices  66.9 us (7%)
  local copies, waits for them, and re-layouts  48.4 us (5%)
  matrix products  42.9 us (4%)
  between operations  23.5 us (2%)
  starting transfers between devices  14.1 us (1%)
    pallas_call x13, Pallas kernels, launch(): pl.pallas_call(body, out_shape=outputs, in_specs=[place for task in tasks...  557 us
    pallas_call x1, Pallas kernels, newton(): pl.pallas_call(functools.partial(newton_any_body, rows), in_specs=[pl.Blo...  47.5 us
    ppermute x9, waiting for transfers between devices, shifted(): return lax.ppermute(parts, axis, pairs)  44.3 us
    pallas_call x5, Pallas kernels, local_call(): pl.pallas_call(body, grid=(1,), in_specs=specs, out_specs=[pl.BlockSpec(a...  28.9 us
    dot_general x5, matrix products, dot(): lax.dot_general(first, second, (((first_dim,), (second_dim,)), ((), ())),...  28.8 us
    pallas_call x1, Pallas kernels, lookup(): pl.pallas_call(lookup_body, in_specs=[pl.BlockSpec(memory_space=pltpu.SME...  28.4 us
    sub x2, other arithmetic, adamw(): weight * (1.0 - rate * decay) - rate * update  22.8 us
    all_gather x1, waiting for transfers between devices, per_device(): out_all = lax.all_gather(grad_out, 'wide', axis=0, tiled=True)  22.4 us
  transfers between devices with their start and end apart: 16, of which 5 were waited for; matrix products, arithmetic and copies ran while one was open for 10% of the time, Pallas kernels for 46%

profile of v10, /device:TPU:17, one launch (start us, length us, event | category | flops | bytes accessed | tf_op | source)
XLA Modules:
  0.0 1003.6 jit_solution(18127902622000732429)
XLA Ops:
  12.5 18.9 %gather_ids.1 = (s32[8,16,128]{2,1,0:T(8,128)}, f32[4,8,8,128]{3,2,1,0:T(8,128)}, bf16[4,256,256]{2,1,0:T(8,128)(2,1)}) custom-call(s32[16,128]{1,0:T(8,128)} %pad_bitcast_fusion.refs_0_, f32[8,128]{1,0:T(8,128)} %bitcast_convert_fusion.refs_1_, bf16[256,256]{1,0:T(8,128)(2,1)} %bitcast.289), custom_call_target="tpu_custom_call" | custom-call | bytes 108032 | tf_op jit(solution)/shard_map/gather_ids/pallas_call | solution.py:139
  32.5 1.6 convert_element_type.134
  35.3 2.5 convert_element_type.125
  39.2 1.9 collective-permute-start
  46.9 28.4 %lookup.1 = (bf16[9216,256]{1,0:T(8,128)(2,1)}, bf16[8192,256]{1,0:T(8,128)(2,1)}, s32[9248]{0:T(1024)}) custom-call(s32[9216]{0:T(1024)} %and_select_fusion.ids_ref, s32[9344]{0:T(1024)} %concatenate.44.turn_ref, f32[8192,256]{1,0:T(8,128)} %table_ref.1), custom_call_target="tpu_custom_call" | custom-call | bytes 8388608 | tf_op jit(solution)/shard_map/lookup/pallas_call | solution.py:1620
  75.4 2.0 collective-permute-done.1.refs_2_
  77.4 11.6 %collective-permute-done.2.refs_3_ = bf16[528,512]{1,0:T(8,128)(2,1)S(1)} collective-permute-done((bf16[528,512]{1,0:T(8,128)(2,1)S(1)}, bf16[528,512]{1,0:T(8,128)(2,1)S(1)}, u32[]{:S(2)}, u32[]{:S(2)}) %collective-permute-start.2) | collective-permute-done | bytes 540704 | tf_op jit(solution)/shard_map/ppermute | solution.py:1732
  89.8 3.1 assemble.1
  97.7 1.9 multiply_sine_fusion
  101.3 5.4 fusion.46
  106.7 96.3 %fetch_rows.1.rows_ref = bf16[288,2048]{1,0:T(8,128)(2,1)} custom-call(bf16[4,2304,256]{2,1,0:T(8,128)(2,1)} %bitcast.252), custom_call_target="tpu_custom_call" | custom-call | bytes 737280 | tf_op jit(solution)/shard_map/fetch_rows/pallas_call | solution.py:139
  203.0 1.7 slice_convert_fusion
  204.7 5.0 make_heads.1
  209.7 37.8 %trade_heads.1 = (bf16[4,1,2,256,128]{4,3,2,1,0:T(8,128)(2,1)}, bf16[4,32,2048]{2,1,0:T(8,128)(2,1)}, bf16[8,256,256]{2,1,0:T(8,128)(2,1)}, bf16[512,2048]{1,0:T(8,128)(2,1)}) custom-call(bf16[4,1,2,256,128]{4,3,2,1,0:T(8,128)(2,1)} %get-tuple-element.124.refs_0_, bf16[32,2048]{1,0:T(8,128)(2,1)} %get-tuple-element.340.refs_1_, ...), custom_call_target="tpu_custom_call" | custom-call | bytes 999424 | tf_op jit(solution)/shard_map/trade_heads/pallas_call | solution.py:139
  247.5 7.0 attend.1
  257.2 2.5 convert_bitcast_fusion
  259.7 1.9 pad_maximum_fusion.2
  262.2 27.8 %settle_middle.1 = (f32[32,2048]{1,0:T(8,128)}, bf16[4,32,2048]{2,1,0:T(8,128)(2,1)}, bf16[8,128,512]{2,1,0:T(8,128)(2,1)}, bf16[8,128,256]{2,1,0:T(8,128)(2,1)}) custom-call(bf16[4,32,2048]{2,1,0:T(8,128)(2,1)} %bitcast.287, f32[32,2048]{1,0:T(8,128)} %get-tuple-element.339.refs_1_.refs_2_, f32[32,2048]{1,0:T(8,128)} %get-tuple-element.339.refs_1_.refs_2_, ...), custom_call_target="tpu_custom_call" | custom-call | bytes 509952 | tf_op jit(solution)/shard_map/settle_middle/pallas_call | solution.py:139
  289.9 13.4 %feed.1 = (f32[8,128,176]{2,1,0:T(8,128)}, f32[8,128,176]{2,1,0:T(8,128)}, bf16[8,128,176]{2,1,0:T(8,128)(2,1)}, bf16[128,2048]{1,0:T(8,128)(2,1)}) custom-call(bf16[128,2048]{1,0:T(8,128)(2,1)} %bitcast.261, bf16[8,3,176,2048]{3,2,1,0:T(8,128)(2,1)} %bitcast.243), custom_call_target="tpu_custom_call" | custom-call | flops 2214592512 | bytes 17301504 | tf_op jit(solution)/shard_map/feed/pallas_call | solution.py:1332
  303.9 30.3 %settle_late.1 = (f32[32,2048]{1,0:T(8,128)}, bf16[4,32,2048]{2,1,0:T(8,128)(2,1)}, bf16[512,2048]{1,0:T(8,128)(2,1)}) custom-call(bf16[4,32,2048]{2,1,0:T(8,128)(2,1)} %bitcast.291, f32[32,2048]{1,0:T(8,128)} %get-tuple-element.138.refs_1_, f32[32,2048]{1,0:T(8,128)} %get-tuple-element.339.refs_1_.refs_2_, f32[1,2048]{1,0:T(1,128)} %broadcast_in_dim.138.refs_3_, ...), custom_call_target="tpu_custom_call" | custom-call | bytes 755712 | tf_op jit(solution)/shard_map/settle_late/pallas_call | solution.py:139
  334.2 34.5 %gather_late.1 = (bf16[8,128,2048]{2,1,0:T(8,128)(2,1)}, bf16[4,352,512]{2,1,0:T(8,128)(2,1)}) custom-call(bf16[128,2048]{1,0:T(8,128)(2,1)} %bitcast.292, bf16[4,352,512]{2,1,0:T(8,128)(2,1)} %get-tuple-element.327.refs_1_), custom_call_target="tpu_custom_call" | custom-call | bytes 950272 | tf_op jit(solution)/shard_map/gather_late/pallas_call | solution.py:139
  368.7 2.0 constant_dynamic-update-slice_fusion.1
  371.5 6.1 fusion.50
  377.6 5.3 copy.195
  383.0 2.8 exponential_reduce_fusion
  385.8 10.0 fusion.51
  395.8 5.3 copy.191
  401.2 3.0 exponential_reduce_fusion.1
  404.6 3.5 select_reduce_fusion.1
  408.7 12.1 %combine_stats.1 = f32[3,8,256]{2,1,0:T(8,128)} custom-call(f32[3,8,256]{2,1,0:T(8,128)} %bitcast.302), custom_call_target="tpu_custom_call" | custom-call | bytes 6144 | tf_op jit(solution)/shard_map/combine_stats/pallas_call | solution.py:139
  421.8 3.3 fusion.2.refs_6_
  425.1 6.5 convolution_convert_fusion.1
  431.6 37.7 %sum_late.1 = (f32[128,2048]{1,0:T(8,128)}, bf16[4,352,512]{2,1,0:T(8,128)(2,1)}) custom-call(bf16[8,128,2048]{2,1,0:T(8,128)(2,1)} %bitcast.259, bf16[4,352,512]{2,1,0:T(8,128)(2,1)} %get-tuple-element.326.refs_1_), custom_call_target="tpu_custom_call" | custom-call | bytes 1015808 | tf_op jit(solution)/shard_map/sum_late/pallas_call | solution.py:139
  469.3 1.5 fusion.4.refs_5_
  471.5 6.1 convolution_convert_fusion
  480.4 26.0 %back_late.1 = (f32[32,2048]{1,0:T(8,128)}, f32[1,2048]{1,0:T(1,128)}, bf16[4,32,2048]{2,1,0:T(8,128)(2,1)}) custom-call(bf16[4,32,2048]{2,1,0:T(8,128)(2,1)} %bitcast.266, f32[32,2048]{1,0:T(8,128)} %get-tuple-element.145.refs_1_, f32[32,2048]{1,0:T(8,128)} %broadcast_in_dim.141.refs_2_, f32[1,2048]{1,0:T(1,128)} %broadcast_in_dim.138.refs_3_, ...), custom_call_target="tpu_custom_call" | custom-call | bytes 232448 | tf_op jit(solution)/shard_map/back_late/pallas_call | solution.py:139
  506.4 14.6 %feed_back.1 = (bf16[8,3,128,176]{3,2,1,0:T(8,128)(2,1)}, bf16[128,2048]{1,0:T(8,128)(2,1)}) custom-call(bf16[128,2048]{1,0:T(8,128)(2,1)} %bitcast.265, bf16[8,3,176,2048]{3,2,1,0:T(8,128)(2,1)} %bitcast.244, f32[8,128,176]{2,1,0:T(8,128)} %get-tuple-element.147.gate_ref, f32[8,128,176]{2,1,0:T(8,128)} %get-tuple-element.148.up_ref, ...), custom_call_target="tpu_custom_call" | custom-call | flops 2214592512 | bytes 17301504 | tf_op jit(solution)/shard_map/feed_back/pallas_call | solution.py:1384
  521.8 29.8 %back_middle.1 = (f32[32,2048]{1,0:T(8,128)}, f32[1,2048]{1,0:T(1,128)}, bf16[4,32,2048]{2,1,0:T(8,128)(2,1)}, bf16[8,3,128,176]{3,2,1,0:T(8,128)(2,1)}) custom-call(bf16[4,32,2048]{2,1,0:T(8,128)(2,1)} %bitcast.284, f32[32,2048]{1,0:T(8,128)} %get-tuple-element.138.refs_1_, f32[32,2048]{1,0:T(8,128)} %broadcast_multiply_fusion.refs_2_, ...), custom_call_target="tpu_custom_call" | custom-call | bytes 502784 | tf_op jit(solution)/shard_map/back_middle/pallas_call | solution.py:139
  551.6 22.4 %all-gather.11.cloned.1.call-done.refs_9_ = bf16[1024,2048]{1,0:T(8,128)(2,1)} async-done(((bf16[128,2048]{1,0:T(8,128)(2,1)}), bf16[1024,2048]{1,0:T(8,128)(2,1)}) %all-gather.11.cloned.1.call-update) | async-done | bytes 4194320 | tf_op jit(solution)/shard_map/all_gather | solution.py:1978
  576.7 3.6 pad_maximum_fusion.mom_ref
  582.3 7.8 attend_back.1
  590.1 43.2 %trade_grads.1 = (bf16[4,1,2,256,128]{4,3,2,1,0:T(8,128)(2,1)}, f32[32,2048]{1,0:T(8,128)}, f32[32,2048]{1,0:T(8,128)}, bf16[8,128,512]{2,1,0:T(8,128)(2,1)}, bf...) custom-call(bf16[4,1,2,256,128]{4,3,2,1,0:T(8,128)(2,1)} %get-tuple-element.158.refs_0_, ...), custom_call_target="tpu_custom_call" | custom-call | bytes 2704384 | tf_op jit(solution)/shard_map/trade_grads/pallas_call | solution.py:139
  633.3 6.0 rows_back.1
  639.3 138.2 %return_rows.1 = (bf16[4,2304,256]{2,1,0:T(8,128)(2,1)}, bf16[4,1024,176]{2,1,0:T(8,128)(2,1)}, bf16[8,256,1024]{2,1,0:T(8,128)(2,1)}, bf16[8,1024,256]{2,1,0:T(...) custom-call(bf16[288,2048]{1,0:T(8,128)(2,1)} %get-tuple-element.178, ...), custom_call_target="tpu_custom_call" | custom-call | bytes 4670464 | tf_op jit(solution)/shard_map/return_rows/pallas_call | solution.py:139
  777.5 3.5 convolution_bitcast_fusion
  783.7 1.7 convolution_bitcast_fusion.2
  788.6 20.8 %spread.1 = (f32[8192,256]{1,0:T(8,128)}, f32[8,256]{1,0:T(8,128)}) custom-call(s32[9216]{0:T(1024)} %and_select_fusion.ids_ref, s32[9248]{0:T(1024)} %get-tuple-element.186.list_ref, bf16[9216,256]{1,0:T(8,128)(2,1)} %bitcast.253, bf16[8192,256]{1,0:T(8,128)(2,1)} %bitcast.256), custom_call_target="tpu_custom_call" | custom-call | flops 2359296 | bytes 16777216 | tf_op jit(solution)/shard_map/spread/pallas_call | solution.py:1694
  811.4 1.9 pad_maximum_fusion.1
  814.2 7.4 fusion.5
  821.7 2.3 fusion.48
  827.3 24.7 %combine_sums.1 = (f32[4,8,256]{2,1,0:T(8,128)}, bf16[4,512,128]{2,1,0:T(8,128)(2,1)}, bf16[4,512,512]{2,1,0:T(8,128)(2,1)}) custom-call(f32[4,8,256]{2,1,0:T(8,128)} %maximum_maximum_fusion.1.refs_0_, bf16[512,128]{1,0:T(8,128)(2,1)} %bitcast.290, bf16[512,512]{1,0:T(8,128)(2,1)} %bitcast.263), custom_call_target="tpu_custom_call" | custom-call | bytes 417792 | tf_op jit(solution)/shard_map/combine_sums/pallas_call | solution.py:139
  857.7 1.5 collective-permute-start.3
  859.2 4.1 collective-permute-start.4
  863.3 2.3 collective-permute-start.5
  865.6 47.5 %newton.1 = bf16[4,704,512]{2,1,0:T(8,128)(2,1)} custom-call(f32[1]{0:T(128)} %bitcast.78.factor_ref, bf16[4,704,512]{2,1,0:T(8,128)(2,1)} %pad_maximum_fusion.mom_ref, f32[704,2048]{1,0:T(8,128)} %bitcast.251, bf16[4,512,512]{2,1,0:T(8,128)(2,1)} %get-tuple-element.199.qo_ref, bf16[4,512,128]{2,1,0:T(8,128)(2,1)} %get-tuple-element.200.kv_ref), custom_call_target="tpu_custom_call" | custom-call | flops 23789568000 | bytes 8650752 | tf_op jit(solution)/shard_map/newton/pallas_call | solution.py:1560
  915.0 2.7 convert_multiply_fusion
  921.5 1.8 copy.212
  923.2 22.1 %multiply_subtract_fusion = (f32[8192,256]{1,0:T(8,128)}, f32[8192,256]{1,0:T(8,128)}, f32[8192,256]{1,0:T(8,128)}) fusion(f32[8192,256]{1,0:T(8,128)} %table_ref.1, f32[8192,256]{1,0:T(8,128)} %get-tuple-element.191, f32[]{:T(128)} %div.51, f32[8192,256]{1,0:T(8,128)} %param.23, f32[8192,256]{1,0:T(8,128)} %param.24), kind=kLoop, calls=%fused_computation.2 | loop fusion | flops 31457280 | bytes 58720260 | tf_op jit(solution)/shard_map/sub | solution.py:1721
  946.1 6.7 bitcast_add_fusion
  952.7 27.5 %collective-permute-done.7 = bf16[704,512]{1,0:T(8,128)(2,1)} collective-permute-done((bf16[704,512]{1,0:T(8,128)(2,1)}, bf16[704,512]{1,0:T(8,128)(2,1)}, u32[]{:S(2)}, u32[]{:S(2)}) %collective-permute-start.7) | collective-permute-done | bytes 720928 | tf_op jit(solution)/shard_map/ppermute | solution.py:1732
  980.2 3.2 collective-permute-done.8
  983.4 3.1 fusion.22
  986.7 2.2 bitcast_subtract_fusion.1
  990.2 5.1 bitcast_subtract_fusion
  (233 shorter events, 56.1 us)
Async XLA Ops:
  7.2 197.5 %all-gather.7.cloned.1.call-start = ((), (), s32[]{:S(2)}) async-start(), calls=%async_computation.2 | async-start | bytes 9437184 | tf_op jit(solution)/shard_map/all_gather | solution.py:1803
  35.3 212.2 %all-gather.15.cloned.1.call-start = ((), (), s32[]{:S(2)}) async-start(), calls=%async_computation.8 | async-start | bytes 19464192 | tf_op jit(solution)/shard_map/all_gather | solution.py:1831
  37.9 5.8 copy-start.33
  39.2 36.2 %collective-permute-start = (bf16[528,512]{1,0:T(8,128)(2,1)}, bf16[528,512]{1,0:T(8,128)(2,1)S(1)}, u32[]{:S(2)}, u32[]{:S(2)}) collective-permute-start(bf16[528,512]{1,0:T(8,128)(2,1)} %get-tuple-element.334), channel_id=1, source_target_pairs={{0,1},{1,2},{2,3},{3,0},{4,5},{5,6},{6,7},{7,4},{8,9},{9,10},{10,1... | collective-permute-start | bytes 1622024 | tf_op jit(solution)/shard_map/ppermute | solution.py:1732
  41.0 36.4 %collective-permute-start.1 = (bf16[528,512]{1,0:T(8,128)(2,1)S(1)}, bf16[528,512]{1,0:T(8,128)(2,1)S(1)}, u32[]{:S(2)}, u32[]{:S(2)}) collective-permute-start(bf16[528,512]{1,0:T(8,128)(2,1)S(1)} %get-tuple-element.333), channel_id=1, source_target_pairs={{0,2},{1,3},{2,0},{3,1},{4,6},{5,7},{6,4},{7,5},{8,10},{9,11},{10,... | collective-permute-start | bytes 1622024 | tf_op jit(solution)/shard_map/ppermute | solution.py:1732
  42.3 46.7 %collective-permute-start.2 = (bf16[528,512]{1,0:T(8,128)(2,1)S(1)}, bf16[528,512]{1,0:T(8,128)(2,1)S(1)}, u32[]{:S(2)}, u32[]{:S(2)}) collective-permute-start(bf16[528,512]{1,0:T(8,128)(2,1)S(1)} %get-tuple-element.332), channel_id=1, source_target_pairs={{0,3},{1,0},{2,1},{3,2},{4,7},{5,4},{6,5},{7,6},{8,11},{9,8},{10,9... | collective-permute-start | bytes 1622024 | tf_op jit(solution)/shard_map/ppermute | solution.py:1732
  75.4 17.7 %copy-start.44 = (s32[1,2]{1,0:T(1,128)S(1)}, s32[1,2]{1,0:T(1,128)}, u32[]{:S(2)}) copy-start(s32[1,2]{1,0:T(1,128)} %param.20) | copy-start | bytes 28
  75.4 17.8 %copy-start.32 = (f32[4,8,8,128]{3,2,1,0:T(8,128)S(1)}, f32[4,8,8,128]{3,2,1,0:T(8,128)}, u32[]{:S(2)}) copy-start(f32[4,8,8,128]{3,2,1,0:T(8,128)} %get-tuple-element.122) | copy-start | bytes 393220
  75.4 19.4 %copy-start.41 = (s32[1,128]{1,0:T(1,128)S(1)}, s32[1,128]{1,0:T(1,128)}, u32[]{:S(2)}) copy-start(s32[1,128]{1,0:T(1,128)} %param.18) | copy-start | bytes 1540
  75.4 13.6 %copy-start.27 = (bf16[528,512]{1,0:T(8,128)(2,1)}, bf16[528,512]{1,0:T(8,128)(2,1)S(1)}, u32[]{:S(2)}) copy-start(bf16[528,512]{1,0:T(8,128)(2,1)S(1)} %collective-permute-done.refs_1_) | copy-start | bytes 1622020
  77.4 11.6 %copy-start.28 = (bf16[528,512]{1,0:T(8,128)(2,1)}, bf16[528,512]{1,0:T(8,128)(2,1)S(1)}, u32[]{:S(2)}) copy-start(bf16[528,512]{1,0:T(8,128)(2,1)S(1)} %collective-permute-done.1.refs_2_) | copy-start | bytes 1622020
  89.0 0.8 copy-start.29
  93.0 292.8 %all-gather.9.cloned.1.call-start = ((), (), s32[]{:S(2)}) async-start(), calls=%async_computation.3 | async-start | bytes 4718592 | tf_op jit(solution)/shard_map/all_gather | solution.py:1884
  96.5 10.2 %copy-start.34 = (s32[1024]{0:T(1024)}, s32[1024]{0:T(1024)S(1)}, u32[]{:S(2)}) copy-start(s32[1024]{0:T(1024)S(1)} %fusion.36) | copy-start | bytes 12292
  99.6 0.8 copy-start.5
  247.5 9.1 copy-start.9
  247.5 9.5 copy-start.24
  254.5 297.1 %reduce-scatter.3.cloned.1.call-start = ((), (), s32[]{:S(2)}) async-start(), calls=%async_computation.4 | async-start | bytes 4718592 | tf_op jit(solution)/shard_map/reduce_scatter | solution.py:1962
  303.9 66.8 %copy-start.16 = (bf16[512,2048]{1,0:T(8,128)(2,1)S(1)}, bf16[512,2048]{1,0:T(8,128)(2,1)}, u32[]{:S(2)}) copy-start(bf16[512,2048]{1,0:T(8,128)(2,1)} %get-tuple-element.140) | copy-start | bytes 6291460
  368.7 2.8 copy-start.7
  371.0 6.7 copy-start.19
  401.2 3.4 copy-start
  420.9 4.2 copy-start.20
  425.1 6.5 copy-start.2
  469.3 2.2 copy-start.21
  471.5 6.1 copy-start.3
  477.6 1.2 copy-start.18
  477.6 96.4 %all-gather.11.cloned.1.call-start = ((), (), s32[]{:S(2)}) async-start(), calls=%async_computation.5 | async-start | bytes 4718592 | tf_op jit(solution)/shard_map/all_gather | solution.py:1978
  506.4 127.0 %all-gather.13.cloned.1.call-start = ((), (), s32[]{:S(2)}) async-start(), calls=%async_computation.6 | async-start | bytes 4718592 | tf_op jit(solution)/shard_map/all_gather | solution.py:1993
  506.4 14.6 %copy-start.23 = (f32[32,2048]{1,0:T(8,128)S(1)}, f32[32,2048]{1,0:T(8,128)}, u32[]{:S(2)}) copy-start(f32[32,2048]{1,0:T(8,128)} %get-tuple-element.151) | copy-start | bytes 786436
  521.0 53.1 %copy-start.6 = (f32[1024,64]{1,0:T(8,128)S(1)}, f32[1024,64]{1,0:T(8,128)}, u32[]{:S(2)}) copy-start(f32[1024,64]{1,0:T(8,128)} %copy-done.5) | copy-start | bytes 786436
  551.5 23.9 %copy-start.4 = (bf16[8,3,128,176]{3,2,1,0:T(8,128)(2,1)S(1)}, bf16[8,3,128,176]{3,2,1,0:T(8,128)(2,1)}, u32[]{:S(2)}) copy-start(bf16[8,3,128,176]{3,2,1,0:T(8,128)(2,1)} %get-tuple-element.179) | copy-start | bytes 3244036
  551.6 25.1 %copy-start.39 = (f32[1,2048]{1,0:T(1,128)S(1)}, f32[1,2048]{1,0:T(1,128)}, u32[]{:S(2)}) copy-start(f32[1,2048]{1,0:T(1,128)} %get-tuple-element.170) | copy-start | bytes 24580
  574.0 247.7 %reduce-scatter.5.cloned.1.call-start = ((), (), s32[]{:S(2)}) async-start(), calls=%async_computation.7 | async-start | bytes 1310720 | tf_op jit(solution)/shard_map/reduce_scatter | solution.py:2039
  576.7 4.8 copy-start.31
  639.3 138.2 %copy-start.11 = (bf16[8,256,256]{2,1,0:T(8,128)(2,1)S(1)}, bf16[8,256,256]{2,1,0:T(8,128)(2,1)}, u32[]{:S(2)}) copy-start(bf16[8,256,256]{2,1,0:T(8,128)(2,1)} %get-tuple-element.177) | copy-start | bytes 3145732
  781.0 2.7 copy-start.30
  781.9 3.5 copy-start.22
  788.6 22.1 %copy-start.38 = (f32[1,2048]{1,0:T(1,128)S(1)}, f32[1,2048]{1,0:T(1,128)}, u32[]{:S(2)}) copy-start(f32[1,2048]{1,0:T(1,128)} %get-tuple-element.185) | copy-start | bytes 24580
  788.6 22.7 %copy-start.35 = (f32[1,2048]{1,0:T(1,128)S(1)}, f32[1,2048]{1,0:T(1,128)}, u32[]{:S(2)}) copy-start(f32[1,2048]{1,0:T(1,128)} %get-tuple-element.172) | copy-start | bytes 24580
  788.6 22.7 %copy-start.36 = (f32[1,2048]{1,0:T(1,128)S(1)}, f32[1,2048]{1,0:T(1,128)}, u32[]{:S(2)}) copy-start(f32[1,2048]{1,0:T(1,128)} %get-tuple-element.171) | copy-start | bytes 24580
  788.6 22.8 %copy-start.40 = (f32[1,2048]{1,0:T(1,128)S(1)}, f32[1,2048]{1,0:T(1,128)}, u32[]{:S(2)}) copy-start(f32[1,2048]{1,0:T(1,128)} %get-tuple-element.169) | copy-start | bytes 24580
  811.4 2.8 copy-start.1
  857.7 55.4 %collective-permute-start.3 = (bf16[3,176,512]{2,1,0:T(8,128)(2,1)S(1)}, bf16[3,176,512]{2,1,0:T(8,128)(2,1)S(1)}, u32[]{:S(2)}, u32[]{:S(2)}) collective-permute-start(bf16[3,176,512]{2,1,0:T(8,128)(2,1)S(1)} %get-tuple-element.330), channel_id=1, source_target_pairs={{0,1},{1,2},{2,3},{3,0},{4,5},{5,6},{6,7},{7,4},{8,9},{9,10},{10,1... | collective-permute-start | bytes 1622024 | tf_op jit(solution)/shard_map/ppermute | solution.py:1732
  859.2 53.9 %collective-permute-start.4 = (bf16[3,176,512]{2,1,0:T(8,128)(2,1)S(1)}, bf16[3,176,512]{2,1,0:T(8,128)(2,1)S(1)}, u32[]{:S(2)}, u32[]{:S(2)}) collective-permute-start(bf16[3,176,512]{2,1,0:T(8,128)(2,1)S(1)} %get-tuple-element.329), channel_id=1, source_target_pairs={{0,2},{1,3},{2,0},{3,1},{4,6},{5,7},{6,4},{7,5},{8,10},{9,11},{10,... | collective-permute-start | bytes 1622024 | tf_op jit(solution)/shard_map/ppermute | solution.py:1732
  863.3 49.8 %collective-permute-start.5 = (bf16[3,176,512]{2,1,0:T(8,128)(2,1)S(1)}, bf16[3,176,512]{2,1,0:T(8,128)(2,1)S(1)}, u32[]{:S(2)}, u32[]{:S(2)}) collective-permute-start(bf16[3,176,512]{2,1,0:T(8,128)(2,1)S(1)} %get-tuple-element.328), channel_id=1, source_target_pairs={{0,3},{1,0},{2,1},{3,2},{4,7},{5,4},{6,5},{7,6},{8,11},{9,8},{10,9... | collective-permute-start | bytes 1622024 | tf_op jit(solution)/shard_map/ppermute | solution.py:1732
  913.4 1.2 copy-start.10
  914.9 2.8 copy-start.12
  914.9 5.6 copy-start.25
  915.0 5.5 copy-start.26
  919.0 33.7 %collective-permute-start.6 = (bf16[704,512]{1,0:T(8,128)(2,1)}, bf16[704,512]{1,0:T(8,128)(2,1)}, u32[]{:S(2)}, u32[]{:S(2)}) collective-permute-start(bf16[704,512]{1,0:T(8,128)(2,1)} %get-tuple-element.325), channel_id=1, source_target_pairs={{0,3},{1,0},{2,1},{3,2},{4,7},{5,4},{6,5},{7,6},{8,11},{9,8},{10,9... | collective-permute-start | bytes 2162696 | tf_op jit(solution)/shard_map/ppermute | solution.py:1732
  919.0 61.2 %collective-permute-start.7 = (bf16[704,512]{1,0:T(8,128)(2,1)}, bf16[704,512]{1,0:T(8,128)(2,1)}, u32[]{:S(2)}, u32[]{:S(2)}) collective-permute-start(bf16[704,512]{1,0:T(8,128)(2,1)} %get-tuple-element.324), channel_id=1, source_target_pairs={{0,2},{1,3},{2,0},{3,1},{4,6},{5,7},{6,4},{7,5},{8,10},{9,11},{10,... | collective-permute-start | bytes 2162696 | tf_op jit(solution)/shard_map/ppermute | solution.py:1732
  920.3 63.1 %collective-permute-start.8 = (bf16[704,512]{1,0:T(8,128)(2,1)}, bf16[704,512]{1,0:T(8,128)(2,1)}, u32[]{:S(2)}, u32[]{:S(2)}) collective-permute-start(bf16[704,512]{1,0:T(8,128)(2,1)} %get-tuple-element.323), channel_id=1, source_target_pairs={{0,1},{1,2},{2,3},{3,0},{4,5},{5,6},{6,7},{7,4},{8,9},{9,10},{10,1... | collective-permute-start | bytes 2162696 | tf_op jit(solution)/shard_map/ppermute | solution.py:1732
  923.2 22.1 %copy-start.37 = (f32[3,64]{1,0:T(4,128)S(1)}, f32[3,64]{1,0:T(4,128)}, u32[]{:S(2)}) copy-start(f32[3,64]{1,0:T(4,128)} %param.31) | copy-start | bytes 2308
  923.2 22.1 %copy-start.42 = (f32[3,64]{1,0:T(4,128)S(1)}, f32[3,64]{1,0:T(4,128)}, u32[]{:S(2)}) copy-start(f32[3,64]{1,0:T(4,128)} %param.32) | copy-start | bytes 2308
  923.2 22.1 %copy-start.43 = (f32[3,64]{1,0:T(4,128)S(1)}, f32[3,64]{1,0:T(4,128)}, u32[]{:S(2)}) copy-start(f32[3,64]{1,0:T(4,128)} %param.33) | copy-start | bytes 2308
  952.7 33.9 %copy-start.8 = (f32[256,2,512]{2,1,0:T(2,128)S(1)}, f32[256,2,512]{2,1,0:T(2,128)}, u32[]{:S(2)}) copy-start(f32[256,2,512]{2,1,0:T(2,128)} %param.25) | copy-start | bytes 3145732
  986.5 2.7 copy-start.17
  986.5 3.7 copy-start.13
  986.5 3.7 copy-start.14
  986.5 3.7 copy-start.15
Sparse Core Ops, SparseCore 0:
  35.4 56.3 all-gather.6
  94.2 92.0 all-gather.14
  254.6 44.6 all-gather.8
  477.7 52.9 reduce-scatter.2
  532.6 41.3 all-gather.10
  575.9 47.5 all-gather.12
  783.2 24.3 reduce-scatter.4

commit v11 on v10

--- a/solution.py
+++ b/solution.py
@@ -272,15 +272,16 @@
     return trade("narrow", values, turned, block_at, shape, patience)
 
 
-def product(lefts, rights, sums):
+def product(lefts, rights, sums, dim=0):
     count = len(lefts)
     columns = rights[0].shape[1]
     block = min(512, columns)
     outputs = 1 if sums else count
-    rows = lefts[0].shape[1]
+    rows = lefts[0].shape[1 - dim]
 
     def steps(ins, outs, scratch):
         left_refs, right_refs = ins[:count], ins[count:]
+        right_refs = [right_refs[at % len(right_refs)] for at in range(count)]
         result_refs, square_ref = outs[:outputs], outs[outputs]
         yield
         square_ref[...] = jnp.zeros_like(square_ref)
@@ -291,7 +292,9 @@
                 spot = pl.ds(pl.multiple_of(part * block, block), block)
                 value = jnp.zeros((rows, block), FULL)
                 for member in members:
-                    value = value + dot(left_refs[member][...], right_refs[member][:, spot], 0, 0)
+                    value = value + dot(
+                        left_refs[member][...], right_refs[member][:, spot], dim, 0
+                    )
                 result_refs[at][:, spot] = value.astype(LOW)
                 if not sums:
                     square_ref[:, spot] = square_ref[:, spot] + jnp.sum(
@@ -305,6 +308,55 @@
     return Task(
         list(lefts) + list(rights),
         [struct((rows, columns), LOW)] * outputs + [struct((1, columns), FULL)],
+        [],
+        steps,
+        VMEM,
+        VMEM,
+        [],
+    )
+
+
+def exit_stats(features, table, targets):
+    rows, vocab = features.shape[0], table.shape[0]
+    block = min(256, vocab)
+
+    def steps(ins, outs, scratch):
+        features_ref, table_ref, targets_ref = ins
+        logits_ref, stats_ref = outs
+        yield
+
+        def strip(part):
+            return pl.ds(pl.multiple_of(part * block, block), block)
+
+        def over(function, start):
+            return lax.fori_loop(0, vocab // block, function, start)
+
+        def fill(part, peak):
+            logits = dot(table_ref[strip(part), :], features_ref[...], 1, 1)
+            logits_ref[strip(part), :] = logits
+            return jnp.maximum(peak, jnp.max(logits, axis=0, keepdims=True))
+
+        peak = over(fill, jnp.full((1, rows), MASKED, FULL))
+        lines = lax.broadcasted_iota(jnp.int32, (block, rows), 0)
+
+        def add(part, carry):
+            total, picked = carry
+            logits = logits_ref[strip(part), :]
+            hit = lines + part * block == targets_ref[...]
+            return (
+                total + jnp.sum(jnp.exp(logits - peak), axis=0, keepdims=True),
+                picked + jnp.sum(jnp.where(hit, logits, 0.0), axis=0, keepdims=True),
+            )
+
+        zero = jnp.zeros((1, rows), FULL)
+        total, picked = over(add, (zero, zero))
+        stats_ref[0:1, :] = peak
+        stats_ref[1:2, :] = total
+        stats_ref[2:3, :] = picked
+
+    return Task(
+        [features, table, targets],
+        [struct((vocab, rows), FULL), struct((3, rows), FULL)],
         [],
         steps,
         VMEM,
@@ -1489,11 +1541,14 @@
     current, low = problem[:2]
     parts, rows, columns = mom_ref.shape
     factor = factor_ref[0]
+    size = grad_ref.shape[1]
     for part in range(parts):
         spot = slice(part * columns, (part + 1) * columns)
-        current[:, spot] = MOMENTUM * mom_ref[part].astype(FULL) + factor * grad_ref[
-            :, spot
-        ].astype(FULL)
+        for source in range(parts):
+            here = slice(source * size, (source + 1) * size)
+            current[here, spot] = MOMENTUM * mom_ref[part, here, :].astype(
+                FULL
+            ) + factor * grad_ref[source, :, spot].astype(FULL)
     newton_steps([problem])
     for part in range(parts):
         out_ref[part] = low[:, part * columns : (part + 1) * columns]
@@ -1899,6 +1954,7 @@
         "settle_middle",
     )
     inner = inner.reshape(sel, width)
+    inner_all = lax.all_gather(inner, "wide", axis=0, tiled=True)
     gate, up, hidden, fed = feed(inner, ffn_w)
     final_own, late_part, table_top = launch(
         [
@@ -1912,31 +1968,32 @@
 
     table_count = table_own.shape[0]
     local_target = targets_all - (narrow_spot * vocab_rows + wide_spot * table_count)
-    has_target = local_target[:, None] == jnp.arange(table_count, dtype=jnp.int32)[None, :]
+    has_target = jnp.arange(table_count, dtype=jnp.int32)[:, None] == local_target[None, :]
     counted = (targets_all >= 0).astype(FULL)
     loss_count = jnp.sum(counted)
 
     def exit_logits(features):
-        logits = dot(features, table_own, 1, 1)
-        peak = jnp.max(logits, axis=-1)
-        total = jnp.sum(jnp.exp(logits - peak[:, None]), axis=-1)
-        picked = jnp.sum(jnp.where(has_target, logits, 0.0), axis=-1)
+        logits = dot(table_own, features, 1, 1)
+        peak = jnp.max(logits, axis=0)
+        total = jnp.sum(jnp.exp(logits - peak[None, :]), axis=0)
+        picked = jnp.sum(jnp.where(has_target, logits, 0.0), axis=0)
         return logits, jnp.stack([peak, total, picked])
 
     half = slot_rows // 2
-    late, mom_top = launch(
+    late, mom_top, early_logits, early_stats = launch(
         [
             gather_wide(late_part.reshape(sel, width)),
             swap_turned(mom_parts[:, :half]),
+            exit_stats(early, table_own, local_target[None, :]),
         ],
         5,
         "gather_late",
     )
     late = late.reshape(total_rows, width)
-    early_logits, early_stats = exit_logits(early)
     late_logits, late_stats = exit_logits(late)
     stats = jnp.concatenate([early_stats, late_stats], axis=1).reshape(3, 8, -1)
     stats = launch([combine(stats, merge_stats)], 6, "combine_stats")[0]
+    stats, inner_all = lax.optimization_barrier((stats, inner_all))
     stats = stats.reshape(3, -1)
     log_norms = stats[0] + jnp.log(stats[1])
     losses = log_norms - stats[2]
@@ -1946,10 +2003,10 @@
 
     def exit_back(logits, log_norm, weight):
         grad_logits = (
-            (jnp.exp(logits - log_norm[:, None]) - has_target.astype(FULL))
-            * (weight * counted)[:, None]
+            (jnp.exp(logits - log_norm[None, :]) - has_target.astype(FULL))
+            * (weight * counted)[None, :]
         ).astype(LOW)
-        return dot(grad_logits, table_own, 1, 0).astype(LOW), grad_logits
+        return dot(grad_logits, table_own, 0, 0).astype(LOW), grad_logits
 
     late_back, late_grad = exit_back(late_logits, log_norms[total_rows:], EXIT_LAST)
     grad_late, mom_low = launch(
@@ -1986,11 +2043,7 @@
         "back_middle",
     )
     acts = jnp.moveaxis(acts, 1, 0).reshape(3, total_rows, ffn_size)
-    grad_branch, grad_early, out_all = lax.optimization_barrier(
-        (grad_branch, grad_early, out_all)
-    )
-    inner, out_all = lax.optimization_barrier((inner, out_all))
-    inner_all = lax.all_gather(inner, "wide", axis=0, tiled=True)
+    grad_branch, grad_early = lax.optimization_barrier((grad_branch, grad_early))
     grad_branch = grad_branch.reshape(sel, width)
 
     kv_parts, grad_queries, pick_part = attend_back(
@@ -2003,12 +2056,12 @@
             sum_narrow(grad_early),
             gather_wide(grad_queries),
             split_columns("wide", grad_branch),
-            product([early_grad, late_grad], [early, late], True),
+            product([early_grad, late_grad], [early, late], True, 1),
         ],
         10,
         "trade_grads",
     )
-    grad_kv, inner_all = lax.optimization_barrier((grad_kv, inner_all))
+    grad_kv, out_all = lax.optimization_barrier((grad_kv, out_all))
     grad_base = grad_mid + grad_final * (1.0 - keep_layer)
     grad_rows, gain_attn, gain_early, grad_kv = rows_back(
         rows_low, gain_w, proj, grad_kv, grad_pick, grad_early, grad_base, repeat
@@ -2050,11 +2103,14 @@
     sums = jnp.stack(
         [gain_attn[0], gain_mid[0], gain_early[0] + gain_late[0], jnp.full((width,), squares)]
     )
-    sums, kv_owned, qo_owned = launch(
+    matrix = jnp.minimum(lax.rem(narrow_spot + narrow_count - turn, narrow_count), 2)
+    right = jnp.where(matrix == 2, out_all, inner_all)
+    sums, kv_owned, qo_owned, *owned, _ = launch(
         [
             combine(sums.reshape(4, 8, -1), add_two),
             send_owner(summed_kv.astype(LOW).reshape(2 * block_rows, kv_size)),
             later(send_owner(summed_qo.astype(LOW).reshape(2 * columns, q_size)), 1),
+            product([acts_owned[at] for at in range(narrow_count)], [right], False),
         ],
         12,
         "combine_sums",
@@ -2067,9 +2123,6 @@
     grad_norm = jnp.sqrt(square_total) / loss_count
     factor = jnp.minimum(1.0, CLIP_NORM / (grad_norm + 1e-06)) / loss_count
 
-    matrix = jnp.minimum(lax.rem(narrow_spot + narrow_count - turn, narrow_count), 2)
-    right = jnp.where(matrix == 2, out_all, inner_all)
-    owned = jnp.einsum("stf,td->sfd", acts_owned, right, preferred_element_type=FULL)
     final_parts, factor = lax.optimization_barrier((jnp.stack(grad_ffn), factor))
     size = width // narrow_count
 
@@ -2081,7 +2134,7 @@
         for step in range(1, narrow_count)
     ]
     directions = newton(
-        factor, mom_owned, owned.reshape(ffn_rows, width), qo_owned, kv_owned
+        factor, mom_owned, jnp.stack(owned), qo_owned, kv_owned
     )
     directions, pieces, ffn, factor = lax.optimization_barrier(
         (directions, pieces, ffn, factor)

time: 1020 us -> 988 us (0.969)
  waiting for transfers between devices: 66.9 us -> 37.8 us
  Pallas kernels: 711 us -> 733 us
    all_gather x1, waiting for transfers between devices: 22.4 us -> 0.02 us  [per_device(): out_all = lax.all_gather(grad_out, 'wide', axis=0, tiled=True)]
    pallas_call x13, Pallas kernels: 557 us -> 576 us  [launch(): pl.pallas_call(body, out_shape=outputs, in_specs=[place for task in tasks...]
    dot_general x2 -> x0, local copies, waits for them, and re-layouts: 10.7 us -> none  [dot(): lax.dot_general(first, second, (((first_dim,), (second_dim,)), ((), ())),...]
    dot_general x5 -> x4, matrix products: 28.8 us -> 26.1 us  [dot(): lax.dot_general(first, second, (((first_dim,), (second_dim,)), ((), ())),...]
  transfers between devices with their start and end apart: 16 -> 16, of which waited for: 5 -> 3; matrix products, arithmetic and copies ran while one was open for 10% -> 11% of each run, Pallas kernels for 46% -> 51%
where the time goes in v11:
time: 988 us; the launch traced here: 978 us
  Pallas kernels  733 us (74%)
  other arithmetic  90.7 us (9%)
  local copies, waits for them, and re-layouts  46.7 us (5%)
  waiting for transfers between devices  37.8 us (4%)
  matrix products  32.7 us (3%)
  between operations  23.2 us (2%)
  starting transfers between devices  14.1 us (1%)
    pallas_call x13, Pallas kernels, launch(): pl.pallas_call(body, out_shape=outputs, in_specs=[place for task in tasks...  576 us
    pallas_call x1, Pallas kernels, newton(): pl.pallas_call(functools.partial(newton_any_body, rows), in_specs=[pl.Blo...  46.8 us
    ppermute x9, waiting for transfers between devices, shifted(): return lax.ppermute(parts, axis, pairs)  37.6 us
    pallas_call x1, Pallas kernels, lookup(): pl.pallas_call(lookup_body, in_specs=[pl.BlockSpec(memory_space=pltpu.SME...  30.7 us
    pallas_call x5, Pallas kernels, local_call(): pl.pallas_call(body, grid=(1,), in_specs=specs, out_specs=[pl.BlockSpec(a...  28.5 us
    dot_general x4, matrix products, dot(): lax.dot_general(first, second, (((first_dim,), (second_dim,)), ((), ())),...  26.1 us
    pallas_call x1, Pallas kernels, spread(): pl.pallas_call(spread_body, in_specs=[smem, smem, VMEM, VMEM], out_specs=...  22.8 us
    sub x2, other arithmetic, adamw(): weight * (1.0 - rate * decay) - rate * update  22.8 us
  transfers between devices with their start and end apart: 16, of which 3 were waited for; matrix products, arithmetic and copies ran while one was open for 11% of the time, Pallas kernels for 51%

profile of v11, /device:TPU:17, one launch (start us, length us, event | category | flops | bytes accessed | tf_op | source)
XLA Modules:
  0.0 977.9 jit_solution(17801219420803690137)
XLA Ops:
  12.5 1.6 convert_element_type.134
  14.2 18.9 %gather_ids.1 = (s32[8,16,128]{2,1,0:T(8,128)}, f32[4,8,8,128]{3,2,1,0:T(8,128)}, bf16[4,256,256]{2,1,0:T(8,128)(2,1)}) custom-call(s32[16,128]{1,0:T(8,128)} %pad_bitcast_fusion.refs_0_, f32[8,128]{1,0:T(8,128)} %bitcast_convert_fusion.refs_1_, bf16[256,256]{1,0:T(8,128)(2,1)} %bitcast.296), custom_call_target="tpu_custom_call" | custom-call | bytes 108032 | tf_op jit(solution)/shard_map/gather_ids/pallas_call | solution.py:139
  35.4 2.5 convert_element_type.125
  39.2 1.9 collective-permute-start
  42.3 1.4 collective-permute-start.2
  47.5 30.7 %lookup.1 = (bf16[9216,256]{1,0:T(8,128)(2,1)}, bf16[8192,256]{1,0:T(8,128)(2,1)}, s32[9248]{0:T(1024)}) custom-call(s32[9216]{0:T(1024)} %and_select_fusion.ids_ref, s32[9344]{0:T(1024)} %concatenate.44.turn_ref, f32[8192,256]{1,0:T(8,128)} %table_ref.1), custom_call_target="tpu_custom_call" | custom-call | bytes 8388608 | tf_op jit(solution)/shard_map/lookup/pallas_call | solution.py:1675
  78.3 10.7 %collective-permute-done.2.refs_3_ = bf16[528,512]{1,0:T(8,128)(2,1)S(1)} collective-permute-done((bf16[528,512]{1,0:T(8,128)(2,1)S(1)}, bf16[528,512]{1,0:T(8,128)(2,1)S(1)}, u32[]{:S(2)}, u32[]{:S(2)}) %collective-permute-start.2) | collective-permute-done | bytes 540704 | tf_op jit(solution)/shard_map/ppermute | solution.py:1787
  89.8 3.1 assemble.1
  97.8 1.9 multiply_sine_fusion
  101.4 5.3 fusion.42
  106.8 96.6 %fetch_rows.1.rows_ref = bf16[288,2048]{1,0:T(8,128)(2,1)} custom-call(bf16[4,2304,256]{2,1,0:T(8,128)(2,1)} %bitcast.253), custom_call_target="tpu_custom_call" | custom-call | bytes 737280 | tf_op jit(solution)/shard_map/fetch_rows/pallas_call | solution.py:139
  203.4 1.7 slice_convert_fusion
  205.1 5.0 make_heads.1
  210.1 37.8 %trade_heads.1 = (bf16[4,1,2,256,128]{4,3,2,1,0:T(8,128)(2,1)}, bf16[4,32,2048]{2,1,0:T(8,128)(2,1)}, bf16[8,256,256]{2,1,0:T(8,128)(2,1)}, bf16[512,2048]{1,0:T(8,128)(2,1)}) custom-call(bf16[4,1,2,256,128]{4,3,2,1,0:T(8,128)(2,1)} %get-tuple-element.129.refs_0_, bf16[32,2048]{1,0:T(8,128)(2,1)} %get-tuple-element.354.refs_1_, ...), custom_call_target="tpu_custom_call" | custom-call | bytes 999424 | tf_op jit(solution)/shard_map/trade_heads/pallas_call | solution.py:139
  247.9 6.9 attend.1
  256.2 27.6 %settle_middle.1 = (f32[32,2048]{1,0:T(8,128)}, bf16[4,32,2048]{2,1,0:T(8,128)(2,1)}, bf16[8,128,512]{2,1,0:T(8,128)(2,1)}, bf16[8,128,256]{2,1,0:T(8,128)(2,1)}) custom-call(bf16[4,32,2048]{2,1,0:T(8,128)(2,1)} %bitcast.294, f32[32,2048]{1,0:T(8,128)} %get-tuple-element.353.refs_1_.refs_2_, f32[32,2048]{1,0:T(8,128)} %get-tuple-element.353.refs_1_.refs_2_, ...), custom_call_target="tpu_custom_call" | custom-call | bytes 509952 | tf_op jit(solution)/shard_map/settle_middle/pallas_call | solution.py:139
  285.8 2.5 convert_bitcast_fusion
  288.3 1.9 pad_maximum_fusion.3
  290.2 13.2 %feed.1 = (f32[8,128,176]{2,1,0:T(8,128)}, f32[8,128,176]{2,1,0:T(8,128)}, bf16[8,128,176]{2,1,0:T(8,128)(2,1)}, bf16[128,2048]{1,0:T(8,128)(2,1)}) custom-call(bf16[128,2048]{1,0:T(8,128)(2,1)} %bitcast.265, bf16[8,3,176,2048]{3,2,1,0:T(8,128)(2,1)} %bitcast.245), custom_call_target="tpu_custom_call" | custom-call | flops 2214592512 | bytes 17301504 | tf_op jit(solution)/shard_map/feed/pallas_call | solution.py:1384
  304.0 36.1 %settle_late.1 = (f32[32,2048]{1,0:T(8,128)}, bf16[4,32,2048]{2,1,0:T(8,128)(2,1)}, bf16[512,2048]{1,0:T(8,128)(2,1)}) custom-call(bf16[4,32,2048]{2,1,0:T(8,128)(2,1)} %bitcast.297, f32[32,2048]{1,0:T(8,128)} %get-tuple-element.142.refs_1_, f32[32,2048]{1,0:T(8,128)} %get-tuple-element.353.refs_1_.refs_2_, f32[1,2048]{1,0:T(1,128)} %broadcast_in_dim.137.refs_3_, ...), custom_call_target="tpu_custom_call" | custom-call | bytes 755712 | tf_op jit(solution)/shard_map/settle_late/pallas_call | solution.py:139
  340.2 3.2 constant_dynamic-update-slice_fusion.1
  343.4 1.6 constant_dynamic-update-slice_fusion.refs_3_
  344.9 38.3 %gather_late.1 = (bf16[8,128,2048]{2,1,0:T(8,128)(2,1)}, bf16[4,352,512]{2,1,0:T(8,128)(2,1)}, f32[1024,1024]{1,0:T(8,128)}, f32[3,1024]{1,0:T(4,128)}) custom-call(bf16[128,2048]{1,0:T(8,128)(2,1)} %bitcast.289, bf16[4,352,512]{2,1,0:T(8,128)(2,1)} %get-tuple-element.337.refs_1_, bf16[1024,2048]{1,0:T(8,128)(2,1)} %all-gather.9.cloned.1.call-done.refs_2_.refs_7_, ...), custom_call_target="tpu_custom_call" | custom-call | bytes 2525184 | tf_op jit(solution)/shard_map/gather_late/pallas_call | solution.py:139
  383.2 7.6 fusion.46
  390.9 2.0 copy-done.1
  394.7 12.1 %combine_stats.1 = f32[3,8,256]{2,1,0:T(8,128)} custom-call(f32[3,8,256]{2,1,0:T(8,128)} %bitcast.311), custom_call_target="tpu_custom_call" | custom-call | bytes 6144 | tf_op jit(solution)/shard_map/combine_stats/pallas_call | solution.py:139
  407.6 3.3 fusion.2.refs_6_
  411.0 9.2 convolution_convert_fusion.1
  420.2 37.4 %sum_late.1 = (f32[128,2048]{1,0:T(8,128)}, bf16[4,352,512]{2,1,0:T(8,128)(2,1)}) custom-call(bf16[8,128,2048]{2,1,0:T(8,128)(2,1)} %bitcast.260, bf16[4,352,512]{2,1,0:T(8,128)(2,1)} %get-tuple-element.336.refs_1_), custom_call_target="tpu_custom_call" | custom-call | bytes 1015808 | tf_op jit(solution)/shard_map/sum_late/pallas_call | solution.py:139
  458.8 9.1 convolution_convert_fusion
  470.6 26.4 %back_late.1 = (f32[32,2048]{1,0:T(8,128)}, f32[1,2048]{1,0:T(1,128)}, bf16[4,32,2048]{2,1,0:T(8,128)(2,1)}) custom-call(bf16[4,32,2048]{2,1,0:T(8,128)(2,1)} %bitcast.266, f32[32,2048]{1,0:T(8,128)} %get-tuple-element.152.refs_1_, f32[32,2048]{1,0:T(8,128)} %broadcast_in_dim.140.refs_2_, f32[1,2048]{1,0:T(1,128)} %broadcast_in_dim.137.refs_3_, ...), custom_call_target="tpu_custom_call" | custom-call | bytes 232448 | tf_op jit(solution)/shard_map/back_late/pallas_call | solution.py:139
  497.2 1.3 pad_maximum_fusion.6
  498.6 14.5 %feed_back.1 = (bf16[8,3,128,176]{3,2,1,0:T(8,128)(2,1)}, bf16[128,2048]{1,0:T(8,128)(2,1)}) custom-call(bf16[128,2048]{1,0:T(8,128)(2,1)} %bitcast.263, bf16[8,3,176,2048]{3,2,1,0:T(8,128)(2,1)} %bitcast.246, f32[8,128,176]{2,1,0:T(8,128)} %get-tuple-element.154.gate_ref, f32[8,128,176]{2,1,0:T(8,128)} %get-tuple-element.155.up_ref, ...), custom_call_target="tpu_custom_call" | custom-call | flops 2214592512 | bytes 17301504 | tf_op jit(solution)/shard_map/feed_back/pallas_call | solution.py:1436
  513.8 31.8 %back_middle.1 = (f32[32,2048]{1,0:T(8,128)}, f32[1,2048]{1,0:T(1,128)}, bf16[4,32,2048]{2,1,0:T(8,128)(2,1)}, bf16[8,3,128,176]{3,2,1,0:T(8,128)(2,1)}) custom-call(bf16[4,32,2048]{2,1,0:T(8,128)(2,1)} %bitcast.290, f32[32,2048]{1,0:T(8,128)} %get-tuple-element.142.refs_1_, f32[32,2048]{1,0:T(8,128)} %broadcast_multiply_fusion.refs_2_, ...), custom_call_target="tpu_custom_call" | custom-call | bytes 502784 | tf_op jit(solution)/shard_map/back_middle/pallas_call | solution.py:139
  546.3 2.8 copy.171
  549.7 1.8 pad_maximum_fusion.mom_ref
  553.5 7.4 attend_back.1
  561.0 44.5 %trade_grads.1 = (bf16[4,1,2,256,128]{4,3,2,1,0:T(8,128)(2,1)}, f32[32,2048]{1,0:T(8,128)}, f32[32,2048]{1,0:T(8,128)}, bf16[8,128,512]{2,1,0:T(8,128)(2,1)}, bf...) custom-call(bf16[4,1,2,256,128]{4,3,2,1,0:T(8,128)(2,1)} %get-tuple-element.166.refs_0_, ...), custom_call_target="tpu_custom_call" | custom-call | bytes 2704384 | tf_op jit(solution)/shard_map/trade_grads/pallas_call | solution.py:139
  605.4 6.0 rows_back.1
  611.4 137.3 %return_rows.1 = (bf16[4,2304,256]{2,1,0:T(8,128)(2,1)}, bf16[4,1024,176]{2,1,0:T(8,128)(2,1)}, bf16[8,256,1024]{2,1,0:T(8,128)(2,1)}, bf16[8,1024,256]{2,1,0:T(...) custom-call(bf16[288,2048]{1,0:T(8,128)(2,1)} %get-tuple-element.184, ...), custom_call_target="tpu_custom_call" | custom-call | bytes 4670464 | tf_op jit(solution)/shard_map/return_rows/pallas_call | solution.py:139
  748.8 3.5 convolution_bitcast_fusion
  754.4 1.7 convolution_bitcast_fusion.1
  756.1 1.5 convolution_bitcast_fusion.2
  760.0 22.8 %spread.1 = (f32[8192,256]{1,0:T(8,128)}, f32[8,256]{1,0:T(8,128)}) custom-call(s32[9216]{0:T(1024)} %and_select_fusion.ids_ref, s32[9248]{0:T(1024)} %get-tuple-element.192.list_ref, bf16[9216,256]{1,0:T(8,128)(2,1)} %bitcast.254, bf16[8192,256]{1,0:T(8,128)(2,1)} %bitcast.257), custom_call_target="tpu_custom_call" | custom-call | flops 2359296 | bytes 16777216 | tf_op jit(solution)/shard_map/spread/pallas_call | solution.py:1749
  784.2 1.9 pad_maximum_fusion.2
  786.1 3.6 slice_bitcast_fusion
  789.7 2.4 broadcast_select_fusion.refs_7_
  792.1 2.3 fusion.44
  797.8 31.3 %combine_sums.1 = (f32[4,8,256]{2,1,0:T(8,128)}, bf16[4,512,128]{2,1,0:T(8,128)(2,1)}, bf16[4,512,512]{2,1,0:T(8,128)(2,1)}, bf16[176,2048]{1,0:T(8,128)(2,1)}, ...) custom-call(f32[4,8,256]{2,1,0:T(8,128)} %maximum_maximum_fusion.1.refs_0_, ...), custom_call_target="tpu_custom_call" | custom-call | bytes 1483776 | tf_op jit(solution)/shard_map/combine_sums/pallas_call | solution.py:139
  829.1 1.3 slice_bitcast_fusion.4
  836.6 4.5 collective-permute-start.4
  841.2 2.4 collective-permute-start.5
  843.5 1.8 pad_maximum_fusion.1.grad_ref
  845.3 46.8 %newton.1 = bf16[4,704,512]{2,1,0:T(8,128)(2,1)} custom-call(f32[1]{0:T(128)} %bitcast.80.factor_ref, bf16[4,704,512]{2,1,0:T(8,128)(2,1)} %pad_maximum_fusion.mom_ref, bf16[4,176,2048]{2,1,0:T(8,128)(2,1)} %pad_maximum_fusion.1.grad_ref, bf16[4,512,512]{2,1,0:T(8,128)(2,1)} %get-tuple-element.209.qo_ref, bf16[4,512,128]{2,1,0:T(8,128)(2,1)} %get-tuple-element.210.kv_ref), custom_call_target="tpu_custom_call" | custom-call | flops 23789568000 | bytes 8650752 | tf_op jit(solution)/shard_map/newton/pallas_call | solution.py:1615
  893.0 1.7 dynamic-slice_bitcast_fusion
  896.5 1.8 copy.182
  899.9 2.7 convert_multiply_fusion
  902.5 22.1 %multiply_subtract_fusion = (f32[8192,256]{1,0:T(8,128)}, f32[8192,256]{1,0:T(8,128)}, f32[8192,256]{1,0:T(8,128)}) fusion(f32[8192,256]{1,0:T(8,128)} %table_ref.1, f32[8192,256]{1,0:T(8,128)} %get-tuple-element.198, f32[]{:T(128)} %div.51, f32[8192,256]{1,0:T(8,128)} %param.23, f32[8192,256]{1,0:T(8,128)} %param.24), kind=kLoop, calls=%fused_computation.2 | loop fusion | flops 31457280 | bytes 58720260 | tf_op jit(solution)/shard_map/sub | solution.py:1776
  925.4 6.7 bitcast_add_fusion
  932.0 23.7 %collective-permute-done.7 = bf16[704,512]{1,0:T(8,128)(2,1)} collective-permute-done((bf16[704,512]{1,0:T(8,128)(2,1)S(1)}, bf16[704,512]{1,0:T(8,128)(2,1)}, u32[]{:S(2)}, u32[]{:S(2)}) %collective-permute-start.7) | collective-permute-done | bytes 720928 | tf_op jit(solution)/shard_map/ppermute | solution.py:1787
  955.7 3.2 collective-permute-done.8
  958.9 2.1 fusion.18
  961.2 2.2 bitcast_subtract_fusion.1
  964.7 5.1 bitcast_subtract_fusion
  (234 shorter events, 50.5 us)
Async XLA Ops:
  7.2 197.9 %all-gather.7.cloned.1.call-start = ((), (), s32[]{:S(2)}) async-start(), calls=%async_computation.2 | async-start | bytes 9437184 | tf_op jit(solution)/shard_map/all_gather | solution.py:1858
  35.3 212.6 %all-gather.15.cloned.1.call-start = ((), (), s32[]{:S(2)}) async-start(), calls=%async_computation.8 | async-start | bytes 19464192 | tf_op jit(solution)/shard_map/all_gather | solution.py:1886
  37.9 5.8 copy-start.35
  39.2 39.1 %collective-permute-start = (bf16[528,512]{1,0:T(8,128)(2,1)}, bf16[528,512]{1,0:T(8,128)(2,1)S(1)}, u32[]{:S(2)}, u32[]{:S(2)}) collective-permute-start(bf16[528,512]{1,0:T(8,128)(2,1)} %get-tuple-element.344), channel_id=1, source_target_pairs={{0,1},{1,2},{2,3},{3,0},{4,5},{5,6},{6,7},{7,4},{8,9},{9,10},{10,1... | collective-permute-start | bytes 1622024 | tf_op jit(solution)/shard_map/ppermute | solution.py:1787
  41.0 37.3 %collective-permute-start.1 = (bf16[528,512]{1,0:T(8,128)(2,1)S(1)}, bf16[528,512]{1,0:T(8,128)(2,1)S(1)}, u32[]{:S(2)}, u32[]{:S(2)}) collective-permute-start(bf16[528,512]{1,0:T(8,128)(2,1)S(1)} %get-tuple-element.343), channel_id=1, source_target_pairs={{0,2},{1,3},{2,0},{3,1},{4,6},{5,7},{6,4},{7,5},{8,10},{9,11},{10,... | collective-permute-start | bytes 1622024 | tf_op jit(solution)/shard_map/ppermute | solution.py:1787
  42.3 46.7 %collective-permute-start.2 = (bf16[528,512]{1,0:T(8,128)(2,1)S(1)}, bf16[528,512]{1,0:T(8,128)(2,1)S(1)}, u32[]{:S(2)}, u32[]{:S(2)}) collective-permute-start(bf16[528,512]{1,0:T(8,128)(2,1)S(1)} %get-tuple-element.342), channel_id=1, source_target_pairs={{0,3},{1,0},{2,1},{3,2},{4,7},{5,4},{6,5},{7,6},{8,11},{9,8},{10,9... | collective-permute-start | bytes 1622024 | tf_op jit(solution)/shard_map/ppermute | solution.py:1787
  78.3 14.8 %copy-start.33 = (f32[4,8,8,128]{3,2,1,0:T(8,128)S(1)}, f32[4,8,8,128]{3,2,1,0:T(8,128)}, u32[]{:S(2)}) copy-start(f32[4,8,8,128]{3,2,1,0:T(8,128)} %get-tuple-element.127) | copy-start | bytes 393220
  78.3 15.7 %copy-start.46 = (s32[1,2]{1,0:T(1,128)S(1)}, s32[1,2]{1,0:T(1,128)}, u32[]{:S(2)}) copy-start(s32[1,2]{1,0:T(1,128)} %param.20) | copy-start | bytes 28
  78.3 16.6 %copy-start.43 = (s32[1,128]{1,0:T(1,128)S(1)}, s32[1,128]{1,0:T(1,128)}, u32[]{:S(2)}) copy-start(s32[1,128]{1,0:T(1,128)} %param.18) | copy-start | bytes 1540
  78.3 10.7 %copy-start.26 = (bf16[528,512]{1,0:T(8,128)(2,1)}, bf16[528,512]{1,0:T(8,128)(2,1)S(1)}, u32[]{:S(2)}) copy-start(bf16[528,512]{1,0:T(8,128)(2,1)S(1)} %collective-permute-done.refs_1_) | copy-start | bytes 1622020
  78.3 10.7 %copy-start.27 = (bf16[528,512]{1,0:T(8,128)(2,1)}, bf16[528,512]{1,0:T(8,128)(2,1)S(1)}, u32[]{:S(2)}) copy-start(bf16[528,512]{1,0:T(8,128)(2,1)S(1)} %collective-permute-done.1.refs_2_) | copy-start | bytes 1622020
  89.0 0.8 copy-start.28
  93.0 251.9 %all-gather.9.cloned.1.call-start = ((), (), s32[]{:S(2)}) async-start(), calls=%async_computation.3 | async-start | bytes 4718592 | tf_op jit(solution)/shard_map/all_gather | solution.py:1939
  96.6 10.2 %copy-start.36 = (s32[1024]{0:T(1024)}, s32[1024]{0:T(1024)S(1)}, u32[]{:S(2)}) copy-start(s32[1024]{0:T(1024)S(1)} %fusion.32) | copy-start | bytes 12292
  99.7 0.8 copy-start.6
  247.9 37.3 %copy-start.20 = (f32[256,2,128]{2,1,0:T(2,128)S(1)}, f32[256,2,128]{2,1,0:T(2,128)}, u32[]{:S(2)}) copy-start(f32[256,2,128]{2,1,0:T(2,128)} %param.28) | copy-start | bytes 786436
  254.8 30.4 %copy-start.10 = (f32[256,2,512]{2,1,0:T(2,128)S(1)}, f32[256,2,512]{2,1,0:T(2,128)}, u32[]{:S(2)}) copy-start(f32[256,2,512]{2,1,0:T(2,128)} %param.26) | copy-start | bytes 3145732
  254.8 152.0 %all-gather.11.cloned.1.call-start = ((), (), s32[]{:S(2)}) async-start(), calls=%async_computation.4 | async-start | bytes 4718592 | tf_op jit(solution)/shard_map/all_gather | solution.py:1957
  283.8 269.7 %reduce-scatter.3.cloned.1.call-start = ((), (), s32[]{:S(2)}) async-start(), calls=%async_computation.5 | async-start | bytes 4718592 | tf_op jit(solution)/shard_map/reduce_scatter | solution.py:2019
  303.4 39.9 %copy-start.13 = (bf16[512,2048]{1,0:T(8,128)(2,1)S(1)}, bf16[512,2048]{1,0:T(8,128)(2,1)}, u32[]{:S(2)}) copy-start(bf16[512,2048]{1,0:T(8,128)(2,1)} %get-tuple-element.146) | copy-start | bytes 6291460
  383.2 9.7 copy-start.34
  390.9 2.0 copy-start.1
  390.9 3.1 copy-start.37
  411.0 9.2 copy-start.3
  420.2 37.4 %copy-start.9 = (f32[1024,1024]{1,0:T(8,128)S(1)}, f32[1024,1024]{1,0:T(8,128)}, u32[]{:S(2)}) copy-start(f32[1024,1024]{1,0:T(8,128)} %get-tuple-element.161) | copy-start | bytes 12582916
  458.7 9.1 copy-start.4
  467.8 1.2 copy-start.17
  467.8 29.4 %copy-start.7 = (f32[1024,64]{1,0:T(8,128)S(1)}, f32[1024,64]{1,0:T(8,128)}, u32[]{:S(2)}) copy-start(f32[1024,64]{1,0:T(8,128)} %copy-done.6) | copy-start | bytes 786436
  467.9 137.6 %all-gather.13.cloned.1.call-start = ((), (), s32[]{:S(2)}) async-start(), calls=%async_computation.6 | async-start | bytes 4718592 | tf_op jit(solution)/shard_map/all_gather | solution.py:2035
  497.1 295.1 %reduce-scatter.5.cloned.1.call-start = ((), (), s32[]{:S(2)}) async-start(), calls=%async_computation.7 | async-start | bytes 1310720 | tf_op jit(solution)/shard_map/reduce_scatter | solution.py:2092
  498.6 14.5 %copy-start.19 = (f32[32,2048]{1,0:T(8,128)S(1)}, f32[32,2048]{1,0:T(8,128)}, u32[]{:S(2)}) copy-start(f32[32,2048]{1,0:T(8,128)} %get-tuple-element.158) | copy-start | bytes 786436
  513.1 36.7 %copy-start.14 = (bf16[4,352,512]{2,1,0:T(8,128)(2,1)S(1)}, bf16[4,352,512]{2,1,0:T(8,128)(2,1)}, u32[]{:S(2)}) copy-start(bf16[4,352,512]{2,1,0:T(8,128)(2,1)} %get-tuple-element.203) | copy-start | bytes 4325380
  513.1 36.6 %copy-start.15 = (bf16[4,352,512]{2,1,0:T(8,128)(2,1)S(1)}, bf16[4,352,512]{2,1,0:T(8,128)(2,1)}, u32[]{:S(2)}) copy-start(bf16[4,352,512]{2,1,0:T(8,128)(2,1)} %get-tuple-element.204) | copy-start | bytes 4325380
  546.3 5.3 copy-start.5
  549.7 3.1 copy-start.32
  611.4 137.3 %copy-start.12 = (bf16[8,256,256]{2,1,0:T(8,128)(2,1)S(1)}, bf16[8,256,256]{2,1,0:T(8,128)(2,1)}, u32[]{:S(2)}) copy-start(bf16[8,256,256]{2,1,0:T(8,128)(2,1)} %get-tuple-element.183) | copy-start | bytes 3145732
  752.2 2.1 copy-start.31
  753.1 2.9 copy-start.18
  754.3 5.0 copy-start.38
  754.3 5.0 copy-start.39
  754.3 5.0 copy-start.42
  754.3 5.0 copy-start.41
  784.1 5.5 copy-start
  784.1 5.5 copy-start.2
  834.5 9.0 copy-start.22
  834.5 9.0 copy-start.23
  834.5 9.0 copy-start.24
  834.5 9.0 copy-start.25
  835.8 56.4 %collective-permute-start.3 = (bf16[3,176,512]{2,1,0:T(8,128)(2,1)}, bf16[3,176,512]{2,1,0:T(8,128)(2,1)S(1)}, u32[]{:S(2)}, u32[]{:S(2)}) collective-permute-start(bf16[3,176,512]{2,1,0:T(8,128)(2,1)} %get-tuple-element.340), channel_id=1, source_target_pairs={{0,1},{1,2},{2,3},{3,0},{4,5},{5,6},{6,7},{7,4},{8,9},{9,10},{10,1... | collective-permute-start | bytes 1622024 | tf_op jit(solution)/shard_map/ppermute | solution.py:1787
  836.6 55.5 %collective-permute-start.4 = (bf16[3,176,512]{2,1,0:T(8,128)(2,1)}, bf16[3,176,512]{2,1,0:T(8,128)(2,1)S(1)}, u32[]{:S(2)}, u32[]{:S(2)}) collective-permute-start(bf16[3,176,512]{2,1,0:T(8,128)(2,1)} %get-tuple-element.339), channel_id=1, source_target_pairs={{0,2},{1,3},{2,0},{3,1},{4,6},{5,7},{6,4},{7,5},{8,10},{9,11},{10,... | collective-permute-start | bytes 1622024 | tf_op jit(solution)/shard_map/ppermute | solution.py:1787
  841.2 51.0 %collective-permute-start.5 = (bf16[3,176,512]{2,1,0:T(8,128)(2,1)}, bf16[3,176,512]{2,1,0:T(8,128)(2,1)S(1)}, u32[]{:S(2)}, u32[]{:S(2)}) collective-permute-start(bf16[3,176,512]{2,1,0:T(8,128)(2,1)} %get-tuple-element.338), channel_id=1, source_target_pairs={{0,3},{1,0},{2,1},{3,2},{4,7},{5,4},{6,5},{7,6},{8,11},{9,8},{10,9... | collective-permute-start | bytes 1622024 | tf_op jit(solution)/shard_map/ppermute | solution.py:1787
  892.1 4.1 copy-start.11
  892.2 0.8 copy-start.29
  893.0 5.4 copy-start.21
  894.7 37.3 %collective-permute-start.6 = (bf16[704,512]{1,0:T(8,128)(2,1)S(1)}, bf16[704,512]{1,0:T(8,128)(2,1)}, u32[]{:S(2)}, u32[]{:S(2)}) collective-permute-start(bf16[704,512]{1,0:T(8,128)(2,1)S(1)} %get-tuple-element.335), channel_id=1, source_target_pairs={{0,3},{1,0},{2,1},{3,2},{4,7},{5,4},{6,5},{7,6},{8,11},{9,8},{10,9... | collective-permute-start | bytes 2162696 | tf_op jit(solution)/shard_map/ppermute | solution.py:1787
  894.8 60.9 %collective-permute-start.7 = (bf16[704,512]{1,0:T(8,128)(2,1)S(1)}, bf16[704,512]{1,0:T(8,128)(2,1)}, u32[]{:S(2)}, u32[]{:S(2)}) collective-permute-start(bf16[704,512]{1,0:T(8,128)(2,1)S(1)} %get-tuple-element.334), channel_id=1, source_target_pairs={{0,2},{1,3},{2,0},{3,1},{4,6},{5,7},{6,4},{7,5},{8,10},{9,11},{10,... | collective-permute-start | bytes 2162696 | tf_op jit(solution)/shard_map/ppermute | solution.py:1787
  896.0 63.0 %collective-permute-start.8 = (bf16[704,512]{1,0:T(8,128)(2,1)S(1)}, bf16[704,512]{1,0:T(8,128)(2,1)}, u32[]{:S(2)}, u32[]{:S(2)}) collective-permute-start(bf16[704,512]{1,0:T(8,128)(2,1)S(1)} %get-tuple-element.333), channel_id=1, source_target_pairs={{0,1},{1,2},{2,3},{3,0},{4,5},{5,6},{6,7},{7,4},{8,9},{9,10},{10,1... | collective-permute-start | bytes 2162696 | tf_op jit(solution)/shard_map/ppermute | solution.py:1787
  896.5 3.0 copy-start.30
  902.5 22.1 %copy-start.40 = (f32[3,64]{1,0:T(4,128)S(1)}, f32[3,64]{1,0:T(4,128)}, u32[]{:S(2)}) copy-start(f32[3,64]{1,0:T(4,128)} %param.31) | copy-start | bytes 2308
  902.5 22.1 %copy-start.44 = (f32[3,64]{1,0:T(4,128)S(1)}, f32[3,64]{1,0:T(4,128)}, u32[]{:S(2)}) copy-start(f32[3,64]{1,0:T(4,128)} %param.32) | copy-start | bytes 2308
  902.5 22.1 %copy-start.45 = (f32[3,64]{1,0:T(4,128)S(1)}, f32[3,64]{1,0:T(4,128)}, u32[]{:S(2)}) copy-start(f32[3,64]{1,0:T(4,128)} %param.33) | copy-start | bytes 2308
  932.0 29.2 %copy-start.8 = (f32[256,2,512]{2,1,0:T(2,128)S(1)}, f32[256,2,512]{2,1,0:T(2,128)}, u32[]{:S(2)}) copy-start(f32[256,2,512]{2,1,0:T(2,128)} %param.25) | copy-start | bytes 3145732
  961.1 2.7 copy-start.16
Sparse Core Ops, SparseCore 0:
  35.4 56.3 all-gather.6
  94.3 92.0 all-gather.14
  255.0 42.5 all-gather.8
  299.3 51.8 all-gather.10
  468.0 52.7 reduce-scatter.2
  522.6 43.0 all-gather.12
  754.5 24.9 reduce-scatter.4

commit v12 on v11

--- a/solution.py
+++ b/solution.py
@@ -272,34 +272,30 @@
     return trade("narrow", values, turned, block_at, shape, patience)
 
 
-def product(lefts, rights, sums, dim=0):
-    count = len(lefts)
+def product(lefts, rights, dim, order):
+    count, rows = len(order), lefts[0].shape[-1 if dim == 0 else -2]
     columns = rights[0].shape[1]
     block = min(512, columns)
-    outputs = 1 if sums else count
-    rows = lefts[0].shape[1 - dim]
 
     def steps(ins, outs, scratch):
-        left_refs, right_refs = ins[:count], ins[count:]
-        right_refs = [right_refs[at % len(right_refs)] for at in range(count)]
-        result_refs, square_ref = outs[:outputs], outs[outputs]
-        yield
+        left_refs, right_refs = ins[: len(lefts)], ins[len(lefts) :]
+        result_ref, square_ref = outs
         square_ref[...] = jnp.zeros_like(square_ref)
-        for at in range(outputs):
-            members = range(count) if sums else [at]
+
+        def left_of(member):
+            return left_refs[0][member] if lefts[0].ndim == 3 else left_refs[member][...]
+
+        for at, members in enumerate(order):
 
             def strip(part, carry):
                 spot = pl.ds(pl.multiple_of(part * block, block), block)
                 value = jnp.zeros((rows, block), FULL)
-                for member in members:
-                    value = value + dot(
-                        left_refs[member][...], right_refs[member][:, spot], dim, 0
-                    )
-                result_refs[at][:, spot] = value.astype(LOW)
-                if not sums:
-                    square_ref[:, spot] = square_ref[:, spot] + jnp.sum(
-                        value * value, axis=0, keepdims=True
-                    )
+                for left, right in members:
+                    value = value + dot(left_of(left), right_refs[right][:, spot], dim, 0)
+                result_ref[at, :, spot] = value.astype(LOW)
+                square_ref[:, spot] = square_ref[:, spot] + jnp.sum(
+                    value * value, axis=0, keepdims=True
+                )
                 return carry
 
             lax.fori_loop(0, columns // block, strip, 0)
@@ -307,7 +303,7 @@
 
     return Task(
         list(lefts) + list(rights),
-        [struct((rows, columns), LOW)] * outputs + [struct((1, columns), FULL)],
+        [struct((count, rows, columns), LOW), struct((1, columns), FULL)],
         [],
         steps,
         VMEM,
@@ -323,7 +319,6 @@
     def steps(ins, outs, scratch):
         features_ref, table_ref, targets_ref = ins
         logits_ref, stats_ref = outs
-        yield
 
         def strip(part):
             return pl.ds(pl.multiple_of(part * block, block), block)
@@ -353,6 +348,7 @@
         stats_ref[0:1, :] = peak
         stats_ref[1:2, :] = total
         stats_ref[2:3, :] = picked
+        yield
 
     return Task(
         [features, table, targets],
@@ -2006,18 +2002,18 @@
             (jnp.exp(logits - log_norm[None, :]) - has_target.astype(FULL))
             * (weight * counted)[None, :]
         ).astype(LOW)
-        return dot(grad_logits, table_own, 0, 0).astype(LOW), grad_logits
-
-    late_back, late_grad = exit_back(late_logits, log_norms[total_rows:], EXIT_LAST)
+        return grad_logits
+
+    late_grad = exit_back(late_logits, log_norms[total_rows:], EXIT_LAST)
+    late_back = dot(late_grad, table_own, 0, 0).astype(LOW)
     grad_late, mom_low = launch(
         [sum_wide(late_back), swap_turned(mom_parts[:, half:])], 7, "sum_late"
     )
     early_norms, grad_late = lax.optimization_barrier((log_norms[:total_rows], grad_late))
-    early_back, early_grad = exit_back(early_logits, early_norms, EXIT_EARLY)
+    early_grad = exit_back(early_logits, early_norms, EXIT_EARLY)
     mom_owned = jnp.concatenate([mom_top, mom_low], axis=1)
 
-    grad_early = lax.psum_scatter(early_back, "wide", scatter_dimension=0, tiled=True)
-    grad_final, gain_late, grad_out = launch(
+    grad_final, gain_late, grad_out, early_back, _ = launch(
         [
             settle_back(
                 grad_late.astype(LOW),
@@ -2026,10 +2022,12 @@
                 keep_row,
                 gain_w[2:3],
             ),
+            product([early_grad], [table_own], 0, [[(0, 0)]]),
         ],
         8,
         "back_late",
     )
+    grad_early = lax.psum_scatter(early_back[0], "wide", scatter_dimension=0, tiled=True)
     grad_layer = grad_final * keep_layer
     grad_out = grad_out.reshape(sel, width)
     out_all = lax.all_gather(grad_out, "wide", axis=0, tiled=True)
@@ -2056,7 +2054,7 @@
             sum_narrow(grad_early),
             gather_wide(grad_queries),
             split_columns("wide", grad_branch),
-            product([early_grad, late_grad], [early, late], True, 1),
+            product([early_grad, late_grad], [early, late], 1, [[(0, 0), (1, 1)]]),
         ],
         10,
         "trade_grads",
@@ -2066,20 +2064,19 @@
     grad_rows, gain_attn, gain_early, grad_kv = rows_back(
         rows_low, gain_w, proj, grad_kv, grad_pick, grad_early, grad_base, repeat
     )
-    rights = (inner_all, inner_all, out_all)
     summed_qo = jnp.stack(
         [
             jnp.einsum("wtc,wtf->cf", pick_cols, queries_wide, preferred_element_type=FULL),
             jnp.einsum("wtc,wtf->cf", branch_cols, mixed_wide, preferred_element_type=FULL),
         ]
     )
-    grad_rows, acts_owned, kv_wide, head_cols_all, *grad_ffn, ffn_squares = launch(
+    grad_rows, acts_owned, kv_wide, head_cols_all, grad_ffn, ffn_squares = launch(
         [
             return_rows(grad_rows),
             swap_owned(acts, 5),
             later(gather_wide(grad_kv, 3), 2),
-            later(split_columns("wide", grad_head, 3), 2),
-            product([acts[j] for j in range(3)], rights, False),
+            later(split_columns("wide", grad_head[0], 3), 2),
+            product([acts], [inner_all, out_all], 0, [[(0, 0)], [(1, 0)], [(2, 1)]]),
         ],
         11,
         "return_rows",
@@ -2105,12 +2102,12 @@
     )
     matrix = jnp.minimum(lax.rem(narrow_spot + narrow_count - turn, narrow_count), 2)
     right = jnp.where(matrix == 2, out_all, inner_all)
-    sums, kv_owned, qo_owned, *owned, _ = launch(
+    sums, kv_owned, qo_owned, owned, _ = launch(
         [
             combine(sums.reshape(4, 8, -1), add_two),
             send_owner(summed_kv.astype(LOW).reshape(2 * block_rows, kv_size)),
             later(send_owner(summed_qo.astype(LOW).reshape(2 * columns, q_size)), 1),
-            product([acts_owned[at] for at in range(narrow_count)], [right], False),
+            later(product([acts_owned], [right], 0, [[(at, 0)] for at in range(narrow_count)]), 2),
         ],
         12,
         "combine_sums",
@@ -2123,7 +2120,7 @@
     grad_norm = jnp.sqrt(square_total) / loss_count
     factor = jnp.minimum(1.0, CLIP_NORM / (grad_norm + 1e-06)) / loss_count
 
-    final_parts, factor = lax.optimization_barrier((jnp.stack(grad_ffn), factor))
+    final_parts, factor = lax.optimization_barrier((grad_ffn, factor))
     size = width // narrow_count
 
     def final_piece(spot):
@@ -2134,7 +2131,7 @@
         for step in range(1, narrow_count)
     ]
     directions = newton(
-        factor, mom_owned, jnp.stack(owned), qo_owned, kv_owned
+        factor, mom_owned, owned, qo_owned, kv_owned
     )
     directions, pieces, ffn, factor = lax.optimization_barrier(
         (directions, pieces, ffn, factor)

time: 988 us -> 996 us (level)
  waiting for transfers between devices: 37.8 us -> 50.4 us
  matrix products: 32.7 us -> 22.6 us
    reduce_scatter x1, waiting for transfers between devices: 0.01 us -> 10.3 us  [per_device(): lax.psum_scatter(early_back[0], 'wide', scatter_dimension=0, tiled=True)]
    dot_general x4 -> x3, matrix products: 26.1 us -> 17 us  [dot(): lax.dot_general(first, second, (((first_dim,), (second_dim,)), ((), ())),...]
  transfers between devices with their start and end apart: 16 -> 16, of which waited for: 3 -> 5; matrix products, arithmetic and copies ran while one was open for 11% -> 10% of each run, Pallas kernels for 51% -> 48%
where the time goes in v12:
time: 996 us; the launch traced here: 983 us
  Pallas kernels  739 us (74%)
  other arithmetic  94.1 us (9%)
  waiting for transfers between devices  50.4 us (5%)
  local copies, waits for them, and re-layouts  39.4 us (4%)
  between operations  23.2 us (2%)
  matrix products  22.6 us (2%)
  starting transfers between devices  14.4 us (1%)
    pallas_call x13, Pallas kernels, launch(): pl.pallas_call(body, out_shape=outputs, in_specs=[place for task in tasks...  585 us
    pallas_call x1, Pallas kernels, newton(): pl.pallas_call(functools.partial(newton_any_body, rows), in_specs=[pl.Blo...  46.8 us
    ppermute x9, waiting for transfers between devices, shifted(): return lax.ppermute(parts, axis, pairs)  39.3 us
    pallas_call x1, Pallas kernels, lookup(): pl.pallas_call(lookup_body, in_specs=[pl.BlockSpec(memory_space=pltpu.SME...  28.9 us
    pallas_call x5, Pallas kernels, local_call(): pl.pallas_call(body, grid=(1,), in_specs=specs, out_specs=[pl.BlockSpec(a...  28.4 us
    sub x2, other arithmetic, adamw(): weight * (1.0 - rate * decay) - rate * update  22.8 us
    pallas_call x1, Pallas kernels, spread(): pl.pallas_call(spread_body, in_specs=[smem, smem, VMEM, VMEM], out_specs=...  21 us
  transfers between devices with their start and end apart: 16, of which 5 were waited for; matrix products, arithmetic and copies ran while one was open for 10% of the time, Pallas kernels for 48%

profile of v12, /device:TPU:17, one launch (start us, length us, event | category | flops | bytes accessed | tf_op | source)
XLA Modules:
  0.0 982.7 jit_solution(5383845741162452058)
XLA Ops:
  12.5 1.6 convert_element_type.131
  14.2 18.9 %gather_ids.1 = (s32[8,16,128]{2,1,0:T(8,128)}, f32[4,8,8,128]{3,2,1,0:T(8,128)}, bf16[4,256,256]{2,1,0:T(8,128)(2,1)}) custom-call(s32[16,128]{1,0:T(8,128)} %pad_bitcast_fusion.refs_0_, f32[8,128]{1,0:T(8,128)} %bitcast_convert_fusion.refs_1_, bf16[256,256]{1,0:T(8,128)(2,1)} %bitcast.270), custom_call_target="tpu_custom_call" | custom-call | bytes 108032 | tf_op jit(solution)/shard_map/gather_ids/pallas_call | solution.py:139
  35.4 2.5 convert_element_type.122
  39.2 1.9 collective-permute-start
  42.3 1.4 collective-permute-start.2
  47.5 28.9 %lookup.1 = (bf16[9216,256]{1,0:T(8,128)(2,1)}, bf16[8192,256]{1,0:T(8,128)(2,1)}, s32[9248]{0:T(1024)}) custom-call(s32[9216]{0:T(1024)} %and_select_fusion.ids_ref, s32[9344]{0:T(1024)} %concatenate.44.turn_ref, f32[8192,256]{1,0:T(8,128)} %table_ref.1), custom_call_target="tpu_custom_call" | custom-call | bytes 8388608 | tf_op jit(solution)/shard_map/lookup/pallas_call | solution.py:1671
  77.4 11.6 %collective-permute-done.2.refs_3_ = bf16[528,512]{1,0:T(8,128)(2,1)S(1)} collective-permute-done((bf16[528,512]{1,0:T(8,128)(2,1)S(1)}, bf16[528,512]{1,0:T(8,128)(2,1)S(1)}, u32[]{:S(2)}, u32[]{:S(2)}) %collective-permute-start.2) | collective-permute-done | bytes 540704 | tf_op jit(solution)/shard_map/ppermute | solution.py:1783
  89.8 3.1 assemble.1
  97.8 1.9 multiply_sine_fusion
  101.4 5.4 fusion.42
  106.7 96.6 %fetch_rows.1.rows_ref = bf16[288,2048]{1,0:T(8,128)(2,1)} custom-call(bf16[4,2304,256]{2,1,0:T(8,128)(2,1)} %bitcast.234), custom_call_target="tpu_custom_call" | custom-call | bytes 737280 | tf_op jit(solution)/shard_map/fetch_rows/pallas_call | solution.py:139
  203.3 1.7 slice_convert_fusion
  205.0 5.0 make_heads.1
  210.0 37.8 %trade_heads.1 = (bf16[4,1,2,256,128]{4,3,2,1,0:T(8,128)(2,1)}, bf16[4,32,2048]{2,1,0:T(8,128)(2,1)}, bf16[8,256,256]{2,1,0:T(8,128)(2,1)}, bf16[512,2048]{1,0:T(8,128)(2,1)}) custom-call(bf16[4,1,2,256,128]{4,3,2,1,0:T(8,128)(2,1)} %get-tuple-element.125.refs_0_, bf16[32,2048]{1,0:T(8,128)(2,1)} %get-tuple-element.339.refs_1_, ...), custom_call_target="tpu_custom_call" | custom-call | bytes 999424 | tf_op jit(solution)/shard_map/trade_heads/pallas_call | solution.py:139
  247.9 6.9 attend.1
  256.1 27.6 %settle_middle.1 = (f32[32,2048]{1,0:T(8,128)}, bf16[4,32,2048]{2,1,0:T(8,128)(2,1)}, bf16[8,128,512]{2,1,0:T(8,128)(2,1)}, bf16[8,128,256]{2,1,0:T(8,128)(2,1)}) custom-call(bf16[4,32,2048]{2,1,0:T(8,128)(2,1)} %bitcast.268, f32[32,2048]{1,0:T(8,128)} %get-tuple-element.338.refs_1_.refs_2_, f32[32,2048]{1,0:T(8,128)} %get-tuple-element.338.refs_1_.refs_2_, ...), custom_call_target="tpu_custom_call" | custom-call | bytes 509952 | tf_op jit(solution)/shard_map/settle_middle/pallas_call | solution.py:139
  285.7 2.5 convert_bitcast_fusion
  288.2 1.9 pad_maximum_fusion.1
  290.1 13.2 %feed.1 = (f32[8,128,176]{2,1,0:T(8,128)}, f32[8,128,176]{2,1,0:T(8,128)}, bf16[8,128,176]{2,1,0:T(8,128)(2,1)}, bf16[128,2048]{1,0:T(8,128)(2,1)}) custom-call(bf16[128,2048]{1,0:T(8,128)(2,1)} %bitcast.249, bf16[8,3,176,2048]{3,2,1,0:T(8,128)(2,1)} %bitcast.227), custom_call_target="tpu_custom_call" | custom-call | flops 2214592512 | bytes 17301504 | tf_op jit(solution)/shard_map/feed/pallas_call | solution.py:1380
  304.0 36.2 %settle_late.1 = (f32[32,2048]{1,0:T(8,128)}, bf16[4,32,2048]{2,1,0:T(8,128)(2,1)}, bf16[512,2048]{1,0:T(8,128)(2,1)}) custom-call(bf16[4,32,2048]{2,1,0:T(8,128)(2,1)} %bitcast.271, f32[32,2048]{1,0:T(8,128)} %get-tuple-element.138.refs_1_, f32[32,2048]{1,0:T(8,128)} %get-tuple-element.338.refs_1_.refs_2_, f32[1,2048]{1,0:T(1,128)} %broadcast_in_dim.137.refs_3_, ...), custom_call_target="tpu_custom_call" | custom-call | bytes 755712 | tf_op jit(solution)/shard_map/settle_late/pallas_call | solution.py:139
  340.2 3.2 constant_dynamic-update-slice_fusion.1
  343.3 1.6 constant_dynamic-update-slice_fusion.refs_3_.refs_6_
  344.9 38.4 %gather_late.1 = (bf16[8,128,2048]{2,1,0:T(8,128)(2,1)}, bf16[4,352,512]{2,1,0:T(8,128)(2,1)}, f32[1024,1024]{1,0:T(8,128)}, f32[3,1024]{1,0:T(4,128)}) custom-call(bf16[128,2048]{1,0:T(8,128)(2,1)} %bitcast.263, bf16[4,352,512]{2,1,0:T(8,128)(2,1)} %get-tuple-element.329.refs_1_, bf16[1024,2048]{1,0:T(8,128)(2,1)} %all-gather.9.cloned.1.call-done.refs_2_.refs_7_, ...), custom_call_target="tpu_custom_call" | custom-call | bytes 2525184 | tf_op jit(solution)/shard_map/gather_late/pallas_call | solution.py:139
  383.3 7.6 fusion.45
  391.0 2.0 copy-done
  394.7 12.2 %combine_stats.1 = f32[3,8,256]{2,1,0:T(8,128)} custom-call(f32[3,8,256]{2,1,0:T(8,128)} %bitcast.285), custom_call_target="tpu_custom_call" | custom-call | bytes 6144 | tf_op jit(solution)/shard_map/combine_stats/pallas_call | solution.py:139
  407.8 3.3 fusion.2.refs_6_
  411.1 9.2 convolution_convert_fusion
  420.4 37.4 %sum_late.1 = (f32[128,2048]{1,0:T(8,128)}, bf16[4,352,512]{2,1,0:T(8,128)(2,1)}) custom-call(bf16[8,128,2048]{2,1,0:T(8,128)(2,1)} %bitcast.242, bf16[4,352,512]{2,1,0:T(8,128)(2,1)} %get-tuple-element.328.refs_1_), custom_call_target="tpu_custom_call" | custom-call | bytes 1015808 | tf_op jit(solution)/shard_map/sum_late/pallas_call | solution.py:139
  457.8 2.1 convert_element_type.146
  459.8 2.5 fusion.4.refs_5_
  463.0 29.8 %back_late.1 = (f32[32,2048]{1,0:T(8,128)}, f32[1,2048]{1,0:T(1,128)}, bf16[4,32,2048]{2,1,0:T(8,128)(2,1)}, bf16[1,1024,2048]{2,1,0:T(8,128)(2,1)}, f32[1,2048]{1,0:T(1,128)}) custom-call(bf16[4,32,2048]{2,1,0:T(8,128)(2,1)} %bitcast.245, f32[32,2048]{1,0:T(8,128)} %get-tuple-element.148.refs_1_, f32[32,2048]{1,0:T(8,128)} %broadcast_in_dim.140.refs_2_, ...), custom_call_target="tpu_custom_call" | custom-call | bytes 1544192 | tf_op jit(solution)/shard_map/back_late/pallas_call | solution.py:139
  493.9 1.3 pad_maximum_fusion.4
  495.2 14.9 %feed_back.1 = (bf16[8,3,128,176]{3,2,1,0:T(8,128)(2,1)}, bf16[128,2048]{1,0:T(8,128)(2,1)}) custom-call(bf16[128,2048]{1,0:T(8,128)(2,1)} %bitcast.247, bf16[8,3,176,2048]{3,2,1,0:T(8,128)(2,1)} %bitcast.228, f32[8,128,176]{2,1,0:T(8,128)} %get-tuple-element.152.gate_ref, f32[8,128,176]{2,1,0:T(8,128)} %get-tuple-element.153.up_ref, ...), custom_call_target="tpu_custom_call" | custom-call | flops 2214592512 | bytes 17301504 | tf_op jit(solution)/shard_map/feed_back/pallas_call | solution.py:1432
  510.8 37.1 %back_middle.1 = (f32[32,2048]{1,0:T(8,128)}, f32[1,2048]{1,0:T(1,128)}, bf16[4,32,2048]{2,1,0:T(8,128)(2,1)}, bf16[8,3,128,176]{3,2,1,0:T(8,128)(2,1)}) custom-call(bf16[4,32,2048]{2,1,0:T(8,128)(2,1)} %bitcast.264, f32[32,2048]{1,0:T(8,128)} %get-tuple-element.138.refs_1_, f32[32,2048]{1,0:T(8,128)} %broadcast_multiply_fusion.refs_2_, ...), custom_call_target="tpu_custom_call" | custom-call | bytes 502784 | tf_op jit(solution)/shard_map/back_middle/pallas_call | solution.py:139
  547.9 2.7 copy.171
  550.6 1.7 multiply_add_fusion.1.base_ref
  552.3 10.3 %reduce-scatter.3.cloned.1.call-done = bf16[128,2048]{1,0:T(8,128)(2,1)} async-done(((bf16[1024,2048]{1,0:T(8,128)(2,1)}), bf16[128,2048]{1,0:T(8,128)(2,1)}) %reduce-scatter.3.cloned.1.call-update) | async-done | bytes 524304 | tf_op jit(solution)/shard_map/reduce_scatter | solution.py:2030
  562.6 7.4 attend_back.1
  570.0 44.0 %trade_grads.1 = (bf16[4,1,2,256,128]{4,3,2,1,0:T(8,128)(2,1)}, f32[32,2048]{1,0:T(8,128)}, f32[32,2048]{1,0:T(8,128)}, bf16[8,128,512]{2,1,0:T(8,128)(2,1)}, bf...) custom-call(bf16[4,1,2,256,128]{4,3,2,1,0:T(8,128)(2,1)} %get-tuple-element.163.refs_0_, ...), custom_call_target="tpu_custom_call" | custom-call | bytes 2704384 | tf_op jit(solution)/shard_map/trade_grads/pallas_call | solution.py:139
  614.0 6.0 rows_back.1
  620.0 136.5 %return_rows.1 = (bf16[4,2304,256]{2,1,0:T(8,128)(2,1)}, bf16[4,1024,176]{2,1,0:T(8,128)(2,1)}, bf16[8,256,1024]{2,1,0:T(8,128)(2,1)}, bf16[8,1024,256]{2,1,0:T(...) custom-call(bf16[288,2048]{1,0:T(8,128)(2,1)} %get-tuple-element.181.refs_0_, ...), custom_call_target="tpu_custom_call" | custom-call | bytes 4146176 | tf_op jit(solution)/shard_map/return_rows/pallas_call | solution.py:139
  756.5 3.5 convolution_bitcast_fusion
  763.5 3.1 pad_maximum_fusion.mom_ref
  767.2 1.7 convolution_bitcast_fusion.2
  771.3 21.0 %spread.1 = (f32[8192,256]{1,0:T(8,128)}, f32[8,256]{1,0:T(8,128)}) custom-call(s32[9216]{0:T(1024)} %and_select_fusion.ids_ref, s32[9248]{0:T(1024)} %get-tuple-element.189.list_ref, bf16[9216,256]{1,0:T(8,128)(2,1)} %bitcast.235, bf16[8192,256]{1,0:T(8,128)(2,1)} %bitcast.238), custom_call_target="tpu_custom_call" | custom-call | flops 2359296 | bytes 16777216 | tf_op jit(solution)/shard_map/spread/pallas_call | solution.py:1745
  793.6 4.6 broadcast_select_fusion.refs_4_
  798.3 2.5 fusion.43
  804.1 33.0 %combine_sums.1 = (f32[4,8,256]{2,1,0:T(8,128)}, bf16[4,512,128]{2,1,0:T(8,128)(2,1)}, bf16[4,512,512]{2,1,0:T(8,128)(2,1)}, bf16[4,176,2048]{2,1,0:T(8,128)(2,1)}, f32[1,2048]{1,0:T(1,128)}) custom-call(f32[4,8,256]{2,1,0:T(8,128)} %maximum_maximum_fusion.1.refs_0_, bf16[512,128]{1,0:T(8,128)(2,1)} %bitcast.265, bf16[512,512]{1,0:T(8,128)(2,1)} %bitcast.254, ...), custom_call_target="tpu_custom_call" | custom-call | bytes 1483776 | tf_op jit(solution)/shard_map/combine_sums/pallas_call | solution.py:139
  837.1 1.3 slice_bitcast_fusion
  842.8 1.6 collective-permute-start.3
  844.4 4.2 collective-permute-start.4
  848.6 2.3 collective-permute-start.5
  850.9 46.8 %newton.1 = bf16[4,704,512]{2,1,0:T(8,128)(2,1)} custom-call(f32[1]{0:T(128)} %bitcast.72.factor_ref, bf16[4,704,512]{2,1,0:T(8,128)(2,1)} %pad_maximum_fusion.mom_ref, bf16[4,176,2048]{2,1,0:T(8,128)(2,1)} %get-tuple-element.200.grad_ref, bf16[4,512,512]{2,1,0:T(8,128)(2,1)} %get-tuple-element.201.qo_ref, bf16[4,512,128]{2,1,0:T(8,128)(2,1)} %get-tuple-element.202.kv_ref), custom_call_target="tpu_custom_call" | custom-call | flops 23789568000 | bytes 8650752 | tf_op jit(solution)/shard_map/newton/pallas_call | solution.py:1611
  897.8 1.8 dynamic-slice_bitcast_fusion
  901.4 1.8 copy.182
  904.7 2.7 convert_multiply_fusion
  907.4 22.1 %multiply_subtract_fusion = (f32[8192,256]{1,0:T(8,128)}, f32[8192,256]{1,0:T(8,128)}, f32[8192,256]{1,0:T(8,128)}) fusion(f32[8192,256]{1,0:T(8,128)} %table_ref.1, f32[8192,256]{1,0:T(8,128)} %get-tuple-element.195, f32[]{:T(128)} %div.51, f32[8192,256]{1,0:T(8,128)} %param.23, f32[8192,256]{1,0:T(8,128)} %param.24), kind=kLoop, calls=%fused_computation.2 | loop fusion | flops 31457280 | bytes 58720260 | tf_op jit(solution)/shard_map/sub | solution.py:1772
  930.2 6.7 bitcast_add_fusion
  936.9 23.8 %collective-permute-done.7 = bf16[704,512]{1,0:T(8,128)(2,1)} collective-permute-done((bf16[704,512]{1,0:T(8,128)(2,1)S(1)}, bf16[704,512]{1,0:T(8,128)(2,1)}, u32[]{:S(2)}, u32[]{:S(2)}) %collective-permute-start.7) | collective-permute-done | bytes 720928 | tf_op jit(solution)/shard_map/ppermute | solution.py:1783
  960.7 3.0 collective-permute-done.8
  963.7 2.1 fusion.18
  966.0 2.2 bitcast_subtract_fusion.1
  969.5 5.1 bitcast_subtract_fusion
  (209 shorter events, 45.0 us)
Async XLA Ops:
  7.2 197.8 %all-gather.7.cloned.1.call-start = ((), (), s32[]{:S(2)}) async-start(), calls=%async_computation.2 | async-start | bytes 9437184 | tf_op jit(solution)/shard_map/all_gather | solution.py:1854
  35.3 212.5 %all-gather.15.cloned.1.call-start = ((), (), s32[]{:S(2)}) async-start(), calls=%async_computation.8 | async-start | bytes 19464192 | tf_op jit(solution)/shard_map/all_gather | solution.py:1882
  37.9 5.8 copy-start.25
  39.2 37.3 %collective-permute-start = (bf16[528,512]{1,0:T(8,128)(2,1)}, bf16[528,512]{1,0:T(8,128)(2,1)S(1)}, u32[]{:S(2)}, u32[]{:S(2)}) collective-permute-start(bf16[528,512]{1,0:T(8,128)(2,1)} %get-tuple-element.336), channel_id=1, source_target_pairs={{0,1},{1,2},{2,3},{3,0},{4,5},{5,6},{6,7},{7,4},{8,9},{9,10},{10,1... | collective-permute-start | bytes 1622024 | tf_op jit(solution)/shard_map/ppermute | solution.py:1783
  41.0 36.4 %collective-permute-start.1 = (bf16[528,512]{1,0:T(8,128)(2,1)S(1)}, bf16[528,512]{1,0:T(8,128)(2,1)S(1)}, u32[]{:S(2)}, u32[]{:S(2)}) collective-permute-start(bf16[528,512]{1,0:T(8,128)(2,1)S(1)} %get-tuple-element.335), channel_id=1, source_target_pairs={{0,2},{1,3},{2,0},{3,1},{4,6},{5,7},{6,4},{7,5},{8,10},{9,11},{10,... | collective-permute-start | bytes 1622024 | tf_op jit(solution)/shard_map/ppermute | solution.py:1783
  42.3 46.7 %collective-permute-start.2 = (bf16[528,512]{1,0:T(8,128)(2,1)S(1)}, bf16[528,512]{1,0:T(8,128)(2,1)S(1)}, u32[]{:S(2)}, u32[]{:S(2)}) collective-permute-start(bf16[528,512]{1,0:T(8,128)(2,1)S(1)} %get-tuple-element.334), channel_id=1, source_target_pairs={{0,3},{1,0},{2,1},{3,2},{4,7},{5,4},{6,5},{7,6},{8,11},{9,8},{10,9... | collective-permute-start | bytes 1622024 | tf_op jit(solution)/shard_map/ppermute | solution.py:1783
  76.4 16.6 %copy-start.23 = (f32[4,8,8,128]{3,2,1,0:T(8,128)S(1)}, f32[4,8,8,128]{3,2,1,0:T(8,128)}, u32[]{:S(2)}) copy-start(f32[4,8,8,128]{3,2,1,0:T(8,128)} %get-tuple-element.123) | copy-start | bytes 393220
  76.4 17.5 %copy-start.36 = (s32[1,2]{1,0:T(1,128)S(1)}, s32[1,2]{1,0:T(1,128)}, u32[]{:S(2)}) copy-start(s32[1,2]{1,0:T(1,128)} %param.20) | copy-start | bytes 28
  76.5 18.4 %copy-start.33 = (s32[1,128]{1,0:T(1,128)S(1)}, s32[1,128]{1,0:T(1,128)}, u32[]{:S(2)}) copy-start(s32[1,128]{1,0:T(1,128)} %param.18) | copy-start | bytes 1540
  76.5 12.5 %copy-start.18 = (bf16[528,512]{1,0:T(8,128)(2,1)}, bf16[528,512]{1,0:T(8,128)(2,1)S(1)}, u32[]{:S(2)}) copy-start(bf16[528,512]{1,0:T(8,128)(2,1)S(1)} %collective-permute-done.refs_1_) | copy-start | bytes 1622020
  77.4 11.6 %copy-start.19 = (bf16[528,512]{1,0:T(8,128)(2,1)}, bf16[528,512]{1,0:T(8,128)(2,1)S(1)}, u32[]{:S(2)}) copy-start(bf16[528,512]{1,0:T(8,128)(2,1)S(1)} %collective-permute-done.1.refs_2_) | copy-start | bytes 1622020
  89.0 0.8 copy-start.20
  93.0 251.9 %all-gather.9.cloned.1.call-start = ((), (), s32[]{:S(2)}) async-start(), calls=%async_computation.3 | async-start | bytes 4718592 | tf_op jit(solution)/shard_map/all_gather | solution.py:1935
  96.5 10.2 %copy-start.26 = (s32[1024]{0:T(1024)}, s32[1024]{0:T(1024)S(1)}, u32[]{:S(2)}) copy-start(s32[1024]{0:T(1024)S(1)} %fusion.32) | copy-start | bytes 12292
  99.7 0.8 copy-start.2
  247.8 37.3 %copy-start.15 = (f32[256,2,128]{2,1,0:T(2,128)S(1)}, f32[256,2,128]{2,1,0:T(2,128)}, u32[]{:S(2)}) copy-start(f32[256,2,128]{2,1,0:T(2,128)} %param.28) | copy-start | bytes 786436
  254.8 30.5 %copy-start.6 = (f32[256,2,512]{2,1,0:T(2,128)S(1)}, f32[256,2,512]{2,1,0:T(2,128)}, u32[]{:S(2)}) copy-start(f32[256,2,512]{2,1,0:T(2,128)} %param.26) | copy-start | bytes 3145732
  254.8 152.2 %all-gather.11.cloned.1.call-start = ((), (), s32[]{:S(2)}) async-start(), calls=%async_computation.4 | async-start | bytes 4718592 | tf_op jit(solution)/shard_map/all_gather | solution.py:1953
  283.8 278.9 %reduce-scatter.3.cloned.1.call-start = ((), (), s32[]{:S(2)}) async-start(), calls=%async_computation.5 | async-start | bytes 4718592 | tf_op jit(solution)/shard_map/reduce_scatter | solution.py:2030
  303.4 39.9 %copy-start.10 = (bf16[512,2048]{1,0:T(8,128)(2,1)S(1)}, bf16[512,2048]{1,0:T(8,128)(2,1)}, u32[]{:S(2)}) copy-start(bf16[512,2048]{1,0:T(8,128)(2,1)} %get-tuple-element.142) | copy-start | bytes 6291460
  383.3 9.7 copy-start.24
  391.0 2.0 copy-start
  391.0 3.1 copy-start.27
  411.1 9.2 copy-start.1
  420.4 39.5 %copy-start.5 = (f32[1024,1024]{1,0:T(8,128)S(1)}, f32[1024,1024]{1,0:T(8,128)}, u32[]{:S(2)}) copy-start(f32[1024,1024]{1,0:T(8,128)} %get-tuple-element.149) | copy-start | bytes 12582916
  492.8 1.0 copy-start.3
  492.9 121.1 %all-gather.13.cloned.1.call-start = ((), (), s32[]{:S(2)}) async-start(), calls=%async_computation.6 | async-start | bytes 4718592 | tf_op jit(solution)/shard_map/all_gather | solution.py:2033
  493.4 304.8 %reduce-scatter.5.cloned.1.call-start = ((), (), s32[]{:S(2)}) async-start(), calls=%async_computation.7 | async-start | bytes 1310720 | tf_op jit(solution)/shard_map/reduce_scatter | solution.py:2089
  495.2 14.9 %copy-start.14 = (f32[32,2048]{1,0:T(8,128)S(1)}, f32[32,2048]{1,0:T(8,128)}, u32[]{:S(2)}) copy-start(f32[32,2048]{1,0:T(8,128)} %get-tuple-element.156) | copy-start | bytes 786436
  620.0 136.5 %copy-start.8 = (bf16[8,256,256]{2,1,0:T(8,128)(2,1)S(1)}, bf16[8,256,256]{2,1,0:T(8,128)(2,1)}, u32[]{:S(2)}) copy-start(bf16[8,256,256]{2,1,0:T(8,128)(2,1)} %get-tuple-element.180) | copy-start | bytes 3145732
  760.0 3.6 copy-start.11
  762.0 4.7 copy-start.13
  762.0 5.1 copy-start.21
  762.1 4.6 copy-start.22
  766.7 3.9 copy-start.28
  766.7 3.9 copy-start.29
  766.7 4.0 copy-start.32
  766.7 4.0 copy-start.31
  798.3 44.2 %copy-start.9 = (bf16[3,176,2048]{2,1,0:T(8,128)(2,1)S(1)}, bf16[3,176,2048]{2,1,0:T(8,128)(2,1)}, u32[]{:S(2)}) copy-start(bf16[3,176,2048]{2,1,0:T(8,128)(2,1)} %get-tuple-element.203) | copy-start | bytes 6488068
  842.8 54.9 %collective-permute-start.3 = (bf16[3,176,512]{2,1,0:T(8,128)(2,1)S(1)}, bf16[3,176,512]{2,1,0:T(8,128)(2,1)S(1)}, u32[]{:S(2)}, u32[]{:S(2)}) collective-permute-start(bf16[3,176,512]{2,1,0:T(8,128)(2,1)S(1)} %get-tuple-element.332), channel_id=1, source_target_pairs={{0,1},{1,2},{2,3},{3,0},{4,5},{5,6},{6,7},{7,4},{8,9},{9,10},{10,1... | collective-permute-start | bytes 1622024 | tf_op jit(solution)/shard_map/ppermute | solution.py:1783
  844.4 53.3 %collective-permute-start.4 = (bf16[3,176,512]{2,1,0:T(8,128)(2,1)S(1)}, bf16[3,176,512]{2,1,0:T(8,128)(2,1)S(1)}, u32[]{:S(2)}, u32[]{:S(2)}) collective-permute-start(bf16[3,176,512]{2,1,0:T(8,128)(2,1)S(1)} %get-tuple-element.331), channel_id=1, source_target_pairs={{0,2},{1,3},{2,0},{3,1},{4,6},{5,7},{6,4},{7,5},{8,10},{9,11},{10,... | collective-permute-start | bytes 1622024 | tf_op jit(solution)/shard_map/ppermute | solution.py:1783
  848.6 49.1 %collective-permute-start.5 = (bf16[3,176,512]{2,1,0:T(8,128)(2,1)S(1)}, bf16[3,176,512]{2,1,0:T(8,128)(2,1)S(1)}, u32[]{:S(2)}, u32[]{:S(2)}) collective-permute-start(bf16[3,176,512]{2,1,0:T(8,128)(2,1)S(1)} %get-tuple-element.330), channel_id=1, source_target_pairs={{0,3},{1,0},{2,1},{3,2},{4,7},{5,4},{6,5},{7,6},{8,11},{9,8},{10,9... | collective-permute-start | bytes 1622024 | tf_op jit(solution)/shard_map/ppermute | solution.py:1783
  897.7 3.4 copy-start.7
  897.7 5.4 copy-start.16
  897.8 5.4 copy-start.17
  899.6 37.3 %collective-permute-start.6 = (bf16[704,512]{1,0:T(8,128)(2,1)S(1)}, bf16[704,512]{1,0:T(8,128)(2,1)}, u32[]{:S(2)}, u32[]{:S(2)}) collective-permute-start(bf16[704,512]{1,0:T(8,128)(2,1)S(1)} %get-tuple-element.327), channel_id=1, source_target_pairs={{0,3},{1,0},{2,1},{3,2},{4,7},{5,4},{6,5},{7,6},{8,11},{9,8},{10,9... | collective-permute-start | bytes 2162696 | tf_op jit(solution)/shard_map/ppermute | solution.py:1783
  899.6 61.0 %collective-permute-start.7 = (bf16[704,512]{1,0:T(8,128)(2,1)S(1)}, bf16[704,512]{1,0:T(8,128)(2,1)}, u32[]{:S(2)}, u32[]{:S(2)}) collective-permute-start(bf16[704,512]{1,0:T(8,128)(2,1)S(1)} %get-tuple-element.326), channel_id=1, source_target_pairs={{0,2},{1,3},{2,0},{3,1},{4,6},{5,7},{6,4},{7,5},{8,10},{9,11},{10,... | collective-permute-start | bytes 2162696 | tf_op jit(solution)/shard_map/ppermute | solution.py:1783
  900.9 62.8 %collective-permute-start.8 = (bf16[704,512]{1,0:T(8,128)(2,1)S(1)}, bf16[704,512]{1,0:T(8,128)(2,1)}, u32[]{:S(2)}, u32[]{:S(2)}) collective-permute-start(bf16[704,512]{1,0:T(8,128)(2,1)S(1)} %get-tuple-element.325), channel_id=1, source_target_pairs={{0,1},{1,2},{2,3},{3,0},{4,5},{5,6},{6,7},{7,4},{8,9},{9,10},{10,1... | collective-permute-start | bytes 2162696 | tf_op jit(solution)/shard_map/ppermute | solution.py:1783
  907.4 22.1 %copy-start.30 = (f32[3,64]{1,0:T(4,128)S(1)}, f32[3,64]{1,0:T(4,128)}, u32[]{:S(2)}) copy-start(f32[3,64]{1,0:T(4,128)} %param.31) | copy-start | bytes 2308
  907.4 22.1 %copy-start.34 = (f32[3,64]{1,0:T(4,128)S(1)}, f32[3,64]{1,0:T(4,128)}, u32[]{:S(2)}) copy-start(f32[3,64]{1,0:T(4,128)} %param.32) | copy-start | bytes 2308
  907.4 22.1 %copy-start.35 = (f32[3,64]{1,0:T(4,128)S(1)}, f32[3,64]{1,0:T(4,128)}, u32[]{:S(2)}) copy-start(f32[3,64]{1,0:T(4,128)} %param.33) | copy-start | bytes 2308
  936.9 29.1 %copy-start.4 = (f32[256,2,512]{2,1,0:T(2,128)S(1)}, f32[256,2,512]{2,1,0:T(2,128)}, u32[]{:S(2)}) copy-start(f32[256,2,512]{2,1,0:T(2,128)} %param.25) | copy-start | bytes 3145732
  965.8 2.7 copy-start.12
Sparse Core Ops, SparseCore 0:
  35.4 56.3 all-gather.6
  94.3 92.0 all-gather.14
  254.9 42.5 all-gather.8
  299.2 51.7 all-gather.10
  493.0 69.6 reduce-scatter.2
  564.5 40.7 all-gather.12
  762.2 24.3 reduce-scatter.4

commit v13 on v12

--- a/solution.py
+++ b/solution.py
@@ -204,11 +204,12 @@
     )
 
 
-def trade(axis, values, source_of, target_of, shape, patience=2):
+def trade(axis, values, source_of, target_of, shape, patience=2, rest=None, rest_at=None):
     count = lax.axis_size(axis)
+    inputs = [values] if rest is None else [values, rest]
 
     def steps(ins, outs, scratch):
-        (x_ref,), (out_ref,), (send, receive, local) = ins, outs, scratch
+        (x_ref, *rest_ref), (out_ref,), (send, receive, local) = ins, outs, scratch
         me = lax.axis_index(axis)
         copies = []
         for step in range(1, count):
@@ -222,8 +223,11 @@
             )
             copy.start()
             copies.append(copy)
-        keep = pltpu.make_async_copy(source_of(x_ref, me), target_of(out_ref, me), local)
-        keep.start()
+        keeps = [pltpu.make_async_copy(source_of(x_ref, me), target_of(out_ref, me), local.at[0])]
+        if rest is not None:
+            keeps.append(pltpu.make_async_copy(rest_ref[0], rest_at(out_ref), local.at[1]))
+        for keep in keeps:
+            keep.start()
         for turn in range(patience):
             yield
         for step in range(1, count):
@@ -233,12 +237,13 @@
             )
         for copy in copies:
             copy.wait_send()
-        keep.wait()
+        for keep in keeps:
+            keep.wait()
 
     return Task(
-        [values],
+        inputs,
         [struct(shape, values.dtype)],
-        [sems(count - 1), sems(count), sems()],
+        [sems(count - 1), sems(count), sems(2)],
         steps,
         ANY,
         ANY,
@@ -272,7 +277,7 @@
     return trade("narrow", values, turned, block_at, shape, patience)
 
 
-def product(lefts, rights, dim, order):
+def product(lefts, rights, dim, order, pause=True, last=None):
     count, rows = len(order), lefts[0].shape[-1 if dim == 0 else -2]
     columns = rights[0].shape[1]
     block = min(512, columns)
@@ -285,13 +290,12 @@
         def left_of(member):
             return left_refs[0][member] if lefts[0].ndim == 3 else left_refs[member][...]
 
-        for at, members in enumerate(order):
-
+        def fill(at, members, shift):
             def strip(part, carry):
                 spot = pl.ds(pl.multiple_of(part * block, block), block)
                 value = jnp.zeros((rows, block), FULL)
                 for left, right in members:
-                    value = value + dot(left_of(left), right_refs[right][:, spot], dim, 0)
+                    value = value + dot(left_of(left), right_refs[right + shift][:, spot], dim, 0)
                 result_ref[at, :, spot] = value.astype(LOW)
                 square_ref[:, spot] = square_ref[:, spot] + jnp.sum(
                     value * value, axis=0, keepdims=True
@@ -299,7 +303,15 @@
                 return carry
 
             lax.fori_loop(0, columns // block, strip, 0)
-            yield
+
+        for at, members in enumerate(order):
+            if last is None:
+                fill(at, members, 0)
+            else:
+                pl.when(last())(functools.partial(fill, at, members, 1))
+                pl.when(jnp.logical_not(last()))(functools.partial(fill, at, members, 0))
+            if pause:
+                yield
 
     return Task(
         list(lefts) + list(rights),
@@ -483,6 +495,31 @@
 def join_columns(axis, values):
     count, rows, size = values.shape
     return trade(axis, values, block_at, columns_of(size), (rows, count * size))
+
+
+def join_below(axis, values, rest):
+    count, rows, size = values.shape
+    above = rest.shape[0]
+
+    def target_of(ref, spot):
+        return ref.at[above:, pl.ds(pl.multiple_of(spot * size, size), size)]
+
+    shape = (above + rows, count * size)
+    return trade(
+        axis, values, block_at, target_of, shape, 2, rest, lambda ref: ref.at[:above]
+    )
+
+
+def swap_below(values, rest):
+    count, above, size = rest.shape
+    shape = (count, above + values.shape[1], size)
+
+    def target_of(ref, spot):
+        return ref.at[spot, above:]
+
+    return trade(
+        "narrow", values, turned, target_of, shape, 2, rest, lambda ref: ref.at[:, :above]
+    )
 
 
 def collect(count, parts_ref, slots, send, receive):
@@ -1449,7 +1486,7 @@
 
 def newton_steps(problems):
     rows, width = problems[0][0].shape
-    block = min(512, width)
+    block = min(1024, width)
     eye = lax.broadcasted_iota(jnp.int32, (rows, rows), 0) == lax.broadcasted_iota(
         jnp.int32, (rows, rows), 1
     )
@@ -1909,12 +1946,12 @@
     by_head, normed_tok = make_heads(
         rows_low, gain_w[0:1], proj, tok_part(cosine_all), tok_part(sine_all), groups, repeat
     )
-    own_head, start_low, tok_cols, table_low = launch(
+    own_head, start_low, tok_cols, table_top = launch(
         [
             swap_blocks("narrow", by_head),
             gather_blocks("narrow", rows_low[tok_rows:]),
             split_columns("wide", normed_tok),
-            join_columns("wide", embed_cut[:, table_half:]),
+            join_columns("wide", embed_cut[:, :table_half]),
         ],
         2,
         "trade_heads",
@@ -1952,15 +1989,14 @@
     inner = inner.reshape(sel, width)
     inner_all = lax.all_gather(inner, "wide", axis=0, tiled=True)
     gate, up, hidden, fed = feed(inner, ffn_w)
-    final_own, late_part, table_top = launch(
+    final_own, late_part, table_own = launch(
         [
             settle(fed, middle, start_own, keep_row, gain_w[2:3]),
-            join_columns("wide", embed_cut[:, :table_half]),
+            join_below("wide", embed_cut[:, table_half:], table_top),
         ],
         4,
         "settle_late",
     )
-    table_own = jnp.concatenate([table_top, table_low])
 
     table_count = table_own.shape[0]
     local_target = targets_all - (narrow_spot * vocab_rows + wide_spot * table_count)
@@ -2006,14 +2042,19 @@
 
     late_grad = exit_back(late_logits, log_norms[total_rows:], EXIT_LAST)
     late_back = dot(late_grad, table_own, 0, 0).astype(LOW)
-    grad_late, mom_low = launch(
-        [sum_wide(late_back), swap_turned(mom_parts[:, half:])], 7, "sum_late"
-    )
-    early_norms, grad_late = lax.optimization_barrier((log_norms[:total_rows], grad_late))
-    early_grad = exit_back(early_logits, early_norms, EXIT_EARLY)
-    mom_owned = jnp.concatenate([mom_top, mom_low], axis=1)
-
-    grad_final, gain_late, grad_out, early_back, _ = launch(
+    early_grad = exit_back(early_logits, log_norms[:total_rows], EXIT_EARLY)
+    grad_late, mom_owned, early_back, _ = launch(
+        [
+            sum_wide(late_back),
+            swap_below(mom_parts[:, half:], mom_top),
+            later(product([early_grad], [table_own], 0, [[(0, 0)]]), 1),
+        ],
+        7,
+        "sum_late",
+    )
+    early_back, grad_late = lax.optimization_barrier((early_back, grad_late))
+    grad_early = lax.psum_scatter(early_back[0], "wide", scatter_dimension=0, tiled=True)
+    grad_final, gain_late, grad_out = launch(
         [
             settle_back(
                 grad_late.astype(LOW),
@@ -2022,12 +2063,10 @@
                 keep_row,
                 gain_w[2:3],
             ),
-            product([early_grad], [table_own], 0, [[(0, 0)]]),
         ],
         8,
         "back_late",
     )
-    grad_early = lax.psum_scatter(early_back[0], "wide", scatter_dimension=0, tiled=True)
     grad_layer = grad_final * keep_layer
     grad_out = grad_out.reshape(sel, width)
     out_all = lax.all_gather(grad_out, "wide", axis=0, tiled=True)
@@ -2100,14 +2139,26 @@
     sums = jnp.stack(
         [gain_attn[0], gain_mid[0], gain_early[0] + gain_late[0], jnp.full((width,), squares)]
     )
-    matrix = jnp.minimum(lax.rem(narrow_spot + narrow_count - turn, narrow_count), 2)
-    right = jnp.where(matrix == 2, out_all, inner_all)
+    def owns_last():
+        away = lax.axis_index("narrow") + narrow_count - lax.rem(lax.axis_index("wide"), 2)
+        return lax.rem(away, narrow_count) >= 2
+
     sums, kv_owned, qo_owned, owned, _ = launch(
         [
             combine(sums.reshape(4, 8, -1), add_two),
             send_owner(summed_kv.astype(LOW).reshape(2 * block_rows, kv_size)),
             later(send_owner(summed_qo.astype(LOW).reshape(2 * columns, q_size)), 1),
-            later(product([acts_owned], [right], 0, [[(at, 0)] for at in range(narrow_count)]), 2),
+            later(
+                product(
+                    [acts_owned],
+                    [inner_all, out_all],
+                    0,
+                    [[(at, 0)] for at in range(narrow_count)],
+                    False,
+                    owns_last,
+                ),
+                1,
+            ),
         ],
         12,
         "combine_sums",

time: 996 us -> 1030 us (1.034)
  Pallas kernels: 739 us -> 796 us
    pallas_call x13, Pallas kernels: 585 us -> 647 us  [launch(): pl.pallas_call(body, out_shape=outputs, in_specs=[place for task in tasks...]
    reduce_scatter x1, waiting for transfers between devices: 10.3 us -> 0.01 us  [per_device(): lax.psum_scatter(early_back[0], 'wide', scatter_dimension=0, tiled=True)]
  transfers between devices with their start and end apart: 16 -> 16, of which waited for: 5 -> 5; matrix products, arithmetic and copies ran while one was open for 10% -> 9% of each run, Pallas kernels for 48% -> 52%
where the time goes in v13:
time: 1030 us; the launch traced here: 1020 us
  Pallas kernels  796 us (77%)
  other arithmetic  86 us (8%)
  waiting for transfers between devices  40.3 us (4%)
  local copies, waits for them, and re-layouts  35.4 us (3%)
  between operations  23.2 us (2%)
  matrix products  19.4 us (2%)
  starting transfers between devices  16 us (2%)
    pallas_call x13, Pallas kernels, launch(): pl.pallas_call(body, out_shape=outputs, in_specs=[place for task in tasks...  647 us
    pallas_call x1, Pallas kernels, newton(): pl.pallas_call(functools.partial(newton_any_body, rows), in_specs=[pl.Blo...  42.7 us
    ppermute x9, waiting for transfers between devices, shifted(): return lax.ppermute(parts, axis, pairs)  40.1 us
    pallas_call x5, Pallas kernels, local_call(): pl.pallas_call(body, grid=(1,), in_specs=specs, out_specs=[pl.BlockSpec(a...  29 us
    pallas_call x1, Pallas kernels, lookup(): pl.pallas_call(lookup_body, in_specs=[pl.BlockSpec(memory_space=pltpu.SME...  28.4 us
    sub x2, other arithmetic, adamw(): weight * (1.0 - rate * decay) - rate * update  22.8 us
  transfers between devices with their start and end apart: 16, of which 5 were waited for; matrix products, arithmetic and copies ran while one was open for 9% of the time, Pallas kernels for 52%

profile of v13, /device:TPU:17, one launch (start us, length us, event | category | flops | bytes accessed | tf_op | source)
XLA Modules:
  0.0 1016.1 jit_solution(15957689223712627300)
XLA Ops:
  12.5 1.6 convert_element_type.131
  14.2 18.9 %gather_ids.1 = (s32[8,16,128]{2,1,0:T(8,128)}, f32[4,8,8,128]{3,2,1,0:T(8,128)}, bf16[4,256,256]{2,1,0:T(8,128)(2,1)}) custom-call(s32[16,128]{1,0:T(8,128)} %pad_bitcast_fusion.refs_0_, f32[8,128]{1,0:T(8,128)} %bitcast_convert_fusion.refs_1_, bf16[256,256]{1,0:T(8,128)(2,1)} %bitcast.271), custom_call_target="tpu_custom_call" | custom-call | bytes 108032 | tf_op jit(solution)/shard_map/gather_ids/pallas_call | solution.py:139
  35.4 2.5 convert_element_type.122
  39.2 1.9 collective-permute-start
  41.1 1.3 collective-permute-start.1
  42.3 1.4 collective-permute-start.2
  47.5 28.4 %lookup.1 = (bf16[9216,256]{1,0:T(8,128)(2,1)}, bf16[8192,256]{1,0:T(8,128)(2,1)}, s32[9248]{0:T(1024)}) custom-call(s32[9216]{0:T(1024)} %and_select_fusion.ids_ref, s32[9344]{0:T(1024)} %concatenate.38.turn_ref, f32[8192,256]{1,0:T(8,128)} %table_ref.1), custom_call_target="tpu_custom_call" | custom-call | bytes 8388608 | tf_op jit(solution)/shard_map/lookup/pallas_call | solution.py:1708
  76.0 1.5 collective-permute-done.1.refs_2_
  77.5 11.6 %collective-permute-done.2.refs_3_ = bf16[528,512]{1,0:T(8,128)(2,1)S(1)} collective-permute-done((bf16[528,512]{1,0:T(8,128)(2,1)S(1)}, bf16[528,512]{1,0:T(8,128)(2,1)S(1)}, u32[]{:S(2)}, u32[]{:S(2)}) %collective-permute-start.2) | collective-permute-done | bytes 540704 | tf_op jit(solution)/shard_map/ppermute | solution.py:1820
  89.8 3.1 assemble.1
  97.8 1.9 multiply_sine_fusion
  101.3 5.4 fusion.42
  106.7 96.3 %fetch_rows.1.rows_ref = bf16[288,2048]{1,0:T(8,128)(2,1)} custom-call(bf16[4,2304,256]{2,1,0:T(8,128)(2,1)} %bitcast.235), custom_call_target="tpu_custom_call" | custom-call | bytes 737280 | tf_op jit(solution)/shard_map/fetch_rows/pallas_call | solution.py:139
  203.0 1.7 slice_convert_fusion
  204.7 5.0 make_heads.1
  209.7 37.8 %trade_heads.1 = (bf16[4,1,2,256,128]{4,3,2,1,0:T(8,128)(2,1)}, bf16[4,32,2048]{2,1,0:T(8,128)(2,1)}, bf16[8,256,256]{2,1,0:T(8,128)(2,1)}, bf16[512,2048]{1,0:T(8,128)(2,1)}) custom-call(bf16[4,1,2,256,128]{4,3,2,1,0:T(8,128)(2,1)} %get-tuple-element.125.refs_0_, bf16[32,2048]{1,0:T(8,128)(2,1)} %get-tuple-element.339.refs_1_, ...), custom_call_target="tpu_custom_call" | custom-call | bytes 999424 | tf_op jit(solution)/shard_map/trade_heads/pallas_call | solution.py:139
  247.6 6.9 attend.1
  255.9 27.6 %settle_middle.1 = (f32[32,2048]{1,0:T(8,128)}, bf16[4,32,2048]{2,1,0:T(8,128)(2,1)}, bf16[8,128,512]{2,1,0:T(8,128)(2,1)}, bf16[8,128,256]{2,1,0:T(8,128)(2,1)}) custom-call(bf16[4,32,2048]{2,1,0:T(8,128)(2,1)} %bitcast.269, f32[32,2048]{1,0:T(8,128)} %get-tuple-element.338.refs_1_.refs_2_, f32[32,2048]{1,0:T(8,128)} %get-tuple-element.338.refs_1_.refs_2_, ...), custom_call_target="tpu_custom_call" | custom-call | bytes 509952 | tf_op jit(solution)/shard_map/settle_middle/pallas_call | solution.py:139
  285.5 2.5 convert_bitcast_fusion
  288.0 1.9 pad_maximum_fusion
  289.9 13.4 %feed.1 = (f32[8,128,176]{2,1,0:T(8,128)}, f32[8,128,176]{2,1,0:T(8,128)}, bf16[8,128,176]{2,1,0:T(8,128)(2,1)}, bf16[128,2048]{1,0:T(8,128)(2,1)}) custom-call(bf16[128,2048]{1,0:T(8,128)(2,1)} %bitcast.247, bf16[8,3,176,2048]{3,2,1,0:T(8,128)(2,1)} %bitcast.227), custom_call_target="tpu_custom_call" | custom-call | flops 2214592512 | bytes 17301504 | tf_op jit(solution)/shard_map/feed/pallas_call | solution.py:1417
  303.9 78.9 %settle_late.1 = (f32[32,2048]{1,0:T(8,128)}, bf16[4,32,2048]{2,1,0:T(8,128)(2,1)}, bf16[1024,2048]{1,0:T(8,128)(2,1)}) custom-call(bf16[4,32,2048]{2,1,0:T(8,128)(2,1)} %bitcast.266, f32[32,2048]{1,0:T(8,128)} %get-tuple-element.138.refs_1_, f32[32,2048]{1,0:T(8,128)} %get-tuple-element.338.refs_1_.refs_2_, f32[1,2048]{1,0:T(1,128)} %broadcast_in_dim.137.refs_3_, ...), custom_call_target="tpu_custom_call" | custom-call | bytes 1280000 | tf_op jit(solution)/shard_map/settle_late/pallas_call | solution.py:139
  382.8 38.5 %gather_late.1 = (bf16[8,128,2048]{2,1,0:T(8,128)(2,1)}, bf16[4,352,512]{2,1,0:T(8,128)(2,1)}, f32[1024,1024]{1,0:T(8,128)}, f32[3,1024]{1,0:T(4,128)}) custom-call(bf16[128,2048]{1,0:T(8,128)(2,1)} %bitcast.264, bf16[4,352,512]{2,1,0:T(8,128)(2,1)} %get-tuple-element.329.refs_1_, bf16[1024,2048]{1,0:T(8,128)(2,1)} %all-gather.9.cloned.1.call-done.refs_2_.refs_7_, ...), custom_call_target="tpu_custom_call" | custom-call | bytes 2525184 | tf_op jit(solution)/shard_map/gather_late/pallas_call | solution.py:139
  421.4 6.4 fusion.45
  427.8 2.0 copy-done.2
  431.5 13.7 %combine_stats.1 = f32[3,8,256]{2,1,0:T(8,128)} custom-call(f32[3,8,256]{2,1,0:T(8,128)} %bitcast.281), custom_call_target="tpu_custom_call" | custom-call | bytes 6144 | tf_op jit(solution)/shard_map/combine_stats/pallas_call | solution.py:139
  446.0 6.8 fusion.4
  452.9 6.1 convolution_convert_fusion
  459.0 64.8 %sum_late.1 = (f32[128,2048]{1,0:T(8,128)}, bf16[4,704,512]{2,1,0:T(8,128)(2,1)}, bf16[1,1024,2048]{2,1,0:T(8,128)(2,1)}, f32[1,2048]{1,0:T(1,128)}) custom-call(bf16[8,128,2048]{2,1,0:T(8,128)(2,1)} %bitcast.238, bf16[4,352,512]{2,1,0:T(8,128)(2,1)} %get-tuple-element.328.refs_1_, bf16[4,352,512]{2,1,0:T(8,128)(2,1)} %get-tuple-element.146.refs_2_, ...), custom_call_target="tpu_custom_call" | custom-call | bytes 2688000 | tf_op jit(solution)/shard_map/sum_late/pallas_call | solution.py:139
  526.6 26.0 %back_late.1 = (f32[32,2048]{1,0:T(8,128)}, f32[1,2048]{1,0:T(1,128)}, bf16[4,32,2048]{2,1,0:T(8,128)(2,1)}) custom-call(bf16[4,32,2048]{2,1,0:T(8,128)(2,1)} %bitcast.250, f32[32,2048]{1,0:T(8,128)} %get-tuple-element.151.refs_1_, f32[32,2048]{1,0:T(8,128)} %broadcast_in_dim.140.refs_2_, f32[1,2048]{1,0:T(1,128)} %broadcast_in_dim.137.refs_3_, ...), custom_call_target="tpu_custom_call" | custom-call | bytes 232448 | tf_op jit(solution)/shard_map/back_late/pallas_call | solution.py:139
  552.6 1.3 pad_maximum_fusion.3
  554.0 14.6 %feed_back.1 = (bf16[8,3,128,176]{3,2,1,0:T(8,128)(2,1)}, bf16[128,2048]{1,0:T(8,128)(2,1)}) custom-call(bf16[128,2048]{1,0:T(8,128)(2,1)} %bitcast.249, bf16[8,3,176,2048]{3,2,1,0:T(8,128)(2,1)} %bitcast.228, f32[8,128,176]{2,1,0:T(8,128)} %get-tuple-element.153.gate_ref, f32[8,128,176]{2,1,0:T(8,128)} %get-tuple-element.154.up_ref, ...), custom_call_target="tpu_custom_call" | custom-call | flops 2214592512 | bytes 17301504 | tf_op jit(solution)/shard_map/feed_back/pallas_call | solution.py:1469
  569.3 30.2 %back_middle.1 = (f32[32,2048]{1,0:T(8,128)}, f32[1,2048]{1,0:T(1,128)}, bf16[4,32,2048]{2,1,0:T(8,128)(2,1)}, bf16[8,3,128,176]{3,2,1,0:T(8,128)(2,1)}) custom-call(bf16[4,32,2048]{2,1,0:T(8,128)(2,1)} %bitcast.265, f32[32,2048]{1,0:T(8,128)} %get-tuple-element.138.refs_1_, f32[32,2048]{1,0:T(8,128)} %broadcast_multiply_fusion.refs_2_, ...), custom_call_target="tpu_custom_call" | custom-call | bytes 502784 | tf_op jit(solution)/shard_map/back_middle/pallas_call | solution.py:139
  599.5 2.7 copy.171
  602.2 1.7 multiply_add_fusion.1.base_ref
  603.8 8.0 attend_back.1
  611.9 44.3 %trade_grads.1 = (bf16[4,1,2,256,128]{4,3,2,1,0:T(8,128)(2,1)}, f32[32,2048]{1,0:T(8,128)}, f32[32,2048]{1,0:T(8,128)}, bf16[8,128,512]{2,1,0:T(8,128)(2,1)}, bf...) custom-call(bf16[4,1,2,256,128]{4,3,2,1,0:T(8,128)(2,1)} %get-tuple-element.164.refs_0_, ...), custom_call_target="tpu_custom_call" | custom-call | bytes 2704384 | tf_op jit(solution)/shard_map/trade_grads/pallas_call | solution.py:139
  656.2 5.9 rows_back.1
  662.2 136.8 %return_rows.1 = (bf16[4,2304,256]{2,1,0:T(8,128)(2,1)}, bf16[4,1024,176]{2,1,0:T(8,128)(2,1)}, bf16[8,256,1024]{2,1,0:T(8,128)(2,1)}, bf16[8,1024,256]{2,1,0:T(...) custom-call(bf16[288,2048]{1,0:T(8,128)(2,1)} %get-tuple-element.182.refs_0_, ...), custom_call_target="tpu_custom_call" | custom-call | bytes 4146176 | tf_op jit(solution)/shard_map/return_rows/pallas_call | solution.py:139
  799.0 3.5 convolution_bitcast_fusion
  803.4 1.2 copy.217
  805.3 1.5 convolution_bitcast_fusion.1
  806.8 1.8 convolution_bitcast_fusion.2
  811.1 20.5 %spread.1 = (f32[8192,256]{1,0:T(8,128)}, f32[8,256]{1,0:T(8,128)}) custom-call(s32[9216]{0:T(1024)} %and_select_fusion.ids_ref, s32[9248]{0:T(1024)} %get-tuple-element.190.list_ref, bf16[9216,256]{1,0:T(8,128)(2,1)} %bitcast.234, bf16[8192,256]{1,0:T(8,128)(2,1)} %bitcast.239), custom_call_target="tpu_custom_call" | custom-call | flops 2359296 | bytes 16777216 | tf_op jit(solution)/shard_map/spread/pallas_call | solution.py:1782
  831.6 1.3 reduce_sum.168
  832.9 2.3 fusion.43
  838.5 33.4 %combine_sums.1 = (f32[4,8,256]{2,1,0:T(8,128)}, bf16[4,512,128]{2,1,0:T(8,128)(2,1)}, bf16[4,512,512]{2,1,0:T(8,128)(2,1)}, bf16[4,176,2048]{2,1,0:T(8,128)(2,1)}, f32[1,2048]{1,0:T(1,128)}) custom-call(f32[4,8,256]{2,1,0:T(8,128)} %maximum_maximum_fusion.1.refs_0_, bf16[512,128]{1,0:T(8,128)(2,1)} %bitcast.260, bf16[512,512]{1,0:T(8,128)(2,1)} %bitcast.245, ...), custom_call_target="tpu_custom_call" | custom-call | bytes 2008064 | tf_op jit(solution)/shard_map/combine_sums/pallas_call | solution.py:139
  872.0 1.3 slice_bitcast_fusion
  877.6 1.6 collective-permute-start.3
  879.3 3.9 collective-permute-start.4
  883.2 2.3 collective-permute-start.5
  885.5 42.7 %newton.1 = bf16[4,704,512]{2,1,0:T(8,128)(2,1)} custom-call(f32[1]{0:T(128)} %bitcast.72.factor_ref, bf16[4,704,512]{2,1,0:T(8,128)(2,1)} %get-tuple-element.199.mom_ref, bf16[4,176,2048]{2,1,0:T(8,128)(2,1)} %get-tuple-element.200.grad_ref, bf16[4,512,512]{2,1,0:T(8,128)(2,1)} %get-tuple-element.201.qo_ref, bf16[4,512,128]{2,1,0:T(8,128)(2,1)} %get-tuple-element.202.kv_ref), custom_call_target="tpu_custom_call" | custom-call | flops 23789568000 | bytes 8650752 | tf_op jit(solution)/shard_map/newton/pallas_call | solution.py:1648
  928.3 1.5 collective-permute-done.5
  929.8 2.6 dynamic-slice_bitcast_fusion
  932.4 2.2 collective-permute-start.6
  934.6 1.2 collective-permute-start.8
  936.1 1.8 copy.182
  939.4 2.7 convert_multiply_fusion
  942.1 22.1 %multiply_subtract_fusion = (f32[8192,256]{1,0:T(8,128)}, f32[8192,256]{1,0:T(8,128)}, f32[8192,256]{1,0:T(8,128)}) fusion(f32[8192,256]{1,0:T(8,128)} %table_ref.1, f32[8192,256]{1,0:T(8,128)} %get-tuple-element.196, f32[]{:T(128)} %div.51, f32[8192,256]{1,0:T(8,128)} %param.23, f32[8192,256]{1,0:T(8,128)} %param.24), kind=kLoop, calls=%fused_computation.2 | loop fusion | flops 31457280 | bytes 58720260 | tf_op jit(solution)/shard_map/sub | solution.py:1809
  964.9 6.7 bitcast_add_fusion
  971.6 24.7 %collective-permute-done.7 = bf16[704,512]{1,0:T(8,128)(2,1)} collective-permute-done((bf16[704,512]{1,0:T(8,128)(2,1)S(1)}, bf16[704,512]{1,0:T(8,128)(2,1)}, u32[]{:S(2)}, u32[]{:S(2)}) %collective-permute-start.7) | collective-permute-done | bytes 720928 | tf_op jit(solution)/shard_map/ppermute | solution.py:1820
  997.0 2.1 fusion.18
  999.4 2.2 bitcast_subtract_fusion.1
  1002.8 5.1 bitcast_subtract_fusion
  (200 shorter events, 39.4 us)
Async XLA Ops:
  7.2 197.5 %all-gather.7.cloned.1.call-start = ((), (), s32[]{:S(2)}) async-start(), calls=%async_computation.2 | async-start | bytes 9437184 | tf_op jit(solution)/shard_map/all_gather | solution.py:1891
  35.3 212.3 %all-gather.15.cloned.1.call-start = ((), (), s32[]{:S(2)}) async-start(), calls=%async_computation.8 | async-start | bytes 19464192 | tf_op jit(solution)/shard_map/all_gather | solution.py:1919
  37.9 5.8 copy-start.21
  39.2 36.7 %collective-permute-start = (bf16[528,512]{1,0:T(8,128)(2,1)}, bf16[528,512]{1,0:T(8,128)(2,1)S(1)}, u32[]{:S(2)}, u32[]{:S(2)}) collective-permute-start(bf16[528,512]{1,0:T(8,128)(2,1)} %get-tuple-element.336), channel_id=1, source_target_pairs={{0,1},{1,2},{2,3},{3,0},{4,5},{5,6},{6,7},{7,4},{8,9},{9,10},{10,1... | collective-permute-start | bytes 1622024 | tf_op jit(solution)/shard_map/ppermute | solution.py:1820
  41.1 36.4 %collective-permute-start.1 = (bf16[528,512]{1,0:T(8,128)(2,1)S(1)}, bf16[528,512]{1,0:T(8,128)(2,1)S(1)}, u32[]{:S(2)}, u32[]{:S(2)}) collective-permute-start(bf16[528,512]{1,0:T(8,128)(2,1)S(1)} %get-tuple-element.335), channel_id=1, source_target_pairs={{0,2},{1,3},{2,0},{3,1},{4,6},{5,7},{6,4},{7,5},{8,10},{9,11},{10,... | collective-permute-start | bytes 1622024 | tf_op jit(solution)/shard_map/ppermute | solution.py:1820
  42.3 46.7 %collective-permute-start.2 = (bf16[528,512]{1,0:T(8,128)(2,1)S(1)}, bf16[528,512]{1,0:T(8,128)(2,1)S(1)}, u32[]{:S(2)}, u32[]{:S(2)}) collective-permute-start(bf16[528,512]{1,0:T(8,128)(2,1)S(1)} %get-tuple-element.334), channel_id=1, source_target_pairs={{0,3},{1,0},{2,1},{3,2},{4,7},{5,4},{6,5},{7,6},{8,11},{9,8},{10,9... | collective-permute-start | bytes 1622024 | tf_op jit(solution)/shard_map/ppermute | solution.py:1820
  75.9 17.2 %copy-start.20 = (f32[4,8,8,128]{3,2,1,0:T(8,128)S(1)}, f32[4,8,8,128]{3,2,1,0:T(8,128)}, u32[]{:S(2)}) copy-start(f32[4,8,8,128]{3,2,1,0:T(8,128)} %get-tuple-element.123) | copy-start | bytes 393220
  75.9 18.1 %copy-start.34 = (s32[1,2]{1,0:T(1,128)S(1)}, s32[1,2]{1,0:T(1,128)}, u32[]{:S(2)}) copy-start(s32[1,2]{1,0:T(1,128)} %param.20) | copy-start | bytes 28
  75.9 18.9 %copy-start.31 = (s32[1,128]{1,0:T(1,128)S(1)}, s32[1,128]{1,0:T(1,128)}, u32[]{:S(2)}) copy-start(s32[1,128]{1,0:T(1,128)} %param.18) | copy-start | bytes 1540
  75.9 13.1 %copy-start.17 = (bf16[528,512]{1,0:T(8,128)(2,1)}, bf16[528,512]{1,0:T(8,128)(2,1)S(1)}, u32[]{:S(2)}) copy-start(bf16[528,512]{1,0:T(8,128)(2,1)S(1)} %collective-permute-done.refs_1_) | copy-start | bytes 1622020
  77.5 11.6 %copy-start.18 = (bf16[528,512]{1,0:T(8,128)(2,1)}, bf16[528,512]{1,0:T(8,128)(2,1)S(1)}, u32[]{:S(2)}) copy-start(bf16[528,512]{1,0:T(8,128)(2,1)S(1)} %collective-permute-done.1.refs_2_) | copy-start | bytes 1622020
  89.0 0.8 copy-start.19
  93.0 289.8 %all-gather.9.cloned.1.call-start = ((), (), s32[]{:S(2)}) async-start(), calls=%async_computation.3 | async-start | bytes 4718592 | tf_op jit(solution)/shard_map/all_gather | solution.py:1972
  96.5 10.2 %copy-start.23 = (s32[1024]{0:T(1024)}, s32[1024]{0:T(1024)S(1)}, u32[]{:S(2)}) copy-start(s32[1024]{0:T(1024)S(1)} %fusion.32) | copy-start | bytes 12292
  99.7 0.8 copy-start.4
  247.6 37.3 %copy-start.15 = (f32[256,2,128]{2,1,0:T(2,128)S(1)}, f32[256,2,128]{2,1,0:T(2,128)}, u32[]{:S(2)}) copy-start(f32[256,2,128]{2,1,0:T(2,128)} %param.28) | copy-start | bytes 786436
  254.5 30.4 %copy-start.7 = (f32[256,2,512]{2,1,0:T(2,128)S(1)}, f32[256,2,512]{2,1,0:T(2,128)}, u32[]{:S(2)}) copy-start(f32[256,2,512]{2,1,0:T(2,128)} %param.26) | copy-start | bytes 3145732
  254.5 190.7 %all-gather.11.cloned.1.call-start = ((), (), s32[]{:S(2)}) async-start(), calls=%async_computation.4 | async-start | bytes 4718592 | tf_op jit(solution)/shard_map/all_gather | solution.py:1990
  283.5 320.3 %reduce-scatter.3.cloned.1.call-start = ((), (), s32[]{:S(2)}) async-start(), calls=%async_computation.5 | async-start | bytes 4718592 | tf_op jit(solution)/shard_map/reduce_scatter | solution.py:2056
  382.8 38.5 %copy-start = (bf16[1024,2048]{1,0:T(8,128)(2,1)S(1)}, bf16[1024,2048]{1,0:T(8,128)(2,1)}, u32[]{:S(2)}) copy-start(bf16[1024,2048]{1,0:T(8,128)(2,1)} %get-tuple-element.142.refs_3_.refs_4_) | copy-start | bytes 12582916
  421.3 8.4 copy-start.22
  427.7 2.0 copy-start.2
  427.8 3.1 copy-start.24
  446.0 6.8 copy-start.1
  452.9 6.1 copy-start.3
  523.8 1.2 copy-start.12
  523.8 28.9 %copy-start.5 = (f32[1024,64]{1,0:T(8,128)S(1)}, f32[1024,64]{1,0:T(8,128)}, u32[]{:S(2)}) copy-start(f32[1024,64]{1,0:T(8,128)} %copy-done.4) | copy-start | bytes 786436
  523.8 132.4 %all-gather.13.cloned.1.call-start = ((), (), s32[]{:S(2)}) async-start(), calls=%async_computation.6 | async-start | bytes 4718592 | tf_op jit(solution)/shard_map/all_gather | solution.py:2072
  552.6 280.3 %reduce-scatter.5.cloned.1.call-start = ((), (), s32[]{:S(2)}) async-start(), calls=%async_computation.7 | async-start | bytes 1310720 | tf_op jit(solution)/shard_map/reduce_scatter | solution.py:2128
  554.0 14.6 %copy-start.14 = (f32[32,2048]{1,0:T(8,128)S(1)}, f32[32,2048]{1,0:T(8,128)}, u32[]{:S(2)}) copy-start(f32[32,2048]{1,0:T(8,128)} %get-tuple-element.157) | copy-start | bytes 786436
  662.2 136.8 %copy-start.9 = (bf16[8,256,256]{2,1,0:T(8,128)(2,1)S(1)}, bf16[8,256,256]{2,1,0:T(8,128)(2,1)}, u32[]{:S(2)}) copy-start(bf16[8,256,256]{2,1,0:T(8,128)(2,1)} %get-tuple-element.181) | copy-start | bytes 3145732
  802.5 2.2 copy-start.29
  802.5 2.8 copy-start.13
  804.6 5.8 copy-start.25
  804.6 5.8 copy-start.26
  804.6 5.9 copy-start.30
  804.6 5.9 copy-start.28
  838.5 38.8 %copy-start.10 = (bf16[3,176,2048]{2,1,0:T(8,128)(2,1)S(1)}, bf16[3,176,2048]{2,1,0:T(8,128)(2,1)}, u32[]{:S(2)}) copy-start(bf16[3,176,2048]{2,1,0:T(8,128)(2,1)} %get-tuple-element.203) | copy-start | bytes 6488068
  877.6 50.6 %collective-permute-start.3 = (bf16[3,176,512]{2,1,0:T(8,128)(2,1)S(1)}, bf16[3,176,512]{2,1,0:T(8,128)(2,1)S(1)}, u32[]{:S(2)}, u32[]{:S(2)}) collective-permute-start(bf16[3,176,512]{2,1,0:T(8,128)(2,1)S(1)} %get-tuple-element.332), channel_id=1, source_target_pairs={{0,1},{1,2},{2,3},{3,0},{4,5},{5,6},{6,7},{7,4},{8,9},{9,10},{10,1... | collective-permute-start | bytes 1622024 | tf_op jit(solution)/shard_map/ppermute | solution.py:1820
  879.3 49.0 %collective-permute-start.4 = (bf16[3,176,512]{2,1,0:T(8,128)(2,1)S(1)}, bf16[3,176,512]{2,1,0:T(8,128)(2,1)S(1)}, u32[]{:S(2)}, u32[]{:S(2)}) collective-permute-start(bf16[3,176,512]{2,1,0:T(8,128)(2,1)S(1)} %get-tuple-element.331), channel_id=1, source_target_pairs={{0,2},{1,3},{2,0},{3,1},{4,6},{5,7},{6,4},{7,5},{8,10},{9,11},{10,... | collective-permute-start | bytes 1622024 | tf_op jit(solution)/shard_map/ppermute | solution.py:1820
  883.2 46.6 %collective-permute-start.5 = (bf16[3,176,512]{2,1,0:T(8,128)(2,1)S(1)}, bf16[3,176,512]{2,1,0:T(8,128)(2,1)S(1)}, u32[]{:S(2)}, u32[]{:S(2)}) collective-permute-start(bf16[3,176,512]{2,1,0:T(8,128)(2,1)S(1)} %get-tuple-element.330), channel_id=1, source_target_pairs={{0,3},{1,0},{2,1},{3,2},{4,7},{5,4},{6,5},{7,6},{8,11},{9,8},{10,9... | collective-permute-start | bytes 1622024 | tf_op jit(solution)/shard_map/ppermute | solution.py:1820
  928.2 7.6 copy-start.8
  929.8 8.1 copy-start.16
  932.4 39.2 %collective-permute-start.6 = (bf16[704,512]{1,0:T(8,128)(2,1)}, bf16[704,512]{1,0:T(8,128)(2,1)}, u32[]{:S(2)}, u32[]{:S(2)}) collective-permute-start(bf16[704,512]{1,0:T(8,128)(2,1)} %get-tuple-element.327), channel_id=1, source_target_pairs={{0,3},{1,0},{2,1},{3,2},{4,7},{5,4},{6,5},{7,6},{8,11},{9,8},{10,9... | collective-permute-start | bytes 2162696 | tf_op jit(solution)/shard_map/ppermute | solution.py:1820
  934.6 61.7 %collective-permute-start.7 = (bf16[704,512]{1,0:T(8,128)(2,1)S(1)}, bf16[704,512]{1,0:T(8,128)(2,1)}, u32[]{:S(2)}, u32[]{:S(2)}) collective-permute-start(bf16[704,512]{1,0:T(8,128)(2,1)S(1)} %get-tuple-element.326), channel_id=1, source_target_pairs={{0,2},{1,3},{2,0},{3,1},{4,6},{5,7},{6,4},{7,5},{8,10},{9,11},{10,... | collective-permute-start | bytes 2162696 | tf_op jit(solution)/shard_map/ppermute | solution.py:1820
  934.6 62.4 %collective-permute-start.8 = (bf16[704,512]{1,0:T(8,128)(2,1)S(1)}, bf16[704,512]{1,0:T(8,128)(2,1)}, u32[]{:S(2)}, u32[]{:S(2)}) collective-permute-start(bf16[704,512]{1,0:T(8,128)(2,1)S(1)} %get-tuple-element.325), channel_id=1, source_target_pairs={{0,1},{1,2},{2,3},{3,0},{4,5},{5,6},{6,7},{7,4},{8,9},{9,10},{10,1... | collective-permute-start | bytes 2162696 | tf_op jit(solution)/shard_map/ppermute | solution.py:1820
  942.1 22.1 %copy-start.27 = (f32[3,64]{1,0:T(4,128)S(1)}, f32[3,64]{1,0:T(4,128)}, u32[]{:S(2)}) copy-start(f32[3,64]{1,0:T(4,128)} %param.31) | copy-start | bytes 2308
  942.1 22.1 %copy-start.32 = (f32[3,64]{1,0:T(4,128)S(1)}, f32[3,64]{1,0:T(4,128)}, u32[]{:S(2)}) copy-start(f32[3,64]{1,0:T(4,128)} %param.32) | copy-start | bytes 2308
  942.1 22.1 %copy-start.33 = (f32[3,64]{1,0:T(4,128)S(1)}, f32[3,64]{1,0:T(4,128)}, u32[]{:S(2)}) copy-start(f32[3,64]{1,0:T(4,128)} %param.33) | copy-start | bytes 2308
  971.6 27.8 %copy-start.6 = (f32[256,2,512]{2,1,0:T(2,128)S(1)}, f32[256,2,512]{2,1,0:T(2,128)}, u32[]{:S(2)}) copy-start(f32[256,2,512]{2,1,0:T(2,128)} %param.25) | copy-start | bytes 3145732
  999.2 2.7 copy-start.11
Sparse Core Ops, SparseCore 0:
  35.4 56.3 all-gather.6
  94.3 92.0 all-gather.14
  254.7 42.5 all-gather.8
  298.9 51.5 all-gather.10
  523.9 51.3 reduce-scatter.2
  577.3 43.2 all-gather.12
  804.7 24.3 reduce-scatter.4

commit v14 on v13

--- a/solution.py
+++ b/solution.py
@@ -200,16 +200,15 @@
 
     shape = struct((count,) + values.shape, values.dtype)
     return Task(
-        [values], [shape], [sems(count - 1), sems(count), sems()], steps, ANY, ANY, ["wide"]
-    )
-
-
-def trade(axis, values, source_of, target_of, shape, patience=2, rest=None, rest_at=None):
+        [values], [shape], [sems(count - 1), sems(count), sems()], steps, VMEM, VMEM, ["wide"]
+    )
+
+
+def trade(axis, values, source_of, target_of, shape, patience=2):
     count = lax.axis_size(axis)
-    inputs = [values] if rest is None else [values, rest]
 
     def steps(ins, outs, scratch):
-        (x_ref, *rest_ref), (out_ref,), (send, receive, local) = ins, outs, scratch
+        (x_ref,), (out_ref,), (send, receive, local) = ins, outs, scratch
         me = lax.axis_index(axis)
         copies = []
         for step in range(1, count):
@@ -223,11 +222,8 @@
             )
             copy.start()
             copies.append(copy)
-        keeps = [pltpu.make_async_copy(source_of(x_ref, me), target_of(out_ref, me), local.at[0])]
-        if rest is not None:
-            keeps.append(pltpu.make_async_copy(rest_ref[0], rest_at(out_ref), local.at[1]))
-        for keep in keeps:
-            keep.start()
+        keep = pltpu.make_async_copy(source_of(x_ref, me), target_of(out_ref, me), local)
+        keep.start()
         for turn in range(patience):
             yield
         for step in range(1, count):
@@ -237,13 +233,12 @@
             )
         for copy in copies:
             copy.wait_send()
-        for keep in keeps:
-            keep.wait()
+        keep.wait()
 
     return Task(
-        inputs,
+        [values],
         [struct(shape, values.dtype)],
-        [sems(count - 1), sems(count), sems(2)],
+        [sems(count - 1), sems(count), sems()],
         steps,
         ANY,
         ANY,
@@ -495,31 +490,6 @@
 def join_columns(axis, values):
     count, rows, size = values.shape
     return trade(axis, values, block_at, columns_of(size), (rows, count * size))
-
-
-def join_below(axis, values, rest):
-    count, rows, size = values.shape
-    above = rest.shape[0]
-
-    def target_of(ref, spot):
-        return ref.at[above:, pl.ds(pl.multiple_of(spot * size, size), size)]
-
-    shape = (above + rows, count * size)
-    return trade(
-        axis, values, block_at, target_of, shape, 2, rest, lambda ref: ref.at[:above]
-    )
-
-
-def swap_below(values, rest):
-    count, above, size = rest.shape
-    shape = (count, above + values.shape[1], size)
-
-    def target_of(ref, spot):
-        return ref.at[spot, above:]
-
-    return trade(
-        "narrow", values, turned, target_of, shape, 2, rest, lambda ref: ref.at[:, :above]
-    )
 
 
 def collect(count, parts_ref, slots, send, receive):
@@ -1989,14 +1959,15 @@
     inner = inner.reshape(sel, width)
     inner_all = lax.all_gather(inner, "wide", axis=0, tiled=True)
     gate, up, hidden, fed = feed(inner, ffn_w)
-    final_own, late_part, table_own = launch(
+    final_own, late_part, table_low = launch(
         [
             settle(fed, middle, start_own, keep_row, gain_w[2:3]),
-            join_below("wide", embed_cut[:, table_half:], table_top),
+            join_columns("wide", embed_cut[:, table_half:]),
         ],
         4,
         "settle_late",
     )
+    table_own = jnp.concatenate([table_top, table_low])
 
     table_count = table_own.shape[0]
     local_target = targets_all - (narrow_spot * vocab_rows + wide_spot * table_count)
@@ -2043,15 +2014,16 @@
     late_grad = exit_back(late_logits, log_norms[total_rows:], EXIT_LAST)
     late_back = dot(late_grad, table_own, 0, 0).astype(LOW)
     early_grad = exit_back(early_logits, log_norms[:total_rows], EXIT_EARLY)
-    grad_late, mom_owned, early_back, _ = launch(
+    grad_late, mom_low, early_back, _ = launch(
         [
             sum_wide(late_back),
-            swap_below(mom_parts[:, half:], mom_top),
+            swap_turned(mom_parts[:, half:]),
             later(product([early_grad], [table_own], 0, [[(0, 0)]]), 1),
         ],
         7,
         "sum_late",
     )
+    mom_owned = jnp.concatenate([mom_top, mom_low], axis=1)
     early_back, grad_late = lax.optimization_barrier((early_back, grad_late))
     grad_early = lax.psum_scatter(early_back[0], "wide", scatter_dimension=0, tiled=True)
     grad_final, gain_late, grad_out = launch(

time: 1030 us -> 975 us (0.947)
  Pallas kernels: 796 us -> 740 us
    pallas_call x13, Pallas kernels: 647 us -> 579 us  [launch(): pl.pallas_call(body, out_shape=outputs, in_specs=[place for task in tasks...]
  transfers between devices with their start and end apart: 16 -> 16, of which waited for: 5 -> 4; matrix products, arithmetic and copies ran while one was open for 9% -> 10% of each run, Pallas kernels for 52% -> 52%
where the time goes in v14:
time: 975 us; the launch traced here: 963 us
  Pallas kernels  740 us (76%)
  other arithmetic  89 us (9%)
  local copies, waits for them, and re-layouts  40.4 us (4%)
  waiting for transfers between devices  33.2 us (3%)
  between operations  23.2 us (2%)
  matrix products  22.4 us (2%)
  starting transfers between devices  14.7 us (2%)
    pallas_call x13, Pallas kernels, launch(): pl.pallas_call(body, out_shape=outputs, in_specs=[place for task in tasks...  579 us
    pallas_call x1, Pallas kernels, newton(): pl.pallas_call(functools.partial(newton_any_body, rows), in_specs=[pl.Blo...  42.7 us
    pallas_call x1, Pallas kernels, lookup(): pl.pallas_call(lookup_body, in_specs=[pl.BlockSpec(memory_space=pltpu.SME...  34.4 us
    ppermute x9, waiting for transfers between devices, shifted(): return lax.ppermute(parts, axis, pairs)  33.1 us
    pallas_call x5, Pallas kernels, local_call(): pl.pallas_call(body, grid=(1,), in_specs=specs, out_specs=[pl.BlockSpec(a...  29 us
    pallas_call x1, Pallas kernels, spread(): pl.pallas_call(spread_body, in_specs=[smem, smem, VMEM, VMEM], out_specs=...  26.5 us
    sub x2, other arithmetic, adamw(): weight * (1.0 - rate * decay) - rate * update  22.8 us
  transfers between devices with their start and end apart: 16, of which 4 were waited for; matrix products, arithmetic and copies ran while one was open for 10% of the time, Pallas kernels for 52%

profile of v14, /device:TPU:17, one launch (start us, length us, event | category | flops | bytes accessed | tf_op | source)
XLA Modules:
  0.0 962.9 jit_solution(725524305021834168)
XLA Ops:
  12.5 1.6 convert_element_type.131
  14.2 18.9 %gather_ids.1 = (s32[8,16,128]{2,1,0:T(8,128)}, f32[4,8,8,128]{3,2,1,0:T(8,128)}, bf16[4,256,256]{2,1,0:T(8,128)(2,1)}) custom-call(s32[16,128]{1,0:T(8,128)} %pad_bitcast_fusion.refs_0_, f32[8,128]{1,0:T(8,128)} %bitcast_convert_fusion.refs_1_, bf16[256,256]{1,0:T(8,128)(2,1)} %bitcast.270), custom_call_target="tpu_custom_call" | custom-call | bytes 108032 | tf_op jit(solution)/shard_map/gather_ids/pallas_call | solution.py:139
  35.4 2.5 convert_element_type.122
  39.2 1.9 collective-permute-start
  41.1 1.3 collective-permute-start.1
  42.4 1.4 collective-permute-start.2
  47.5 34.4 %lookup.1 = (bf16[9216,256]{1,0:T(8,128)(2,1)}, bf16[8192,256]{1,0:T(8,128)(2,1)}, s32[9248]{0:T(1024)}) custom-call(s32[9216]{0:T(1024)} %and_select_fusion.ids_ref, s32[9344]{0:T(1024)} %concatenate.44.turn_ref, f32[8192,256]{1,0:T(8,128)} %table_ref.1), custom_call_target="tpu_custom_call" | custom-call | bytes 8388608 | tf_op jit(solution)/shard_map/lookup/pallas_call | solution.py:1678
  82.0 7.0 collective-permute-done.2.refs_3_
  89.9 3.1 assemble.1
  97.9 1.9 multiply_sine_fusion
  101.4 5.4 fusion.42
  106.8 96.3 %fetch_rows.1.rows_ref = bf16[288,2048]{1,0:T(8,128)(2,1)} custom-call(bf16[4,2304,256]{2,1,0:T(8,128)(2,1)} %bitcast.235), custom_call_target="tpu_custom_call" | custom-call | bytes 737280 | tf_op jit(solution)/shard_map/fetch_rows/pallas_call | solution.py:139
  203.1 1.7 slice_convert_fusion
  204.8 5.0 make_heads.1
  209.8 37.8 %trade_heads.1 = (bf16[4,1,2,256,128]{4,3,2,1,0:T(8,128)(2,1)}, bf16[4,32,2048]{2,1,0:T(8,128)(2,1)}, bf16[8,256,256]{2,1,0:T(8,128)(2,1)}, bf16[512,2048]{1,0:T(8,128)(2,1)}) custom-call(bf16[4,1,2,256,128]{4,3,2,1,0:T(8,128)(2,1)} %get-tuple-element.125.refs_0_, bf16[32,2048]{1,0:T(8,128)(2,1)} %get-tuple-element.339.refs_1_, ...), custom_call_target="tpu_custom_call" | custom-call | bytes 999424 | tf_op jit(solution)/shard_map/trade_heads/pallas_call | solution.py:139
  247.6 6.9 attend.1
  255.9 28.0 %settle_middle.1 = (f32[32,2048]{1,0:T(8,128)}, bf16[4,32,2048]{2,1,0:T(8,128)(2,1)}, bf16[8,128,512]{2,1,0:T(8,128)(2,1)}, bf16[8,128,256]{2,1,0:T(8,128)(2,1)}) custom-call(bf16[4,32,2048]{2,1,0:T(8,128)(2,1)} %bitcast.268, f32[32,2048]{1,0:T(8,128)} %get-tuple-element.338.refs_1_.refs_2_, f32[32,2048]{1,0:T(8,128)} %get-tuple-element.338.refs_1_.refs_2_, ...), custom_call_target="tpu_custom_call" | custom-call | bytes 509952 | tf_op jit(solution)/shard_map/settle_middle/pallas_call | solution.py:139
  285.9 2.6 convert_bitcast_fusion
  288.4 1.9 pad_maximum_fusion.1
  290.7 1.5 constant_dynamic-update-slice_fusion.1
  292.2 13.4 %feed.1 = (f32[8,128,176]{2,1,0:T(8,128)}, f32[8,128,176]{2,1,0:T(8,128)}, bf16[8,128,176]{2,1,0:T(8,128)(2,1)}, bf16[128,2048]{1,0:T(8,128)(2,1)}) custom-call(bf16[128,2048]{1,0:T(8,128)(2,1)} %bitcast.247, bf16[8,3,176,2048]{3,2,1,0:T(8,128)(2,1)} %bitcast.227), custom_call_target="tpu_custom_call" | custom-call | flops 2214592512 | bytes 17301504 | tf_op jit(solution)/shard_map/feed/pallas_call | solution.py:1387
  306.2 36.2 %settle_late.1 = (f32[32,2048]{1,0:T(8,128)}, bf16[4,32,2048]{2,1,0:T(8,128)(2,1)}, bf16[512,2048]{1,0:T(8,128)(2,1)}) custom-call(bf16[4,32,2048]{2,1,0:T(8,128)(2,1)} %bitcast.271, f32[32,2048]{1,0:T(8,128)} %get-tuple-element.138.refs_1_, f32[32,2048]{1,0:T(8,128)} %get-tuple-element.338.refs_1_.refs_2_, f32[1,2048]{1,0:T(1,128)} %broadcast_in_dim.137.refs_3_, ...), custom_call_target="tpu_custom_call" | custom-call | bytes 755712 | tf_op jit(solution)/shard_map/settle_late/pallas_call | solution.py:139
  342.4 3.2 constant_dynamic-update-slice_fusion.refs_3_
  345.5 39.3 %gather_late.1 = (bf16[8,128,2048]{2,1,0:T(8,128)(2,1)}, bf16[4,352,512]{2,1,0:T(8,128)(2,1)}, f32[1024,1024]{1,0:T(8,128)}, f32[3,1024]{1,0:T(4,128)}) custom-call(bf16[128,2048]{1,0:T(8,128)(2,1)} %bitcast.264, bf16[4,352,512]{2,1,0:T(8,128)(2,1)} %get-tuple-element.329.refs_1_, bf16[1024,2048]{1,0:T(8,128)(2,1)} %all-gather.9.cloned.1.call-done.refs_2_.refs_7_, ...), custom_call_target="tpu_custom_call" | custom-call | bytes 2525184 | tf_op jit(solution)/shard_map/gather_late/pallas_call | solution.py:139
  384.8 7.6 fusion.45
  392.5 2.0 copy-done
  396.2 13.6 %combine_stats.1 = f32[3,8,256]{2,1,0:T(8,128)} custom-call(f32[3,8,256]{2,1,0:T(8,128)} %bitcast.281), custom_call_target="tpu_custom_call" | custom-call | bytes 6144 | tf_op jit(solution)/shard_map/combine_stats/pallas_call | solution.py:139
  410.6 6.7 fusion.4
  417.3 9.1 convolution_convert_fusion
  426.4 40.4 %sum_late.1 = (f32[128,2048]{1,0:T(8,128)}, bf16[4,352,512]{2,1,0:T(8,128)(2,1)}, bf16[1,1024,2048]{2,1,0:T(8,128)(2,1)}, f32[1,2048]{1,0:T(1,128)}) custom-call(bf16[8,128,2048]{2,1,0:T(8,128)(2,1)} %bitcast.238, bf16[4,352,512]{2,1,0:T(8,128)(2,1)} %get-tuple-element.328.refs_1_, bf16[1024,1024]{1,0:T(8,128)(2,1)} %get-tuple-element.354.refs_2_.refs_5_, ...), custom_call_target="tpu_custom_call" | custom-call | bytes 2327552 | tf_op jit(solution)/shard_map/sum_late/pallas_call | solution.py:139
  469.6 26.4 %back_late.1 = (f32[32,2048]{1,0:T(8,128)}, f32[1,2048]{1,0:T(1,128)}, bf16[4,32,2048]{2,1,0:T(8,128)(2,1)}) custom-call(bf16[4,32,2048]{2,1,0:T(8,128)(2,1)} %bitcast.250, f32[32,2048]{1,0:T(8,128)} %get-tuple-element.150.refs_1_, f32[32,2048]{1,0:T(8,128)} %broadcast_in_dim.140.refs_2_, f32[1,2048]{1,0:T(1,128)} %broadcast_in_dim.137.refs_3_, ...), custom_call_target="tpu_custom_call" | custom-call | bytes 232448 | tf_op jit(solution)/shard_map/back_late/pallas_call | solution.py:139
  496.1 1.3 pad_maximum_fusion.4
  497.4 14.5 %feed_back.1 = (bf16[8,3,128,176]{3,2,1,0:T(8,128)(2,1)}, bf16[128,2048]{1,0:T(8,128)(2,1)}) custom-call(bf16[128,2048]{1,0:T(8,128)(2,1)} %bitcast.249, bf16[8,3,176,2048]{3,2,1,0:T(8,128)(2,1)} %bitcast.228, f32[8,128,176]{2,1,0:T(8,128)} %get-tuple-element.152.gate_ref, f32[8,128,176]{2,1,0:T(8,128)} %get-tuple-element.153.up_ref, ...), custom_call_target="tpu_custom_call" | custom-call | flops 2214592512 | bytes 17301504 | tf_op jit(solution)/shard_map/feed_back/pallas_call | solution.py:1439
  512.6 30.9 %back_middle.1 = (f32[32,2048]{1,0:T(8,128)}, f32[1,2048]{1,0:T(1,128)}, bf16[4,32,2048]{2,1,0:T(8,128)(2,1)}, bf16[8,3,128,176]{3,2,1,0:T(8,128)(2,1)}) custom-call(bf16[4,32,2048]{2,1,0:T(8,128)(2,1)} %bitcast.265, f32[32,2048]{1,0:T(8,128)} %get-tuple-element.138.refs_1_, f32[32,2048]{1,0:T(8,128)} %broadcast_multiply_fusion.refs_2_, ...), custom_call_target="tpu_custom_call" | custom-call | bytes 502784 | tf_op jit(solution)/shard_map/back_middle/pallas_call | solution.py:139
  543.5 2.7 copy.171
  546.2 1.7 multiply_add_fusion.1.base_ref
  547.9 8.1 attend_back.1
  556.0 45.0 %trade_grads.1 = (bf16[4,1,2,256,128]{4,3,2,1,0:T(8,128)(2,1)}, f32[32,2048]{1,0:T(8,128)}, f32[32,2048]{1,0:T(8,128)}, bf16[8,128,512]{2,1,0:T(8,128)(2,1)}, bf...) custom-call(bf16[4,1,2,256,128]{4,3,2,1,0:T(8,128)(2,1)} %get-tuple-element.163.refs_0_, ...), custom_call_target="tpu_custom_call" | custom-call | bytes 2704384 | tf_op jit(solution)/shard_map/trade_grads/pallas_call | solution.py:139
  601.0 6.0 rows_back.1
  607.0 137.5 %return_rows.1 = (bf16[4,2304,256]{2,1,0:T(8,128)(2,1)}, bf16[4,1024,176]{2,1,0:T(8,128)(2,1)}, bf16[8,256,1024]{2,1,0:T(8,128)(2,1)}, bf16[8,1024,256]{2,1,0:T(...) custom-call(bf16[288,2048]{1,0:T(8,128)(2,1)} %get-tuple-element.181.refs_0_, ...), custom_call_target="tpu_custom_call" | custom-call | bytes 4146176 | tf_op jit(solution)/shard_map/return_rows/pallas_call | solution.py:139
  744.5 3.5 convolution_bitcast_fusion
  748.9 1.2 copy.217
  751.6 3.1 pad_maximum_fusion.mom_ref
  755.2 1.7 convolution_bitcast_fusion.2
  759.3 26.5 %spread.1 = (f32[8192,256]{1,0:T(8,128)}, f32[8,256]{1,0:T(8,128)}) custom-call(s32[9216]{0:T(1024)} %and_select_fusion.ids_ref, s32[9248]{0:T(1024)} %get-tuple-element.189.list_ref, bf16[9216,256]{1,0:T(8,128)(2,1)} %bitcast.234, bf16[8192,256]{1,0:T(8,128)(2,1)} %bitcast.239), custom_call_target="tpu_custom_call" | custom-call | flops 2359296 | bytes 16777216 | tf_op jit(solution)/shard_map/spread/pallas_call | solution.py:1752
  785.8 1.3 reduce_sum.168
  787.2 2.3 fusion.43
  792.8 29.2 %combine_sums.1 = (f32[4,8,256]{2,1,0:T(8,128)}, bf16[4,512,128]{2,1,0:T(8,128)(2,1)}, bf16[4,512,512]{2,1,0:T(8,128)(2,1)}, bf16[4,176,2048]{2,1,0:T(8,128)(2,1)}, f32[1,2048]{1,0:T(1,128)}) custom-call(f32[4,8,256]{2,1,0:T(8,128)} %maximum_maximum_fusion.1.refs_0_, bf16[512,128]{1,0:T(8,128)(2,1)} %bitcast.260, bf16[512,512]{1,0:T(8,128)(2,1)} %bitcast.245, ...), custom_call_target="tpu_custom_call" | custom-call | bytes 2008064 | tf_op jit(solution)/shard_map/combine_sums/pallas_call | solution.py:139
  822.0 1.3 slice_bitcast_fusion
  827.7 4.0 collective-permute-start.4
  831.8 2.3 collective-permute-start.5
  834.0 42.7 %newton.1 = bf16[4,704,512]{2,1,0:T(8,128)(2,1)} custom-call(f32[1]{0:T(128)} %bitcast.72.factor_ref, bf16[4,704,512]{2,1,0:T(8,128)(2,1)} %pad_maximum_fusion.mom_ref, bf16[4,176,2048]{2,1,0:T(8,128)(2,1)} %get-tuple-element.200.grad_ref, bf16[4,512,512]{2,1,0:T(8,128)(2,1)} %get-tuple-element.201.qo_ref, bf16[4,512,128]{2,1,0:T(8,128)(2,1)} %get-tuple-element.202.kv_ref), custom_call_target="tpu_custom_call" | custom-call | flops 23789568000 | bytes 8650752 | tf_op jit(solution)/shard_map/newton/pallas_call | solution.py:1618
  876.8 1.4 collective-permute-done.5
  878.2 1.7 dynamic-slice_bitcast_fusion
  879.9 2.3 collective-permute-start.6
  882.2 1.3 collective-permute-start.8
  883.8 1.8 copy.182
  887.1 2.7 convert_multiply_fusion
  889.8 22.1 %multiply_subtract_fusion = (f32[8192,256]{1,0:T(8,128)}, f32[8192,256]{1,0:T(8,128)}, f32[8192,256]{1,0:T(8,128)}) fusion(f32[8192,256]{1,0:T(8,128)} %table_ref.1, f32[8192,256]{1,0:T(8,128)} %get-tuple-element.195, f32[]{:T(128)} %div.51, f32[8192,256]{1,0:T(8,128)} %param.23, f32[8192,256]{1,0:T(8,128)} %param.24), kind=kLoop, calls=%fused_computation.2 | loop fusion | flops 31457280 | bytes 58720260 | tf_op jit(solution)/shard_map/sub | solution.py:1779
  912.6 6.7 bitcast_add_fusion
  919.2 23.9 %collective-permute-done.7 = bf16[704,512]{1,0:T(8,128)(2,1)} collective-permute-done((bf16[704,512]{1,0:T(8,128)(2,1)S(1)}, bf16[704,512]{1,0:T(8,128)(2,1)}, u32[]{:S(2)}, u32[]{:S(2)}) %collective-permute-start.7) | collective-permute-done | bytes 720928 | tf_op jit(solution)/shard_map/ppermute | solution.py:1790
  943.9 2.1 fusion.18
  946.2 2.2 bitcast_subtract_fusion.1
  949.7 5.1 bitcast_subtract_fusion
  (207 shorter events, 41.1 us)
Async XLA Ops:
  7.2 197.6 %all-gather.7.cloned.1.call-start = ((), (), s32[]{:S(2)}) async-start(), calls=%async_computation.2 | async-start | bytes 9437184 | tf_op jit(solution)/shard_map/all_gather | solution.py:1861
  35.3 212.3 %all-gather.15.cloned.1.call-start = ((), (), s32[]{:S(2)}) async-start(), calls=%async_computation.8 | async-start | bytes 19464192 | tf_op jit(solution)/shard_map/all_gather | solution.py:1889
  37.9 5.8 copy-start.24
  39.2 42.8 %collective-permute-start = (bf16[528,512]{1,0:T(8,128)(2,1)}, bf16[528,512]{1,0:T(8,128)(2,1)S(1)}, u32[]{:S(2)}, u32[]{:S(2)}) collective-permute-start(bf16[528,512]{1,0:T(8,128)(2,1)} %get-tuple-element.336), channel_id=1, source_target_pairs={{0,1},{1,2},{2,3},{3,0},{4,5},{5,6},{6,7},{7,4},{8,9},{9,10},{10,1... | collective-permute-start | bytes 1622024 | tf_op jit(solution)/shard_map/ppermute | solution.py:1790
  41.1 40.9 %collective-permute-start.1 = (bf16[528,512]{1,0:T(8,128)(2,1)S(1)}, bf16[528,512]{1,0:T(8,128)(2,1)S(1)}, u32[]{:S(2)}, u32[]{:S(2)}) collective-permute-start(bf16[528,512]{1,0:T(8,128)(2,1)S(1)} %get-tuple-element.335), channel_id=1, source_target_pairs={{0,2},{1,3},{2,0},{3,1},{4,6},{5,7},{6,4},{7,5},{8,10},{9,11},{10,... | collective-permute-start | bytes 1622024 | tf_op jit(solution)/shard_map/ppermute | solution.py:1790
  42.4 46.7 %collective-permute-start.2 = (bf16[528,512]{1,0:T(8,128)(2,1)S(1)}, bf16[528,512]{1,0:T(8,128)(2,1)S(1)}, u32[]{:S(2)}, u32[]{:S(2)}) collective-permute-start(bf16[528,512]{1,0:T(8,128)(2,1)S(1)} %get-tuple-element.334), channel_id=1, source_target_pairs={{0,3},{1,0},{2,1},{3,2},{4,7},{5,4},{6,5},{7,6},{8,11},{9,8},{10,9... | collective-permute-start | bytes 1622024 | tf_op jit(solution)/shard_map/ppermute | solution.py:1790
  82.0 11.1 %copy-start.23 = (f32[4,8,8,128]{3,2,1,0:T(8,128)S(1)}, f32[4,8,8,128]{3,2,1,0:T(8,128)}, u32[]{:S(2)}) copy-start(f32[4,8,8,128]{3,2,1,0:T(8,128)} %get-tuple-element.123) | copy-start | bytes 393220
  82.0 12.0 %copy-start.36 = (s32[1,2]{1,0:T(1,128)S(1)}, s32[1,2]{1,0:T(1,128)}, u32[]{:S(2)}) copy-start(s32[1,2]{1,0:T(1,128)} %param.20) | copy-start | bytes 28
  82.0 12.9 %copy-start.33 = (s32[1,128]{1,0:T(1,128)S(1)}, s32[1,128]{1,0:T(1,128)}, u32[]{:S(2)}) copy-start(s32[1,128]{1,0:T(1,128)} %param.18) | copy-start | bytes 1540
  82.0 7.1 copy-start.18
  82.0 7.0 copy-start.19
  89.1 0.8 copy-start.20
  93.0 252.5 %all-gather.9.cloned.1.call-start = ((), (), s32[]{:S(2)}) async-start(), calls=%async_computation.3 | async-start | bytes 4718592 | tf_op jit(solution)/shard_map/all_gather | solution.py:1942
  96.6 10.2 %copy-start.26 = (s32[1024]{0:T(1024)}, s32[1024]{0:T(1024)S(1)}, u32[]{:S(2)}) copy-start(s32[1024]{0:T(1024)S(1)} %fusion.32) | copy-start | bytes 12292
  99.8 0.8 copy-start.2
  247.6 37.7 %copy-start.15 = (f32[256,2,128]{2,1,0:T(2,128)S(1)}, f32[256,2,128]{2,1,0:T(2,128)}, u32[]{:S(2)}) copy-start(f32[256,2,128]{2,1,0:T(2,128)} %param.28) | copy-start | bytes 786436
  254.5 30.8 %copy-start.5 = (f32[256,2,512]{2,1,0:T(2,128)S(1)}, f32[256,2,512]{2,1,0:T(2,128)}, u32[]{:S(2)}) copy-start(f32[256,2,512]{2,1,0:T(2,128)} %param.26) | copy-start | bytes 3145732
  254.5 155.3 %all-gather.11.cloned.1.call-start = ((), (), s32[]{:S(2)}) async-start(), calls=%async_computation.4 | async-start | bytes 4718592 | tf_op jit(solution)/shard_map/all_gather | solution.py:1960
  283.9 264.0 %reduce-scatter.3.cloned.1.call-start = ((), (), s32[]{:S(2)}) async-start(), calls=%async_computation.5 | async-start | bytes 4718592 | tf_op jit(solution)/shard_map/reduce_scatter | solution.py:2028
  288.4 2.3 copy-start.9
  384.8 9.7 %copy-start.25 = (s32[8,128]{1,0:T(8,128)S(1)}, s32[8,128]{1,0:T(8,128)}, u32[]{:S(2)}) copy-start(s32[8,128]{1,0:T(8,128)} %get-tuple-element.342) | copy-start | bytes 12292
  392.5 2.0 copy-start
  392.5 3.1 copy-start.27
  417.3 9.1 copy-start.1
  466.8 1.2 copy-start.12
  466.8 29.3 %copy-start.3 = (f32[1024,64]{1,0:T(8,128)S(1)}, f32[1024,64]{1,0:T(8,128)}, u32[]{:S(2)}) copy-start(f32[1024,64]{1,0:T(8,128)} %copy-done.2) | copy-start | bytes 786436
  466.8 134.2 %all-gather.13.cloned.1.call-start = ((), (), s32[]{:S(2)}) async-start(), calls=%async_computation.6 | async-start | bytes 4718592 | tf_op jit(solution)/shard_map/all_gather | solution.py:2044
  496.0 291.1 %reduce-scatter.5.cloned.1.call-start = ((), (), s32[]{:S(2)}) async-start(), calls=%async_computation.7 | async-start | bytes 1310720 | tf_op jit(solution)/shard_map/reduce_scatter | solution.py:2100
  497.4 14.5 %copy-start.14 = (f32[32,2048]{1,0:T(8,128)S(1)}, f32[32,2048]{1,0:T(8,128)}, u32[]{:S(2)}) copy-start(f32[32,2048]{1,0:T(8,128)} %get-tuple-element.156) | copy-start | bytes 786436
  607.0 137.5 %copy-start.7 = (bf16[8,256,256]{2,1,0:T(8,128)(2,1)S(1)}, bf16[8,256,256]{2,1,0:T(8,128)(2,1)}, u32[]{:S(2)}) copy-start(bf16[8,256,256]{2,1,0:T(8,128)(2,1)} %get-tuple-element.180) | copy-start | bytes 3145732
  748.0 3.6 copy-start.10
  750.0 4.7 copy-start.13
  750.1 5.2 copy-start.21
  750.2 4.6 copy-start.22
  754.7 3.9 copy-start.28
  754.7 3.9 copy-start.29
  754.7 4.0 copy-start.32
  754.7 4.0 copy-start.31
  792.8 34.6 %copy-start.8 = (bf16[3,176,2048]{2,1,0:T(8,128)(2,1)S(1)}, bf16[3,176,2048]{2,1,0:T(8,128)(2,1)}, u32[]{:S(2)}) copy-start(bf16[3,176,2048]{2,1,0:T(8,128)(2,1)} %get-tuple-element.203) | copy-start | bytes 6488068
  827.7 49.1 %collective-permute-start.3 = (bf16[3,176,512]{2,1,0:T(8,128)(2,1)S(1)}, bf16[3,176,512]{2,1,0:T(8,128)(2,1)S(1)}, u32[]{:S(2)}, u32[]{:S(2)}) collective-permute-start(bf16[3,176,512]{2,1,0:T(8,128)(2,1)S(1)} %get-tuple-element.332), channel_id=1, source_target_pairs={{0,1},{1,2},{2,3},{3,0},{4,5},{5,6},{6,7},{7,4},{8,9},{9,10},{10,1... | collective-permute-start | bytes 1622024 | tf_op jit(solution)/shard_map/ppermute | solution.py:1790
  827.7 49.1 %collective-permute-start.4 = (bf16[3,176,512]{2,1,0:T(8,128)(2,1)S(1)}, bf16[3,176,512]{2,1,0:T(8,128)(2,1)S(1)}, u32[]{:S(2)}, u32[]{:S(2)}) collective-permute-start(bf16[3,176,512]{2,1,0:T(8,128)(2,1)S(1)} %get-tuple-element.331), channel_id=1, source_target_pairs={{0,2},{1,3},{2,0},{3,1},{4,6},{5,7},{6,4},{7,5},{8,10},{9,11},{10,... | collective-permute-start | bytes 1622024 | tf_op jit(solution)/shard_map/ppermute | solution.py:1790
  831.8 46.4 %collective-permute-start.5 = (bf16[3,176,512]{2,1,0:T(8,128)(2,1)S(1)}, bf16[3,176,512]{2,1,0:T(8,128)(2,1)S(1)}, u32[]{:S(2)}, u32[]{:S(2)}) collective-permute-start(bf16[3,176,512]{2,1,0:T(8,128)(2,1)S(1)} %get-tuple-element.330), channel_id=1, source_target_pairs={{0,3},{1,0},{2,1},{3,2},{4,7},{5,4},{6,5},{7,6},{8,11},{9,8},{10,9... | collective-permute-start | bytes 1622024 | tf_op jit(solution)/shard_map/ppermute | solution.py:1790
  876.7 6.7 copy-start.6
  878.2 7.4 copy-start.16
  878.2 7.4 copy-start.17
  879.9 39.3 %collective-permute-start.6 = (bf16[704,512]{1,0:T(8,128)(2,1)S(1)}, bf16[704,512]{1,0:T(8,128)(2,1)}, u32[]{:S(2)}, u32[]{:S(2)}) collective-permute-start(bf16[704,512]{1,0:T(8,128)(2,1)S(1)} %get-tuple-element.327), channel_id=1, source_target_pairs={{0,3},{1,0},{2,1},{3,2},{4,7},{5,4},{6,5},{7,6},{8,11},{9,8},{10,9... | collective-permute-start | bytes 2162696 | tf_op jit(solution)/shard_map/ppermute | solution.py:1790
  882.2 60.9 %collective-permute-start.7 = (bf16[704,512]{1,0:T(8,128)(2,1)S(1)}, bf16[704,512]{1,0:T(8,128)(2,1)}, u32[]{:S(2)}, u32[]{:S(2)}) collective-permute-start(bf16[704,512]{1,0:T(8,128)(2,1)S(1)} %get-tuple-element.326), channel_id=1, source_target_pairs={{0,2},{1,3},{2,0},{3,1},{4,6},{5,7},{6,4},{7,5},{8,10},{9,11},{10,... | collective-permute-start | bytes 2162696 | tf_op jit(solution)/shard_map/ppermute | solution.py:1790
  882.2 61.7 %collective-permute-start.8 = (bf16[704,512]{1,0:T(8,128)(2,1)S(1)}, bf16[704,512]{1,0:T(8,128)(2,1)}, u32[]{:S(2)}, u32[]{:S(2)}) collective-permute-start(bf16[704,512]{1,0:T(8,128)(2,1)S(1)} %get-tuple-element.325), channel_id=1, source_target_pairs={{0,1},{1,2},{2,3},{3,0},{4,5},{5,6},{6,7},{7,4},{8,9},{9,10},{10,1... | collective-permute-start | bytes 2162696 | tf_op jit(solution)/shard_map/ppermute | solution.py:1790
  889.8 22.1 %copy-start.30 = (f32[3,64]{1,0:T(4,128)S(1)}, f32[3,64]{1,0:T(4,128)}, u32[]{:S(2)}) copy-start(f32[3,64]{1,0:T(4,128)} %param.31) | copy-start | bytes 2308
  889.8 22.1 %copy-start.34 = (f32[3,64]{1,0:T(4,128)S(1)}, f32[3,64]{1,0:T(4,128)}, u32[]{:S(2)}) copy-start(f32[3,64]{1,0:T(4,128)} %param.32) | copy-start | bytes 2308
  889.8 22.1 %copy-start.35 = (f32[3,64]{1,0:T(4,128)S(1)}, f32[3,64]{1,0:T(4,128)}, u32[]{:S(2)}) copy-start(f32[3,64]{1,0:T(4,128)} %param.33) | copy-start | bytes 2308
  919.2 26.9 %copy-start.4 = (f32[256,2,512]{2,1,0:T(2,128)S(1)}, f32[256,2,512]{2,1,0:T(2,128)}, u32[]{:S(2)}) copy-start(f32[256,2,512]{2,1,0:T(2,128)} %param.25) | copy-start | bytes 3145732
  946.0 2.7 copy-start.11
Sparse Core Ops, SparseCore 0:
  35.5 56.3 all-gather.6
  94.3 92.0 all-gather.14
  254.7 42.3 all-gather.8
  298.8 51.5 all-gather.10
  466.9 52.5 reduce-scatter.2
  521.4 42.7 all-gather.12
  750.2 24.3 reduce-scatter.4

commit v15 on v14

--- a/solution.py
+++ b/solution.py
@@ -1211,9 +1211,14 @@
     sin_ref,
     cos_all_ref,
     sin_all_ref,
+    start_ref,
+    gains_ref,
+    early_ref,
     out_ref,
     grad_q_ref,
     part_ref,
+    attn_gain_ref,
+    early_gain_ref,
 ):
     count, groups, _, tok_rows, head = kv_ref.shape
     heads_own = probs_ref.shape[0]
@@ -1240,23 +1245,45 @@
             rows = slice(part * tok_rows, (part + 1) * tok_rows)
             out_ref[part, group, 0] = grad_keys[rows].astype(LOW)
             out_ref[part, group, 1] = grad_values[rows].astype(LOW)
-    part_ref[...] = dot(grad_q_ref[...], q_ref[...], 1, 1).astype(LOW)
-
-
-def attend_back(grad, proj, own_head, queries, probs, cosine, sine, cosine_all, sine_all):
+    pick = dot(grad_q_ref[...], q_ref[...], 1, 1)
+    early = early_ref[...].astype(FULL)
+    start = start_ref[...].astype(FULL)
+    start = start * lax.rsqrt(jnp.mean(start * start, axis=-1, keepdims=True) + NORM_EPS)
+    attn_gain_ref[...] = jnp.sum(start * pick, axis=0, keepdims=True)
+    early_gain_ref[...] = jnp.sum(start * early, axis=0, keepdims=True)
+    part_ref[...] = (gains_ref[0:1, :] * pick + gains_ref[2:3, :] * early).astype(LOW)
+
+
+def attend_back(
+    grad,
+    proj,
+    own_head,
+    queries,
+    probs,
+    cosine,
+    sine,
+    cosine_all,
+    sine_all,
+    start_low,
+    gains,
+    early,
+):
     count, groups, _, tok_rows, head = own_head.shape
     sel, width = grad.shape
     size = queries.shape[1]
     first = 2 * KVH * HD // size
     return local_call(
         attend_back_body,
-        [grad, proj, proj, own_head, queries, probs, cosine, sine, cosine_all, sine_all],
+        [grad, proj, proj, own_head, queries, probs, cosine, sine, cosine_all, sine_all]
+        + [start_low, gains, early],
         [entire(grad), column_block(proj, size, first), column_block(proj, size, first + 1)]
         + [
             entire(a)
             for a in (own_head, queries, probs, cosine, sine, cosine_all, sine_all)
+            + (start_low, gains, early)
         ],
-        [struct(own_head.shape, LOW), struct((sel, size), LOW), struct((sel, width), LOW)],
+        [struct(own_head.shape, LOW), struct((sel, size), LOW), struct((sel, width), LOW)]
+        + [struct((1, width), FULL)] * 2,
         8 * sel * size * width,
         "attend_back",
     )
@@ -1277,11 +1304,9 @@
     kv_ref,
     heads_ref,
     pick_ref,
-    early_ref,
     base_ref,
     out_ref,
-    attn_gain_ref,
-    early_gain_ref,
+    gain_grad_ref,
     grad_kv_ref,
 ):
     count, groups, _, tok_rows, head = heads_ref.shape
@@ -1304,26 +1329,23 @@
     tok_part, tok_gain = norm_back_rows(
         values[:tok_rows], gains_ref[0:1, :], dot(grad_kv_ref[...], kv_ref[...], 1, 1)
     )
-    pick_part, pick_gain = norm_back_rows(own, gains_ref[0:1, :], pick_ref[...])
-    early_part, early_gain = norm_back_rows(own, gains_ref[2:3, :], early_ref[...])
-    attn_gain_ref[...] = tok_gain + pick_gain
-    early_gain_ref[...] = early_gain
+    pick_part, _ = norm_back_rows(own, 1.0, pick_ref[...])
+    gain_grad_ref[...] = tok_gain
     out_ref[0:tok_rows, :] = tok_part.astype(LOW)
-    out_ref[tok_rows:, :] = (pick_part + early_part + base_ref[...]).astype(LOW)
-
-
-def rows_back(rows_low, gains, proj, heads, grad_pick, grad_early, base, rep):
+    out_ref[tok_rows:, :] = (pick_part + base_ref[...]).astype(LOW)
+
+
+def rows_back(rows_low, gains, proj, heads, grad_pick, base, rep):
     tok_rows = heads.shape[3]
     width = rows_low.shape[1]
     size = 2 * KVH * HD
     return local_call(
         functools.partial(rows_back_body, rep),
-        [rows_low, gains, proj, heads, grad_pick, grad_early, base],
+        [rows_low, gains, proj, heads, grad_pick, base],
         [entire(rows_low), entire(gains), column_block(proj, size, 0)]
-        + [entire(a) for a in (heads, grad_pick, grad_early, base)],
+        + [entire(a) for a in (heads, grad_pick, base)],
         [
             struct(rows_low.shape, LOW),
-            struct((1, width), FULL),
             struct((1, width), FULL),
             struct((tok_rows, size), LOW),
         ],
@@ -2055,14 +2077,24 @@
     grad_branch, grad_early = lax.optimization_barrier((grad_branch, grad_early))
     grad_branch = grad_branch.reshape(sel, width)
 
-    kv_parts, grad_queries, pick_part = attend_back(
-        grad_branch, proj, own_head, queries, probs, cosine, sine, cosine_all, sine_all
-    )
-    grad_kv, grad_pick, grad_early, queries_wide, branch_cols, grad_head, _ = launch(
+    kv_parts, grad_queries, pick_part, gain_pick, gain_early = attend_back(
+        grad_branch,
+        proj,
+        own_head,
+        queries,
+        probs,
+        cosine,
+        sine,
+        cosine_all,
+        sine_all,
+        start_low,
+        gain_w,
+        grad_early,
+    )
+    grad_kv, grad_pick, queries_wide, branch_cols, grad_head, _ = launch(
         [
             swap_blocks("narrow", kv_parts),
             sum_narrow(pick_part),
-            sum_narrow(grad_early),
             gather_wide(grad_queries),
             split_columns("wide", grad_branch),
             product([early_grad, late_grad], [early, late], 1, [[(0, 0), (1, 1)]]),
@@ -2072,9 +2104,10 @@
     )
     grad_kv, out_all = lax.optimization_barrier((grad_kv, out_all))
     grad_base = grad_mid + grad_final * (1.0 - keep_layer)
-    grad_rows, gain_attn, gain_early, grad_kv = rows_back(
-        rows_low, gain_w, proj, grad_kv, grad_pick, grad_early, grad_base, repeat
-    )
+    grad_rows, gain_attn, grad_kv = rows_back(
+        rows_low, gain_w, proj, grad_kv, grad_pick, grad_base, repeat
+    )
+    gain_attn = gain_attn + gain_pick
     summed_qo = jnp.stack(
         [
             jnp.einsum("wtc,wtf->cf", pick_cols, queries_wide, preferred_element_type=FULL),

time: 975 us -> 965 us (0.990)
  Pallas kernels: 740 us -> 728 us
    pallas_call x13, Pallas kernels: 579 us -> 568 us  [launch(): pl.pallas_call(body, out_shape=outputs, in_specs=[place for task in tasks...]
  transfers between devices with their start and end apart: 16 -> 16, of which waited for: 4 -> 4; matrix products, arithmetic and copies ran while one was open for 10% -> 10% of each run, Pallas kernels for 52% -> 51%
where the time goes in v15:
time: 965 us; the launch traced here: 952 us
  Pallas kernels  728 us (75%)
  other arithmetic  89 us (9%)
  local copies, waits for them, and re-layouts  40.4 us (4%)
  waiting for transfers between devices  33.9 us (4%)
  matrix products  23.5 us (2%)
  between operations  23.2 us (2%)
  starting transfers between devices  14.6 us (2%)
    pallas_call x13, Pallas kernels, launch(): pl.pallas_call(body, out_shape=outputs, in_specs=[place for task in tasks...  568 us
    pallas_call x1, Pallas kernels, newton(): pl.pallas_call(functools.partial(newton_any_body, rows), in_specs=[pl.Blo...  42.7 us
    ppermute x9, waiting for transfers between devices, shifted(): return lax.ppermute(parts, axis, pairs)  33.7 us
    pallas_call x1, Pallas kernels, lookup(): pl.pallas_call(lookup_body, in_specs=[pl.BlockSpec(memory_space=pltpu.SME...  33.7 us
    pallas_call x5, Pallas kernels, local_call(): pl.pallas_call(body, grid=(1,), in_specs=specs, out_specs=[pl.BlockSpec(a...  29.5 us
    pallas_call x1, Pallas kernels, spread(): pl.pallas_call(spread_body, in_specs=[smem, smem, VMEM, VMEM], out_specs=...  25.8 us
    sub x2, other arithmetic, adamw(): weight * (1.0 - rate * decay) - rate * update  22.8 us
  transfers between devices with their start and end apart: 16, of which 4 were waited for; matrix products, arithmetic and copies ran while one was open for 10% of the time, Pallas kernels for 51%

profile of v15, /device:TPU:17, one launch (start us, length us, event | category | flops | bytes accessed | tf_op | source)
XLA Modules:
  0.0 952.4 jit_solution(11130938277482303641)
XLA Ops:
  12.5 1.6 convert_element_type.131
  14.2 19.0 %gather_ids.1 = (s32[8,16,128]{2,1,0:T(8,128)}, f32[4,8,8,128]{3,2,1,0:T(8,128)}, bf16[4,256,256]{2,1,0:T(8,128)(2,1)}) custom-call(s32[16,128]{1,0:T(8,128)} %pad_bitcast_fusion.refs_0_, f32[8,128]{1,0:T(8,128)} %bitcast_convert_fusion.refs_1_, bf16[256,256]{1,0:T(8,128)(2,1)} %bitcast.265), custom_call_target="tpu_custom_call" | custom-call | bytes 108032 | tf_op jit(solution)/shard_map/gather_ids/pallas_call | solution.py:139
  35.4 2.5 convert_element_type.122
  39.2 1.9 collective-permute-start
  41.1 1.3 collective-permute-start.1
  42.4 1.4 collective-permute-start.2
  47.6 33.7 %lookup.1 = (bf16[9216,256]{1,0:T(8,128)(2,1)}, bf16[8192,256]{1,0:T(8,128)(2,1)}, s32[9248]{0:T(1024)}) custom-call(s32[9216]{0:T(1024)} %and_select_fusion.ids_ref, s32[9344]{0:T(1024)} %concatenate.44.turn_ref, f32[8192,256]{1,0:T(8,128)} %table_ref.1), custom_call_target="tpu_custom_call" | custom-call | bytes 8388608 | tf_op jit(solution)/shard_map/lookup/pallas_call | solution.py:1700
  81.3 7.7 collective-permute-done.2.refs_3_
  89.9 3.1 assemble.1
  97.9 1.9 multiply_sine_fusion
  101.4 5.4 fusion.42
  106.8 96.3 %fetch_rows.1.rows_ref = bf16[288,2048]{1,0:T(8,128)(2,1)} custom-call(bf16[4,2304,256]{2,1,0:T(8,128)(2,1)} %bitcast.230), custom_call_target="tpu_custom_call" | custom-call | bytes 737280 | tf_op jit(solution)/shard_map/fetch_rows/pallas_call | solution.py:139
  203.1 1.7 slice_convert_fusion
  204.8 5.0 make_heads.1
  209.8 37.8 %trade_heads.1 = (bf16[4,1,2,256,128]{4,3,2,1,0:T(8,128)(2,1)}, bf16[4,32,2048]{2,1,0:T(8,128)(2,1)}, bf16[8,256,256]{2,1,0:T(8,128)(2,1)}, bf16[512,2048]{1,0:T(8,128)(2,1)}) custom-call(bf16[4,1,2,256,128]{4,3,2,1,0:T(8,128)(2,1)} %get-tuple-element.125.refs_0_, bf16[32,2048]{1,0:T(8,128)(2,1)} %get-tuple-element.339.refs_1_, ...), custom_call_target="tpu_custom_call" | custom-call | bytes 999424 | tf_op jit(solution)/shard_map/trade_heads/pallas_call | solution.py:139
  247.6 6.9 attend.1
  255.9 28.0 %settle_middle.1 = (f32[32,2048]{1,0:T(8,128)}, bf16[4,32,2048]{2,1,0:T(8,128)(2,1)}, bf16[8,128,512]{2,1,0:T(8,128)(2,1)}, bf16[8,128,256]{2,1,0:T(8,128)(2,1)}) custom-call(bf16[4,32,2048]{2,1,0:T(8,128)(2,1)} %bitcast.263, f32[32,2048]{1,0:T(8,128)} %get-tuple-element.338.refs_1_.refs_2_, f32[32,2048]{1,0:T(8,128)} %get-tuple-element.338.refs_1_.refs_2_, ...), custom_call_target="tpu_custom_call" | custom-call | bytes 509952 | tf_op jit(solution)/shard_map/settle_middle/pallas_call | solution.py:139
  285.9 2.6 convert_bitcast_fusion
  288.5 1.9 pad_maximum_fusion.1
  290.8 1.5 constant_dynamic-update-slice_fusion.1
  292.2 13.4 %feed.1 = (f32[8,128,176]{2,1,0:T(8,128)}, f32[8,128,176]{2,1,0:T(8,128)}, bf16[8,128,176]{2,1,0:T(8,128)(2,1)}, bf16[128,2048]{1,0:T(8,128)(2,1)}) custom-call(bf16[128,2048]{1,0:T(8,128)(2,1)} %bitcast.246, bf16[8,3,176,2048]{3,2,1,0:T(8,128)(2,1)} %bitcast.222), custom_call_target="tpu_custom_call" | custom-call | flops 2214592512 | bytes 17301504 | tf_op jit(solution)/shard_map/feed/pallas_call | solution.py:1409
  306.2 36.1 %settle_late.1 = (f32[32,2048]{1,0:T(8,128)}, bf16[4,32,2048]{2,1,0:T(8,128)(2,1)}, bf16[512,2048]{1,0:T(8,128)(2,1)}) custom-call(bf16[4,32,2048]{2,1,0:T(8,128)(2,1)} %bitcast.266, f32[32,2048]{1,0:T(8,128)} %get-tuple-element.138.refs_1_, f32[32,2048]{1,0:T(8,128)} %get-tuple-element.338.refs_1_.refs_2_, f32[1,2048]{1,0:T(1,128)} %broadcast_in_dim.137.refs_3_, ...), custom_call_target="tpu_custom_call" | custom-call | bytes 755712 | tf_op jit(solution)/shard_map/settle_late/pallas_call | solution.py:139
  342.3 3.2 constant_dynamic-update-slice_fusion.refs_3_
  345.5 39.3 %gather_late.1 = (bf16[8,128,2048]{2,1,0:T(8,128)(2,1)}, bf16[4,352,512]{2,1,0:T(8,128)(2,1)}, f32[1024,1024]{1,0:T(8,128)}, f32[3,1024]{1,0:T(4,128)}) custom-call(bf16[128,2048]{1,0:T(8,128)(2,1)} %bitcast.259, bf16[4,352,512]{2,1,0:T(8,128)(2,1)} %get-tuple-element.329.refs_1_, bf16[1024,2048]{1,0:T(8,128)(2,1)} %all-gather.9.cloned.1.call-done.refs_2_.refs_6_, ...), custom_call_target="tpu_custom_call" | custom-call | bytes 2525184 | tf_op jit(solution)/shard_map/gather_late/pallas_call | solution.py:139
  384.9 7.6 fusion.45
  392.5 2.0 copy-done
  396.3 13.3 %combine_stats.1 = f32[3,8,256]{2,1,0:T(8,128)} custom-call(f32[3,8,256]{2,1,0:T(8,128)} %bitcast.276), custom_call_target="tpu_custom_call" | custom-call | bytes 6144 | tf_op jit(solution)/shard_map/combine_stats/pallas_call | solution.py:139
  410.4 6.7 fusion.4
  417.1 9.1 convolution_convert_fusion
  426.1 40.7 %sum_late.1 = (f32[128,2048]{1,0:T(8,128)}, bf16[4,352,512]{2,1,0:T(8,128)(2,1)}, bf16[1,1024,2048]{2,1,0:T(8,128)(2,1)}, f32[1,2048]{1,0:T(1,128)}) custom-call(bf16[8,128,2048]{2,1,0:T(8,128)(2,1)} %bitcast.233, bf16[4,352,512]{2,1,0:T(8,128)(2,1)} %get-tuple-element.328.refs_1_, bf16[1024,1024]{1,0:T(8,128)(2,1)} %get-tuple-element.354.refs_2_.refs_4_, ...), custom_call_target="tpu_custom_call" | custom-call | bytes 2327552 | tf_op jit(solution)/shard_map/sum_late/pallas_call | solution.py:139
  469.6 26.4 %back_late.1 = (f32[32,2048]{1,0:T(8,128)}, f32[1,2048]{1,0:T(1,128)}, bf16[4,32,2048]{2,1,0:T(8,128)(2,1)}) custom-call(bf16[4,32,2048]{2,1,0:T(8,128)(2,1)} %bitcast.249, f32[32,2048]{1,0:T(8,128)} %get-tuple-element.150.refs_1_, f32[32,2048]{1,0:T(8,128)} %broadcast_in_dim.140.refs_2_, f32[1,2048]{1,0:T(1,128)} %broadcast_in_dim.137.refs_3_, ...), custom_call_target="tpu_custom_call" | custom-call | bytes 232448 | tf_op jit(solution)/shard_map/back_late/pallas_call | solution.py:139
  496.1 1.3 pad_maximum_fusion.4
  497.5 14.5 %feed_back.1 = (bf16[8,3,128,176]{3,2,1,0:T(8,128)(2,1)}, bf16[128,2048]{1,0:T(8,128)(2,1)}) custom-call(bf16[128,2048]{1,0:T(8,128)(2,1)} %bitcast.248, bf16[8,3,176,2048]{3,2,1,0:T(8,128)(2,1)} %bitcast.223, f32[8,128,176]{2,1,0:T(8,128)} %get-tuple-element.152.gate_ref, f32[8,128,176]{2,1,0:T(8,128)} %get-tuple-element.153.up_ref, ...), custom_call_target="tpu_custom_call" | custom-call | flops 2214592512 | bytes 17301504 | tf_op jit(solution)/shard_map/feed_back/pallas_call | solution.py:1461
  512.7 30.9 %back_middle.1 = (f32[32,2048]{1,0:T(8,128)}, f32[1,2048]{1,0:T(1,128)}, bf16[4,32,2048]{2,1,0:T(8,128)(2,1)}, bf16[8,3,128,176]{3,2,1,0:T(8,128)(2,1)}) custom-call(bf16[4,32,2048]{2,1,0:T(8,128)(2,1)} %bitcast.260, f32[32,2048]{1,0:T(8,128)} %get-tuple-element.138.refs_1_, f32[32,2048]{1,0:T(8,128)} %broadcast_multiply_fusion.refs_2_, ...), custom_call_target="tpu_custom_call" | custom-call | bytes 502784 | tf_op jit(solution)/shard_map/back_middle/pallas_call | solution.py:139
  543.6 2.7 copy.171
  546.3 1.7 multiply_add_fusion.1.base_ref
  548.0 8.5 attend_back.1
  556.5 33.6 %trade_grads.1 = (bf16[4,1,2,256,128]{4,3,2,1,0:T(8,128)(2,1)}, f32[32,2048]{1,0:T(8,128)}, bf16[8,128,512]{2,1,0:T(8,128)(2,1)}, bf16[8,128,256]{2,1,0:T(8,128)...) custom-call(bf16[4,1,2,256,128]{4,3,2,1,0:T(8,128)(2,1)} %get-tuple-element.164.refs_0_, ...), custom_call_target="tpu_custom_call" | custom-call | bytes 2606080 | tf_op jit(solution)/shard_map/trade_grads/pallas_call | solution.py:139
  590.1 6.0 rows_back.1
  596.0 137.6 %return_rows.1 = (bf16[4,2304,256]{2,1,0:T(8,128)(2,1)}, bf16[4,1024,176]{2,1,0:T(8,128)(2,1)}, bf16[8,256,1024]{2,1,0:T(8,128)(2,1)}, bf16[8,1024,256]{2,1,0:T(...) custom-call(bf16[288,2048]{1,0:T(8,128)(2,1)} %get-tuple-element.181.refs_0_, ...), custom_call_target="tpu_custom_call" | custom-call | bytes 4146176 | tf_op jit(solution)/shard_map/return_rows/pallas_call | solution.py:139
  733.6 3.5 convolution_bitcast_fusion
  740.7 3.1 pad_maximum_fusion.mom_ref
  743.9 1.6 convolution_bitcast_fusion.1
  745.5 1.7 convolution_bitcast_fusion.2
  749.6 25.8 %spread.1 = (f32[8192,256]{1,0:T(8,128)}, f32[8,256]{1,0:T(8,128)}) custom-call(s32[9216]{0:T(1024)} %and_select_fusion.ids_ref, s32[9248]{0:T(1024)} %get-tuple-element.189.list_ref, bf16[9216,256]{1,0:T(8,128)(2,1)} %bitcast.229, bf16[8192,256]{1,0:T(8,128)(2,1)} %bitcast.234), custom_call_target="tpu_custom_call" | custom-call | flops 2359296 | bytes 16777216 | tf_op jit(solution)/shard_map/spread/pallas_call | solution.py:1774
  775.4 1.3 reduce_sum.168
  776.7 2.3 fusion.43
  782.3 29.2 %combine_sums.1 = (f32[4,8,256]{2,1,0:T(8,128)}, bf16[4,512,128]{2,1,0:T(8,128)(2,1)}, bf16[4,512,512]{2,1,0:T(8,128)(2,1)}, bf16[4,176,2048]{2,1,0:T(8,128)(2,1)}, f32[1,2048]{1,0:T(1,128)}) custom-call(f32[4,8,256]{2,1,0:T(8,128)} %maximum_maximum_fusion.1.refs_0_, bf16[512,128]{1,0:T(8,128)(2,1)} %bitcast.258, bf16[512,512]{1,0:T(8,128)(2,1)} %bitcast.244, ...), custom_call_target="tpu_custom_call" | custom-call | bytes 2008064 | tf_op jit(solution)/shard_map/combine_sums/pallas_call | solution.py:139
  811.6 1.3 slice_bitcast_fusion
  817.3 4.0 collective-permute-start.4
  821.3 2.3 collective-permute-start.5
  823.6 42.7 %newton.1 = bf16[4,704,512]{2,1,0:T(8,128)(2,1)} custom-call(f32[1]{0:T(128)} %bitcast.71.factor_ref, bf16[4,704,512]{2,1,0:T(8,128)(2,1)} %pad_maximum_fusion.mom_ref, bf16[4,176,2048]{2,1,0:T(8,128)(2,1)} %get-tuple-element.200.grad_ref, bf16[4,512,512]{2,1,0:T(8,128)(2,1)} %get-tuple-element.201.qo_ref, bf16[4,512,128]{2,1,0:T(8,128)(2,1)} %get-tuple-element.202.kv_ref), custom_call_target="tpu_custom_call" | custom-call | flops 23789568000 | bytes 8650752 | tf_op jit(solution)/shard_map/newton/pallas_call | solution.py:1640
  866.3 1.4 collective-permute-done.5
  867.7 1.7 dynamic-slice_bitcast_fusion
  869.4 2.3 collective-permute-start.6
  871.7 1.3 collective-permute-start.8
  873.3 1.8 copy.182
  876.6 2.7 convert_multiply_fusion
  879.2 22.1 %multiply_subtract_fusion = (f32[8192,256]{1,0:T(8,128)}, f32[8192,256]{1,0:T(8,128)}, f32[8192,256]{1,0:T(8,128)}) fusion(f32[8192,256]{1,0:T(8,128)} %table_ref.1, f32[8192,256]{1,0:T(8,128)} %get-tuple-element.195, f32[]{:T(128)} %div.51, f32[8192,256]{1,0:T(8,128)} %param.23, f32[8192,256]{1,0:T(8,128)} %param.24), kind=kLoop, calls=%fused_computation.2 | loop fusion | flops 31457280 | bytes 58720260 | tf_op jit(solution)/shard_map/sub | solution.py:1801
  902.1 6.7 bitcast_add_fusion
  908.7 23.8 %collective-permute-done.7 = bf16[704,512]{1,0:T(8,128)(2,1)} collective-permute-done((bf16[704,512]{1,0:T(8,128)(2,1)S(1)}, bf16[704,512]{1,0:T(8,128)(2,1)}, u32[]{:S(2)}, u32[]{:S(2)}) %collective-permute-start.7) | collective-permute-done | bytes 720928 | tf_op jit(solution)/shard_map/ppermute | solution.py:1812
  933.3 2.1 fusion.18
  935.7 2.2 bitcast_subtract_fusion.1
  939.1 5.1 bitcast_subtract_fusion
  (208 shorter events, 41.9 us)
Async XLA Ops:
  7.2 197.6 %all-gather.7.cloned.1.call-start = ((), (), s32[]{:S(2)}) async-start(), calls=%async_computation.2 | async-start | bytes 9437184 | tf_op jit(solution)/shard_map/all_gather | solution.py:1883
  35.4 212.3 %all-gather.15.cloned.1.call-start = ((), (), s32[]{:S(2)}) async-start(), calls=%async_computation.8 | async-start | bytes 19464192 | tf_op jit(solution)/shard_map/all_gather | solution.py:1911
  37.9 5.8 copy-start.23
  39.2 42.0 %collective-permute-start = (bf16[528,512]{1,0:T(8,128)(2,1)}, bf16[528,512]{1,0:T(8,128)(2,1)S(1)}, u32[]{:S(2)}, u32[]{:S(2)}) collective-permute-start(bf16[528,512]{1,0:T(8,128)(2,1)} %get-tuple-element.336), channel_id=1, source_target_pairs={{0,1},{1,2},{2,3},{3,0},{4,5},{5,6},{6,7},{7,4},{8,9},{9,10},{10,1... | collective-permute-start | bytes 1622024 | tf_op jit(solution)/shard_map/ppermute | solution.py:1812
  41.1 40.2 %collective-permute-start.1 = (bf16[528,512]{1,0:T(8,128)(2,1)S(1)}, bf16[528,512]{1,0:T(8,128)(2,1)S(1)}, u32[]{:S(2)}, u32[]{:S(2)}) collective-permute-start(bf16[528,512]{1,0:T(8,128)(2,1)S(1)} %get-tuple-element.335), channel_id=1, source_target_pairs={{0,2},{1,3},{2,0},{3,1},{4,6},{5,7},{6,4},{7,5},{8,10},{9,11},{10,... | collective-permute-start | bytes 1622024 | tf_op jit(solution)/shard_map/ppermute | solution.py:1812
  42.4 46.7 %collective-permute-start.2 = (bf16[528,512]{1,0:T(8,128)(2,1)S(1)}, bf16[528,512]{1,0:T(8,128)(2,1)S(1)}, u32[]{:S(2)}, u32[]{:S(2)}) collective-permute-start(bf16[528,512]{1,0:T(8,128)(2,1)S(1)} %get-tuple-element.334), channel_id=1, source_target_pairs={{0,3},{1,0},{2,1},{3,2},{4,7},{5,4},{6,5},{7,6},{8,11},{9,8},{10,9... | collective-permute-start | bytes 1622024 | tf_op jit(solution)/shard_map/ppermute | solution.py:1812
  81.2 11.8 %copy-start.22 = (f32[4,8,8,128]{3,2,1,0:T(8,128)S(1)}, f32[4,8,8,128]{3,2,1,0:T(8,128)}, u32[]{:S(2)}) copy-start(f32[4,8,8,128]{3,2,1,0:T(8,128)} %get-tuple-element.123) | copy-start | bytes 393220
  81.3 12.8 %copy-start.36 = (s32[1,2]{1,0:T(1,128)S(1)}, s32[1,2]{1,0:T(1,128)}, u32[]{:S(2)}) copy-start(s32[1,2]{1,0:T(1,128)} %param.20) | copy-start | bytes 28
  81.3 13.6 %copy-start.33 = (s32[1,128]{1,0:T(1,128)S(1)}, s32[1,128]{1,0:T(1,128)}, u32[]{:S(2)}) copy-start(s32[1,128]{1,0:T(1,128)} %param.18) | copy-start | bytes 1540
  81.3 7.8 copy-start.18
  81.3 7.8 copy-start.19
  89.1 0.8 copy-start.20
  93.0 252.5 %all-gather.9.cloned.1.call-start = ((), (), s32[]{:S(2)}) async-start(), calls=%async_computation.3 | async-start | bytes 4718592 | tf_op jit(solution)/shard_map/all_gather | solution.py:1964
  96.6 10.2 %copy-start.25 = (s32[1024]{0:T(1024)}, s32[1024]{0:T(1024)S(1)}, u32[]{:S(2)}) copy-start(s32[1024]{0:T(1024)S(1)} %fusion.32) | copy-start | bytes 12292
  99.8 0.8 copy-start.2
  247.6 37.7 %copy-start.15 = (f32[256,2,128]{2,1,0:T(2,128)S(1)}, f32[256,2,128]{2,1,0:T(2,128)}, u32[]{:S(2)}) copy-start(f32[256,2,128]{2,1,0:T(2,128)} %param.28) | copy-start | bytes 786436
  254.5 30.9 %copy-start.5 = (f32[256,2,512]{2,1,0:T(2,128)S(1)}, f32[256,2,512]{2,1,0:T(2,128)}, u32[]{:S(2)}) copy-start(f32[256,2,512]{2,1,0:T(2,128)} %param.26) | copy-start | bytes 3145732
  254.6 155.0 %all-gather.11.cloned.1.call-start = ((), (), s32[]{:S(2)}) async-start(), calls=%async_computation.4 | async-start | bytes 4718592 | tf_op jit(solution)/shard_map/all_gather | solution.py:1982
  283.9 264.0 %reduce-scatter.3.cloned.1.call-start = ((), (), s32[]{:S(2)}) async-start(), calls=%async_computation.5 | async-start | bytes 4718592 | tf_op jit(solution)/shard_map/reduce_scatter | solution.py:2050
  288.5 2.3 copy-start.9
  384.9 9.7 %copy-start.24 = (s32[8,128]{1,0:T(8,128)S(1)}, s32[8,128]{1,0:T(8,128)}, u32[]{:S(2)}) copy-start(s32[8,128]{1,0:T(8,128)} %get-tuple-element.342) | copy-start | bytes 12292
  392.5 2.0 copy-start
  392.5 3.1 copy-start.26
  417.1 9.1 copy-start.1
  466.8 1.2 copy-start.12
  466.8 29.3 %copy-start.3 = (f32[1024,64]{1,0:T(8,128)S(1)}, f32[1024,64]{1,0:T(8,128)}, u32[]{:S(2)}) copy-start(f32[1024,64]{1,0:T(8,128)} %copy-done.2) | copy-start | bytes 786436
  466.9 123.2 %all-gather.13.cloned.1.call-start = ((), (), s32[]{:S(2)}) async-start(), calls=%async_computation.6 | async-start | bytes 4718592 | tf_op jit(solution)/shard_map/all_gather | solution.py:2066
  496.1 280.6 %reduce-scatter.5.cloned.1.call-start = ((), (), s32[]{:S(2)}) async-start(), calls=%async_computation.7 | async-start | bytes 1310720 | tf_op jit(solution)/shard_map/reduce_scatter | solution.py:2133
  497.5 14.5 %copy-start.14 = (f32[32,2048]{1,0:T(8,128)S(1)}, f32[32,2048]{1,0:T(8,128)}, u32[]{:S(2)}) copy-start(f32[32,2048]{1,0:T(8,128)} %get-tuple-element.156) | copy-start | bytes 786436
  596.0 137.6 %copy-start.7 = (bf16[8,256,256]{2,1,0:T(8,128)(2,1)S(1)}, bf16[8,256,256]{2,1,0:T(8,128)(2,1)}, u32[]{:S(2)}) copy-start(bf16[8,256,256]{2,1,0:T(8,128)(2,1)} %get-tuple-element.180) | copy-start | bytes 3145732
  737.1 3.6 copy-start.10
  738.0 5.8 copy-start.27
  738.0 5.8 copy-start.29
  739.2 4.7 copy-start.13
  739.2 6.3 copy-start.21
  743.8 5.1 copy-start.28
  743.8 5.1 copy-start.30
  743.8 5.1 copy-start.32
  782.3 34.6 %copy-start.8 = (bf16[3,176,2048]{2,1,0:T(8,128)(2,1)S(1)}, bf16[3,176,2048]{2,1,0:T(8,128)(2,1)}, u32[]{:S(2)}) copy-start(bf16[3,176,2048]{2,1,0:T(8,128)(2,1)} %get-tuple-element.203) | copy-start | bytes 6488068
  817.2 49.1 %collective-permute-start.3 = (bf16[3,176,512]{2,1,0:T(8,128)(2,1)S(1)}, bf16[3,176,512]{2,1,0:T(8,128)(2,1)S(1)}, u32[]{:S(2)}, u32[]{:S(2)}) collective-permute-start(bf16[3,176,512]{2,1,0:T(8,128)(2,1)S(1)} %get-tuple-element.332), channel_id=1, source_target_pairs={{0,1},{1,2},{2,3},{3,0},{4,5},{5,6},{6,7},{7,4},{8,9},{9,10},{10,1... | collective-permute-start | bytes 1622024 | tf_op jit(solution)/shard_map/ppermute | solution.py:1812
  817.3 49.0 %collective-permute-start.4 = (bf16[3,176,512]{2,1,0:T(8,128)(2,1)S(1)}, bf16[3,176,512]{2,1,0:T(8,128)(2,1)S(1)}, u32[]{:S(2)}, u32[]{:S(2)}) collective-permute-start(bf16[3,176,512]{2,1,0:T(8,128)(2,1)S(1)} %get-tuple-element.331), channel_id=1, source_target_pairs={{0,2},{1,3},{2,0},{3,1},{4,6},{5,7},{6,4},{7,5},{8,10},{9,11},{10,... | collective-permute-start | bytes 1622024 | tf_op jit(solution)/shard_map/ppermute | solution.py:1812
  821.3 46.4 %collective-permute-start.5 = (bf16[3,176,512]{2,1,0:T(8,128)(2,1)S(1)}, bf16[3,176,512]{2,1,0:T(8,128)(2,1)S(1)}, u32[]{:S(2)}, u32[]{:S(2)}) collective-permute-start(bf16[3,176,512]{2,1,0:T(8,128)(2,1)S(1)} %get-tuple-element.330), channel_id=1, source_target_pairs={{0,3},{1,0},{2,1},{3,2},{4,7},{5,4},{6,5},{7,6},{8,11},{9,8},{10,9... | collective-permute-start | bytes 1622024 | tf_op jit(solution)/shard_map/ppermute | solution.py:1812
  866.3 6.7 copy-start.6
  867.7 7.4 copy-start.16
  867.7 7.4 copy-start.17
  869.4 39.3 %collective-permute-start.6 = (bf16[704,512]{1,0:T(8,128)(2,1)S(1)}, bf16[704,512]{1,0:T(8,128)(2,1)}, u32[]{:S(2)}, u32[]{:S(2)}) collective-permute-start(bf16[704,512]{1,0:T(8,128)(2,1)S(1)} %get-tuple-element.327), channel_id=1, source_target_pairs={{0,3},{1,0},{2,1},{3,2},{4,7},{5,4},{6,5},{7,6},{8,11},{9,8},{10,9... | collective-permute-start | bytes 2162696 | tf_op jit(solution)/shard_map/ppermute | solution.py:1812
  871.7 60.9 %collective-permute-start.7 = (bf16[704,512]{1,0:T(8,128)(2,1)S(1)}, bf16[704,512]{1,0:T(8,128)(2,1)}, u32[]{:S(2)}, u32[]{:S(2)}) collective-permute-start(bf16[704,512]{1,0:T(8,128)(2,1)S(1)} %get-tuple-element.326), channel_id=1, source_target_pairs={{0,2},{1,3},{2,0},{3,1},{4,6},{5,7},{6,4},{7,5},{8,10},{9,11},{10,... | collective-permute-start | bytes 2162696 | tf_op jit(solution)/shard_map/ppermute | solution.py:1812
  871.7 61.7 %collective-permute-start.8 = (bf16[704,512]{1,0:T(8,128)(2,1)S(1)}, bf16[704,512]{1,0:T(8,128)(2,1)}, u32[]{:S(2)}, u32[]{:S(2)}) collective-permute-start(bf16[704,512]{1,0:T(8,128)(2,1)S(1)} %get-tuple-element.325), channel_id=1, source_target_pairs={{0,1},{1,2},{2,3},{3,0},{4,5},{5,6},{6,7},{7,4},{8,9},{9,10},{10,1... | collective-permute-start | bytes 2162696 | tf_op jit(solution)/shard_map/ppermute | solution.py:1812
  879.2 22.1 %copy-start.31 = (f32[3,64]{1,0:T(4,128)S(1)}, f32[3,64]{1,0:T(4,128)}, u32[]{:S(2)}) copy-start(f32[3,64]{1,0:T(4,128)} %param.31) | copy-start | bytes 2308
  879.2 22.1 %copy-start.34 = (f32[3,64]{1,0:T(4,128)S(1)}, f32[3,64]{1,0:T(4,128)}, u32[]{:S(2)}) copy-start(f32[3,64]{1,0:T(4,128)} %param.32) | copy-start | bytes 2308
  879.2 22.1 %copy-start.35 = (f32[3,64]{1,0:T(4,128)S(1)}, f32[3,64]{1,0:T(4,128)}, u32[]{:S(2)}) copy-start(f32[3,64]{1,0:T(4,128)} %param.33) | copy-start | bytes 2308
  908.7 26.9 %copy-start.4 = (f32[256,2,512]{2,1,0:T(2,128)S(1)}, f32[256,2,512]{2,1,0:T(2,128)}, u32[]{:S(2)}) copy-start(f32[256,2,512]{2,1,0:T(2,128)} %param.25) | copy-start | bytes 3145732
  935.5 2.7 copy-start.11
Sparse Core Ops, SparseCore 0:
  35.5 56.3 all-gather.6
  94.3 92.0 all-gather.14
  254.7 42.3 all-gather.8
  298.8 51.5 all-gather.10
  467.0 52.5 reduce-scatter.2
  521.4 42.8 all-gather.12
  739.3 24.4 reduce-scatter.4

commit v16 on v15

--- a/solution.py
+++ b/solution.py
@@ -1911,7 +1911,7 @@
     ffn_w = lax.all_gather(ffn_sub, "wide", axis=0)
     found = found.reshape(narrow_count, wide_count * all_rows, columns)
     embed_cut = embed_low.reshape(wide_count, vocab_rows // wide_count, columns)
-    table_half = embed_cut.shape[1] // 2
+    third = embed_cut.shape[1] // 48 * 16
     rows_low = launch([fetch_rows(found, all_rows)], 1, "fetch_rows")[0]
 
     mom_qo = jnp.moveaxis(attn_qo_mom, 1, 0)
@@ -1938,12 +1938,11 @@
     by_head, normed_tok = make_heads(
         rows_low, gain_w[0:1], proj, tok_part(cosine_all), tok_part(sine_all), groups, repeat
     )
-    own_head, start_low, tok_cols, table_top = launch(
+    own_head, start_low, table_top = launch(
         [
             swap_blocks("narrow", by_head),
             gather_blocks("narrow", rows_low[tok_rows:]),
-            split_columns("wide", normed_tok),
-            join_columns("wide", embed_cut[:, :table_half]),
+            join_columns("wide", embed_cut[:, :third]),
         ],
         2,
         "trade_heads",
@@ -1963,7 +1962,7 @@
     )
     early = lax.all_gather(early_part, "wide", axis=0, tiled=True)
     start_own = rows_low[tok_rows:].astype(FULL)
-    middle, inner, mixed_wide, pick_cols = launch(
+    middle, inner, table_middle = launch(
         [
             settle(
                 attn_part,
@@ -1972,8 +1971,7 @@
                 jnp.ones((1, width), FULL),
                 gain_w[1:2],
             ),
-            gather_wide(mixed),
-            split_columns("wide", normed),
+            join_columns("wide", embed_cut[:, third : 2 * third]),
         ],
         3,
         "settle_middle",
@@ -1984,12 +1982,12 @@
     final_own, late_part, table_low = launch(
         [
             settle(fed, middle, start_own, keep_row, gain_w[2:3]),
-            join_columns("wide", embed_cut[:, table_half:]),
+            join_columns("wide", embed_cut[:, 2 * third :]),
         ],
         4,
         "settle_late",
     )
-    table_own = jnp.concatenate([table_top, table_low])
+    table_own = jnp.concatenate([table_top, table_middle, table_low])
 
     table_count = table_own.shape[0]
     local_target = targets_all - (narrow_spot * vocab_rows + wide_spot * table_count)
@@ -2048,7 +2046,7 @@
     mom_owned = jnp.concatenate([mom_top, mom_low], axis=1)
     early_back, grad_late = lax.optimization_barrier((early_back, grad_late))
     grad_early = lax.psum_scatter(early_back[0], "wide", scatter_dimension=0, tiled=True)
-    grad_final, gain_late, grad_out = launch(
+    grad_final, gain_late, grad_out, mixed_wide, pick_cols = launch(
         [
             settle_back(
                 grad_late.astype(LOW),
@@ -2057,6 +2055,8 @@
                 keep_row,
                 gain_w[2:3],
             ),
+            gather_wide(mixed),
+            split_columns("wide", normed),
         ],
         8,
         "back_late",
@@ -2065,10 +2065,11 @@
     grad_out = grad_out.reshape(sel, width)
     out_all = lax.all_gather(grad_out, "wide", axis=0, tiled=True)
     acts, fed_back = feed_back(grad_out, ffn_w, gate, up, hidden)
-    grad_mid, gain_mid, grad_branch, acts = launch(
+    grad_mid, gain_mid, grad_branch, acts, tok_cols = launch(
         [
             settle_back(fed_back, middle, grad_layer, keep_row, gain_w[1:2]),
             swap_blocks("wide", acts),
+            split_columns("wide", normed_tok),
         ],
         9,
         "back_middle",

time: 965 us -> 959 us (level)
  Pallas kernels: 728 us -> 710 us
  transfers between devices with their start and end apart: 16 -> 16, of which waited for: 4 -> 5; matrix products, arithmetic and copies ran while one was open for 10% -> 11% of each run, Pallas kernels for 51% -> 50%
where the time goes in v16:
time: 959 us; the launch traced here: 944 us
  Pallas kernels  710 us (74%)
  other arithmetic  89 us (9%)
  local copies, waits for them, and re-layouts  41.7 us (4%)
  waiting for transfers between devices  40.5 us (4%)
  matrix products  23.5 us (2%)
  between operations  23.2 us (2%)
  starting transfers between devices  15.9 us (2%)
    pallas_call x13, Pallas kernels, launch(): pl.pallas_call(body, out_shape=outputs, in_specs=[place for task in tasks...  563 us
    pallas_call x1, Pallas kernels, newton(): pl.pallas_call(functools.partial(newton_any_body, rows), in_specs=[pl.Blo...  42.7 us
    ppermute x9, waiting for transfers between devices, shifted(): return lax.ppermute(parts, axis, pairs)  40.3 us
    pallas_call x5, Pallas kernels, local_call(): pl.pallas_call(body, grid=(1,), in_specs=specs, out_specs=[pl.BlockSpec(a...  28.9 us
    pallas_call x1, Pallas kernels, lookup(): pl.pallas_call(lookup_body, in_specs=[pl.BlockSpec(memory_space=pltpu.SME...  27.7 us
    sub x2, other arithmetic, adamw(): weight * (1.0 - rate * decay) - rate * update  22.8 us
    pallas_call x1, Pallas kernels, spread(): pl.pallas_call(spread_body, in_specs=[smem, smem, VMEM, VMEM], out_specs=...  19.9 us
  transfers between devices with their start and end apart: 16, of which 5 were waited for; matrix products, arithmetic and copies ran while one was open for 11% of the time, Pallas kernels for 50%

profile of v16, /device:TPU:17, one launch (start us, length us, event | category | flops | bytes accessed | tf_op | source)
XLA Modules:
  0.0 944.0 jit_solution(919145164980243069)
XLA Ops:
  12.5 1.6 convert_element_type.131
  14.2 19.0 %gather_ids.1 = (s32[8,16,128]{2,1,0:T(8,128)}, f32[4,8,8,128]{3,2,1,0:T(8,128)}, bf16[4,256,256]{2,1,0:T(8,128)(2,1)}) custom-call(s32[16,128]{1,0:T(8,128)} %pad_bitcast_fusion.refs_0_, f32[8,128]{1,0:T(8,128)} %bitcast_convert_fusion.refs_1_, bf16[256,256]{1,0:T(8,128)(2,1)} %bitcast.267), custom_call_target="tpu_custom_call" | custom-call | bytes 108032 | tf_op jit(solution)/shard_map/gather_ids/pallas_call | solution.py:139
  35.4 2.5 convert_element_type.122
  39.2 1.9 collective-permute-start
  42.4 1.4 collective-permute-start.2
  47.6 27.7 %lookup.1 = (bf16[9216,256]{1,0:T(8,128)(2,1)}, bf16[8192,256]{1,0:T(8,128)(2,1)}, s32[9248]{0:T(1024)}) custom-call(s32[9216]{0:T(1024)} %and_select_fusion.ids_ref, s32[9344]{0:T(1024)} %concatenate.44.turn_ref, f32[8192,256]{1,0:T(8,128)} %table_ref.1), custom_call_target="tpu_custom_call" | custom-call | bytes 8388608 | tf_op jit(solution)/shard_map/lookup/pallas_call | solution.py:1700
  75.4 2.1 collective-permute-done.1.refs_2_
  77.5 11.6 %collective-permute-done.2.refs_3_ = bf16[528,512]{1,0:T(8,128)(2,1)S(1)} collective-permute-done((bf16[528,512]{1,0:T(8,128)(2,1)S(1)}, bf16[528,512]{1,0:T(8,128)(2,1)S(1)}, u32[]{:S(2)}, u32[]{:S(2)}) %collective-permute-start.2) | collective-permute-done | bytes 540704 | tf_op jit(solution)/shard_map/ppermute | solution.py:1812
  89.9 3.1 assemble.1
  97.8 1.9 multiply_sine_fusion
  101.4 4.0 fusion.42
  105.4 96.6 %fetch_rows.1.rows_ref = bf16[288,2048]{1,0:T(8,128)(2,1)} custom-call(bf16[4,2304,256]{2,1,0:T(8,128)(2,1)} %bitcast.230), custom_call_target="tpu_custom_call" | custom-call | bytes 737280 | tf_op jit(solution)/shard_map/fetch_rows/pallas_call | solution.py:139
  202.0 1.7 slice_convert_fusion
  203.7 5.0 make_heads.1
  208.7 24.9 %trade_heads.1 = (bf16[4,1,2,256,128]{4,3,2,1,0:T(8,128)(2,1)}, bf16[4,32,2048]{2,1,0:T(8,128)(2,1)}, bf16[336,2048]{1,0:T(8,128)(2,1)}) custom-call(bf16[4,1,2,256,128]{4,3,2,1,0:T(8,128)(2,1)} %get-tuple-element.126.refs_0_, bf16[32,2048]{1,0:T(8,128)(2,1)} %get-tuple-element.341.refs_1_, bf16[8,336,256]{2,1,0:T(8,128)(2,1)} %get-tuple-element.326.refs_2_), custom_call_target="tpu_custom_call" | custom-call | bytes 557056 | tf_op jit(solution)/shard_map/trade_heads/pallas_call | solution.py:139
  233.6 6.9 attend.1
  241.9 27.4 %settle_middle.1 = (f32[32,2048]{1,0:T(8,128)}, bf16[4,32,2048]{2,1,0:T(8,128)(2,1)}, bf16[336,2048]{1,0:T(8,128)(2,1)}) custom-call(bf16[4,32,2048]{2,1,0:T(8,128)(2,1)} %bitcast.260, f32[32,2048]{1,0:T(8,128)} %get-tuple-element.340.refs_1_.refs_2_, f32[32,2048]{1,0:T(8,128)} %get-tuple-element.340.refs_1_.refs_2_, f32[1,2048]{1,0:T(1,128)} %broadcast_in_dim.136.refs_3_, ...), custom_call_target="tpu_custom_call" | custom-call | bytes 575488 | tf_op jit(solution)/shard_map/settle_middle/pallas_call | solution.py:139
  269.4 2.6 slice.148.refs_5_
  273.9 2.5 convert_bitcast_fusion
  276.4 1.9 pad_maximum_fusion.1
  279.5 13.5 %feed.1 = (f32[8,128,176]{2,1,0:T(8,128)}, f32[8,128,176]{2,1,0:T(8,128)}, bf16[8,128,176]{2,1,0:T(8,128)(2,1)}, bf16[128,2048]{1,0:T(8,128)(2,1)}) custom-call(bf16[128,2048]{1,0:T(8,128)(2,1)} %bitcast.247, bf16[8,3,176,2048]{3,2,1,0:T(8,128)(2,1)} %bitcast.222), custom_call_target="tpu_custom_call" | custom-call | flops 2214592512 | bytes 17301504 | tf_op jit(solution)/shard_map/feed/pallas_call | solution.py:1409
  293.6 28.7 %settle_late.1 = (f32[32,2048]{1,0:T(8,128)}, bf16[4,32,2048]{2,1,0:T(8,128)(2,1)}, bf16[352,2048]{1,0:T(8,128)(2,1)}) custom-call(bf16[4,32,2048]{2,1,0:T(8,128)(2,1)} %bitcast.263, f32[32,2048]{1,0:T(8,128)} %get-tuple-element.136.refs_1_, f32[32,2048]{1,0:T(8,128)} %get-tuple-element.340.refs_1_.refs_2_, f32[1,2048]{1,0:T(1,128)} %broadcast_in_dim.137.refs_3_, ...), custom_call_target="tpu_custom_call" | custom-call | bytes 591872 | tf_op jit(solution)/shard_map/settle_late/pallas_call | solution.py:139
  323.6 2.7 constant_dynamic-update-slice_fusion.refs_3_
  326.3 40.8 %gather_late.1 = (bf16[8,128,2048]{2,1,0:T(8,128)(2,1)}, bf16[4,352,512]{2,1,0:T(8,128)(2,1)}, f32[1024,1024]{1,0:T(8,128)}, f32[3,1024]{1,0:T(4,128)}) custom-call(bf16[128,2048]{1,0:T(8,128)(2,1)} %bitcast.261, bf16[4,352,512]{2,1,0:T(8,128)(2,1)} %get-tuple-element.331.refs_1_, bf16[1024,2048]{1,0:T(8,128)(2,1)} %all-gather.9.cloned.1.call-done.refs_2_.refs_6_, ...), custom_call_target="tpu_custom_call" | custom-call | bytes 2525184 | tf_op jit(solution)/shard_map/gather_late/pallas_call | solution.py:139
  367.1 7.6 fusion.45
  374.7 2.0 copy-done
  378.5 13.6 %combine_stats.1 = f32[3,8,256]{2,1,0:T(8,128)} custom-call(f32[3,8,256]{2,1,0:T(8,128)} %bitcast.277), custom_call_target="tpu_custom_call" | custom-call | bytes 6144 | tf_op jit(solution)/shard_map/combine_stats/pallas_call | solution.py:139
  392.9 6.7 fusion.4
  399.6 9.1 convolution_convert_fusion
  408.7 40.5 %sum_late.1 = (f32[128,2048]{1,0:T(8,128)}, bf16[4,352,512]{2,1,0:T(8,128)(2,1)}, bf16[1,1024,2048]{2,1,0:T(8,128)(2,1)}, f32[1,2048]{1,0:T(1,128)}) custom-call(bf16[8,128,2048]{2,1,0:T(8,128)(2,1)} %bitcast.233, bf16[4,352,512]{2,1,0:T(8,128)(2,1)} %get-tuple-element.330.refs_1_, bf16[1024,1024]{1,0:T(8,128)(2,1)} %get-tuple-element.356.refs_2_.refs_4_, ...), custom_call_target="tpu_custom_call" | custom-call | bytes 2327552 | tf_op jit(solution)/shard_map/sum_late/pallas_call | solution.py:139
  452.0 27.5 %back_late.1 = (f32[32,2048]{1,0:T(8,128)}, f32[1,2048]{1,0:T(1,128)}, bf16[4,32,2048]{2,1,0:T(8,128)(2,1)}, bf16[8,128,512]{2,1,0:T(8,128)(2,1)}, bf16[8,128,256]{2,1,0:T(8,128)(2,1)}) custom-call(bf16[4,32,2048]{2,1,0:T(8,128)(2,1)} %bitcast.250, f32[32,2048]{1,0:T(8,128)} %get-tuple-element.149.refs_1_, f32[32,2048]{1,0:T(8,128)} %broadcast_in_dim.140.refs_2_, ...), custom_call_target="tpu_custom_call" | custom-call | bytes 510976 | tf_op jit(solution)/shard_map/back_late/pallas_call | solution.py:139
  479.6 1.3 pad_maximum_fusion.4
  480.9 14.6 %feed_back.1 = (bf16[8,3,128,176]{3,2,1,0:T(8,128)(2,1)}, bf16[128,2048]{1,0:T(8,128)(2,1)}) custom-call(bf16[128,2048]{1,0:T(8,128)(2,1)} %bitcast.249, bf16[8,3,176,2048]{3,2,1,0:T(8,128)(2,1)} %bitcast.223, f32[8,128,176]{2,1,0:T(8,128)} %get-tuple-element.153.gate_ref, f32[8,128,176]{2,1,0:T(8,128)} %get-tuple-element.154.up_ref, ...), custom_call_target="tpu_custom_call" | custom-call | flops 2214592512 | bytes 17301504 | tf_op jit(solution)/shard_map/feed_back/pallas_call | solution.py:1461
  496.2 45.4 %back_middle.1 = (f32[32,2048]{1,0:T(8,128)}, f32[1,2048]{1,0:T(1,128)}, bf16[4,32,2048]{2,1,0:T(8,128)(2,1)}, bf16[8,3,128,176]{3,2,1,0:T(8,128)(2,1)}, bf16[8,256,256]{2,1,0:T(8,128)(2,1)}) custom-call(bf16[4,32,2048]{2,1,0:T(8,128)(2,1)} %bitcast.262, f32[32,2048]{1,0:T(8,128)} %get-tuple-element.136.refs_1_, f32[32,2048]{1,0:T(8,128)} %broadcast_multiply_fusion.refs_2_, ...), custom_call_target="tpu_custom_call" | custom-call | bytes 764928 | tf_op jit(solution)/shard_map/back_middle/pallas_call | solution.py:139
  541.6 2.7 copy.171
  544.3 1.7 multiply_add_fusion.1.base_ref
  546.0 7.9 attend_back.1
  553.9 32.2 %trade_grads.1 = (bf16[4,1,2,256,128]{4,3,2,1,0:T(8,128)(2,1)}, f32[32,2048]{1,0:T(8,128)}, bf16[8,128,512]{2,1,0:T(8,128)(2,1)}, bf16[8,128,256]{2,1,0:T(8,128)...) custom-call(bf16[4,1,2,256,128]{4,3,2,1,0:T(8,128)(2,1)} %get-tuple-element.166.refs_0_, ...), custom_call_target="tpu_custom_call" | custom-call | bytes 2606080 | tf_op jit(solution)/shard_map/trade_grads/pallas_call | solution.py:139
  586.1 6.0 rows_back.1
  592.1 136.9 %return_rows.1 = (bf16[4,2304,256]{2,1,0:T(8,128)(2,1)}, bf16[4,1024,176]{2,1,0:T(8,128)(2,1)}, bf16[8,256,1024]{2,1,0:T(8,128)(2,1)}, bf16[8,1024,256]{2,1,0:T(...) custom-call(bf16[288,2048]{1,0:T(8,128)(2,1)} %get-tuple-element.183.refs_0_, ...), custom_call_target="tpu_custom_call" | custom-call | bytes 4146176 | tf_op jit(solution)/shard_map/return_rows/pallas_call | solution.py:139
  729.1 3.5 convolution_bitcast_fusion
  736.1 3.1 pad_maximum_fusion.mom_ref
  739.3 1.5 convolution_bitcast_fusion.1
  740.9 1.7 convolution_bitcast_fusion.2
  744.9 19.9 %spread.1 = (f32[8192,256]{1,0:T(8,128)}, f32[8,256]{1,0:T(8,128)}) custom-call(s32[9216]{0:T(1024)} %and_select_fusion.ids_ref, s32[9248]{0:T(1024)} %get-tuple-element.191.list_ref, bf16[9216,256]{1,0:T(8,128)(2,1)} %bitcast.229, bf16[8192,256]{1,0:T(8,128)(2,1)} %bitcast.234), custom_call_target="tpu_custom_call" | custom-call | flops 2359296 | bytes 16777216 | tf_op jit(solution)/shard_map/spread/pallas_call | solution.py:1774
  764.8 1.3 reduce_sum.168
  766.1 2.3 fusion.43
  771.8 29.4 %combine_sums.1 = (f32[4,8,256]{2,1,0:T(8,128)}, bf16[4,512,128]{2,1,0:T(8,128)(2,1)}, bf16[4,512,512]{2,1,0:T(8,128)(2,1)}, bf16[4,176,2048]{2,1,0:T(8,128)(2,1)}, f32[1,2048]{1,0:T(1,128)}) custom-call(f32[4,8,256]{2,1,0:T(8,128)} %maximum_maximum_fusion.1.refs_0_, bf16[512,128]{1,0:T(8,128)(2,1)} %bitcast.259, bf16[512,512]{1,0:T(8,128)(2,1)} %bitcast.245, ...), custom_call_target="tpu_custom_call" | custom-call | bytes 2008064 | tf_op jit(solution)/shard_map/combine_sums/pallas_call | solution.py:139
  801.2 1.3 slice_bitcast_fusion
  806.8 1.7 collective-permute-start.3
  808.5 3.7 collective-permute-start.4
  812.2 2.3 collective-permute-start.5
  814.5 42.7 %newton.1 = bf16[4,704,512]{2,1,0:T(8,128)(2,1)} custom-call(f32[1]{0:T(128)} %bitcast.71.factor_ref, bf16[4,704,512]{2,1,0:T(8,128)(2,1)} %pad_maximum_fusion.mom_ref, bf16[4,176,2048]{2,1,0:T(8,128)(2,1)} %get-tuple-element.202.grad_ref, bf16[4,512,512]{2,1,0:T(8,128)(2,1)} %get-tuple-element.203.qo_ref, bf16[4,512,128]{2,1,0:T(8,128)(2,1)} %get-tuple-element.204.kv_ref), custom_call_target="tpu_custom_call" | custom-call | flops 23789568000 | bytes 8650752 | tf_op jit(solution)/shard_map/newton/pallas_call | solution.py:1640
  857.3 1.6 collective-permute-done.5
  858.8 1.7 dynamic-slice_bitcast_fusion
  860.6 2.3 collective-permute-start.6
  864.4 1.8 copy.182
  867.7 2.7 convert_multiply_fusion
  870.4 22.1 %multiply_subtract_fusion = (f32[8192,256]{1,0:T(8,128)}, f32[8192,256]{1,0:T(8,128)}, f32[8192,256]{1,0:T(8,128)}) fusion(f32[8192,256]{1,0:T(8,128)} %table_ref.1, f32[8192,256]{1,0:T(8,128)} %get-tuple-element.197, f32[]{:T(128)} %div.51, f32[8192,256]{1,0:T(8,128)} %param.23, f32[8192,256]{1,0:T(8,128)} %param.24), kind=kLoop, calls=%fused_computation.2 | loop fusion | flops 31457280 | bytes 58720260 | tf_op jit(solution)/shard_map/sub | solution.py:1801
  893.2 6.7 bitcast_add_fusion
  899.9 24.4 %collective-permute-done.7 = bf16[704,512]{1,0:T(8,128)(2,1)} collective-permute-done((bf16[704,512]{1,0:T(8,128)(2,1)S(1)}, bf16[704,512]{1,0:T(8,128)(2,1)}, u32[]{:S(2)}, u32[]{:S(2)}) %collective-permute-start.7) | collective-permute-done | bytes 720928 | tf_op jit(solution)/shard_map/ppermute | solution.py:1812
  924.9 2.1 fusion.18
  927.2 2.2 bitcast_subtract_fusion.1
  930.7 5.1 bitcast_subtract_fusion
  (212 shorter events, 46.3 us)
Async XLA Ops:
  7.2 196.5 %all-gather.7.cloned.1.call-start = ((), (), s32[]{:S(2)}) async-start(), calls=%async_computation.2 | async-start | bytes 9437184 | tf_op jit(solution)/shard_map/all_gather | solution.py:1883
  35.4 198.3 %all-gather.15.cloned.1.call-start = ((), (), s32[]{:S(2)}) async-start(), calls=%async_computation.8 | async-start | bytes 19464192 | tf_op jit(solution)/shard_map/all_gather | solution.py:1911
  37.9 5.8 copy-start.24
  39.2 36.1 %collective-permute-start = (bf16[528,512]{1,0:T(8,128)(2,1)}, bf16[528,512]{1,0:T(8,128)(2,1)S(1)}, u32[]{:S(2)}, u32[]{:S(2)}) collective-permute-start(bf16[528,512]{1,0:T(8,128)(2,1)} %get-tuple-element.338), channel_id=1, source_target_pairs={{0,1},{1,2},{2,3},{3,0},{4,5},{5,6},{6,7},{7,4},{8,9},{9,10},{10,1... | collective-permute-start | bytes 1622024 | tf_op jit(solution)/shard_map/ppermute | solution.py:1812
  41.1 36.4 %collective-permute-start.1 = (bf16[528,512]{1,0:T(8,128)(2,1)S(1)}, bf16[528,512]{1,0:T(8,128)(2,1)S(1)}, u32[]{:S(2)}, u32[]{:S(2)}) collective-permute-start(bf16[528,512]{1,0:T(8,128)(2,1)S(1)} %get-tuple-element.337), channel_id=1, source_target_pairs={{0,2},{1,3},{2,0},{3,1},{4,6},{5,7},{6,4},{7,5},{8,10},{9,11},{10,... | collective-permute-start | bytes 1622024 | tf_op jit(solution)/shard_map/ppermute | solution.py:1812
  42.4 46.7 %collective-permute-start.2 = (bf16[528,512]{1,0:T(8,128)(2,1)S(1)}, bf16[528,512]{1,0:T(8,128)(2,1)S(1)}, u32[]{:S(2)}, u32[]{:S(2)}) collective-permute-start(bf16[528,512]{1,0:T(8,128)(2,1)S(1)} %get-tuple-element.336), channel_id=1, source_target_pairs={{0,3},{1,0},{2,1},{3,2},{4,7},{5,4},{6,5},{7,6},{8,11},{9,8},{10,9... | collective-permute-start | bytes 1622024 | tf_op jit(solution)/shard_map/ppermute | solution.py:1812
  75.3 17.8 %copy-start.23 = (f32[4,8,8,128]{3,2,1,0:T(8,128)S(1)}, f32[4,8,8,128]{3,2,1,0:T(8,128)}, u32[]{:S(2)}) copy-start(f32[4,8,8,128]{3,2,1,0:T(8,128)} %get-tuple-element.124) | copy-start | bytes 393220
  75.3 18.7 %copy-start.37 = (s32[1,2]{1,0:T(1,128)S(1)}, s32[1,2]{1,0:T(1,128)}, u32[]{:S(2)}) copy-start(s32[1,2]{1,0:T(1,128)} %param.20) | copy-start | bytes 28
  75.3 19.6 %copy-start.34 = (s32[1,128]{1,0:T(1,128)S(1)}, s32[1,128]{1,0:T(1,128)}, u32[]{:S(2)}) copy-start(s32[1,128]{1,0:T(1,128)} %param.18) | copy-start | bytes 1540
  75.3 13.7 %copy-start.19 = (bf16[528,512]{1,0:T(8,128)(2,1)}, bf16[528,512]{1,0:T(8,128)(2,1)S(1)}, u32[]{:S(2)}) copy-start(bf16[528,512]{1,0:T(8,128)(2,1)S(1)} %collective-permute-done.refs_1_) | copy-start | bytes 1622020
  77.5 11.6 %copy-start.20 = (bf16[528,512]{1,0:T(8,128)(2,1)}, bf16[528,512]{1,0:T(8,128)(2,1)S(1)}, u32[]{:S(2)}) copy-start(bf16[528,512]{1,0:T(8,128)(2,1)S(1)} %collective-permute-done.1.refs_2_) | copy-start | bytes 1622020
  89.1 0.8 copy-start.21
  93.0 233.2 %all-gather.9.cloned.1.call-start = ((), (), s32[]{:S(2)}) async-start(), calls=%async_computation.3 | async-start | bytes 4718592 | tf_op jit(solution)/shard_map/all_gather | solution.py:1963
  96.6 8.8 copy-start.26
  99.7 0.8 copy-start.2
  240.5 32.8 %copy-start.16 = (f32[256,2,128]{2,1,0:T(2,128)S(1)}, f32[256,2,128]{2,1,0:T(2,128)}, u32[]{:S(2)}) copy-start(f32[256,2,128]{2,1,0:T(2,128)} %param.28) | copy-start | bytes 786436
  240.5 32.9 %copy-start.5 = (f32[256,2,512]{2,1,0:T(2,128)S(1)}, f32[256,2,512]{2,1,0:T(2,128)}, u32[]{:S(2)}) copy-start(f32[256,2,512]{2,1,0:T(2,128)} %param.26) | copy-start | bytes 3145732
  240.5 151.6 %all-gather.11.cloned.1.call-start = ((), (), s32[]{:S(2)}) async-start(), calls=%async_computation.4 | async-start | bytes 4718592 | tf_op jit(solution)/shard_map/all_gather | solution.py:1980
  269.3 276.7 %reduce-scatter.3.cloned.1.call-start = ((), (), s32[]{:S(2)}) async-start(), calls=%async_computation.5 | async-start | bytes 4718592 | tf_op jit(solution)/shard_map/reduce_scatter | solution.py:2048
  276.4 1.9 copy-start.10
  279.5 42.8 %copy-start.11 = (bf16[336,2048]{1,0:T(8,128)(2,1)S(1)}, bf16[336,2048]{1,0:T(8,128)(2,1)}, u32[]{:S(2)}) copy-start(bf16[336,2048]{1,0:T(8,128)(2,1)} %get-tuple-element.140) | copy-start | bytes 4128772
  367.1 9.7 %copy-start.25 = (s32[8,128]{1,0:T(8,128)S(1)}, s32[8,128]{1,0:T(8,128)}, u32[]{:S(2)}) copy-start(s32[8,128]{1,0:T(8,128)} %get-tuple-element.344) | copy-start | bytes 12292
  374.7 2.0 copy-start
  374.7 3.1 copy-start.27
  399.6 9.1 copy-start.1
  449.2 1.2 copy-start.13
  449.2 30.4 %copy-start.3 = (f32[1024,64]{1,0:T(8,128)S(1)}, f32[1024,64]{1,0:T(8,128)}, u32[]{:S(2)}) copy-start(f32[1024,64]{1,0:T(8,128)} %copy-done.2) | copy-start | bytes 786436
  449.2 136.9 %all-gather.13.cloned.1.call-start = ((), (), s32[]{:S(2)}) async-start(), calls=%async_computation.6 | async-start | bytes 4718592 | tf_op jit(solution)/shard_map/all_gather | solution.py:2066
  479.5 286.6 %reduce-scatter.5.cloned.1.call-start = ((), (), s32[]{:S(2)}) async-start(), calls=%async_computation.7 | async-start | bytes 1310720 | tf_op jit(solution)/shard_map/reduce_scatter | solution.py:2134
  480.9 14.6 %copy-start.15 = (f32[32,2048]{1,0:T(8,128)S(1)}, f32[32,2048]{1,0:T(8,128)}, u32[]{:S(2)}) copy-start(f32[32,2048]{1,0:T(8,128)} %get-tuple-element.157) | copy-start | bytes 786436
  592.1 136.9 %copy-start.7 = (bf16[8,256,256]{2,1,0:T(8,128)(2,1)S(1)}, bf16[8,256,256]{2,1,0:T(8,128)(2,1)}, u32[]{:S(2)}) copy-start(bf16[8,256,256]{2,1,0:T(8,128)(2,1)} %get-tuple-element.182) | copy-start | bytes 3145732
  732.5 3.6 copy-start.9
  733.4 5.8 copy-start.28
  733.4 5.8 copy-start.30
  734.6 4.7 copy-start.14
  734.6 6.2 copy-start.22
  739.3 5.0 copy-start.29
  739.3 5.0 copy-start.31
  739.3 5.1 copy-start.33
  771.8 34.8 %copy-start.8 = (bf16[3,176,2048]{2,1,0:T(8,128)(2,1)S(1)}, bf16[3,176,2048]{2,1,0:T(8,128)(2,1)}, u32[]{:S(2)}) copy-start(bf16[3,176,2048]{2,1,0:T(8,128)(2,1)} %get-tuple-element.205) | copy-start | bytes 6488068
  806.8 50.4 %collective-permute-start.3 = (bf16[3,176,512]{2,1,0:T(8,128)(2,1)S(1)}, bf16[3,176,512]{2,1,0:T(8,128)(2,1)S(1)}, u32[]{:S(2)}, u32[]{:S(2)}) collective-permute-start(bf16[3,176,512]{2,1,0:T(8,128)(2,1)S(1)} %get-tuple-element.334), channel_id=1, source_target_pairs={{0,1},{1,2},{2,3},{3,0},{4,5},{5,6},{6,7},{7,4},{8,9},{9,10},{10,1... | collective-permute-start | bytes 1622024 | tf_op jit(solution)/shard_map/ppermute | solution.py:1812
  808.5 48.7 %collective-permute-start.4 = (bf16[3,176,512]{2,1,0:T(8,128)(2,1)S(1)}, bf16[3,176,512]{2,1,0:T(8,128)(2,1)S(1)}, u32[]{:S(2)}, u32[]{:S(2)}) collective-permute-start(bf16[3,176,512]{2,1,0:T(8,128)(2,1)S(1)} %get-tuple-element.333), channel_id=1, source_target_pairs={{0,2},{1,3},{2,0},{3,1},{4,6},{5,7},{6,4},{7,5},{8,10},{9,11},{10,... | collective-permute-start | bytes 1622024 | tf_op jit(solution)/shard_map/ppermute | solution.py:1812
  812.2 46.6 %collective-permute-start.5 = (bf16[3,176,512]{2,1,0:T(8,128)(2,1)S(1)}, bf16[3,176,512]{2,1,0:T(8,128)(2,1)S(1)}, u32[]{:S(2)}, u32[]{:S(2)}) collective-permute-start(bf16[3,176,512]{2,1,0:T(8,128)(2,1)S(1)} %get-tuple-element.332), channel_id=1, source_target_pairs={{0,3},{1,0},{2,1},{3,2},{4,7},{5,4},{6,5},{7,6},{8,11},{9,8},{10,9... | collective-permute-start | bytes 1622024 | tf_op jit(solution)/shard_map/ppermute | solution.py:1812
  857.2 6.9 copy-start.6
  858.8 7.4 copy-start.17
  858.8 7.4 copy-start.18
  860.6 39.3 %collective-permute-start.6 = (bf16[704,512]{1,0:T(8,128)(2,1)S(1)}, bf16[704,512]{1,0:T(8,128)(2,1)}, u32[]{:S(2)}, u32[]{:S(2)}) collective-permute-start(bf16[704,512]{1,0:T(8,128)(2,1)S(1)} %get-tuple-element.329), channel_id=1, source_target_pairs={{0,3},{1,0},{2,1},{3,2},{4,7},{5,4},{6,5},{7,6},{8,11},{9,8},{10,9... | collective-permute-start | bytes 2162696 | tf_op jit(solution)/shard_map/ppermute | solution.py:1812
  862.8 61.4 %collective-permute-start.7 = (bf16[704,512]{1,0:T(8,128)(2,1)S(1)}, bf16[704,512]{1,0:T(8,128)(2,1)}, u32[]{:S(2)}, u32[]{:S(2)}) collective-permute-start(bf16[704,512]{1,0:T(8,128)(2,1)S(1)} %get-tuple-element.328), channel_id=1, source_target_pairs={{0,2},{1,3},{2,0},{3,1},{4,6},{5,7},{6,4},{7,5},{8,10},{9,11},{10,... | collective-permute-start | bytes 2162696 | tf_op jit(solution)/shard_map/ppermute | solution.py:1812
  862.8 62.1 %collective-permute-start.8 = (bf16[704,512]{1,0:T(8,128)(2,1)S(1)}, bf16[704,512]{1,0:T(8,128)(2,1)}, u32[]{:S(2)}, u32[]{:S(2)}) collective-permute-start(bf16[704,512]{1,0:T(8,128)(2,1)S(1)} %get-tuple-element.327), channel_id=1, source_target_pairs={{0,1},{1,2},{2,3},{3,0},{4,5},{5,6},{6,7},{7,4},{8,9},{9,10},{10,1... | collective-permute-start | bytes 2162696 | tf_op jit(solution)/shard_map/ppermute | solution.py:1812
  870.4 22.1 %copy-start.32 = (f32[3,64]{1,0:T(4,128)S(1)}, f32[3,64]{1,0:T(4,128)}, u32[]{:S(2)}) copy-start(f32[3,64]{1,0:T(4,128)} %param.31) | copy-start | bytes 2308
  870.4 22.1 %copy-start.35 = (f32[3,64]{1,0:T(4,128)S(1)}, f32[3,64]{1,0:T(4,128)}, u32[]{:S(2)}) copy-start(f32[3,64]{1,0:T(4,128)} %param.32) | copy-start | bytes 2308
  870.4 22.1 %copy-start.36 = (f32[3,64]{1,0:T(4,128)S(1)}, f32[3,64]{1,0:T(4,128)}, u32[]{:S(2)}) copy-start(f32[3,64]{1,0:T(4,128)} %param.33) | copy-start | bytes 2308
  899.9 27.3 %copy-start.4 = (f32[256,2,512]{2,1,0:T(2,128)S(1)}, f32[256,2,512]{2,1,0:T(2,128)}, u32[]{:S(2)}) copy-start(f32[256,2,512]{2,1,0:T(2,128)} %param.25) | copy-start | bytes 3145732
  927.1 2.7 copy-start.12
Sparse Core Ops, SparseCore 0:
  35.5 56.3 all-gather.6
  94.3 92.0 all-gather.14
  240.7 47.2 all-gather.8
  289.7 50.8 all-gather.10
  449.4 52.7 reduce-scatter.2
  504.0 50.2 all-gather.12
  734.8 24.9 reduce-scatter.4

commit v17 on v16

--- a/solution.py
+++ b/solution.py
@@ -1938,10 +1938,11 @@
     by_head, normed_tok = make_heads(
         rows_low, gain_w[0:1], proj, tok_part(cosine_all), tok_part(sine_all), groups, repeat
     )
-    own_head, start_low, table_top = launch(
+    own_head, start_low, tok_cols, table_top = launch(
         [
             swap_blocks("narrow", by_head),
             gather_blocks("narrow", rows_low[tok_rows:]),
+            split_columns("wide", normed_tok),
             join_columns("wide", embed_cut[:, :third]),
         ],
         2,
@@ -2065,11 +2066,10 @@
     grad_out = grad_out.reshape(sel, width)
     out_all = lax.all_gather(grad_out, "wide", axis=0, tiled=True)
     acts, fed_back = feed_back(grad_out, ffn_w, gate, up, hidden)
-    grad_mid, gain_mid, grad_branch, acts, tok_cols = launch(
+    grad_mid, gain_mid, grad_branch, acts = launch(
         [
             settle_back(fed_back, middle, grad_layer, keep_row, gain_w[1:2]),
             swap_blocks("wide", acts),
-            split_columns("wide", normed_tok),
         ],
         9,
         "back_middle",

time: 959 us -> 954 us (level)
  no operation moved by 1% of the time
where the time goes in v17:
time: 954 us; the launch traced here: 938 us
  Pallas kernels  708 us (74%)
  other arithmetic  89 us (9%)
  local copies, waits for them, and re-layouts  41.7 us (4%)
  waiting for transfers between devices  38 us (4%)
  matrix products  23.5 us (2%)
  between operations  23.2 us (2%)
  starting transfers between devices  14.5 us (2%)
    pallas_call x13, Pallas kernels, launch(): pl.pallas_call(body, out_shape=outputs, in_specs=[place for task in tasks...  558 us
    pallas_call x1, Pallas kernels, newton(): pl.pallas_call(functools.partial(newton_any_body, rows), in_specs=[pl.Blo...  42.7 us
    ppermute x9, waiting for transfers between devices, shifted(): return lax.ppermute(parts, axis, pairs)  37.8 us
    pallas_call x1, Pallas kernels, lookup(): pl.pallas_call(lookup_body, in_specs=[pl.BlockSpec(memory_space=pltpu.SME...  29 us
    pallas_call x5, Pallas kernels, local_call(): pl.pallas_call(body, grid=(1,), in_specs=specs, out_specs=[pl.BlockSpec(a...  28.9 us
    sub x2, other arithmetic, adamw(): weight * (1.0 - rate * decay) - rate * update  22.8 us
    pallas_call x1, Pallas kernels, spread(): pl.pallas_call(spread_body, in_specs=[smem, smem, VMEM, VMEM], out_specs=...  21.1 us
  transfers between devices with their start and end apart: 16, of which 5 were waited for; matrix products, arithmetic and copies ran while one was open for 11% of the time, Pallas kernels for 50%

profile of v17, /device:TPU:17, one launch (start us, length us, event | category | flops | bytes accessed | tf_op | source)
XLA Modules:
  0.0 937.9 jit_solution(7388755551426836397)
XLA Ops:
  12.5 1.6 convert_element_type.131
  14.2 19.0 %gather_ids.1 = (s32[8,16,128]{2,1,0:T(8,128)}, f32[4,8,8,128]{3,2,1,0:T(8,128)}, bf16[4,256,256]{2,1,0:T(8,128)(2,1)}) custom-call(s32[16,128]{1,0:T(8,128)} %pad_bitcast_fusion.refs_0_, f32[8,128]{1,0:T(8,128)} %bitcast_convert_fusion.refs_1_, bf16[256,256]{1,0:T(8,128)(2,1)} %bitcast.267), custom_call_target="tpu_custom_call" | custom-call | bytes 108032 | tf_op jit(solution)/shard_map/gather_ids/pallas_call | solution.py:139
  35.4 2.5 convert_element_type.122
  39.2 1.9 collective-permute-start
  41.1 1.3 collective-permute-start.1
  42.4 1.4 collective-permute-start.2
  47.6 29.0 %lookup.1 = (bf16[9216,256]{1,0:T(8,128)(2,1)}, bf16[8192,256]{1,0:T(8,128)(2,1)}, s32[9248]{0:T(1024)}) custom-call(s32[9216]{0:T(1024)} %and_select_fusion.ids_ref, s32[9344]{0:T(1024)} %concatenate.44.turn_ref, f32[8192,256]{1,0:T(8,128)} %table_ref.1), custom_call_target="tpu_custom_call" | custom-call | bytes 8388608 | tf_op jit(solution)/shard_map/lookup/pallas_call | solution.py:1700
  77.5 11.6 %collective-permute-done.2.refs_3_ = bf16[528,512]{1,0:T(8,128)(2,1)S(1)} collective-permute-done((bf16[528,512]{1,0:T(8,128)(2,1)S(1)}, bf16[528,512]{1,0:T(8,128)(2,1)S(1)}, u32[]{:S(2)}, u32[]{:S(2)}) %collective-permute-start.2) | collective-permute-done | bytes 540704 | tf_op jit(solution)/shard_map/ppermute | solution.py:1812
  89.9 3.1 assemble.1
  97.8 1.9 multiply_sine_fusion
  101.4 4.0 fusion.42
  105.4 96.6 %fetch_rows.1.rows_ref = bf16[288,2048]{1,0:T(8,128)(2,1)} custom-call(bf16[4,2304,256]{2,1,0:T(8,128)(2,1)} %bitcast.230), custom_call_target="tpu_custom_call" | custom-call | bytes 737280 | tf_op jit(solution)/shard_map/fetch_rows/pallas_call | solution.py:139
  202.0 1.7 slice_convert_fusion
  203.7 5.0 make_heads.1
  208.7 29.9 %trade_heads.1 = (bf16[4,1,2,256,128]{4,3,2,1,0:T(8,128)(2,1)}, bf16[4,32,2048]{2,1,0:T(8,128)(2,1)}, bf16[8,256,256]{2,1,0:T(8,128)(2,1)}, bf16[336,2048]{1,0:T(8,128)(2,1)}) custom-call(bf16[4,1,2,256,128]{4,3,2,1,0:T(8,128)(2,1)} %get-tuple-element.126.refs_0_, bf16[32,2048]{1,0:T(8,128)(2,1)} %get-tuple-element.341.refs_1_, ...), custom_call_target="tpu_custom_call" | custom-call | bytes 819200 | tf_op jit(solution)/shard_map/trade_heads/pallas_call | solution.py:139
  238.7 6.9 attend.1
  246.9 27.3 %settle_middle.1 = (f32[32,2048]{1,0:T(8,128)}, bf16[4,32,2048]{2,1,0:T(8,128)(2,1)}, bf16[336,2048]{1,0:T(8,128)(2,1)}) custom-call(bf16[4,32,2048]{2,1,0:T(8,128)(2,1)} %bitcast.260, f32[32,2048]{1,0:T(8,128)} %get-tuple-element.340.refs_1_.refs_2_, f32[32,2048]{1,0:T(8,128)} %get-tuple-element.340.refs_1_.refs_2_, f32[1,2048]{1,0:T(1,128)} %broadcast_in_dim.136.refs_3_, ...), custom_call_target="tpu_custom_call" | custom-call | bytes 575488 | tf_op jit(solution)/shard_map/settle_middle/pallas_call | solution.py:139
  274.3 2.6 slice.148.refs_5_
  278.7 2.5 convert_bitcast_fusion
  281.3 1.9 pad_maximum_fusion.1
  284.4 13.5 %feed.1 = (f32[8,128,176]{2,1,0:T(8,128)}, f32[8,128,176]{2,1,0:T(8,128)}, bf16[8,128,176]{2,1,0:T(8,128)(2,1)}, bf16[128,2048]{1,0:T(8,128)(2,1)}) custom-call(bf16[128,2048]{1,0:T(8,128)(2,1)} %bitcast.247, bf16[8,3,176,2048]{3,2,1,0:T(8,128)(2,1)} %bitcast.222), custom_call_target="tpu_custom_call" | custom-call | flops 2214592512 | bytes 17301504 | tf_op jit(solution)/shard_map/feed/pallas_call | solution.py:1409
  298.5 28.0 %settle_late.1 = (f32[32,2048]{1,0:T(8,128)}, bf16[4,32,2048]{2,1,0:T(8,128)(2,1)}, bf16[352,2048]{1,0:T(8,128)(2,1)}) custom-call(bf16[4,32,2048]{2,1,0:T(8,128)(2,1)} %bitcast.263, f32[32,2048]{1,0:T(8,128)} %get-tuple-element.137.refs_1_, f32[32,2048]{1,0:T(8,128)} %get-tuple-element.340.refs_1_.refs_2_, f32[1,2048]{1,0:T(1,128)} %broadcast_in_dim.137.refs_3_, ...), custom_call_target="tpu_custom_call" | custom-call | bytes 591872 | tf_op jit(solution)/shard_map/settle_late/pallas_call | solution.py:139
  326.5 1.2 constant_dynamic-update-slice_fusion.1
  327.8 2.7 constant_dynamic-update-slice_fusion.refs_3_
  330.4 42.0 %gather_late.1 = (bf16[8,128,2048]{2,1,0:T(8,128)(2,1)}, bf16[4,352,512]{2,1,0:T(8,128)(2,1)}, f32[1024,1024]{1,0:T(8,128)}, f32[3,1024]{1,0:T(4,128)}) custom-call(bf16[128,2048]{1,0:T(8,128)(2,1)} %bitcast.261, bf16[4,352,512]{2,1,0:T(8,128)(2,1)} %get-tuple-element.331.refs_1_, bf16[1024,2048]{1,0:T(8,128)(2,1)} %all-gather.9.cloned.1.call-done.refs_2_.refs_6_, ...), custom_call_target="tpu_custom_call" | custom-call | bytes 2525184 | tf_op jit(solution)/shard_map/gather_late/pallas_call | solution.py:139
  372.5 7.6 fusion.45
  380.1 2.0 copy-done
  383.9 13.4 %combine_stats.1 = f32[3,8,256]{2,1,0:T(8,128)} custom-call(f32[3,8,256]{2,1,0:T(8,128)} %bitcast.277), custom_call_target="tpu_custom_call" | custom-call | bytes 6144 | tf_op jit(solution)/shard_map/combine_stats/pallas_call | solution.py:139
  398.1 6.7 fusion.4
  404.8 9.1 convolution_convert_fusion
  413.8 40.5 %sum_late.1 = (f32[128,2048]{1,0:T(8,128)}, bf16[4,352,512]{2,1,0:T(8,128)(2,1)}, bf16[1,1024,2048]{2,1,0:T(8,128)(2,1)}, f32[1,2048]{1,0:T(1,128)}) custom-call(bf16[8,128,2048]{2,1,0:T(8,128)(2,1)} %bitcast.233, bf16[4,352,512]{2,1,0:T(8,128)(2,1)} %get-tuple-element.330.refs_1_, bf16[1024,1024]{1,0:T(8,128)(2,1)} %get-tuple-element.356.refs_2_.refs_4_, ...), custom_call_target="tpu_custom_call" | custom-call | bytes 2327552 | tf_op jit(solution)/shard_map/sum_late/pallas_call | solution.py:139
  457.1 27.4 %back_late.1 = (f32[32,2048]{1,0:T(8,128)}, f32[1,2048]{1,0:T(1,128)}, bf16[4,32,2048]{2,1,0:T(8,128)(2,1)}, bf16[8,128,512]{2,1,0:T(8,128)(2,1)}, bf16[8,128,256]{2,1,0:T(8,128)(2,1)}) custom-call(bf16[4,32,2048]{2,1,0:T(8,128)(2,1)} %bitcast.250, f32[32,2048]{1,0:T(8,128)} %get-tuple-element.150.refs_1_, f32[32,2048]{1,0:T(8,128)} %broadcast_in_dim.140.refs_2_, ...), custom_call_target="tpu_custom_call" | custom-call | bytes 510976 | tf_op jit(solution)/shard_map/back_late/pallas_call | solution.py:139
  484.6 1.3 pad_maximum_fusion.4
  485.9 14.6 %feed_back.1 = (bf16[8,3,128,176]{3,2,1,0:T(8,128)(2,1)}, bf16[128,2048]{1,0:T(8,128)(2,1)}) custom-call(bf16[128,2048]{1,0:T(8,128)(2,1)} %bitcast.249, bf16[8,3,176,2048]{3,2,1,0:T(8,128)(2,1)} %bitcast.223, f32[8,128,176]{2,1,0:T(8,128)} %get-tuple-element.154.gate_ref, f32[8,128,176]{2,1,0:T(8,128)} %get-tuple-element.155.up_ref, ...), custom_call_target="tpu_custom_call" | custom-call | flops 2214592512 | bytes 17301504 | tf_op jit(solution)/shard_map/feed_back/pallas_call | solution.py:1461
  501.2 34.2 %back_middle.1 = (f32[32,2048]{1,0:T(8,128)}, f32[1,2048]{1,0:T(1,128)}, bf16[4,32,2048]{2,1,0:T(8,128)(2,1)}, bf16[8,3,128,176]{3,2,1,0:T(8,128)(2,1)}) custom-call(bf16[4,32,2048]{2,1,0:T(8,128)(2,1)} %bitcast.262, f32[32,2048]{1,0:T(8,128)} %get-tuple-element.137.refs_1_, f32[32,2048]{1,0:T(8,128)} %broadcast_multiply_fusion.refs_2_, ...), custom_call_target="tpu_custom_call" | custom-call | bytes 502784 | tf_op jit(solution)/shard_map/back_middle/pallas_call | solution.py:139
  535.5 2.7 copy.171
  538.2 1.7 multiply_add_fusion.1.base_ref
  539.8 7.9 attend_back.1
  547.7 31.4 %trade_grads.1 = (bf16[4,1,2,256,128]{4,3,2,1,0:T(8,128)(2,1)}, f32[32,2048]{1,0:T(8,128)}, bf16[8,128,512]{2,1,0:T(8,128)(2,1)}, bf16[8,128,256]{2,1,0:T(8,128)...) custom-call(bf16[4,1,2,256,128]{4,3,2,1,0:T(8,128)(2,1)} %get-tuple-element.166.refs_0_, ...), custom_call_target="tpu_custom_call" | custom-call | bytes 2606080 | tf_op jit(solution)/shard_map/trade_grads/pallas_call | solution.py:139
  579.2 6.0 rows_back.1
  585.2 139.2 %return_rows.1 = (bf16[4,2304,256]{2,1,0:T(8,128)(2,1)}, bf16[4,1024,176]{2,1,0:T(8,128)(2,1)}, bf16[8,256,1024]{2,1,0:T(8,128)(2,1)}, bf16[8,1024,256]{2,1,0:T(...) custom-call(bf16[288,2048]{1,0:T(8,128)(2,1)} %get-tuple-element.183.refs_0_, ...), custom_call_target="tpu_custom_call" | custom-call | bytes 4146176 | tf_op jit(solution)/shard_map/return_rows/pallas_call | solution.py:139
  724.4 3.5 convolution_bitcast_fusion
  731.5 3.1 pad_maximum_fusion.mom_ref
  734.7 1.5 convolution_bitcast_fusion.1
  736.2 1.7 convolution_bitcast_fusion.2
  740.3 21.1 %spread.1 = (f32[8192,256]{1,0:T(8,128)}, f32[8,256]{1,0:T(8,128)}) custom-call(s32[9216]{0:T(1024)} %and_select_fusion.ids_ref, s32[9248]{0:T(1024)} %get-tuple-element.191.list_ref, bf16[9216,256]{1,0:T(8,128)(2,1)} %bitcast.229, bf16[8192,256]{1,0:T(8,128)(2,1)} %bitcast.234), custom_call_target="tpu_custom_call" | custom-call | flops 2359296 | bytes 16777216 | tf_op jit(solution)/shard_map/spread/pallas_call | solution.py:1774
  761.5 1.3 reduce_sum.168
  762.8 2.3 fusion.43
  768.4 29.3 %combine_sums.1 = (f32[4,8,256]{2,1,0:T(8,128)}, bf16[4,512,128]{2,1,0:T(8,128)(2,1)}, bf16[4,512,512]{2,1,0:T(8,128)(2,1)}, bf16[4,176,2048]{2,1,0:T(8,128)(2,1)}, f32[1,2048]{1,0:T(1,128)}) custom-call(f32[4,8,256]{2,1,0:T(8,128)} %maximum_maximum_fusion.1.refs_0_, bf16[512,128]{1,0:T(8,128)(2,1)} %bitcast.259, bf16[512,512]{1,0:T(8,128)(2,1)} %bitcast.245, ...), custom_call_target="tpu_custom_call" | custom-call | bytes 2008064 | tf_op jit(solution)/shard_map/combine_sums/pallas_call | solution.py:139
  797.8 1.3 slice_bitcast_fusion
  803.5 3.9 collective-permute-start.4
  807.4 2.3 collective-permute-start.5
  809.7 42.7 %newton.1 = bf16[4,704,512]{2,1,0:T(8,128)(2,1)} custom-call(f32[1]{0:T(128)} %bitcast.71.factor_ref, bf16[4,704,512]{2,1,0:T(8,128)(2,1)} %pad_maximum_fusion.mom_ref, bf16[4,176,2048]{2,1,0:T(8,128)(2,1)} %get-tuple-element.202.grad_ref, bf16[4,512,512]{2,1,0:T(8,128)(2,1)} %get-tuple-element.203.qo_ref, bf16[4,512,128]{2,1,0:T(8,128)(2,1)} %get-tuple-element.204.kv_ref), custom_call_target="tpu_custom_call" | custom-call | flops 23789568000 | bytes 8650752 | tf_op jit(solution)/shard_map/newton/pallas_call | solution.py:1640
  853.3 1.7 dynamic-slice_bitcast_fusion
  855.1 2.3 collective-permute-start.6
  857.3 1.3 collective-permute-start.8
  858.9 1.8 copy.182
  862.2 2.7 convert_multiply_fusion
  864.9 22.1 %multiply_subtract_fusion = (f32[8192,256]{1,0:T(8,128)}, f32[8192,256]{1,0:T(8,128)}, f32[8192,256]{1,0:T(8,128)}) fusion(f32[8192,256]{1,0:T(8,128)} %table_ref.1, f32[8192,256]{1,0:T(8,128)} %get-tuple-element.197, f32[]{:T(128)} %div.51, f32[8192,256]{1,0:T(8,128)} %param.23, f32[8192,256]{1,0:T(8,128)} %param.24), kind=kLoop, calls=%fused_computation.2 | loop fusion | flops 31457280 | bytes 58720260 | tf_op jit(solution)/shard_map/sub | solution.py:1801
  887.7 6.7 bitcast_add_fusion
  894.4 23.3 %collective-permute-done.7 = bf16[704,512]{1,0:T(8,128)(2,1)} collective-permute-done((bf16[704,512]{1,0:T(8,128)(2,1)S(1)}, bf16[704,512]{1,0:T(8,128)(2,1)}, u32[]{:S(2)}, u32[]{:S(2)}) %collective-permute-start.7) | collective-permute-done | bytes 720928 | tf_op jit(solution)/shard_map/ppermute | solution.py:1812
  918.9 2.1 fusion.18
  921.2 2.2 bitcast_subtract_fusion.1
  924.6 5.1 bitcast_subtract_fusion
  (212 shorter events, 44.8 us)
Async XLA Ops:
  7.2 196.5 %all-gather.7.cloned.1.call-start = ((), (), s32[]{:S(2)}) async-start(), calls=%async_computation.2 | async-start | bytes 9437184 | tf_op jit(solution)/shard_map/all_gather | solution.py:1883
  35.4 203.3 %all-gather.15.cloned.1.call-start = ((), (), s32[]{:S(2)}) async-start(), calls=%async_computation.8 | async-start | bytes 19464192 | tf_op jit(solution)/shard_map/all_gather | solution.py:1911
  37.9 5.8 copy-start.24
  39.2 37.4 %collective-permute-start = (bf16[528,512]{1,0:T(8,128)(2,1)}, bf16[528,512]{1,0:T(8,128)(2,1)S(1)}, u32[]{:S(2)}, u32[]{:S(2)}) collective-permute-start(bf16[528,512]{1,0:T(8,128)(2,1)} %get-tuple-element.338), channel_id=1, source_target_pairs={{0,1},{1,2},{2,3},{3,0},{4,5},{5,6},{6,7},{7,4},{8,9},{9,10},{10,1... | collective-permute-start | bytes 1622024 | tf_op jit(solution)/shard_map/ppermute | solution.py:1812
  41.1 36.4 %collective-permute-start.1 = (bf16[528,512]{1,0:T(8,128)(2,1)S(1)}, bf16[528,512]{1,0:T(8,128)(2,1)S(1)}, u32[]{:S(2)}, u32[]{:S(2)}) collective-permute-start(bf16[528,512]{1,0:T(8,128)(2,1)S(1)} %get-tuple-element.337), channel_id=1, source_target_pairs={{0,2},{1,3},{2,0},{3,1},{4,6},{5,7},{6,4},{7,5},{8,10},{9,11},{10,... | collective-permute-start | bytes 1622024 | tf_op jit(solution)/shard_map/ppermute | solution.py:1812
  42.4 46.7 %collective-permute-start.2 = (bf16[528,512]{1,0:T(8,128)(2,1)S(1)}, bf16[528,512]{1,0:T(8,128)(2,1)S(1)}, u32[]{:S(2)}, u32[]{:S(2)}) collective-permute-start(bf16[528,512]{1,0:T(8,128)(2,1)S(1)} %get-tuple-element.336), channel_id=1, source_target_pairs={{0,3},{1,0},{2,1},{3,2},{4,7},{5,4},{6,5},{7,6},{8,11},{9,8},{10,9... | collective-permute-start | bytes 1622024 | tf_op jit(solution)/shard_map/ppermute | solution.py:1812
  76.6 16.5 %copy-start.23 = (f32[4,8,8,128]{3,2,1,0:T(8,128)S(1)}, f32[4,8,8,128]{3,2,1,0:T(8,128)}, u32[]{:S(2)}) copy-start(f32[4,8,8,128]{3,2,1,0:T(8,128)} %get-tuple-element.124) | copy-start | bytes 393220
  76.6 17.5 %copy-start.37 = (s32[1,2]{1,0:T(1,128)S(1)}, s32[1,2]{1,0:T(1,128)}, u32[]{:S(2)}) copy-start(s32[1,2]{1,0:T(1,128)} %param.20) | copy-start | bytes 28
  76.6 18.3 %copy-start.34 = (s32[1,128]{1,0:T(1,128)S(1)}, s32[1,128]{1,0:T(1,128)}, u32[]{:S(2)}) copy-start(s32[1,128]{1,0:T(1,128)} %param.18) | copy-start | bytes 1540
  76.6 12.5 %copy-start.19 = (bf16[528,512]{1,0:T(8,128)(2,1)}, bf16[528,512]{1,0:T(8,128)(2,1)S(1)}, u32[]{:S(2)}) copy-start(bf16[528,512]{1,0:T(8,128)(2,1)S(1)} %collective-permute-done.refs_1_) | copy-start | bytes 1622020
  77.5 11.6 %copy-start.20 = (bf16[528,512]{1,0:T(8,128)(2,1)}, bf16[528,512]{1,0:T(8,128)(2,1)S(1)}, u32[]{:S(2)}) copy-start(bf16[528,512]{1,0:T(8,128)(2,1)S(1)} %collective-permute-done.1.refs_2_) | copy-start | bytes 1622020
  89.1 0.8 copy-start.21
  93.0 237.4 %all-gather.9.cloned.1.call-start = ((), (), s32[]{:S(2)}) async-start(), calls=%async_computation.3 | async-start | bytes 4718592 | tf_op jit(solution)/shard_map/all_gather | solution.py:1964
  96.6 8.8 copy-start.26
  99.7 0.8 copy-start.2
  245.5 32.6 %copy-start.16 = (f32[256,2,128]{2,1,0:T(2,128)S(1)}, f32[256,2,128]{2,1,0:T(2,128)}, u32[]{:S(2)}) copy-start(f32[256,2,128]{2,1,0:T(2,128)} %param.28) | copy-start | bytes 786436
  245.5 32.7 %copy-start.5 = (f32[256,2,512]{2,1,0:T(2,128)S(1)}, f32[256,2,512]{2,1,0:T(2,128)}, u32[]{:S(2)}) copy-start(f32[256,2,512]{2,1,0:T(2,128)} %param.26) | copy-start | bytes 3145732
  245.6 151.7 %all-gather.11.cloned.1.call-start = ((), (), s32[]{:S(2)}) async-start(), calls=%async_computation.4 | async-start | bytes 4718592 | tf_op jit(solution)/shard_map/all_gather | solution.py:1981
  274.2 265.6 %reduce-scatter.3.cloned.1.call-start = ((), (), s32[]{:S(2)}) async-start(), calls=%async_computation.5 | async-start | bytes 4718592 | tf_op jit(solution)/shard_map/reduce_scatter | solution.py:2049
  281.3 1.9 copy-start.10
  284.4 42.1 %copy-start.11 = (bf16[336,2048]{1,0:T(8,128)(2,1)S(1)}, bf16[336,2048]{1,0:T(8,128)(2,1)}, u32[]{:S(2)}) copy-start(bf16[336,2048]{1,0:T(8,128)(2,1)} %get-tuple-element.141) | copy-start | bytes 4128772
  372.4 9.7 %copy-start.25 = (s32[8,128]{1,0:T(8,128)S(1)}, s32[8,128]{1,0:T(8,128)}, u32[]{:S(2)}) copy-start(s32[8,128]{1,0:T(8,128)} %get-tuple-element.344) | copy-start | bytes 12292
  380.1 2.0 copy-start
  380.1 3.1 copy-start.27
  404.8 9.1 copy-start.1
  454.3 1.2 copy-start.13
  454.3 30.3 %copy-start.3 = (f32[1024,64]{1,0:T(8,128)S(1)}, f32[1024,64]{1,0:T(8,128)}, u32[]{:S(2)}) copy-start(f32[1024,64]{1,0:T(8,128)} %copy-done.2) | copy-start | bytes 786436
  454.4 124.8 %all-gather.13.cloned.1.call-start = ((), (), s32[]{:S(2)}) async-start(), calls=%async_computation.6 | async-start | bytes 4718592 | tf_op jit(solution)/shard_map/all_gather | solution.py:2067
  484.6 278.2 %reduce-scatter.5.cloned.1.call-start = ((), (), s32[]{:S(2)}) async-start(), calls=%async_computation.7 | async-start | bytes 1310720 | tf_op jit(solution)/shard_map/reduce_scatter | solution.py:2134
  485.9 14.6 %copy-start.15 = (f32[32,2048]{1,0:T(8,128)S(1)}, f32[32,2048]{1,0:T(8,128)}, u32[]{:S(2)}) copy-start(f32[32,2048]{1,0:T(8,128)} %get-tuple-element.158) | copy-start | bytes 786436
  585.2 139.2 %copy-start.7 = (bf16[8,256,256]{2,1,0:T(8,128)(2,1)S(1)}, bf16[8,256,256]{2,1,0:T(8,128)(2,1)}, u32[]{:S(2)}) copy-start(bf16[8,256,256]{2,1,0:T(8,128)(2,1)} %get-tuple-element.182) | copy-start | bytes 3145732
  727.9 3.6 copy-start.9
  728.8 5.8 copy-start.28
  728.8 5.8 copy-start.30
  730.0 4.7 copy-start.14
  730.0 6.2 copy-start.22
  734.6 5.0 copy-start.29
  734.6 5.0 copy-start.31
  734.6 5.1 copy-start.33
  768.4 34.8 %copy-start.8 = (bf16[3,176,2048]{2,1,0:T(8,128)(2,1)S(1)}, bf16[3,176,2048]{2,1,0:T(8,128)(2,1)}, u32[]{:S(2)}) copy-start(bf16[3,176,2048]{2,1,0:T(8,128)(2,1)} %get-tuple-element.205) | copy-start | bytes 6488068
  803.5 49.0 %collective-permute-start.3 = (bf16[3,176,512]{2,1,0:T(8,128)(2,1)S(1)}, bf16[3,176,512]{2,1,0:T(8,128)(2,1)S(1)}, u32[]{:S(2)}, u32[]{:S(2)}) collective-permute-start(bf16[3,176,512]{2,1,0:T(8,128)(2,1)S(1)} %get-tuple-element.334), channel_id=1, source_target_pairs={{0,1},{1,2},{2,3},{3,0},{4,5},{5,6},{6,7},{7,4},{8,9},{9,10},{10,1... | collective-permute-start | bytes 1622024 | tf_op jit(solution)/shard_map/ppermute | solution.py:1812
  803.5 48.9 %collective-permute-start.4 = (bf16[3,176,512]{2,1,0:T(8,128)(2,1)S(1)}, bf16[3,176,512]{2,1,0:T(8,128)(2,1)S(1)}, u32[]{:S(2)}, u32[]{:S(2)}) collective-permute-start(bf16[3,176,512]{2,1,0:T(8,128)(2,1)S(1)} %get-tuple-element.333), channel_id=1, source_target_pairs={{0,2},{1,3},{2,0},{3,1},{4,6},{5,7},{6,4},{7,5},{8,10},{9,11},{10,... | collective-permute-start | bytes 1622024 | tf_op jit(solution)/shard_map/ppermute | solution.py:1812
  807.4 45.9 %collective-permute-start.5 = (bf16[3,176,512]{2,1,0:T(8,128)(2,1)S(1)}, bf16[3,176,512]{2,1,0:T(8,128)(2,1)S(1)}, u32[]{:S(2)}, u32[]{:S(2)}) collective-permute-start(bf16[3,176,512]{2,1,0:T(8,128)(2,1)S(1)} %get-tuple-element.332), channel_id=1, source_target_pairs={{0,3},{1,0},{2,1},{3,2},{4,7},{5,4},{6,5},{7,6},{8,11},{9,8},{10,9... | collective-permute-start | bytes 1622024 | tf_op jit(solution)/shard_map/ppermute | solution.py:1812
  852.4 6.2 copy-start.6
  853.3 7.4 copy-start.17
  853.3 7.4 copy-start.18
  855.1 39.3 %collective-permute-start.6 = (bf16[704,512]{1,0:T(8,128)(2,1)S(1)}, bf16[704,512]{1,0:T(8,128)(2,1)}, u32[]{:S(2)}, u32[]{:S(2)}) collective-permute-start(bf16[704,512]{1,0:T(8,128)(2,1)S(1)} %get-tuple-element.329), channel_id=1, source_target_pairs={{0,3},{1,0},{2,1},{3,2},{4,7},{5,4},{6,5},{7,6},{8,11},{9,8},{10,9... | collective-permute-start | bytes 2162696 | tf_op jit(solution)/shard_map/ppermute | solution.py:1812
  857.3 60.4 %collective-permute-start.7 = (bf16[704,512]{1,0:T(8,128)(2,1)S(1)}, bf16[704,512]{1,0:T(8,128)(2,1)}, u32[]{:S(2)}, u32[]{:S(2)}) collective-permute-start(bf16[704,512]{1,0:T(8,128)(2,1)S(1)} %get-tuple-element.328), channel_id=1, source_target_pairs={{0,2},{1,3},{2,0},{3,1},{4,6},{5,7},{6,4},{7,5},{8,10},{9,11},{10,... | collective-permute-start | bytes 2162696 | tf_op jit(solution)/shard_map/ppermute | solution.py:1812
  857.3 61.5 %collective-permute-start.8 = (bf16[704,512]{1,0:T(8,128)(2,1)S(1)}, bf16[704,512]{1,0:T(8,128)(2,1)}, u32[]{:S(2)}, u32[]{:S(2)}) collective-permute-start(bf16[704,512]{1,0:T(8,128)(2,1)S(1)} %get-tuple-element.327), channel_id=1, source_target_pairs={{0,1},{1,2},{2,3},{3,0},{4,5},{5,6},{6,7},{7,4},{8,9},{9,10},{10,1... | collective-permute-start | bytes 2162696 | tf_op jit(solution)/shard_map/ppermute | solution.py:1812
  864.9 22.1 %copy-start.32 = (f32[3,64]{1,0:T(4,128)S(1)}, f32[3,64]{1,0:T(4,128)}, u32[]{:S(2)}) copy-start(f32[3,64]{1,0:T(4,128)} %param.31) | copy-start | bytes 2308
  864.9 22.1 %copy-start.35 = (f32[3,64]{1,0:T(4,128)S(1)}, f32[3,64]{1,0:T(4,128)}, u32[]{:S(2)}) copy-start(f32[3,64]{1,0:T(4,128)} %param.32) | copy-start | bytes 2308
  864.9 22.1 %copy-start.36 = (f32[3,64]{1,0:T(4,128)S(1)}, f32[3,64]{1,0:T(4,128)}, u32[]{:S(2)}) copy-start(f32[3,64]{1,0:T(4,128)} %param.33) | copy-start | bytes 2308
  894.4 26.8 %copy-start.4 = (f32[256,2,512]{2,1,0:T(2,128)S(1)}, f32[256,2,512]{2,1,0:T(2,128)}, u32[]{:S(2)}) copy-start(f32[256,2,512]{2,1,0:T(2,128)} %param.25) | copy-start | bytes 3145732
  921.0 2.7 copy-start.12
Sparse Core Ops, SparseCore 0:
  35.5 56.3 all-gather.6
  94.3 92.0 all-gather.14
  245.7 45.0 all-gather.8
  292.5 45.7 all-gather.10
  454.5 52.6 reduce-scatter.2
  509.1 43.0 all-gather.12
  730.1 24.6 reduce-scatter.4
